TPU v7x, 32 devices: a whole 2x2x4 slice. The times are simulated.
32 devices in a mesh: rep: 8 (over y, x, core), exp: 4 (over z).
Axes of the slice: x: 2, y: 2, z: 4, core: 2. Of those that a mesh axis runs over, the one named last changes fastest.
Arguments:
- grad_out: bfloat16 [4096, 3584], P(('rep', 'exp')), may hold values from -6 to 6
- routes: int32 [4096, 4], P(('rep', 'exp')), may hold values from 0 to 15, as said below
- affinity: float32 [4096, 4], P(('rep', 'exp')), may hold values from 0.02 to 0.98
- saved_hidden: bfloat16 [8, 16, 4, 60, 1024], P('rep', 'exp'), may hold values from -0.29882812 to 0.29882812
- down_proj: bfloat16 [1024, 16, 3584], P('rep', 'exp'), may hold values from -0.1875 to 0.1875
Outputs:
- affinity_grad: float32 [4096, 4], P(('rep', 'exp'))
- hidden_grad: bfloat16 [8, 16, 4, 60, 1024], P('rep', 'exp')
- down_grad: float32 [1024, 16, 3584], P('rep', 'exp')
Inputs may be any that keep to these rules, and one draw needn't show every extreme that they name: `routes`: each row names 4 different experts. Among the tokens of one device no expert is named more than 60 times; in every replica group one expert is named exactly 60 times by the tokens of each device of the group.
All inputs are finite; a program needn't handle non-finite values.
Results may differ from a plain program's by a relative error of at most 0.02.
Values may be sent and summed in bfloat16 or wider, within the bound.
No kernel may reach another device: no remote copies, remote signals or barrier semaphores. Data moves between devices by JAX's collectives and lax.ppermute only.
A program may use at most 192 MiB of HBM per device.

v0:
```python
import jax
import jax.numpy as jnp
from jax import lax
from jax.sharding import PartitionSpec as P

ROUTE_SCALE = 2.5


def pack_routes(grad_rows, route_ids, route_weight, expert_count, most):
    expert_ids = jnp.arange(expert_count, dtype=jnp.int32)
    naming = jnp.sum((route_ids[:, :, None] == expert_ids[None, None, :]).astype(jnp.int32), axis=1)
    before = jnp.cumsum(naming, axis=0) - naming
    slot_ids = jnp.take_along_axis(before, route_ids, axis=1)
    placed = (route_ids * most + slot_ids).reshape(-1)
    token_ids = jnp.repeat(jnp.arange(grad_rows.shape[0], dtype=jnp.int32), route_ids.shape[1])
    source = jnp.zeros((expert_count * most,), jnp.int32).at[placed].set(token_ids)
    filled = jnp.zeros((expert_count * most,), jnp.int32).at[placed].set(1)
    weights = (
        jnp.zeros((expert_count * most,), route_weight.dtype)
        .at[placed]
        .set(route_weight.reshape(-1))
    )
    fetched = jnp.take(grad_rows, source, axis=0)
    packed = jnp.where(filled[:, None] > 0, fetched, jnp.zeros_like(fetched))
    return (packed, weights, placed)


def on_device(grad_out, routes, affinity, saved_hidden, down_proj):
    exp_devices = lax.axis_size("exp")
    local_experts = down_proj.shape[1]
    expert_count = exp_devices * local_experts
    most = saved_hidden.shape[3]
    width = grad_out.shape[1]
    hidden_units = saved_hidden.shape[4]
    row_count = exp_devices * most
    totals = jnp.sum(affinity, axis=-1, keepdims=True)
    shares = affinity / totals
    route_weight = (ROUTE_SCALE * shares).astype(jnp.bfloat16)
    packed, weights, placed = pack_routes(grad_out, routes, route_weight, expert_count, most)
    outgoing = packed.reshape(exp_devices, local_experts, 1, most, width)
    outgoing_weight = weights.reshape(exp_devices, local_experts, 1, most)
    received, received_weight = (
        lax.all_to_all(outgoing, "exp", split_axis=0, concat_axis=2, tiled=True),
        lax.all_to_all(outgoing_weight, "exp", split_axis=0, concat_axis=2, tiled=True),
    )
    received = received.reshape(local_experts, row_count, width)
    row_scale = received_weight.reshape(local_experts, row_count).astype(jnp.float32)
    hidden = saved_hidden.reshape(local_experts, row_count, hidden_units)
    gathered = lax.all_gather(down_proj, "rep", axis=0, tiled=True)
    projected = jnp.einsum("erd,hed->erh", received, gathered, preferred_element_type=jnp.float32)
    hidden_grad = (row_scale[:, :, None] * projected).astype(jnp.bfloat16)
    combine_grad = ROUTE_SCALE * jnp.sum(hidden.astype(jnp.float32) * projected, axis=-1)
    scaled = (row_scale[:, :, None] * received.astype(jnp.float32)).astype(jnp.bfloat16)
    grad_term = jnp.einsum("erh,erd->hed", hidden, scaled, preferred_element_type=jnp.float32)
    down_grad = lax.psum_scatter(
        grad_term.astype(jnp.bfloat16), "rep", scatter_dimension=0, tiled=True
    ).astype(jnp.float32)
    returned = lax.all_to_all(
        combine_grad.reshape(local_experts, exp_devices, most),
        "exp",
        split_axis=1,
        concat_axis=0,
        tiled=True,
    )
    route_grad = jnp.take(returned.reshape(-1), placed).reshape(routes.shape)
    affinity_grad = (route_grad - jnp.sum(route_grad * shares, axis=-1, keepdims=True)) / totals
    return (affinity_grad, hidden_grad.reshape(saved_hidden.shape), down_grad)


def solution(mesh):
    return jax.shard_map(
        on_device,
        mesh=mesh,
        in_specs=(
            P(("rep", "exp"), None),
            P(("rep", "exp"), None),
            P(("rep", "exp"), None),
            P("rep", "exp", None, None, None),
            P("rep", "exp", None),
        ),
        out_specs=(
            P(("rep", "exp"), None),
            P("rep", "exp", None, None, None),
            P("rep", "exp", None),
        ),
        check_vma=False,
    )
```

profile of v0, /device:TPU:0, one launch (start us, length us, event | category | flops | bytes accessed | tf_op | source)
XLA Modules:
  0.0 482.6 jit_solution(16572833865437565524)
XLA Ops:
  7.2 4.7 copy.127
  12.0 0.1 copy.131
  12.1 0.1 reshape.183
  12.3 0.1 copy.119
  12.4 0.1 copy.121
  12.5 0.1 reshape.157
  12.6 0.2 reduce_window_sum.11
  12.8 3.8 gather_fusion.2
  16.6 0.1 reshape.160
  16.7 0.1 copy.125
  16.9 0.1 reshape.132
  17.0 3.8 scatter_custom_fusion.2
  20.8 0.7 reshape.137
  21.5 6.3 %all-to-all-start.2 = ((bf16[4,4,1,60]{3,1,2,0:T(4,128)(2,1)}), bf16[4,4,1,60]{3,1,2,0:T(4,128)(2,1)S(1)}, u32[]{:S(2)}, u32[]{:S(2)}) async-start(bf16[4,4,1,60]{3,1,2,0:T(4,128)(2,1)} %bitcast.8), calls=%async_computation.2 | async-start | bytes 8192 | tf_op jit(solution)/shard_map/all_to_all | solution.py:44
  27.8 2.4 scatter_custom_fusion
  30.2 0.1 broadcast_in_dim.58
  30.4 0.1 reshape.175
  30.5 2.6 scatter_custom_fusion.1
  33.1 0.1 broadcast_in_dim.61
  33.2 7.2 %gather_fusion = bf16[960,3584]{1,0:T(8,128)(2,1)} fusion(bf16[128,3584]{1,0:T(8,128)(2,1)S(1)} %copy-done, s32[1024]{0:T(1024)S(1)} %pad_clamp_fusion.1), kind=kCustom, calls=%fused_computation | custom fusion | bytes 13766400 | tf_op jit(solution)/shard_map/jit(_take)/gather | solution.py:23
  40.4 8.6 %gather.18 = bf16[4,4,1,60,3584]{4,3,1,0,2:T(8,128)(2,1)} reshape(bf16[960,3584]{1,0:T(8,128)(2,1)} %gather_fusion) | data formatting | bytes 13762560 | tf_op jit(solution)/shard_map/jit(_take)/gather | solution.py:23
  49.0 7.1 %select_select_fusion = bf16[4,4,1,60,3584]{4,3,1,0,2:T(8,128)(2,1)} fusion(bf16[4,4,1,60,3584]{4,3,1,0,2:T(8,128)(2,1)} %gather.18, pred[4,4,60]{2,1,0:T(4,128)(4,1)S(1)} %broadcast_in_dim.61, pred[4,4,60]{2,1,0:T(4,128)(4,1)S(1)} %broadcast_in_dim.58), kind=kLoop, calls=%fused_computation.8 | loop fusion | flops 6881280 | bytes 13764480 | tf_op jit(solution)/shard_map/jit(_where)/select_n | solution.py:24
  56.1 11.2 %copy.126 = bf16[4,4,1,60,3584]{4,1,3,2,0:T(4,128)(2,1)} copy(bf16[4,4,1,60,3584]{4,3,1,0,2:T(8,128)(2,1)} %select_select_fusion) | data formatting | bytes 13762560 | tf_op jit(solution)/shard_map/jit(_where)/select_n | solution.py:24
  67.3 5.4 %all-to-all-start = ((bf16[4,4,1,60,3584]{4,1,3,2,0:T(4,128)(2,1)}), bf16[4,4,1,60,3584]{4,1,3,2,0:T(4,128)(2,1)}, u32[]{:S(2)}, u32[]{:S(2)}) async-start(bf16[4,4,1,60,3584]{4,1,3,2,0:T(4,128)(2,1)} %copy.126), calls=%async_computation | async-start | bytes 13762560 | tf_op jit(solution)/shard_map/all_to_all | solution.py:43
  72.6 0.3 reduce-scatter.4.cloned.1.call-start
  72.9 3.7 copy.123
  76.6 0.1 reshape.139
  76.7 0.1 copy.135
  76.8 146.7 %all-to-all-done = bf16[4,4,1,60,3584]{4,1,3,2,0:T(4,128)(2,1)} async-done(((bf16[4,4,1,60,3584]{4,1,3,2,0:T(4,128)(2,1)}), bf16[4,4,1,60,3584]{4,1,3,2,0:T(4,128)(2,1)}, u32[]{:S(2)}, u32[]{:S(2)}) %all-to-all-start) | async-done | bytes 6881312 | tf_op jit(solution)/shard_map/all_to_all | solution.py:43
  223.5 9.7 %multiply_convert_fusion = bf16[4,240,3584]{2,0,1:T(4,128)(2,1)} fusion(f32[4,240]{0,1:T(8,128)S(1)} %copy.135, bf16[4,4,1,60,3584]{4,1,3,2,0:T(4,128)(2,1)} %all-to-all-done), kind=kLoop, calls=%fused_computation.7 | loop fusion | flops 10321920 | bytes 13766400 | tf_op jit(solution)/shard_map/convert_element_type | solution.py:53
  233.2 15.3 %convolution_convert_fusion = bf16[4,3584,1024]{2,1,0:T(8,128)(2,1)} fusion(bf16[4,240,3584]{2,0,1:T(4,128)(2,1)} %multiply_convert_fusion, bf16[4,240,1024]{2,0,1:T(4,128)(2,1)S(1)} %bitcast.43), kind=kOutput, calls=%fused_computation.6 | convolution fusion | flops 7061110784 | bytes 38207488 | tf_op jit(solution)/shard_map/erh,erd->hed/dot_general | solution.py:54
  248.6 35.3 %copy.142 = bf16[1024,14336]{1,0:T(8,128)(2,1)} copy(bf16[1024,14336]{0,1:T(8,128)(2,1)} %bitcast.41) | data formatting | bytes 58720256
  284.0 21.5 %multiply_convert_fusion.1 = (bf16[4,240,1024]{2,1,0:T(8,128)(2,1)}, f32[4,240]{1,0:T(4,128)S(1)}) fusion(f32[4,240]{1,0:T(4,128)S(1)} %reshape.139, bf16[4,240,1024]{2,0,1:T(4,128)(2,1)S(1)} %bitcast.44, bf16[1024,4,3584]{2,0,1:T(8,128)(2,1)} %all-gather.2.cloned.1.call-done, bf16[4,240,3584]{2,0,1:T(4,128)(2,1)} %bitcast.5), kind=kOutput, calls=%fused_computation.12 | convolution fusion | flops 7051344896 | bytes 40181248 | tf_op jit(solution)/shard_map/erd,hed->erh/dot_general | solution.py:50
  305.4 0.1 mul.49
  305.5 0.7 reshape.201
  306.2 3.5 all-to-all-start.1
  309.7 3.6 copy.134
  313.3 2.8 copy.138
  316.1 0.5 broadcast.118
  316.6 0.7 reduce
  317.3 0.1 reshape.202
  317.4 0.1 reshape.135
  317.5 2.3 gather_fusion.1
  319.8 0.1 gather.20
  320.0 0.6 subtract_divide_fusion
  320.6 141.3 %reduce-scatter.4.cloned.1.call-done = bf16[128,14336]{1,0:T(8,128)(2,1)} async-done(((bf16[1024,14336]{1,0:T(8,128)(2,1)}), bf16[128,14336]{1,0:T(8,128)(2,1)}) %reduce-scatter.4.cloned.1.call-update) | async-done | bytes 3670032
  461.9 6.1 %copy.143 = bf16[128,14336]{0,1:T(8,128)(2,1)} copy(bf16[128,14336]{1,0:T(8,128)(2,1)} %reduce-scatter.4.cloned.1.call-done) | data formatting | bytes 7340032
  468.0 7.8 %copy.139 = f32[128,4,3584]{2,1,0:T(4,128)} copy(bf16[128,4,3584]{0,2,1:T(8,128)(2,1)} %bitcast.42) | data formatting | bytes 11010048
  (36 shorter events, 0.4 us)
Async XLA Ops:
  7.2 26.1 %copy-start = (bf16[128,3584]{1,0:T(8,128)(2,1)S(1)}, bf16[128,3584]{1,0:T(8,128)(2,1)}, u32[]{:S(2)}) copy-start(bf16[128,3584]{1,0:T(8,128)(2,1)} %param.5) | copy-start | bytes 2752516
  7.2 4.7 copy-start.3
  7.2 5.0 %copy-start.2 = (s32[128,4]{0,1:T(4,128)S(1)}, s32[128,4]{0,1:T(4,128)}, u32[]{:S(2)}) copy-start(s32[128,4]{0,1:T(4,128)} %param.6) | copy-start | bytes 6148
  7.2 276.7 %all-gather.2.cloned.1.call-start = ((), (), s32[]{:S(2)}) async-start(), calls=%async_computation.4 | async-start | bytes 33030144 | tf_op jit(solution)/shard_map/all_gather | solution.py:49
  21.5 45.8 %all-to-all-start.2 = ((bf16[4,4,1,60]{3,1,2,0:T(4,128)(2,1)}), bf16[4,4,1,60]{3,1,2,0:T(4,128)(2,1)S(1)}, u32[]{:S(2)}, u32[]{:S(2)}) async-start(bf16[4,4,1,60]{3,1,2,0:T(4,128)(2,1)} %bitcast.8), calls=%async_computation.2 | async-start | bytes 8192 | tf_op jit(solution)/shard_map/all_to_all | solution.py:44
  67.3 156.2 %all-to-all-start = ((bf16[4,4,1,60,3584]{4,1,3,2,0:T(4,128)(2,1)}), bf16[4,4,1,60,3584]{4,1,3,2,0:T(4,128)(2,1)}, u32[]{:S(2)}, u32[]{:S(2)}) async-start(bf16[4,4,1,60,3584]{4,1,3,2,0:T(4,128)(2,1)} %copy.126), calls=%async_computation | async-start | bytes 13762560 | tf_op jit(solution)/shard_map/all_to_all | solution.py:43
  72.6 389.3 %reduce-scatter.4.cloned.1.call-start = ((), (), s32[]{:S(2)}) async-start(), calls=%async_computation.5 | async-start | bytes 33030144
  306.2 9.9 %all-to-all-start.1 = ((f32[4,1,240]{2,1,0:T(1,128)}), f32[4,1,240]{2,1,0:T(1,128)S(1)}, u32[]{:S(2)}, u32[]{:S(2)}) async-start(f32[4,1,240]{2,1,0:T(1,128)} %reshape.201), calls=%async_computation.1 | async-start | bytes 8192 | tf_op jit(solution)/shard_map/all_to_all | solution.py:58
  461.9 13.9 %copy-start.1 = (bf16[128,3584]{1,0:T(8,128)(2,1)S(1)}, bf16[128,3584]{1,0:T(8,128)(2,1)}, u32[]{:S(2)}) copy-start(bf16[128,3584]{1,0:T(8,128)(2,1)} %param.5) | copy-start | bytes 2752516
Sparse Core Ops, SparseCore 0:
  12.0 145.7 all-gather.1
  284.0 177.8 reduce-scatter.3
where the time goes:
time: 484 us; the launch traced here: 483 us
  waiting for transfers between devices  288 us (60%)
  local copies, waits for them, and re-layouts  110 us (23%)
  matrix products  36.8 us (8%)
  other arithmetic  18.4 us (4%)
  starting transfers between devices  15.5 us (3%)
  between operations  14.3 us (3%)
    all_to_all x1, waiting for transfers between devices, on_device(): lax.all_to_all(outgoing, 'exp', split_axis=0, concat_axis=2, tiled=True)  147 us
    unnamed x3, waiting for transfers between devices  141 us
    unnamed x16, local copies, waits for them, and re-layouts  61.1 us
    dot_general x1, matrix products, on_device(): jnp.einsum('erd,hed->erh', received, gathered, preferred_element_type=jnp...  21.5 us
    gather x2, local copies, waits for them, and re-layouts, pack_routes(): fetched = jnp.take(grad_rows, source, axis=0)  15.8 us
    dot_general x1, matrix products, on_device(): jnp.einsum('erh,erd->hed', hidden, scaled, preferred_element_type=jnp.flo...  15.3 us
    select_n x1, local copies, waits for them, and re-layouts, pack_routes(): packed = jnp.where(filled[:, None] > 0, fetched, jnp.zeros_like(fetched))  11.2 us
    convert_element_type x1, other arithmetic, on_device(): (row_scale[:, :, None] * received.astype(jnp.float32)).astype(jnp.bfloat16)  9.75 us
  transfers between devices with their start and end apart: 5, of which 2 were waited for; matrix products, arithmetic and copies ran while one was open for 30% of the time, Pallas kernels for 0%

commit v1 on v0

--- a/solution.py
+++ b/solution.py
@@ -1,6 +1,9 @@
+import functools
 import jax
 import jax.numpy as jnp
 from jax import lax
+from jax.experimental import pallas as pl
+from jax.experimental.pallas import tpu as pltpu
 from jax.sharding import PartitionSpec as P
 
 ROUTE_SCALE = 2.5
@@ -25,7 +28,7 @@
     return (packed, weights, placed)
 
 
-def on_device(grad_out, routes, affinity, saved_hidden, down_proj):
+def on_device_weights(grad_out, routes, affinity, saved_hidden, down_proj):
     exp_devices = lax.axis_size("exp")
     local_experts = down_proj.shape[1]
     expert_count = exp_devices * local_experts
@@ -67,6 +70,221 @@
     return (affinity_grad, hidden_grad.reshape(saved_hidden.shape), down_grad)
 
 
+SLOT_PAD = 64
+F32 = jnp.float32
+BF16 = jnp.bfloat16
+
+
+def nt_dot(a, b):
+    return lax.dot_general(a, b, (((1,), (1,)), ((), ())), preferred_element_type=F32)
+
+
+def tn_dot(a, b):
+    return lax.dot_general(a, b, (((0,), (0,)), ((), ())), preferred_element_type=F32)
+
+
+def project_kernel(
+    top_k, idx_ref, rows_ref, weight_ref, hidden_ref, meta_ref, grad_ref, combine_ref, scatter_ref, terms
+):
+    reps, experts, slots, block = grad_ref.shape
+    tokens = rows_ref.shape[0] // reps
+    base = idx_ref[1].astype(F32)
+    projected = nt_dot(rows_ref[...], weight_ref[...])
+    earlier = (
+        lax.broadcasted_iota(jnp.int32, (tokens, tokens), 0)
+        < lax.broadcasted_iota(jnp.int32, (tokens, tokens), 1)
+    ).astype(BF16)
+    expert_ids = lax.broadcasted_iota(jnp.int32, (8, tokens), 0).astype(F32) + base
+    slot_ids = lax.broadcasted_iota(jnp.int32, (slots, tokens), 0).astype(F32)
+    ones = jnp.ones((8, block), BF16)
+    for rep in range(reps):
+        meta = meta_ref[rep, 0]
+        named = jnp.zeros((8, tokens), F32)
+        scale = jnp.zeros((8, tokens), F32)
+        for k in range(top_k):
+            hit = meta[k : k + 1, :] == expert_ids
+            named = jnp.where(hit, 1.0, named)
+            scale = jnp.where(hit, meta[top_k + k : top_k + k + 1, :], scale)
+        before = jnp.dot(named.astype(BF16), earlier, preferred_element_type=F32)
+        slot = jnp.where(named > 0, before, -1.0)
+        scale_columns = jnp.transpose(scale)
+        span = slice(rep * tokens, (rep + 1) * tokens)
+        for e in range(experts):
+            pick = (slot[e : e + 1, :] == slot_ids).astype(BF16)
+            column = scale_columns[:, e : e + 1]
+            own = projected[span, e * block : (e + 1) * block]
+            hidden = tn_dot(pick, hidden_ref[rep, e, 0])
+            grad_ref[rep, e] = jnp.dot(
+                pick, (column * own).astype(BF16), preferred_element_type=F32
+            ).astype(BF16)
+            product = hidden * own
+            high = product.astype(BF16)
+            low = (product - high.astype(F32)).astype(BF16)
+            combine_ref[rep, e : e + 1] = (nt_dot(ones, high) + nt_dot(ones, low))[0:1]
+            terms[span, e * block : (e + 1) * block] = (column * hidden).astype(BF16)
+    width = experts * block
+    row = lax.broadcasted_iota(jnp.int32, (width, width), 0)
+    col = lax.broadcasted_iota(jnp.int32, (width, width), 1)
+    order = (col == lax.rem(row, experts) * block + lax.div(row, experts)).astype(BF16)
+    scatter_ref[...] = nt_dot(order, terms[...]).astype(BF16)
+
+
+def project(index, rows, weight, hidden, meta, top_k, step_reps):
+    reps, experts, sources, slots, block = hidden.shape
+    tokens = rows.shape[0] // reps
+    width = rows.shape[1]
+    count = step_reps * tokens
+    return pl.pallas_call(
+        functools.partial(project_kernel, top_k),
+        grid_spec=pltpu.PrefetchScalarGridSpec(
+            num_scalar_prefetch=1,
+            grid=(reps // step_reps,),
+            in_specs=[
+                pl.BlockSpec((count, width), lambda i, idx: (i, 0)),
+                pl.BlockSpec((experts * block, width), lambda i, idx: (0, 0)),
+                pl.BlockSpec((step_reps, experts, 1, slots, block), lambda i, idx: (i, 0, idx[0], 0, 0)),
+                pl.BlockSpec((step_reps, 1, 2 * top_k, tokens), lambda i, idx: (i, idx[0], 0, 0)),
+            ],
+            out_specs=[
+                pl.BlockSpec((step_reps, experts, slots, block), lambda i, idx: (i, 0, 0, 0)),
+                pl.BlockSpec((step_reps, experts, tokens), lambda i, idx: (i, 0, 0)),
+                pl.BlockSpec((experts * block, count), lambda i, idx: (0, i)),
+            ],
+            scratch_shapes=[pltpu.VMEM((count, experts * block), BF16)],
+        ),
+        out_shape=[
+            jax.ShapeDtypeStruct((reps, experts, slots, block), BF16),
+            jax.ShapeDtypeStruct((reps, experts, tokens), F32),
+            jax.ShapeDtypeStruct((experts * block, reps * tokens), BF16),
+        ],
+        compiler_params=pltpu.CompilerParams(vmem_limit_bytes=40 * 2**20),
+        cost_estimate=pl.CostEstimate(
+            flops=2 * reps * tokens * width * experts * block,
+            bytes_accessed=2 * (rows.size + weight.size),
+            transcendentals=0,
+        ),
+    )(index, rows, weight, hidden, meta)
+
+
+def weight_grad_kernel(first, last, *refs):
+    if first:
+        scatter_ref, rows_ref, out_ref = refs
+        total = jnp.dot(scatter_ref[...], rows_ref[...], preferred_element_type=F32)
+    else:
+        scatter_ref, rows_ref, before_ref, out_ref = refs[:4]
+        total = before_ref[...] + jnp.dot(scatter_ref[...], rows_ref[...], preferred_element_type=F32)
+    if not last:
+        out_ref[...] = total
+        return
+    held = refs[4]
+    held[...] = total
+    experts = out_ref.shape[1]
+
+    group = 8 // experts
+
+    def move(i, carry):
+        both = held[pl.ds(pl.multiple_of(i * 8, 8), 8), :]
+        for j in range(group):
+            out_ref[i * group + j] = both[j * experts : (j + 1) * experts]
+        return carry
+
+    lax.fori_loop(0, out_ref.shape[0] // group, move, 0, unroll=4)
+
+
+def weight_grad(scatter, rows, before, last, experts, tile):
+    height, count = scatter.shape
+    width = rows.shape[1]
+    block = height // experts
+    first = before is None
+    in_specs = [
+        pl.BlockSpec((height, count), lambda i: (0, 0)),
+        pl.BlockSpec((count, tile), lambda i: (0, i)),
+    ]
+    args = [scatter, rows]
+    if not first:
+        in_specs.append(pl.BlockSpec((height, tile), lambda i: (0, i)))
+        args.append(before)
+    if last:
+        out_spec = pl.BlockSpec((block, experts, tile), lambda i: (0, 0, i))
+        out_shape = jax.ShapeDtypeStruct((block, experts, width), F32)
+        scratch = [pltpu.VMEM((height, tile), F32)]
+    else:
+        out_spec = pl.BlockSpec((height, tile), lambda i: (0, i))
+        out_shape = jax.ShapeDtypeStruct((height, width), F32)
+        scratch = []
+    return pl.pallas_call(
+        functools.partial(weight_grad_kernel, first, last),
+        grid=(width // tile,),
+        in_specs=in_specs,
+        out_specs=out_spec,
+        out_shape=out_shape,
+        scratch_shapes=scratch,
+        input_output_aliases={2: 0} if not first and not last else {},
+        compiler_params=pltpu.CompilerParams(vmem_limit_bytes=40 * 2**20),
+        cost_estimate=pl.CostEstimate(
+            flops=2 * height * count * width,
+            bytes_accessed=2 * (scatter.size + rows.size) + 8 * height * width,
+            transcendentals=0,
+        ),
+    )(*args)
+
+
+def on_device_tokens(grad_out, routes, affinity, saved_hidden, down_proj):
+    reps, sources = lax.axis_size("rep"), lax.axis_size("exp")
+    block, experts, width = down_proj.shape
+    tokens, top_k = routes.shape
+    most, hidden_units = saved_hidden.shape[3:]
+    me = lax.axis_index("exp")
+    totals = jnp.sum(affinity, axis=-1, keepdims=True)
+    shares = affinity / totals
+    route_weight = (ROUTE_SCALE * shares).astype(BF16).astype(F32)
+    meta = jnp.concatenate([routes.astype(F32).T, route_weight.T], axis=0)
+    meta = lax.all_gather(meta, ("rep", "exp"), axis=0).reshape(reps, sources, 2 * top_k, tokens)
+    weight = jnp.transpose(down_proj, (1, 0, 2)).reshape(experts * block, width)
+    pieces = saved_hidden.reshape(experts, sources, most, reps, block)
+    pieces = jnp.transpose(pieces, (3, 0, 1, 2, 4))
+    pieces = jnp.pad(pieces, ((0, 0), (0, 0), (0, 0), (0, SLOT_PAD - most), (0, 0)))
+    hidden = lax.all_to_all(pieces, "rep", split_axis=0, concat_axis=0, tiled=True)
+    ring = [(i, (i + 1) % sources) for i in range(sources)]
+    carried = grad_out
+    total = None
+    grads, combines = [], []
+    for step in range(sources):
+        rows = lax.all_gather(carried, "rep", axis=0, tiled=True)
+        if step < sources - 1:
+            carried = lax.ppermute(carried, "exp", ring)
+        source = lax.rem(me - step + sources, sources)
+        index = jnp.stack([source, me * experts]).astype(jnp.int32)
+        grad, combine, scatter = project(index, rows, weight, hidden, meta, top_k, 2)
+        total = weight_grad(scatter, rows, total, step == sources - 1, experts, 512)
+        grads.append(lax.all_to_all(grad, "rep", split_axis=0, concat_axis=0, tiled=True))
+        combines.append(combine)
+    at_source = lax.rem(me - jnp.arange(sources) + sources, sources)
+    grads = jnp.take(jnp.stack(grads), at_source, axis=0)[:, :, :, :most]
+    hidden_grad = jnp.transpose(grads, (2, 0, 3, 1, 4)).reshape(saved_hidden.shape)
+    combine = jnp.take(jnp.stack(combines, axis=1), at_source, axis=1)
+    combine = combine.reshape(reps * sources, experts, tokens)
+    combine = lax.all_to_all(combine, ("rep", "exp"), split_axis=0, concat_axis=0, tiled=True)
+    combine = jnp.sum(combine.reshape(reps, sources * experts, tokens), axis=0)
+    expert_ids = jnp.arange(sources * experts, dtype=routes.dtype)
+    named = routes.T[:, None, :] == expert_ids[None, :, None]
+    route_grad = ROUTE_SCALE * jnp.sum(jnp.where(named, combine[None], 0.0), axis=1).T
+    affinity_grad = (route_grad - jnp.sum(route_grad * shares, axis=-1, keepdims=True)) / totals
+    return (affinity_grad, hidden_grad, total)
+
+
+def on_device(grad_out, routes, affinity, saved_hidden, down_proj):
+    reps, sources = lax.axis_size("rep"), lax.axis_size("exp")
+    block, experts, width = down_proj.shape
+    tokens = grad_out.shape[0]
+    most = saved_hidden.shape[3]
+    fits = block % 128 == 0 and tokens % 128 == 0 and width % 512 == 0 and 8 % experts == 0
+    fits = fits and most <= SLOT_PAD and reps % 2 == 0 and routes.shape[1] == 4
+    if fits and reps * sources * tokens <= 2 * reps * block * experts:
+        return on_device_tokens(grad_out, routes, affinity, saved_hidden, down_proj)
+    return on_device_weights(grad_out, routes, affinity, saved_hidden, down_proj)
+
+
 def solution(mesh):
     return jax.shard_map(
         on_device,

time: 484 us -> 321 us (0.66)
  waiting for transfers between devices: 288 us -> 78.6 us
  Pallas kernels: 0 us -> 86.9 us
  local copies, waits for them, and re-layouts: 110 us -> 41.1 us
  blocking collectives: 0 us -> 67.2 us
  matrix products: 36.8 us -> 0 us
  other arithmetic: 18.4 us -> 4.58 us
  starting transfers between devices: 15.5 us -> 26.6 us
    unnamed x3 -> x4, waiting for transfers between devices: 141 us -> 0.73 us
    all_to_all x3 -> x6, waiting for transfers between devices: 147 us -> 9.11 us  [the longest x4 9.1 us: on_device_tokens(): lax.all_to_all(grad, 'rep', split_axis=0, concat_axis=0, tiled=True)]
    pallas_call x0 -> x8, Pallas kernels: none -> 86.9 us  [the longest x4 51.7 us: project(): pl.pallas_call(functools.partial(project_kernel, top_k), grid_spec=pltpu....]
    ppermute x0 -> x3, waiting for transfers between devices: none -> 68.7 us  [on_device_tokens(): carried = lax.ppermute(carried, 'exp', ring)]
    all_gather x0 -> x1, blocking collectives: none -> 67.2 us  [on_device_tokens(): lax.all_gather(meta, ('rep', 'exp'), axis=0)]
    dot_general x2 -> x0, matrix products: 36.8 us -> none  [the longest x1 21.5 us: on_device(): jnp.einsum('erd,hed->erh', received, gathered, preferred_element_type=jnp...]
    unnamed x16 -> x32, local copies, waits for them, and re-layouts: 61.1 us -> 24.4 us
    gather x10 -> x3, local copies, waits for them, and re-layouts: 22.4 us -> 2.8 us  [the longest x1 2.16 us: on_device_tokens(): grads = jnp.take(jnp.stack(grads), at_source, axis=0)[:, :, :, :most]]
  transfers between devices with their start and end apart: 5 -> 13, of which waited for: 2 -> 4; matrix products, arithmetic and copies ran while one was open for 30% -> 4% of each run, Pallas kernels for 0% -> 27%
where the time goes in v1:
time: 321 us; the launch traced here: 319 us
  Pallas kernels  86.9 us (27%)
  waiting for transfers between devices  78.6 us (24%)
  blocking collectives  67.2 us (21%)
  local copies, waits for them, and re-layouts  41.1 us (13%)
  starting transfers between devices  26.6 us (8%)
  between operations  14.1 us (4%)
  other arithmetic  4.58 us (1%)
    ppermute x3, waiting for transfers between devices, on_device_tokens(): carried = lax.ppermute(carried, 'exp', ring)  68.7 us
    all_gather x1, blocking collectives, on_device_tokens(): lax.all_gather(meta, ('rep', 'exp'), axis=0)  67.2 us
    pallas_call x4, Pallas kernels, project(): pl.pallas_call(functools.partial(project_kernel, top_k), grid_spec=pltpu....  51.7 us
    pallas_call x4, Pallas kernels, weight_grad(): pl.pallas_call(functools.partial(weight_grad_kernel, first, last), grid=(...  35.2 us
    unnamed x32, local copies, waits for them, and re-layouts  24.4 us
    all_to_all x4, starting transfers between devices, on_device_tokens(): lax.all_to_all(grad, 'rep', split_axis=0, concat_axis=0, tiled=True)  16.6 us
    all_to_all x4, waiting for transfers between devices, on_device_tokens(): lax.all_to_all(grad, 'rep', split_axis=0, concat_axis=0, tiled=True)  9.1 us
  transfers between devices with their start and end apart: 13, of which 4 were waited for; matrix products, arithmetic and copies ran while one was open for 4% of the time, Pallas kernels for 27%

profile of v1, /device:TPU:0, one launch (start us, length us, event | category | flops | bytes accessed | tf_op | source)
XLA Modules:
  0.0 319.1 jit_solution(1420251566676278596)
XLA Ops:
  7.2 0.7 all-gather.6.cloned.1.call-update
  7.9 3.1 collective-permute-start
  11.0 22.6 %collective-permute-done = bf16[128,3584]{1,0:T(8,128)(2,1)S(1)} collective-permute-done((bf16[128,3584]{1,0:T(8,128)(2,1)}, bf16[128,3584]{1,0:T(8,128)(2,1)S(1)}, u32[]{:S(2)}, u32[]{:S(2)}) %collective-permute-start) | collective-permute-done | bytes 917536 | tf_op jit(solution)/shard_map/ppermute | solution.py:255
  33.6 0.9 copy-done.13
  34.7 23.5 %collective-permute-done.1 = bf16[128,3584]{1,0:T(8,128)(2,1)S(1)} collective-permute-done((bf16[128,3584]{1,0:T(8,128)(2,1)}, bf16[128,3584]{1,0:T(8,128)(2,1)S(1)}, u32[]{:S(2)}, u32[]{:S(2)}) %collective-permute-start.1) | collective-permute-done | bytes 917536 | tf_op jit(solution)/shard_map/ppermute | solution.py:255
  58.2 0.9 copy-done.12
  59.3 22.6 %collective-permute-done.2 = bf16[128,3584]{1,0:T(8,128)(2,1)S(1)} collective-permute-done((bf16[128,3584]{1,0:T(8,128)(2,1)}, bf16[128,3584]{1,0:T(8,128)(2,1)S(1)}, u32[]{:S(2)}, u32[]{:S(2)}) %collective-permute-start.2) | collective-permute-done | bytes 917536 | tf_op jit(solution)/shard_map/ppermute | solution.py:255
  81.9 0.9 copy-done.11
  82.8 3.2 reshape.71
  86.0 0.8 copy.31
  86.8 1.6 pad.4
  88.4 3.6 %all-to-all-start = ((bf16[8,4,4,64,128]{4,3,2,1,0:T(8,128)(2,1)}), bf16[8,4,4,64,128]{4,3,2,1,0:T(8,128)(2,1)S(1)}, u32[]{:S(2)}, u32[]{:S(2)}) async-start(bf16[8,4,4,64,128]{4,3,2,1,0:T(8,128)(2,1)} %pad.4), calls=%async_computation | async-start | bytes 4194304 | tf_op jit(solution)/shard_map/all_to_all | solution.py:247
  92.0 4.4 %copy.25 = bf16[4,128,3584]{2,1,0:T(8,128)(2,1)} copy(bf16[4,128,3584]{2,0,1:T(4,128)(2,1)} %bitcast.59) | data formatting | bytes 7340032 | tf_op jit(solution)/shard_map/transpose | solution.py:243
  96.5 0.1 broadcast_in_dim.42
  96.6 67.2 %all-gather = f32[256,128]{1,0:T(8,128)S(1)} all-gather(f32[8,128]{1,0:T(8,128)S(1)} %pad_maximum_fusion.2), channel_id=2, replica_groups=mesh['rep'=8,'exp'=4] {'rep','exp'}, dimensions={0}, use_global_device_ids=true | all-gather | bytes 135168 | tf_op jit(solution)/shard_map/all_gather | solution.py:242
  163.9 0.1 pad_add_fusion.idx_ref
  164.2 2.5 copy-done.6
  166.7 12.6 %shard_map.76 = (bf16[8,4,64,128]{3,2,1,0:T(8,128)(2,1)S(1)}, f32[8,4,128]{2,1,0:T(4,128)S(1)}, bf16[512,1024]{1,0:T(8,128)(2,1)S(1)}) custom-call(s32[2]{0:T(128)S(1)} %pad_add_fusion.idx_ref, bf16[1024,3584]{1,0:T(8,128)(2,1)} %all-gather.6.cloned.1.call-done.rows_ref.refs_1_, bf16[512,3584]{1,0:T(8,128)(2,1)S(1)} %bitcast.46, ...), custom_call_target="tpu_custom_call" | custom-call | flops 3758096384 | bytes 11010048 | tf_op jit(solution)/shard_map/pallas_call | solution.py:137
  179.3 0.8 copy-done.10
  180.1 4.1 %all-to-all-start.2 = ((bf16[8,4,64,128]{3,2,1,0:T(8,128)(2,1)}), bf16[8,4,64,128]{3,2,1,0:T(8,128)(2,1)}, u32[]{:S(2)}, u32[]{:S(2)}) async-start(bf16[8,4,64,128]{3,2,1,0:T(8,128)(2,1)} %copy-done.10), calls=%async_computation.2 | async-start | bytes 1048576 | tf_op jit(solution)/shard_map/all_to_all | solution.py:260
  184.2 8.2 %shard_map.80.refs_2_ = f32[512,3584]{1,0:T(8,128)S(1)} custom-call(bf16[512,1024]{1,0:T(8,128)(2,1)S(1)} %get-tuple-element.26.refs_0_, bf16[1024,3584]{1,0:T(8,128)(2,1)} %all-gather.6.cloned.1.call-done.rows_ref.refs_1_), custom_call_target="tpu_custom_call" | custom-call | flops 3758096384 | bytes 23068672 | tf_op jit(solution)/shard_map/pallas_call | solution.py:215
  192.4 3.0 copy-done
  195.5 2.0 copy-done.7
  197.5 13.1 %shard_map.77 = (bf16[8,4,64,128]{3,2,1,0:T(8,128)(2,1)}, f32[8,4,128]{2,1,0:T(4,128)S(1)}, bf16[512,1024]{1,0:T(8,128)(2,1)S(1)}) custom-call(s32[2]{0:T(128)S(1)} %pad_add_fusion.1.idx_ref, bf16[1024,3584]{1,0:T(8,128)(2,1)} %all-gather.8.cloned.1.call-done.rows_ref.refs_1_, bf16[512,3584]{1,0:T(8,128)(2,1)S(1)} %bitcast.47, ...), custom_call_target="tpu_custom_call" | custom-call | flops 3758096384 | bytes 11010048 | tf_op jit(solution)/shard_map/pallas_call | solution.py:137
  210.6 8.1 %shard_map.81.refs_2_ = f32[512,3584]{1,0:T(8,128)S(1)} custom-call(bf16[512,1024]{1,0:T(8,128)(2,1)S(1)} %get-tuple-element.25.refs_0_, bf16[1024,3584]{1,0:T(8,128)(2,1)} %all-gather.8.cloned.1.call-done.rows_ref.refs_1_, f32[512,3584]{1,0:T(8,128)S(1)} %copy-done.1), custom_call_target="tpu_custom_call", output_to_operand_aliasing={{}: (2, {})} | custom-call | flops 3758096384 | bytes 23068672 | tf_op jit(solution)/shard_map/pallas_call | solution.py:215
  218.7 3.0 copy-done.2
  221.7 4.1 %all-to-all-start.3 = ((bf16[8,4,64,128]{3,2,1,0:T(8,128)(2,1)}), bf16[8,4,64,128]{3,2,1,0:T(8,128)(2,1)}, u32[]{:S(2)}, u32[]{:S(2)}) async-start(bf16[8,4,64,128]{3,2,1,0:T(8,128)(2,1)} %get-tuple-element.20), calls=%async_computation.3 | async-start | bytes 1048576 | tf_op jit(solution)/shard_map/all_to_all | solution.py:260
  225.9 2.1 copy-done.8
  228.0 13.2 %shard_map.78 = (bf16[8,4,64,128]{3,2,1,0:T(8,128)(2,1)}, f32[8,4,128]{2,1,0:T(4,128)S(1)}, bf16[512,1024]{1,0:T(8,128)(2,1)S(1)}) custom-call(s32[2]{0:T(128)S(1)} %pad_add_fusion.2.idx_ref, bf16[1024,3584]{1,0:T(8,128)(2,1)} %all-gather.10.cloned.1.call-done.rows_ref.refs_1_, bf16[512,3584]{1,0:T(8,128)(2,1)S(1)} %bitcast.48, ...), custom_call_target="tpu_custom_call" | custom-call | flops 3758096384 | bytes 11010048 | tf_op jit(solution)/shard_map/pallas_call | solution.py:137
  241.2 8.1 %shard_map.82.refs_2_ = f32[512,3584]{1,0:T(8,128)S(1)} custom-call(bf16[512,1024]{1,0:T(8,128)(2,1)S(1)} %get-tuple-element.24.refs_0_, bf16[1024,3584]{1,0:T(8,128)(2,1)} %all-gather.10.cloned.1.call-done.rows_ref.refs_1_, f32[512,3584]{1,0:T(8,128)S(1)} %copy-done.3), custom_call_target="tpu_custom_call", output_to_operand_aliasing={{}: (2, {})} | custom-call | flops 3758096384 | bytes 23068672 | tf_op jit(solution)/shard_map/pallas_call | solution.py:215
  249.3 3.0 copy-done.4
  252.3 4.3 %all-to-all-start.4 = ((bf16[8,4,64,128]{3,2,1,0:T(8,128)(2,1)}), bf16[8,4,64,128]{3,2,1,0:T(8,128)(2,1)}, u32[]{:S(2)}, u32[]{:S(2)}) async-start(bf16[8,4,64,128]{3,2,1,0:T(8,128)(2,1)} %get-tuple-element.21), calls=%async_computation.4 | async-start | bytes 1048576 | tf_op jit(solution)/shard_map/all_to_all | solution.py:260
  256.7 2.0 copy-done.9
  258.7 12.8 %shard_map.79 = (bf16[8,4,64,128]{3,2,1,0:T(8,128)(2,1)}, f32[8,4,128]{2,1,0:T(4,128)S(1)}, bf16[512,1024]{1,0:T(8,128)(2,1)S(1)}) custom-call(s32[2]{0:T(128)S(1)} %pad_add_fusion.3.idx_ref, bf16[1024,3584]{1,0:T(8,128)(2,1)} %all-gather.12.cloned.1.call-done.rows_ref.refs_1_, bf16[512,3584]{1,0:T(8,128)(2,1)S(1)} %bitcast.49, ...), custom_call_target="tpu_custom_call" | custom-call | flops 3758096384 | bytes 11010048 | tf_op jit(solution)/shard_map/pallas_call | solution.py:137
  271.6 0.6 gather_fusion
  272.2 0.1 broadcast_select_fusion
  272.3 0.7 copy.28
  273.0 3.0 all-to-all-start.1
  276.1 3.1 copy-done.5
  279.1 10.8 %shard_map.83 = f32[128,4,3584]{2,1,0:T(4,128)} custom-call(bf16[512,1024]{1,0:T(8,128)(2,1)S(1)} %get-tuple-element.23.refs_0_, bf16[1024,3584]{1,0:T(8,128)(2,1)S(1)} %copy-done.5, f32[512,3584]{1,0:T(8,128)} %copy-done.4), custom_call_target="tpu_custom_call" | custom-call | flops 3758096384 | bytes 23068672 | tf_op jit(solution)/shard_map/pallas_call | solution.py:215
  289.9 4.0 %all-to-all-start.5 = ((bf16[8,4,64,128]{3,2,1,0:T(8,128)(2,1)}), bf16[8,4,64,128]{3,2,1,0:T(8,128)(2,1)S(1)}, u32[]{:S(2)}, u32[]{:S(2)}) async-start(bf16[8,4,64,128]{3,2,1,0:T(8,128)(2,1)} %get-tuple-element.22), calls=%async_computation.5 | async-start | bytes 1048576 | tf_op jit(solution)/shard_map/all_to_all | solution.py:260
  293.9 0.6 fusion.2
  294.5 9.1 %all-to-all-done.5 = bf16[8,4,64,128]{3,2,1,0:T(8,128)(2,1)S(1)} async-done(((bf16[8,4,64,128]{3,2,1,0:T(8,128)(2,1)}), bf16[8,4,64,128]{3,2,1,0:T(8,128)(2,1)S(1)}, u32[]{:S(2)}, u32[]{:S(2)}) %all-to-all-start.5) | async-done | bytes 524320 | tf_op jit(solution)/shard_map/all_to_all | solution.py:260
  303.6 1.6 pad_maximum_fusion
  305.2 2.2 gather_fusion.1
  307.4 1.9 fusion
  309.3 1.3 copy.29
  310.5 2.0 reshape.74
  (54 shorter events, 0.9 us)
Async XLA Ops:
  7.2 157.0 %all-gather.6.cloned.1.call-start = ((), (), s32[]{:S(2)}) async-start(), calls=%async_computation.6 | async-start | bytes 8257536 | tf_op jit(solution)/shard_map/all_gather | solution.py:253
  7.9 187.6 %all-gather.8.cloned.1.call-start = ((), (), s32[]{:S(2)}) async-start(), calls=%async_computation.7 | async-start | bytes 8257536 | tf_op jit(solution)/shard_map/all_gather | solution.py:253
  7.9 25.7 %collective-permute-start = (bf16[128,3584]{1,0:T(8,128)(2,1)}, bf16[128,3584]{1,0:T(8,128)(2,1)S(1)}, u32[]{:S(2)}, u32[]{:S(2)}) collective-permute-start(bf16[128,3584]{1,0:T(8,128)(2,1)} %param.5), channel_id=1, source_target_pairs={{0,1},{1,2},{2,3},{3,0},{4,5},{5,6},{6,7},{7,4},{8,9},{9,10},{10,1... | collective-permute-start | bytes 2752520 | tf_op jit(solution)/shard_map/ppermute | solution.py:255
  33.6 0.9 copy-start.13
  34.6 191.4 %all-gather.10.cloned.1.call-start = ((), (), s32[]{:S(2)}) async-start(), calls=%async_computation.8 | async-start | bytes 8257536 | tf_op jit(solution)/shard_map/all_gather | solution.py:253
  34.6 23.6 %collective-permute-start.1 = (bf16[128,3584]{1,0:T(8,128)(2,1)}, bf16[128,3584]{1,0:T(8,128)(2,1)S(1)}, u32[]{:S(2)}, u32[]{:S(2)}) collective-permute-start(bf16[128,3584]{1,0:T(8,128)(2,1)} %copy-done.13), channel_id=1, source_target_pairs={{0,1},{1,2},{2,3},{3,0},{4,5},{5,6},{6,7},{7,4},{8,9},{9,10},{10,1... | collective-permute-start | bytes 2752520 | tf_op jit(solution)/shard_map/ppermute | solution.py:255
  58.2 0.9 copy-start.12
  59.2 197.5 %all-gather.12.cloned.1.call-start = ((), (), s32[]{:S(2)}) async-start(), calls=%async_computation.9 | async-start | bytes 8257536 | tf_op jit(solution)/shard_map/all_gather | solution.py:253
  59.2 22.7 %collective-permute-start.2 = (bf16[128,3584]{1,0:T(8,128)(2,1)}, bf16[128,3584]{1,0:T(8,128)(2,1)S(1)}, u32[]{:S(2)}, u32[]{:S(2)}) collective-permute-start(bf16[128,3584]{1,0:T(8,128)(2,1)} %copy-done.12), channel_id=1, source_target_pairs={{0,1},{1,2},{2,3},{3,0},{4,5},{5,6},{6,7},{7,4},{8,9},{9,10},{10,1... | collective-permute-start | bytes 2752520 | tf_op jit(solution)/shard_map/ppermute | solution.py:255
  81.9 0.9 copy-start.11
  88.4 75.8 %all-to-all-start = ((bf16[8,4,4,64,128]{4,3,2,1,0:T(8,128)(2,1)}), bf16[8,4,4,64,128]{4,3,2,1,0:T(8,128)(2,1)S(1)}, u32[]{:S(2)}, u32[]{:S(2)}) async-start(bf16[8,4,4,64,128]{4,3,2,1,0:T(8,128)(2,1)} %pad.4), calls=%async_computation | async-start | bytes 4194304 | tf_op jit(solution)/shard_map/all_to_all | solution.py:247
  92.0 4.6 %copy-start.14 = (f32[128,4]{0,1:T(4,128)S(1)}, f32[128,4]{0,1:T(4,128)}, u32[]{:S(2)}) copy-start(f32[128,4]{0,1:T(4,128)} %param.7) | copy-start | bytes 6148
  92.0 4.6 %copy-start.15 = (s32[128,4]{0,1:T(4,128)S(1)}, s32[128,4]{0,1:T(4,128)}, u32[]{:S(2)}) copy-start(s32[128,4]{0,1:T(4,128)} %param.6) | copy-start | bytes 6148
  164.2 2.5 copy-start.6
  179.3 0.8 copy-start.10
  180.1 41.7 %all-to-all-start.2 = ((bf16[8,4,64,128]{3,2,1,0:T(8,128)(2,1)}), bf16[8,4,64,128]{3,2,1,0:T(8,128)(2,1)}, u32[]{:S(2)}, u32[]{:S(2)}) async-start(bf16[8,4,64,128]{3,2,1,0:T(8,128)(2,1)} %copy-done.10), calls=%async_computation.2 | async-start | bytes 1048576 | tf_op jit(solution)/shard_map/all_to_all | solution.py:260
  192.4 3.1 copy-start
  195.5 2.0 copy-start.7
  197.5 13.1 %copy-start.1 = (f32[512,3584]{1,0:T(8,128)S(1)}, f32[512,3584]{1,0:T(8,128)}, u32[]{:S(2)}) copy-start(f32[512,3584]{1,0:T(8,128)} %copy-done) | copy-start | bytes 22020100
  218.7 3.1 copy-start.2
  221.7 30.6 %all-to-all-start.3 = ((bf16[8,4,64,128]{3,2,1,0:T(8,128)(2,1)}), bf16[8,4,64,128]{3,2,1,0:T(8,128)(2,1)}, u32[]{:S(2)}, u32[]{:S(2)}) async-start(bf16[8,4,64,128]{3,2,1,0:T(8,128)(2,1)} %get-tuple-element.20), calls=%async_computation.3 | async-start | bytes 1048576 | tf_op jit(solution)/shard_map/all_to_all | solution.py:260
  225.9 2.1 copy-start.8
  228.0 13.2 %copy-start.3 = (f32[512,3584]{1,0:T(8,128)S(1)}, f32[512,3584]{1,0:T(8,128)}, u32[]{:S(2)}) copy-start(f32[512,3584]{1,0:T(8,128)} %copy-done.2) | copy-start | bytes 22020100
  249.3 3.0 copy-start.4
  252.3 20.7 %all-to-all-start.4 = ((bf16[8,4,64,128]{3,2,1,0:T(8,128)(2,1)}), bf16[8,4,64,128]{3,2,1,0:T(8,128)(2,1)}, u32[]{:S(2)}, u32[]{:S(2)}) async-start(bf16[8,4,64,128]{3,2,1,0:T(8,128)(2,1)} %get-tuple-element.21), calls=%async_computation.4 | async-start | bytes 1048576 | tf_op jit(solution)/shard_map/all_to_all | solution.py:260
  256.7 2.0 copy-start.9
  273.0 16.9 %all-to-all-start.1 = ((f32[32,4,128]{2,1,0:T(4,128)}), f32[32,4,128]{2,1,0:T(4,128)S(1)}, u32[]{:S(2)}, u32[]{:S(2)}) async-start(f32[32,4,128]{2,1,0:T(4,128)} %copy.28), calls=%async_computation.1 | async-start | bytes 131072 | tf_op jit(solution)/shard_map/all_to_all | solution.py:267
  276.0 3.1 copy-start.5
  289.9 13.7 %all-to-all-start.5 = ((bf16[8,4,64,128]{3,2,1,0:T(8,128)(2,1)}), bf16[8,4,64,128]{3,2,1,0:T(8,128)(2,1)S(1)}, u32[]{:S(2)}, u32[]{:S(2)}) async-start(bf16[8,4,64,128]{3,2,1,0:T(8,128)(2,1)} %get-tuple-element.22), calls=%async_computation.5 | async-start | bytes 1048576 | tf_op jit(solution)/shard_map/all_to_all | solution.py:260
Sparse Core Ops, SparseCore 0:
  9.9 52.6 all-gather.5
  65.0 68.1 all-gather.7
  135.1 52.7 all-gather.9
  189.7 61.2 all-gather.11

commit v2 on v0

--- a/solution.py
+++ b/solution.py
@@ -1,6 +1,9 @@
+import functools
 import jax
 import jax.numpy as jnp
 from jax import lax
+from jax.experimental import pallas as pl
+from jax.experimental.pallas import tpu as pltpu
 from jax.sharding import PartitionSpec as P
 
 ROUTE_SCALE = 2.5
@@ -25,7 +28,7 @@
     return (packed, weights, placed)
 
 
-def on_device(grad_out, routes, affinity, saved_hidden, down_proj):
+def on_device_weights(grad_out, routes, affinity, saved_hidden, down_proj):
     exp_devices = lax.axis_size("exp")
     local_experts = down_proj.shape[1]
     expert_count = exp_devices * local_experts
@@ -67,6 +70,351 @@
     return (affinity_grad, hidden_grad.reshape(saved_hidden.shape), down_grad)
 
 
+SLOT_PAD = 64
+F32 = jnp.float32
+BF16 = jnp.bfloat16
+VMEM_BYTES = 40 * 2**20
+
+
+def nt_dot(a, b):
+    return lax.dot_general(a, b, (((1,), (1,)), ((), ())), preferred_element_type=F32)
+
+
+def tn_dot(a, b):
+    return lax.dot_general(a, b, (((0,), (0,)), ((), ())), preferred_element_type=F32)
+
+
+def project_kernel(top_k, sizes, idx_ref, *refs):
+    parts = len(sizes)
+    pieces, (weight_ref,) = refs[:parts], refs[parts : parts + 1]
+    hidden_refs = refs[parts + 1 : parts + 5]
+    grad_refs = refs[parts + 5 : parts + 9]
+    scatter_ref, rows_out, rows, sems, out_sem = refs[parts + 9 :]
+    e = pl.program_id(0)
+    slots, pair = grad_refs[0].shape[1:]
+    tokens = rows.shape[0] // 4
+    spare = slots - 8
+    store = pltpu.make_async_copy(rows, rows_out, out_sem)
+
+    @pl.when(e == 0)
+    def _():
+        copies, at = [], 0
+        for i, size in enumerate(sizes):
+            copies.append(pltpu.make_async_copy(pieces[i], rows.at[at : at + size], sems.at[i]))
+            at += size
+        for copy in copies:
+            copy.start()
+        for copy in copies:
+            copy.wait()
+        store.start()
+
+    projected = nt_dot(weight_ref[...], rows[...])
+    earlier = (
+        lax.broadcasted_iota(jnp.int32, (tokens, tokens), 0)
+        < lax.broadcasted_iota(jnp.int32, (tokens, tokens), 1)
+    ).astype(BF16)
+    slot_ids = lax.broadcasted_iota(jnp.int32, (slots, tokens), 0).astype(F32)
+    slot_rows = lax.broadcasted_iota(jnp.int32, (slots, pair), 0)
+    expert = (idx_ref[1] + e).astype(F32)
+    for m in range(4):
+        held = hidden_refs[m][0, 0]
+        meta = held[spare:].astype(F32)[8 - top_k :]
+        named = jnp.zeros((1, tokens), F32)
+        scale = jnp.zeros((1, tokens), F32)
+        for k in range(top_k):
+            hit = meta[k : k + 1, :tokens] == expert
+            named = jnp.where(hit, 1.0, named)
+            scale = jnp.where(hit, meta[k : k + 1, tokens:], scale)
+        before = jnp.dot(
+            jnp.broadcast_to(named, (8, tokens)).astype(BF16), earlier, preferred_element_type=F32
+        )[0:1]
+        slot = jnp.where(named > 0, before, -1.0)
+        pick = (slot == slot_ids).astype(BF16)
+        own = projected[:, m * tokens : (m + 1) * tokens]
+        hidden = tn_dot(held, pick)
+        grad = nt_dot(pick, (scale * own).astype(BF16))
+        combine = jnp.sum(hidden * own, axis=0, keepdims=True)
+        high = combine.astype(BF16).astype(F32)
+        partial = jnp.concatenate([high, combine - high], axis=1)
+        grad_refs[m][0] = jnp.where(slot_rows == slots - top_k, partial, grad).astype(BF16)
+        scatter = (scale * hidden).astype(BF16)
+        for half in range(2):
+            scatter_ref[half, :, m * tokens : (m + 1) * tokens] = scatter[
+                half * (pair // 2) : (half + 1) * (pair // 2)
+            ]
+
+    @pl.when(e == pl.num_programs(0) - 1)
+    def _():
+        store.wait()
+
+
+def project(index, pieces, weight, hidden, top_k):
+    experts, sources, slots, pair = hidden[0].shape
+    width = weight.shape[1]
+    sizes = [p.shape[0] for p in pieces]
+    count = sum(sizes)
+    block = pair // 2
+    return pl.pallas_call(
+        functools.partial(project_kernel, top_k, sizes),
+        grid_spec=pltpu.PrefetchScalarGridSpec(
+            num_scalar_prefetch=1,
+            grid=(experts,),
+            in_specs=[pl.BlockSpec(memory_space=pl.ANY)] * len(sizes)
+            + [pl.BlockSpec((pair, width), lambda e, idx: (e, 0))]
+            + [pl.BlockSpec((1, 1, slots, pair), lambda e, idx: (e, idx[0], 0, 0))] * 4,
+            out_specs=[pl.BlockSpec((1, slots, pair), lambda e, idx: (e, 0, 0))] * 4
+            + [
+                pl.BlockSpec((2, block, count), lambda e, idx: (0, e, 0)),
+                pl.BlockSpec(memory_space=pl.ANY),
+            ],
+            scratch_shapes=[
+                pltpu.VMEM((count, width), BF16),
+                pltpu.SemaphoreType.DMA((len(sizes),)),
+                pltpu.SemaphoreType.DMA,
+            ],
+        ),
+        out_shape=[jax.ShapeDtypeStruct((experts, slots, pair), BF16)] * 4
+        + [
+            jax.ShapeDtypeStruct((2, experts * block, count), BF16),
+            jax.ShapeDtypeStruct((count, width), BF16),
+        ],
+        compiler_params=pltpu.CompilerParams(vmem_limit_bytes=VMEM_BYTES),
+        cost_estimate=pl.CostEstimate(
+            flops=4 * count * width * experts * pair,
+            bytes_accessed=2 * (2 * count * width + weight.size),
+            transcendentals=0,
+        ),
+    )(index, *pieces, weight, *hidden)
+
+
+def early_grad_kernel(terms, *refs):
+    out_ref = refs[-1]
+    for half in range(2):
+        total = jnp.dot(refs[0][half], refs[terms][...], preferred_element_type=F32)
+        for i in range(1, terms):
+            total += jnp.dot(refs[i][half], refs[terms + i][...], preferred_element_type=F32)
+        out_ref[half] = total
+
+
+def early_grad(scatters, rows, tile):
+    _, height, count = scatters[0].shape
+    width = rows[0].shape[1]
+    terms = len(rows)
+    return pl.pallas_call(
+        functools.partial(early_grad_kernel, terms),
+        grid=(width // tile,),
+        in_specs=[pl.BlockSpec((2, height, count), lambda i: (0, 0, 0))] * terms
+        + [pl.BlockSpec((count, tile), lambda i: (0, i))] * terms,
+        out_specs=pl.BlockSpec((2, height, tile), lambda i: (0, 0, i)),
+        out_shape=jax.ShapeDtypeStruct((2, height, width), F32),
+        compiler_params=pltpu.CompilerParams(vmem_limit_bytes=VMEM_BYTES),
+        cost_estimate=pl.CostEstimate(
+            flops=4 * height * count * width * terms,
+            bytes_accessed=2 * terms * (rows[0].size + scatters[0].size) + 8 * height * width,
+            transcendentals=0,
+        ),
+    )(*scatters, *rows)
+
+
+def partner_grad_kernel(idx_ref, scatter_ref, rows_ref, before_ref, out_ref):
+    total = before_ref[0] + jnp.dot(scatter_ref[0], rows_ref[...], preferred_element_type=F32)
+    out_ref[...] = total.astype(BF16)
+
+
+def own_grad_kernel(idx_ref, scatter_ref, rows_ref, before_ref, arrived_ref, out_ref, held):
+    total = before_ref[0] + jnp.dot(scatter_ref[0], rows_ref[...], preferred_element_type=F32)
+    total += arrived_ref[...].astype(F32)
+    block, experts, _ = out_ref.shape
+    held[...] = total
+
+    def move(h, carry):
+        out_ref[h] = jnp.concatenate([held[pl.ds(e * block + h, 1), :] for e in range(experts)], axis=0)
+        return carry
+
+    lax.fori_loop(0, block, move, 0, unroll=8)
+
+
+def late_grad(index, scatter, rows, before, arrived, experts, tile):
+    _, height, count = scatter.shape
+    width = rows.shape[1]
+    in_specs = [
+        pl.BlockSpec((1, height, count), lambda i, idx: (idx[0], 0, 0)),
+        pl.BlockSpec((count, tile), lambda i, idx: (0, i)),
+        pl.BlockSpec((1, height, tile), lambda i, idx: (idx[0], 0, i)),
+    ]
+    args = [scatter, rows, before]
+    if arrived is None:
+        kernel, scratch = partner_grad_kernel, []
+        out_spec = pl.BlockSpec((height, tile), lambda i, idx: (0, i))
+        out_shape = jax.ShapeDtypeStruct((height, width), BF16)
+    else:
+        kernel, scratch = own_grad_kernel, [pltpu.VMEM((height, tile), F32)]
+        in_specs.append(pl.BlockSpec((height, tile), lambda i, idx: (0, i)))
+        args.append(arrived)
+        out_spec = pl.BlockSpec((height // experts, experts, tile), lambda i, idx: (0, 0, i))
+        out_shape = jax.ShapeDtypeStruct((height // experts, experts, width), F32)
+    return pl.pallas_call(
+        kernel,
+        grid_spec=pltpu.PrefetchScalarGridSpec(
+            num_scalar_prefetch=1,
+            grid=(width // tile,),
+            in_specs=in_specs,
+            out_specs=out_spec,
+            scratch_shapes=scratch,
+        ),
+        out_shape=out_shape,
+        compiler_params=pltpu.CompilerParams(vmem_limit_bytes=VMEM_BYTES),
+        cost_estimate=pl.CostEstimate(
+            flops=2 * height * count * width,
+            bytes_accessed=2 * (rows.size + scatter.size) + 8 * height * width,
+            transcendentals=0,
+        ),
+    )(index, *args)
+
+
+def place_kernel(top_k, first, idx_ref, *refs):
+    pieces = refs[:4]
+    out_ref, sum_ref = refs[-2:]
+    experts, slots, pair = pieces[0].shape
+    m = pl.program_id(0)
+
+    @pl.when(m == 0)
+    def _():
+        sum_ref[...] = jnp.zeros_like(sum_ref)
+
+    for i in range(4):
+
+        @pl.when(m == i)
+        def _():
+            out_ref[0] = pieces[i][...]
+            for e in range(experts):
+                row = pieces[i][e, slots - 8 :].astype(F32)[8 - top_k : 9 - top_k]
+                sum_ref[e : e + 1] += row[:, : pair // 2] + row[:, pair // 2 :]
+
+
+def place(index, pieces, before, sources, top_k):
+    experts, slots, pair = pieces[0].shape
+    first = before is None
+    shape = (sources, experts, slots, 4 * pair)
+    return pl.pallas_call(
+        functools.partial(place_kernel, top_k, first),
+        grid_spec=pltpu.PrefetchScalarGridSpec(
+            num_scalar_prefetch=1,
+            grid=(4,),
+            in_specs=[pl.BlockSpec((experts, slots, pair), lambda m, idx: (0, 0, 0))] * 4
+            + ([] if first else [pl.BlockSpec(memory_space=pl.ANY)]),
+            out_specs=[
+                pl.BlockSpec((1, experts, slots, pair), lambda m, idx: (idx[0], 0, 0, idx[1 + m])),
+                pl.BlockSpec((experts, pair // 2), lambda m, idx: (0, 0)),
+            ],
+        ),
+        out_shape=[
+            jax.ShapeDtypeStruct(shape, BF16),
+            jax.ShapeDtypeStruct((experts, pair // 2), F32),
+        ],
+        input_output_aliases={} if first else {5: 0},
+        compiler_params=pltpu.CompilerParams(vmem_limit_bytes=VMEM_BYTES),
+        cost_estimate=pl.CostEstimate(
+            flops=0, bytes_accessed=16 * experts * slots * pair, transcendentals=0
+        ),
+    )(index, *pieces, *([] if first else [before]))
+
+
+def on_device_tokens(grad_out, routes, affinity, saved_hidden, down_proj):
+    reps, sources = lax.axis_size("rep"), lax.axis_size("exp")
+    block, experts, width = down_proj.shape
+    tokens, top_k = routes.shape
+    most, hidden_units = saved_hidden.shape[3:]
+    pair = 2 * block
+    me = lax.axis_index("exp")
+    rep = lax.axis_index("rep")
+    chip, core = lax.div(rep, 2), lax.rem(rep, 2)
+    chips = [jnp.bitwise_xor(chip, m) for m in range(4)]
+
+    def across(array, bits):
+        return lax.ppermute(array, "rep", [(i, i ^ bits) for i in range(reps)])
+
+    def around(array, shift):
+        return lax.ppermute(array, "exp", [(i, (i + shift) % sources) for i in range(sources)])
+
+    totals = jnp.sum(affinity, axis=-1, keepdims=True)
+    shares = affinity / totals
+    route_weight = (ROUTE_SCALE * shares).astype(BF16)
+    meta = jnp.concatenate([routes.astype(BF16).T, route_weight.T], axis=1)
+    metas = jnp.stack([meta] + [around(meta, shift) for shift in range(1, sources)])
+    metas = jnp.take(metas, lax.rem(me - jnp.arange(sources) + sources, sources), axis=0)
+    blank = jnp.zeros((experts, sources, SLOT_PAD - most - top_k, pair), BF16)
+    metas = jnp.broadcast_to(metas[None], (experts, sources, top_k, pair))
+
+    held = saved_hidden.reshape(experts, sources, most, 4, pair)
+    held = jnp.transpose(held, (3, 0, 1, 2, 4))
+    hidden = []
+    for m in range(4):
+        piece = lax.dynamic_index_in_dim(held, chips[m], axis=0, keepdims=False)
+        piece = jnp.concatenate([piece, blank, metas], axis=2)
+        hidden.append(across(piece, 2 * m) if m else piece)
+
+    own_weight = jnp.transpose(down_proj, (1, 0, 2))
+    partner_weight = across(own_weight, 1)
+    weight = jnp.concatenate(
+        [
+            jnp.where(core == 0, own_weight, partner_weight),
+            jnp.where(core == 0, partner_weight, own_weight),
+        ],
+        axis=1,
+    ).reshape(experts * pair, width)
+
+    carried = grad_out
+    half = tokens // 2
+    scatters, rows, returned, indices = [], [], [], []
+    before = None
+    for step in range(sources):
+        from_x, from_y = across(carried, 2), across(carried, 4)
+        own = carried
+        if step < sources - 1:
+            carried = around(carried, 1)
+        top, bottom = across(from_x[:half], 4), across(from_y[half:], 2)
+        source = lax.rem(me - step + sources, sources)
+        index = jnp.stack([source, me * experts]).astype(jnp.int32)
+        *grads, scatter, row = project(
+            index, [own, from_x, from_y, top, bottom], weight, hidden, top_k
+        )
+        scatters.append(scatter)
+        rows.append(row)
+        returned.append([grads[0]] + [across(grads[m], 2 * m) for m in range(1, 4)])
+        indices.append(jnp.stack([source] + chips).astype(jnp.int32))
+        if step == sources - 2:
+            before = early_grad(scatters, rows, 512)
+    partner = late_grad((1 - core).reshape(1), scatters[-1], rows[-1], before, None, experts, 512)
+    partner = across(partner, 1)
+    placed, route_grad = None, 0.0
+    expert_ids = jnp.arange(experts, dtype=routes.dtype)
+    for step in range(sources):
+        placed, combine = place(indices[step], returned[step], placed, sources, top_k)
+        if step:
+            combine = around(combine, -step)
+        ids = lax.rem(me + step, sources) * experts + expert_ids
+        named = routes.T[:, None, :] == ids[None, :, None]
+        route_grad += jnp.sum(jnp.where(named, combine[None], 0.0), axis=1)
+    hidden_grad = jnp.transpose(placed[:, :, :most], (1, 0, 2, 3)).reshape(saved_hidden.shape)
+    route_grad = ROUTE_SCALE * route_grad.T
+    affinity_grad = (route_grad - jnp.sum(route_grad * shares, axis=-1, keepdims=True)) / totals
+    down_grad = late_grad(core.reshape(1), scatters[-1], rows[-1], before, partner, experts, 512)
+    return (affinity_grad, hidden_grad, down_grad)
+
+
+def on_device(grad_out, routes, affinity, saved_hidden, down_proj):
+    reps, sources = lax.axis_size("rep"), lax.axis_size("exp")
+    block, experts, width = down_proj.shape
+    tokens, top_k = routes.shape
+    most = saved_hidden.shape[3]
+    fits = block == 128 and tokens == 128 and width % 512 == 0 and reps == 8
+    fits = fits and sources > 1 and most + top_k <= SLOT_PAD and top_k <= 8
+    if fits and sources * tokens <= 2 * block * experts:
+        return on_device_tokens(grad_out, routes, affinity, saved_hidden, down_proj)
+    return on_device_weights(grad_out, routes, affinity, saved_hidden, down_proj)
+
+
 def solution(mesh):
     return jax.shard_map(
         on_device,

time: 484 us -> 284 us (0.59)
  waiting for transfers between devices: 288 us -> 77.1 us
  Pallas kernels: 0 us -> 87.2 us
  local copies, waits for them, and re-layouts: 110 us -> 43.3 us
  matrix products: 36.8 us -> 0 us
  starting transfers between devices: 15.5 us -> 51.8 us
  between operations: 14.3 us -> 0.95 us
    all_to_all x3 -> x0, waiting for transfers between devices: 147 us -> none  [the longest x1 147 us: on_device(): lax.all_to_all(outgoing, 'exp', split_axis=0, concat_axis=2, tiled=True)]
    unnamed x3 -> x0, waiting for transfers between devices: 141 us -> none
    pallas_call x0 -> x11, Pallas kernels: none -> 87.2 us  [the longest x4 46.9 us: project(): pl.pallas_call(functools.partial(project_kernel, top_k, sizes), grid_spec...]
    ppermute x0 -> x42, waiting for transfers between devices: none -> 77.1 us  [the longest x33 58.9 us: across(): return lax.ppermute(array, 'rep', [(i, i ^ bits) for i in range(reps)])]
    ppermute x0 -> x42, starting transfers between devices: none -> 51.8 us  [the longest x33 36.6 us: across(): return lax.ppermute(array, 'rep', [(i, i ^ bits) for i in range(reps)])]
    unnamed x16 -> x27, local copies, waits for them, and re-layouts: 61.1 us -> 10.5 us
    dot_general x2 -> x0, matrix products: 36.8 us -> none  [the longest x1 21.5 us: on_device(): jnp.einsum('erd,hed->erh', received, gathered, preferred_element_type=jnp...]
    gather x10 -> x1, local copies, waits for them, and re-layouts: 22.4 us -> 0.57 us  [on_device_tokens(): jnp.take(metas, lax.rem(me - jnp.arange(sources) + sources, sources), axi...]
  transfers between devices with their start and end apart: 5 -> 42, of which waited for: 2 -> 13; matrix products, arithmetic and copies ran while one was open for 30% -> 21% of each run, Pallas kernels for 0% -> 19%
where the time goes in v2:
time: 284 us; the launch traced here: 283 us
  Pallas kernels  87.2 us (31%)
  waiting for transfers between devices  77.1 us (27%)
  starting transfers between devices  51.8 us (18%)
  local copies, waits for them, and re-layouts  43.3 us (15%)
  other arithmetic  22.4 us (8%)
    ppermute x33, waiting for transfers between devices, across(): return lax.ppermute(array, 'rep', [(i, i ^ bits) for i in range(reps)])  58.9 us
    pallas_call x4, Pallas kernels, project(): pl.pallas_call(functools.partial(project_kernel, top_k, sizes), grid_spec...  46.9 us
    ppermute x33, starting transfers between devices, across(): return lax.ppermute(array, 'rep', [(i, i ^ bits) for i in range(reps)])  36.6 us
    pallas_call x2, Pallas kernels, late_grad(): pl.pallas_call(kernel, grid_spec=pltpu.PrefetchScalarGridSpec(num_scalar_...  22.5 us
    ppermute x9, waiting for transfers between devices, around(): lax.ppermute(array, 'exp', [(i, (i + shift) % sources) for i in range(sou...  18.2 us
    ppermute x9, starting transfers between devices, around(): lax.ppermute(array, 'exp', [(i, (i + shift) % sources) for i in range(sou...  15.2 us
    pallas_call x1, Pallas kernels, early_grad(): pl.pallas_call(functools.partial(early_grad_kernel, terms), grid=(width /...  14.7 us
    unnamed x27, local copies, waits for them, and re-layouts  10.5 us
  transfers between devices with their start and end apart: 42, of which 13 were waited for; matrix products, arithmetic and copies ran while one was open for 21% of the time, Pallas kernels for 19%

profile of v2, /device:TPU:0, one launch (start us, length us, event | category | flops | bytes accessed | tf_op | source)
XLA Modules:
  0.0 282.8 jit_solution(7098477473546998440)
XLA Ops:
  1.1 2.6 collective-permute-start.14
  5.9 2.1 collective-permute-start.7
  9.0 1.6 collective-permute-start.5
  10.6 13.8 %collective-permute-done.7 = bf16[4,256]{1,0:T(4,128)(2,1)S(1)} collective-permute-done((bf16[4,256]{1,0:T(4,128)(2,1)S(1)}, bf16[4,256]{1,0:T(4,128)(2,1)S(1)}, u32[]{:S(2)}, u32[]{:S(2)}) %collective-permute-start.7) | collective-permute-done | bytes 2080 | tf_op jit(solution)/shard_map/ppermute | solution.py:338
  24.4 1.5 collective-permute-start
  25.9 1.5 collective-permute-start.1
  28.7 2.0 collective-permute-start.23
  30.8 4.8 %reshape.98 = bf16[4,4,60,4,256]{4,3,1,2,0:T(4,128)(2,1)} reshape(bf16[1,4,4,60,1024]{4,2,3,1,0:T(4,128)(2,1)} %param.8) | data formatting | bytes 3932160 | tf_op jit(solution)/shard_map/reshape | solution.py:349
  35.8 8.8 %constant_dynamic-slice_fusion = (bf16[4,4,60,1,256]{4,3,1,2,0:T(2,128)(2,1)S(1)}, bf16[4,4,60,1,256]{4,3,1,2,0:T(2,128)(2,1)S(1)}, bf16[4,4,60,1,256]{4,3,1,2,0:T(2,128)(2,1)}, bf16[4,4,60,1,256]{4,3,1,2,0:T(2,128)(2,1)}) fusion(bf16[4,4,60,4,256]{4,3,1,2,0:T(4,128)(2,1)} %reshape.98, s32[]{:T(128)S(6)} %select_n.71, s32[]{:T(128)S(6)} %select_n.70, ...), kind=kLoop, calls=%fused_computation.37 | loop fusion | bytes 3932176 | tf_op jit(solution)/shard_map/dynamic-slice.3
  45.9 1.9 collective-permute-done.refs_1_
  47.9 1.5 collective-permute-start.16
  49.4 3.0 %collective-permute-done.23.refs_0_ = bf16[128,3584]{1,0:T(8,128)(2,1)} collective-permute-done((bf16[128,3584]{1,0:T(8,128)(2,1)}, bf16[128,3584]{1,0:T(8,128)(2,1)}, u32[]{:S(2)}, u32[]{:S(2)}) %collective-permute-start.23) | collective-permute-done | bytes 917536 | tf_op jit(solution)/shard_map/ppermute | solution.py:338
  54.5 13.1 %collective-permute-done.15.refs_1_ = bf16[128,3584]{1,0:T(8,128)(2,1)S(1)} collective-permute-done((bf16[128,3584]{1,0:T(8,128)(2,1)}, bf16[128,3584]{1,0:T(8,128)(2,1)S(1)}, u32[]{:S(2)}, u32[]{:S(2)}) %collective-permute-start.15) | collective-permute-done | bytes 917536 | tf_op jit(solution)/shard_map/ppermute | solution.py:335
  67.6 2.8 copy_bitcast_fusion.2
  71.1 1.9 pad_maximum_fusion.1
  73.1 1.6 collective-permute-start.8
  75.7 11.6 %collective-permute-done.24.refs_1_ = bf16[128,3584]{1,0:T(8,128)(2,1)} collective-permute-done((bf16[128,3584]{1,0:T(8,128)(2,1)}, bf16[128,3584]{1,0:T(8,128)(2,1)}, u32[]{:S(2)}, u32[]{:S(2)}) %collective-permute-start.24) | collective-permute-done | bytes 917536 | tf_op jit(solution)/shard_map/ppermute | solution.py:335
  87.3 1.5 collective-permute-start.9
  88.8 1.8 slice.42
  92.1 1.9 slice.43
  94.5 1.5 collective-permute-start.34
  96.0 9.2 %broadcast_select_fusion.1 = (bf16[4,128,3584]{2,0,1:T(4,128)(2,1)}, bf16[4,128,3584]{2,0,1:T(4,128)(2,1)}) fusion(bf16[4,128,3584]{2,0,1:T(4,128)(2,1)} %collective-permute-done.4, pred[]{:T(512)S(6)} %eq.23, bf16[128,4,3584]{2,1,0:T(4,128)(2,1)} %param.9), kind=kLoop, calls=%fused_computation.3 | loop fusion | flops 3670016 | bytes 14680065 | tf_op jit(solution)/shard_map/jit(_where)/select_n | solution.py:361
  105.2 22.7 %collective-permute-done.33.refs_1_ = bf16[128,3584]{1,0:T(8,128)(2,1)S(1)} collective-permute-done((bf16[128,3584]{1,0:T(8,128)(2,1)}, bf16[128,3584]{1,0:T(8,128)(2,1)S(1)}, u32[]{:S(2)}, u32[]{:S(2)}) %collective-permute-start.33) | collective-permute-done | bytes 917536 | tf_op jit(solution)/shard_map/ppermute | solution.py:335
  127.9 1.5 collective-permute-start.17
  129.7 1.5 collective-permute-start.18
  131.2 7.5 %pad_maximum_fusion = bf16[4,256,3584]{2,0,1:T(4,128)(2,1)} fusion(bf16[4,128,3584]{2,0,1:T(4,128)(2,1)} %get-tuple-element.80, bf16[4,128,3584]{2,0,1:T(4,128)(2,1)} %get-tuple-element.79), kind=kLoop, calls=%fused_computation.1 | loop fusion | flops 3670016 | bytes 14680064 | tf_op jit(solution)/shard_map/concatenate | solution.py:359
  138.7 7.4 %copy.17 = bf16[4,256,3584]{2,1,0:T(8,128)(2,1)} copy(bf16[4,256,3584]{2,0,1:T(4,128)(2,1)} %pad_maximum_fusion) | data formatting | bytes 14680064 | tf_op jit(solution)/shard_map/concatenate | solution.py:359
  147.8 1.5 collective-permute-start.2
  150.3 1.5 collective-permute-start.27
  151.8 1.5 collective-permute-start.35
  153.4 11.5 %shard_map.78 = (bf16[4,64,256]{2,1,0:T(8,128)(2,1)S(1)}, bf16[4,64,256]{2,1,0:T(8,128)(2,1)S(1)}, bf16[4,64,256]{2,1,0:T(8,128)(2,1)S(1)}, bf16[4,64,256]{2,1,0...) custom-call(s32[2]{0:T(128)S(1)} %pad_add_fusion.1.idx_ref, ...), custom_call_target="tpu_custom_call" | custom-call | flops 7516192768 | bytes 14680064 | tf_op jit(solution)/shard_map/pallas_call | solution.py:157
  164.8 1.8 copy-done.3
  167.2 11.3 %shard_map.76 = (bf16[4,64,256]{2,1,0:T(8,128)(2,1)S(1)}, bf16[4,64,256]{2,1,0:T(8,128)(2,1)S(1)}, bf16[4,64,256]{2,1,0:T(8,128)(2,1)S(1)}, bf16[4,64,256]{2,1,0...) custom-call(s32[2]{0:T(128)S(1)} %pad_add_fusion.idx_ref, ...), custom_call_target="tpu_custom_call" | custom-call | flops 7516192768 | bytes 14680064 | tf_op jit(solution)/shard_map/pallas_call | solution.py:157
  178.4 1.8 copy-done.5
  180.3 12.4 %shard_map.80 = (bf16[4,64,256]{2,1,0:T(8,128)(2,1)S(1)}, bf16[4,64,256]{2,1,0:T(8,128)(2,1)}, bf16[4,64,256]{2,1,0:T(8,128)(2,1)S(1)}, bf16[4,64,256]{2,1,0:T(8...) custom-call(s32[2]{0:T(128)S(1)} %pad_add_fusion.2.idx_ref, ...), custom_call_target="tpu_custom_call" | custom-call | flops 7516192768 | bytes 14680064 | tf_op jit(solution)/shard_map/pallas_call | solution.py:157
  192.7 2.0 copy-done.4
  194.7 2.0 copy-done.6
  196.7 14.7 %shard_map.84.before_ref = f32[2,512,3584]{2,1,0:T(8,128)} custom-call(bf16[2,512,512]{2,1,0:T(8,128)(2,1)S(1)} %get-tuple-element.61.refs_0_, bf16[2,512,512]{2,1,0:T(8,128)(2,1)S(1)} %get-tuple-element.62.refs_1_, bf16[2,512,512]{2,1,0:T(8,128)(2,1)S(1)} %get-tuple-element.63.refs_2_, bf16[512,3584]{1,0:T(8,128)(2,1)S(1)} %copy-done.6, ...), custom_call_target="tpu_custom_call" | custom-call | flops 11274289152 | bytes 28835840 | tf_op jit(solution)/shard_map/pallas_call | solution.py:203
  211.5 11.8 %shard_map.82 = (bf16[4,64,256]{2,1,0:T(8,128)(2,1)S(1)}, bf16[4,64,256]{2,1,0:T(8,128)(2,1)}, bf16[4,64,256]{2,1,0:T(8,128)(2,1)S(1)}, bf16[4,64,256]{2,1,0:T(8...) custom-call(s32[2]{0:T(128)S(1)} %pad_add_fusion.3.idx_ref, ...), custom_call_target="tpu_custom_call" | custom-call | flops 7516192768 | bytes 14680064 | tf_op jit(solution)/shard_map/pallas_call | solution.py:157
  223.3 9.2 %shard_map.85 = bf16[512,3584]{1,0:T(8,128)(2,1)} custom-call(s32[1]{0:T(128)} %bitcast.27.idx_ref, bf16[2,512,512]{2,1,0:T(8,128)(2,1)S(1)} %get-tuple-element.59.scatter_ref, bf16[512,3584]{1,0:T(8,128)(2,1)S(1)} %get-tuple-element.60.rows_ref, f32[2,512,3584]{2,1,0:T(8,128)} %shard_map.84.before_ref), custom_call_target="tpu_custom_call" | custom-call | flops 1879048192 | bytes 19398656 | tf_op jit(solution)/shard_map/pallas_call | solution.py:256
  234.5 1.5 collective-permute-start.21
  239.3 3.8 %collective-permute-done.20.refs_2_ = bf16[4,64,256]{2,1,0:T(8,128)(2,1)S(1)} collective-permute-done((bf16[4,64,256]{2,1,0:T(8,128)(2,1)S(1)}, bf16[4,64,256]{2,1,0:T(8,128)(2,1)S(1)}, u32[]{:S(2)}, u32[]{:S(2)}) %collective-permute-start.20) | collective-permute-done | bytes 131104 | tf_op jit(solution)/shard_map/ppermute | solution.py:335
  244.8 1.9 collective-permute-start.29
  247.4 3.2 %collective-permute-done.13.refs_3_ = bf16[4,64,256]{2,1,0:T(8,128)(2,1)S(1)} collective-permute-done((bf16[4,64,256]{2,1,0:T(8,128)(2,1)S(1)}, bf16[4,64,256]{2,1,0:T(8,128)(2,1)S(1)}, u32[]{:S(2)}, u32[]{:S(2)}) %collective-permute-start.13) | collective-permute-done | bytes 131104 | tf_op jit(solution)/shard_map/ppermute | solution.py:335
  251.0 2.9 %collective-permute-start.38 = (bf16[4,64,256]{2,1,0:T(8,128)(2,1)S(1)}, bf16[4,64,256]{2,1,0:T(8,128)(2,1)S(1)}, u32[]{:S(2)}, u32[]{:S(2)}) collective-permute-start(bf16[4,64,256]{2,1,0:T(8,128)(2,1)S(1)} %get-tuple-element.54), channel_id=1, source_target_pairs={{0,16},{4,20},{8,24},{12,28},{16,0},{20,4},{24,8},{28,12},{1,17},{... | collective-permute-start | bytes 393224 | tf_op jit(solution)/shard_map/ppermute | solution.py:335
  257.0 4.7 %collective-permute-start.22 = (f32[4,128]{1,0:T(4,128)S(1)}, f32[4,128]{1,0:T(4,128)S(1)}, u32[]{:S(2)}, u32[]{:S(2)}) collective-permute-start(f32[4,128]{1,0:T(4,128)S(1)} %get-tuple-element.45), channel_id=1, source_target_pairs={{0,3},{1,0},{2,1},{3,2},{4,7},{5,4},{6,5},{7,6},{8,11},{9,8},{10,9... | collective-permute-start | bytes 6152 | tf_op jit(solution)/shard_map/ppermute | solution.py:338
  264.7 2.8 copy.22
  269.6 13.3 %shard_map.86 = f32[128,4,3584]{2,1,0:T(4,128)} custom-call(s32[1]{0:T(128)} %bitcast.26.idx_ref, bf16[2,512,512]{2,1,0:T(8,128)(2,1)S(1)} %get-tuple-element.59.scatter_ref, bf16[512,3584]{1,0:T(8,128)(2,1)S(1)} %copy-done.1, f32[2,512,3584]{2,1,0:T(8,128)} %shard_map.84.before_ref, bf16[512,3584]{1,0:T(8,128)(2,1)} %collective-permute-done.41.arrived_ref), custom_call_target="tpu_custom_call" | custom-call | flops 1879048192 | bytes 19398656 | tf_op jit(solution)/shard_map/pallas_call | solution.py:256
  (115 shorter events, 32.1 us)
Async XLA Ops:
  0.6 93.8 %collective-permute-start.4 = (bf16[4,128,3584]{2,0,1:T(4,128)(2,1)}, bf16[4,128,3584]{2,0,1:T(4,128)(2,1)}, u32[]{:S(2)}, u32[]{:S(2)}) collective-permute-start(bf16[4,128,3584]{2,0,1:T(4,128)(2,1)} %bitcast.52), channel_id=1, source_target_pairs={{0,4},{4,0},{8,12},{12,8},{16,20},{20,16},{24,28},{28,24},{1,5},{5... | collective-permute-start | bytes 11010056 | tf_op jit(solution)/shard_map/ppermute | solution.py:335
  1.1 26.3 %collective-permute-start.14 = (bf16[128,3584]{1,0:T(8,128)(2,1)}, bf16[128,3584]{1,0:T(8,128)(2,1)}, u32[]{:S(2)}, u32[]{:S(2)}) collective-permute-start(bf16[128,3584]{1,0:T(8,128)(2,1)} %refs_0_.1), channel_id=1, source_target_pairs={{0,1},{1,2},{2,3},{3,0},{4,5},{5,6},{6,7},{7,4},{8,9},{9,10},{10,1... | collective-permute-start | bytes 2752520 | tf_op jit(solution)/shard_map/ppermute | solution.py:338
  4.5 6.1 %copy-start.9 = (f32[128]{0:T(128)}, f32[128]{0:T(128)S(1)}, u32[]{:S(2)}) copy-start(f32[128]{0:T(128)S(1)} %reduce_sum.54) | copy-start | bytes 1540
  5.9 18.5 %collective-permute-start.7 = (bf16[4,256]{1,0:T(4,128)(2,1)S(1)}, bf16[4,256]{1,0:T(4,128)(2,1)S(1)}, u32[]{:S(2)}, u32[]{:S(2)}) collective-permute-start(bf16[4,256]{1,0:T(4,128)(2,1)S(1)} %get-tuple-element.90), channel_id=1, source_target_pairs={{0,3},{1,0},{2,1},{3,2},{4,7},{5,4},{6,5},{7,6},{8,11},{9,8},{10,9... | collective-permute-start | bytes 6152 | tf_op jit(solution)/shard_map/ppermute | solution.py:338
  8.0 17.9 %collective-permute-start.6 = (bf16[4,256]{1,0:T(4,128)(2,1)S(1)}, bf16[4,256]{1,0:T(4,128)(2,1)S(1)}, u32[]{:S(2)}, u32[]{:S(2)}) collective-permute-start(bf16[4,256]{1,0:T(4,128)(2,1)S(1)} %get-tuple-element.90), channel_id=1, source_target_pairs={{0,2},{1,3},{2,0},{3,1},{4,6},{5,7},{6,4},{7,5},{8,10},{9,11},{10,... | collective-permute-start | bytes 6152 | tf_op jit(solution)/shard_map/ppermute | solution.py:338
  9.0 19.7 %collective-permute-start.5 = (bf16[4,256]{1,0:T(4,128)(2,1)S(1)}, bf16[4,256]{1,0:T(4,128)(2,1)S(1)}, u32[]{:S(2)}, u32[]{:S(2)}) collective-permute-start(bf16[4,256]{1,0:T(4,128)(2,1)S(1)} %get-tuple-element.90), channel_id=1, source_target_pairs={{0,1},{1,2},{2,3},{3,0},{4,5},{5,6},{6,7},{7,4},{8,9},{9,10},{10,1... | collective-permute-start | bytes 6152 | tf_op jit(solution)/shard_map/ppermute | solution.py:338
  24.4 23.5 %collective-permute-start = (bf16[128,3584]{1,0:T(8,128)(2,1)}, bf16[128,3584]{1,0:T(8,128)(2,1)S(1)}, u32[]{:S(2)}, u32[]{:S(2)}) collective-permute-start(bf16[128,3584]{1,0:T(8,128)(2,1)} %refs_0_.1), channel_id=1, source_target_pairs={{0,8},{4,12},{8,0},{12,4},{16,24},{20,28},{24,16},{28,20},{1,9},{5... | collective-permute-start | bytes 2752520 | tf_op jit(solution)/shard_map/ppermute | solution.py:335
  25.9 27.2 %collective-permute-start.1 = (bf16[128,3584]{1,0:T(8,128)(2,1)}, bf16[128,3584]{1,0:T(8,128)(2,1)S(1)}, u32[]{:S(2)}, u32[]{:S(2)}) collective-permute-start(bf16[128,3584]{1,0:T(8,128)(2,1)} %refs_0_.1), channel_id=1, source_target_pairs={{0,16},{4,20},{8,24},{12,28},{16,0},{20,4},{24,8},{28,12},{1,17},{... | collective-permute-start | bytes 2752520 | tf_op jit(solution)/shard_map/ppermute | solution.py:335
  27.4 40.1 %collective-permute-start.15 = (bf16[128,3584]{1,0:T(8,128)(2,1)}, bf16[128,3584]{1,0:T(8,128)(2,1)S(1)}, u32[]{:S(2)}, u32[]{:S(2)}) collective-permute-start(bf16[128,3584]{1,0:T(8,128)(2,1)} %collective-permute-done.14.refs_0_), channel_id=1, source_target_pairs={{0,8},{4,12},{8,0},{12,4},{16,24},{20,28},{24,16},{28,20},{1,9},{5... | collective-permute-start | bytes 2752520 | tf_op jit(solution)/shard_map/ppermute | solution.py:335
  28.7 23.7 %collective-permute-start.23 = (bf16[128,3584]{1,0:T(8,128)(2,1)}, bf16[128,3584]{1,0:T(8,128)(2,1)}, u32[]{:S(2)}, u32[]{:S(2)}) collective-permute-start(bf16[128,3584]{1,0:T(8,128)(2,1)} %collective-permute-done.14.refs_0_), channel_id=1, source_target_pairs={{0,1},{1,2},{2,3},{3,0},{4,5},{5,6},{6,7},{7,4},{8,9},{9,10},{10,1... | collective-permute-start | bytes 2752520 | tf_op jit(solution)/shard_map/ppermute | solution.py:338
  47.9 25.3 %collective-permute-start.16 = (bf16[128,3584]{1,0:T(8,128)(2,1)}, bf16[128,3584]{1,0:T(8,128)(2,1)}, u32[]{:S(2)}, u32[]{:S(2)}) collective-permute-start(bf16[128,3584]{1,0:T(8,128)(2,1)} %collective-permute-done.14.refs_0_), channel_id=1, source_target_pairs={{0,16},{4,20},{8,24},{12,28},{16,0},{20,4},{24,8},{28,12},{1,17},{... | collective-permute-start | bytes 2752520 | tf_op jit(solution)/shard_map/ppermute | solution.py:335
  52.4 34.9 %collective-permute-start.24 = (bf16[128,3584]{1,0:T(8,128)(2,1)}, bf16[128,3584]{1,0:T(8,128)(2,1)}, u32[]{:S(2)}, u32[]{:S(2)}) collective-permute-start(bf16[128,3584]{1,0:T(8,128)(2,1)} %collective-permute-done.23.refs_0_), channel_id=1, source_target_pairs={{0,8},{4,12},{8,0},{12,4},{16,24},{20,28},{24,16},{28,20},{1,9},{5... | collective-permute-start | bytes 2752520 | tf_op jit(solution)/shard_map/ppermute | solution.py:335
  53.1 37.5 %collective-permute-start.25 = (bf16[128,3584]{1,0:T(8,128)(2,1)}, bf16[128,3584]{1,0:T(8,128)(2,1)}, u32[]{:S(2)}, u32[]{:S(2)}) collective-permute-start(bf16[128,3584]{1,0:T(8,128)(2,1)} %collective-permute-done.23.refs_0_), channel_id=1, source_target_pairs={{0,16},{4,20},{8,24},{12,28},{16,0},{20,4},{24,8},{28,12},{1,17},{... | collective-permute-start | bytes 2752520 | tf_op jit(solution)/shard_map/ppermute | solution.py:335
  67.5 26.4 %collective-permute-start.32 = (bf16[128,3584]{1,0:T(8,128)(2,1)}, bf16[128,3584]{1,0:T(8,128)(2,1)}, u32[]{:S(2)}, u32[]{:S(2)}) collective-permute-start(bf16[128,3584]{1,0:T(8,128)(2,1)} %collective-permute-done.23.refs_0_), channel_id=1, source_target_pairs={{0,1},{1,2},{2,3},{3,0},{4,5},{5,6},{6,7},{7,4},{8,9},{9,10},{10,1... | collective-permute-start | bytes 2752520 | tf_op jit(solution)/shard_map/ppermute | solution.py:338
  73.1 74.6 %collective-permute-start.8 = (bf16[4,4,64,256]{3,2,1,0:T(8,128)(2,1)S(1)}, bf16[4,4,64,256]{3,2,1,0:T(8,128)(2,1)S(1)}, u32[]{:S(2)}, u32[]{:S(2)}) collective-permute-start(bf16[4,4,64,256]{3,2,1,0:T(8,128)(2,1)S(1)} %get-tuple-element.86), channel_id=1, source_target_pairs={{0,8},{4,12},{8,0},{12,4},{16,24},{20,28},{24,16},{28,20},{1,9},{5... | collective-permute-start | bytes 1572872 | tf_op jit(solution)/shard_map/ppermute | solution.py:335
  87.3 62.0 %collective-permute-start.9 = (bf16[4,4,64,256]{3,2,1,0:T(8,128)(2,1)S(1)}, bf16[4,4,64,256]{3,2,1,0:T(8,128)(2,1)S(1)}, u32[]{:S(2)}, u32[]{:S(2)}) collective-permute-start(bf16[4,4,64,256]{3,2,1,0:T(8,128)(2,1)S(1)} %get-tuple-element.87), channel_id=1, source_target_pairs={{0,16},{4,20},{8,24},{12,28},{16,0},{20,4},{24,8},{28,12},{1,17},{... | collective-permute-start | bytes 1572872 | tf_op jit(solution)/shard_map/ppermute | solution.py:335
  90.6 59.2 %collective-permute-start.10 = (bf16[4,4,64,256]{3,2,1,0:T(8,128)(2,1)S(1)}, bf16[4,4,64,256]{3,2,1,0:T(8,128)(2,1)S(1)}, u32[]{:S(2)}, u32[]{:S(2)}) collective-permute-start(bf16[4,4,64,256]{3,2,1,0:T(8,128)(2,1)S(1)} %get-tuple-element.85), channel_id=1, source_target_pairs={{0,24},{4,28},{8,16},{12,20},{16,8},{20,12},{24,0},{28,4},{1,25},{... | collective-permute-start | bytes 1572872 | tf_op jit(solution)/shard_map/ppermute | solution.py:335
  93.9 34.0 %collective-permute-start.33 = (bf16[128,3584]{1,0:T(8,128)(2,1)}, bf16[128,3584]{1,0:T(8,128)(2,1)S(1)}, u32[]{:S(2)}, u32[]{:S(2)}) collective-permute-start(bf16[128,3584]{1,0:T(8,128)(2,1)} %collective-permute-done.32.refs_0_), channel_id=1, source_target_pairs={{0,8},{4,12},{8,0},{12,4},{16,24},{20,28},{24,16},{28,20},{1,9},{5... | collective-permute-start | bytes 2752520 | tf_op jit(solution)/shard_map/ppermute | solution.py:335
  94.5 35.2 %collective-permute-start.34 = (bf16[128,3584]{1,0:T(8,128)(2,1)}, bf16[128,3584]{1,0:T(8,128)(2,1)S(1)}, u32[]{:S(2)}, u32[]{:S(2)}) collective-permute-start(bf16[128,3584]{1,0:T(8,128)(2,1)} %collective-permute-done.32.refs_0_), channel_id=1, source_target_pairs={{0,16},{4,20},{8,24},{12,28},{16,0},{20,4},{24,8},{28,12},{1,17},{... | collective-permute-start | bytes 2752520 | tf_op jit(solution)/shard_map/ppermute | solution.py:335
  127.9 22.4 %collective-permute-start.17 = (bf16[64,3584]{1,0:T(8,128)(2,1)S(1)}, bf16[64,3584]{1,0:T(8,128)(2,1)S(1)}, u32[]{:S(2)}, u32[]{:S(2)}) collective-permute-start(bf16[64,3584]{1,0:T(8,128)(2,1)S(1)} %slice.40), channel_id=1, source_target_pairs={{0,16},{4,20},{8,24},{12,28},{16,0},{20,4},{24,8},{28,12},{1,17},{... | collective-permute-start | bytes 1376264 | tf_op jit(solution)/shard_map/ppermute | solution.py:335
  129.7 22.2 %collective-permute-start.18 = (bf16[64,3584]{1,0:T(8,128)(2,1)S(1)}, bf16[64,3584]{1,0:T(8,128)(2,1)S(1)}, u32[]{:S(2)}, u32[]{:S(2)}) collective-permute-start(bf16[64,3584]{1,0:T(8,128)(2,1)S(1)} %slice.41), channel_id=1, source_target_pairs={{0,8},{4,12},{8,0},{12,4},{16,24},{20,28},{24,16},{28,20},{1,9},{5... | collective-permute-start | bytes 1376264 | tf_op jit(solution)/shard_map/ppermute | solution.py:335
  147.8 18.8 %collective-permute-start.2 = (bf16[64,3584]{1,0:T(8,128)(2,1)S(1)}, bf16[64,3584]{1,0:T(8,128)(2,1)S(1)}, u32[]{:S(2)}, u32[]{:S(2)}) collective-permute-start(bf16[64,3584]{1,0:T(8,128)(2,1)S(1)} %slice.38), channel_id=1, source_target_pairs={{0,16},{4,20},{8,24},{12,28},{16,0},{20,4},{24,8},{28,12},{1,17},{... | collective-permute-start | bytes 1376264 | tf_op jit(solution)/shard_map/ppermute | solution.py:335
  149.3 17.8 %collective-permute-start.3 = (bf16[64,3584]{1,0:T(8,128)(2,1)S(1)}, bf16[64,3584]{1,0:T(8,128)(2,1)S(1)}, u32[]{:S(2)}, u32[]{:S(2)}) collective-permute-start(bf16[64,3584]{1,0:T(8,128)(2,1)S(1)} %slice.39), channel_id=1, source_target_pairs={{0,8},{4,12},{8,0},{12,4},{16,24},{20,28},{24,16},{28,20},{1,9},{5... | collective-permute-start | bytes 1376264 | tf_op jit(solution)/shard_map/ppermute | solution.py:335
  149.8 30.4 %collective-permute-start.26 = (bf16[64,3584]{1,0:T(8,128)(2,1)}, bf16[64,3584]{1,0:T(8,128)(2,1)S(1)}, u32[]{:S(2)}, u32[]{:S(2)}) collective-permute-start(bf16[64,3584]{1,0:T(8,128)(2,1)} %slice.42), channel_id=1, source_target_pairs={{0,16},{4,20},{8,24},{12,28},{16,0},{20,4},{24,8},{28,12},{1,17},{... | collective-permute-start | bytes 1376264 | tf_op jit(solution)/shard_map/ppermute | solution.py:335
  150.3 29.9 %collective-permute-start.27 = (bf16[64,3584]{1,0:T(8,128)(2,1)}, bf16[64,3584]{1,0:T(8,128)(2,1)S(1)}, u32[]{:S(2)}, u32[]{:S(2)}) collective-permute-start(bf16[64,3584]{1,0:T(8,128)(2,1)} %slice.43), channel_id=1, source_target_pairs={{0,8},{4,12},{8,0},{12,4},{16,24},{20,28},{24,16},{28,20},{1,9},{5... | collective-permute-start | bytes 1376264 | tf_op jit(solution)/shard_map/ppermute | solution.py:335
  151.8 59.6 %collective-permute-start.35 = (bf16[64,3584]{1,0:T(8,128)(2,1)}, bf16[64,3584]{1,0:T(8,128)(2,1)S(1)}, u32[]{:S(2)}, u32[]{:S(2)}) collective-permute-start(bf16[64,3584]{1,0:T(8,128)(2,1)} %slice.44), channel_id=1, source_target_pairs={{0,16},{4,20},{8,24},{12,28},{16,0},{20,4},{24,8},{28,12},{1,17},{... | collective-permute-start | bytes 1376264 | tf_op jit(solution)/shard_map/ppermute | solution.py:335
  153.4 13.8 %copy-start.2 = (bf16[128,3584]{1,0:T(8,128)(2,1)S(1)}, bf16[128,3584]{1,0:T(8,128)(2,1)}, u32[]{:S(2)}) copy-start(bf16[128,3584]{1,0:T(8,128)(2,1)} %refs_0_.1) | copy-start | bytes 2752516
  166.6 44.9 %collective-permute-start.36 = (bf16[64,3584]{1,0:T(8,128)(2,1)}, bf16[64,3584]{1,0:T(8,128)(2,1)S(1)}, u32[]{:S(2)}, u32[]{:S(2)}) collective-permute-start(bf16[64,3584]{1,0:T(8,128)(2,1)} %slice.45), channel_id=1, source_target_pairs={{0,8},{4,12},{8,0},{12,4},{16,24},{20,28},{24,16},{28,20},{1,9},{5... | collective-permute-start | bytes 1376264 | tf_op jit(solution)/shard_map/ppermute | solution.py:335
  223.3 9.2 %copy-start = (bf16[512,3584]{1,0:T(8,128)(2,1)}, bf16[512,3584]{1,0:T(8,128)(2,1)S(1)}, u32[]{:S(2)}) copy-start(bf16[512,3584]{1,0:T(8,128)(2,1)S(1)} %get-tuple-element.60.rows_ref) | copy-start | bytes 11010052
  232.5 37.1 %collective-permute-start.41 = (bf16[512,3584]{1,0:T(8,128)(2,1)}, bf16[512,3584]{1,0:T(8,128)(2,1)}, u32[]{:S(2)}, u32[]{:S(2)}) collective-permute-start(bf16[512,3584]{1,0:T(8,128)(2,1)} %shard_map.85), channel_id=1, source_target_pairs={{0,4},{4,0},{8,12},{12,8},{16,20},{20,16},{24,28},{28,24},{1,5},{5... | collective-permute-start | bytes 11010056 | tf_op jit(solution)/shard_map/ppermute | solution.py:335
  232.5 6.3 %collective-permute-start.19 = (bf16[4,64,256]{2,1,0:T(8,128)(2,1)S(1)}, bf16[4,64,256]{2,1,0:T(8,128)(2,1)S(1)}, u32[]{:S(2)}, u32[]{:S(2)}) collective-permute-start(bf16[4,64,256]{2,1,0:T(8,128)(2,1)S(1)} %get-tuple-element.41), channel_id=1, source_target_pairs={{0,8},{4,12},{8,0},{12,4},{16,24},{20,28},{24,16},{28,20},{1,9},{5... | collective-permute-start | bytes 393224 | tf_op jit(solution)/shard_map/ppermute | solution.py:335
  234.0 9.1 %collective-permute-start.20 = (bf16[4,64,256]{2,1,0:T(8,128)(2,1)S(1)}, bf16[4,64,256]{2,1,0:T(8,128)(2,1)S(1)}, u32[]{:S(2)}, u32[]{:S(2)}) collective-permute-start(bf16[4,64,256]{2,1,0:T(8,128)(2,1)S(1)} %get-tuple-element.42), channel_id=1, source_target_pairs={{0,16},{4,20},{8,24},{12,28},{16,0},{20,4},{24,8},{28,12},{1,17},{... | collective-permute-start | bytes 393224 | tf_op jit(solution)/shard_map/ppermute | solution.py:335
  234.5 8.6 %collective-permute-start.21 = (bf16[4,64,256]{2,1,0:T(8,128)(2,1)S(1)}, bf16[4,64,256]{2,1,0:T(8,128)(2,1)S(1)}, u32[]{:S(2)}, u32[]{:S(2)}) collective-permute-start(bf16[4,64,256]{2,1,0:T(8,128)(2,1)S(1)} %get-tuple-element.43), channel_id=1, source_target_pairs={{0,24},{4,28},{8,16},{12,20},{16,8},{20,12},{24,0},{28,4},{1,25},{... | collective-permute-start | bytes 393224 | tf_op jit(solution)/shard_map/ppermute | solution.py:335
  236.0 8.8 %collective-permute-start.11 = (bf16[4,64,256]{2,1,0:T(8,128)(2,1)S(1)}, bf16[4,64,256]{2,1,0:T(8,128)(2,1)S(1)}, u32[]{:S(2)}, u32[]{:S(2)}) collective-permute-start(bf16[4,64,256]{2,1,0:T(8,128)(2,1)S(1)} %get-tuple-element.36), channel_id=1, source_target_pairs={{0,8},{4,12},{8,0},{12,4},{16,24},{20,28},{24,16},{28,20},{1,9},{5... | collective-permute-start | bytes 393224 | tf_op jit(solution)/shard_map/ppermute | solution.py:335
  238.8 7.8 %collective-permute-start.12 = (bf16[4,64,256]{2,1,0:T(8,128)(2,1)S(1)}, bf16[4,64,256]{2,1,0:T(8,128)(2,1)S(1)}, u32[]{:S(2)}, u32[]{:S(2)}) collective-permute-start(bf16[4,64,256]{2,1,0:T(8,128)(2,1)S(1)} %get-tuple-element.37), channel_id=1, source_target_pairs={{0,16},{4,20},{8,24},{12,28},{16,0},{20,4},{24,8},{28,12},{1,17},{... | collective-permute-start | bytes 393224 | tf_op jit(solution)/shard_map/ppermute | solution.py:335
  243.1 7.4 %collective-permute-start.13 = (bf16[4,64,256]{2,1,0:T(8,128)(2,1)S(1)}, bf16[4,64,256]{2,1,0:T(8,128)(2,1)S(1)}, u32[]{:S(2)}, u32[]{:S(2)}) collective-permute-start(bf16[4,64,256]{2,1,0:T(8,128)(2,1)S(1)} %get-tuple-element.38), channel_id=1, source_target_pairs={{0,24},{4,28},{8,16},{12,20},{16,8},{20,12},{24,0},{28,4},{1,25},{... | collective-permute-start | bytes 393224 | tf_op jit(solution)/shard_map/ppermute | solution.py:335
  243.1 7.9 %collective-permute-start.28 = (bf16[4,64,256]{2,1,0:T(8,128)(2,1)}, bf16[4,64,256]{2,1,0:T(8,128)(2,1)S(1)}, u32[]{:S(2)}, u32[]{:S(2)}) collective-permute-start(bf16[4,64,256]{2,1,0:T(8,128)(2,1)} %get-tuple-element.47), channel_id=1, source_target_pairs={{0,8},{4,12},{8,0},{12,4},{16,24},{20,28},{24,16},{28,20},{1,9},{5... | collective-permute-start | bytes 393224 | tf_op jit(solution)/shard_map/ppermute | solution.py:335
  244.8 9.1 %collective-permute-start.29 = (bf16[4,64,256]{2,1,0:T(8,128)(2,1)S(1)}, bf16[4,64,256]{2,1,0:T(8,128)(2,1)S(1)}, u32[]{:S(2)}, u32[]{:S(2)}) collective-permute-start(bf16[4,64,256]{2,1,0:T(8,128)(2,1)S(1)} %get-tuple-element.48), channel_id=1, source_target_pairs={{0,16},{4,20},{8,24},{12,28},{16,0},{20,4},{24,8},{28,12},{1,17},{... | collective-permute-start | bytes 393224 | tf_op jit(solution)/shard_map/ppermute | solution.py:335
  246.6 10.3 %collective-permute-start.30 = (bf16[4,64,256]{2,1,0:T(8,128)(2,1)S(1)}, bf16[4,64,256]{2,1,0:T(8,128)(2,1)S(1)}, u32[]{:S(2)}, u32[]{:S(2)}) collective-permute-start(bf16[4,64,256]{2,1,0:T(8,128)(2,1)S(1)} %get-tuple-element.49), channel_id=1, source_target_pairs={{0,24},{4,28},{8,16},{12,20},{16,8},{20,12},{24,0},{28,4},{1,25},{... | collective-permute-start | bytes 393224 | tf_op jit(solution)/shard_map/ppermute | solution.py:335
  250.6 11.9 %collective-permute-start.37 = (bf16[4,64,256]{2,1,0:T(8,128)(2,1)}, bf16[4,64,256]{2,1,0:T(8,128)(2,1)S(1)}, u32[]{:S(2)}, u32[]{:S(2)}) collective-permute-start(bf16[4,64,256]{2,1,0:T(8,128)(2,1)} %get-tuple-element.53), channel_id=1, source_target_pairs={{0,8},{4,12},{8,0},{12,4},{16,24},{20,28},{24,16},{28,20},{1,9},{5... | collective-permute-start | bytes 393224 | tf_op jit(solution)/shard_map/ppermute | solution.py:335
  251.0 11.6 %collective-permute-start.38 = (bf16[4,64,256]{2,1,0:T(8,128)(2,1)S(1)}, bf16[4,64,256]{2,1,0:T(8,128)(2,1)S(1)}, u32[]{:S(2)}, u32[]{:S(2)}) collective-permute-start(bf16[4,64,256]{2,1,0:T(8,128)(2,1)S(1)} %get-tuple-element.54), channel_id=1, source_target_pairs={{0,16},{4,20},{8,24},{12,28},{16,0},{20,4},{24,8},{28,12},{1,17},{... | collective-permute-start | bytes 393224 | tf_op jit(solution)/shard_map/ppermute | solution.py:335
  253.9 8.7 %collective-permute-start.39 = (bf16[4,64,256]{2,1,0:T(8,128)(2,1)S(1)}, bf16[4,64,256]{2,1,0:T(8,128)(2,1)S(1)}, u32[]{:S(2)}, u32[]{:S(2)}) collective-permute-start(bf16[4,64,256]{2,1,0:T(8,128)(2,1)S(1)} %get-tuple-element.55), channel_id=1, source_target_pairs={{0,24},{4,28},{8,16},{12,20},{16,8},{20,12},{24,0},{28,4},{1,25},{... | collective-permute-start | bytes 393224 | tf_op jit(solution)/shard_map/ppermute | solution.py:335
  257.0 10.5 %collective-permute-start.22 = (f32[4,128]{1,0:T(4,128)S(1)}, f32[4,128]{1,0:T(4,128)S(1)}, u32[]{:S(2)}, u32[]{:S(2)}) collective-permute-start(f32[4,128]{1,0:T(4,128)S(1)} %get-tuple-element.45), channel_id=1, source_target_pairs={{0,3},{1,0},{2,1},{3,2},{4,7},{5,4},{6,5},{7,6},{8,11},{9,8},{10,9... | collective-permute-start | bytes 6152 | tf_op jit(solution)/shard_map/ppermute | solution.py:338
  262.5 5.0 %collective-permute-start.31 = (f32[4,128]{1,0:T(4,128)S(1)}, f32[4,128]{1,0:T(4,128)S(1)}, u32[]{:S(2)}, u32[]{:S(2)}) collective-permute-start(f32[4,128]{1,0:T(4,128)S(1)} %get-tuple-element.51), channel_id=1, source_target_pairs={{0,2},{1,3},{2,0},{3,1},{4,6},{5,7},{6,4},{7,5},{8,10},{9,11},{10,... | collective-permute-start | bytes 6152 | tf_op jit(solution)/shard_map/ppermute | solution.py:338
  263.4 5.4 %collective-permute-start.40 = (f32[4,128]{1,0:T(4,128)S(1)}, f32[4,128]{1,0:T(4,128)S(1)}, u32[]{:S(2)}, u32[]{:S(2)}) collective-permute-start(f32[4,128]{1,0:T(4,128)S(1)} %get-tuple-element.57), channel_id=1, source_target_pairs={{0,1},{1,2},{2,3},{3,0},{4,5},{5,6},{6,7},{7,4},{8,9},{9,10},{10,1... | collective-permute-start | bytes 6152 | tf_op jit(solution)/shard_map/ppermute | solution.py:338
  264.4 4.5 %copy-start.7 = (f32[128,4]{0,1:T(4,128)S(1)}, f32[128,4]{0,1:T(4,128)}, u32[]{:S(2)}) copy-start(f32[128,4]{0,1:T(4,128)} %param.7) | copy-start | bytes 6148
  264.5 4.5 %copy-start.10 = (f32[128]{0:T(128)S(1)}, f32[128]{0:T(128)}, u32[]{:S(2)}) copy-start(f32[128]{0:T(128)} %copy-done.9) | copy-start | bytes 1540
  264.5 5.1 %copy-start.1 = (bf16[512,3584]{1,0:T(8,128)(2,1)S(1)}, bf16[512,3584]{1,0:T(8,128)(2,1)}, u32[]{:S(2)}) copy-start(bf16[512,3584]{1,0:T(8,128)(2,1)} %copy-done) | copy-start | bytes 11010052
  (7 other events, 20.8 us)

commit v3 on v2

--- a/solution.py
+++ b/solution.py
@@ -73,7 +73,7 @@
 SLOT_PAD = 64
 F32 = jnp.float32
 BF16 = jnp.bfloat16
-VMEM_BYTES = 40 * 2**20
+VMEM_BYTES = 24 * 2**20
 
 
 def nt_dot(a, b):
@@ -86,10 +86,10 @@
 
 def project_kernel(top_k, sizes, idx_ref, *refs):
     parts = len(sizes)
-    pieces, (weight_ref,) = refs[:parts], refs[parts : parts + 1]
-    hidden_refs = refs[parts + 1 : parts + 5]
-    grad_refs = refs[parts + 5 : parts + 9]
-    scatter_ref, rows_out, rows, sems, out_sem = refs[parts + 9 :]
+    pieces, (own_weight, partner_weight) = refs[:parts], refs[parts : parts + 2]
+    hidden_refs = refs[parts + 2 : parts + 6]
+    grad_refs = refs[parts + 6 : parts + 10]
+    scatter_ref, rows_out, rows, weight, terms, sems, out_sem = refs[parts + 10 :]
     e = pl.program_id(0)
     slots, pair = grad_refs[0].shape[1:]
     tokens = rows.shape[0] // 4
@@ -108,7 +108,11 @@
             copy.wait()
         store.start()
 
-    projected = nt_dot(weight_ref[...], rows[...])
+    block = pair // 2
+    core = idx_ref[2]
+    weight[pl.ds(pl.multiple_of(core * block, block), block), :] = own_weight[...]
+    weight[pl.ds(pl.multiple_of((1 - core) * block, block), block), :] = partner_weight[...]
+    projected = nt_dot(weight[...], rows[...])
     earlier = (
         lax.broadcasted_iota(jnp.int32, (tokens, tokens), 0)
         < lax.broadcasted_iota(jnp.int32, (tokens, tokens), 1)
@@ -139,18 +143,25 @@
         grad_refs[m][0] = jnp.where(slot_rows == slots - top_k, partial, grad).astype(BF16)
         scatter = (scale * hidden).astype(BF16)
         for half in range(2):
-            scatter_ref[half, :, m * tokens : (m + 1) * tokens] = scatter[
-                half * (pair // 2) : (half + 1) * (pair // 2)
-            ]
+            terms[half, pl.ds(pl.multiple_of(e * block, block), block), m * tokens : (m + 1) * tokens] = (
+                scatter[half * block : (half + 1) * block]
+            )
 
     @pl.when(e == pl.num_programs(0) - 1)
     def _():
+        height = terms.shape[1]
+        experts = height // block
+        row = lax.broadcasted_iota(jnp.int32, (height, height), 0)
+        col = lax.broadcasted_iota(jnp.int32, (height, height), 1)
+        order = (col == lax.rem(row, experts) * block + lax.div(row, experts)).astype(BF16)
+        for half in range(2):
+            scatter_ref[half] = jnp.dot(order, terms[half], preferred_element_type=F32).astype(BF16)
         store.wait()
 
 
-def project(index, pieces, weight, hidden, top_k):
+def project(index, pieces, own_weight, partner_weight, hidden, top_k):
     experts, sources, slots, pair = hidden[0].shape
-    width = weight.shape[1]
+    width = own_weight.shape[1]
     sizes = [p.shape[0] for p in pieces]
     count = sum(sizes)
     block = pair // 2
@@ -160,15 +171,17 @@
             num_scalar_prefetch=1,
             grid=(experts,),
             in_specs=[pl.BlockSpec(memory_space=pl.ANY)] * len(sizes)
-            + [pl.BlockSpec((pair, width), lambda e, idx: (e, 0))]
+            + [pl.BlockSpec((block, width), lambda e, idx: (e, 0))] * 2
             + [pl.BlockSpec((1, 1, slots, pair), lambda e, idx: (e, idx[0], 0, 0))] * 4,
             out_specs=[pl.BlockSpec((1, slots, pair), lambda e, idx: (e, 0, 0))] * 4
             + [
-                pl.BlockSpec((2, block, count), lambda e, idx: (0, e, 0)),
+                pl.BlockSpec((2, experts * block, count), lambda e, idx: (0, 0, 0)),
                 pl.BlockSpec(memory_space=pl.ANY),
             ],
             scratch_shapes=[
                 pltpu.VMEM((count, width), BF16),
+                pltpu.VMEM((pair, width), BF16),
+                pltpu.VMEM((2, experts * block, count), BF16),
                 pltpu.SemaphoreType.DMA((len(sizes),)),
                 pltpu.SemaphoreType.DMA,
             ],
@@ -181,10 +194,10 @@
         compiler_params=pltpu.CompilerParams(vmem_limit_bytes=VMEM_BYTES),
         cost_estimate=pl.CostEstimate(
             flops=4 * count * width * experts * pair,
-            bytes_accessed=2 * (2 * count * width + weight.size),
+            bytes_accessed=2 * (2 * count * width + 2 * own_weight.size),
             transcendentals=0,
         ),
-    )(index, *pieces, weight, *hidden)
+    )(index, *pieces, own_weight, partner_weight, *hidden)
 
 
 def early_grad_kernel(terms, *refs):
@@ -226,12 +239,15 @@
     total += arrived_ref[...].astype(F32)
     block, experts, _ = out_ref.shape
     held[...] = total
-
-    def move(h, carry):
-        out_ref[h] = jnp.concatenate([held[pl.ds(e * block + h, 1), :] for e in range(experts)], axis=0)
+    group = 8 // experts
+
+    def move(i, carry):
+        both = held[pl.ds(pl.multiple_of(i * 8, 8), 8), :]
+        for j in range(group):
+            out_ref[i * group + j] = both[j * experts : (j + 1) * experts]
         return carry
 
-    lax.fori_loop(0, block, move, 0, unroll=8)
+    lax.fori_loop(0, block // group, move, 0, unroll=4)
 
 
 def late_grad(index, scatter, rows, before, arrived, experts, tile):
@@ -337,69 +353,71 @@
     def around(array, shift):
         return lax.ppermute(array, "exp", [(i, (i + shift) % sources) for i in range(sources)])
 
+    def after(array, other):
+        return lax.optimization_barrier((array, other))[0]
+
     totals = jnp.sum(affinity, axis=-1, keepdims=True)
     shares = affinity / totals
     route_weight = (ROUTE_SCALE * shares).astype(BF16)
     meta = jnp.concatenate([routes.astype(BF16).T, route_weight.T], axis=1)
     metas = jnp.stack([meta] + [around(meta, shift) for shift in range(1, sources)])
+    carried = after(grad_out, metas)
     metas = jnp.take(metas, lax.rem(me - jnp.arange(sources) + sources, sources), axis=0)
     blank = jnp.zeros((experts, sources, SLOT_PAD - most - top_k, pair), BF16)
     metas = jnp.broadcast_to(metas[None], (experts, sources, top_k, pair))
 
     held = saved_hidden.reshape(experts, sources, most, 4, pair)
-    held = jnp.transpose(held, (3, 0, 1, 2, 4))
+    held = lax.optimization_barrier(jnp.transpose(held, (3, 0, 1, 2, 4)))
     hidden = []
     for m in range(4):
         piece = lax.dynamic_index_in_dim(held, chips[m], axis=0, keepdims=False)
         piece = jnp.concatenate([piece, blank, metas], axis=2)
         hidden.append(across(piece, 2 * m) if m else piece)
 
-    own_weight = jnp.transpose(down_proj, (1, 0, 2))
+    own_weight = jnp.transpose(down_proj, (1, 0, 2)).reshape(experts * block, width)
+    own_weight = lax.optimization_barrier(own_weight)
     partner_weight = across(own_weight, 1)
-    weight = jnp.concatenate(
-        [
-            jnp.where(core == 0, own_weight, partner_weight),
-            jnp.where(core == 0, partner_weight, own_weight),
-        ],
-        axis=1,
-    ).reshape(experts * pair, width)
-
-    carried = grad_out
+
     half = tokens // 2
-    scatters, rows, returned, indices = [], [], [], []
-    before = None
+    shards = [grad_out]
+    for step in range(1, sources):
+        carried = around(carried, 1)
+        shards.append(carried)
+    scatters, rows, returned, indices, placed, combines = [], [], [], [], [None], []
     for step in range(sources):
-        from_x, from_y = across(carried, 2), across(carried, 4)
-        own = carried
-        if step < sources - 1:
-            carried = around(carried, 1)
+        own = shards[step]
+        sent = own if step < 2 else after(own, scatters[step - 2])
+        from_x, from_y = across(sent, 2), across(sent, 4)
         top, bottom = across(from_x[:half], 4), across(from_y[half:], 2)
         source = lax.rem(me - step + sources, sources)
-        index = jnp.stack([source, me * experts]).astype(jnp.int32)
+        index = jnp.stack([source, me * experts, core]).astype(jnp.int32)
+        if step >= 2:
+            own = after(own, combines[step - 2])
+        if step == sources - 1:
+            before = early_grad(scatters, rows, 512)
+            own = after(own, before)
         *grads, scatter, row = project(
-            index, [own, from_x, from_y, top, bottom], weight, hidden, top_k
+            index, [own, from_x, from_y, top, bottom], own_weight, partner_weight, hidden, top_k
         )
         scatters.append(scatter)
         rows.append(row)
-        returned.append([grads[0]] + [across(grads[m], 2 * m) for m in range(1, 4)])
-        indices.append(jnp.stack([source] + chips).astype(jnp.int32))
-        if step == sources - 2:
-            before = early_grad(scatters, rows, 512)
-    partner = late_grad((1 - core).reshape(1), scatters[-1], rows[-1], before, None, experts, 512)
+        returned = [grads[0]] + [across(grads[m], 2 * m) for m in range(1, 4)]
+        indices = jnp.stack([source] + chips).astype(jnp.int32)
+        spot, combine = place(indices, returned, placed[-1], sources, top_k)
+        placed.append(spot)
+        combines.append(around(combine, -step) if step else combine)
+    partner = late_grad((1 - core).reshape(1), scatters[-1], rows[-1], before, None, experts, 896)
     partner = across(partner, 1)
-    placed, route_grad = None, 0.0
+    route_grad = 0.0
     expert_ids = jnp.arange(experts, dtype=routes.dtype)
     for step in range(sources):
-        placed, combine = place(indices[step], returned[step], placed, sources, top_k)
-        if step:
-            combine = around(combine, -step)
         ids = lax.rem(me + step, sources) * experts + expert_ids
         named = routes.T[:, None, :] == ids[None, :, None]
-        route_grad += jnp.sum(jnp.where(named, combine[None], 0.0), axis=1)
-    hidden_grad = jnp.transpose(placed[:, :, :most], (1, 0, 2, 3)).reshape(saved_hidden.shape)
+        route_grad += jnp.sum(jnp.where(named, combines[step][None], 0.0), axis=1)
+    hidden_grad = jnp.transpose(placed[-1][:, :, :most], (1, 0, 2, 3)).reshape(saved_hidden.shape)
     route_grad = ROUTE_SCALE * route_grad.T
     affinity_grad = (route_grad - jnp.sum(route_grad * shares, axis=-1, keepdims=True)) / totals
-    down_grad = late_grad(core.reshape(1), scatters[-1], rows[-1], before, partner, experts, 512)
+    down_grad = late_grad(core.reshape(1), scatters[-1], rows[-1], before, partner, experts, 896)
     return (affinity_grad, hidden_grad, down_grad)
 
 
@@ -408,7 +426,7 @@
     block, experts, width = down_proj.shape
     tokens, top_k = routes.shape
     most = saved_hidden.shape[3]
-    fits = block == 128 and tokens == 128 and width % 512 == 0 and reps == 8
+    fits = block == 128 and tokens == 128 and width % 3584 == 0 and reps == 8 and 8 % experts == 0
     fits = fits and sources > 1 and most + top_k <= SLOT_PAD and top_k <= 8
     if fits and sources * tokens <= 2 * block * experts:
         return on_device_tokens(grad_out, routes, affinity, saved_hidden, down_proj)

time: 284 us -> 305 us (1.074)
  other arithmetic: 22.4 us -> 4.16 us
  waiting for transfers between devices: 77.1 us -> 95 us
  local copies, waits for them, and re-layouts: 43.3 us -> 60.6 us
  starting transfers between devices: 51.8 us -> 55.2 us
    ppermute x33, waiting for transfers between devices: 58.9 us -> 92.2 us  [across(): return lax.ppermute(array, 'rep', [(i, i ^ bits) for i in range(reps)])]
    unnamed x27 -> x127, local copies, waits for them, and re-layouts: 10.5 us -> 43.2 us
    ppermute x9, waiting for transfers between devices: 18.2 us -> 2.78 us  [around(): lax.ppermute(array, 'exp', [(i, (i + shift) % sources) for i in range(sou...]
    pallas_call x2, Pallas kernels: 22.5 us -> 12.3 us  [late_grad(): pl.pallas_call(kernel, grid_spec=pltpu.PrefetchScalarGridSpec(num_scalar_...]
    select_n x1 -> x0, other arithmetic: 9.23 us -> none  [on_device_tokens(): jnp.where(core == 0, own_weight, partner_weight)]
    another operation x5 -> x4, local copies, waits for them, and re-layouts: 9.16 us -> 0.33 us  [on_device_tokens(): indices = jnp.stack([source] + chips).astype(jnp.int32)]
    pallas_call x4, Pallas kernels: 46.9 us -> 54.7 us  [project(): pl.pallas_call(functools.partial(project_kernel, top_k, sizes), grid_spec...]
    concatenate x1 -> x0, other arithmetic: 7.52 us -> none  [on_device_tokens(): jnp.concatenate([jnp.where(core == 0, own_weight, partner_weight), jnp.wh...]
  transfers between devices with their start and end apart: 42 -> 42, of which waited for: 13 -> 15; matrix products, arithmetic and copies ran while one was open for 21% -> 6% of each run, Pallas kernels for 19% -> 20%
where the time goes in v3:
time: 305 us; the launch traced here: 304 us
  waiting for transfers between devices  95 us (31%)
  Pallas kernels  87.9 us (29%)
  local copies, waits for them, and re-layouts  60.6 us (20%)
  starting transfers between devices  55.2 us (18%)
  other arithmetic  4.16 us (1%)
    ppermute x33, waiting for transfers between devices, across(): return lax.ppermute(array, 'rep', [(i, i ^ bits) for i in range(reps)])  92.2 us
    pallas_call x4, Pallas kernels, project(): pl.pallas_call(functools.partial(project_kernel, top_k, sizes), grid_spec...  54.7 us
    unnamed x127, local copies, waits for them, and re-layouts  43.2 us
    ppermute x33, starting transfers between devices, across(): return lax.ppermute(array, 'rep', [(i, i ^ bits) for i in range(reps)])  39.2 us
    ppermute x9, starting transfers between devices, around(): lax.ppermute(array, 'exp', [(i, (i + shift) % sources) for i in range(sou...  15.9 us
    pallas_call x1, Pallas kernels, early_grad(): pl.pallas_call(functools.partial(early_grad_kernel, terms), grid=(width /...  14.2 us
    pallas_call x2, Pallas kernels, late_grad(): pl.pallas_call(kernel, grid_spec=pltpu.PrefetchScalarGridSpec(num_scalar_...  12.3 us
    pallas_call x4, Pallas kernels, place(): pl.pallas_call(functools.partial(place_kernel, top_k, first), grid_spec=p...  6.62 us
  transfers between devices with their start and end apart: 42, of which 15 were waited for; matrix products, arithmetic and copies ran while one was open for 6% of the time, Pallas kernels for 20%

profile of v3, /device:TPU:0, one launch (start us, length us, event | category | flops | bytes accessed | tf_op | source)
XLA Modules:
  0.0 304.0 jit_solution(17462494390347286182)
XLA Ops:
  0.7 4.6 %copy.14 = bf16[4,128,3584]{2,1,0:T(8,128)(2,1)} copy(bf16[4,128,3584]{2,0,1:T(4,128)(2,1)} %bitcast.50) | data formatting | bytes 7340032 | tf_op jit(solution)/shard_map/transpose | solution.py:377
  5.8 4.7 %collective-permute-start.7 = (bf16[4,256]{1,0:T(4,128)(2,1)S(1)}, bf16[4,256]{1,0:T(4,128)(2,1)S(1)}, u32[]{:S(2)}, u32[]{:S(2)}) collective-permute-start(bf16[4,256]{1,0:T(4,128)(2,1)S(1)} %get-tuple-element.100), channel_id=1, source_target_pairs={{0,3},{1,0},{2,1},{3,2},{4,7},{5,4},{6,5},{7,6},{8,11},{9,8},{10,9... | collective-permute-start | bytes 6152 | tf_op jit(solution)/shard_map/ppermute | solution.py:354
  11.5 2.2 reshape.88
  13.7 2.2 copy.18
  17.2 2.5 collective-permute-start.14
  20.4 2.4 pad_maximum_fusion
  22.8 1.5 collective-permute-start.8
  24.3 1.5 collective-permute-start.9
  26.3 11.3 %collective-permute-done.8.refs_8_ = bf16[4,4,64,256]{3,2,1,0:T(8,128)(2,1)S(1)} collective-permute-done((bf16[4,4,64,256]{3,2,1,0:T(8,128)(2,1)S(1)}, bf16[4,4,64,256]{3,2,1,0:T(8,128)(2,1)S(1)}, u32[]{:S(2)}, u32[]{:S(2)}) %collective-permute-start.8) | collective-permute-done | bytes 524320 | tf_op jit(solution)/shard_map/ppermute | solution.py:351
  38.5 1.5 collective-permute-start.1
  43.6 1.5 collective-permute-start.16
  45.1 12.2 %collective-permute-done.refs_1_ = bf16[128,3584]{1,0:T(8,128)(2,1)S(1)} collective-permute-done((bf16[128,3584]{1,0:T(8,128)(2,1)}, bf16[128,3584]{1,0:T(8,128)(2,1)S(1)}, u32[]{:S(2)}, u32[]{:S(2)}) %collective-permute-start) | collective-permute-done | bytes 917536 | tf_op jit(solution)/shard_map/ppermute | solution.py:351
  57.3 4.6 %collective-permute-done.1.refs_2_ = bf16[128,3584]{1,0:T(8,128)(2,1)S(1)} collective-permute-done((bf16[128,3584]{1,0:T(8,128)(2,1)}, bf16[128,3584]{1,0:T(8,128)(2,1)S(1)}, u32[]{:S(2)}, u32[]{:S(2)}) %collective-permute-start.1) | collective-permute-done | bytes 917536 | tf_op jit(solution)/shard_map/ppermute | solution.py:351
  62.0 2.4 collective-permute-start.10
  65.2 11.8 %collective-permute-done.15.refs_1_ = bf16[128,3584]{1,0:T(8,128)(2,1)S(1)} collective-permute-done((bf16[128,3584]{1,0:T(8,128)(2,1)}, bf16[128,3584]{1,0:T(8,128)(2,1)S(1)}, u32[]{:S(2)}, u32[]{:S(2)}) %collective-permute-start.15) | collective-permute-done | bytes 917536 | tf_op jit(solution)/shard_map/ppermute | solution.py:351
  77.0 1.5 collective-permute-start.2
  79.3 11.2 %collective-permute-done.16.refs_2_ = bf16[128,3584]{1,0:T(8,128)(2,1)S(1)} collective-permute-done((bf16[128,3584]{1,0:T(8,128)(2,1)}, bf16[128,3584]{1,0:T(8,128)(2,1)S(1)}, u32[]{:S(2)}, u32[]{:S(2)}) %collective-permute-start.16) | collective-permute-done | bytes 917536 | tf_op jit(solution)/shard_map/ppermute | solution.py:351
  90.5 1.5 collective-permute-start.3
  92.3 2.1 collective-permute-start.17
  94.4 6.1 %collective-permute-done.2.refs_3_ = bf16[64,3584]{1,0:T(8,128)(2,1)} collective-permute-done((bf16[64,3584]{1,0:T(8,128)(2,1)}, bf16[64,3584]{1,0:T(8,128)(2,1)}, u32[]{:S(2)}, u32[]{:S(2)}) %collective-permute-start.2) | collective-permute-done | bytes 458784 | tf_op jit(solution)/shard_map/ppermute | solution.py:351
  105.8 12.5 %shard_map.76 = (bf16[4,64,256]{2,1,0:T(8,128)(2,1)S(1)}, bf16[4,64,256]{2,1,0:T(8,128)(2,1)S(1)}, bf16[4,64,256]{2,1,0:T(8,128)(2,1)S(1)}, bf16[4,64,256]{2,1,0...) custom-call(s32[3]{0:T(128)S(1)} %add_add_fusion.idx_ref, bf16[128,3584]{1,0:T(8,128)(2,1)} %refs_0_.1, ...), custom_call_target="tpu_custom_call" | custom-call | flops 7516192768 | bytes 14680064 | tf_op jit(solution)/shard_map/pallas_call | solution.py:168
  119.0 1.8 copy-done.43
  122.4 2.1 collective-permute-start.25
  124.5 12.7 %shard_map.78 = (bf16[4,64,256]{2,1,0:T(8,128)(2,1)S(1)}, bf16[4,64,256]{2,1,0:T(8,128)(2,1)S(1)}, bf16[4,64,256]{2,1,0:T(8,128)(2,1)S(1)}, bf16[4,64,256]{2,1,0...) custom-call(s32[3]{0:T(128)S(1)} %add_add_fusion.1.idx_ref, ...), custom_call_target="tpu_custom_call" | custom-call | flops 7516192768 | bytes 14680064 | tf_op jit(solution)/shard_map/pallas_call | solution.py:168
  137.9 1.9 copy-done.45
  140.8 1.5 collective-permute-start.33
  142.8 19.9 %collective-permute-done.19.refs_1_ = bf16[4,64,256]{2,1,0:T(8,128)(2,1)S(1)} collective-permute-done((bf16[4,64,256]{2,1,0:T(8,128)(2,1)S(1)}, bf16[4,64,256]{2,1,0:T(8,128)(2,1)S(1)}, u32[]{:S(2)}, u32[]{:S(2)}) %collective-permute-start.19) | collective-permute-done | bytes 131104 | tf_op jit(solution)/shard_map/ppermute | solution.py:351
  173.1 2.0 collective-permute-start.13
  175.1 8.8 %collective-permute-done.13.refs_3_ = bf16[4,64,256]{2,1,0:T(8,128)(2,1)S(1)} collective-permute-done((bf16[4,64,256]{2,1,0:T(8,128)(2,1)S(1)}, bf16[4,64,256]{2,1,0:T(8,128)(2,1)S(1)}, u32[]{:S(2)}, u32[]{:S(2)}) %collective-permute-start.13) | collective-permute-done | bytes 131104 | tf_op jit(solution)/shard_map/ppermute | solution.py:351
  193.5 2.3 shard_map.79
  195.8 3.3 %collective-permute-start.22 = (f32[4,128]{1,0:T(4,128)}, f32[4,128]{1,0:T(4,128)S(1)}, u32[]{:S(2)}, u32[]{:S(2)}) collective-permute-start(f32[4,128]{1,0:T(4,128)} %get-tuple-element.52), channel_id=1, source_target_pairs={{0,3},{1,0},{2,1},{3,2},{4,7},{5,4},{6,5},{7,6},{8,11},{9,8},{10,9... | collective-permute-start | bytes 6152 | tf_op jit(solution)/shard_map/ppermute | solution.py:354
  202.5 1.8 slice.45
  209.9 13.3 %shard_map.80 = (bf16[4,64,256]{2,1,0:T(8,128)(2,1)S(1)}, bf16[4,64,256]{2,1,0:T(8,128)(2,1)}, bf16[4,64,256]{2,1,0:T(8,128)(2,1)}, bf16[4,64,256]{2,1,0:T(8,128...) custom-call(s32[3]{0:T(128)S(1)} %add_add_fusion.2.idx_ref, ...), custom_call_target="tpu_custom_call" | custom-call | flops 7516192768 | bytes 14680064 | tf_op jit(solution)/shard_map/pallas_call | solution.py:168
  225.5 2.0 copy-done.44
  227.5 2.0 copy-done.46
  230.8 14.2 %shard_map.82.before_ref = f32[2,512,3584]{2,1,0:T(8,128)S(1)} custom-call(bf16[2,512,512]{2,1,0:T(8,128)(2,1)S(1)} %copy-done.48, bf16[2,512,512]{2,1,0:T(8,128)(2,1)S(1)} %copy-done.50, bf16[2,512,512]{2,1,0:T(8,128)(2,1)S(1)} %copy-done.52, bf16[512,3584]{1,0:T(8,128)(2,1)S(1)} %copy-done.44, bf16[512,3584]{1,0:T(8,128)(2,1)S(1)} %copy-done.46, ...), custom_call_target="tpu_custom_call" | custom-call | flops 11274289152 | bytes 28835840 | tf_op jit(solution)/shard_map/pallas_call | solution.py:216
  245.1 16.2 %shard_map.83 = (bf16[4,64,256]{2,1,0:T(8,128)(2,1)S(1)}, bf16[4,64,256]{2,1,0:T(8,128)(2,1)S(1)}, bf16[4,64,256]{2,1,0:T(8,128)(2,1)S(1)}, bf16[4,64,256]{2,1,0...) custom-call(s32[3]{0:T(128)S(1)} %add_add_fusion.3.idx_ref, ...), custom_call_target="tpu_custom_call" | custom-call | flops 7516192768 | bytes 14680064 | tf_op jit(solution)/shard_map/pallas_call | solution.py:168
  262.0 4.8 %shard_map.85 = bf16[512,3584]{1,0:T(8,128)(2,1)} custom-call(s32[1]{0:T(128)} %bitcast.28.idx_ref, bf16[2,512,512]{2,1,0:T(8,128)(2,1)S(1)} %get-tuple-element.77.scatter_ref, bf16[512,3584]{1,0:T(8,128)(2,1)S(1)} %get-tuple-element.78.rows_ref, f32[2,512,3584]{2,1,0:T(8,128)S(1)} %shard_map.82.before_ref), custom_call_target="tpu_custom_call" | custom-call | flops 1879048192 | bytes 19398656 | tf_op jit(solution)/shard_map/pallas_call | solution.py:272
  268.9 1.5 collective-permute-start.30
  271.4 2.0 collective-permute-done.28.refs_1_
  274.4 2.0 collective-permute-done.29.refs_2_
  276.4 1.8 collective-permute-start.39
  279.0 1.8 shard_map.81
  282.6 1.8 shard_map.84
  284.4 3.0 collective-permute-start.40
  287.7 2.8 copy.16
  291.3 5.2 %copy-done.1 = f32[2,512,3584]{2,1,0:T(8,128)S(1)} copy-done((f32[2,512,3584]{2,1,0:T(8,128)S(1)}, f32[2,512,3584]{2,1,0:T(8,128)}, u32[]{:S(2)}) %copy-start.1) | copy-done | bytes 14680088
  296.4 7.6 %shard_map.86 = f32[128,4,3584]{2,1,0:T(4,128)} custom-call(s32[1]{0:T(128)} %bitcast.7.idx_ref, bf16[2,512,512]{2,1,0:T(8,128)(2,1)S(1)} %get-tuple-element.77.scatter_ref, bf16[512,3584]{1,0:T(8,128)(2,1)S(1)} %copy-done.3, f32[2,512,3584]{2,1,0:T(8,128)S(1)} %copy-done.1, bf16[512,3584]{1,0:T(8,128)(2,1)} %collective-permute-done.41.arrived_ref), custom_call_target="tpu_custom_call" | custom-call | flops 1879048192 | bytes 19398656 | tf_op jit(solution)/shard_map/pallas_call | solution.py:272
  (212 shorter events, 60.7 us)
Async XLA Ops:
  5.3 97.3 %collective-permute-start.4 = (bf16[512,3584]{1,0:T(8,128)(2,1)}, bf16[512,3584]{1,0:T(8,128)(2,1)}, u32[]{:S(2)}, u32[]{:S(2)}) collective-permute-start(bf16[512,3584]{1,0:T(8,128)(2,1)} %bitcast.9.refs_5_), channel_id=1, source_target_pairs={{0,4},{4,0},{8,12},{12,8},{16,20},{20,16},{24,28},{28,24},{1,5},{5... | collective-permute-start | bytes 11010056 | tf_op jit(solution)/shard_map/ppermute | solution.py:351
  5.8 11.4 %collective-permute-start.7 = (bf16[4,256]{1,0:T(4,128)(2,1)S(1)}, bf16[4,256]{1,0:T(4,128)(2,1)S(1)}, u32[]{:S(2)}, u32[]{:S(2)}) collective-permute-start(bf16[4,256]{1,0:T(4,128)(2,1)S(1)} %get-tuple-element.100), channel_id=1, source_target_pairs={{0,3},{1,0},{2,1},{3,2},{4,7},{5,4},{6,5},{7,6},{8,11},{9,8},{10,9... | collective-permute-start | bytes 6152 | tf_op jit(solution)/shard_map/ppermute | solution.py:354
  10.5 6.7 %collective-permute-start.6 = (bf16[4,256]{1,0:T(4,128)(2,1)S(1)}, bf16[4,256]{1,0:T(4,128)(2,1)S(1)}, u32[]{:S(2)}, u32[]{:S(2)}) collective-permute-start(bf16[4,256]{1,0:T(4,128)(2,1)S(1)} %get-tuple-element.100), channel_id=1, source_target_pairs={{0,2},{1,3},{2,0},{3,1},{4,6},{5,7},{6,4},{7,5},{8,10},{9,11},{10,... | collective-permute-start | bytes 6152 | tf_op jit(solution)/shard_map/ppermute | solution.py:354
  10.5 6.7 %collective-permute-start.5 = (bf16[4,256]{1,0:T(4,128)(2,1)S(1)}, bf16[4,256]{1,0:T(4,128)(2,1)S(1)}, u32[]{:S(2)}, u32[]{:S(2)}) collective-permute-start(bf16[4,256]{1,0:T(4,128)(2,1)S(1)} %get-tuple-element.100), channel_id=1, source_target_pairs={{0,1},{1,2},{2,3},{3,0},{4,5},{5,6},{6,7},{7,4},{8,9},{9,10},{10,1... | collective-permute-start | bytes 6152 | tf_op jit(solution)/shard_map/ppermute | solution.py:354
  17.2 24.1 %collective-permute-start.14 = (bf16[128,3584]{1,0:T(8,128)(2,1)}, bf16[128,3584]{1,0:T(8,128)(2,1)}, u32[]{:S(2)}, u32[]{:S(2)}) collective-permute-start(bf16[128,3584]{1,0:T(8,128)(2,1)} %refs_0_.1), channel_id=1, source_target_pairs={{0,1},{1,2},{2,3},{3,0},{4,5},{5,6},{6,7},{7,4},{8,9},{9,10},{10,1... | collective-permute-start | bytes 2752520 | tf_op jit(solution)/shard_map/ppermute | solution.py:354
  22.8 182.6 %copy-start.4 = (bf16[4,4,64,256]{3,2,1,0:T(8,128)(2,1)}, bf16[4,4,64,256]{3,2,1,0:T(8,128)(2,1)S(1)}, u32[]{:S(2)}) copy-start(bf16[4,4,64,256]{3,2,1,0:T(8,128)(2,1)S(1)} %get-tuple-element.98.refs_7_) | copy-start | bytes 1572868
  22.8 14.9 %collective-permute-start.8 = (bf16[4,4,64,256]{3,2,1,0:T(8,128)(2,1)S(1)}, bf16[4,4,64,256]{3,2,1,0:T(8,128)(2,1)S(1)}, u32[]{:S(2)}, u32[]{:S(2)}) collective-permute-start(bf16[4,4,64,256]{3,2,1,0:T(8,128)(2,1)S(1)} %get-tuple-element.96), channel_id=1, source_target_pairs={{0,8},{4,12},{8,0},{12,4},{16,24},{20,28},{24,16},{28,20},{1,9},{5... | collective-permute-start | bytes 1572872 | tf_op jit(solution)/shard_map/ppermute | solution.py:351
  24.3 18.5 %collective-permute-start.9 = (bf16[4,4,64,256]{3,2,1,0:T(8,128)(2,1)S(1)}, bf16[4,4,64,256]{3,2,1,0:T(8,128)(2,1)S(1)}, u32[]{:S(2)}, u32[]{:S(2)}) collective-permute-start(bf16[4,4,64,256]{3,2,1,0:T(8,128)(2,1)S(1)} %get-tuple-element.97), channel_id=1, source_target_pairs={{0,16},{4,20},{8,24},{12,28},{16,0},{20,4},{24,8},{28,12},{1,17},{... | collective-permute-start | bytes 1572872 | tf_op jit(solution)/shard_map/ppermute | solution.py:351
  25.8 31.5 %collective-permute-start = (bf16[128,3584]{1,0:T(8,128)(2,1)}, bf16[128,3584]{1,0:T(8,128)(2,1)S(1)}, u32[]{:S(2)}, u32[]{:S(2)}) collective-permute-start(bf16[128,3584]{1,0:T(8,128)(2,1)} %refs_0_.1), channel_id=1, source_target_pairs={{0,8},{4,12},{8,0},{12,4},{16,24},{20,28},{24,16},{28,20},{1,9},{5... | collective-permute-start | bytes 2752520 | tf_op jit(solution)/shard_map/ppermute | solution.py:351
  38.5 23.5 %collective-permute-start.1 = (bf16[128,3584]{1,0:T(8,128)(2,1)}, bf16[128,3584]{1,0:T(8,128)(2,1)S(1)}, u32[]{:S(2)}, u32[]{:S(2)}) collective-permute-start(bf16[128,3584]{1,0:T(8,128)(2,1)} %refs_0_.1), channel_id=1, source_target_pairs={{0,16},{4,20},{8,24},{12,28},{16,0},{20,4},{24,8},{28,12},{1,17},{... | collective-permute-start | bytes 2752520 | tf_op jit(solution)/shard_map/ppermute | solution.py:351
  41.3 35.7 %collective-permute-start.15 = (bf16[128,3584]{1,0:T(8,128)(2,1)}, bf16[128,3584]{1,0:T(8,128)(2,1)S(1)}, u32[]{:S(2)}, u32[]{:S(2)}) collective-permute-start(bf16[128,3584]{1,0:T(8,128)(2,1)} %collective-permute-done.14.refs_0_), channel_id=1, source_target_pairs={{0,8},{4,12},{8,0},{12,4},{16,24},{20,28},{24,16},{28,20},{1,9},{5... | collective-permute-start | bytes 2752520 | tf_op jit(solution)/shard_map/ppermute | solution.py:351
  43.6 46.9 %collective-permute-start.16 = (bf16[128,3584]{1,0:T(8,128)(2,1)}, bf16[128,3584]{1,0:T(8,128)(2,1)S(1)}, u32[]{:S(2)}, u32[]{:S(2)}) collective-permute-start(bf16[128,3584]{1,0:T(8,128)(2,1)} %collective-permute-done.14.refs_0_), channel_id=1, source_target_pairs={{0,16},{4,20},{8,24},{12,28},{16,0},{20,4},{24,8},{28,12},{1,17},{... | collective-permute-start | bytes 2752520 | tf_op jit(solution)/shard_map/ppermute | solution.py:351
  57.3 44.6 %collective-permute-start.23 = (bf16[128,3584]{1,0:T(8,128)(2,1)}, bf16[128,3584]{1,0:T(8,128)(2,1)}, u32[]{:S(2)}, u32[]{:S(2)}) collective-permute-start(bf16[128,3584]{1,0:T(8,128)(2,1)} %collective-permute-done.14.refs_0_), channel_id=1, source_target_pairs={{0,1},{1,2},{2,3},{3,0},{4,5},{5,6},{6,7},{7,4},{8,9},{9,10},{10,1... | collective-permute-start | bytes 2752520 | tf_op jit(solution)/shard_map/ppermute | solution.py:354
  62.0 28.6 %copy-start.12 = (bf16[128,3584]{1,0:T(8,128)(2,1)}, bf16[128,3584]{1,0:T(8,128)(2,1)S(1)}, u32[]{:S(2)}) copy-start(bf16[128,3584]{1,0:T(8,128)(2,1)S(1)} %collective-permute-done.1.refs_2_) | copy-start | bytes 2752516
  62.0 30.3 %collective-permute-start.10 = (bf16[4,4,64,256]{3,2,1,0:T(8,128)(2,1)}, bf16[4,4,64,256]{3,2,1,0:T(8,128)(2,1)}, u32[]{:S(2)}, u32[]{:S(2)}) collective-permute-start(bf16[4,4,64,256]{3,2,1,0:T(8,128)(2,1)} %get-tuple-element.95), channel_id=1, source_target_pairs={{0,24},{4,28},{8,16},{12,20},{16,8},{20,12},{24,0},{28,4},{1,25},{... | collective-permute-start | bytes 1572872 | tf_op jit(solution)/shard_map/ppermute | solution.py:351
  77.0 23.5 %collective-permute-start.2 = (bf16[64,3584]{1,0:T(8,128)(2,1)}, bf16[64,3584]{1,0:T(8,128)(2,1)}, u32[]{:S(2)}, u32[]{:S(2)}) collective-permute-start(bf16[64,3584]{1,0:T(8,128)(2,1)} %slice.38), channel_id=1, source_target_pairs={{0,16},{4,20},{8,24},{12,28},{16,0},{20,4},{24,8},{28,12},{1,17},{... | collective-permute-start | bytes 1376264 | tf_op jit(solution)/shard_map/ppermute | solution.py:351
  90.5 12.0 %collective-permute-start.3 = (bf16[64,3584]{1,0:T(8,128)(2,1)}, bf16[64,3584]{1,0:T(8,128)(2,1)}, u32[]{:S(2)}, u32[]{:S(2)}) collective-permute-start(bf16[64,3584]{1,0:T(8,128)(2,1)} %slice.39), channel_id=1, source_target_pairs={{0,8},{4,12},{8,0},{12,4},{16,24},{20,28},{24,16},{28,20},{1,9},{5... | collective-permute-start | bytes 1376264 | tf_op jit(solution)/shard_map/ppermute | solution.py:351
  92.3 32.2 %collective-permute-start.17 = (bf16[64,3584]{1,0:T(8,128)(2,1)S(1)}, bf16[64,3584]{1,0:T(8,128)(2,1)S(1)}, u32[]{:S(2)}, u32[]{:S(2)}) collective-permute-start(bf16[64,3584]{1,0:T(8,128)(2,1)S(1)} %slice.40), channel_id=1, source_target_pairs={{0,16},{4,20},{8,24},{12,28},{16,0},{20,4},{24,8},{28,12},{1,17},{... | collective-permute-start | bytes 1376264 | tf_op jit(solution)/shard_map/ppermute | solution.py:351
  100.5 24.0 %collective-permute-start.18 = (bf16[64,3584]{1,0:T(8,128)(2,1)S(1)}, bf16[64,3584]{1,0:T(8,128)(2,1)S(1)}, u32[]{:S(2)}, u32[]{:S(2)}) collective-permute-start(bf16[64,3584]{1,0:T(8,128)(2,1)S(1)} %slice.41), channel_id=1, source_target_pairs={{0,8},{4,12},{8,0},{12,4},{16,24},{20,28},{24,16},{28,20},{1,9},{5... | collective-permute-start | bytes 1376264 | tf_op jit(solution)/shard_map/ppermute | solution.py:351
  102.0 38.8 %collective-permute-start.32 = (bf16[128,3584]{1,0:T(8,128)(2,1)}, bf16[128,3584]{1,0:T(8,128)(2,1)}, u32[]{:S(2)}, u32[]{:S(2)}) collective-permute-start(bf16[128,3584]{1,0:T(8,128)(2,1)} %collective-permute-done.23.refs_0_), channel_id=1, source_target_pairs={{0,1},{1,2},{2,3},{3,0},{4,5},{5,6},{6,7},{7,4},{8,9},{9,10},{10,1... | collective-permute-start | bytes 2752520 | tf_op jit(solution)/shard_map/ppermute | solution.py:354
  105.8 18.7 %copy-start.36 = (bf16[4,4,64,256]{3,2,1,0:T(8,128)(2,1)S(1)}, bf16[4,4,64,256]{3,2,1,0:T(8,128)(2,1)}, u32[]{:S(2)}) copy-start(bf16[4,4,64,256]{3,2,1,0:T(8,128)(2,1)} %copy-done.34) | copy-start | bytes 1572868
  121.8 42.5 %collective-permute-start.24 = (bf16[128,3584]{1,0:T(8,128)(2,1)}, bf16[128,3584]{1,0:T(8,128)(2,1)S(1)}, u32[]{:S(2)}, u32[]{:S(2)}) collective-permute-start(bf16[128,3584]{1,0:T(8,128)(2,1)} %collective-permute-done.23.refs_0_), channel_id=1, source_target_pairs={{0,8},{4,12},{8,0},{12,4},{16,24},{20,28},{24,16},{28,20},{1,9},{5... | collective-permute-start | bytes 2752520 | tf_op jit(solution)/shard_map/ppermute | solution.py:351
  122.4 42.7 %collective-permute-start.25 = (bf16[128,3584]{1,0:T(8,128)(2,1)}, bf16[128,3584]{1,0:T(8,128)(2,1)S(1)}, u32[]{:S(2)}, u32[]{:S(2)}) collective-permute-start(bf16[128,3584]{1,0:T(8,128)(2,1)} %collective-permute-done.23.refs_0_), channel_id=1, source_target_pairs={{0,16},{4,20},{8,24},{12,28},{16,0},{20,4},{24,8},{28,12},{1,17},{... | collective-permute-start | bytes 2752520 | tf_op jit(solution)/shard_map/ppermute | solution.py:351
  140.8 59.8 %collective-permute-start.33 = (bf16[128,3584]{1,0:T(8,128)(2,1)}, bf16[128,3584]{1,0:T(8,128)(2,1)S(1)}, u32[]{:S(2)}, u32[]{:S(2)}) collective-permute-start(bf16[128,3584]{1,0:T(8,128)(2,1)} %collective-permute-done.32.refs_0_), channel_id=1, source_target_pairs={{0,8},{4,12},{8,0},{12,4},{16,24},{20,28},{24,16},{28,20},{1,9},{5... | collective-permute-start | bytes 2752520 | tf_op jit(solution)/shard_map/ppermute | solution.py:351
  142.3 60.2 %collective-permute-start.34 = (bf16[128,3584]{1,0:T(8,128)(2,1)}, bf16[128,3584]{1,0:T(8,128)(2,1)}, u32[]{:S(2)}, u32[]{:S(2)}) collective-permute-start(bf16[128,3584]{1,0:T(8,128)(2,1)} %collective-permute-done.32.refs_0_), channel_id=1, source_target_pairs={{0,16},{4,20},{8,24},{12,28},{16,0},{20,4},{24,8},{28,12},{1,17},{... | collective-permute-start | bytes 2752520 | tf_op jit(solution)/shard_map/ppermute | solution.py:351
  142.3 20.5 %collective-permute-start.19 = (bf16[4,64,256]{2,1,0:T(8,128)(2,1)S(1)}, bf16[4,64,256]{2,1,0:T(8,128)(2,1)S(1)}, u32[]{:S(2)}, u32[]{:S(2)}) collective-permute-start(bf16[4,64,256]{2,1,0:T(8,128)(2,1)S(1)} %get-tuple-element.48), channel_id=1, source_target_pairs={{0,8},{4,12},{8,0},{12,4},{16,24},{20,28},{24,16},{28,20},{1,9},{5... | collective-permute-start | bytes 393224 | tf_op jit(solution)/shard_map/ppermute | solution.py:351
  163.4 6.2 %collective-permute-start.20 = (bf16[4,64,256]{2,1,0:T(8,128)(2,1)S(1)}, bf16[4,64,256]{2,1,0:T(8,128)(2,1)S(1)}, u32[]{:S(2)}, u32[]{:S(2)}) collective-permute-start(bf16[4,64,256]{2,1,0:T(8,128)(2,1)S(1)} %get-tuple-element.49), channel_id=1, source_target_pairs={{0,16},{4,20},{8,24},{12,28},{16,0},{20,4},{24,8},{28,12},{1,17},{... | collective-permute-start | bytes 393224 | tf_op jit(solution)/shard_map/ppermute | solution.py:351
  164.4 6.3 %collective-permute-start.11 = (bf16[4,64,256]{2,1,0:T(8,128)(2,1)S(1)}, bf16[4,64,256]{2,1,0:T(8,128)(2,1)S(1)}, u32[]{:S(2)}, u32[]{:S(2)}) collective-permute-start(bf16[4,64,256]{2,1,0:T(8,128)(2,1)S(1)} %get-tuple-element.42), channel_id=1, source_target_pairs={{0,8},{4,12},{8,0},{12,4},{16,24},{20,28},{24,16},{28,20},{1,9},{5... | collective-permute-start | bytes 393224 | tf_op jit(solution)/shard_map/ppermute | solution.py:351
  165.0 7.4 %collective-permute-start.12 = (bf16[4,64,256]{2,1,0:T(8,128)(2,1)S(1)}, bf16[4,64,256]{2,1,0:T(8,128)(2,1)S(1)}, u32[]{:S(2)}, u32[]{:S(2)}) collective-permute-start(bf16[4,64,256]{2,1,0:T(8,128)(2,1)S(1)} %get-tuple-element.43), channel_id=1, source_target_pairs={{0,16},{4,20},{8,24},{12,28},{16,0},{20,4},{24,8},{28,12},{1,17},{... | collective-permute-start | bytes 393224 | tf_op jit(solution)/shard_map/ppermute | solution.py:351
  170.3 35.1 %collective-permute-start.26 = (bf16[64,3584]{1,0:T(8,128)(2,1)}, bf16[64,3584]{1,0:T(8,128)(2,1)}, u32[]{:S(2)}, u32[]{:S(2)}) collective-permute-start(bf16[64,3584]{1,0:T(8,128)(2,1)} %slice.42), channel_id=1, source_target_pairs={{0,16},{4,20},{8,24},{12,28},{16,0},{20,4},{24,8},{28,12},{1,17},{... | collective-permute-start | bytes 1376264 | tf_op jit(solution)/shard_map/ppermute | solution.py:351
  171.3 34.1 %collective-permute-start.27 = (bf16[64,3584]{1,0:T(8,128)(2,1)}, bf16[64,3584]{1,0:T(8,128)(2,1)}, u32[]{:S(2)}, u32[]{:S(2)}) collective-permute-start(bf16[64,3584]{1,0:T(8,128)(2,1)} %slice.43), channel_id=1, source_target_pairs={{0,8},{4,12},{8,0},{12,4},{16,24},{20,28},{24,16},{28,20},{1,9},{5... | collective-permute-start | bytes 1376264 | tf_op jit(solution)/shard_map/ppermute | solution.py:351
  173.1 10.9 %collective-permute-start.13 = (bf16[4,64,256]{2,1,0:T(8,128)(2,1)S(1)}, bf16[4,64,256]{2,1,0:T(8,128)(2,1)S(1)}, u32[]{:S(2)}, u32[]{:S(2)}) collective-permute-start(bf16[4,64,256]{2,1,0:T(8,128)(2,1)S(1)} %get-tuple-element.44), channel_id=1, source_target_pairs={{0,24},{4,28},{8,16},{12,20},{16,8},{20,12},{24,0},{28,4},{1,25},{... | collective-permute-start | bytes 393224 | tf_op jit(solution)/shard_map/ppermute | solution.py:351
  184.6 6.2 %collective-permute-start.21 = (bf16[4,64,256]{2,1,0:T(8,128)(2,1)}, bf16[4,64,256]{2,1,0:T(8,128)(2,1)}, u32[]{:S(2)}, u32[]{:S(2)}) collective-permute-start(bf16[4,64,256]{2,1,0:T(8,128)(2,1)} %get-tuple-element.50), channel_id=1, source_target_pairs={{0,24},{4,28},{8,16},{12,20},{16,8},{20,12},{24,0},{28,4},{1,25},{... | collective-permute-start | bytes 393224 | tf_op jit(solution)/shard_map/ppermute | solution.py:351
  195.8 4.8 %collective-permute-start.22 = (f32[4,128]{1,0:T(4,128)}, f32[4,128]{1,0:T(4,128)S(1)}, u32[]{:S(2)}, u32[]{:S(2)}) collective-permute-start(f32[4,128]{1,0:T(4,128)} %get-tuple-element.52), channel_id=1, source_target_pairs={{0,3},{1,0},{2,1},{3,2},{4,7},{5,4},{6,5},{7,6},{8,11},{9,8},{10,9... | collective-permute-start | bytes 6152 | tf_op jit(solution)/shard_map/ppermute | solution.py:354
  200.6 22.6 %copy-start.60 = (f32[4,128]{1,0:T(4,128)}, f32[4,128]{1,0:T(4,128)S(1)}, u32[]{:S(2)}) copy-start(f32[4,128]{1,0:T(4,128)S(1)} %collective-permute-done.22) | copy-start | bytes 6148
  200.6 22.6 %copy-start.6 = (bf16[128,3584]{1,0:T(8,128)(2,1)}, bf16[128,3584]{1,0:T(8,128)(2,1)S(1)}, u32[]{:S(2)}) copy-start(bf16[128,3584]{1,0:T(8,128)(2,1)S(1)} %collective-permute-done.33.refs_1_) | copy-start | bytes 2752516
  201.5 43.6 %collective-permute-start.35 = (bf16[64,3584]{1,0:T(8,128)(2,1)}, bf16[64,3584]{1,0:T(8,128)(2,1)S(1)}, u32[]{:S(2)}, u32[]{:S(2)}) collective-permute-start(bf16[64,3584]{1,0:T(8,128)(2,1)} %slice.44), channel_id=1, source_target_pairs={{0,16},{4,20},{8,24},{12,28},{16,0},{20,4},{24,8},{28,12},{1,17},{... | collective-permute-start | bytes 1376264 | tf_op jit(solution)/shard_map/ppermute | solution.py:351
  204.4 40.7 %collective-permute-start.36 = (bf16[64,3584]{1,0:T(8,128)(2,1)}, bf16[64,3584]{1,0:T(8,128)(2,1)S(1)}, u32[]{:S(2)}, u32[]{:S(2)}) collective-permute-start(bf16[64,3584]{1,0:T(8,128)(2,1)} %slice.45), channel_id=1, source_target_pairs={{0,8},{4,12},{8,0},{12,4},{16,24},{20,28},{24,16},{28,20},{1,9},{5... | collective-permute-start | bytes 1376264 | tf_op jit(solution)/shard_map/ppermute | solution.py:351
  262.0 17.1 %copy-start.17 = (bf16[4,64,256]{2,1,0:T(8,128)(2,1)S(1)}, bf16[4,64,256]{2,1,0:T(8,128)(2,1)}, u32[]{:S(2)}) copy-start(bf16[4,64,256]{2,1,0:T(8,128)(2,1)} %copy-done.16) | copy-start | bytes 393220
  266.7 24.5 %collective-permute-start.41 = (bf16[512,3584]{1,0:T(8,128)(2,1)}, bf16[512,3584]{1,0:T(8,128)(2,1)}, u32[]{:S(2)}, u32[]{:S(2)}) collective-permute-start(bf16[512,3584]{1,0:T(8,128)(2,1)} %shard_map.85), channel_id=1, source_target_pairs={{0,4},{4,0},{8,12},{12,8},{16,20},{20,16},{24,28},{28,24},{1,5},{5... | collective-permute-start | bytes 11010056 | tf_op jit(solution)/shard_map/ppermute | solution.py:351
  266.8 6.6 %collective-permute-start.28 = (bf16[4,64,256]{2,1,0:T(8,128)(2,1)}, bf16[4,64,256]{2,1,0:T(8,128)(2,1)S(1)}, u32[]{:S(2)}, u32[]{:S(2)}) collective-permute-start(bf16[4,64,256]{2,1,0:T(8,128)(2,1)} %get-tuple-element.57), channel_id=1, source_target_pairs={{0,8},{4,12},{8,0},{12,4},{16,24},{20,28},{24,16},{28,20},{1,9},{5... | collective-permute-start | bytes 393224 | tf_op jit(solution)/shard_map/ppermute | solution.py:351
  267.9 8.5 %collective-permute-start.29 = (bf16[4,64,256]{2,1,0:T(8,128)(2,1)}, bf16[4,64,256]{2,1,0:T(8,128)(2,1)}, u32[]{:S(2)}, u32[]{:S(2)}) collective-permute-start(bf16[4,64,256]{2,1,0:T(8,128)(2,1)} %get-tuple-element.58), channel_id=1, source_target_pairs={{0,16},{4,20},{8,24},{12,28},{16,0},{20,4},{24,8},{28,12},{1,17},{... | collective-permute-start | bytes 393224 | tf_op jit(solution)/shard_map/ppermute | solution.py:351
  268.9 10.2 %collective-permute-start.30 = (bf16[4,64,256]{2,1,0:T(8,128)(2,1)}, bf16[4,64,256]{2,1,0:T(8,128)(2,1)}, u32[]{:S(2)}, u32[]{:S(2)}) collective-permute-start(bf16[4,64,256]{2,1,0:T(8,128)(2,1)} %copy-done.39), channel_id=1, source_target_pairs={{0,24},{4,28},{8,16},{12,20},{16,8},{20,12},{24,0},{28,4},{1,25},{... | collective-permute-start | bytes 393224 | tf_op jit(solution)/shard_map/ppermute | solution.py:351
  270.4 11.3 %collective-permute-start.37 = (bf16[4,64,256]{2,1,0:T(8,128)(2,1)}, bf16[4,64,256]{2,1,0:T(8,128)(2,1)}, u32[]{:S(2)}, u32[]{:S(2)}) collective-permute-start(bf16[4,64,256]{2,1,0:T(8,128)(2,1)} %copy-done.42), channel_id=1, source_target_pairs={{0,8},{4,12},{8,0},{12,4},{16,24},{20,28},{24,16},{28,20},{1,9},{5... | collective-permute-start | bytes 393224 | tf_op jit(solution)/shard_map/ppermute | solution.py:351
  273.4 8.3 %collective-permute-start.38 = (bf16[4,64,256]{2,1,0:T(8,128)(2,1)}, bf16[4,64,256]{2,1,0:T(8,128)(2,1)}, u32[]{:S(2)}, u32[]{:S(2)}) collective-permute-start(bf16[4,64,256]{2,1,0:T(8,128)(2,1)} %copy-done.41), channel_id=1, source_target_pairs={{0,16},{4,20},{8,24},{12,28},{16,0},{20,4},{24,8},{28,12},{1,17},{... | collective-permute-start | bytes 393224 | tf_op jit(solution)/shard_map/ppermute | solution.py:351
  276.4 6.2 %collective-permute-start.39 = (bf16[4,64,256]{2,1,0:T(8,128)(2,1)}, bf16[4,64,256]{2,1,0:T(8,128)(2,1)}, u32[]{:S(2)}, u32[]{:S(2)}) collective-permute-start(bf16[4,64,256]{2,1,0:T(8,128)(2,1)} %copy-done.40), channel_id=1, source_target_pairs={{0,24},{4,28},{8,16},{12,20},{16,8},{20,12},{24,0},{28,4},{1,25},{... | collective-permute-start | bytes 393224 | tf_op jit(solution)/shard_map/ppermute | solution.py:351
  280.8 9.7 %collective-permute-start.31 = (f32[4,128]{1,0:T(4,128)S(1)}, f32[4,128]{1,0:T(4,128)S(1)}, u32[]{:S(2)}, u32[]{:S(2)}) collective-permute-start(f32[4,128]{1,0:T(4,128)S(1)} %get-tuple-element.61), channel_id=1, source_target_pairs={{0,2},{1,3},{2,0},{3,1},{4,6},{5,7},{6,4},{7,5},{8,10},{9,11},{10,... | collective-permute-start | bytes 6152 | tf_op jit(solution)/shard_map/ppermute | solution.py:354
  284.4 6.1 %collective-permute-start.40 = (f32[4,128]{1,0:T(4,128)S(1)}, f32[4,128]{1,0:T(4,128)S(1)}, u32[]{:S(2)}, u32[]{:S(2)}) collective-permute-start(f32[4,128]{1,0:T(4,128)S(1)} %get-tuple-element.75), channel_id=1, source_target_pairs={{0,1},{1,2},{2,3},{3,0},{4,5},{5,6},{6,7},{7,4},{8,9},{9,10},{10,1... | collective-permute-start | bytes 6152 | tf_op jit(solution)/shard_map/ppermute | solution.py:354
  (57 other events, 208.6 us)

commit v4 on v3

--- a/solution.py
+++ b/solution.py
@@ -84,8 +84,8 @@
     return lax.dot_general(a, b, (((0,), (0,)), ((), ())), preferred_element_type=F32)
 
 
-def project_kernel(top_k, sizes, idx_ref, *refs):
-    parts = len(sizes)
+def project_kernel(top_k, idx_ref, *refs):
+    parts = 1
     pieces, (own_weight, partner_weight) = refs[:parts], refs[parts : parts + 2]
     hidden_refs = refs[parts + 2 : parts + 6]
     grad_refs = refs[parts + 6 : parts + 10]
@@ -98,10 +98,11 @@
 
     @pl.when(e == 0)
     def _():
-        copies, at = [], 0
-        for i, size in enumerate(sizes):
-            copies.append(pltpu.make_async_copy(pieces[i], rows.at[at : at + size], sems.at[i]))
-            at += size
+        copies = []
+        for m in range(4):
+            at = pl.ds(pl.multiple_of(idx_ref[3 + m] * tokens, tokens), tokens)
+            to = rows.at[m * tokens : (m + 1) * tokens]
+            copies.append(pltpu.make_async_copy(pieces[0].at[at], to, sems.at[m]))
         for copy in copies:
             copy.start()
         for copy in copies:
@@ -159,18 +160,17 @@
         store.wait()
 
 
-def project(index, pieces, own_weight, partner_weight, hidden, top_k):
+def project(index, gathered, own_weight, partner_weight, hidden, top_k):
     experts, sources, slots, pair = hidden[0].shape
     width = own_weight.shape[1]
-    sizes = [p.shape[0] for p in pieces]
-    count = sum(sizes)
+    count = gathered.shape[0]
     block = pair // 2
     return pl.pallas_call(
-        functools.partial(project_kernel, top_k, sizes),
+        functools.partial(project_kernel, top_k),
         grid_spec=pltpu.PrefetchScalarGridSpec(
             num_scalar_prefetch=1,
             grid=(experts,),
-            in_specs=[pl.BlockSpec(memory_space=pl.ANY)] * len(sizes)
+            in_specs=[pl.BlockSpec(memory_space=pl.ANY)]
             + [pl.BlockSpec((block, width), lambda e, idx: (e, 0))] * 2
             + [pl.BlockSpec((1, 1, slots, pair), lambda e, idx: (e, idx[0], 0, 0))] * 4,
             out_specs=[pl.BlockSpec((1, slots, pair), lambda e, idx: (e, 0, 0))] * 4
@@ -182,7 +182,7 @@
                 pltpu.VMEM((count, width), BF16),
                 pltpu.VMEM((pair, width), BF16),
                 pltpu.VMEM((2, experts * block, count), BF16),
-                pltpu.SemaphoreType.DMA((len(sizes),)),
+                pltpu.SemaphoreType.DMA((4,)),
                 pltpu.SemaphoreType.DMA,
             ],
         ),
@@ -197,7 +197,7 @@
             bytes_accessed=2 * (2 * count * width + 2 * own_weight.size),
             transcendentals=0,
         ),
-    )(index, *pieces, own_weight, partner_weight, *hidden)
+    )(index, gathered, own_weight, partner_weight, *hidden)
 
 
 def early_grad_kernel(terms, *refs):
@@ -378,27 +378,24 @@
     own_weight = lax.optimization_barrier(own_weight)
     partner_weight = across(own_weight, 1)
 
-    half = tokens // 2
     shards = [grad_out]
     for step in range(1, sources):
+        if step == 2:
+            carried = after(carried, hidden)
         carried = around(carried, 1)
         shards.append(carried)
+    same_core = [[i for i in range(reps) if i % 2 == c] for c in range(2)]
     scatters, rows, returned, indices, placed, combines = [], [], [], [], [None], []
     for step in range(sources):
-        own = shards[step]
-        sent = own if step < 2 else after(own, scatters[step - 2])
-        from_x, from_y = across(sent, 2), across(sent, 4)
-        top, bottom = across(from_x[:half], 4), across(from_y[half:], 2)
+        gathered = lax.all_gather(shards[step], "rep", axis=0, tiled=True, axis_index_groups=same_core)
         source = lax.rem(me - step + sources, sources)
-        index = jnp.stack([source, me * experts, core]).astype(jnp.int32)
+        index = jnp.stack([source, me * experts, core] + chips).astype(jnp.int32)
         if step >= 2:
-            own = after(own, combines[step - 2])
+            gathered = after(gathered, combines[step - 2])
         if step == sources - 1:
             before = early_grad(scatters, rows, 512)
-            own = after(own, before)
-        *grads, scatter, row = project(
-            index, [own, from_x, from_y, top, bottom], own_weight, partner_weight, hidden, top_k
-        )
+            gathered = after(gathered, before)
+        *grads, scatter, row = project(index, gathered, own_weight, partner_weight, hidden, top_k)
         scatters.append(scatter)
         rows.append(row)
         returned = [grads[0]] + [across(grads[m], 2 * m) for m in range(1, 4)]

time: 305 us -> 298 us (0.977)
  starting transfers between devices: 55.2 us -> 32.7 us
  between operations: 1.2 us -> 14.2 us
  waiting for transfers between devices: 95 us -> 107 us
  Pallas kernels: 87.9 us -> 81.1 us
  local copies, waits for them, and re-layouts: 60.6 us -> 56.9 us
    ppermute x9, waiting for transfers between devices: 2.78 us -> 69.7 us  [around(): lax.ppermute(array, 'exp', [(i, (i + shift) % sources) for i in range(sou...]
    ppermute x33 -> x17, waiting for transfers between devices: 92.2 us -> 36.2 us  [across(): return lax.ppermute(array, 'rep', [(i, i ^ bits) for i in range(reps)])]
    ppermute x33 -> x17, starting transfers between devices: 39.2 us -> 17.2 us  [across(): return lax.ppermute(array, 'rep', [(i, i ^ bits) for i in range(reps)])]
    pallas_call x4, Pallas kernels: 54.7 us -> 48.4 us  [project(): pl.pallas_call(functools.partial(project_kernel, top_k), grid_spec=pltpu....]
    slice x8 -> x0, local copies, waits for them, and re-layouts: 6.04 us -> none  [on_device_tokens(): top, bottom = (across(from_x[:half], 4), across(from_y[half:], 2))]
    unnamed x127 -> x91, local copies, waits for them, and re-layouts: 43.2 us -> 42 us
  transfers between devices with their start and end apart: 42 -> 30, of which waited for: 15 -> 12; matrix products, arithmetic and copies ran while one was open for 6% -> 8% of each run, Pallas kernels for 20% -> 19%
where the time goes in v4:
time: 298 us; the launch traced here: 297 us
  waiting for transfers between devices  107 us (36%)
  Pallas kernels  81.1 us (27%)
  local copies, waits for them, and re-layouts  56.9 us (19%)
  starting transfers between devices  32.7 us (11%)
  between operations  14.2 us (5%)
  other arithmetic  5.02 us (2%)
    ppermute x9, waiting for transfers between devices, around(): lax.ppermute(array, 'exp', [(i, (i + shift) % sources) for i in range(sou...  69.7 us
    pallas_call x4, Pallas kernels, project(): pl.pallas_call(functools.partial(project_kernel, top_k), grid_spec=pltpu....  48.4 us
    unnamed x91, local copies, waits for them, and re-layouts  42 us
    ppermute x17, waiting for transfers between devices, across(): return lax.ppermute(array, 'rep', [(i, i ^ bits) for i in range(reps)])  36.2 us
    ppermute x17, starting transfers between devices, across(): return lax.ppermute(array, 'rep', [(i, i ^ bits) for i in range(reps)])  17.2 us
    ppermute x9, starting transfers between devices, around(): lax.ppermute(array, 'exp', [(i, (i + shift) % sources) for i in range(sou...  15.3 us
    pallas_call x1, Pallas kernels, early_grad(): pl.pallas_call(functools.partial(early_grad_kernel, terms), grid=(width /...  14.2 us
    pallas_call x2, Pallas kernels, late_grad(): pl.pallas_call(kernel, grid_spec=pltpu.PrefetchScalarGridSpec(num_scalar_...  12.5 us
  transfers between devices with their start and end apart: 30, of which 12 were waited for; matrix products, arithmetic and copies ran while one was open for 8% of the time, Pallas kernels for 19%

profile of v4, /device:TPU:0, one launch (start us, length us, event | category | flops | bytes accessed | tf_op | source)
XLA Modules:
  0.0 296.6 jit_solution(5757240658471347486)
XLA Ops:
  10.0 3.1 %collective-permute-start.1 = (bf16[4,256]{1,0:T(4,128)(2,1)S(1)}, bf16[4,256]{1,0:T(4,128)(2,1)S(1)}, u32[]{:S(2)}, u32[]{:S(2)}) collective-permute-start(bf16[4,256]{1,0:T(4,128)(2,1)S(1)} %get-tuple-element.98), channel_id=1, source_target_pairs={{0,1},{1,2},{2,3},{3,0},{4,5},{5,6},{6,7},{7,4},{8,9},{9,10},{10,1... | collective-permute-start | bytes 6152 | tf_op jit(solution)/shard_map/ppermute | solution.py:354
  13.1 2.6 collective-permute-start.2
  15.7 1.3 collective-permute-start.3
  17.6 1.7 collective-permute-done.3
  19.4 22.6 %collective-permute-done.10 = bf16[128,3584]{1,0:T(8,128)(2,1)S(1)} collective-permute-done((bf16[128,3584]{1,0:T(8,128)(2,1)}, bf16[128,3584]{1,0:T(8,128)(2,1)S(1)}, u32[]{:S(2)}, u32[]{:S(2)}) %collective-permute-start.10) | collective-permute-done | bytes 917536 | tf_op jit(solution)/shard_map/ppermute | solution.py:354
  43.1 4.8 %reshape.88 = bf16[4,4,60,4,256]{4,3,1,2,0:T(4,128)(2,1)} reshape(bf16[1,4,4,60,1024]{4,2,3,1,0:T(4,128)(2,1)} %param.8) | data formatting | bytes 3932160 | tf_op jit(solution)/shard_map/reshape | solution.py:369
  47.9 2.2 copy.18
  50.2 1.2 dynamic-slice_bitcast_fusion
  52.1 1.6 pad_maximum_fusion
  53.7 1.6 collective-permute-start.4
  55.3 1.5 collective-permute-start.5
  57.3 15.7 %collective-permute-done.4.refs_4_ = bf16[4,4,64,256]{3,2,1,0:T(8,128)(2,1)S(1)} collective-permute-done((bf16[4,4,64,256]{3,2,1,0:T(8,128)(2,1)S(1)}, bf16[4,4,64,256]{3,2,1,0:T(8,128)(2,1)S(1)}, u32[]{:S(2)}, u32[]{:S(2)}) %collective-permute-start.4) | collective-permute-done | bytes 524320 | tf_op jit(solution)/shard_map/ppermute | solution.py:351
  73.0 13.6 %collective-permute-done.6.refs_6_ = bf16[4,4,64,256]{3,2,1,0:T(8,128)(2,1)S(1)} collective-permute-done((bf16[4,4,64,256]{3,2,1,0:T(8,128)(2,1)S(1)}, bf16[4,4,64,256]{3,2,1,0:T(8,128)(2,1)S(1)}, u32[]{:S(2)}, u32[]{:S(2)}) %collective-permute-start.6) | collective-permute-done | bytes 524320 | tf_op jit(solution)/shard_map/ppermute | solution.py:351
  86.6 1.4 collective-permute-start.15
  88.0 19.5 %collective-permute-done.15 = bf16[128,3584]{1,0:T(8,128)(2,1)S(1)} collective-permute-done((bf16[128,3584]{1,0:T(8,128)(2,1)}, bf16[128,3584]{1,0:T(8,128)(2,1)S(1)}, u32[]{:S(2)}, u32[]{:S(2)}) %collective-permute-start.15) | collective-permute-done | bytes 917536 | tf_op jit(solution)/shard_map/ppermute | solution.py:354
  108.5 4.6 %copy.14 = bf16[4,128,3584]{2,1,0:T(8,128)(2,1)} copy(bf16[4,128,3584]{2,0,1:T(4,128)(2,1)} %bitcast.50) | data formatting | bytes 7340032 | tf_op jit(solution)/shard_map/transpose | solution.py:377
  113.1 24.6 %collective-permute-done.20 = bf16[128,3584]{1,0:T(8,128)(2,1)S(1)} collective-permute-done((bf16[128,3584]{1,0:T(8,128)(2,1)S(1)}, bf16[128,3584]{1,0:T(8,128)(2,1)S(1)}, u32[]{:S(2)}, u32[]{:S(2)}) %collective-permute-start.20) | collective-permute-done | bytes 917536 | tf_op jit(solution)/shard_map/ppermute | solution.py:354
  138.9 2.0 copy-done.8
  140.9 11.6 %shard_map.76 = (bf16[4,64,256]{2,1,0:T(8,128)(2,1)S(1)}, bf16[4,64,256]{2,1,0:T(8,128)(2,1)S(1)}, bf16[4,64,256]{2,1,0:T(8,128)(2,1)S(1)}, bf16[4,64,256]{2,1,0...) custom-call(s32[7]{0:T(128)S(1)} %stack.54.idx_ref, bf16[512,3584]{1,0:T(8,128)(2,1)S(1)} %copy-done.8, ...), custom_call_target="tpu_custom_call" | custom-call | flops 7516192768 | bytes 14680064 | tf_op jit(solution)/shard_map/pallas_call | solution.py:168
  152.5 1.8 copy-done.24
  156.3 2.5 collective-permute-start.9
  158.8 2.0 copy-done.9
  160.9 12.3 %shard_map.78 = (bf16[4,64,256]{2,1,0:T(8,128)(2,1)S(1)}, bf16[4,64,256]{2,1,0:T(8,128)(2,1)}, bf16[4,64,256]{2,1,0:T(8,128)(2,1)}, bf16[4,64,256]{2,1,0:T(8,128...) custom-call(s32[7]{0:T(128)S(1)} %stack.123.idx_ref, bf16[512,3584]{1,0:T(8,128)(2,1)S(1)} %copy-done.9, ...), custom_call_target="tpu_custom_call" | custom-call | flops 7516192768 | bytes 14680064 | tf_op jit(solution)/shard_map/pallas_call | solution.py:168
  173.2 1.8 copy-done.26
  177.0 2.5 collective-permute-start.13
  182.0 1.6 collective-permute-done.12.refs_2_
  183.6 1.7 shard_map.79
  185.3 2.8 collective-permute-start.14
  188.8 2.4 copy-done.11
  194.3 12.6 %shard_map.80 = (bf16[4,64,256]{2,1,0:T(8,128)(2,1)S(1)}, bf16[4,64,256]{2,1,0:T(8,128)(2,1)}, bf16[4,64,256]{2,1,0:T(8,128)(2,1)}, bf16[4,64,256]{2,1,0:T(8,128...) custom-call(s32[7]{0:T(128)S(1)} %copy-done.7, bf16[512,3584]{1,0:T(8,128)(2,1)S(1)} %copy-done.11, ...), custom_call_target="tpu_custom_call" | custom-call | flops 7516192768 | bytes 14680064 | tf_op jit(solution)/shard_map/pallas_call | solution.py:168
  206.9 1.8 copy-done.28
  208.8 2.0 copy-done.29
  210.8 14.2 %shard_map.82.before_ref = f32[2,512,3584]{2,1,0:T(8,128)S(1)} custom-call(bf16[2,512,512]{2,1,0:T(8,128)(2,1)S(1)} %copy-done.31, bf16[2,512,512]{2,1,0:T(8,128)(2,1)S(1)} %copy-done.33, bf16[2,512,512]{2,1,0:T(8,128)(2,1)S(1)} %get-tuple-element.63.refs_2_, bf16[512,3584]{1,0:T(8,128)(2,1)S(1)} %copy-done.25, bf16[512,3584]{1,0:T(8,128)(2,1)S(1)} %copy-done.27, ...), custom_call_target="tpu_custom_call" | custom-call | flops 11274289152 | bytes 28835840 | tf_op jit(solution)/shard_map/pallas_call | solution.py:216
  225.0 5.2 %copy-done = f32[2,512,3584]{2,1,0:T(8,128)} copy-done((f32[2,512,3584]{2,1,0:T(8,128)}, f32[2,512,3584]{2,1,0:T(8,128)S(1)}, u32[]{:S(2)}) %copy-start) | copy-done | bytes 14680088
  231.2 2.0 copy-done.10
  236.4 11.9 %shard_map.83 = (bf16[4,64,256]{2,1,0:T(8,128)(2,1)S(1)}, bf16[4,64,256]{2,1,0:T(8,128)(2,1)S(1)}, bf16[4,64,256]{2,1,0:T(8,128)(2,1)S(1)}, bf16[4,64,256]{2,1,0...) custom-call(s32[7]{0:T(128)S(1)} %stack.129.idx_ref, ...), custom_call_target="tpu_custom_call" | custom-call | flops 7516192768 | bytes 14680064 | tf_op jit(solution)/shard_map/pallas_call | solution.py:168
  248.3 4.9 %shard_map.85 = bf16[512,3584]{1,0:T(8,128)(2,1)} custom-call(s32[1]{0:T(128)} %bitcast.28.idx_ref, bf16[2,512,512]{2,1,0:T(8,128)(2,1)S(1)} %get-tuple-element.75.scatter_ref, bf16[512,3584]{1,0:T(8,128)(2,1)S(1)} %get-tuple-element.76.rows_ref, f32[2,512,3584]{2,1,0:T(8,128)S(1)} %copy-done.1), custom_call_target="tpu_custom_call" | custom-call | flops 1879048192 | bytes 19398656 | tf_op jit(solution)/shard_map/pallas_call | solution.py:272
  255.2 1.7 collective-permute-start.18
  257.7 2.3 collective-permute-done.16.refs_1_
  260.8 2.1 collective-permute-done.17.refs_2_
  263.0 1.4 collective-permute-start.23
  265.0 1.8 shard_map.81
  266.9 2.4 collective-permute-start.19
  269.3 1.8 shard_map.84
  271.1 1.5 collective-permute-start.24
  272.9 2.8 copy.16
  277.3 5.2 %copy-done.2 = f32[2,512,3584]{2,1,0:T(8,128)S(1)} copy-done((f32[2,512,3584]{2,1,0:T(8,128)S(1)}, f32[2,512,3584]{2,1,0:T(8,128)}, u32[]{:S(2)}) %copy-start.2) | copy-done | bytes 14680088
  282.5 7.6 %shard_map.86 = f32[128,4,3584]{2,1,0:T(4,128)} custom-call(s32[1]{0:T(128)} %bitcast.7.idx_ref, bf16[2,512,512]{2,1,0:T(8,128)(2,1)S(1)} %get-tuple-element.75.scatter_ref, bf16[512,3584]{1,0:T(8,128)(2,1)S(1)} %copy-done.4, f32[2,512,3584]{2,1,0:T(8,128)S(1)} %copy-done.2, bf16[512,3584]{1,0:T(8,128)(2,1)} %collective-permute-done.25.arrived_ref), custom_call_target="tpu_custom_call" | custom-call | flops 1879048192 | bytes 19398656 | tf_op jit(solution)/shard_map/pallas_call | solution.py:272
  (148 shorter events, 28.5 us)
Async XLA Ops:
  7.2 131.7 %all-gather.5.cloned.1.call-start = ((), (), s32[]{:S(2)}) async-start(), calls=%async_computation | async-start | bytes 4587520 | tf_op jit(solution)/shard_map/all_gather | solution.py:390
  7.9 150.9 %all-gather.7.cloned.1.call-start = ((), (), s32[]{:S(2)}) async-start(), calls=%async_computation.1 | async-start | bytes 4587520 | tf_op jit(solution)/shard_map/all_gather | solution.py:390
  8.6 10.6 %copy-start.40 = (f32[128]{0:T(128)}, f32[128]{0:T(128)S(1)}, u32[]{:S(2)}) copy-start(f32[128]{0:T(128)S(1)} %reduce_sum.54) | copy-start | bytes 1540
  10.0 7.0 %collective-permute-start.1 = (bf16[4,256]{1,0:T(4,128)(2,1)S(1)}, bf16[4,256]{1,0:T(4,128)(2,1)S(1)}, u32[]{:S(2)}, u32[]{:S(2)}) collective-permute-start(bf16[4,256]{1,0:T(4,128)(2,1)S(1)} %get-tuple-element.98), channel_id=1, source_target_pairs={{0,1},{1,2},{2,3},{3,0},{4,5},{5,6},{6,7},{7,4},{8,9},{9,10},{10,1... | collective-permute-start | bytes 6152 | tf_op jit(solution)/shard_map/ppermute | solution.py:354
  13.1 4.5 %collective-permute-start.2 = (bf16[4,256]{1,0:T(4,128)(2,1)S(1)}, bf16[4,256]{1,0:T(4,128)(2,1)S(1)}, u32[]{:S(2)}, u32[]{:S(2)}) collective-permute-start(bf16[4,256]{1,0:T(4,128)(2,1)S(1)} %get-tuple-element.98), channel_id=1, source_target_pairs={{0,2},{1,3},{2,0},{3,1},{4,6},{5,7},{6,4},{7,5},{8,10},{9,11},{10,... | collective-permute-start | bytes 6152 | tf_op jit(solution)/shard_map/ppermute | solution.py:354
  15.7 3.6 %collective-permute-start.3 = (bf16[4,256]{1,0:T(4,128)(2,1)S(1)}, bf16[4,256]{1,0:T(4,128)(2,1)S(1)}, u32[]{:S(2)}, u32[]{:S(2)}) collective-permute-start(bf16[4,256]{1,0:T(4,128)(2,1)S(1)} %get-tuple-element.98), channel_id=1, source_target_pairs={{0,3},{1,0},{2,1},{3,2},{4,7},{5,4},{6,5},{7,6},{8,11},{9,8},{10,9... | collective-permute-start | bytes 6152 | tf_op jit(solution)/shard_map/ppermute | solution.py:354
  19.3 22.7 %collective-permute-start.10 = (bf16[128,3584]{1,0:T(8,128)(2,1)}, bf16[128,3584]{1,0:T(8,128)(2,1)S(1)}, u32[]{:S(2)}, u32[]{:S(2)}) collective-permute-start(bf16[128,3584]{1,0:T(8,128)(2,1)} %param.5), channel_id=1, source_target_pairs={{0,1},{1,2},{2,3},{3,0},{4,5},{5,6},{6,7},{7,4},{8,9},{9,10},{10,1... | collective-permute-start | bytes 2752520 | tf_op jit(solution)/shard_map/ppermute | solution.py:354
  43.0 145.1 %all-gather.9.cloned.1.call-start = ((), (), s32[]{:S(2)}) async-start(), calls=%async_computation.2 | async-start | bytes 4587520 | tf_op jit(solution)/shard_map/all_gather | solution.py:390
  53.7 134.4 %copy-start.5 = (bf16[4,4,64,256]{3,2,1,0:T(8,128)(2,1)}, bf16[4,4,64,256]{3,2,1,0:T(8,128)(2,1)S(1)}, u32[]{:S(2)}) copy-start(bf16[4,4,64,256]{3,2,1,0:T(8,128)(2,1)S(1)} %get-tuple-element.96.refs_3_) | copy-start | bytes 1572868
  53.7 19.3 %collective-permute-start.4 = (bf16[4,4,64,256]{3,2,1,0:T(8,128)(2,1)S(1)}, bf16[4,4,64,256]{3,2,1,0:T(8,128)(2,1)S(1)}, u32[]{:S(2)}, u32[]{:S(2)}) collective-permute-start(bf16[4,4,64,256]{3,2,1,0:T(8,128)(2,1)S(1)} %get-tuple-element.94), channel_id=1, source_target_pairs={{0,8},{4,12},{8,0},{12,4},{16,24},{20,28},{24,16},{28,20},{1,9},{5... | collective-permute-start | bytes 1572872 | tf_op jit(solution)/shard_map/ppermute | solution.py:351
  55.3 17.7 %collective-permute-start.5 = (bf16[4,4,64,256]{3,2,1,0:T(8,128)(2,1)S(1)}, bf16[4,4,64,256]{3,2,1,0:T(8,128)(2,1)S(1)}, u32[]{:S(2)}, u32[]{:S(2)}) collective-permute-start(bf16[4,4,64,256]{3,2,1,0:T(8,128)(2,1)S(1)} %get-tuple-element.95), channel_id=1, source_target_pairs={{0,16},{4,20},{8,24},{12,28},{16,0},{20,4},{24,8},{28,12},{1,17},{... | collective-permute-start | bytes 1572872 | tf_op jit(solution)/shard_map/ppermute | solution.py:351
  56.8 29.8 %collective-permute-start.6 = (bf16[4,4,64,256]{3,2,1,0:T(8,128)(2,1)S(1)}, bf16[4,4,64,256]{3,2,1,0:T(8,128)(2,1)S(1)}, u32[]{:S(2)}, u32[]{:S(2)}) collective-permute-start(bf16[4,4,64,256]{3,2,1,0:T(8,128)(2,1)S(1)} %get-tuple-element.93), channel_id=1, source_target_pairs={{0,24},{4,28},{8,16},{12,20},{16,8},{20,12},{24,0},{28,4},{1,25},{... | collective-permute-start | bytes 1572872 | tf_op jit(solution)/shard_map/ppermute | solution.py:351
  73.0 85.8 %copy-start.12 = (bf16[4,4,64,256]{3,2,1,0:T(8,128)(2,1)}, bf16[4,4,64,256]{3,2,1,0:T(8,128)(2,1)S(1)}, u32[]{:S(2)}) copy-start(bf16[4,4,64,256]{3,2,1,0:T(8,128)(2,1)S(1)} %collective-permute-done.4.refs_4_) | copy-start | bytes 1572868
  73.0 85.8 %copy-start.15 = (bf16[4,4,64,256]{3,2,1,0:T(8,128)(2,1)}, bf16[4,4,64,256]{3,2,1,0:T(8,128)(2,1)S(1)}, u32[]{:S(2)}) copy-start(bf16[4,4,64,256]{3,2,1,0:T(8,128)(2,1)S(1)} %collective-permute-done.5.refs_5_) | copy-start | bytes 1572868
  86.6 72.2 %copy-start.18 = (bf16[4,4,64,256]{3,2,1,0:T(8,128)(2,1)}, bf16[4,4,64,256]{3,2,1,0:T(8,128)(2,1)S(1)}, u32[]{:S(2)}) copy-start(bf16[4,4,64,256]{3,2,1,0:T(8,128)(2,1)S(1)} %collective-permute-done.6.refs_6_) | copy-start | bytes 1572868
  86.6 20.9 %collective-permute-start.15 = (bf16[128,3584]{1,0:T(8,128)(2,1)}, bf16[128,3584]{1,0:T(8,128)(2,1)S(1)}, u32[]{:S(2)}, u32[]{:S(2)}) collective-permute-start(bf16[128,3584]{1,0:T(8,128)(2,1)} %copy-done.34), channel_id=1, source_target_pairs={{0,1},{1,2},{2,3},{3,0},{4,5},{5,6},{6,7},{7,4},{8,9},{9,10},{10,1... | collective-permute-start | bytes 2752520 | tf_op jit(solution)/shard_map/ppermute | solution.py:354
  108.5 121.7 %all-gather.11.cloned.1.call-start = ((), (), s32[]{:S(2)}) async-start(), calls=%async_computation.3 | async-start | bytes 4587520 | tf_op jit(solution)/shard_map/all_gather | solution.py:390
  113.1 25.7 %collective-permute-start = (bf16[512,3584]{1,0:T(8,128)(2,1)}, bf16[512,3584]{1,0:T(8,128)(2,1)}, u32[]{:S(2)}, u32[]{:S(2)}) collective-permute-start(bf16[512,3584]{1,0:T(8,128)(2,1)} %bitcast.9.refs_1_), channel_id=1, source_target_pairs={{0,4},{4,0},{8,12},{12,8},{16,20},{20,16},{24,28},{28,24},{1,5},{5... | collective-permute-start | bytes 11010056 | tf_op jit(solution)/shard_map/ppermute | solution.py:351
  113.1 24.6 %collective-permute-start.20 = (bf16[128,3584]{1,0:T(8,128)(2,1)S(1)}, bf16[128,3584]{1,0:T(8,128)(2,1)S(1)}, u32[]{:S(2)}, u32[]{:S(2)}) collective-permute-start(bf16[128,3584]{1,0:T(8,128)(2,1)S(1)} %copy-done.37), channel_id=1, source_target_pairs={{0,1},{1,2},{2,3},{3,0},{4,5},{5,6},{6,7},{7,4},{8,9},{9,10},{10,1... | collective-permute-start | bytes 2752520 | tf_op jit(solution)/shard_map/ppermute | solution.py:354
  155.3 21.7 %collective-permute-start.7 = (bf16[4,64,256]{2,1,0:T(8,128)(2,1)S(1)}, bf16[4,64,256]{2,1,0:T(8,128)(2,1)S(1)}, u32[]{:S(2)}, u32[]{:S(2)}) collective-permute-start(bf16[4,64,256]{2,1,0:T(8,128)(2,1)S(1)} %get-tuple-element.41), channel_id=1, source_target_pairs={{0,8},{4,12},{8,0},{12,4},{16,24},{20,28},{24,16},{28,20},{1,9},{5... | collective-permute-start | bytes 393224 | tf_op jit(solution)/shard_map/ppermute | solution.py:351
  155.9 24.6 %collective-permute-start.8 = (bf16[4,64,256]{2,1,0:T(8,128)(2,1)S(1)}, bf16[4,64,256]{2,1,0:T(8,128)(2,1)S(1)}, u32[]{:S(2)}, u32[]{:S(2)}) collective-permute-start(bf16[4,64,256]{2,1,0:T(8,128)(2,1)S(1)} %get-tuple-element.42), channel_id=1, source_target_pairs={{0,16},{4,20},{8,24},{12,28},{16,0},{20,4},{24,8},{28,12},{1,17},{... | collective-permute-start | bytes 393224 | tf_op jit(solution)/shard_map/ppermute | solution.py:351
  156.3 24.2 %collective-permute-start.9 = (bf16[4,64,256]{2,1,0:T(8,128)(2,1)S(1)}, bf16[4,64,256]{2,1,0:T(8,128)(2,1)S(1)}, u32[]{:S(2)}, u32[]{:S(2)}) collective-permute-start(bf16[4,64,256]{2,1,0:T(8,128)(2,1)S(1)} %get-tuple-element.43), channel_id=1, source_target_pairs={{0,24},{4,28},{8,16},{12,20},{16,8},{20,12},{24,0},{28,4},{1,25},{... | collective-permute-start | bytes 393224 | tf_op jit(solution)/shard_map/ppermute | solution.py:351
  176.0 6.0 %collective-permute-start.11 = (bf16[4,64,256]{2,1,0:T(8,128)(2,1)}, bf16[4,64,256]{2,1,0:T(8,128)(2,1)S(1)}, u32[]{:S(2)}, u32[]{:S(2)}) collective-permute-start(bf16[4,64,256]{2,1,0:T(8,128)(2,1)} %get-tuple-element.47), channel_id=1, source_target_pairs={{0,8},{4,12},{8,0},{12,4},{16,24},{20,28},{24,16},{28,20},{1,9},{5... | collective-permute-start | bytes 393224 | tf_op jit(solution)/shard_map/ppermute | solution.py:351
  176.6 7.0 %collective-permute-start.12 = (bf16[4,64,256]{2,1,0:T(8,128)(2,1)}, bf16[4,64,256]{2,1,0:T(8,128)(2,1)S(1)}, u32[]{:S(2)}, u32[]{:S(2)}) collective-permute-start(bf16[4,64,256]{2,1,0:T(8,128)(2,1)} %get-tuple-element.48), channel_id=1, source_target_pairs={{0,16},{4,20},{8,24},{12,28},{16,0},{20,4},{24,8},{28,12},{1,17},{... | collective-permute-start | bytes 393224 | tf_op jit(solution)/shard_map/ppermute | solution.py:351
  177.0 6.6 %collective-permute-start.13 = (bf16[4,64,256]{2,1,0:T(8,128)(2,1)}, bf16[4,64,256]{2,1,0:T(8,128)(2,1)}, u32[]{:S(2)}, u32[]{:S(2)}) collective-permute-start(bf16[4,64,256]{2,1,0:T(8,128)(2,1)} %get-tuple-element.49), channel_id=1, source_target_pairs={{0,24},{4,28},{8,16},{12,20},{16,8},{20,12},{24,0},{28,4},{1,25},{... | collective-permute-start | bytes 393224 | tf_op jit(solution)/shard_map/ppermute | solution.py:351
  185.3 44.9 %collective-permute-start.14 = (f32[4,128]{1,0:T(4,128)S(1)}, f32[4,128]{1,0:T(4,128)S(1)}, u32[]{:S(2)}, u32[]{:S(2)}) collective-permute-start(f32[4,128]{1,0:T(4,128)S(1)} %get-tuple-element.51), channel_id=1, source_target_pairs={{0,3},{1,0},{2,1},{3,2},{4,7},{5,4},{6,5},{7,6},{8,11},{9,8},{10,9... | collective-permute-start | bytes 6152 | tf_op jit(solution)/shard_map/ppermute | solution.py:354
  194.3 14.4 %copy-start.25 = (bf16[512,3584]{1,0:T(8,128)(2,1)S(1)}, bf16[512,3584]{1,0:T(8,128)(2,1)}, u32[]{:S(2)}) copy-start(bf16[512,3584]{1,0:T(8,128)(2,1)} %copy-done.24) | copy-start | bytes 11010052
  194.3 14.4 %copy-start.27 = (bf16[512,3584]{1,0:T(8,128)(2,1)S(1)}, bf16[512,3584]{1,0:T(8,128)(2,1)}, u32[]{:S(2)}) copy-start(bf16[512,3584]{1,0:T(8,128)(2,1)} %copy-done.26) | copy-start | bytes 11010052
  194.3 14.4 %copy-start.31 = (bf16[2,512,512]{2,1,0:T(8,128)(2,1)S(1)}, bf16[2,512,512]{2,1,0:T(8,128)(2,1)}, u32[]{:S(2)}) copy-start(bf16[2,512,512]{2,1,0:T(8,128)(2,1)} %copy-done.30) | copy-start | bytes 3145732
  194.3 14.4 %copy-start.33 = (bf16[2,512,512]{2,1,0:T(8,128)(2,1)S(1)}, bf16[2,512,512]{2,1,0:T(8,128)(2,1)}, u32[]{:S(2)}) copy-start(bf16[2,512,512]{2,1,0:T(8,128)(2,1)} %copy-done.32) | copy-start | bytes 3145732
  225.0 5.2 %copy-start = (f32[2,512,3584]{2,1,0:T(8,128)}, f32[2,512,3584]{2,1,0:T(8,128)S(1)}, u32[]{:S(2)}) copy-start(f32[2,512,3584]{2,1,0:T(8,128)S(1)} %shard_map.82.before_ref) | copy-start | bytes 44040196
  230.2 18.1 %copy-start.42 = (f32[4,128]{1,0:T(4,128)}, f32[4,128]{1,0:T(4,128)S(1)}, u32[]{:S(2)}) copy-start(f32[4,128]{1,0:T(4,128)S(1)} %collective-permute-done.14) | copy-start | bytes 6148
  236.4 11.9 %copy-start.1 = (f32[2,512,3584]{2,1,0:T(8,128)S(1)}, f32[2,512,3584]{2,1,0:T(8,128)}, u32[]{:S(2)}) copy-start(f32[2,512,3584]{2,1,0:T(8,128)} %copy-done) | copy-start | bytes 44040196
  248.3 4.9 %copy-start.3 = (bf16[512,3584]{1,0:T(8,128)(2,1)}, bf16[512,3584]{1,0:T(8,128)(2,1)S(1)}, u32[]{:S(2)}) copy-start(bf16[512,3584]{1,0:T(8,128)(2,1)S(1)} %get-tuple-element.76.rows_ref) | copy-start | bytes 11010052
  248.3 4.9 %copy-start.21 = (bf16[4,64,256]{2,1,0:T(8,128)(2,1)}, bf16[4,64,256]{2,1,0:T(8,128)(2,1)S(1)}, u32[]{:S(2)}) copy-start(bf16[4,64,256]{2,1,0:T(8,128)(2,1)S(1)} %get-tuple-element.71) | copy-start | bytes 393220
  248.3 4.9 %copy-start.22 = (bf16[4,64,256]{2,1,0:T(8,128)(2,1)}, bf16[4,64,256]{2,1,0:T(8,128)(2,1)S(1)}, u32[]{:S(2)}) copy-start(bf16[4,64,256]{2,1,0:T(8,128)(2,1)S(1)} %get-tuple-element.70) | copy-start | bytes 393220
  248.3 4.9 %copy-start.23 = (bf16[4,64,256]{2,1,0:T(8,128)(2,1)}, bf16[4,64,256]{2,1,0:T(8,128)(2,1)S(1)}, u32[]{:S(2)}) copy-start(bf16[4,64,256]{2,1,0:T(8,128)(2,1)S(1)} %get-tuple-element.69) | copy-start | bytes 393220
  253.2 24.0 %collective-permute-start.25 = (bf16[512,3584]{1,0:T(8,128)(2,1)}, bf16[512,3584]{1,0:T(8,128)(2,1)}, u32[]{:S(2)}, u32[]{:S(2)}) collective-permute-start(bf16[512,3584]{1,0:T(8,128)(2,1)} %shard_map.85), channel_id=1, source_target_pairs={{0,4},{4,0},{8,12},{12,8},{16,20},{20,16},{24,28},{28,24},{1,5},{5... | collective-permute-start | bytes 11010056 | tf_op jit(solution)/shard_map/ppermute | solution.py:351
  253.3 6.7 %collective-permute-start.16 = (bf16[4,64,256]{2,1,0:T(8,128)(2,1)}, bf16[4,64,256]{2,1,0:T(8,128)(2,1)}, u32[]{:S(2)}, u32[]{:S(2)}) collective-permute-start(bf16[4,64,256]{2,1,0:T(8,128)(2,1)} %get-tuple-element.55), channel_id=1, source_target_pairs={{0,8},{4,12},{8,0},{12,4},{16,24},{20,28},{24,16},{28,20},{1,9},{5... | collective-permute-start | bytes 393224 | tf_op jit(solution)/shard_map/ppermute | solution.py:351
  254.2 8.7 %collective-permute-start.17 = (bf16[4,64,256]{2,1,0:T(8,128)(2,1)}, bf16[4,64,256]{2,1,0:T(8,128)(2,1)}, u32[]{:S(2)}, u32[]{:S(2)}) collective-permute-start(bf16[4,64,256]{2,1,0:T(8,128)(2,1)} %get-tuple-element.56), channel_id=1, source_target_pairs={{0,16},{4,20},{8,24},{12,28},{16,0},{20,4},{24,8},{28,12},{1,17},{... | collective-permute-start | bytes 393224 | tf_op jit(solution)/shard_map/ppermute | solution.py:351
  255.2 9.8 %collective-permute-start.18 = (bf16[4,64,256]{2,1,0:T(8,128)(2,1)}, bf16[4,64,256]{2,1,0:T(8,128)(2,1)}, u32[]{:S(2)}, u32[]{:S(2)}) collective-permute-start(bf16[4,64,256]{2,1,0:T(8,128)(2,1)} %get-tuple-element.57), channel_id=1, source_target_pairs={{0,24},{4,28},{8,16},{12,20},{16,8},{20,12},{24,0},{28,4},{1,25},{... | collective-permute-start | bytes 393224 | tf_op jit(solution)/shard_map/ppermute | solution.py:351
  256.9 12.4 %collective-permute-start.21 = (bf16[4,64,256]{2,1,0:T(8,128)(2,1)}, bf16[4,64,256]{2,1,0:T(8,128)(2,1)S(1)}, u32[]{:S(2)}, u32[]{:S(2)}) collective-permute-start(bf16[4,64,256]{2,1,0:T(8,128)(2,1)} %copy-done.23), channel_id=1, source_target_pairs={{0,8},{4,12},{8,0},{12,4},{16,24},{20,28},{24,16},{28,20},{1,9},{5... | collective-permute-start | bytes 393224 | tf_op jit(solution)/shard_map/ppermute | solution.py:351
  260.0 9.3 %collective-permute-start.22 = (bf16[4,64,256]{2,1,0:T(8,128)(2,1)}, bf16[4,64,256]{2,1,0:T(8,128)(2,1)}, u32[]{:S(2)}, u32[]{:S(2)}) collective-permute-start(bf16[4,64,256]{2,1,0:T(8,128)(2,1)} %copy-done.22), channel_id=1, source_target_pairs={{0,16},{4,20},{8,24},{12,28},{16,0},{20,4},{24,8},{28,12},{1,17},{... | collective-permute-start | bytes 393224 | tf_op jit(solution)/shard_map/ppermute | solution.py:351
  263.0 6.4 %collective-permute-start.23 = (bf16[4,64,256]{2,1,0:T(8,128)(2,1)}, bf16[4,64,256]{2,1,0:T(8,128)(2,1)}, u32[]{:S(2)}, u32[]{:S(2)}) collective-permute-start(bf16[4,64,256]{2,1,0:T(8,128)(2,1)} %copy-done.21), channel_id=1, source_target_pairs={{0,24},{4,28},{8,16},{12,20},{16,8},{20,12},{24,0},{28,4},{1,25},{... | collective-permute-start | bytes 393224 | tf_op jit(solution)/shard_map/ppermute | solution.py:351
  266.9 8.8 %collective-permute-start.19 = (f32[4,128]{1,0:T(4,128)S(1)}, f32[4,128]{1,0:T(4,128)S(1)}, u32[]{:S(2)}, u32[]{:S(2)}) collective-permute-start(f32[4,128]{1,0:T(4,128)S(1)} %get-tuple-element.59), channel_id=1, source_target_pairs={{0,2},{1,3},{2,0},{3,1},{4,6},{5,7},{6,4},{7,5},{8,10},{9,11},{10,... | collective-permute-start | bytes 6152 | tf_op jit(solution)/shard_map/ppermute | solution.py:354
  271.1 5.4 %collective-permute-start.24 = (f32[4,128]{1,0:T(4,128)S(1)}, f32[4,128]{1,0:T(4,128)S(1)}, u32[]{:S(2)}, u32[]{:S(2)}) collective-permute-start(f32[4,128]{1,0:T(4,128)S(1)} %get-tuple-element.73), channel_id=1, source_target_pairs={{0,1},{1,2},{2,3},{3,0},{4,5},{5,6},{6,7},{7,4},{8,9},{9,10},{10,1... | collective-permute-start | bytes 6152 | tf_op jit(solution)/shard_map/ppermute | solution.py:354
  272.6 4.6 %copy-start.4 = (bf16[512,3584]{1,0:T(8,128)(2,1)S(1)}, bf16[512,3584]{1,0:T(8,128)(2,1)}, u32[]{:S(2)}) copy-start(bf16[512,3584]{1,0:T(8,128)(2,1)} %copy-done.3) | copy-start | bytes 11010052
  277.3 5.2 %copy-start.2 = (f32[2,512,3584]{2,1,0:T(8,128)S(1)}, f32[2,512,3584]{2,1,0:T(8,128)}, u32[]{:S(2)}) copy-start(f32[2,512,3584]{2,1,0:T(8,128)} %copy-done) | copy-start | bytes 44040196
  (27 other events, 53.2 us)
Sparse Core Ops, SparseCore 0:
  9.8 56.8 all-gather.4
  68.6 52.1 all-gather.6
  122.6 53.9 all-gather.8
  178.3 51.1 all-gather.10

commit v5 on v3

--- a/solution.py
+++ b/solution.py
@@ -353,71 +353,97 @@
     def around(array, shift):
         return lax.ppermute(array, "exp", [(i, (i + shift) % sources) for i in range(sources)])
 
-    def after(array, other):
-        return lax.optimization_barrier((array, other))[0]
-
     totals = jnp.sum(affinity, axis=-1, keepdims=True)
     shares = affinity / totals
     route_weight = (ROUTE_SCALE * shares).astype(BF16)
     meta = jnp.concatenate([routes.astype(BF16).T, route_weight.T], axis=1)
-    metas = jnp.stack([meta] + [around(meta, shift) for shift in range(1, sources)])
-    carried = after(grad_out, metas)
-    metas = jnp.take(metas, lax.rem(me - jnp.arange(sources) + sources, sources), axis=0)
+    fence = lax.optimization_barrier
+    half = tokens // 2
+
+    def kernel(step, pieces):
+        source = lax.rem(me - step + sources, sources)
+        index = jnp.stack([source, me * experts, core]).astype(jnp.int32)
+        *grads, scatter, row = project(index, pieces, own_weight, partner_weight, hidden, top_k)
+        return grads, scatter, row
+
+    def send_back(grads):
+        return [grads[0]] + [across(grads[m], 2 * m) for m in range(1, 4)]
+
+    def put(step, returned, placed):
+        source = lax.rem(me - step + sources, sources)
+        return place(jnp.stack([source] + chips).astype(jnp.int32), returned, placed, sources, top_k)
+
+    metas = [meta] + [around(meta, shift) for shift in range(1, sources)]
+    x0, y0, next1 = across(grad_out, 2), across(grad_out, 4), around(grad_out, 1)
+    held = jnp.transpose(saved_hidden.reshape(experts, sources, most, 4, pair), (3, 0, 1, 2, 4))
+    held = fence(held)
+    own_weight = jnp.transpose(down_proj, (1, 0, 2)).reshape(experts * block, width)
+    metas, x0, y0, next1, held, own_weight = fence((metas, x0, y0, next1, held, own_weight))
+
+    metas = jnp.take(jnp.stack(metas), lax.rem(me - jnp.arange(sources) + sources, sources), axis=0)
     blank = jnp.zeros((experts, sources, SLOT_PAD - most - top_k, pair), BF16)
     metas = jnp.broadcast_to(metas[None], (experts, sources, top_k, pair))
-
-    held = saved_hidden.reshape(experts, sources, most, 4, pair)
-    held = lax.optimization_barrier(jnp.transpose(held, (3, 0, 1, 2, 4)))
     hidden = []
     for m in range(4):
         piece = lax.dynamic_index_in_dim(held, chips[m], axis=0, keepdims=False)
         piece = jnp.concatenate([piece, blank, metas], axis=2)
         hidden.append(across(piece, 2 * m) if m else piece)
-
-    own_weight = jnp.transpose(down_proj, (1, 0, 2)).reshape(experts * block, width)
-    own_weight = lax.optimization_barrier(own_weight)
+    top0, bottom0 = across(x0[:half], 4), across(y0[half:], 2)
+    next2 = around(next1, 1)
     partner_weight = across(own_weight, 1)
-
-    half = tokens // 2
-    shards = [grad_out]
-    for step in range(1, sources):
-        carried = around(carried, 1)
-        shards.append(carried)
-    scatters, rows, returned, indices, placed, combines = [], [], [], [], [None], []
-    for step in range(sources):
-        own = shards[step]
-        sent = own if step < 2 else after(own, scatters[step - 2])
-        from_x, from_y = across(sent, 2), across(sent, 4)
-        top, bottom = across(from_x[:half], 4), across(from_y[half:], 2)
-        source = lax.rem(me - step + sources, sources)
-        index = jnp.stack([source, me * experts, core]).astype(jnp.int32)
-        if step >= 2:
-            own = after(own, combines[step - 2])
-        if step == sources - 1:
-            before = early_grad(scatters, rows, 512)
-            own = after(own, before)
-        *grads, scatter, row = project(
-            index, [own, from_x, from_y, top, bottom], own_weight, partner_weight, hidden, top_k
-        )
-        scatters.append(scatter)
-        rows.append(row)
-        returned = [grads[0]] + [across(grads[m], 2 * m) for m in range(1, 4)]
-        indices = jnp.stack([source] + chips).astype(jnp.int32)
-        spot, combine = place(indices, returned, placed[-1], sources, top_k)
-        placed.append(spot)
-        combines.append(around(combine, -step) if step else combine)
-    partner = late_grad((1 - core).reshape(1), scatters[-1], rows[-1], before, None, experts, 896)
+    hidden, top0, bottom0, next2, partner_weight, x0, y0, next1 = fence(
+        (hidden, top0, bottom0, next2, partner_weight, x0, y0, next1)
+    )
+
+    x1, y1, x3 = across(next1, 2), across(next1, 4), around(x0, -1)
+    grads0, scatter0, row0 = kernel(0, [grad_out, x0, y0, top0, bottom0])
+    x1, y1, x3, grads0, scatter0, row0, y0, top0, bottom0, next2 = fence(
+        (x1, y1, x3, grads0, scatter0, row0, y0, top0, bottom0, next2)
+    )
+
+    top1, bottom1 = across(x1[:half], 4), across(y1[half:], 2)
+    x2, y2, y3, own3 = across(next2, 2), across(next2, 4), around(y0, -1), around(grad_out, -1)
+    returned0 = send_back(grads0)
+    top1, bottom1, x2, y2, y3, own3, returned0, top0, bottom0 = fence(
+        (top1, bottom1, x2, y2, y3, own3, returned0, top0, bottom0)
+    )
+
+    top2, bottom2 = across(x2[:half], 4), across(y2[half:], 2)
+    top3, bottom3 = around(top0, -1), around(bottom0, -1)
+    grads1, scatter1, row1 = kernel(1, [next1, x1, y1, top1, bottom1])
+    placed, combine0 = put(0, returned0, None)
+    top2, bottom2, top3, bottom3, grads1, scatter1, row1, placed, combine0, x3 = fence(
+        (top2, bottom2, top3, bottom3, grads1, scatter1, row1, placed, combine0, x3)
+    )
+
+    returned1 = send_back(grads1)
+    grads2, scatter2, row2 = kernel(2, [next2, x2, y2, top2, bottom2])
+    returned1, grads2, scatter2, row2, x3 = fence((returned1, grads2, scatter2, row2, x3))
+
+    returned2 = send_back(grads2)
+    placed, combine1 = put(1, returned1, placed)
+    grads3, scatter3, row3 = kernel(3, [own3, x3, y3, top3, bottom3])
+    before = early_grad([scatter0, scatter1, scatter2], [row0, row1, row2], 512)
+    returned2, placed, combine1, grads3, scatter3, row3, before = fence(
+        (returned2, placed, combine1, grads3, scatter3, row3, before)
+    )
+
+    returned3 = send_back(grads3)
+    partner = late_grad((1 - core).reshape(1), scatter3, row3, before, None, experts, 896)
     partner = across(partner, 1)
+    placed, combine2 = put(2, returned2, placed)
+    placed, combine3 = put(3, returned3, placed)
+    combines = [combine0, around(combine1, -1), around(combine2, -2), around(combine3, 1)]
     route_grad = 0.0
     expert_ids = jnp.arange(experts, dtype=routes.dtype)
     for step in range(sources):
         ids = lax.rem(me + step, sources) * experts + expert_ids
         named = routes.T[:, None, :] == ids[None, :, None]
         route_grad += jnp.sum(jnp.where(named, combines[step][None], 0.0), axis=1)
-    hidden_grad = jnp.transpose(placed[-1][:, :, :most], (1, 0, 2, 3)).reshape(saved_hidden.shape)
+    hidden_grad = jnp.transpose(placed[:, :, :most], (1, 0, 2, 3)).reshape(saved_hidden.shape)
     route_grad = ROUTE_SCALE * route_grad.T
     affinity_grad = (route_grad - jnp.sum(route_grad * shares, axis=-1, keepdims=True)) / totals
-    down_grad = late_grad(core.reshape(1), scatters[-1], rows[-1], before, partner, experts, 896)
+    down_grad = late_grad(core.reshape(1), scatter3, row3, before, partner, experts, 896)
     return (affinity_grad, hidden_grad, down_grad)
 
 
@@ -427,7 +453,7 @@
     tokens, top_k = routes.shape
     most = saved_hidden.shape[3]
     fits = block == 128 and tokens == 128 and width % 3584 == 0 and reps == 8 and 8 % experts == 0
-    fits = fits and sources > 1 and most + top_k <= SLOT_PAD and top_k <= 8
+    fits = fits and sources == 4 and most + top_k <= SLOT_PAD and top_k <= 8
     if fits and sources * tokens <= 2 * block * experts:
         return on_device_tokens(grad_out, routes, affinity, saved_hidden, down_proj)
     return on_device_weights(grad_out, routes, affinity, saved_hidden, down_proj)

time: 305 us -> 270 us (0.89)
  waiting for transfers between devices: 95 us -> 60.8 us
  starting transfers between devices: 55.2 us -> 61.8 us
  local copies, waits for them, and re-layouts: 60.6 us -> 55.2 us
  Pallas kernels: 87.9 us -> 84.6 us
    ppermute x33 -> x29, waiting for transfers between devices: 92.2 us -> 35.8 us  [across(): return lax.ppermute(array, 'rep', [(i, i ^ bits) for i in range(reps)])]
    ppermute x9 -> x13, waiting for transfers between devices: 2.78 us -> 25 us  [around(): lax.ppermute(array, 'exp', [(i, (i + shift) % sources) for i in range(sou...]
    ppermute x9 -> x13, starting transfers between devices: 15.9 us -> 24.5 us  [around(): lax.ppermute(array, 'exp', [(i, (i + shift) % sources) for i in range(sou...]
    unnamed x127 -> x107, local copies, waits for them, and re-layouts: 43.2 us -> 34.6 us
    reshape x3, local copies, waits for them, and re-layouts: 4.63 us -> 8.71 us  [the longest x2 8.48 us: on_device_tokens(): saved_hidden.reshape(experts, sources, most, 4, pair)]
    ppermute x33 -> x29, starting transfers between devices: 39.2 us -> 37.3 us  [across(): return lax.ppermute(array, 'rep', [(i, i ^ bits) for i in range(reps)])]
  transfers between devices with their start and end apart: 42 -> 42, of which waited for: 15 -> 11; matrix products, arithmetic and copies ran while one was open for 6% -> 10% of each run, Pallas kernels for 20% -> 27%
where the time goes in v5:
time: 270 us; the launch traced here: 269 us
  Pallas kernels  84.6 us (31%)
  starting transfers between devices  61.8 us (23%)
  waiting for transfers between devices  60.8 us (23%)
  local copies, waits for them, and re-layouts  55.2 us (20%)
  other arithmetic  5.36 us (2%)
    pallas_call x4, Pallas kernels, project(): pl.pallas_call(functools.partial(project_kernel, top_k, sizes), grid_spec...  53.8 us
    ppermute x29, starting transfers between devices, across(): return lax.ppermute(array, 'rep', [(i, i ^ bits) for i in range(reps)])  37.3 us
    ppermute x29, waiting for transfers between devices, across(): return lax.ppermute(array, 'rep', [(i, i ^ bits) for i in range(reps)])  35.8 us
    unnamed x107, local copies, waits for them, and re-layouts  34.6 us
    ppermute x13, waiting for transfers between devices, around(): lax.ppermute(array, 'exp', [(i, (i + shift) % sources) for i in range(sou...  25 us
    ppermute x13, starting transfers between devices, around(): lax.ppermute(array, 'exp', [(i, (i + shift) % sources) for i in range(sou...  24.5 us
    pallas_call x1, Pallas kernels, early_grad(): pl.pallas_call(functools.partial(early_grad_kernel, terms), grid=(width /...  14.2 us
    pallas_call x2, Pallas kernels, late_grad(): pl.pallas_call(kernel, grid_spec=pltpu.PrefetchScalarGridSpec(num_scalar_...  12.4 us
  transfers between devices with their start and end apart: 42, of which 11 were waited for; matrix products, arithmetic and copies ran while one was open for 10% of the time, Pallas kernels for 27%

profile of v5, /device:TPU:0, one launch (start us, length us, event | category | flops | bytes accessed | tf_op | source)
XLA Modules:
  0.0 269.0 jit_solution(1500310585427523887)
XLA Ops:
  0.6 3.1 %collective-permute-start.5 = (bf16[128,3584]{1,0:T(8,128)(2,1)}, bf16[128,3584]{1,0:T(8,128)(2,1)}, u32[]{:S(2)}, u32[]{:S(2)}) collective-permute-start(bf16[128,3584]{1,0:T(8,128)(2,1)} %refs_0_.1), channel_id=1, source_target_pairs={{0,1},{1,2},{2,3},{3,0},{4,5},{5,6},{6,7},{7,4},{8,9},{9,10},{10,1... | collective-permute-start | bytes 2752520 | tf_op jit(solution)/shard_map/ppermute | solution.py:354
  8.8 2.3 collective-permute-start.2
  11.9 11.8 %collective-permute-done.2 = bf16[4,256]{1,0:T(4,128)(2,1)S(1)} collective-permute-done((bf16[4,256]{1,0:T(4,128)(2,1)S(1)}, bf16[4,256]{1,0:T(4,128)(2,1)S(1)}, u32[]{:S(2)}, u32[]{:S(2)}) %collective-permute-start.2) | collective-permute-done | bytes 2080 | tf_op jit(solution)/shard_map/ppermute | solution.py:354
  23.7 4.8 %reshape.87 = bf16[4,4,60,4,256]{4,3,1,2,0:T(4,128)(2,1)} reshape(bf16[1,4,4,60,1024]{4,2,3,1,0:T(4,128)(2,1)} %param.8) | data formatting | bytes 3932160 | tf_op jit(solution)/shard_map/reshape | solution.py:378
  28.5 3.7 %copy.18 = bf16[4,4,60,4,256]{4,2,1,0,3:T(8,128)(2,1)} copy(bf16[4,4,60,4,256]{4,3,1,2,0:T(4,128)(2,1)} %reshape.87) | data formatting | bytes 3932160 | tf_op jit(solution)/shard_map/reshape | solution.py:378
  32.2 2.4 copy.15
  39.4 3.8 %collective-permute-start.11 = (bf16[128,3584]{1,0:T(8,128)(2,1)}, bf16[128,3584]{1,0:T(8,128)(2,1)}, u32[]{:S(2)}, u32[]{:S(2)}) collective-permute-start(bf16[128,3584]{1,0:T(8,128)(2,1)} %collective-permute-done.5.refs_0_), channel_id=1, source_target_pairs={{0,1},{1,2},{2,3},{3,0},{4,5},{5,6},{6,7},{7,4},{8,9},{9,10},{10,1... | collective-permute-start | bytes 2752520 | tf_op jit(solution)/shard_map/ppermute | solution.py:354
  43.3 2.9 %dynamic-slice_bitcast_fusion = (bf16[4,4,60,256]{3,2,1,0:T(8,128)(2,1)}, bf16[4,4,60,256]{3,2,1,0:T(8,128)(2,1)}, bf16[4,4,60,256]{3,2,1,0:T(8,128)(2,1)}, bf16[4,4,60,256]{3,2,1,0:T(8,128)(2,1)}) fusion(bf16[4,4,4,60,256]{4,3,2,1,0:T(8,128)(2,1)} %bitcast.48, s32[]{:T(128)S(6)} %select_n.56, s32[]{:T(128)S(6)} %select_n.55, s32[]{:T(128)S(6)} %select_n.54, ...), kind=kLoop, calls=%fused_computation.7 | loop fusion | bytes 3932176 | tf_op jit(solution)/shard_map/jit(dynamic_index_in_dim)/squeeze | solution.py:388
  46.8 1.7 pad_maximum_fusion
  51.0 1.5 collective-permute-start.7
  52.5 11.9 %collective-permute-done.8.refs_10_ = bf16[4,4,64,256]{3,2,1,0:T(8,128)(2,1)S(1)} collective-permute-done((bf16[4,4,64,256]{3,2,1,0:T(8,128)(2,1)S(1)}, bf16[4,4,64,256]{3,2,1,0:T(8,128)(2,1)S(1)}, u32[]{:S(2)}, u32[]{:S(2)}) %collective-permute-start.8) | collective-permute-done | bytes 524320 | tf_op jit(solution)/shard_map/ppermute | solution.py:351
  65.3 8.0 %collective-permute-done.6.refs_8_ = bf16[4,4,64,256]{3,2,1,0:T(8,128)(2,1)S(1)} collective-permute-done((bf16[4,4,64,256]{3,2,1,0:T(8,128)(2,1)S(1)}, bf16[4,4,64,256]{3,2,1,0:T(8,128)(2,1)S(1)}, u32[]{:S(2)}, u32[]{:S(2)}) %collective-permute-start.6) | collective-permute-done | bytes 524320 | tf_op jit(solution)/shard_map/ppermute | solution.py:351
  75.1 5.0 %collective-permute-start.15 = (bf16[128,3584]{1,0:T(8,128)(2,1)S(1)}, bf16[128,3584]{1,0:T(8,128)(2,1)}, u32[]{:S(2)}, u32[]{:S(2)}) collective-permute-start(bf16[128,3584]{1,0:T(8,128)(2,1)S(1)} %collective-permute-done.3.refs_1_), channel_id=1, source_target_pairs={{0,3},{1,0},{2,1},{3,2},{4,7},{5,4},{6,5},{7,6},{8,11},{9,8},{10,9... | collective-permute-start | bytes 2752520 | tf_op jit(solution)/shard_map/ppermute | solution.py:354
  80.1 1.7 collective-permute-start.14
  81.8 2.0 collective-permute-start.21
  89.1 12.1 %shard_map.76 = (bf16[4,64,256]{2,1,0:T(8,128)(2,1)S(1)}, bf16[4,64,256]{2,1,0:T(8,128)(2,1)S(1)}, bf16[4,64,256]{2,1,0:T(8,128)(2,1)S(1)}, bf16[4,64,256]{2,1,0...) custom-call(s32[3]{0:T(128)S(1)} %get-tuple-element.251.idx_ref, ...), custom_call_target="tpu_custom_call" | custom-call | flops 7516192768 | bytes 14680064 | tf_op jit(solution)/shard_map/pallas_call | solution.py:168
  101.8 1.8 copy-done.36
  103.7 1.6 collective-permute-start.20
  105.3 1.7 collective-permute-start.19
  107.0 2.0 collective-permute-start.22
  109.1 11.6 %collective-permute-done.21.refs_0_ = bf16[128,3584]{1,0:T(8,128)(2,1)} collective-permute-done((bf16[128,3584]{1,0:T(8,128)(2,1)}, bf16[128,3584]{1,0:T(8,128)(2,1)}, u32[]{:S(2)}, u32[]{:S(2)}) %collective-permute-start.21) | collective-permute-done | bytes 917536 | tf_op jit(solution)/shard_map/ppermute | solution.py:354
  120.7 1.7 collective-permute-start.23
  122.4 5.9 %collective-permute-done.22.refs_1_ = bf16[4,64,256]{2,1,0:T(8,128)(2,1)S(1)} collective-permute-done((bf16[4,64,256]{2,1,0:T(8,128)(2,1)S(1)}, bf16[4,64,256]{2,1,0:T(8,128)(2,1)S(1)}, u32[]{:S(2)}, u32[]{:S(2)}) %collective-permute-start.22) | collective-permute-done | bytes 131104 | tf_op jit(solution)/shard_map/ppermute | solution.py:351
  128.3 2.7 %collective-permute-start.24 = (bf16[4,64,256]{2,1,0:T(8,128)(2,1)S(1)}, bf16[4,64,256]{2,1,0:T(8,128)(2,1)S(1)}, u32[]{:S(2)}, u32[]{:S(2)}) collective-permute-start(bf16[4,64,256]{2,1,0:T(8,128)(2,1)S(1)} %get-tuple-element.150), channel_id=1, source_target_pairs={{0,24},{4,28},{8,16},{12,20},{16,8},{20,12},{24,0},{28,4},{1,25},{... | collective-permute-start | bytes 393224 | tf_op jit(solution)/shard_map/ppermute | solution.py:351
  131.0 1.8 slice.23
  136.3 1.7 collective-permute-start.16
  138.3 4.2 %collective-permute-done.17.refs_4_ = bf16[64,3584]{1,0:T(8,128)(2,1)} collective-permute-done((bf16[64,3584]{1,0:T(8,128)(2,1)}, bf16[64,3584]{1,0:T(8,128)(2,1)}, u32[]{:S(2)}, u32[]{:S(2)}) %collective-permute-start.17) | collective-permute-done | bytes 458784 | tf_op jit(solution)/shard_map/ppermute | solution.py:351
  142.5 3.7 %collective-permute-done.16.refs_3_ = bf16[64,3584]{1,0:T(8,128)(2,1)} collective-permute-done((bf16[64,3584]{1,0:T(8,128)(2,1)}, bf16[64,3584]{1,0:T(8,128)(2,1)}, u32[]{:S(2)}, u32[]{:S(2)}) %collective-permute-start.16) | collective-permute-done | bytes 458784 | tf_op jit(solution)/shard_map/ppermute | solution.py:351
  147.6 2.2 collective-permute-start.26
  149.9 2.5 collective-permute-start.25
  152.4 2.8 %collective-permute-start.28 = (bf16[64,3584]{1,0:T(8,128)(2,1)}, bf16[64,3584]{1,0:T(8,128)(2,1)S(1)}, u32[]{:S(2)}, u32[]{:S(2)}) collective-permute-start(bf16[64,3584]{1,0:T(8,128)(2,1)} %copy-done.29), channel_id=1, source_target_pairs={{0,3},{1,0},{2,1},{3,2},{4,7},{5,4},{6,5},{7,6},{8,11},{9,8},{10,9... | collective-permute-start | bytes 1376264 | tf_op jit(solution)/shard_map/ppermute | solution.py:354
  159.6 12.6 %shard_map.77 = (bf16[4,64,256]{2,1,0:T(8,128)(2,1)S(1)}, bf16[4,64,256]{2,1,0:T(8,128)(2,1)S(1)}, bf16[4,64,256]{2,1,0:T(8,128)(2,1)S(1)}, bf16[4,64,256]{2,1,0...) custom-call(s32[3]{0:T(128)S(1)} %get-tuple-element.252.idx_ref, ...), custom_call_target="tpu_custom_call" | custom-call | flops 7516192768 | bytes 14680064 | tf_op jit(solution)/shard_map/pallas_call | solution.py:168
  172.2 1.9 copy-done.38
  175.4 3.3 %collective-permute-start.31 = (bf16[4,64,256]{2,1,0:T(8,128)(2,1)S(1)}, bf16[4,64,256]{2,1,0:T(8,128)(2,1)S(1)}, u32[]{:S(2)}, u32[]{:S(2)}) collective-permute-start(bf16[4,64,256]{2,1,0:T(8,128)(2,1)S(1)} %get-tuple-element.176), channel_id=1, source_target_pairs={{0,24},{4,28},{8,16},{12,20},{16,8},{20,12},{24,0},{28,4},{1,25},{... | collective-permute-start | bytes 393224 | tf_op jit(solution)/shard_map/ppermute | solution.py:351
  178.7 12.3 %shard_map.79 = (bf16[4,64,256]{2,1,0:T(8,128)(2,1)S(1)}, bf16[4,64,256]{2,1,0:T(8,128)(2,1)S(1)}, bf16[4,64,256]{2,1,0:T(8,128)(2,1)S(1)}, bf16[4,64,256]{2,1,0...) custom-call(s32[3]{0:T(128)S(1)} %get-tuple-element.253.idx_ref, ...), custom_call_target="tpu_custom_call" | custom-call | flops 7516192768 | bytes 14680064 | tf_op jit(solution)/shard_map/pallas_call | solution.py:168
  192.7 2.9 %collective-permute-start.34 = (bf16[4,64,256]{2,1,0:T(8,128)(2,1)S(1)}, bf16[4,64,256]{2,1,0:T(8,128)(2,1)S(1)}, u32[]{:S(2)}, u32[]{:S(2)}) collective-permute-start(bf16[4,64,256]{2,1,0:T(8,128)(2,1)S(1)} %get-tuple-element.189), channel_id=1, source_target_pairs={{0,24},{4,28},{8,16},{12,20},{16,8},{20,12},{24,0},{28,4},{1,25},{... | collective-permute-start | bytes 393224 | tf_op jit(solution)/shard_map/ppermute | solution.py:351
  195.6 2.0 copy-done.37
  197.7 2.0 copy-done.39
  202.2 14.2 %shard_map.82.before_ref = f32[2,512,3584]{2,1,0:T(8,128)S(1)} custom-call(bf16[2,512,512]{2,1,0:T(8,128)(2,1)S(1)} %copy-done.41, bf16[2,512,512]{2,1,0:T(8,128)(2,1)S(1)} %copy-done.43, bf16[2,512,512]{2,1,0:T(8,128)(2,1)S(1)} %copy-done.45, bf16[512,3584]{1,0:T(8,128)(2,1)S(1)} %copy-done.37, bf16[512,3584]{1,0:T(8,128)(2,1)S(1)} %copy-done.39, ...), custom_call_target="tpu_custom_call" | custom-call | flops 11274289152 | bytes 28835840 | tf_op jit(solution)/shard_map/pallas_call | solution.py:216
  216.4 16.9 %shard_map.81 = (bf16[4,64,256]{2,1,0:T(8,128)(2,1)S(1)}, bf16[4,64,256]{2,1,0:T(8,128)(2,1)S(1)}, bf16[4,64,256]{2,1,0:T(8,128)(2,1)S(1)}, bf16[4,64,256]{2,1,0...) custom-call(s32[3]{0:T(128)S(1)} %get-tuple-element.254.idx_ref, ...), custom_call_target="tpu_custom_call" | custom-call | flops 7516192768 | bytes 14680064 | tf_op jit(solution)/shard_map/pallas_call | solution.py:168
  234.2 4.8 %shard_map.85 = bf16[512,3584]{1,0:T(8,128)(2,1)} custom-call(s32[1]{0:T(128)} %bitcast.28.idx_ref, bf16[2,512,512]{2,1,0:T(8,128)(2,1)S(1)} %get-tuple-element.228.scatter_ref, bf16[512,3584]{1,0:T(8,128)(2,1)S(1)} %get-tuple-element.229.rows_ref, f32[2,512,3584]{2,1,0:T(8,128)S(1)} %shard_map.82.before_ref), custom_call_target="tpu_custom_call" | custom-call | flops 1879048192 | bytes 19398656 | tf_op jit(solution)/shard_map/pallas_call | solution.py:272
  239.8 2.9 %collective-permute-start.39 = (bf16[4,64,256]{2,1,0:T(8,128)(2,1)}, bf16[4,64,256]{2,1,0:T(8,128)(2,1)}, u32[]{:S(2)}, u32[]{:S(2)}) collective-permute-start(bf16[4,64,256]{2,1,0:T(8,128)(2,1)} %copy-done.33), channel_id=1, source_target_pairs={{0,24},{4,28},{8,16},{12,20},{16,8},{20,12},{24,0},{28,4},{1,25},{... | collective-permute-start | bytes 393224 | tf_op jit(solution)/shard_map/ppermute | solution.py:351
  243.4 2.2 collective-permute-start.35
  248.2 1.8 shard_map.84
  251.2 2.8 %copy.16 = bf16[1,4,4,60,1024]{4,2,3,1,0:T(4,128)(2,1)} copy(bf16[1,4,4,60,1024]{4,3,1,2,0:T(8,128)(2,1)S(1)} %slice_bitcast_fusion) | data formatting | bytes 3932160
  254.0 1.5 collective-permute-done.40
  256.3 5.2 %copy-done.1 = f32[2,512,3584]{2,1,0:T(8,128)S(1)} copy-done((f32[2,512,3584]{2,1,0:T(8,128)S(1)}, f32[2,512,3584]{2,1,0:T(8,128)}, u32[]{:S(2)}) %copy-start.1) | copy-done | bytes 14680088
  261.4 7.6 %shard_map.86 = f32[128,4,3584]{2,1,0:T(4,128)} custom-call(s32[1]{0:T(128)} %bitcast.17.idx_ref, bf16[2,512,512]{2,1,0:T(8,128)(2,1)S(1)} %get-tuple-element.228.scatter_ref, bf16[512,3584]{1,0:T(8,128)(2,1)S(1)} %copy-done.3, f32[2,512,3584]{2,1,0:T(8,128)S(1)} %copy-done.1, bf16[512,3584]{1,0:T(8,128)(2,1)} %collective-permute-done.41.arrived_ref), custom_call_target="tpu_custom_call" | custom-call | flops 1879048192 | bytes 19398656 | tf_op jit(solution)/shard_map/pallas_call | solution.py:272
  (188 shorter events, 43.8 us)
Async XLA Ops:
  0.6 34.0 %collective-permute-start.5 = (bf16[128,3584]{1,0:T(8,128)(2,1)}, bf16[128,3584]{1,0:T(8,128)(2,1)}, u32[]{:S(2)}, u32[]{:S(2)}) collective-permute-start(bf16[128,3584]{1,0:T(8,128)(2,1)} %refs_0_.1), channel_id=1, source_target_pairs={{0,1},{1,2},{2,3},{3,0},{4,5},{5,6},{6,7},{7,4},{8,9},{9,10},{10,1... | collective-permute-start | bytes 2752520 | tf_op jit(solution)/shard_map/ppermute | solution.py:354
  3.7 30.9 %collective-permute-start.4 = (bf16[128,3584]{1,0:T(8,128)(2,1)}, bf16[128,3584]{1,0:T(8,128)(2,1)S(1)}, u32[]{:S(2)}, u32[]{:S(2)}) collective-permute-start(bf16[128,3584]{1,0:T(8,128)(2,1)} %refs_0_.1), channel_id=1, source_target_pairs={{0,16},{4,20},{8,24},{12,28},{16,0},{20,4},{24,8},{28,12},{1,17},{... | collective-permute-start | bytes 2752520 | tf_op jit(solution)/shard_map/ppermute | solution.py:351
  5.2 29.4 %collective-permute-start.3 = (bf16[128,3584]{1,0:T(8,128)(2,1)}, bf16[128,3584]{1,0:T(8,128)(2,1)S(1)}, u32[]{:S(2)}, u32[]{:S(2)}) collective-permute-start(bf16[128,3584]{1,0:T(8,128)(2,1)} %refs_0_.1), channel_id=1, source_target_pairs={{0,8},{4,12},{8,0},{12,4},{16,24},{20,28},{24,16},{28,20},{1,9},{5... | collective-permute-start | bytes 2752520 | tf_op jit(solution)/shard_map/ppermute | solution.py:351
  7.4 24.8 %copy-start.49 = (f32[128]{0:T(128)}, f32[128]{0:T(128)S(1)}, u32[]{:S(2)}) copy-start(f32[128]{0:T(128)S(1)} %reduce_sum.54) | copy-start | bytes 1540
  8.8 14.9 %collective-permute-start.2 = (bf16[4,256]{1,0:T(4,128)(2,1)S(1)}, bf16[4,256]{1,0:T(4,128)(2,1)S(1)}, u32[]{:S(2)}, u32[]{:S(2)}) collective-permute-start(bf16[4,256]{1,0:T(4,128)(2,1)S(1)} %pad_maximum_fusion.5), channel_id=1, source_target_pairs={{0,3},{1,0},{2,1},{3,2},{4,7},{5,4},{6,5},{7,6},{8,11},{9,8},{10,9... | collective-permute-start | bytes 6152 | tf_op jit(solution)/shard_map/ppermute | solution.py:354
  11.1 23.5 %collective-permute-start.1 = (bf16[4,256]{1,0:T(4,128)(2,1)S(1)}, bf16[4,256]{1,0:T(4,128)(2,1)S(1)}, u32[]{:S(2)}, u32[]{:S(2)}) collective-permute-start(bf16[4,256]{1,0:T(4,128)(2,1)S(1)} %pad_maximum_fusion.5), channel_id=1, source_target_pairs={{0,2},{1,3},{2,0},{3,1},{4,6},{5,7},{6,4},{7,5},{8,10},{9,11},{10,... | collective-permute-start | bytes 6152 | tf_op jit(solution)/shard_map/ppermute | solution.py:354
  23.7 10.9 %collective-permute-start = (bf16[4,256]{1,0:T(4,128)(2,1)S(1)}, bf16[4,256]{1,0:T(4,128)(2,1)S(1)}, u32[]{:S(2)}, u32[]{:S(2)}) collective-permute-start(bf16[4,256]{1,0:T(4,128)(2,1)S(1)} %pad_maximum_fusion.5), channel_id=1, source_target_pairs={{0,1},{1,2},{2,3},{3,0},{4,5},{5,6},{6,7},{7,4},{8,9},{9,10},{10,1... | collective-permute-start | bytes 6152 | tf_op jit(solution)/shard_map/ppermute | solution.py:354
  34.7 40.4 %collective-permute-start.12 = (bf16[512,3584]{1,0:T(8,128)(2,1)}, bf16[512,3584]{1,0:T(8,128)(2,1)}, u32[]{:S(2)}, u32[]{:S(2)}) collective-permute-start(bf16[512,3584]{1,0:T(8,128)(2,1)} %bitcast.5.refs_5_), channel_id=1, source_target_pairs={{0,4},{4,0},{8,12},{12,8},{16,20},{20,16},{24,28},{28,24},{1,5},{5... | collective-permute-start | bytes 11010056 | tf_op jit(solution)/shard_map/ppermute | solution.py:351
  36.4 13.1 %collective-permute-start.10 = (bf16[64,3584]{1,0:T(8,128)(2,1)}, bf16[64,3584]{1,0:T(8,128)(2,1)S(1)}, u32[]{:S(2)}, u32[]{:S(2)}) collective-permute-start(bf16[64,3584]{1,0:T(8,128)(2,1)} %slice.22), channel_id=1, source_target_pairs={{0,8},{4,12},{8,0},{12,4},{16,24},{20,28},{24,16},{28,20},{1,9},{5... | collective-permute-start | bytes 1376264 | tf_op jit(solution)/shard_map/ppermute | solution.py:351
  37.9 13.1 %collective-permute-start.9 = (bf16[64,3584]{1,0:T(8,128)(2,1)}, bf16[64,3584]{1,0:T(8,128)(2,1)S(1)}, u32[]{:S(2)}, u32[]{:S(2)}) collective-permute-start(bf16[64,3584]{1,0:T(8,128)(2,1)} %slice.21), channel_id=1, source_target_pairs={{0,16},{4,20},{8,24},{12,28},{16,0},{20,4},{24,8},{28,12},{1,17},{... | collective-permute-start | bytes 1376264 | tf_op jit(solution)/shard_map/ppermute | solution.py:351
  39.4 35.6 %collective-permute-start.11 = (bf16[128,3584]{1,0:T(8,128)(2,1)}, bf16[128,3584]{1,0:T(8,128)(2,1)}, u32[]{:S(2)}, u32[]{:S(2)}) collective-permute-start(bf16[128,3584]{1,0:T(8,128)(2,1)} %collective-permute-done.5.refs_0_), channel_id=1, source_target_pairs={{0,1},{1,2},{2,3},{3,0},{4,5},{5,6},{6,7},{7,4},{8,9},{9,10},{10,1... | collective-permute-start | bytes 2752520 | tf_op jit(solution)/shard_map/ppermute | solution.py:354
  48.6 130.1 %copy-start.4 = (bf16[4,4,64,256]{3,2,1,0:T(8,128)(2,1)}, bf16[4,4,64,256]{3,2,1,0:T(8,128)(2,1)S(1)}, u32[]{:S(2)}) copy-start(bf16[4,4,64,256]{3,2,1,0:T(8,128)(2,1)S(1)} %get-tuple-element.132.refs_7_) | copy-start | bytes 1572868
  48.6 15.9 %collective-permute-start.8 = (bf16[4,4,64,256]{3,2,1,0:T(8,128)(2,1)S(1)}, bf16[4,4,64,256]{3,2,1,0:T(8,128)(2,1)S(1)}, u32[]{:S(2)}, u32[]{:S(2)}) collective-permute-start(bf16[4,4,64,256]{3,2,1,0:T(8,128)(2,1)S(1)} %get-tuple-element.247), channel_id=1, source_target_pairs={{0,24},{4,28},{8,16},{12,20},{16,8},{20,12},{24,0},{28,4},{1,25},{... | collective-permute-start | bytes 1572872 | tf_op jit(solution)/shard_map/ppermute | solution.py:351
  49.5 25.5 %copy-start.29 = (bf16[64,3584]{1,0:T(8,128)(2,1)}, bf16[64,3584]{1,0:T(8,128)(2,1)S(1)}, u32[]{:S(2)}) copy-start(bf16[64,3584]{1,0:T(8,128)(2,1)S(1)} %collective-permute-done.10.refs_4_) | copy-start | bytes 1376260
  49.5 23.8 %collective-permute-start.6 = (bf16[4,4,64,256]{3,2,1,0:T(8,128)(2,1)S(1)}, bf16[4,4,64,256]{3,2,1,0:T(8,128)(2,1)S(1)}, u32[]{:S(2)}, u32[]{:S(2)}) collective-permute-start(bf16[4,4,64,256]{3,2,1,0:T(8,128)(2,1)S(1)} %get-tuple-element.248), channel_id=1, source_target_pairs={{0,8},{4,12},{8,0},{12,4},{16,24},{20,28},{24,16},{28,20},{1,9},{5... | collective-permute-start | bytes 1572872 | tf_op jit(solution)/shard_map/ppermute | solution.py:351
  51.0 23.2 %collective-permute-start.7 = (bf16[4,4,64,256]{3,2,1,0:T(8,128)(2,1)S(1)}, bf16[4,4,64,256]{3,2,1,0:T(8,128)(2,1)S(1)}, u32[]{:S(2)}, u32[]{:S(2)}) collective-permute-start(bf16[4,4,64,256]{3,2,1,0:T(8,128)(2,1)S(1)} %get-tuple-element.249), channel_id=1, source_target_pairs={{0,16},{4,20},{8,24},{12,28},{16,0},{20,4},{24,8},{28,12},{1,17},{... | collective-permute-start | bytes 1572872 | tf_op jit(solution)/shard_map/ppermute | solution.py:351
  75.1 28.6 %collective-permute-start.15 = (bf16[128,3584]{1,0:T(8,128)(2,1)S(1)}, bf16[128,3584]{1,0:T(8,128)(2,1)}, u32[]{:S(2)}, u32[]{:S(2)}) collective-permute-start(bf16[128,3584]{1,0:T(8,128)(2,1)S(1)} %collective-permute-done.3.refs_1_), channel_id=1, source_target_pairs={{0,3},{1,0},{2,1},{3,2},{4,7},{5,4},{6,5},{7,6},{8,11},{9,8},{10,9... | collective-permute-start | bytes 2752520 | tf_op jit(solution)/shard_map/ppermute | solution.py:354
  80.1 23.6 %collective-permute-start.14 = (bf16[128,3584]{1,0:T(8,128)(2,1)}, bf16[128,3584]{1,0:T(8,128)(2,1)S(1)}, u32[]{:S(2)}, u32[]{:S(2)}) collective-permute-start(bf16[128,3584]{1,0:T(8,128)(2,1)} %collective-permute-done.5.refs_0_), channel_id=1, source_target_pairs={{0,16},{4,20},{8,24},{12,28},{16,0},{20,4},{24,8},{28,12},{1,17},{... | collective-permute-start | bytes 2752520 | tf_op jit(solution)/shard_map/ppermute | solution.py:351
  81.8 21.8 %collective-permute-start.13 = (bf16[128,3584]{1,0:T(8,128)(2,1)}, bf16[128,3584]{1,0:T(8,128)(2,1)}, u32[]{:S(2)}, u32[]{:S(2)}) collective-permute-start(bf16[128,3584]{1,0:T(8,128)(2,1)} %collective-permute-done.5.refs_0_), channel_id=1, source_target_pairs={{0,8},{4,12},{8,0},{12,4},{16,24},{20,28},{24,16},{28,20},{1,9},{5... | collective-permute-start | bytes 2752520 | tf_op jit(solution)/shard_map/ppermute | solution.py:351
  81.8 38.8 %collective-permute-start.21 = (bf16[128,3584]{1,0:T(8,128)(2,1)}, bf16[128,3584]{1,0:T(8,128)(2,1)}, u32[]{:S(2)}, u32[]{:S(2)}) collective-permute-start(bf16[128,3584]{1,0:T(8,128)(2,1)} %refs_0_.1), channel_id=1, source_target_pairs={{0,3},{1,0},{2,1},{3,2},{4,7},{5,4},{6,5},{7,6},{8,11},{9,8},{10,9... | collective-permute-start | bytes 2752520 | tf_op jit(solution)/shard_map/ppermute | solution.py:354
  103.7 32.0 %copy-start.40 = (bf16[2,512,512]{2,1,0:T(8,128)(2,1)}, bf16[2,512,512]{2,1,0:T(8,128)(2,1)S(1)}, u32[]{:S(2)}) copy-start(bf16[2,512,512]{2,1,0:T(8,128)(2,1)S(1)} %get-tuple-element.208.refs_0_) | copy-start | bytes 3145732
  103.7 42.5 %collective-permute-start.20 = (bf16[128,3584]{1,0:T(8,128)(2,1)S(1)}, bf16[128,3584]{1,0:T(8,128)(2,1)}, u32[]{:S(2)}, u32[]{:S(2)}) collective-permute-start(bf16[128,3584]{1,0:T(8,128)(2,1)S(1)} %collective-permute-done.4.refs_2_), channel_id=1, source_target_pairs={{0,3},{1,0},{2,1},{3,2},{4,7},{5,4},{6,5},{7,6},{8,11},{9,8},{10,9... | collective-permute-start | bytes 2752520 | tf_op jit(solution)/shard_map/ppermute | solution.py:354
  105.3 40.9 %collective-permute-start.19 = (bf16[128,3584]{1,0:T(8,128)(2,1)}, bf16[128,3584]{1,0:T(8,128)(2,1)S(1)}, u32[]{:S(2)}, u32[]{:S(2)}) collective-permute-start(bf16[128,3584]{1,0:T(8,128)(2,1)} %collective-permute-done.11.refs_0_), channel_id=1, source_target_pairs={{0,16},{4,20},{8,24},{12,28},{16,0},{20,4},{24,8},{28,12},{1,17},{... | collective-permute-start | bytes 2752520 | tf_op jit(solution)/shard_map/ppermute | solution.py:351
  107.0 39.2 %collective-permute-start.18 = (bf16[128,3584]{1,0:T(8,128)(2,1)}, bf16[128,3584]{1,0:T(8,128)(2,1)}, u32[]{:S(2)}, u32[]{:S(2)}) collective-permute-start(bf16[128,3584]{1,0:T(8,128)(2,1)} %collective-permute-done.11.refs_0_), channel_id=1, source_target_pairs={{0,8},{4,12},{8,0},{12,4},{16,24},{20,28},{24,16},{28,20},{1,9},{5... | collective-permute-start | bytes 2752520 | tf_op jit(solution)/shard_map/ppermute | solution.py:351
  107.0 21.2 %collective-permute-start.22 = (bf16[4,64,256]{2,1,0:T(8,128)(2,1)S(1)}, bf16[4,64,256]{2,1,0:T(8,128)(2,1)S(1)}, u32[]{:S(2)}, u32[]{:S(2)}) collective-permute-start(bf16[4,64,256]{2,1,0:T(8,128)(2,1)S(1)} %get-tuple-element.148), channel_id=1, source_target_pairs={{0,8},{4,12},{8,0},{12,4},{16,24},{20,28},{24,16},{28,20},{1,9},{5... | collective-permute-start | bytes 393224 | tf_op jit(solution)/shard_map/ppermute | solution.py:351
  120.7 13.0 %collective-permute-start.23 = (bf16[4,64,256]{2,1,0:T(8,128)(2,1)S(1)}, bf16[4,64,256]{2,1,0:T(8,128)(2,1)S(1)}, u32[]{:S(2)}, u32[]{:S(2)}) collective-permute-start(bf16[4,64,256]{2,1,0:T(8,128)(2,1)S(1)} %get-tuple-element.149), channel_id=1, source_target_pairs={{0,16},{4,20},{8,24},{12,28},{16,0},{20,4},{24,8},{28,12},{1,17},{... | collective-permute-start | bytes 393224 | tf_op jit(solution)/shard_map/ppermute | solution.py:351
  128.3 24.1 %copy-start.14 = (bf16[4,64,256]{2,1,0:T(8,128)(2,1)}, bf16[4,64,256]{2,1,0:T(8,128)(2,1)S(1)}, u32[]{:S(2)}) copy-start(bf16[4,64,256]{2,1,0:T(8,128)(2,1)S(1)} %collective-permute-done.22.refs_1_) | copy-start | bytes 393220
  128.3 7.3 %collective-permute-start.24 = (bf16[4,64,256]{2,1,0:T(8,128)(2,1)S(1)}, bf16[4,64,256]{2,1,0:T(8,128)(2,1)S(1)}, u32[]{:S(2)}, u32[]{:S(2)}) collective-permute-start(bf16[4,64,256]{2,1,0:T(8,128)(2,1)S(1)} %get-tuple-element.150), channel_id=1, source_target_pairs={{0,24},{4,28},{8,16},{12,20},{16,8},{20,12},{24,0},{28,4},{1,25},{... | collective-permute-start | bytes 393224 | tf_op jit(solution)/shard_map/ppermute | solution.py:351
  133.7 8.8 %collective-permute-start.17 = (bf16[64,3584]{1,0:T(8,128)(2,1)}, bf16[64,3584]{1,0:T(8,128)(2,1)}, u32[]{:S(2)}, u32[]{:S(2)}) collective-permute-start(bf16[64,3584]{1,0:T(8,128)(2,1)} %slice.24), channel_id=1, source_target_pairs={{0,8},{4,12},{8,0},{12,4},{16,24},{20,28},{24,16},{28,20},{1,9},{5... | collective-permute-start | bytes 1376264 | tf_op jit(solution)/shard_map/ppermute | solution.py:351
  136.3 9.9 %collective-permute-start.16 = (bf16[64,3584]{1,0:T(8,128)(2,1)}, bf16[64,3584]{1,0:T(8,128)(2,1)}, u32[]{:S(2)}, u32[]{:S(2)}) collective-permute-start(bf16[64,3584]{1,0:T(8,128)(2,1)} %slice.23), channel_id=1, source_target_pairs={{0,16},{4,20},{8,24},{12,28},{16,0},{20,4},{24,8},{28,12},{1,17},{... | collective-permute-start | bytes 1376264 | tf_op jit(solution)/shard_map/ppermute | solution.py:351
  147.6 27.5 %collective-permute-start.26 = (bf16[64,3584]{1,0:T(8,128)(2,1)S(1)}, bf16[64,3584]{1,0:T(8,128)(2,1)S(1)}, u32[]{:S(2)}, u32[]{:S(2)}) collective-permute-start(bf16[64,3584]{1,0:T(8,128)(2,1)S(1)} %slice.26), channel_id=1, source_target_pairs={{0,8},{4,12},{8,0},{12,4},{16,24},{20,28},{24,16},{28,20},{1,9},{5... | collective-permute-start | bytes 1376264 | tf_op jit(solution)/shard_map/ppermute | solution.py:351
  149.9 25.3 %collective-permute-start.25 = (bf16[64,3584]{1,0:T(8,128)(2,1)S(1)}, bf16[64,3584]{1,0:T(8,128)(2,1)S(1)}, u32[]{:S(2)}, u32[]{:S(2)}) collective-permute-start(bf16[64,3584]{1,0:T(8,128)(2,1)S(1)} %slice.25), channel_id=1, source_target_pairs={{0,16},{4,20},{8,24},{12,28},{16,0},{20,4},{24,8},{28,12},{1,17},{... | collective-permute-start | bytes 1376264 | tf_op jit(solution)/shard_map/ppermute | solution.py:351
  152.4 22.8 %collective-permute-start.27 = (bf16[64,3584]{1,0:T(8,128)(2,1)}, bf16[64,3584]{1,0:T(8,128)(2,1)S(1)}, u32[]{:S(2)}, u32[]{:S(2)}) collective-permute-start(bf16[64,3584]{1,0:T(8,128)(2,1)} %copy-done.31), channel_id=1, source_target_pairs={{0,3},{1,0},{2,1},{3,2},{4,7},{5,4},{6,5},{7,6},{8,11},{9,8},{10,9... | collective-permute-start | bytes 1376264 | tf_op jit(solution)/shard_map/ppermute | solution.py:354
  152.4 22.8 %collective-permute-start.28 = (bf16[64,3584]{1,0:T(8,128)(2,1)}, bf16[64,3584]{1,0:T(8,128)(2,1)S(1)}, u32[]{:S(2)}, u32[]{:S(2)}) collective-permute-start(bf16[64,3584]{1,0:T(8,128)(2,1)} %copy-done.29), channel_id=1, source_target_pairs={{0,3},{1,0},{2,1},{3,2},{4,7},{5,4},{6,5},{7,6},{8,11},{9,8},{10,9... | collective-permute-start | bytes 1376264 | tf_op jit(solution)/shard_map/ppermute | solution.py:354
  175.1 16.9 %collective-permute-start.29 = (bf16[4,64,256]{2,1,0:T(8,128)(2,1)S(1)}, bf16[4,64,256]{2,1,0:T(8,128)(2,1)S(1)}, u32[]{:S(2)}, u32[]{:S(2)}) collective-permute-start(bf16[4,64,256]{2,1,0:T(8,128)(2,1)S(1)} %get-tuple-element.174), channel_id=1, source_target_pairs={{0,8},{4,12},{8,0},{12,4},{16,24},{20,28},{24,16},{28,20},{1,9},{5... | collective-permute-start | bytes 393224 | tf_op jit(solution)/shard_map/ppermute | solution.py:351
  175.3 16.8 %collective-permute-start.30 = (bf16[4,64,256]{2,1,0:T(8,128)(2,1)S(1)}, bf16[4,64,256]{2,1,0:T(8,128)(2,1)S(1)}, u32[]{:S(2)}, u32[]{:S(2)}) collective-permute-start(bf16[4,64,256]{2,1,0:T(8,128)(2,1)S(1)} %get-tuple-element.175), channel_id=1, source_target_pairs={{0,16},{4,20},{8,24},{12,28},{16,0},{20,4},{24,8},{28,12},{1,17},{... | collective-permute-start | bytes 393224 | tf_op jit(solution)/shard_map/ppermute | solution.py:351
  175.4 16.7 %collective-permute-start.31 = (bf16[4,64,256]{2,1,0:T(8,128)(2,1)S(1)}, bf16[4,64,256]{2,1,0:T(8,128)(2,1)S(1)}, u32[]{:S(2)}, u32[]{:S(2)}) collective-permute-start(bf16[4,64,256]{2,1,0:T(8,128)(2,1)S(1)} %get-tuple-element.176), channel_id=1, source_target_pairs={{0,24},{4,28},{8,16},{12,20},{16,8},{20,12},{24,0},{28,4},{1,25},{... | collective-permute-start | bytes 393224 | tf_op jit(solution)/shard_map/ppermute | solution.py:351
  192.1 24.3 %copy-start.5 = (bf16[4,4,64,256]{3,2,1,0:T(8,128)(2,1)S(1)}, bf16[4,4,64,256]{3,2,1,0:T(8,128)(2,1)}, u32[]{:S(2)}) copy-start(bf16[4,4,64,256]{3,2,1,0:T(8,128)(2,1)} %copy-done.4) | copy-start | bytes 1572868
  192.1 42.0 %collective-permute-start.32 = (bf16[4,64,256]{2,1,0:T(8,128)(2,1)S(1)}, bf16[4,64,256]{2,1,0:T(8,128)(2,1)S(1)}, u32[]{:S(2)}, u32[]{:S(2)}) collective-permute-start(bf16[4,64,256]{2,1,0:T(8,128)(2,1)S(1)} %get-tuple-element.187), channel_id=1, source_target_pairs={{0,8},{4,12},{8,0},{12,4},{16,24},{20,28},{24,16},{28,20},{1,9},{5... | collective-permute-start | bytes 393224 | tf_op jit(solution)/shard_map/ppermute | solution.py:351
  192.2 41.9 %collective-permute-start.33 = (bf16[4,64,256]{2,1,0:T(8,128)(2,1)S(1)}, bf16[4,64,256]{2,1,0:T(8,128)(2,1)S(1)}, u32[]{:S(2)}, u32[]{:S(2)}) collective-permute-start(bf16[4,64,256]{2,1,0:T(8,128)(2,1)S(1)} %get-tuple-element.188), channel_id=1, source_target_pairs={{0,16},{4,20},{8,24},{12,28},{16,0},{20,4},{24,8},{28,12},{1,17},{... | collective-permute-start | bytes 393224 | tf_op jit(solution)/shard_map/ppermute | solution.py:351
  192.7 41.4 %collective-permute-start.34 = (bf16[4,64,256]{2,1,0:T(8,128)(2,1)S(1)}, bf16[4,64,256]{2,1,0:T(8,128)(2,1)S(1)}, u32[]{:S(2)}, u32[]{:S(2)}) collective-permute-start(bf16[4,64,256]{2,1,0:T(8,128)(2,1)S(1)} %get-tuple-element.189), channel_id=1, source_target_pairs={{0,24},{4,28},{8,16},{12,20},{16,8},{20,12},{24,0},{28,4},{1,25},{... | collective-permute-start | bytes 393224 | tf_op jit(solution)/shard_map/ppermute | solution.py:351
  239.0 17.3 %collective-permute-start.41 = (bf16[512,3584]{1,0:T(8,128)(2,1)}, bf16[512,3584]{1,0:T(8,128)(2,1)}, u32[]{:S(2)}, u32[]{:S(2)}) collective-permute-start(bf16[512,3584]{1,0:T(8,128)(2,1)} %shard_map.85), channel_id=1, source_target_pairs={{0,4},{4,0},{8,12},{12,8},{16,20},{20,16},{24,28},{28,24},{1,5},{5... | collective-permute-start | bytes 11010056 | tf_op jit(solution)/shard_map/ppermute | solution.py:351
  239.1 9.0 %collective-permute-start.37 = (bf16[4,64,256]{2,1,0:T(8,128)(2,1)}, bf16[4,64,256]{2,1,0:T(8,128)(2,1)}, u32[]{:S(2)}, u32[]{:S(2)}) collective-permute-start(bf16[4,64,256]{2,1,0:T(8,128)(2,1)} %copy-done.35), channel_id=1, source_target_pairs={{0,8},{4,12},{8,0},{12,4},{16,24},{20,28},{24,16},{28,20},{1,9},{5... | collective-permute-start | bytes 393224 | tf_op jit(solution)/shard_map/ppermute | solution.py:351
  239.3 9.0 %collective-permute-start.38 = (bf16[4,64,256]{2,1,0:T(8,128)(2,1)}, bf16[4,64,256]{2,1,0:T(8,128)(2,1)}, u32[]{:S(2)}, u32[]{:S(2)}) collective-permute-start(bf16[4,64,256]{2,1,0:T(8,128)(2,1)} %copy-done.34), channel_id=1, source_target_pairs={{0,16},{4,20},{8,24},{12,28},{16,0},{20,4},{24,8},{28,12},{1,17},{... | collective-permute-start | bytes 393224 | tf_op jit(solution)/shard_map/ppermute | solution.py:351
  239.8 8.5 %collective-permute-start.39 = (bf16[4,64,256]{2,1,0:T(8,128)(2,1)}, bf16[4,64,256]{2,1,0:T(8,128)(2,1)}, u32[]{:S(2)}, u32[]{:S(2)}) collective-permute-start(bf16[4,64,256]{2,1,0:T(8,128)(2,1)} %copy-done.33), channel_id=1, source_target_pairs={{0,24},{4,28},{8,16},{12,20},{16,8},{20,12},{24,0},{28,4},{1,25},{... | collective-permute-start | bytes 393224 | tf_op jit(solution)/shard_map/ppermute | solution.py:351
  243.4 10.6 %collective-permute-start.35 = (f32[4,128]{1,0:T(4,128)S(1)}, f32[4,128]{1,0:T(4,128)S(1)}, u32[]{:S(2)}, u32[]{:S(2)}) collective-permute-start(f32[4,128]{1,0:T(4,128)S(1)} %get-tuple-element.214), channel_id=1, source_target_pairs={{0,3},{1,0},{2,1},{3,2},{4,7},{5,4},{6,5},{7,6},{8,11},{9,8},{10,9... | collective-permute-start | bytes 6152 | tf_op jit(solution)/shard_map/ppermute | solution.py:354
  248.1 5.8 %collective-permute-start.36 = (f32[4,128]{1,0:T(4,128)S(1)}, f32[4,128]{1,0:T(4,128)S(1)}, u32[]{:S(2)}, u32[]{:S(2)}) collective-permute-start(f32[4,128]{1,0:T(4,128)S(1)} %get-tuple-element.220), channel_id=1, source_target_pairs={{0,2},{1,3},{2,0},{3,1},{4,6},{5,7},{6,4},{7,5},{8,10},{9,11},{10,... | collective-permute-start | bytes 6152 | tf_op jit(solution)/shard_map/ppermute | solution.py:354
  250.1 5.4 %collective-permute-start.40 = (f32[4,128]{1,0:T(4,128)S(1)}, f32[4,128]{1,0:T(4,128)S(1)}, u32[]{:S(2)}, u32[]{:S(2)}) collective-permute-start(f32[4,128]{1,0:T(4,128)S(1)} %get-tuple-element.226), channel_id=1, source_target_pairs={{0,1},{1,2},{2,3},{3,0},{4,5},{5,6},{6,7},{7,4},{8,9},{9,10},{10,1... | collective-permute-start | bytes 6152 | tf_op jit(solution)/shard_map/ppermute | solution.py:354
  (47 other events, 262.2 us)

commit v6 on v5

v6 whole, which is shorter than its diff:
```python
import functools
import jax
import jax.numpy as jnp
from jax import lax
from jax.experimental import pallas as pl
from jax.experimental.pallas import tpu as pltpu
from jax.sharding import PartitionSpec as P

ROUTE_SCALE = 2.5


def pack_routes(grad_rows, route_ids, route_weight, expert_count, most):
    expert_ids = jnp.arange(expert_count, dtype=jnp.int32)
    naming = jnp.sum((route_ids[:, :, None] == expert_ids[None, None, :]).astype(jnp.int32), axis=1)
    before = jnp.cumsum(naming, axis=0) - naming
    slot_ids = jnp.take_along_axis(before, route_ids, axis=1)
    placed = (route_ids * most + slot_ids).reshape(-1)
    token_ids = jnp.repeat(jnp.arange(grad_rows.shape[0], dtype=jnp.int32), route_ids.shape[1])
    source = jnp.zeros((expert_count * most,), jnp.int32).at[placed].set(token_ids)
    filled = jnp.zeros((expert_count * most,), jnp.int32).at[placed].set(1)
    weights = (
        jnp.zeros((expert_count * most,), route_weight.dtype)
        .at[placed]
        .set(route_weight.reshape(-1))
    )
    fetched = jnp.take(grad_rows, source, axis=0)
    packed = jnp.where(filled[:, None] > 0, fetched, jnp.zeros_like(fetched))
    return (packed, weights, placed)


def on_device_weights(grad_out, routes, affinity, saved_hidden, down_proj):
    exp_devices = lax.axis_size("exp")
    local_experts = down_proj.shape[1]
    expert_count = exp_devices * local_experts
    most = saved_hidden.shape[3]
    width = grad_out.shape[1]
    hidden_units = saved_hidden.shape[4]
    row_count = exp_devices * most
    totals = jnp.sum(affinity, axis=-1, keepdims=True)
    shares = affinity / totals
    route_weight = (ROUTE_SCALE * shares).astype(jnp.bfloat16)
    packed, weights, placed = pack_routes(grad_out, routes, route_weight, expert_count, most)
    outgoing = packed.reshape(exp_devices, local_experts, 1, most, width)
    outgoing_weight = weights.reshape(exp_devices, local_experts, 1, most)
    received, received_weight = (
        lax.all_to_all(outgoing, "exp", split_axis=0, concat_axis=2, tiled=True),
        lax.all_to_all(outgoing_weight, "exp", split_axis=0, concat_axis=2, tiled=True),
    )
    received = received.reshape(local_experts, row_count, width)
    row_scale = received_weight.reshape(local_experts, row_count).astype(jnp.float32)
    hidden = saved_hidden.reshape(local_experts, row_count, hidden_units)
    gathered = lax.all_gather(down_proj, "rep", axis=0, tiled=True)
    projected = jnp.einsum("erd,hed->erh", received, gathered, preferred_element_type=jnp.float32)
    hidden_grad = (row_scale[:, :, None] * projected).astype(jnp.bfloat16)
    combine_grad = ROUTE_SCALE * jnp.sum(hidden.astype(jnp.float32) * projected, axis=-1)
    scaled = (row_scale[:, :, None] * received.astype(jnp.float32)).astype(jnp.bfloat16)
    grad_term = jnp.einsum("erh,erd->hed", hidden, scaled, preferred_element_type=jnp.float32)
    down_grad = lax.psum_scatter(
        grad_term.astype(jnp.bfloat16), "rep", scatter_dimension=0, tiled=True
    ).astype(jnp.float32)
    returned = lax.all_to_all(
        combine_grad.reshape(local_experts, exp_devices, most),
        "exp",
        split_axis=1,
        concat_axis=0,
        tiled=True,
    )
    route_grad = jnp.take(returned.reshape(-1), placed).reshape(routes.shape)
    affinity_grad = (route_grad - jnp.sum(route_grad * shares, axis=-1, keepdims=True)) / totals
    return (affinity_grad, hidden_grad.reshape(saved_hidden.shape), down_grad)


SLOT_PAD = 64
F32 = jnp.float32
BF16 = jnp.bfloat16
VMEM_BYTES = 32 * 2**20


def nt_dot(a, b):
    return lax.dot_general(a, b, (((1,), (1,)), ((), ())), preferred_element_type=F32)


def tn_dot(a, b):
    return lax.dot_general(a, b, (((0,), (0,)), ((), ())), preferred_element_type=F32)


def project_kernel(top_k, sizes, items, idx_ref, *refs):
    parts = len(sizes)
    pieces, (own_weight, partner_weight) = refs[:parts], refs[parts : parts + 2]
    hidden_refs = refs[parts + 2 : parts + 2 + items]
    grad_refs = refs[parts + 2 + items : parts + 2 + 2 * items]
    scatter_ref, rows, weight, terms, slot_ref, scale_ref, sems = refs[parts + 2 + 2 * items :]
    step = pl.program_id(0)
    group, slots, pair = grad_refs[0].shape
    block = pair // 2
    tokens = rows.shape[0] // items
    experts = slot_ref.shape[0]
    core = idx_ref[5]

    @pl.when(step == 0)
    def _():
        copies, at = [], 0
        for i, size in enumerate(sizes):
            copies.append(pltpu.make_async_copy(pieces[i], rows.at[at : at + size], sems.at[i]))
            at += size
        for copy in copies:
            copy.start()
        metas = [hidden_refs[i][0, 0][slots - 8 :].astype(F32)[8 - top_k :] for i in range(items)]
        fill = jnp.full((8 - items, tokens), -1.0, F32)
        routes = [jnp.concatenate([m[k : k + 1, :tokens] for m in metas] + [fill], axis=0) for k in range(top_k)]
        weights = [jnp.concatenate([m[k : k + 1, tokens:] for m in metas] + [fill], axis=0) for k in range(top_k)]
        earlier = (
            lax.broadcasted_iota(jnp.int32, (tokens, tokens), 0)
            < lax.broadcasted_iota(jnp.int32, (tokens, tokens), 1)
        ).astype(BF16)
        every = []
        for e in range(experts):
            expert = (idx_ref[4] + e).astype(F32)
            named = jnp.zeros((8, tokens), F32)
            scale = jnp.zeros((8, tokens), F32)
            for k in range(top_k):
                hit = routes[k] == expert
                named = jnp.where(hit, 1.0, named)
                scale = jnp.where(hit, weights[k], scale)
            scale_ref[e] = scale
            every.append(named)
        named = jnp.concatenate(every, axis=0)
        before = jnp.dot(named.astype(BF16), earlier, preferred_element_type=F32)
        slot = jnp.where(named > 0, before, -1.0)
        for e in range(experts):
            slot_ref[e] = slot[e * 8 : (e + 1) * 8]
        for copy in copies:
            copy.wait()

    for q in range(group):
        to = pl.multiple_of(q * pair + core * block, block)
        weight[pl.ds(to, block), :] = own_weight[q * block : (q + 1) * block]
        to = pl.multiple_of(q * pair + (1 - core) * block, block)
        weight[pl.ds(to, block), :] = partner_weight[q * block : (q + 1) * block]
    projected = nt_dot(weight[...], rows[...])
    slot_ids = lax.broadcasted_iota(jnp.int32, (slots, tokens), 0).astype(F32)
    slot_rows = lax.broadcasted_iota(jnp.int32, (slots, pair), 0)
    for q in range(group):
        e = step * group + q
        slot_all, scale_all = slot_ref[e], scale_ref[e]
        for i in range(items):
            scale = scale_all[i : i + 1]
            pick = (slot_all[i : i + 1] == slot_ids).astype(BF16)
            own = projected[q * pair : (q + 1) * pair, i * tokens : (i + 1) * tokens]
            hidden = tn_dot(hidden_refs[i][q, 0], pick)
            grad = nt_dot(pick, (scale * own).astype(BF16))
            combine = jnp.sum(hidden * own, axis=0, keepdims=True)
            high = combine.astype(BF16).astype(F32)
            partial = jnp.concatenate([high, combine - high], axis=1)
            grad_refs[i][q] = jnp.where(slot_rows == slots - top_k, partial, grad).astype(BF16)
            scatter = (scale * hidden).astype(BF16)
            for half in range(2):
                at = pl.ds(pl.multiple_of(e * block, block), block)
                terms[half, at, i * tokens : (i + 1) * tokens] = scatter[half * block : (half + 1) * block]

    @pl.when(step == pl.num_programs(0) - 1)
    def _():
        height = terms.shape[1]
        row = lax.broadcasted_iota(jnp.int32, (height, height), 0)
        col = lax.broadcasted_iota(jnp.int32, (height, height), 1)
        order = (col == lax.rem(row, experts) * block + lax.div(row, experts)).astype(BF16)
        for half in range(2):
            scatter_ref[half] = jnp.dot(order, terms[half], preferred_element_type=F32).astype(BF16)


def project(index, items, own_weight, partner_weight, hidden, top_k, group=2):
    experts, sources, slots, pair = hidden[0].shape
    width = own_weight.shape[1]
    pieces = [piece for rows, _, _ in items for piece in rows]
    sizes = [p.shape[0] for p in pieces]
    count = sum(sizes)
    block = pair // 2
    return pl.pallas_call(
        functools.partial(project_kernel, top_k, sizes, len(items)),
        grid_spec=pltpu.PrefetchScalarGridSpec(
            num_scalar_prefetch=1,
            grid=(experts // group,),
            in_specs=[pl.BlockSpec(memory_space=pl.ANY)] * len(sizes)
            + [pl.BlockSpec((group * block, width), lambda e, idx: (e, 0))] * 2
            + [
                pl.BlockSpec((group, 1, slots, pair), lambda e, idx, k=k: (e, idx[k], 0, 0))
                for _, _, k in items
            ],
            out_specs=[pl.BlockSpec((group, slots, pair), lambda e, idx: (e, 0, 0))] * len(items)
            + [pl.BlockSpec((2, experts * block, count), lambda e, idx: (0, 0, 0))],
            scratch_shapes=[
                pltpu.VMEM((count, width), BF16),
                pltpu.VMEM((group * pair, width), BF16),
                pltpu.VMEM((2, experts * block, count), BF16),
                pltpu.VMEM((experts, 8, block), F32),
                pltpu.VMEM((experts, 8, block), F32),
                pltpu.SemaphoreType.DMA((len(sizes),)),
            ],
        ),
        out_shape=[jax.ShapeDtypeStruct((experts, slots, pair), BF16)] * len(items)
        + [jax.ShapeDtypeStruct((2, experts * block, count), BF16)],
        compiler_params=pltpu.CompilerParams(vmem_limit_bytes=VMEM_BYTES),
        cost_estimate=pl.CostEstimate(
            flops=4 * count * width * experts * pair,
            bytes_accessed=2 * (count * width + 2 * own_weight.size),
            transcendentals=0,
        ),
    )(index, *pieces, own_weight, partner_weight, *[hidden[m] for _, m, _ in items])


def fill_rows(pieces, rows):
    at = 0
    for piece in pieces:
        size = piece.shape[0]
        rows[at : at + size, :] = piece[...]
        at += size


def sum_terms(scatters, rows, half):
    total, at = None, 0
    for scatter in scatters:
        count = scatter.shape[2]
        term = jnp.dot(scatter[half], rows[at : at + count, :], preferred_element_type=F32)
        total = term if total is None else total + term
        at += count
    return total


def early_grad_kernel(terms, *refs):
    scatters, pieces, out_ref, rows = refs[:terms], refs[terms:-2], refs[-2], refs[-1]
    fill_rows(pieces, rows)
    for half in range(2):
        out_ref[half] = sum_terms(scatters, rows, half)


def early_grad(scatters, pieces, tile):
    height = scatters[0].shape[1]
    width = pieces[0].shape[1]
    count = sum(p.shape[0] for p in pieces)
    return pl.pallas_call(
        functools.partial(early_grad_kernel, len(scatters)),
        grid=(width // tile,),
        in_specs=[pl.BlockSpec(a.shape, lambda i: (0, 0, 0)) for a in scatters]
        + [pl.BlockSpec((p.shape[0], tile), lambda i: (0, i)) for p in pieces],
        out_specs=pl.BlockSpec((2, height, tile), lambda i: (0, 0, i)),
        out_shape=jax.ShapeDtypeStruct((2, height, width), F32),
        scratch_shapes=[pltpu.VMEM((count, tile), BF16)],
        compiler_params=pltpu.CompilerParams(vmem_limit_bytes=VMEM_BYTES),
        cost_estimate=pl.CostEstimate(
            flops=4 * height * count * width,
            bytes_accessed=2 * count * (width + 2 * height) + 8 * height * width,
            transcendentals=0,
        ),
    )(*scatters, *pieces)


def late_grad_kernel(terms, last, idx_ref, *refs):
    scatters, before_ref = refs[:terms], refs[terms]
    if not last:
        pieces, out_ref, rows = refs[terms + 1 : -2], refs[-2], refs[-1]
    else:
        arrived_ref, pieces, out_ref, rows, held = refs[terms + 1], refs[terms + 2 : -3], *refs[-3:]
    fill_rows(pieces, rows)
    total = before_ref[0] + sum_terms(scatters, rows, 0)
    if not last:
        out_ref[...] = total.astype(BF16)
        return
    held[...] = total + arrived_ref[...].astype(F32)
    block, experts, _ = out_ref.shape
    group = 8 // experts

    def move(i, carry):
        both = held[pl.ds(pl.multiple_of(i * 8, 8), 8), :]
        for j in range(group):
            out_ref[i * group + j] = both[j * experts : (j + 1) * experts]
        return carry

    lax.fori_loop(0, block // group, move, 0, unroll=4)


def late_grad(index, scatters, pieces, before, arrived, experts, tile):
    height = scatters[0].shape[1]
    width = pieces[0].shape[1]
    count = sum(p.shape[0] for p in pieces)
    in_specs = [pl.BlockSpec((1,) + a.shape[1:], lambda i, idx: (idx[0], 0, 0)) for a in scatters]
    in_specs.append(pl.BlockSpec((1, height, tile), lambda i, idx: (idx[0], 0, i)))
    args = [*scatters, before]
    scratch = [pltpu.VMEM((count, tile), BF16)]
    last = arrived is not None
    if last:
        in_specs.append(pl.BlockSpec((height, tile), lambda i, idx: (0, i)))
        args.append(arrived)
        scratch.append(pltpu.VMEM((height, tile), F32))
        out_spec = pl.BlockSpec((height // experts, experts, tile), lambda i, idx: (0, 0, i))
        out_shape = jax.ShapeDtypeStruct((height // experts, experts, width), F32)
    else:
        out_spec = pl.BlockSpec((height, tile), lambda i, idx: (0, i))
        out_shape = jax.ShapeDtypeStruct((height, width), BF16)
    in_specs += [pl.BlockSpec((p.shape[0], tile), lambda i, idx: (0, i)) for p in pieces]
    return pl.pallas_call(
        functools.partial(late_grad_kernel, len(scatters), last),
        grid_spec=pltpu.PrefetchScalarGridSpec(
            num_scalar_prefetch=1,
            grid=(width // tile,),
            in_specs=in_specs,
            out_specs=out_spec,
            scratch_shapes=scratch,
        ),
        out_shape=out_shape,
        compiler_params=pltpu.CompilerParams(vmem_limit_bytes=VMEM_BYTES),
        cost_estimate=pl.CostEstimate(
            flops=2 * height * count * width,
            bytes_accessed=2 * count * (width + height) + 8 * height * width,
            transcendentals=0,
        ),
    )(index, *args, *pieces)


def place_kernel(top_k, first, idx_ref, *refs):
    pieces = refs[:4]
    out_ref, sum_ref = refs[-2:]
    experts, slots, pair = pieces[0].shape
    m = pl.program_id(0)

    @pl.when(m == 0)
    def _():
        sum_ref[...] = jnp.zeros_like(sum_ref)

    for i in range(4):

        @pl.when(m == i)
        def _():
            out_ref[0] = pieces[i][...]
            for e in range(experts):
                row = pieces[i][e, slots - 8 :].astype(F32)[8 - top_k : 9 - top_k]
                sum_ref[e : e + 1] += row[:, : pair // 2] + row[:, pair // 2 :]


def place(index, pieces, before, sources, top_k):
    experts, slots, pair = pieces[0].shape
    first = before is None
    shape = (sources, experts, slots, 4 * pair)
    return pl.pallas_call(
        functools.partial(place_kernel, top_k, first),
        grid_spec=pltpu.PrefetchScalarGridSpec(
            num_scalar_prefetch=1,
            grid=(4,),
            in_specs=[pl.BlockSpec((experts, slots, pair), lambda m, idx: (0, 0, 0))] * 4
            + ([] if first else [pl.BlockSpec(memory_space=pl.ANY)]),
            out_specs=[
                pl.BlockSpec((1, experts, slots, pair), lambda m, idx: (idx[0], 0, 0, idx[1 + m])),
                pl.BlockSpec((experts, pair // 2), lambda m, idx: (0, 0)),
            ],
        ),
        out_shape=[
            jax.ShapeDtypeStruct(shape, BF16),
            jax.ShapeDtypeStruct((experts, pair // 2), F32),
        ],
        input_output_aliases={} if first else {5: 0},
        compiler_params=pltpu.CompilerParams(vmem_limit_bytes=VMEM_BYTES),
        cost_estimate=pl.CostEstimate(
            flops=0, bytes_accessed=16 * experts * slots * pair, transcendentals=0
        ),
    )(index, *pieces, *([] if first else [before]))


def on_device_tokens(grad_out, routes, affinity, saved_hidden, down_proj):
    reps, sources = lax.axis_size("rep"), lax.axis_size("exp")
    block, experts, width = down_proj.shape
    tokens, top_k = routes.shape
    most, hidden_units = saved_hidden.shape[3:]
    pair = 2 * block
    me = lax.axis_index("exp")
    rep = lax.axis_index("rep")
    chip, core = lax.div(rep, 2), lax.rem(rep, 2)
    chips = [jnp.bitwise_xor(chip, m) for m in range(4)]

    def across(array, bits):
        return lax.ppermute(array, "rep", [(i, i ^ bits) for i in range(reps)])

    def around(array, shift):
        return lax.ppermute(array, "exp", [(i, (i + shift) % sources) for i in range(sources)])

    totals = jnp.sum(affinity, axis=-1, keepdims=True)
    shares = affinity / totals
    route_weight = (ROUTE_SCALE * shares).astype(BF16)
    meta = jnp.concatenate([routes.astype(BF16).T, route_weight.T], axis=1)
    fence = lax.optimization_barrier
    half = tokens // 2

    slabs = [lax.rem(me - step + sources, sources) for step in range(sources)]
    index = jnp.stack(slabs + [me * experts, core]).astype(jnp.int32)

    def kernel(items):
        *grads, scatter = project(index, items, own_weight, partner_weight, hidden, top_k)
        return grads, scatter

    def send_back(grads, chip_of):
        return [across(g, 2 * m) if m else g for g, m in zip(grads, chip_of)]

    def put(step, returned, placed):
        spots = jnp.stack([slabs[step]] + chips).astype(jnp.int32)
        return place(spots, returned, placed, sources, top_k)

    x0, y0, next1 = across(grad_out, 2), across(grad_out, 4), around(grad_out, 1)
    metas = [meta, around(meta, 1), around(meta, 2), around(fence((meta, x0))[0], 3)]
    held = jnp.transpose(saved_hidden.reshape(experts, sources, most, 4, pair), (3, 0, 1, 2, 4))
    held = fence(held)
    held = [lax.dynamic_index_in_dim(held, chips[m], axis=0, keepdims=False) for m in range(4)]
    own_weight = jnp.transpose(down_proj, (1, 0, 2)).reshape(experts * block, width)
    metas, x0, y0, next1, held, own_weight = fence((metas, x0, y0, next1, held, own_weight))

    metas = jnp.take(jnp.stack(metas), lax.rem(me - jnp.arange(sources) + sources, sources), axis=0)
    blank = jnp.zeros((experts, sources, SLOT_PAD - most - top_k, pair), BF16)
    metas = jnp.broadcast_to(metas[None], (experts, sources, top_k, pair))
    hidden = []
    for m in range(4):
        piece = jnp.concatenate([held[m], blank, metas], axis=2)
        hidden.append(across(piece, 2 * m) if m else piece)
    top0, bottom0 = across(x0[:half], 4), across(y0[half:], 2)
    next2 = around(next1, 1)
    partner_weight = across(own_weight, 1)
    hidden, top0, bottom0, next2, partner_weight, x0, y0, next1 = fence(
        (hidden, top0, bottom0, next2, partner_weight, x0, y0, next1)
    )

    x1, y1, x3 = across(next1, 2), across(next1, 4), around(x0, -1)
    grads0, scatter0 = kernel([([grad_out], 0, 0), ([x0], 1, 0), ([y0], 2, 0), ([top0, bottom0], 3, 0)])
    x1, y1, x3, grads0, scatter0, y0, top0, bottom0, next2 = fence(
        (x1, y1, x3, grads0, scatter0, y0, top0, bottom0, next2)
    )

    top1, bottom1 = across(x1[:half], 4), across(y1[half:], 2)
    x2, y2, y3, own3 = across(next2, 2), across(next2, 4), around(y0, -1), around(grad_out, -1)
    returned0 = send_back(grads0, (0, 1, 2, 3))
    grads1, scatter1 = kernel([([next1], 0, 1), ([x1], 1, 1), ([y1], 2, 1), ([next2], 0, 2), ([x3], 1, 3)])
    top1, bottom1, x2, y2, y3, own3, returned0, top0, bottom0, grads1, scatter1 = fence(
        (top1, bottom1, x2, y2, y3, own3, returned0, top0, bottom0, grads1, scatter1)
    )

    top2, bottom2 = across(x2[:half], 4), across(y2[half:], 2)
    top3, bottom3 = around(top0, -1), around(bottom0, -1)
    returned1 = send_back(grads1, (0, 1, 2, 0, 1))
    grads2, scatter2 = kernel(
        [([x2], 1, 2), ([y2], 2, 2), ([y3], 2, 3), ([own3], 0, 3), ([top1, bottom1], 3, 1)]
    )
    before = early_grad(
        [scatter0, scatter1], [grad_out, x0, y0, top0, bottom0, next1, x1, y1, next2, x3], 512
    )
    placed, combine0 = put(0, returned0, None)
    top2, bottom2, top3, bottom3, returned1, grads2, scatter2, before, placed, combine0 = fence(
        (top2, bottom2, top3, bottom3, returned1, grads2, scatter2, before, placed, combine0)
    )

    returned2 = send_back(grads2, (1, 2, 2, 0, 3))
    grads3, scatter3 = kernel([([top2, bottom2], 3, 2), ([top3, bottom3], 3, 3)])
    returned3 = send_back(grads3, (3, 3))
    late = [x2, y2, y3, own3, top1, bottom1, top2, bottom2, top3, bottom3]
    late_scatters = [scatter2, scatter3]
    partner = late_grad((1 - core).reshape(1), late_scatters, late, before, None, experts, 896)
    partner = across(partner, 1)
    placed, combine1 = put(1, [*returned1[:3], returned2[4]], placed)
    placed, combine2 = put(2, [returned1[3], returned2[0], returned2[1], returned3[0]], placed)
    placed, combine3 = put(3, [returned2[3], returned1[4], returned2[2], returned3[1]], placed)
    combines = [combine0, around(combine1, -1), around(combine2, -2), around(combine3, 1)]
    route_grad = 0.0
    expert_ids = jnp.arange(experts, dtype=routes.dtype)
    for step in range(sources):
        ids = lax.rem(me + step, sources) * experts + expert_ids
        named = routes.T[:, None, :] == ids[None, :, None]
        route_grad += jnp.sum(jnp.where(named, combines[step][None], 0.0), axis=1)
    hidden_grad = jnp.transpose(placed[:, :, :most], (1, 0, 2, 3)).reshape(saved_hidden.shape)
    route_grad = ROUTE_SCALE * route_grad.T
    affinity_grad = (route_grad - jnp.sum(route_grad * shares, axis=-1, keepdims=True)) / totals
    down_grad = late_grad(core.reshape(1), late_scatters, late, before, partner, experts, 896)
    return (affinity_grad, hidden_grad, down_grad)


def on_device(grad_out, routes, affinity, saved_hidden, down_proj):
    reps, sources = lax.axis_size("rep"), lax.axis_size("exp")
    block, experts, width = down_proj.shape
    tokens, top_k = routes.shape
    most = saved_hidden.shape[3]
    fits = block == 128 and tokens == 128 and width % 3584 == 0 and reps == 8 and 8 % experts == 0
    fits = fits and sources == 4 and most + top_k <= SLOT_PAD and top_k <= 8
    if fits and sources * tokens <= 2 * block * experts:
        return on_device_tokens(grad_out, routes, affinity, saved_hidden, down_proj)
    return on_device_weights(grad_out, routes, affinity, saved_hidden, down_proj)


def solution(mesh):
    return jax.shard_map(
        on_device,
        mesh=mesh,
        in_specs=(
            P(("rep", "exp"), None),
            P(("rep", "exp"), None),
            P(("rep", "exp"), None),
            P("rep", "exp", None, None, None),
            P("rep", "exp", None),
        ),
        out_specs=(
            P(("rep", "exp"), None),
            P("rep", "exp", None, None, None),
            P("rep", "exp", None),
        ),
        check_vma=False,
    )
```

time: 270 us -> 247 us (0.915)
  local copies, waits for them, and re-layouts: 55.2 us -> 40.1 us
  starting transfers between devices: 61.8 us -> 55.3 us
  waiting for transfers between devices: 60.8 us -> 56.5 us
    unnamed x107 -> x149, local copies, waits for them, and re-layouts: 34.6 us -> 21.2 us
    ppermute x13, waiting for transfers between devices: 25 us -> 16.4 us  [around(): lax.ppermute(array, 'exp', [(i, (i + shift) % sources) for i in range(sou...]
    ppermute x29, starting transfers between devices: 37.3 us -> 32.6 us  [across(): return lax.ppermute(array, 'rep', [(i, i ^ bits) for i in range(reps)])]
    ppermute x29, waiting for transfers between devices: 35.8 us -> 40.1 us  [across(): return lax.ppermute(array, 'rep', [(i, i ^ bits) for i in range(reps)])]
  transfers between devices with their start and end apart: 42 -> 42, of which waited for: 11 -> 10; matrix products, arithmetic and copies ran while one was open for 10% -> 11% of each run, Pallas kernels for 27% -> 24%
where the time goes in v6:
time: 247 us; the launch traced here: 246 us
  Pallas kernels  86.9 us (35%)
  waiting for transfers between devices  56.5 us (23%)
  starting transfers between devices  55.3 us (22%)
  local copies, waits for them, and re-layouts  40.1 us (16%)
  other arithmetic  5.23 us (2%)
    pallas_call x4, Pallas kernels, project(): pl.pallas_call(functools.partial(project_kernel, top_k, sizes, len(items)...  47.6 us
    ppermute x29, waiting for transfers between devices, across(): return lax.ppermute(array, 'rep', [(i, i ^ bits) for i in range(reps)])  40.1 us
    ppermute x29, starting transfers between devices, across(): return lax.ppermute(array, 'rep', [(i, i ^ bits) for i in range(reps)])  32.6 us
    ppermute x13, starting transfers between devices, around(): lax.ppermute(array, 'exp', [(i, (i + shift) % sources) for i in range(sou...  22.8 us
    unnamed x149, local copies, waits for them, and re-layouts  21.2 us
    pallas_call x2, Pallas kernels, late_grad(): pl.pallas_call(functools.partial(late_grad_kernel, len(scatters), last),...  18.7 us
    ppermute x13, waiting for transfers between devices, around(): lax.ppermute(array, 'exp', [(i, (i + shift) % sources) for i in range(sou...  16.4 us
    pallas_call x1, Pallas kernels, early_grad(): pl.pallas_call(functools.partial(early_grad_kernel, len(scatters)), grid=...  14.6 us
  transfers between devices with their start and end apart: 42, of which 10 were waited for; matrix products, arithmetic and copies ran while one was open for 11% of the time, Pallas kernels for 24%

profile of v6, /device:TPU:0, one launch (start us, length us, event | category | flops | bytes accessed | tf_op | source)
XLA Modules:
  0.0 245.5 jit_solution(4788736271061304494)
XLA Ops:
  0.6 3.0 %collective-permute-start.2 = (bf16[128,3584]{1,0:T(8,128)(2,1)}, bf16[128,3584]{1,0:T(8,128)(2,1)S(1)}, u32[]{:S(2)}, u32[]{:S(2)}) collective-permute-start(bf16[128,3584]{1,0:T(8,128)(2,1)} %refs_2_.1), channel_id=1, source_target_pairs={{0,8},{4,12},{8,0},{12,4},{16,24},{20,28},{24,16},{28,20},{1,9},{5... | collective-permute-start | bytes 2752520 | tf_op jit(solution)/shard_map/ppermute | solution.py:379
  3.6 1.5 collective-permute-start.4
  5.2 1.6 collective-permute-start.5
  8.8 1.6 collective-permute-start
  11.7 4.8 %reshape.87 = bf16[4,4,60,4,256]{4,3,1,2,0:T(4,128)(2,1)} reshape(bf16[1,4,4,60,1024]{4,2,3,1,0:T(4,128)(2,1)} %param.8) | data formatting | bytes 3932160 | tf_op jit(solution)/shard_map/reshape | solution.py:407
  16.5 3.6 %copy.18 = bf16[4,4,60,4,256]{4,2,1,0,3:T(8,128)(2,1)} copy(bf16[4,4,60,4,256]{4,3,1,2,0:T(4,128)(2,1)} %reshape.87) | data formatting | bytes 3932160 | tf_op jit(solution)/shard_map/reshape | solution.py:407
  20.0 4.2 %collective-permute-done.2.refs_1_.refs_3_ = bf16[128,3584]{1,0:T(8,128)(2,1)S(1)} collective-permute-done((bf16[128,3584]{1,0:T(8,128)(2,1)}, bf16[128,3584]{1,0:T(8,128)(2,1)S(1)}, u32[]{:S(2)}, u32[]{:S(2)}) %collective-permute-start.2) | collective-permute-done | bytes 917536 | tf_op jit(solution)/shard_map/ppermute | solution.py:379
  24.2 3.8 %collective-permute-start.3 = (bf16[4,256]{1,0:T(4,128)(2,1)S(1)}, bf16[4,256]{1,0:T(4,128)(2,1)S(1)}, u32[]{:S(2)}, u32[]{:S(2)}) collective-permute-start(bf16[4,256]{1,0:T(4,128)(2,1)S(1)} %pad_maximum_fusion.5), channel_id=1, source_target_pairs={{0,3},{1,0},{2,1},{3,2},{4,7},{5,4},{6,5},{7,6},{8,11},{9,8},{10,9... | collective-permute-start | bytes 6152 | tf_op jit(solution)/shard_map/ppermute | solution.py:382
  28.0 2.9 %dynamic-slice_bitcast_fusion = (bf16[4,4,60,256]{3,2,1,0:T(8,128)(2,1)}, bf16[4,4,60,256]{3,2,1,0:T(8,128)(2,1)}, bf16[4,4,60,256]{3,2,1,0:T(8,128)(2,1)}, bf16[4,4,60,256]{3,2,1,0:T(8,128)(2,1)}) fusion(bf16[4,4,4,60,256]{4,3,2,1,0:T(8,128)(2,1)} %bitcast.48, s32[]{:T(128)S(6)} %select_n.53, s32[]{:T(128)S(6)} %select_n.52, s32[]{:T(128)S(6)} %select_n.51, ...), kind=kLoop, calls=%fused_computation.7 | loop fusion | bytes 3932176 | tf_op jit(solution)/shard_map/jit(dynamic_index_in_dim)/squeeze | solution.py:409
  30.9 2.4 copy.15
  34.5 1.5 collective-permute-start.10
  36.8 1.5 collective-permute-start.9
  39.0 1.7 pad_maximum_fusion
  41.3 6.7 %collective-permute-done.10.refs_4_.refs_6_ = bf16[64,3584]{1,0:T(8,128)(2,1)S(1)} collective-permute-done((bf16[64,3584]{1,0:T(8,128)(2,1)}, bf16[64,3584]{1,0:T(8,128)(2,1)S(1)}, u32[]{:S(2)}, u32[]{:S(2)}) %collective-permute-start.10) | collective-permute-done | bytes 458784 | tf_op jit(solution)/shard_map/ppermute | solution.py:379
  48.8 1.5 collective-permute-start.7
  51.1 1.4 collective-permute-start.8
  52.5 6.7 %collective-permute-done.6.refs_8_.refs_11_ = bf16[4,4,64,256]{3,2,1,0:T(8,128)(2,1)S(1)} collective-permute-done((bf16[4,4,64,256]{3,2,1,0:T(8,128)(2,1)S(1)}, bf16[4,4,64,256]{3,2,1,0:T(8,128)(2,1)S(1)}, u32[]{:S(2)}, u32[]{:S(2)}) %collective-permute-start.6) | collective-permute-done | bytes 524320 | tf_op jit(solution)/shard_map/ppermute | solution.py:379
  60.1 12.9 %collective-permute-done.7.refs_9_.refs_10_ = bf16[4,4,64,256]{3,2,1,0:T(8,128)(2,1)S(1)} collective-permute-done((bf16[4,4,64,256]{3,2,1,0:T(8,128)(2,1)S(1)}, bf16[4,4,64,256]{3,2,1,0:T(8,128)(2,1)S(1)}, u32[]{:S(2)}, u32[]{:S(2)}) %collective-permute-start.7) | collective-permute-done | bytes 524320 | tf_op jit(solution)/shard_map/ppermute | solution.py:379
  74.6 1.5 collective-permute-start.13
  76.1 1.5 collective-permute-start.14
  77.6 1.6 collective-permute-start.15
  84.5 10.7 %shard_map.76 = (bf16[4,64,256]{2,1,0:T(8,128)(2,1)S(1)}, bf16[4,64,256]{2,1,0:T(8,128)(2,1)S(1)}, bf16[4,64,256]{2,1,0:T(8,128)(2,1)}, bf16[4,64,256]{2,1,0:T(8,128)(2,1)}, bf16[2,512,512]{2,1,0:T(8,128)(2,1)S(1)}) custom-call(s32[6]{0:T(128)S(1)} %stack.87.idx_ref, bf16[128,3584]{1,0:T(8,128)(2,1)} %refs_2_.1, ...), custom_call_target="tpu_custom_call" | custom-call | flops 7516192768 | bytes 11010048 | tf_op jit(solution)/shard_map/pallas_call | solution.py:178
  96.8 4.1 %collective-permute-done.15.refs_4_.refs_11_ = bf16[128,3584]{1,0:T(8,128)(2,1)} collective-permute-done((bf16[128,3584]{1,0:T(8,128)(2,1)S(1)}, bf16[128,3584]{1,0:T(8,128)(2,1)}, u32[]{:S(2)}, u32[]{:S(2)}) %collective-permute-start.15) | collective-permute-done | bytes 917536 | tf_op jit(solution)/shard_map/ppermute | solution.py:382
  102.0 2.4 collective-permute-start.24
  105.0 12.2 %collective-permute-done.21.refs_3_.refs_6_.refs_7_ = bf16[128,3584]{1,0:T(8,128)(2,1)S(1)} collective-permute-done((bf16[128,3584]{1,0:T(8,128)(2,1)}, bf16[128,3584]{1,0:T(8,128)(2,1)S(1)}, u32[]{:S(2)}, u32[]{:S(2)}) %collective-permute-start.21) | collective-permute-done | bytes 917536 | tf_op jit(solution)/shard_map/ppermute | solution.py:382
  118.4 4.2 %collective-permute-start.20 = (bf16[128,3584]{1,0:T(8,128)(2,1)}, bf16[128,3584]{1,0:T(8,128)(2,1)}, u32[]{:S(2)}, u32[]{:S(2)}) collective-permute-start(bf16[128,3584]{1,0:T(8,128)(2,1)} %copy-done.22), channel_id=1, source_target_pairs={{0,3},{1,0},{2,1},{3,2},{4,7},{5,4},{6,5},{7,6},{8,11},{9,8},{10,9... | collective-permute-start | bytes 2752520 | tf_op jit(solution)/shard_map/ppermute | solution.py:382
  124.9 1.6 collective-permute-start.16
  126.5 1.4 collective-permute-start.17
  130.0 13.9 %shard_map.77 = (bf16[4,64,256]{2,1,0:T(8,128)(2,1)S(1)}, bf16[4,64,256]{2,1,0:T(8,128)(2,1)S(1)}, bf16[4,64,256]{2,1,0:T(8,128)(2,1)S(1)}, bf16[4,64,256]{2,1,0...) custom-call(s32[6]{0:T(128)S(1)} %stack.87.idx_ref, ...), custom_call_target="tpu_custom_call" | custom-call | flops 9395240960 | bytes 11927552 | tf_op jit(solution)/shard_map/pallas_call | solution.py:178
  143.9 3.7 %collective-permute-done.16.refs_4_.refs_7_.refs_8_ = bf16[64,3584]{1,0:T(8,128)(2,1)S(1)} collective-permute-done((bf16[64,3584]{1,0:T(8,128)(2,1)S(1)}, bf16[64,3584]{1,0:T(8,128)(2,1)S(1)}, u32[]{:S(2)}, u32[]{:S(2)}) %collective-permute-start.16) | collective-permute-done | bytes 458784 | tf_op jit(solution)/shard_map/ppermute | solution.py:379
  148.4 1.4 collective-permute-start.26
  149.8 4.2 %collective-permute-start.27 = (bf16[64,3584]{1,0:T(8,128)(2,1)S(1)}, bf16[64,3584]{1,0:T(8,128)(2,1)S(1)}, u32[]{:S(2)}, u32[]{:S(2)}) collective-permute-start(bf16[64,3584]{1,0:T(8,128)(2,1)S(1)} %copy-done.60), channel_id=1, source_target_pairs={{0,3},{1,0},{2,1},{3,2},{4,7},{5,4},{6,5},{7,6},{8,11},{9,8},{10,9... | collective-permute-start | bytes 1376264 | tf_op jit(solution)/shard_map/ppermute | solution.py:382
  154.6 1.5 collective-permute-start.30
  156.2 13.8 %shard_map.78 = (bf16[4,64,256]{2,1,0:T(8,128)(2,1)S(1)}, bf16[4,64,256]{2,1,0:T(8,128)(2,1)S(1)}, bf16[4,64,256]{2,1,0:T(8,128)(2,1)S(1)}, bf16[4,64,256]{2,1,0...) custom-call(s32[6]{0:T(128)S(1)} %stack.87.idx_ref, ...), custom_call_target="tpu_custom_call" | custom-call | flops 9395240960 | bytes 11927552 | tf_op jit(solution)/shard_map/pallas_call | solution.py:178
  172.1 1.4 collective-permute-start.31
  173.6 14.6 %shard_map.79.refs_2_ = f32[2,512,3584]{2,1,0:T(8,128)} custom-call(bf16[2,512,512]{2,1,0:T(8,128)(2,1)S(1)} %copy-done.66, bf16[2,512,640]{2,1,0:T(8,128)(2,1)S(1)} %get-tuple-element.169.refs_1_, bf16[128,3584]{1,0:T(8,128)(2,1)} %refs_2_.1, bf16[128,3584]{1,0:T(8,128)(2,1)S(1)} %copy-done.21, bf16[128,3584]{1,0:T(8,128)(2,1)S(1)} %copy-done.23, ...), custom_call_target="tpu_custom_call" | custom-call | flops 8455716864 | bytes 25296896 | tf_op jit(solution)/shard_map/pallas_call | solution.py:240
  189.1 9.1 %shard_map.82 = (bf16[4,64,256]{2,1,0:T(8,128)(2,1)}, bf16[4,64,256]{2,1,0:T(8,128)(2,1)S(1)}, bf16[2,512,256]{2,1,0:T(8,128)(2,1)S(1)}) custom-call(s32[6]{0:T(128)S(1)} %stack.87.idx_ref, bf16[64,3584]{1,0:T(8,128)(2,1)S(1)} %collective-permute-done.25.refs_0_.refs_9_.refs_10_, bf16[64,3584]{1,0:T(8,128)(2,1)S(1)} %collective-permute-done.26.refs_1_.refs_10_.refs_11_, ...), custom_call_target="tpu_custom_call" | custom-call | flops 3758096384 | bytes 9175040 | tf_op jit(solution)/shard_map/pallas_call | solution.py:178
  198.3 8.4 %shard_map.85 = bf16[512,3584]{1,0:T(8,128)(2,1)} custom-call(s32[1]{0:T(128)} %bitcast.28.idx_ref, bf16[2,512,640]{2,1,0:T(8,128)(2,1)S(1)} %get-tuple-element.200.refs_0_, bf16[2,512,256]{2,1,0:T(8,128)(2,1)S(1)} %get-tuple-element.201.refs_1_, f32[2,512,3584]{2,1,0:T(8,128)} %shard_map.79.refs_2_, ...), custom_call_target="tpu_custom_call" | custom-call | flops 3288334336 | bytes 22020096 | tf_op jit(solution)/shard_map/pallas_call | solution.py:300
  207.3 2.3 collective-permute-start.32
  210.8 3.5 %collective-permute-done.36.refs_3_ = bf16[4,64,256]{2,1,0:T(8,128)(2,1)} collective-permute-done((bf16[4,64,256]{2,1,0:T(8,128)(2,1)}, bf16[4,64,256]{2,1,0:T(8,128)(2,1)}, u32[]{:S(2)}, u32[]{:S(2)}) %collective-permute-start.36) | collective-permute-done | bytes 131104 | tf_op jit(solution)/shard_map/ppermute | solution.py:379
  214.9 2.2 collective-permute-done.32.refs_3_
  221.2 1.7 shard_map.81
  222.9 1.8 shard_map.83
  225.0 1.8 shard_map.84
  226.8 2.0 collective-permute-start.40
  228.8 2.4 collective-permute-start.33
  231.6 2.8 %copy.16 = bf16[1,4,4,60,1024]{4,2,3,1,0:T(4,128)(2,1)} copy(bf16[1,4,4,60,1024]{4,3,1,2,0:T(8,128)(2,1)S(1)} %slice_bitcast_fusion) | data formatting | bytes 3932160
  235.2 10.3 %shard_map.86 = f32[128,4,3584]{2,1,0:T(4,128)} custom-call(s32[1]{0:T(128)} %bitcast.20.idx_ref, bf16[2,512,640]{2,1,0:T(8,128)(2,1)S(1)} %copy-done.4, bf16[2,512,256]{2,1,0:T(8,128)(2,1)S(1)} %get-tuple-element.201.refs_1_, f32[2,512,3584]{2,1,0:T(8,128)} %shard_map.79.refs_2_, bf16[512,3584]{1,0:T(8,128)(2,1)} %collective-permute-done.41.refs_3_, ...), custom_call_target="tpu_custom_call" | custom-call | flops 3288334336 | bytes 22020096 | tf_op jit(solution)/shard_map/pallas_call | solution.py:300
  (229 shorter events, 36.5 us)
Async XLA Ops:
  0.6 23.6 %collective-permute-start.2 = (bf16[128,3584]{1,0:T(8,128)(2,1)}, bf16[128,3584]{1,0:T(8,128)(2,1)S(1)}, u32[]{:S(2)}, u32[]{:S(2)}) collective-permute-start(bf16[128,3584]{1,0:T(8,128)(2,1)} %refs_2_.1), channel_id=1, source_target_pairs={{0,8},{4,12},{8,0},{12,4},{16,24},{20,28},{24,16},{28,20},{1,9},{5... | collective-permute-start | bytes 2752520 | tf_op jit(solution)/shard_map/ppermute | solution.py:379
  3.6 29.8 %collective-permute-start.4 = (bf16[128,3584]{1,0:T(8,128)(2,1)}, bf16[128,3584]{1,0:T(8,128)(2,1)S(1)}, u32[]{:S(2)}, u32[]{:S(2)}) collective-permute-start(bf16[128,3584]{1,0:T(8,128)(2,1)} %refs_2_.1), channel_id=1, source_target_pairs={{0,16},{4,20},{8,24},{12,28},{16,0},{20,4},{24,8},{28,12},{1,17},{... | collective-permute-start | bytes 2752520 | tf_op jit(solution)/shard_map/ppermute | solution.py:379
  5.2 28.2 %collective-permute-start.5 = (bf16[128,3584]{1,0:T(8,128)(2,1)}, bf16[128,3584]{1,0:T(8,128)(2,1)}, u32[]{:S(2)}, u32[]{:S(2)}) collective-permute-start(bf16[128,3584]{1,0:T(8,128)(2,1)} %refs_2_.1), channel_id=1, source_target_pairs={{0,1},{1,2},{2,3},{3,0},{4,5},{5,6},{6,7},{7,4},{8,9},{9,10},{10,1... | collective-permute-start | bytes 2752520 | tf_op jit(solution)/shard_map/ppermute | solution.py:382
  8.8 24.6 %collective-permute-start = (bf16[4,256]{1,0:T(4,128)(2,1)S(1)}, bf16[4,256]{1,0:T(4,128)(2,1)S(1)}, u32[]{:S(2)}, u32[]{:S(2)}) collective-permute-start(bf16[4,256]{1,0:T(4,128)(2,1)S(1)} %pad_maximum_fusion.5), channel_id=1, source_target_pairs={{0,1},{1,2},{2,3},{3,0},{4,5},{5,6},{6,7},{7,4},{8,9},{9,10},{10,1... | collective-permute-start | bytes 6152 | tf_op jit(solution)/shard_map/ppermute | solution.py:382
  10.4 22.9 %collective-permute-start.1 = (bf16[4,256]{1,0:T(4,128)(2,1)S(1)}, bf16[4,256]{1,0:T(4,128)(2,1)S(1)}, u32[]{:S(2)}, u32[]{:S(2)}) collective-permute-start(bf16[4,256]{1,0:T(4,128)(2,1)S(1)} %pad_maximum_fusion.5), channel_id=1, source_target_pairs={{0,2},{1,3},{2,0},{3,1},{4,6},{5,7},{6,4},{7,5},{8,10},{9,11},{10,... | collective-permute-start | bytes 6152 | tf_op jit(solution)/shard_map/ppermute | solution.py:382
  24.2 55.1 %copy-start.20 = (bf16[128,3584]{1,0:T(8,128)(2,1)}, bf16[128,3584]{1,0:T(8,128)(2,1)S(1)}, u32[]{:S(2)}) copy-start(bf16[128,3584]{1,0:T(8,128)(2,1)S(1)} %collective-permute-done.2.refs_1_.refs_3_) | copy-start | bytes 2752516
  24.2 9.2 %collective-permute-start.3 = (bf16[4,256]{1,0:T(4,128)(2,1)S(1)}, bf16[4,256]{1,0:T(4,128)(2,1)S(1)}, u32[]{:S(2)}, u32[]{:S(2)}) collective-permute-start(bf16[4,256]{1,0:T(4,128)(2,1)S(1)} %pad_maximum_fusion.5), channel_id=1, source_target_pairs={{0,3},{1,0},{2,1},{3,2},{4,7},{5,4},{6,5},{7,6},{8,11},{9,8},{10,9... | collective-permute-start | bytes 6152 | tf_op jit(solution)/shard_map/ppermute | solution.py:382
  33.4 45.9 %copy-start.22 = (bf16[128,3584]{1,0:T(8,128)(2,1)}, bf16[128,3584]{1,0:T(8,128)(2,1)S(1)}, u32[]{:S(2)}) copy-start(bf16[128,3584]{1,0:T(8,128)(2,1)S(1)} %collective-permute-done.4.refs_2_.refs_4_) | copy-start | bytes 2752516
  33.4 41.2 %collective-permute-start.12 = (bf16[512,3584]{1,0:T(8,128)(2,1)}, bf16[512,3584]{1,0:T(8,128)(2,1)}, u32[]{:S(2)}, u32[]{:S(2)}) collective-permute-start(bf16[512,3584]{1,0:T(8,128)(2,1)} %bitcast.9.refs_5_.refs_6_.refs_4_), channel_id=1, source_target_pairs={{0,4},{4,0},{8,12},{12,8},{16,20},{20,16},{24,28},{28,24},{1,5},{5... | collective-permute-start | bytes 11010056 | tf_op jit(solution)/shard_map/ppermute | solution.py:379
  34.5 13.5 %collective-permute-start.10 = (bf16[64,3584]{1,0:T(8,128)(2,1)}, bf16[64,3584]{1,0:T(8,128)(2,1)S(1)}, u32[]{:S(2)}, u32[]{:S(2)}) collective-permute-start(bf16[64,3584]{1,0:T(8,128)(2,1)} %slice.22), channel_id=1, source_target_pairs={{0,8},{4,12},{8,0},{12,4},{16,24},{20,28},{24,16},{28,20},{1,9},{5... | collective-permute-start | bytes 1376264 | tf_op jit(solution)/shard_map/ppermute | solution.py:379
  36.0 38.6 %collective-permute-start.11 = (bf16[128,3584]{1,0:T(8,128)(2,1)}, bf16[128,3584]{1,0:T(8,128)(2,1)}, u32[]{:S(2)}, u32[]{:S(2)}) collective-permute-start(bf16[128,3584]{1,0:T(8,128)(2,1)} %collective-permute-done.5.refs_0_.refs_7_), channel_id=1, source_target_pairs={{0,1},{1,2},{2,3},{3,0},{4,5},{5,6},{6,7},{7,4},{8,9},{9,10},{10,1... | collective-permute-start | bytes 2752520 | tf_op jit(solution)/shard_map/ppermute | solution.py:382
  36.8 13.5 %collective-permute-start.9 = (bf16[64,3584]{1,0:T(8,128)(2,1)}, bf16[64,3584]{1,0:T(8,128)(2,1)S(1)}, u32[]{:S(2)}, u32[]{:S(2)}) collective-permute-start(bf16[64,3584]{1,0:T(8,128)(2,1)} %slice.21), channel_id=1, source_target_pairs={{0,16},{4,20},{8,24},{12,28},{16,0},{20,4},{24,8},{28,12},{1,17},{... | collective-permute-start | bytes 1376264 | tf_op jit(solution)/shard_map/ppermute | solution.py:379
  40.7 18.5 %collective-permute-start.6 = (bf16[4,4,64,256]{3,2,1,0:T(8,128)(2,1)S(1)}, bf16[4,4,64,256]{3,2,1,0:T(8,128)(2,1)S(1)}, u32[]{:S(2)}, u32[]{:S(2)}) collective-permute-start(bf16[4,4,64,256]{3,2,1,0:T(8,128)(2,1)S(1)} %get-tuple-element.220), channel_id=1, source_target_pairs={{0,8},{4,12},{8,0},{12,4},{16,24},{20,28},{24,16},{28,20},{1,9},{5... | collective-permute-start | bytes 1572872 | tf_op jit(solution)/shard_map/ppermute | solution.py:379
  48.8 24.2 %collective-permute-start.7 = (bf16[4,4,64,256]{3,2,1,0:T(8,128)(2,1)S(1)}, bf16[4,4,64,256]{3,2,1,0:T(8,128)(2,1)S(1)}, u32[]{:S(2)}, u32[]{:S(2)}) collective-permute-start(bf16[4,4,64,256]{3,2,1,0:T(8,128)(2,1)S(1)} %get-tuple-element.221), channel_id=1, source_target_pairs={{0,16},{4,20},{8,24},{12,28},{16,0},{20,4},{24,8},{28,12},{1,17},{... | collective-permute-start | bytes 1572872 | tf_op jit(solution)/shard_map/ppermute | solution.py:379
  51.1 22.7 %collective-permute-start.8 = (bf16[4,4,64,256]{3,2,1,0:T(8,128)(2,1)S(1)}, bf16[4,4,64,256]{3,2,1,0:T(8,128)(2,1)S(1)}, u32[]{:S(2)}, u32[]{:S(2)}) collective-permute-start(bf16[4,4,64,256]{3,2,1,0:T(8,128)(2,1)S(1)} %get-tuple-element.219), channel_id=1, source_target_pairs={{0,24},{4,28},{8,16},{12,20},{16,8},{20,12},{24,0},{28,4},{1,25},{... | collective-permute-start | bytes 1572872 | tf_op jit(solution)/shard_map/ppermute | solution.py:379
  74.6 22.3 %collective-permute-start.13 = (bf16[128,3584]{1,0:T(8,128)(2,1)}, bf16[128,3584]{1,0:T(8,128)(2,1)}, u32[]{:S(2)}, u32[]{:S(2)}) collective-permute-start(bf16[128,3584]{1,0:T(8,128)(2,1)} %collective-permute-done.5.refs_0_.refs_7_), channel_id=1, source_target_pairs={{0,8},{4,12},{8,0},{12,4},{16,24},{20,28},{24,16},{28,20},{1,9},{5... | collective-permute-start | bytes 2752520 | tf_op jit(solution)/shard_map/ppermute | solution.py:379
  76.1 20.8 %collective-permute-start.14 = (bf16[128,3584]{1,0:T(8,128)(2,1)}, bf16[128,3584]{1,0:T(8,128)(2,1)}, u32[]{:S(2)}, u32[]{:S(2)}) collective-permute-start(bf16[128,3584]{1,0:T(8,128)(2,1)} %collective-permute-done.5.refs_0_.refs_7_), channel_id=1, source_target_pairs={{0,16},{4,20},{8,24},{12,28},{16,0},{20,4},{24,8},{28,12},{1,17},{... | collective-permute-start | bytes 2752520 | tf_op jit(solution)/shard_map/ppermute | solution.py:379
  77.6 23.4 %collective-permute-start.15 = (bf16[128,3584]{1,0:T(8,128)(2,1)S(1)}, bf16[128,3584]{1,0:T(8,128)(2,1)}, u32[]{:S(2)}, u32[]{:S(2)}) collective-permute-start(bf16[128,3584]{1,0:T(8,128)(2,1)S(1)} %collective-permute-done.2.refs_1_.refs_3_), channel_id=1, source_target_pairs={{0,3},{1,0},{2,1},{3,2},{4,7},{5,4},{6,5},{7,6},{8,11},{9,8},{10,9... | collective-permute-start | bytes 2752520 | tf_op jit(solution)/shard_map/ppermute | solution.py:382
  79.2 38.0 %collective-permute-start.21 = (bf16[128,3584]{1,0:T(8,128)(2,1)}, bf16[128,3584]{1,0:T(8,128)(2,1)S(1)}, u32[]{:S(2)}, u32[]{:S(2)}) collective-permute-start(bf16[128,3584]{1,0:T(8,128)(2,1)} %refs_2_.1), channel_id=1, source_target_pairs={{0,3},{1,0},{2,1},{3,2},{4,7},{5,4},{6,5},{7,6},{8,11},{9,8},{10,9... | collective-permute-start | bytes 2752520 | tf_op jit(solution)/shard_map/ppermute | solution.py:382
  101.0 16.7 %collective-permute-start.22 = (bf16[4,64,256]{2,1,0:T(8,128)(2,1)S(1)}, bf16[4,64,256]{2,1,0:T(8,128)(2,1)S(1)}, u32[]{:S(2)}, u32[]{:S(2)}) collective-permute-start(bf16[4,64,256]{2,1,0:T(8,128)(2,1)S(1)} %get-tuple-element.137), channel_id=1, source_target_pairs={{0,8},{4,12},{8,0},{12,4},{16,24},{20,28},{24,16},{28,20},{1,9},{5... | collective-permute-start | bytes 393224 | tf_op jit(solution)/shard_map/ppermute | solution.py:379
  101.5 23.4 %collective-permute-start.23 = (bf16[4,64,256]{2,1,0:T(8,128)(2,1)}, bf16[4,64,256]{2,1,0:T(8,128)(2,1)S(1)}, u32[]{:S(2)}, u32[]{:S(2)}) collective-permute-start(bf16[4,64,256]{2,1,0:T(8,128)(2,1)} %get-tuple-element.138), channel_id=1, source_target_pairs={{0,16},{4,20},{8,24},{12,28},{16,0},{20,4},{24,8},{28,12},{1,17},{... | collective-permute-start | bytes 393224 | tf_op jit(solution)/shard_map/ppermute | solution.py:379
  102.0 24.5 %collective-permute-start.24 = (bf16[4,64,256]{2,1,0:T(8,128)(2,1)}, bf16[4,64,256]{2,1,0:T(8,128)(2,1)S(1)}, u32[]{:S(2)}, u32[]{:S(2)}) collective-permute-start(bf16[4,64,256]{2,1,0:T(8,128)(2,1)} %get-tuple-element.139), channel_id=1, source_target_pairs={{0,24},{4,28},{8,16},{12,20},{16,8},{20,12},{24,0},{28,4},{1,25},{... | collective-permute-start | bytes 393224 | tf_op jit(solution)/shard_map/ppermute | solution.py:379
  104.5 43.1 %collective-permute-start.18 = (bf16[128,3584]{1,0:T(8,128)(2,1)}, bf16[128,3584]{1,0:T(8,128)(2,1)S(1)}, u32[]{:S(2)}, u32[]{:S(2)}) collective-permute-start(bf16[128,3584]{1,0:T(8,128)(2,1)} %collective-permute-done.11.refs_3_.refs_10_), channel_id=1, source_target_pairs={{0,8},{4,12},{8,0},{12,4},{16,24},{20,28},{24,16},{28,20},{1,9},{5... | collective-permute-start | bytes 2752520 | tf_op jit(solution)/shard_map/ppermute | solution.py:379
  117.2 38.9 %copy-start.5 = (bf16[128,3584]{1,0:T(8,128)(2,1)}, bf16[128,3584]{1,0:T(8,128)(2,1)S(1)}, u32[]{:S(2)}) copy-start(bf16[128,3584]{1,0:T(8,128)(2,1)S(1)} %collective-permute-done.21.refs_3_.refs_6_.refs_7_) | copy-start | bytes 2752516
  117.2 30.4 %collective-permute-start.19 = (bf16[128,3584]{1,0:T(8,128)(2,1)}, bf16[128,3584]{1,0:T(8,128)(2,1)S(1)}, u32[]{:S(2)}, u32[]{:S(2)}) collective-permute-start(bf16[128,3584]{1,0:T(8,128)(2,1)} %collective-permute-done.11.refs_3_.refs_10_), channel_id=1, source_target_pairs={{0,16},{4,20},{8,24},{12,28},{16,0},{20,4},{24,8},{28,12},{1,17},{... | collective-permute-start | bytes 2752520 | tf_op jit(solution)/shard_map/ppermute | solution.py:379
  118.4 29.3 %collective-permute-start.20 = (bf16[128,3584]{1,0:T(8,128)(2,1)}, bf16[128,3584]{1,0:T(8,128)(2,1)}, u32[]{:S(2)}, u32[]{:S(2)}) collective-permute-start(bf16[128,3584]{1,0:T(8,128)(2,1)} %copy-done.22), channel_id=1, source_target_pairs={{0,3},{1,0},{2,1},{3,2},{4,7},{5,4},{6,5},{7,6},{8,11},{9,8},{10,9... | collective-permute-start | bytes 2752520 | tf_op jit(solution)/shard_map/ppermute | solution.py:382
  122.6 33.5 %copy-start.54 = (bf16[4,4,64,256]{3,2,1,0:T(8,128)(2,1)S(1)}, bf16[4,4,64,256]{3,2,1,0:T(8,128)(2,1)}, u32[]{:S(2)}) copy-start(bf16[4,4,64,256]{3,2,1,0:T(8,128)(2,1)} %copy-done.51) | copy-start | bytes 1572868
  124.9 22.7 %collective-permute-start.16 = (bf16[64,3584]{1,0:T(8,128)(2,1)S(1)}, bf16[64,3584]{1,0:T(8,128)(2,1)S(1)}, u32[]{:S(2)}, u32[]{:S(2)}) collective-permute-start(bf16[64,3584]{1,0:T(8,128)(2,1)S(1)} %slice.23), channel_id=1, source_target_pairs={{0,16},{4,20},{8,24},{12,28},{16,0},{20,4},{24,8},{28,12},{1,17},{... | collective-permute-start | bytes 1376264 | tf_op jit(solution)/shard_map/ppermute | solution.py:379
  126.5 21.1 %collective-permute-start.17 = (bf16[64,3584]{1,0:T(8,128)(2,1)S(1)}, bf16[64,3584]{1,0:T(8,128)(2,1)S(1)}, u32[]{:S(2)}, u32[]{:S(2)}) collective-permute-start(bf16[64,3584]{1,0:T(8,128)(2,1)S(1)} %slice.24), channel_id=1, source_target_pairs={{0,8},{4,12},{8,0},{12,4},{16,24},{20,28},{24,16},{28,20},{1,9},{5... | collective-permute-start | bytes 1376264 | tf_op jit(solution)/shard_map/ppermute | solution.py:379
  147.6 50.6 %copy-start.8 = (bf16[64,3584]{1,0:T(8,128)(2,1)}, bf16[64,3584]{1,0:T(8,128)(2,1)S(1)}, u32[]{:S(2)}) copy-start(bf16[64,3584]{1,0:T(8,128)(2,1)S(1)} %collective-permute-done.16.refs_4_.refs_7_.refs_8_) | copy-start | bytes 1376260
  147.6 50.6 %copy-start.10 = (bf16[64,3584]{1,0:T(8,128)(2,1)}, bf16[64,3584]{1,0:T(8,128)(2,1)S(1)}, u32[]{:S(2)}) copy-start(bf16[64,3584]{1,0:T(8,128)(2,1)S(1)} %collective-permute-done.17.refs_5_.refs_8_.refs_9_) | copy-start | bytes 1376260
  147.7 41.3 %collective-permute-start.25 = (bf16[64,3584]{1,0:T(8,128)(2,1)S(1)}, bf16[64,3584]{1,0:T(8,128)(2,1)S(1)}, u32[]{:S(2)}, u32[]{:S(2)}) collective-permute-start(bf16[64,3584]{1,0:T(8,128)(2,1)S(1)} %slice.25), channel_id=1, source_target_pairs={{0,16},{4,20},{8,24},{12,28},{16,0},{20,4},{24,8},{28,12},{1,17},{... | collective-permute-start | bytes 1376264 | tf_op jit(solution)/shard_map/ppermute | solution.py:379
  148.4 40.7 %collective-permute-start.26 = (bf16[64,3584]{1,0:T(8,128)(2,1)S(1)}, bf16[64,3584]{1,0:T(8,128)(2,1)S(1)}, u32[]{:S(2)}, u32[]{:S(2)}) collective-permute-start(bf16[64,3584]{1,0:T(8,128)(2,1)S(1)} %slice.26), channel_id=1, source_target_pairs={{0,8},{4,12},{8,0},{12,4},{16,24},{20,28},{24,16},{28,20},{1,9},{5... | collective-permute-start | bytes 1376264 | tf_op jit(solution)/shard_map/ppermute | solution.py:379
  149.8 39.2 %collective-permute-start.27 = (bf16[64,3584]{1,0:T(8,128)(2,1)S(1)}, bf16[64,3584]{1,0:T(8,128)(2,1)S(1)}, u32[]{:S(2)}, u32[]{:S(2)}) collective-permute-start(bf16[64,3584]{1,0:T(8,128)(2,1)S(1)} %copy-done.60), channel_id=1, source_target_pairs={{0,3},{1,0},{2,1},{3,2},{4,7},{5,4},{6,5},{7,6},{8,11},{9,8},{10,9... | collective-permute-start | bytes 1376264 | tf_op jit(solution)/shard_map/ppermute | solution.py:382
  154.0 18.0 %collective-permute-start.29 = (bf16[4,64,256]{2,1,0:T(8,128)(2,1)S(1)}, bf16[4,64,256]{2,1,0:T(8,128)(2,1)S(1)}, u32[]{:S(2)}, u32[]{:S(2)}) collective-permute-start(bf16[4,64,256]{2,1,0:T(8,128)(2,1)S(1)} %get-tuple-element.154), channel_id=1, source_target_pairs={{0,8},{4,12},{8,0},{12,4},{16,24},{20,28},{24,16},{28,20},{1,9},{5... | collective-permute-start | bytes 393224 | tf_op jit(solution)/shard_map/ppermute | solution.py:379
  154.6 17.5 %collective-permute-start.30 = (bf16[4,64,256]{2,1,0:T(8,128)(2,1)S(1)}, bf16[4,64,256]{2,1,0:T(8,128)(2,1)S(1)}, u32[]{:S(2)}, u32[]{:S(2)}) collective-permute-start(bf16[4,64,256]{2,1,0:T(8,128)(2,1)S(1)} %get-tuple-element.155), channel_id=1, source_target_pairs={{0,16},{4,20},{8,24},{12,28},{16,0},{20,4},{24,8},{28,12},{1,17},{... | collective-permute-start | bytes 393224 | tf_op jit(solution)/shard_map/ppermute | solution.py:379
  172.0 17.1 %collective-permute-start.28 = (bf16[64,3584]{1,0:T(8,128)(2,1)S(1)}, bf16[64,3584]{1,0:T(8,128)(2,1)S(1)}, u32[]{:S(2)}, u32[]{:S(2)}) collective-permute-start(bf16[64,3584]{1,0:T(8,128)(2,1)S(1)} %copy-done.57), channel_id=1, source_target_pairs={{0,3},{1,0},{2,1},{3,2},{4,7},{5,4},{6,5},{7,6},{8,11},{9,8},{10,9... | collective-permute-start | bytes 1376264 | tf_op jit(solution)/shard_map/ppermute | solution.py:382
  172.1 16.9 %collective-permute-start.31 = (bf16[4,64,256]{2,1,0:T(8,128)(2,1)S(1)}, bf16[4,64,256]{2,1,0:T(8,128)(2,1)S(1)}, u32[]{:S(2)}, u32[]{:S(2)}) collective-permute-start(bf16[4,64,256]{2,1,0:T(8,128)(2,1)S(1)} %get-tuple-element.157), channel_id=1, source_target_pairs={{0,8},{4,12},{8,0},{12,4},{16,24},{20,28},{24,16},{28,20},{1,9},{5... | collective-permute-start | bytes 393224 | tf_op jit(solution)/shard_map/ppermute | solution.py:379
  206.7 28.5 %collective-permute-start.41 = (bf16[512,3584]{1,0:T(8,128)(2,1)}, bf16[512,3584]{1,0:T(8,128)(2,1)}, u32[]{:S(2)}, u32[]{:S(2)}) collective-permute-start(bf16[512,3584]{1,0:T(8,128)(2,1)} %shard_map.85), channel_id=1, source_target_pairs={{0,4},{4,0},{8,12},{12,8},{16,20},{20,16},{24,28},{28,24},{1,5},{5... | collective-permute-start | bytes 11010056 | tf_op jit(solution)/shard_map/ppermute | solution.py:379
  206.7 7.7 %collective-permute-start.36 = (bf16[4,64,256]{2,1,0:T(8,128)(2,1)}, bf16[4,64,256]{2,1,0:T(8,128)(2,1)}, u32[]{:S(2)}, u32[]{:S(2)}) collective-permute-start(bf16[4,64,256]{2,1,0:T(8,128)(2,1)} %get-tuple-element.190), channel_id=1, source_target_pairs={{0,24},{4,28},{8,16},{12,20},{16,8},{20,12},{24,0},{28,4},{1,25},{... | collective-permute-start | bytes 393224 | tf_op jit(solution)/shard_map/ppermute | solution.py:379
  207.3 9.8 %collective-permute-start.32 = (bf16[4,64,256]{2,1,0:T(8,128)(2,1)}, bf16[4,64,256]{2,1,0:T(8,128)(2,1)}, u32[]{:S(2)}, u32[]{:S(2)}) collective-permute-start(bf16[4,64,256]{2,1,0:T(8,128)(2,1)} %get-tuple-element.180), channel_id=1, source_target_pairs={{0,24},{4,28},{8,16},{12,20},{16,8},{20,12},{24,0},{28,4},{1,25},{... | collective-permute-start | bytes 393224 | tf_op jit(solution)/shard_map/ppermute | solution.py:379
  209.7 13.2 %collective-permute-start.34 = (bf16[4,64,256]{2,1,0:T(8,128)(2,1)}, bf16[4,64,256]{2,1,0:T(8,128)(2,1)}, u32[]{:S(2)}, u32[]{:S(2)}) collective-permute-start(bf16[4,64,256]{2,1,0:T(8,128)(2,1)} %copy-done.63), channel_id=1, source_target_pairs={{0,8},{4,12},{8,0},{12,4},{16,24},{20,28},{24,16},{28,20},{1,9},{5... | collective-permute-start | bytes 393224 | tf_op jit(solution)/shard_map/ppermute | solution.py:379
  210.3 12.6 %collective-permute-start.35 = (bf16[4,64,256]{2,1,0:T(8,128)(2,1)}, bf16[4,64,256]{2,1,0:T(8,128)(2,1)}, u32[]{:S(2)}, u32[]{:S(2)}) collective-permute-start(bf16[4,64,256]{2,1,0:T(8,128)(2,1)} %copy-done.62), channel_id=1, source_target_pairs={{0,16},{4,20},{8,24},{12,28},{16,0},{20,4},{24,8},{28,12},{1,17},{... | collective-permute-start | bytes 393224 | tf_op jit(solution)/shard_map/ppermute | solution.py:379
  214.4 10.4 %collective-permute-start.39 = (bf16[4,64,256]{2,1,0:T(8,128)(2,1)}, bf16[4,64,256]{2,1,0:T(8,128)(2,1)}, u32[]{:S(2)}, u32[]{:S(2)}) collective-permute-start(bf16[4,64,256]{2,1,0:T(8,128)(2,1)} %copy-done.64), channel_id=1, source_target_pairs={{0,24},{4,28},{8,16},{12,20},{16,8},{20,12},{24,0},{28,4},{1,25},{... | collective-permute-start | bytes 393224 | tf_op jit(solution)/shard_map/ppermute | solution.py:379
  217.1 7.9 %collective-permute-start.38 = (bf16[4,64,256]{2,1,0:T(8,128)(2,1)}, bf16[4,64,256]{2,1,0:T(8,128)(2,1)}, u32[]{:S(2)}, u32[]{:S(2)}) collective-permute-start(bf16[4,64,256]{2,1,0:T(8,128)(2,1)} %copy-done.61), channel_id=1, source_target_pairs={{0,16},{4,20},{8,24},{12,28},{16,0},{20,4},{24,8},{28,12},{1,17},{... | collective-permute-start | bytes 393224 | tf_op jit(solution)/shard_map/ppermute | solution.py:379
  226.8 7.6 %collective-permute-start.40 = (f32[4,128]{1,0:T(4,128)S(1)}, f32[4,128]{1,0:T(4,128)S(1)}, u32[]{:S(2)}, u32[]{:S(2)}) collective-permute-start(f32[4,128]{1,0:T(4,128)S(1)} %get-tuple-element.198), channel_id=1, source_target_pairs={{0,1},{1,2},{2,3},{3,0},{4,5},{5,6},{6,7},{7,4},{8,9},{9,10},{10,1... | collective-permute-start | bytes 6152 | tf_op jit(solution)/shard_map/ppermute | solution.py:382
  228.8 5.6 %collective-permute-start.37 = (f32[4,128]{1,0:T(4,128)S(1)}, f32[4,128]{1,0:T(4,128)S(1)}, u32[]{:S(2)}, u32[]{:S(2)}) collective-permute-start(f32[4,128]{1,0:T(4,128)S(1)} %get-tuple-element.192), channel_id=1, source_target_pairs={{0,2},{1,3},{2,0},{3,1},{4,6},{5,7},{6,4},{7,5},{8,10},{9,11},{10,... | collective-permute-start | bytes 6152 | tf_op jit(solution)/shard_map/ppermute | solution.py:382
  228.8 5.6 %collective-permute-start.33 = (f32[4,128]{1,0:T(4,128)S(1)}, f32[4,128]{1,0:T(4,128)S(1)}, u32[]{:S(2)}, u32[]{:S(2)}) collective-permute-start(f32[4,128]{1,0:T(4,128)S(1)} %get-tuple-element.182), channel_id=1, source_target_pairs={{0,3},{1,0},{2,1},{3,2},{4,7},{5,4},{6,5},{7,6},{8,11},{9,8},{10,9... | collective-permute-start | bytes 6152 | tf_op jit(solution)/shard_map/ppermute | solution.py:382
  (68 other events, 572.6 us)

commit v7 on v6

--- a/solution.py
+++ b/solution.py
@@ -73,7 +73,7 @@
 SLOT_PAD = 64
 F32 = jnp.float32
 BF16 = jnp.bfloat16
-VMEM_BYTES = 32 * 2**20
+VMEM_BYTES = 36 * 2**20
 
 
 def nt_dot(a, b):
@@ -162,8 +162,10 @@
     def _():
         height = terms.shape[1]
         row = lax.broadcasted_iota(jnp.int32, (height, height), 0)
-        col = lax.broadcasted_iota(jnp.int32, (height, height), 1)
-        order = (col == lax.rem(row, experts) * block + lax.div(row, experts)).astype(BF16)
+        col = lax.broadcasted_iota(jnp.int32, (8, height), 1)
+        shift = block.bit_length() - 1
+        to = (jnp.bitwise_and(col, block - 1) * experts + jnp.right_shift(col, shift))[0:1]
+        order = (row == to).astype(BF16)
         for half in range(2):
             scatter_ref[half] = jnp.dot(order, terms[half], preferred_element_type=F32).astype(BF16)
 
@@ -226,46 +228,20 @@
     return total
 
 
-def early_grad_kernel(terms, *refs):
-    scatters, pieces, out_ref, rows = refs[:terms], refs[terms:-2], refs[-2], refs[-1]
+def half_grad_kernel(terms, arrivals, last, idx_ref, *refs):
+    scatters, arrived = refs[:terms], refs[terms : terms + arrivals]
+    if last:
+        pieces, (out_ref, rows, held) = refs[terms + arrivals : -3], refs[-3:]
+    else:
+        pieces, (out_ref, rows) = refs[terms + arrivals : -2], refs[-2:]
     fill_rows(pieces, rows)
-    for half in range(2):
-        out_ref[half] = sum_terms(scatters, rows, half)
-
-
-def early_grad(scatters, pieces, tile):
-    height = scatters[0].shape[1]
-    width = pieces[0].shape[1]
-    count = sum(p.shape[0] for p in pieces)
-    return pl.pallas_call(
-        functools.partial(early_grad_kernel, len(scatters)),
-        grid=(width // tile,),
-        in_specs=[pl.BlockSpec(a.shape, lambda i: (0, 0, 0)) for a in scatters]
-        + [pl.BlockSpec((p.shape[0], tile), lambda i: (0, i)) for p in pieces],
-        out_specs=pl.BlockSpec((2, height, tile), lambda i: (0, 0, i)),
-        out_shape=jax.ShapeDtypeStruct((2, height, width), F32),
-        scratch_shapes=[pltpu.VMEM((count, tile), BF16)],
-        compiler_params=pltpu.CompilerParams(vmem_limit_bytes=VMEM_BYTES),
-        cost_estimate=pl.CostEstimate(
-            flops=4 * height * count * width,
-            bytes_accessed=2 * count * (width + 2 * height) + 8 * height * width,
-            transcendentals=0,
-        ),
-    )(*scatters, *pieces)
-
-
-def late_grad_kernel(terms, last, idx_ref, *refs):
-    scatters, before_ref = refs[:terms], refs[terms]
-    if not last:
-        pieces, out_ref, rows = refs[terms + 1 : -2], refs[-2], refs[-1]
-    else:
-        arrived_ref, pieces, out_ref, rows, held = refs[terms + 1], refs[terms + 2 : -3], *refs[-3:]
-    fill_rows(pieces, rows)
-    total = before_ref[0] + sum_terms(scatters, rows, 0)
+    total = sum_terms(scatters, rows, 0)
+    for array in arrived:
+        total += array[...].astype(F32)
     if not last:
         out_ref[...] = total.astype(BF16)
         return
-    held[...] = total + arrived_ref[...].astype(F32)
+    held[...] = total
     block, experts, _ = out_ref.shape
     group = 8 // experts
 
@@ -278,27 +254,23 @@
     lax.fori_loop(0, block // group, move, 0, unroll=4)
 
 
-def late_grad(index, scatters, pieces, before, arrived, experts, tile):
+def half_grad(index, scatters, pieces, arrived, experts, tile, last):
     height = scatters[0].shape[1]
     width = pieces[0].shape[1]
     count = sum(p.shape[0] for p in pieces)
     in_specs = [pl.BlockSpec((1,) + a.shape[1:], lambda i, idx: (idx[0], 0, 0)) for a in scatters]
-    in_specs.append(pl.BlockSpec((1, height, tile), lambda i, idx: (idx[0], 0, i)))
-    args = [*scatters, before]
+    in_specs += [pl.BlockSpec((height, tile), lambda i, idx: (0, i)) for _ in arrived]
+    in_specs += [pl.BlockSpec((p.shape[0], tile), lambda i, idx: (0, i)) for p in pieces]
     scratch = [pltpu.VMEM((count, tile), BF16)]
-    last = arrived is not None
     if last:
-        in_specs.append(pl.BlockSpec((height, tile), lambda i, idx: (0, i)))
-        args.append(arrived)
         scratch.append(pltpu.VMEM((height, tile), F32))
         out_spec = pl.BlockSpec((height // experts, experts, tile), lambda i, idx: (0, 0, i))
         out_shape = jax.ShapeDtypeStruct((height // experts, experts, width), F32)
     else:
         out_spec = pl.BlockSpec((height, tile), lambda i, idx: (0, i))
         out_shape = jax.ShapeDtypeStruct((height, width), BF16)
-    in_specs += [pl.BlockSpec((p.shape[0], tile), lambda i, idx: (0, i)) for p in pieces]
     return pl.pallas_call(
-        functools.partial(late_grad_kernel, len(scatters), last),
+        functools.partial(half_grad_kernel, len(scatters), len(arrived), last),
         grid_spec=pltpu.PrefetchScalarGridSpec(
             num_scalar_prefetch=1,
             grid=(width // tile,),
@@ -310,10 +282,10 @@
         compiler_params=pltpu.CompilerParams(vmem_limit_bytes=VMEM_BYTES),
         cost_estimate=pl.CostEstimate(
             flops=2 * height * count * width,
-            bytes_accessed=2 * count * (width + height) + 8 * height * width,
+            bytes_accessed=2 * count * (width + height) + 4 * height * width,
             transcendentals=0,
         ),
-    )(index, *args, *pieces)
+    )(index, *scatters, *arrived, *pieces)
 
 
 def place_kernel(top_k, first, idx_ref, *refs):
@@ -386,7 +358,6 @@
     route_weight = (ROUTE_SCALE * shares).astype(BF16)
     meta = jnp.concatenate([routes.astype(BF16).T, route_weight.T], axis=1)
     fence = lax.optimization_barrier
-    half = tokens // 2
 
     slabs = [lax.rem(me - step + sources, sources) for step in range(sources)]
     index = jnp.stack(slabs + [me * experts, core]).astype(jnp.int32)
@@ -403,13 +374,16 @@
         return place(spots, returned, placed, sources, top_k)
 
     x0, y0, next1 = across(grad_out, 2), across(grad_out, 4), around(grad_out, 1)
-    metas = [meta, around(meta, 1), around(meta, 2), around(fence((meta, x0))[0], 3)]
     held = jnp.transpose(saved_hidden.reshape(experts, sources, most, 4, pair), (3, 0, 1, 2, 4))
     held = fence(held)
     held = [lax.dynamic_index_in_dim(held, chips[m], axis=0, keepdims=False) for m in range(4)]
     own_weight = jnp.transpose(down_proj, (1, 0, 2)).reshape(experts * block, width)
+    last_meta, held, own_weight = fence((meta, held, own_weight))
+    metas = [meta, around(meta, 1), around(meta, 2), around(last_meta, 3)]
     metas, x0, y0, next1, held, own_weight = fence((metas, x0, y0, next1, held, own_weight))
 
+    xy0, x1 = across(x0, 4), across(next1, 2)
+    next2, own3 = around(next1, 1), around(fence((grad_out, y0))[0], -1)
     metas = jnp.take(jnp.stack(metas), lax.rem(me - jnp.arange(sources) + sources, sources), axis=0)
     blank = jnp.zeros((experts, sources, SLOT_PAD - most - top_k, pair), BF16)
     metas = jnp.broadcast_to(metas[None], (experts, sources, top_k, pair))
@@ -417,51 +391,46 @@
     for m in range(4):
         piece = jnp.concatenate([held[m], blank, metas], axis=2)
         hidden.append(across(piece, 2 * m) if m else piece)
-    top0, bottom0 = across(x0[:half], 4), across(y0[half:], 2)
-    next2 = around(next1, 1)
     partner_weight = across(own_weight, 1)
-    hidden, top0, bottom0, next2, partner_weight, x0, y0, next1 = fence(
-        (hidden, top0, bottom0, next2, partner_weight, x0, y0, next1)
-    )
-
-    x1, y1, x3 = across(next1, 2), across(next1, 4), around(x0, -1)
-    grads0, scatter0 = kernel([([grad_out], 0, 0), ([x0], 1, 0), ([y0], 2, 0), ([top0, bottom0], 3, 0)])
-    x1, y1, x3, grads0, scatter0, y0, top0, bottom0, next2 = fence(
-        (x1, y1, x3, grads0, scatter0, y0, top0, bottom0, next2)
-    )
-
-    top1, bottom1 = across(x1[:half], 4), across(y1[half:], 2)
-    x2, y2, y3, own3 = across(next2, 2), across(next2, 4), around(y0, -1), around(grad_out, -1)
+    hidden, xy0, x1, next2, own3, partner_weight, x0, y0, next1 = fence(
+        (hidden, xy0, x1, next2, own3, partner_weight, x0, y0, next1)
+    )
+
+    y1, x2, x3 = across(next1, 4), across(next2, 2), around(x0, -1)
+    grads0, scatter0 = kernel([([grad_out], 0, 0), ([x0], 1, 0), ([y0], 2, 0), ([xy0], 3, 0)])
+    y1, x2, x3, grads0, scatter0, y0, xy0, next2, x1 = fence(
+        (y1, x2, x3, grads0, scatter0, y0, xy0, next2, x1)
+    )
+
+    xy1, y2, y3 = across(y1, 2), across(next2, 4), around(y0, -1)
+    grads1, scatter1 = kernel(
+        [([next1], 0, 1), ([x1], 1, 1), ([y1], 2, 1), ([next2], 0, 2), ([x2], 1, 2), ([x3], 1, 3)]
+    )
+    xy1, y2, y3, grads1, scatter1, xy0, x2, grads0 = fence((xy1, y2, y3, grads1, scatter1, xy0, x2, grads0))
+
+    xy2, xy3 = across(x2, 4), around(xy0, -1)
     returned0 = send_back(grads0, (0, 1, 2, 3))
-    grads1, scatter1 = kernel([([next1], 0, 1), ([x1], 1, 1), ([y1], 2, 1), ([next2], 0, 2), ([x3], 1, 3)])
-    top1, bottom1, x2, y2, y3, own3, returned0, top0, bottom0, grads1, scatter1 = fence(
-        (top1, bottom1, x2, y2, y3, own3, returned0, top0, bottom0, grads1, scatter1)
-    )
-
-    top2, bottom2 = across(x2[:half], 4), across(y2[half:], 2)
-    top3, bottom3 = around(top0, -1), around(bottom0, -1)
-    returned1 = send_back(grads1, (0, 1, 2, 0, 1))
-    grads2, scatter2 = kernel(
-        [([x2], 1, 2), ([y2], 2, 2), ([y3], 2, 3), ([own3], 0, 3), ([top1, bottom1], 3, 1)]
-    )
-    before = early_grad(
-        [scatter0, scatter1], [grad_out, x0, y0, top0, bottom0, next1, x1, y1, next2, x3], 512
-    )
+    grads2, scatter2 = kernel([([xy1], 3, 1), ([y2], 2, 2), ([own3], 0, 3), ([y3], 2, 3)])
+    first = [grad_out, x0, y0, xy0, next1, x1, y1, next2, x2, x3]
+    other, mine = (1 - core).reshape(1), core.reshape(1)
+    partner = half_grad(other, [scatter0, scatter1], first, [], experts, 896, False)
+    xy2, xy3, returned0, grads2, scatter2, partner, grads1 = fence(
+        (xy2, xy3, returned0, grads2, scatter2, partner, grads1)
+    )
+
+    partner = across(partner, 1)
+    returned1 = send_back(grads1, (0, 1, 2, 0, 1, 1))
+    grads3, scatter3 = kernel([([xy2], 3, 2), ([xy3], 3, 3)])
+    late = [xy1, y2, own3, y3, xy2, xy3]
+    later = half_grad(other, [scatter2, scatter3], late, [], experts, 896, False)
+    partner, returned1, later, grads3, scatter3 = fence((partner, returned1, later, grads3, scatter3))
+    later = across(later, 1)
+    returned2 = send_back(grads2, (3, 2, 0, 2))
+    returned3 = send_back(grads3, (3, 3))
     placed, combine0 = put(0, returned0, None)
-    top2, bottom2, top3, bottom3, returned1, grads2, scatter2, before, placed, combine0 = fence(
-        (top2, bottom2, top3, bottom3, returned1, grads2, scatter2, before, placed, combine0)
-    )
-
-    returned2 = send_back(grads2, (1, 2, 2, 0, 3))
-    grads3, scatter3 = kernel([([top2, bottom2], 3, 2), ([top3, bottom3], 3, 3)])
-    returned3 = send_back(grads3, (3, 3))
-    late = [x2, y2, y3, own3, top1, bottom1, top2, bottom2, top3, bottom3]
-    late_scatters = [scatter2, scatter3]
-    partner = late_grad((1 - core).reshape(1), late_scatters, late, before, None, experts, 896)
-    partner = across(partner, 1)
-    placed, combine1 = put(1, [*returned1[:3], returned2[4]], placed)
-    placed, combine2 = put(2, [returned1[3], returned2[0], returned2[1], returned3[0]], placed)
-    placed, combine3 = put(3, [returned2[3], returned1[4], returned2[2], returned3[1]], placed)
+    placed, combine1 = put(1, [*returned1[:3], returned2[0]], placed)
+    placed, combine2 = put(2, [returned1[3], returned1[4], returned2[1], returned3[0]], placed)
+    placed, combine3 = put(3, [returned2[2], returned1[5], returned2[3], returned3[1]], placed)
     combines = [combine0, around(combine1, -1), around(combine2, -2), around(combine3, 1)]
     route_grad = 0.0
     expert_ids = jnp.arange(experts, dtype=routes.dtype)
@@ -472,7 +441,8 @@
     hidden_grad = jnp.transpose(placed[:, :, :most], (1, 0, 2, 3)).reshape(saved_hidden.shape)
     route_grad = ROUTE_SCALE * route_grad.T
     affinity_grad = (route_grad - jnp.sum(route_grad * shares, axis=-1, keepdims=True)) / totals
-    down_grad = late_grad(core.reshape(1), late_scatters, late, before, partner, experts, 896)
+    scatters = [scatter0, scatter1, scatter2, scatter3]
+    down_grad = half_grad(mine, scatters, first + late, [partner, later], experts, 896, True)
     return (affinity_grad, hidden_grad, down_grad)
 
 

time: 247 us -> 226 us (0.915)
  Pallas kernels: 86.9 us -> 77 us
  waiting for transfers between devices: 56.5 us -> 50.1 us
  local copies, waits for them, and re-layouts: 40.1 us -> 37 us
    ppermute x13 -> x12, waiting for transfers between devices: 16.4 us -> 9.31 us  [around(): lax.ppermute(array, 'exp', [(i, (i + shift) % sources) for i in range(sou...]
    pallas_call x4, Pallas kernels: 47.6 us -> 42.6 us  [project(): pl.pallas_call(functools.partial(project_kernel, top_k, sizes, len(items)...]
    pallas_call x3, Pallas kernels: 33.2 us -> 28.4 us  [half_grad(): pl.pallas_call(functools.partial(half_grad_kernel, len(scatters), len(arr...]
    slice x6 -> x0, local copies, waits for them, and re-layouts: 4.05 us -> none  [the longest x2 2.24 us: on_device_tokens(): top1, bottom1 = (across(x1[:half], 4), across(y1[half:], 2))]
    ppermute x29 -> x27, starting transfers between devices: 32.6 us -> 28.8 us  [across(): return lax.ppermute(array, 'rep', [(i, i ^ bits) for i in range(reps)])]
    ppermute x13 -> x12, starting transfers between devices: 22.8 us -> 25.4 us  [around(): lax.ppermute(array, 'exp', [(i, (i + shift) % sources) for i in range(sou...]
    unnamed x149 -> x131, local copies, waits for them, and re-layouts: 21.2 us -> 22.1 us
    ppermute x29 -> x27, waiting for transfers between devices: 40.1 us -> 40.8 us  [across(): return lax.ppermute(array, 'rep', [(i, i ^ bits) for i in range(reps)])]
  transfers between devices with their start and end apart: 42 -> 39, of which waited for: 10 -> 12; matrix products, arithmetic and copies ran while one was open for 11% -> 10% of each run, Pallas kernels for 24% -> 28%
where the time goes in v7:
time: 226 us; the launch traced here: 225 us
  Pallas kernels  77 us (34%)
  starting transfers between devices  54.2 us (24%)
  waiting for transfers between devices  50.1 us (22%)
  local copies, waits for them, and re-layouts  37 us (16%)
  other arithmetic  5.18 us (2%)
    pallas_call x4, Pallas kernels, project(): pl.pallas_call(functools.partial(project_kernel, top_k, sizes, len(items)...  42.6 us
    ppermute x27, waiting for transfers between devices, across(): return lax.ppermute(array, 'rep', [(i, i ^ bits) for i in range(reps)])  40.8 us
    ppermute x27, starting transfers between devices, across(): return lax.ppermute(array, 'rep', [(i, i ^ bits) for i in range(reps)])  28.8 us
    pallas_call x3, Pallas kernels, half_grad(): pl.pallas_call(functools.partial(half_grad_kernel, len(scatters), len(arr...  28.4 us
    ppermute x12, starting transfers between devices, around(): lax.ppermute(array, 'exp', [(i, (i + shift) % sources) for i in range(sou...  25.4 us
    unnamed x131, local copies, waits for them, and re-layouts  22.1 us
    ppermute x12, waiting for transfers between devices, around(): lax.ppermute(array, 'exp', [(i, (i + shift) % sources) for i in range(sou...  9.31 us
    reshape x2, local copies, waits for them, and re-layouts, on_device_tokens(): saved_hidden.reshape(experts, sources, most, 4, pair)  8.35 us
  transfers between devices with their start and end apart: 39, of which 12 were waited for; matrix products, arithmetic and copies ran while one was open for 10% of the time, Pallas kernels for 28%

profile of v7, /device:TPU:0, one launch (start us, length us, event | category | flops | bytes accessed | tf_op | source)
XLA Modules:
  0.0 224.8 jit_solution(12462960007733061555)
XLA Ops:
  0.6 3.1 %collective-permute-start.5 = (bf16[128,3584]{1,0:T(8,128)(2,1)}, bf16[128,3584]{1,0:T(8,128)(2,1)S(1)}, u32[]{:S(2)}, u32[]{:S(2)}) collective-permute-start(bf16[128,3584]{1,0:T(8,128)(2,1)} %refs_6_.1), channel_id=1, source_target_pairs={{0,1},{1,2},{2,3},{3,0},{4,5},{5,6},{6,7},{7,4},{8,9},{9,10},{10,1... | collective-permute-start | bytes 2752520 | tf_op jit(solution)/shard_map/ppermute | solution.py:354
  3.7 1.5 collective-permute-start.4
  5.2 1.5 collective-permute-start.3
  8.8 2.7 %collective-permute-start.1 = (bf16[4,256]{1,0:T(4,128)(2,1)S(1)}, bf16[4,256]{1,0:T(4,128)(2,1)S(1)}, u32[]{:S(2)}, u32[]{:S(2)}) collective-permute-start(bf16[4,256]{1,0:T(4,128)(2,1)S(1)} %pad_maximum_fusion.5), channel_id=1, source_target_pairs={{0,2},{1,3},{2,0},{3,1},{4,6},{5,7},{6,4},{7,5},{8,10},{9,11},{10,... | collective-permute-start | bytes 6152 | tf_op jit(solution)/shard_map/ppermute | solution.py:354
  11.7 4.8 %reshape.87 = bf16[4,4,60,4,256]{4,3,1,2,0:T(4,128)(2,1)} reshape(bf16[1,4,4,60,1024]{4,2,3,1,0:T(4,128)(2,1)} %param.8) | data formatting | bytes 3932160 | tf_op jit(solution)/shard_map/reshape | solution.py:377
  16.5 3.6 %copy.18 = bf16[4,4,60,4,256]{4,2,1,0,3:T(8,128)(2,1)} copy(bf16[4,4,60,4,256]{4,3,1,2,0:T(4,128)(2,1)} %reshape.87) | data formatting | bytes 3932160 | tf_op jit(solution)/shard_map/reshape | solution.py:377
  20.0 2.9 %dynamic-slice_bitcast_fusion = (bf16[4,4,60,256]{3,2,1,0:T(8,128)(2,1)S(1)}, bf16[4,4,60,256]{3,2,1,0:T(8,128)(2,1)}, bf16[4,4,60,256]{3,2,1,0:T(8,128)(2,1)}, bf16[4,4,60,256]{3,2,1,0:T(8,128)(2,1)}) fusion(bf16[4,4,4,60,256]{4,3,2,1,0:T(8,128)(2,1)} %bitcast.48, s32[]{:T(128)S(6)} %select_n.53, s32[]{:T(128)S(6)} %select_n.52, s32[]{:T(128)S(6)} %select_n.51, ...), kind=kLoop, calls=%fused_computation.7 | loop fusion | bytes 3932176 | tf_op jit(solution)/shard_map/jit(dynamic_index_in_dim)/squeeze | solution.py:379
  22.9 2.4 %copy.15 = bf16[4,128,3584]{2,1,0:T(8,128)(2,1)} copy(bf16[4,128,3584]{2,0,1:T(4,128)(2,1)S(1)} %bitcast.49) | data formatting | bytes 7340032 | tf_op jit(solution)/shard_map/transpose | solution.py:380
  25.4 3.6 %collective-permute-start.2 = (bf16[4,256]{1,0:T(4,128)(2,1)S(1)}, bf16[4,256]{1,0:T(4,128)(2,1)S(1)}, u32[]{:S(2)}, u32[]{:S(2)}) collective-permute-start(bf16[4,256]{1,0:T(4,128)(2,1)S(1)} %pad_maximum_fusion.5), channel_id=1, source_target_pairs={{0,3},{1,0},{2,1},{3,2},{4,7},{5,4},{6,5},{7,6},{8,11},{9,8},{10,9... | collective-permute-start | bytes 6152 | tf_op jit(solution)/shard_map/ppermute | solution.py:354
  29.0 1.3 collective-permute-done.2
  31.1 1.7 pad_maximum_fusion
  32.8 1.7 collective-permute-start.8
  35.0 1.4 collective-permute-start.7
  36.3 4.1 %collective-permute-start.12 = (bf16[128,3584]{1,0:T(8,128)(2,1)S(1)}, bf16[128,3584]{1,0:T(8,128)(2,1)S(1)}, u32[]{:S(2)}, u32[]{:S(2)}) collective-permute-start(bf16[128,3584]{1,0:T(8,128)(2,1)S(1)} %copy-done.11), channel_id=1, source_target_pairs={{0,3},{1,0},{2,1},{3,2},{4,7},{5,4},{6,5},{7,6},{8,11},{9,8},{10,9... | collective-permute-start | bytes 2752520 | tf_op jit(solution)/shard_map/ppermute | solution.py:354
  40.4 8.1 %collective-permute-done.8.refs_9_.refs_6_.refs_4_.refs_5_ = bf16[4,4,64,256]{3,2,1,0:T(8,128)(2,1)S(1)} collective-permute-done((bf16[4,4,64,256]{3,2,1,0:T(8,128)(2,1)S(1)}, bf16[4,4,64,256]{3,2,1,0:T(8,128)(2,1)S(1)}, u32[]{:S(2)}, u32[]{:S(2)}) %collective-permute-start.8) | collective-permute-done | bytes 524320 | tf_op jit(solution)/shard_map/ppermute | solution.py:351
  50.0 8.5 %collective-permute-done.6.refs_7_.refs_9_.refs_12_.refs_13_ = bf16[4,4,64,256]{3,2,1,0:T(8,128)(2,1)S(1)} collective-permute-done((bf16[4,4,64,256]{3,2,1,0:T(8,128)(2,1)S(1)}, bf16[4,4,64,256]{3,2,1,0:T(8,128)(2,1)S(1)}, u32[]{:S(2)}, u32[]{:S(2)}) %collective-permute-start.6) | collective-permute-done | bytes 524320 | tf_op jit(solution)/shard_map/ppermute | solution.py:351
  61.3 1.5 collective-permute-start.10
  62.8 16.2 %collective-permute-done.9.refs_3_.refs_5_.refs_9_ = bf16[128,3584]{1,0:T(8,128)(2,1)S(1)} collective-permute-done((bf16[128,3584]{1,0:T(8,128)(2,1)}, bf16[128,3584]{1,0:T(8,128)(2,1)S(1)}, u32[]{:S(2)}, u32[]{:S(2)}) %collective-permute-start.9) | collective-permute-done | bytes 917536 | tf_op jit(solution)/shard_map/ppermute | solution.py:351
  79.9 3.8 %collective-permute-done.11.refs_3_.refs_9_.refs_13_ = bf16[128,3584]{1,0:T(8,128)(2,1)} collective-permute-done((bf16[128,3584]{1,0:T(8,128)(2,1)S(1)}, bf16[128,3584]{1,0:T(8,128)(2,1)}, u32[]{:S(2)}, u32[]{:S(2)}) %collective-permute-start.11) | collective-permute-done | bytes 917536 | tf_op jit(solution)/shard_map/ppermute | solution.py:354
  84.7 1.5 collective-permute-start.15
  86.7 2.9 %collective-permute-start.16 = (bf16[128,3584]{1,0:T(8,128)(2,1)}, bf16[128,3584]{1,0:T(8,128)(2,1)}, u32[]{:S(2)}, u32[]{:S(2)}) collective-permute-start(bf16[128,3584]{1,0:T(8,128)(2,1)} %collective-permute-done.3.refs_1_.refs_3_.refs_7_), channel_id=1, source_target_pairs={{0,3},{1,0},{2,1},{3,2},{4,7},{5,4},{6,5},{7,6},{8,11},{9,8},{10,9... | collective-permute-start | bytes 2752520 | tf_op jit(solution)/shard_map/ppermute | solution.py:354
  94.0 10.8 %shard_map.76 = (bf16[4,64,256]{2,1,0:T(8,128)(2,1)S(1)}, bf16[4,64,256]{2,1,0:T(8,128)(2,1)S(1)}, bf16[4,64,256]{2,1,0:T(8,128)(2,1)S(1)}, bf16[4,64,256]{2,1,0:T(8,128)(2,1)S(1)}, bf16[2,512,512]{2,1,0:T(8,128)(2,1)S(1)}) custom-call(s32[6]{0:T(128)S(1)} %stack.92.idx_ref, bf16[128,3584]{1,0:T(8,128)(2,1)S(1)} %copy-done.11, ...), custom_call_target="tpu_custom_call" | custom-call | flops 7516192768 | bytes 11010048 | tf_op jit(solution)/shard_map/pallas_call | solution.py:180
  104.8 1.6 collective-permute-done.15.refs_4_.refs_10_.refs_14_
  108.2 4.3 %collective-permute-start.19 = (bf16[128,3584]{1,0:T(8,128)(2,1)}, bf16[128,3584]{1,0:T(8,128)(2,1)S(1)}, u32[]{:S(2)}, u32[]{:S(2)}) collective-permute-start(bf16[128,3584]{1,0:T(8,128)(2,1)} %collective-permute-done.4.refs_2_.refs_4_.refs_8_), channel_id=1, source_target_pairs={{0,3},{1,0},{2,1},{3,2},{4,7},{5,4},{6,5},{7,6},{8,11},{9,8},{10,9... | collective-permute-start | bytes 2752520 | tf_op jit(solution)/shard_map/ppermute | solution.py:354
  114.4 14.5 %shard_map.77 = (bf16[4,64,256]{2,1,0:T(8,128)(2,1)S(1)}, bf16[4,64,256]{2,1,0:T(8,128)(2,1)S(1)}, bf16[4,64,256]{2,1,0:T(8,128)(2,1)S(1)}, bf16[4,64,256]{2,1,0...) custom-call(s32[6]{0:T(128)S(1)} %stack.92.idx_ref, ...), custom_call_target="tpu_custom_call" | custom-call | flops 11274289152 | bytes 12845056 | tf_op jit(solution)/shard_map/pallas_call | solution.py:180
  130.1 3.0 %collective-permute-done.17.refs_0_.refs_2_.refs_16_ = bf16[128,3584]{1,0:T(8,128)(2,1)S(1)} collective-permute-done((bf16[128,3584]{1,0:T(8,128)(2,1)}, bf16[128,3584]{1,0:T(8,128)(2,1)S(1)}, u32[]{:S(2)}, u32[]{:S(2)}) %collective-permute-start.17) | collective-permute-done | bytes 917536 | tf_op jit(solution)/shard_map/ppermute | solution.py:351
  133.1 1.7 collective-permute-start.22
  135.2 1.5 collective-permute-start.24
  136.7 1.6 collective-permute-start.20
  138.7 10.3 %shard_map.78 = (bf16[4,64,256]{2,1,0:T(8,128)(2,1)}, bf16[4,64,256]{2,1,0:T(8,128)(2,1)S(1)}, bf16[4,64,256]{2,1,0:T(8,128)(2,1)S(1)}, bf16[4,64,256]{2,1,0:T(8,128)(2,1)S(1)}, bf16[2,512,512]{2,1,0:T(8,128)(2,1)S(1)}) custom-call(s32[6]{0:T(128)S(1)} %stack.92.idx_ref, bf16[128,3584]{1,0:T(8,128)(2,1)S(1)} %collective-permute-done.17.refs_0_.refs_2_.refs_16_, ...), custom_call_target="tpu_custom_call" | custom-call | flops 7516192768 | bytes 11010048 | tf_op jit(solution)/shard_map/pallas_call | solution.py:180
  149.7 8.3 %shard_map.79 = bf16[512,3584]{1,0:T(8,128)(2,1)S(1)} custom-call(s32[1]{0:T(128)} %bitcast.25.idx_ref, bf16[2,512,512]{2,1,0:T(8,128)(2,1)S(1)} %get-tuple-element.187.refs_0_, bf16[2,512,768]{2,1,0:T(8,128)(2,1)S(1)} %get-tuple-element.188.refs_1_, bf16[128,3584]{1,0:T(8,128)(2,1)S(1)} %copy-done.12, ...), custom_call_target="tpu_custom_call" | custom-call | flops 4697620480 | bytes 17825792 | tf_op jit(solution)/shard_map/pallas_call | solution.py:272
  158.2 1.3 collective-permute-start.26
  160.2 1.4 collective-permute-start.28
  162.2 7.1 %shard_map.81 = (bf16[4,64,256]{2,1,0:T(8,128)(2,1)S(1)}, bf16[4,64,256]{2,1,0:T(8,128)(2,1)S(1)}, bf16[2,512,256]{2,1,0:T(8,128)(2,1)S(1)}) custom-call(s32[6]{0:T(128)S(1)} %stack.92.idx_ref, bf16[128,3584]{1,0:T(8,128)(2,1)S(1)} %collective-permute-done.20.refs_0_.refs_6_.refs_20_, bf16[128,3584]{1,0:T(8,128)(2,1)S(1)} %collective-permute-done.21.refs_1_.refs_7_.refs_21_, ...), custom_call_target="tpu_custom_call" | custom-call | flops 3758096384 | bytes 9175040 | tf_op jit(solution)/shard_map/pallas_call | solution.py:180
  169.4 5.5 %shard_map.82 = bf16[512,3584]{1,0:T(8,128)(2,1)} custom-call(s32[1]{0:T(128)} %bitcast.25.idx_ref, bf16[2,512,512]{2,1,0:T(8,128)(2,1)S(1)} %get-tuple-element.207.refs_0_.refs_2_, bf16[2,512,256]{2,1,0:T(8,128)(2,1)S(1)} %get-tuple-element.232.refs_1_.refs_3_, bf16[128,3584]{1,0:T(8,128)(2,1)S(1)} %collective-permute-done.17.refs_0_.refs_2_.refs_16_, ...), custom_call_target="tpu_custom_call" | custom-call | flops 2818572288 | bytes 13631488 | tf_op jit(solution)/shard_map/pallas_call | solution.py:272
  177.5 1.8 copy-done.57
  179.4 1.6 collective-permute-start.30
  180.9 1.2 collective-permute-start.32
  183.0 1.3 collective-permute-start.33
  184.3 2.3 %collective-permute-done.30.refs_3_ = bf16[4,64,256]{2,1,0:T(8,128)(2,1)} collective-permute-done((bf16[4,64,256]{2,1,0:T(8,128)(2,1)}, bf16[4,64,256]{2,1,0:T(8,128)(2,1)}, u32[]{:S(2)}, u32[]{:S(2)}) %collective-permute-start.30) | collective-permute-done | bytes 131104 | tf_op jit(solution)/shard_map/ppermute | solution.py:351
  186.6 1.9 collective-permute-start.36
  195.6 1.7 shard_map.83
  197.3 1.9 collective-permute-start.31
  199.3 1.8 shard_map.84
  202.2 1.8 shard_map.85
  204.4 2.8 %copy.16 = bf16[1,4,4,60,1024]{4,2,3,1,0:T(4,128)(2,1)} copy(bf16[1,4,4,60,1024]{4,3,1,2,0:T(8,128)(2,1)S(1)} %slice_bitcast_fusion) | data formatting | bytes 3932160
  207.2 2.2 collective-permute-done.37
  210.2 14.6 %shard_map.86 = f32[128,4,3584]{2,1,0:T(4,128)} custom-call(s32[1]{0:T(128)} %bitcast.24.idx_ref, bf16[2,512,512]{2,1,0:T(8,128)(2,1)S(1)} %copy-done.10, bf16[2,512,768]{2,1,0:T(8,128)(2,1)} %copy-done.8, bf16[2,512,512]{2,1,0:T(8,128)(2,1)S(1)} %get-tuple-element.207.refs_0_.refs_2_, bf16[2,512,256]{2,1,0:T(8,128)(2,1)S(1)} %get-tuple-element.232.refs_1_.refs_3_, ...), custom_call_target="tpu_custom_call" | custom-call | flops 7516192768 | bytes 24117248 | tf_op jit(solution)/shard_map/pallas_call | solution.py:272
  (199 shorter events, 35.1 us)
Async XLA Ops:
  0.6 29.6 %collective-permute-start.5 = (bf16[128,3584]{1,0:T(8,128)(2,1)}, bf16[128,3584]{1,0:T(8,128)(2,1)S(1)}, u32[]{:S(2)}, u32[]{:S(2)}) collective-permute-start(bf16[128,3584]{1,0:T(8,128)(2,1)} %refs_6_.1), channel_id=1, source_target_pairs={{0,1},{1,2},{2,3},{3,0},{4,5},{5,6},{6,7},{7,4},{8,9},{9,10},{10,1... | collective-permute-start | bytes 2752520 | tf_op jit(solution)/shard_map/ppermute | solution.py:354
  3.7 26.6 %collective-permute-start.4 = (bf16[128,3584]{1,0:T(8,128)(2,1)}, bf16[128,3584]{1,0:T(8,128)(2,1)}, u32[]{:S(2)}, u32[]{:S(2)}) collective-permute-start(bf16[128,3584]{1,0:T(8,128)(2,1)} %refs_6_.1), channel_id=1, source_target_pairs={{0,16},{4,20},{8,24},{12,28},{16,0},{20,4},{24,8},{28,12},{1,17},{... | collective-permute-start | bytes 2752520 | tf_op jit(solution)/shard_map/ppermute | solution.py:351
  5.2 25.1 %collective-permute-start.3 = (bf16[128,3584]{1,0:T(8,128)(2,1)}, bf16[128,3584]{1,0:T(8,128)(2,1)}, u32[]{:S(2)}, u32[]{:S(2)}) collective-permute-start(bf16[128,3584]{1,0:T(8,128)(2,1)} %refs_6_.1), channel_id=1, source_target_pairs={{0,8},{4,12},{8,0},{12,4},{16,24},{20,28},{24,16},{28,20},{1,9},{5... | collective-permute-start | bytes 2752520 | tf_op jit(solution)/shard_map/ppermute | solution.py:351
  8.8 16.6 %collective-permute-start.1 = (bf16[4,256]{1,0:T(4,128)(2,1)S(1)}, bf16[4,256]{1,0:T(4,128)(2,1)S(1)}, u32[]{:S(2)}, u32[]{:S(2)}) collective-permute-start(bf16[4,256]{1,0:T(4,128)(2,1)S(1)} %pad_maximum_fusion.5), channel_id=1, source_target_pairs={{0,2},{1,3},{2,0},{3,1},{4,6},{5,7},{6,4},{7,5},{8,10},{9,11},{10,... | collective-permute-start | bytes 6152 | tf_op jit(solution)/shard_map/ppermute | solution.py:354
  11.5 17.5 %collective-permute-start = (bf16[4,256]{1,0:T(4,128)(2,1)S(1)}, bf16[4,256]{1,0:T(4,128)(2,1)S(1)}, u32[]{:S(2)}, u32[]{:S(2)}) collective-permute-start(bf16[4,256]{1,0:T(4,128)(2,1)S(1)} %pad_maximum_fusion.5), channel_id=1, source_target_pairs={{0,1},{1,2},{2,3},{3,0},{4,5},{5,6},{6,7},{7,4},{8,9},{9,10},{10,1... | collective-permute-start | bytes 6152 | tf_op jit(solution)/shard_map/ppermute | solution.py:354
  25.4 4.9 %collective-permute-start.2 = (bf16[4,256]{1,0:T(4,128)(2,1)S(1)}, bf16[4,256]{1,0:T(4,128)(2,1)S(1)}, u32[]{:S(2)}, u32[]{:S(2)}) collective-permute-start(bf16[4,256]{1,0:T(4,128)(2,1)S(1)} %pad_maximum_fusion.5), channel_id=1, source_target_pairs={{0,3},{1,0},{2,1},{3,2},{4,7},{5,4},{6,5},{7,6},{8,11},{9,8},{10,9... | collective-permute-start | bytes 6152 | tf_op jit(solution)/shard_map/ppermute | solution.py:354
  30.3 55.9 %copy-start.14 = (bf16[128,3584]{1,0:T(8,128)(2,1)}, bf16[128,3584]{1,0:T(8,128)(2,1)S(1)}, u32[]{:S(2)}) copy-start(bf16[128,3584]{1,0:T(8,128)(2,1)S(1)} %collective-permute-done.5.refs_0_.refs_6_.refs_10_) | copy-start | bytes 2752516
  30.3 54.4 %collective-permute-start.13 = (bf16[512,3584]{1,0:T(8,128)(2,1)}, bf16[512,3584]{1,0:T(8,128)(2,1)}, u32[]{:S(2)}, u32[]{:S(2)}) collective-permute-start(bf16[512,3584]{1,0:T(8,128)(2,1)} %bitcast.14.refs_4_.refs_6_.refs_2_), channel_id=1, source_target_pairs={{0,4},{4,0},{8,12},{12,8},{16,20},{20,16},{24,28},{28,24},{1,5},{5... | collective-permute-start | bytes 11010056 | tf_op jit(solution)/shard_map/ppermute | solution.py:351
  32.8 15.7 %collective-permute-start.8 = (bf16[4,4,64,256]{3,2,1,0:T(8,128)(2,1)S(1)}, bf16[4,4,64,256]{3,2,1,0:T(8,128)(2,1)S(1)}, u32[]{:S(2)}, u32[]{:S(2)}) collective-permute-start(bf16[4,4,64,256]{3,2,1,0:T(8,128)(2,1)S(1)} %get-tuple-element.251), channel_id=1, source_target_pairs={{0,24},{4,28},{8,16},{12,20},{16,8},{20,12},{24,0},{28,4},{1,25},{... | collective-permute-start | bytes 1572872 | tf_op jit(solution)/shard_map/ppermute | solution.py:351
  34.5 24.1 %collective-permute-start.6 = (bf16[4,4,64,256]{3,2,1,0:T(8,128)(2,1)S(1)}, bf16[4,4,64,256]{3,2,1,0:T(8,128)(2,1)S(1)}, u32[]{:S(2)}, u32[]{:S(2)}) collective-permute-start(bf16[4,4,64,256]{3,2,1,0:T(8,128)(2,1)S(1)} %get-tuple-element.252), channel_id=1, source_target_pairs={{0,8},{4,12},{8,0},{12,4},{16,24},{20,28},{24,16},{28,20},{1,9},{5... | collective-permute-start | bytes 1572872 | tf_op jit(solution)/shard_map/ppermute | solution.py:351
  35.0 25.5 %collective-permute-start.7 = (bf16[4,4,64,256]{3,2,1,0:T(8,128)(2,1)S(1)}, bf16[4,4,64,256]{3,2,1,0:T(8,128)(2,1)S(1)}, u32[]{:S(2)}, u32[]{:S(2)}) collective-permute-start(bf16[4,4,64,256]{3,2,1,0:T(8,128)(2,1)S(1)} %get-tuple-element.253), channel_id=1, source_target_pairs={{0,16},{4,20},{8,24},{12,28},{16,0},{20,4},{24,8},{28,12},{1,17},{... | collective-permute-start | bytes 1572872 | tf_op jit(solution)/shard_map/ppermute | solution.py:351
  36.3 26.4 %collective-permute-start.12 = (bf16[128,3584]{1,0:T(8,128)(2,1)S(1)}, bf16[128,3584]{1,0:T(8,128)(2,1)S(1)}, u32[]{:S(2)}, u32[]{:S(2)}) collective-permute-start(bf16[128,3584]{1,0:T(8,128)(2,1)S(1)} %copy-done.11), channel_id=1, source_target_pairs={{0,3},{1,0},{2,1},{3,2},{4,7},{5,4},{6,5},{7,6},{8,11},{9,8},{10,9... | collective-permute-start | bytes 2752520 | tf_op jit(solution)/shard_map/ppermute | solution.py:354
  49.3 29.6 %collective-permute-start.9 = (bf16[128,3584]{1,0:T(8,128)(2,1)}, bf16[128,3584]{1,0:T(8,128)(2,1)S(1)}, u32[]{:S(2)}, u32[]{:S(2)}) collective-permute-start(bf16[128,3584]{1,0:T(8,128)(2,1)} %collective-permute-done.3.refs_1_.refs_3_.refs_7_), channel_id=1, source_target_pairs={{0,16},{4,20},{8,24},{12,28},{16,0},{20,4},{24,8},{28,12},{1,17},{... | collective-permute-start | bytes 2752520 | tf_op jit(solution)/shard_map/ppermute | solution.py:351
  59.4 24.4 %collective-permute-start.11 = (bf16[128,3584]{1,0:T(8,128)(2,1)S(1)}, bf16[128,3584]{1,0:T(8,128)(2,1)}, u32[]{:S(2)}, u32[]{:S(2)}) collective-permute-start(bf16[128,3584]{1,0:T(8,128)(2,1)S(1)} %collective-permute-done.5.refs_0_.refs_6_.refs_10_), channel_id=1, source_target_pairs={{0,1},{1,2},{2,3},{3,0},{4,5},{5,6},{6,7},{7,4},{8,9},{9,10},{10,1... | collective-permute-start | bytes 2752520 | tf_op jit(solution)/shard_map/ppermute | solution.py:354
  61.3 22.5 %collective-permute-start.10 = (bf16[128,3584]{1,0:T(8,128)(2,1)S(1)}, bf16[128,3584]{1,0:T(8,128)(2,1)S(1)}, u32[]{:S(2)}, u32[]{:S(2)}) collective-permute-start(bf16[128,3584]{1,0:T(8,128)(2,1)S(1)} %collective-permute-done.5.refs_0_.refs_6_.refs_10_), channel_id=1, source_target_pairs={{0,8},{4,12},{8,0},{12,4},{16,24},{20,28},{24,16},{28,20},{1,9},{5... | collective-permute-start | bytes 2752520 | tf_op jit(solution)/shard_map/ppermute | solution.py:351
  84.7 21.7 %collective-permute-start.15 = (bf16[128,3584]{1,0:T(8,128)(2,1)}, bf16[128,3584]{1,0:T(8,128)(2,1)}, u32[]{:S(2)}, u32[]{:S(2)}) collective-permute-start(bf16[128,3584]{1,0:T(8,128)(2,1)} %collective-permute-done.11.refs_3_.refs_9_.refs_13_), channel_id=1, source_target_pairs={{0,8},{4,12},{8,0},{12,4},{16,24},{20,28},{24,16},{28,20},{1,9},{5... | collective-permute-start | bytes 2752520 | tf_op jit(solution)/shard_map/ppermute | solution.py:351
  86.2 21.2 %collective-permute-start.14 = (bf16[128,3584]{1,0:T(8,128)(2,1)S(1)}, bf16[128,3584]{1,0:T(8,128)(2,1)}, u32[]{:S(2)}, u32[]{:S(2)}) collective-permute-start(bf16[128,3584]{1,0:T(8,128)(2,1)S(1)} %collective-permute-done.5.refs_0_.refs_6_.refs_10_), channel_id=1, source_target_pairs={{0,16},{4,20},{8,24},{12,28},{16,0},{20,4},{24,8},{28,12},{1,17},{... | collective-permute-start | bytes 2752520 | tf_op jit(solution)/shard_map/ppermute | solution.py:351
  86.7 21.5 %collective-permute-start.16 = (bf16[128,3584]{1,0:T(8,128)(2,1)}, bf16[128,3584]{1,0:T(8,128)(2,1)}, u32[]{:S(2)}, u32[]{:S(2)}) collective-permute-start(bf16[128,3584]{1,0:T(8,128)(2,1)} %collective-permute-done.3.refs_1_.refs_3_.refs_7_), channel_id=1, source_target_pairs={{0,3},{1,0},{2,1},{3,2},{4,7},{5,4},{6,5},{7,6},{8,11},{9,8},{10,9... | collective-permute-start | bytes 2752520 | tf_op jit(solution)/shard_map/ppermute | solution.py:354
  94.0 20.5 %copy-start.49 = (bf16[4,4,64,256]{3,2,1,0:T(8,128)(2,1)S(1)}, bf16[4,4,64,256]{3,2,1,0:T(8,128)(2,1)}, u32[]{:S(2)}) copy-start(bf16[4,4,64,256]{3,2,1,0:T(8,128)(2,1)} %copy-done.47) | copy-start | bytes 1572868
  94.0 20.5 %copy-start.52 = (bf16[4,4,64,256]{3,2,1,0:T(8,128)(2,1)S(1)}, bf16[4,4,64,256]{3,2,1,0:T(8,128)(2,1)}, u32[]{:S(2)}) copy-start(bf16[4,4,64,256]{3,2,1,0:T(8,128)(2,1)} %copy-done.50) | copy-start | bytes 1572868
  104.7 45.0 %copy-start.9 = (bf16[2,512,512]{2,1,0:T(8,128)(2,1)}, bf16[2,512,512]{2,1,0:T(8,128)(2,1)S(1)}, u32[]{:S(2)}) copy-start(bf16[2,512,512]{2,1,0:T(8,128)(2,1)S(1)} %get-tuple-element.187.refs_0_) | copy-start | bytes 3145732
  108.2 30.1 %copy-start.19 = (bf16[128,3584]{1,0:T(8,128)(2,1)S(1)}, bf16[128,3584]{1,0:T(8,128)(2,1)}, u32[]{:S(2)}) copy-start(bf16[128,3584]{1,0:T(8,128)(2,1)} %copy-done.17) | copy-start | bytes 2752516
  108.2 30.5 %copy-start.46 = (bf16[4,4,64,256]{3,2,1,0:T(8,128)(2,1)S(1)}, bf16[4,4,64,256]{3,2,1,0:T(8,128)(2,1)}, u32[]{:S(2)}) copy-start(bf16[4,4,64,256]{3,2,1,0:T(8,128)(2,1)} %copy-done.44) | copy-start | bytes 1572868
  108.2 21.9 %collective-permute-start.19 = (bf16[128,3584]{1,0:T(8,128)(2,1)}, bf16[128,3584]{1,0:T(8,128)(2,1)S(1)}, u32[]{:S(2)}, u32[]{:S(2)}) collective-permute-start(bf16[128,3584]{1,0:T(8,128)(2,1)} %collective-permute-done.4.refs_2_.refs_4_.refs_8_), channel_id=1, source_target_pairs={{0,3},{1,0},{2,1},{3,2},{4,7},{5,4},{6,5},{7,6},{8,11},{9,8},{10,9... | collective-permute-start | bytes 2752520 | tf_op jit(solution)/shard_map/ppermute | solution.py:354
  112.4 20.6 %collective-permute-start.17 = (bf16[128,3584]{1,0:T(8,128)(2,1)}, bf16[128,3584]{1,0:T(8,128)(2,1)S(1)}, u32[]{:S(2)}, u32[]{:S(2)}) collective-permute-start(bf16[128,3584]{1,0:T(8,128)(2,1)} %collective-permute-done.14.refs_2_.refs_8_.refs_12_), channel_id=1, source_target_pairs={{0,8},{4,12},{8,0},{12,4},{16,24},{20,28},{24,16},{28,20},{1,9},{5... | collective-permute-start | bytes 2752520 | tf_op jit(solution)/shard_map/ppermute | solution.py:351
  113.2 19.9 %collective-permute-start.18 = (bf16[128,3584]{1,0:T(8,128)(2,1)}, bf16[128,3584]{1,0:T(8,128)(2,1)S(1)}, u32[]{:S(2)}, u32[]{:S(2)}) collective-permute-start(bf16[128,3584]{1,0:T(8,128)(2,1)} %collective-permute-done.11.refs_3_.refs_9_.refs_13_), channel_id=1, source_target_pairs={{0,16},{4,20},{8,24},{12,28},{16,0},{20,4},{24,8},{28,12},{1,17},{... | collective-permute-start | bytes 2752520 | tf_op jit(solution)/shard_map/ppermute | solution.py:351
  128.9 20.8 %copy-start.8 = (bf16[2,512,768]{2,1,0:T(8,128)(2,1)}, bf16[2,512,768]{2,1,0:T(8,128)(2,1)S(1)}, u32[]{:S(2)}) copy-start(bf16[2,512,768]{2,1,0:T(8,128)(2,1)S(1)} %get-tuple-element.188.refs_1_) | copy-start | bytes 4718596
  133.1 36.2 %copy-start = (bf16[128,3584]{1,0:T(8,128)(2,1)}, bf16[128,3584]{1,0:T(8,128)(2,1)S(1)}, u32[]{:S(2)}) copy-start(bf16[128,3584]{1,0:T(8,128)(2,1)S(1)} %collective-permute-done.17.refs_0_.refs_2_.refs_16_) | copy-start | bytes 2752516
  133.1 36.2 %copy-start.2 = (bf16[128,3584]{1,0:T(8,128)(2,1)}, bf16[128,3584]{1,0:T(8,128)(2,1)S(1)}, u32[]{:S(2)}) copy-start(bf16[128,3584]{1,0:T(8,128)(2,1)S(1)} %collective-permute-done.18.refs_1_.refs_3_.refs_17_) | copy-start | bytes 2752516
  133.1 24.9 %collective-permute-start.22 = (bf16[4,64,256]{2,1,0:T(8,128)(2,1)S(1)}, bf16[4,64,256]{2,1,0:T(8,128)(2,1)S(1)}, u32[]{:S(2)}, u32[]{:S(2)}) collective-permute-start(bf16[4,64,256]{2,1,0:T(8,128)(2,1)S(1)} %get-tuple-element.175), channel_id=1, source_target_pairs={{0,8},{4,12},{8,0},{12,4},{16,24},{20,28},{24,16},{28,20},{1,9},{5... | collective-permute-start | bytes 393224 | tf_op jit(solution)/shard_map/ppermute | solution.py:351
  134.8 23.2 %collective-permute-start.23 = (bf16[4,64,256]{2,1,0:T(8,128)(2,1)S(1)}, bf16[4,64,256]{2,1,0:T(8,128)(2,1)S(1)}, u32[]{:S(2)}, u32[]{:S(2)}) collective-permute-start(bf16[4,64,256]{2,1,0:T(8,128)(2,1)S(1)} %get-tuple-element.176), channel_id=1, source_target_pairs={{0,16},{4,20},{8,24},{12,28},{16,0},{20,4},{24,8},{28,12},{1,17},{... | collective-permute-start | bytes 393224 | tf_op jit(solution)/shard_map/ppermute | solution.py:351
  135.2 22.9 %collective-permute-start.24 = (bf16[4,64,256]{2,1,0:T(8,128)(2,1)S(1)}, bf16[4,64,256]{2,1,0:T(8,128)(2,1)S(1)}, u32[]{:S(2)}, u32[]{:S(2)}) collective-permute-start(bf16[4,64,256]{2,1,0:T(8,128)(2,1)S(1)} %get-tuple-element.177), channel_id=1, source_target_pairs={{0,24},{4,28},{8,16},{12,20},{16,8},{20,12},{24,0},{28,4},{1,25},{... | collective-permute-start | bytes 393224 | tf_op jit(solution)/shard_map/ppermute | solution.py:351
  136.7 21.4 %collective-permute-start.20 = (bf16[128,3584]{1,0:T(8,128)(2,1)}, bf16[128,3584]{1,0:T(8,128)(2,1)S(1)}, u32[]{:S(2)}, u32[]{:S(2)}) collective-permute-start(bf16[128,3584]{1,0:T(8,128)(2,1)} %collective-permute-done.15.refs_4_.refs_10_.refs_14_), channel_id=1, source_target_pairs={{0,16},{4,20},{8,24},{12,28},{16,0},{20,4},{24,8},{28,12},{1,17},{... | collective-permute-start | bytes 2752520 | tf_op jit(solution)/shard_map/ppermute | solution.py:351
  138.3 19.8 %collective-permute-start.21 = (bf16[128,3584]{1,0:T(8,128)(2,1)S(1)}, bf16[128,3584]{1,0:T(8,128)(2,1)S(1)}, u32[]{:S(2)}, u32[]{:S(2)}) collective-permute-start(bf16[128,3584]{1,0:T(8,128)(2,1)S(1)} %copy-done.19), channel_id=1, source_target_pairs={{0,3},{1,0},{2,1},{3,2},{4,7},{5,4},{6,5},{7,6},{8,11},{9,8},{10,9... | collective-permute-start | bytes 2752520 | tf_op jit(solution)/shard_map/ppermute | solution.py:354
  158.1 19.4 %collective-permute-start.25 = (bf16[512,3584]{1,0:T(8,128)(2,1)S(1)}, bf16[512,3584]{1,0:T(8,128)(2,1)S(1)}, u32[]{:S(2)}, u32[]{:S(2)}) collective-permute-start(bf16[512,3584]{1,0:T(8,128)(2,1)S(1)} %shard_map.79), channel_id=1, source_target_pairs={{0,4},{4,0},{8,12},{12,8},{16,20},{20,16},{24,28},{28,24},{1,5},{5... | collective-permute-start | bytes 11010056 | tf_op jit(solution)/shard_map/ppermute | solution.py:351
  158.2 16.7 %collective-permute-start.26 = (bf16[4,64,256]{2,1,0:T(8,128)(2,1)S(1)}, bf16[4,64,256]{2,1,0:T(8,128)(2,1)S(1)}, u32[]{:S(2)}, u32[]{:S(2)}) collective-permute-start(bf16[4,64,256]{2,1,0:T(8,128)(2,1)S(1)} %get-tuple-element.202), channel_id=1, source_target_pairs={{0,8},{4,12},{8,0},{12,4},{16,24},{20,28},{24,16},{28,20},{1,9},{5... | collective-permute-start | bytes 393224 | tf_op jit(solution)/shard_map/ppermute | solution.py:351
  159.6 16.0 %collective-permute-start.27 = (bf16[4,64,256]{2,1,0:T(8,128)(2,1)S(1)}, bf16[4,64,256]{2,1,0:T(8,128)(2,1)S(1)}, u32[]{:S(2)}, u32[]{:S(2)}) collective-permute-start(bf16[4,64,256]{2,1,0:T(8,128)(2,1)S(1)} %get-tuple-element.203), channel_id=1, source_target_pairs={{0,16},{4,20},{8,24},{12,28},{16,0},{20,4},{24,8},{28,12},{1,17},{... | collective-permute-start | bytes 393224 | tf_op jit(solution)/shard_map/ppermute | solution.py:351
  160.2 16.0 %collective-permute-start.28 = (bf16[4,64,256]{2,1,0:T(8,128)(2,1)S(1)}, bf16[4,64,256]{2,1,0:T(8,128)(2,1)S(1)}, u32[]{:S(2)}, u32[]{:S(2)}) collective-permute-start(bf16[4,64,256]{2,1,0:T(8,128)(2,1)S(1)} %get-tuple-element.205), channel_id=1, source_target_pairs={{0,8},{4,12},{8,0},{12,4},{16,24},{20,28},{24,16},{28,20},{1,9},{5... | collective-permute-start | bytes 393224 | tf_op jit(solution)/shard_map/ppermute | solution.py:351
  161.6 15.3 %collective-permute-start.29 = (bf16[4,64,256]{2,1,0:T(8,128)(2,1)S(1)}, bf16[4,64,256]{2,1,0:T(8,128)(2,1)S(1)}, u32[]{:S(2)}, u32[]{:S(2)}) collective-permute-start(bf16[4,64,256]{2,1,0:T(8,128)(2,1)S(1)} %get-tuple-element.206), channel_id=1, source_target_pairs={{0,8},{4,12},{8,0},{12,4},{16,24},{20,28},{24,16},{28,20},{1,9},{5... | collective-permute-start | bytes 393224 | tf_op jit(solution)/shard_map/ppermute | solution.py:351
  179.4 30.8 %collective-permute-start.38 = (bf16[512,3584]{1,0:T(8,128)(2,1)}, bf16[512,3584]{1,0:T(8,128)(2,1)}, u32[]{:S(2)}, u32[]{:S(2)}) collective-permute-start(bf16[512,3584]{1,0:T(8,128)(2,1)} %shard_map.82), channel_id=1, source_target_pairs={{0,4},{4,0},{8,12},{12,8},{16,20},{20,16},{24,28},{28,24},{1,5},{5... | collective-permute-start | bytes 11010056 | tf_op jit(solution)/shard_map/ppermute | solution.py:351
  179.4 7.2 %collective-permute-start.30 = (bf16[4,64,256]{2,1,0:T(8,128)(2,1)}, bf16[4,64,256]{2,1,0:T(8,128)(2,1)}, u32[]{:S(2)}, u32[]{:S(2)}) collective-permute-start(bf16[4,64,256]{2,1,0:T(8,128)(2,1)} %get-tuple-element.216), channel_id=1, source_target_pairs={{0,24},{4,28},{8,16},{12,20},{16,8},{20,12},{24,0},{28,4},{1,25},{... | collective-permute-start | bytes 393224 | tf_op jit(solution)/shard_map/ppermute | solution.py:351
  180.9 16.4 %collective-permute-start.32 = (bf16[4,64,256]{2,1,0:T(8,128)(2,1)}, bf16[4,64,256]{2,1,0:T(8,128)(2,1)}, u32[]{:S(2)}, u32[]{:S(2)}) collective-permute-start(bf16[4,64,256]{2,1,0:T(8,128)(2,1)} %copy-done.54), channel_id=1, source_target_pairs={{0,16},{4,20},{8,24},{12,28},{16,0},{20,4},{24,8},{28,12},{1,17},{... | collective-permute-start | bytes 393224 | tf_op jit(solution)/shard_map/ppermute | solution.py:351
  182.2 20.0 %collective-permute-start.35 = (bf16[4,64,256]{2,1,0:T(8,128)(2,1)}, bf16[4,64,256]{2,1,0:T(8,128)(2,1)}, u32[]{:S(2)}, u32[]{:S(2)}) collective-permute-start(bf16[4,64,256]{2,1,0:T(8,128)(2,1)} %copy-done.53), channel_id=1, source_target_pairs={{0,16},{4,20},{8,24},{12,28},{16,0},{20,4},{24,8},{28,12},{1,17},{... | collective-permute-start | bytes 393224 | tf_op jit(solution)/shard_map/ppermute | solution.py:351
  183.0 16.3 %collective-permute-start.33 = (bf16[4,64,256]{2,1,0:T(8,128)(2,1)}, bf16[4,64,256]{2,1,0:T(8,128)(2,1)}, u32[]{:S(2)}, u32[]{:S(2)}) collective-permute-start(bf16[4,64,256]{2,1,0:T(8,128)(2,1)} %copy-done.56), channel_id=1, source_target_pairs={{0,24},{4,28},{8,16},{12,20},{16,8},{20,12},{24,0},{28,4},{1,25},{... | collective-permute-start | bytes 393224 | tf_op jit(solution)/shard_map/ppermute | solution.py:351
  186.6 15.6 %collective-permute-start.36 = (bf16[4,64,256]{2,1,0:T(8,128)(2,1)}, bf16[4,64,256]{2,1,0:T(8,128)(2,1)}, u32[]{:S(2)}, u32[]{:S(2)}) collective-permute-start(bf16[4,64,256]{2,1,0:T(8,128)(2,1)} %copy-done.55), channel_id=1, source_target_pairs={{0,24},{4,28},{8,16},{12,20},{16,8},{20,12},{24,0},{28,4},{1,25},{... | collective-permute-start | bytes 393224 | tf_op jit(solution)/shard_map/ppermute | solution.py:351
  197.3 9.8 %collective-permute-start.31 = (f32[4,128]{1,0:T(4,128)S(1)}, f32[4,128]{1,0:T(4,128)S(1)}, u32[]{:S(2)}, u32[]{:S(2)}) collective-permute-start(f32[4,128]{1,0:T(4,128)S(1)} %get-tuple-element.218), channel_id=1, source_target_pairs={{0,3},{1,0},{2,1},{3,2},{4,7},{5,4},{6,5},{7,6},{8,11},{9,8},{10,9... | collective-permute-start | bytes 6152 | tf_op jit(solution)/shard_map/ppermute | solution.py:354
  201.0 6.1 %collective-permute-start.34 = (f32[4,128]{1,0:T(4,128)S(1)}, f32[4,128]{1,0:T(4,128)S(1)}, u32[]{:S(2)}, u32[]{:S(2)}) collective-permute-start(f32[4,128]{1,0:T(4,128)S(1)} %get-tuple-element.224), channel_id=1, source_target_pairs={{0,2},{1,3},{2,0},{3,1},{4,6},{5,7},{6,4},{7,5},{8,10},{9,11},{10,... | collective-permute-start | bytes 6152 | tf_op jit(solution)/shard_map/ppermute | solution.py:354
  204.0 5.4 %collective-permute-start.37 = (f32[4,128]{1,0:T(4,128)S(1)}, f32[4,128]{1,0:T(4,128)S(1)}, u32[]{:S(2)}, u32[]{:S(2)}) collective-permute-start(f32[4,128]{1,0:T(4,128)S(1)} %get-tuple-element.230), channel_id=1, source_target_pairs={{0,1},{1,2},{2,3},{3,0},{4,5},{5,6},{6,7},{7,4},{8,9},{9,10},{10,1... | collective-permute-start | bytes 6152 | tf_op jit(solution)/shard_map/ppermute | solution.py:354
  (56 other events, 333.2 us)

commit v8 on v7

--- a/solution.py
+++ b/solution.py
@@ -86,7 +86,7 @@
 
 def project_kernel(top_k, sizes, items, idx_ref, *refs):
     parts = len(sizes)
-    pieces, (own_weight, partner_weight) = refs[:parts], refs[parts : parts + 2]
+    pieces, weight_refs = refs[:parts], refs[parts : parts + 2]
     hidden_refs = refs[parts + 2 : parts + 2 + items]
     grad_refs = refs[parts + 2 + items : parts + 2 + 2 * items]
     scatter_ref, rows, weight, terms, slot_ref, scale_ref, sems = refs[parts + 2 + 2 * items :]
@@ -95,7 +95,6 @@
     block = pair // 2
     tokens = rows.shape[0] // items
     experts = slot_ref.shape[0]
-    core = idx_ref[5]
 
     @pl.when(step == 0)
     def _():
@@ -133,10 +132,9 @@
             copy.wait()
 
     for q in range(group):
-        to = pl.multiple_of(q * pair + core * block, block)
-        weight[pl.ds(to, block), :] = own_weight[q * block : (q + 1) * block]
-        to = pl.multiple_of(q * pair + (1 - core) * block, block)
-        weight[pl.ds(to, block), :] = partner_weight[q * block : (q + 1) * block]
+        for c in range(2):
+            at = q * pair + c * block
+            weight[at : at + block, :] = weight_refs[c][0, q * block : (q + 1) * block]
     projected = nt_dot(weight[...], rows[...])
     slot_ids = lax.broadcasted_iota(jnp.int32, (slots, tokens), 0).astype(F32)
     slot_rows = lax.broadcasted_iota(jnp.int32, (slots, pair), 0)
@@ -170,9 +168,9 @@
             scatter_ref[half] = jnp.dot(order, terms[half], preferred_element_type=F32).astype(BF16)
 
 
-def project(index, items, own_weight, partner_weight, hidden, top_k, group=2):
+def project(index, items, weights, hidden, top_k, group=2):
     experts, sources, slots, pair = hidden[0].shape
-    width = own_weight.shape[1]
+    width = weights.shape[2]
     pieces = [piece for rows, _, _ in items for piece in rows]
     sizes = [p.shape[0] for p in pieces]
     count = sum(sizes)
@@ -183,7 +181,7 @@
             num_scalar_prefetch=1,
             grid=(experts // group,),
             in_specs=[pl.BlockSpec(memory_space=pl.ANY)] * len(sizes)
-            + [pl.BlockSpec((group * block, width), lambda e, idx: (e, 0))] * 2
+            + [pl.BlockSpec((1, group * block, width), lambda e, idx, c=c: (c, e, 0)) for c in range(2)]
             + [
                 pl.BlockSpec((group, 1, slots, pair), lambda e, idx, k=k: (e, idx[k], 0, 0))
                 for _, _, k in items
@@ -204,10 +202,10 @@
         compiler_params=pltpu.CompilerParams(vmem_limit_bytes=VMEM_BYTES),
         cost_estimate=pl.CostEstimate(
             flops=4 * count * width * experts * pair,
-            bytes_accessed=2 * (count * width + 2 * own_weight.size),
+            bytes_accessed=2 * (count * width + weights.size),
             transcendentals=0,
         ),
-    )(index, *pieces, own_weight, partner_weight, *[hidden[m] for _, m, _ in items])
+    )(index, *pieces, weights, weights, *[hidden[m] for _, m, _ in items])
 
 
 def fill_rows(pieces, rows):
@@ -288,52 +286,59 @@
     )(index, *scatters, *arrived, *pieces)
 
 
-def place_kernel(top_k, first, idx_ref, *refs):
-    pieces = refs[:4]
-    out_ref, sum_ref = refs[-2:]
+def place_kernel(top_k, idx_ref, *refs):
+    count = len(refs) - 5
+    pieces, (out_ref, sum_ref, tails, out_sems, tail_sems) = refs[:count], refs[count:]
     experts, slots, pair = pieces[0].shape
-    m = pl.program_id(0)
-
-    @pl.when(m == 0)
-    def _():
-        sum_ref[...] = jnp.zeros_like(sum_ref)
-
-    for i in range(4):
-
-        @pl.when(m == i)
-        def _():
-            out_ref[0] = pieces[i][...]
-            for e in range(experts):
-                row = pieces[i][e, slots - 8 :].astype(F32)[8 - top_k : 9 - top_k]
-                sum_ref[e : e + 1] += row[:, : pair // 2] + row[:, pair // 2 :]
-
-
-def place(index, pieces, before, sources, top_k):
+    rows = tails.shape[2]
+    slabs = count // 4
+    stores, loads = [], []
+    for i in range(count):
+        column = pl.multiple_of(idx_ref[slabs + i % 4] * pair, pair)
+        to = out_ref.at[idx_ref[i // 4], :, :, pl.ds(column, pair)]
+        stores.append(pltpu.make_async_copy(pieces[i], to, out_sems.at[i]))
+        loads.append(pltpu.make_async_copy(pieces[i].at[:, slots - rows :, :], tails.at[i], tail_sems.at[i]))
+    for copy in loads + stores:
+        copy.start()
+    for copy in loads:
+        copy.wait()
+    for k in range(slabs):
+        for e in range(experts):
+            total = sum(tails[4 * k + m, e].astype(F32) for m in range(4))
+            row = total[rows - top_k : rows - top_k + 1]
+            sum_ref[k * experts + e : k * experts + e + 1] = row[:, : pair // 2] + row[:, pair // 2 :]
+    for copy in stores:
+        copy.wait()
+
+
+def place(index, pieces, top_k):
     experts, slots, pair = pieces[0].shape
-    first = before is None
-    shape = (sources, experts, slots, 4 * pair)
+    slabs = len(pieces) // 4
     return pl.pallas_call(
-        functools.partial(place_kernel, top_k, first),
+        functools.partial(place_kernel, top_k),
         grid_spec=pltpu.PrefetchScalarGridSpec(
             num_scalar_prefetch=1,
-            grid=(4,),
-            in_specs=[pl.BlockSpec((experts, slots, pair), lambda m, idx: (0, 0, 0))] * 4
-            + ([] if first else [pl.BlockSpec(memory_space=pl.ANY)]),
+            grid=(1,),
+            in_specs=[pl.BlockSpec(memory_space=pl.ANY)] * len(pieces),
             out_specs=[
-                pl.BlockSpec((1, experts, slots, pair), lambda m, idx: (idx[0], 0, 0, idx[1 + m])),
-                pl.BlockSpec((experts, pair // 2), lambda m, idx: (0, 0)),
+                pl.BlockSpec(memory_space=pl.ANY),
+                pl.BlockSpec((slabs * experts, pair // 2), lambda i, idx: (0, 0)),
             ],
+            scratch_shapes=[
+                pltpu.VMEM((len(pieces), experts, 16, pair), BF16),
+                pltpu.SemaphoreType.DMA((len(pieces),)),
+                pltpu.SemaphoreType.DMA((len(pieces),)),
+            ],
         ),
         out_shape=[
-            jax.ShapeDtypeStruct(shape, BF16),
-            jax.ShapeDtypeStruct((experts, pair // 2), F32),
+            jax.ShapeDtypeStruct((slabs, experts, slots, 4 * pair), BF16),
+            jax.ShapeDtypeStruct((slabs * experts, pair // 2), F32),
         ],
-        input_output_aliases={} if first else {5: 0},
-        compiler_params=pltpu.CompilerParams(vmem_limit_bytes=VMEM_BYTES),
+        compiler_params=pltpu.CompilerParams(vmem_limit_bytes=8 * 2**20),
         cost_estimate=pl.CostEstimate(
-            flops=0, bytes_accessed=16 * experts * slots * pair, transcendentals=0
-        ),
-    )(index, *pieces, *([] if first else [before]))
+            flops=0, bytes_accessed=4 * len(pieces) * experts * slots * pair, transcendentals=0
+        ),
+    )(index, *pieces)
 
 
 def on_device_tokens(grad_out, routes, affinity, saved_hidden, down_proj):
@@ -360,30 +365,28 @@
     fence = lax.optimization_barrier
 
     slabs = [lax.rem(me - step + sources, sources) for step in range(sources)]
-    index = jnp.stack(slabs + [me * experts, core]).astype(jnp.int32)
+    index = jnp.stack(slabs + [me * experts]).astype(jnp.int32)
 
     def kernel(items):
-        *grads, scatter = project(index, items, own_weight, partner_weight, hidden, top_k)
+        *grads, scatter = project(index, items, weights, hidden, top_k)
         return grads, scatter
 
     def send_back(grads, chip_of):
         return [across(g, 2 * m) if m else g for g, m in zip(grads, chip_of)]
-
-    def put(step, returned, placed):
-        spots = jnp.stack([slabs[step]] + chips).astype(jnp.int32)
-        return place(spots, returned, placed, sources, top_k)
 
     x0, y0, next1 = across(grad_out, 2), across(grad_out, 4), around(grad_out, 1)
     held = jnp.transpose(saved_hidden.reshape(experts, sources, most, 4, pair), (3, 0, 1, 2, 4))
     held = fence(held)
     held = [lax.dynamic_index_in_dim(held, chips[m], axis=0, keepdims=False) for m in range(4)]
+    last_meta, down_proj, held = fence((meta, down_proj, held))
     own_weight = jnp.transpose(down_proj, (1, 0, 2)).reshape(experts * block, width)
-    last_meta, held, own_weight = fence((meta, held, own_weight))
+    cores = [[i, i + 1] for i in range(0, reps, 2)]
+    weights = lax.all_gather(own_weight, "rep", axis=0, axis_index_groups=cores)
     metas = [meta, around(meta, 1), around(meta, 2), around(last_meta, 3)]
-    metas, x0, y0, next1, held, own_weight = fence((metas, x0, y0, next1, held, own_weight))
-
-    xy0, x1 = across(x0, 4), across(next1, 2)
-    next2, own3 = around(next1, 1), around(fence((grad_out, y0))[0], -1)
+    metas, x0, y0, next1, held = fence((metas, x0, y0, next1, held))
+
+    xy0, x1, next2 = across(x0, 4), across(next1, 2), around(next1, 1)
+    own3 = around(fence((grad_out, next2))[0], -1)
     metas = jnp.take(jnp.stack(metas), lax.rem(me - jnp.arange(sources) + sources, sources), axis=0)
     blank = jnp.zeros((experts, sources, SLOT_PAD - most - top_k, pair), BF16)
     metas = jnp.broadcast_to(metas[None], (experts, sources, top_k, pair))
@@ -391,10 +394,7 @@
     for m in range(4):
         piece = jnp.concatenate([held[m], blank, metas], axis=2)
         hidden.append(across(piece, 2 * m) if m else piece)
-    partner_weight = across(own_weight, 1)
-    hidden, xy0, x1, next2, own3, partner_weight, x0, y0, next1 = fence(
-        (hidden, xy0, x1, next2, own3, partner_weight, x0, y0, next1)
-    )
+    hidden, xy0, x1, next2, own3, x0, y0, next1 = fence((hidden, xy0, x1, next2, own3, x0, y0, next1))
 
     y1, x2, x3 = across(next1, 4), across(next2, 2), around(x0, -1)
     grads0, scatter0 = kernel([([grad_out], 0, 0), ([x0], 1, 0), ([y0], 2, 0), ([xy0], 3, 0)])
@@ -427,11 +427,22 @@
     later = across(later, 1)
     returned2 = send_back(grads2, (3, 2, 0, 2))
     returned3 = send_back(grads3, (3, 3))
-    placed, combine0 = put(0, returned0, None)
-    placed, combine1 = put(1, [*returned1[:3], returned2[0]], placed)
-    placed, combine2 = put(2, [returned1[3], returned1[4], returned2[1], returned3[0]], placed)
-    placed, combine3 = put(3, [returned2[2], returned1[5], returned2[3], returned3[1]], placed)
-    combines = [combine0, around(combine1, -1), around(combine2, -2), around(combine3, 1)]
+    returned = [
+        *returned0,
+        *returned1[:3],
+        returned2[0],
+        returned1[3],
+        returned1[4],
+        returned2[1],
+        returned3[0],
+        returned2[2],
+        returned1[5],
+        returned2[3],
+        returned3[1],
+    ]
+    placed, combine = place(jnp.stack(slabs + chips).astype(jnp.int32), returned, top_k)
+    combine = combine.reshape(sources, experts, tokens)
+    combines = [combine[0], around(combine[1], -1), around(combine[2], -2), around(combine[3], 1)]
     route_grad = 0.0
     expert_ids = jnp.arange(experts, dtype=routes.dtype)
     for step in range(sources):

time: 226 us -> 258 us (1.14)
  waiting for transfers between devices: 50.1 us -> 70.4 us
  local copies, waits for them, and re-layouts: 37 us -> 50.3 us
  between operations: 1.34 us -> 14.6 us
  Pallas kernels: 77 us -> 64.3 us
    ppermute x12, waiting for transfers between devices: 9.31 us -> 32.8 us  [around(): lax.ppermute(array, 'exp', [(i, (i + shift) % sources) for i in range(sou...]
    unnamed x131 -> x135, local copies, waits for them, and re-layouts: 22.1 us -> 38.7 us
    pallas_call x4, Pallas kernels: 42.6 us -> 33.7 us  [project(): pl.pallas_call(functools.partial(project_kernel, top_k, sizes, len(items)...]
    pallas_call x4 -> x1, Pallas kernels: 5.98 us -> 2.25 us  [place(): pl.pallas_call(functools.partial(place_kernel, top_k), grid_spec=pltpu.Pr...]
    ppermute x27 -> x26, waiting for transfers between devices: 40.8 us -> 37.6 us  [across(): return lax.ppermute(array, 'rep', [(i, i ^ bits) for i in range(reps)])]
    ppermute x27 -> x26, starting transfers between devices: 28.8 us -> 27 us  [across(): return lax.ppermute(array, 'rep', [(i, i ^ bits) for i in range(reps)])]
  transfers between devices with their start and end apart: 39 -> 39, of which waited for: 12 -> 13; matrix products, arithmetic and copies ran while one was open for 10% -> 3% of each run, Pallas kernels for 28% -> 19%
where the time goes in v8:
time: 258 us; the launch traced here: 257 us
  waiting for transfers between devices  70.4 us (27%)
  Pallas kernels  64.3 us (25%)
  starting transfers between devices  51.9 us (20%)
  local copies, waits for them, and re-layouts  50.3 us (19%)
  between operations  14.6 us (6%)
  other arithmetic  5.33 us (2%)
    unnamed x135, local copies, waits for them, and re-layouts  38.7 us
    ppermute x26, waiting for transfers between devices, across(): return lax.ppermute(array, 'rep', [(i, i ^ bits) for i in range(reps)])  37.6 us
    pallas_call x4, Pallas kernels, project(): pl.pallas_call(functools.partial(project_kernel, top_k, sizes, len(items)...  33.7 us
    ppermute x12, waiting for transfers between devices, around(): lax.ppermute(array, 'exp', [(i, (i + shift) % sources) for i in range(sou...  32.8 us
    pallas_call x3, Pallas kernels, half_grad(): pl.pallas_call(functools.partial(half_grad_kernel, len(scatters), len(arr...  28.4 us
    ppermute x26, starting transfers between devices, across(): return lax.ppermute(array, 'rep', [(i, i ^ bits) for i in range(reps)])  27 us
    ppermute x12, starting transfers between devices, around(): lax.ppermute(array, 'exp', [(i, (i + shift) % sources) for i in range(sou...  24.8 us
    reshape x2, local copies, waits for them, and re-layouts, on_device_tokens(): saved_hidden.reshape(experts, sources, most, 4, pair)  7.02 us
  transfers between devices with their start and end apart: 39, of which 13 were waited for; matrix products, arithmetic and copies ran while one was open for 3% of the time, Pallas kernels for 19%

profile of v8, /device:TPU:0, one launch (start us, length us, event | category | flops | bytes accessed | tf_op | source)
XLA Modules:
  0.0 256.8 jit_solution(8296049384142978164)
XLA Ops:
  9.3 4.8 %reshape.94 = bf16[4,4,60,4,256]{4,3,1,2,0:T(4,128)(2,1)} reshape(bf16[1,4,4,60,1024]{4,2,3,1,0:T(4,128)(2,1)} %param.8) | data formatting | bytes 3932160 | tf_op jit(solution)/shard_map/reshape | solution.py:378
  14.1 2.2 copy.18
  16.4 1.2 dynamic-slice_bitcast_fusion
  17.6 1.4 copy-done.64
  19.0 2.4 copy.15
  22.6 3.0 %collective-permute-start.5 = (bf16[128,3584]{1,0:T(8,128)(2,1)S(1)}, bf16[128,3584]{1,0:T(8,128)(2,1)S(1)}, u32[]{:S(2)}, u32[]{:S(2)}) collective-permute-start(bf16[128,3584]{1,0:T(8,128)(2,1)S(1)} %copy-done.21), channel_id=1, source_target_pairs={{0,1},{1,2},{2,3},{3,0},{4,5},{5,6},{6,7},{7,4},{8,9},{9,10},{10,1... | collective-permute-start | bytes 2752520 | tf_op jit(solution)/shard_map/ppermute | solution.py:359
  25.6 1.5 collective-permute-start.4
  27.2 1.5 collective-permute-start.3
  28.6 2.6 %collective-permute-start.1 = (bf16[4,256]{1,0:T(4,128)(2,1)S(1)}, bf16[4,256]{1,0:T(4,128)(2,1)S(1)}, u32[]{:S(2)}, u32[]{:S(2)}) collective-permute-start(bf16[4,256]{1,0:T(4,128)(2,1)S(1)} %pad_maximum_fusion.5), channel_id=1, source_target_pairs={{0,2},{1,3},{2,0},{3,1},{4,6},{5,7},{6,4},{7,5},{8,10},{9,11},{10,... | collective-permute-start | bytes 6152 | tf_op jit(solution)/shard_map/ppermute | solution.py:359
  31.5 13.9 %collective-permute-done.1 = bf16[4,256]{1,0:T(4,128)(2,1)S(1)} collective-permute-done((bf16[4,256]{1,0:T(4,128)(2,1)S(1)}, bf16[4,256]{1,0:T(4,128)(2,1)S(1)}, u32[]{:S(2)}, u32[]{:S(2)}) %collective-permute-start.1) | collective-permute-done | bytes 2080 | tf_op jit(solution)/shard_map/ppermute | solution.py:359
  45.3 4.5 %collective-permute-start.2 = (bf16[4,256]{1,0:T(4,128)(2,1)S(1)}, bf16[4,256]{1,0:T(4,128)(2,1)S(1)}, u32[]{:S(2)}, u32[]{:S(2)}) collective-permute-start(bf16[4,256]{1,0:T(4,128)(2,1)S(1)} %pad_maximum_fusion.5), channel_id=1, source_target_pairs={{0,3},{1,0},{2,1},{3,2},{4,7},{5,4},{6,5},{7,6},{8,11},{9,8},{10,9... | collective-permute-start | bytes 6152 | tf_op jit(solution)/shard_map/ppermute | solution.py:359
  49.8 1.3 collective-permute-done.2
  51.2 1.2 collective-permute-start.11
  53.1 2.4 pad_maximum_fusion
  55.5 2.4 collective-permute-start.8
  59.0 15.1 %collective-permute-done.11.refs_3_.refs_9_.refs_13_ = bf16[128,3584]{1,0:T(8,128)(2,1)} collective-permute-done((bf16[128,3584]{1,0:T(8,128)(2,1)S(1)}, bf16[128,3584]{1,0:T(8,128)(2,1)}, u32[]{:S(2)}, u32[]{:S(2)}) %collective-permute-start.11) | collective-permute-done | bytes 917536 | tf_op jit(solution)/shard_map/ppermute | solution.py:359
  75.1 1.5 collective-permute-start.6
  76.6 1.5 collective-permute-start.7
  78.1 20.4 %collective-permute-done.6.refs_7_.refs_9_.refs_12_.refs_13_ = bf16[4,4,64,256]{3,2,1,0:T(8,128)(2,1)S(1)} collective-permute-done((bf16[4,4,64,256]{3,2,1,0:T(8,128)(2,1)S(1)}, bf16[4,4,64,256]{3,2,1,0:T(8,128)(2,1)S(1)}, u32[]{:S(2)}, u32[]{:S(2)}) %collective-permute-start.6) | collective-permute-done | bytes 524320 | tf_op jit(solution)/shard_map/ppermute | solution.py:356
  102.0 1.5 collective-permute-start.14
  104.4 2.8 %collective-permute-start.15 = (bf16[128,3584]{1,0:T(8,128)(2,1)}, bf16[128,3584]{1,0:T(8,128)(2,1)}, u32[]{:S(2)}, u32[]{:S(2)}) collective-permute-start(bf16[128,3584]{1,0:T(8,128)(2,1)} %collective-permute-done.3.refs_1_.refs_3_.refs_7_), channel_id=1, source_target_pairs={{0,3},{1,0},{2,1},{3,2},{4,7},{5,4},{6,5},{7,6},{8,11},{9,8},{10,9... | collective-permute-start | bytes 2752520 | tf_op jit(solution)/shard_map/ppermute | solution.py:359
  107.3 3.1 %copy-done = bf16[2,512,3584]{2,1,0:T(8,128)(2,1)S(1)} copy-done((bf16[2,512,3584]{2,1,0:T(8,128)(2,1)S(1)}, bf16[2,512,3584]{2,1,0:T(8,128)(2,1)}, u32[]{:S(2)}) %copy-start) | copy-done | bytes 7340056
  113.5 9.0 %shard_map.76 = (bf16[4,64,256]{2,1,0:T(8,128)(2,1)S(1)}, bf16[4,64,256]{2,1,0:T(8,128)(2,1)}, bf16[4,64,256]{2,1,0:T(8,128)(2,1)S(1)}, bf16[4,64,256]{2,1,0:T(8,128)(2,1)S(1)}, bf16[2,512,512]{2,1,0:T(8,128)(2,1)S(1)}) custom-call(s32[5]{0:T(128)S(1)} %stack.67.idx_ref, bf16[128,3584]{1,0:T(8,128)(2,1)S(1)} %copy-done.21, ...), custom_call_target="tpu_custom_call" | custom-call | flops 7516192768 | bytes 11010048 | tf_op jit(solution)/shard_map/pallas_call | solution.py:178
  125.1 1.6 collective-permute-done.15.refs_5_.refs_11_.refs_15_
  126.8 4.3 %collective-permute-start.18 = (bf16[128,3584]{1,0:T(8,128)(2,1)S(1)}, bf16[128,3584]{1,0:T(8,128)(2,1)S(1)}, u32[]{:S(2)}, u32[]{:S(2)}) collective-permute-start(bf16[128,3584]{1,0:T(8,128)(2,1)S(1)} %collective-permute-done.4.refs_2_.refs_4_.refs_8_), channel_id=1, source_target_pairs={{0,3},{1,0},{2,1},{3,2},{4,7},{5,4},{6,5},{7,6},{8,11},{9,8},{10,9... | collective-permute-start | bytes 2752520 | tf_op jit(solution)/shard_map/ppermute | solution.py:359
  132.1 1.2 copy-done.31
  136.4 12.0 %shard_map.77 = (bf16[4,64,256]{2,1,0:T(8,128)(2,1)S(1)}, bf16[4,64,256]{2,1,0:T(8,128)(2,1)S(1)}, bf16[4,64,256]{2,1,0:T(8,128)(2,1)S(1)}, bf16[4,64,256]{2,1,0...) custom-call(s32[5]{0:T(128)S(1)} %stack.67.idx_ref, ...), custom_call_target="tpu_custom_call" | custom-call | flops 11274289152 | bytes 12845056 | tf_op jit(solution)/shard_map/pallas_call | solution.py:178
  149.4 2.4 collective-permute-done.16.refs_0_.refs_2_.refs_16_
  152.0 1.6 collective-permute-start.21
  153.9 1.7 collective-permute-start.23
  155.9 1.4 collective-permute-start.20
  157.3 8.0 %shard_map.78 = (bf16[4,64,256]{2,1,0:T(8,128)(2,1)}, bf16[4,64,256]{2,1,0:T(8,128)(2,1)S(1)}, bf16[4,64,256]{2,1,0:T(8,128)(2,1)S(1)}, bf16[4,64,256]{2,1,0:T(8,128)(2,1)S(1)}, bf16[2,512,512]{2,1,0:T(8,128)(2,1)S(1)}) custom-call(s32[5]{0:T(128)S(1)} %stack.67.idx_ref, bf16[128,3584]{1,0:T(8,128)(2,1)S(1)} %collective-permute-done.16.refs_0_.refs_2_.refs_16_, ...), custom_call_target="tpu_custom_call" | custom-call | flops 7516192768 | bytes 11010048 | tf_op jit(solution)/shard_map/pallas_call | solution.py:178
  168.1 1.4 copy-done.17
  171.9 8.3 %shard_map.79 = bf16[512,3584]{1,0:T(8,128)(2,1)S(1)} custom-call(s32[1]{0:T(128)} %bitcast.24.idx_ref, bf16[2,512,512]{2,1,0:T(8,128)(2,1)S(1)} %copy-done.19, bf16[2,512,768]{2,1,0:T(8,128)(2,1)S(1)} %copy-done.17, bf16[128,3584]{1,0:T(8,128)(2,1)S(1)} %copy-done.22, bf16[128,3584]{1,0:T(8,128)(2,1)} %collective-permute-done.3.refs_1_.refs_3_.refs_7_, ...), custom_call_target="tpu_custom_call" | custom-call | flops 4697620480 | bytes 17825792 | tf_op jit(solution)/shard_map/pallas_call | solution.py:270
  181.0 2.0 collective-permute-start.26
  183.0 1.5 collective-permute-start.27
  185.0 4.7 %shard_map.80 = (bf16[4,64,256]{2,1,0:T(8,128)(2,1)S(1)}, bf16[4,64,256]{2,1,0:T(8,128)(2,1)S(1)}, bf16[2,512,256]{2,1,0:T(8,128)(2,1)S(1)}) custom-call(s32[5]{0:T(128)S(1)} %stack.67.idx_ref, bf16[128,3584]{1,0:T(8,128)(2,1)S(1)} %collective-permute-done.19.refs_0_.refs_6_.refs_20_, bf16[128,3584]{1,0:T(8,128)(2,1)S(1)} %collective-permute-done.20.refs_1_.refs_7_.refs_21_, ...), custom_call_target="tpu_custom_call" | custom-call | flops 3758096384 | bytes 9175040 | tf_op jit(solution)/shard_map/pallas_call | solution.py:178
  189.7 5.5 %shard_map.81 = bf16[512,3584]{1,0:T(8,128)(2,1)} custom-call(s32[1]{0:T(128)} %bitcast.24.idx_ref, bf16[2,512,512]{2,1,0:T(8,128)(2,1)S(1)} %get-tuple-element.196.refs_0_.refs_2_, bf16[2,512,256]{2,1,0:T(8,128)(2,1)S(1)} %get-tuple-element.216.refs_1_.refs_3_, bf16[128,3584]{1,0:T(8,128)(2,1)S(1)} %copy-done.9, bf16[128,3584]{1,0:T(8,128)(2,1)S(1)} %copy-done.12, ...), custom_call_target="tpu_custom_call" | custom-call | flops 2818572288 | bytes 13631488 | tf_op jit(solution)/shard_map/pallas_call | solution.py:270
  197.9 1.8 copy-done.63
  200.6 2.0 collective-permute-start.30
  202.7 2.0 collective-permute-start.31
  204.7 2.7 %collective-permute-done.29.refs_7_ = bf16[4,64,256]{2,1,0:T(8,128)(2,1)} collective-permute-done((bf16[4,64,256]{2,1,0:T(8,128)(2,1)}, bf16[4,64,256]{2,1,0:T(8,128)(2,1)}, u32[]{:S(2)}, u32[]{:S(2)}) %collective-permute-start.29) | collective-permute-done | bytes 131104 | tf_op jit(solution)/shard_map/ppermute | solution.py:356
  208.0 7.3 %collective-permute-done.30.refs_10_ = bf16[4,64,256]{2,1,0:T(8,128)(2,1)} collective-permute-done((bf16[4,64,256]{2,1,0:T(8,128)(2,1)}, bf16[4,64,256]{2,1,0:T(8,128)(2,1)}, u32[]{:S(2)}, u32[]{:S(2)}) %collective-permute-start.30) | collective-permute-done | bytes 131104 | tf_op jit(solution)/shard_map/ppermute | solution.py:356
  215.3 2.8 %collective-permute-done.32.refs_14_ = bf16[4,64,256]{2,1,0:T(8,128)(2,1)} collective-permute-done((bf16[4,64,256]{2,1,0:T(8,128)(2,1)}, bf16[4,64,256]{2,1,0:T(8,128)(2,1)}, u32[]{:S(2)}, u32[]{:S(2)}) %collective-permute-start.32) | collective-permute-done | bytes 131104 | tf_op jit(solution)/shard_map/ppermute | solution.py:356
  225.3 2.2 shard_map.82
  228.2 3.2 %collective-permute-start.34 = (f32[4,128]{1,0:T(4,128)S(1)}, f32[4,128]{1,0:T(4,128)S(1)}, u32[]{:S(2)}, u32[]{:S(2)}) collective-permute-start(f32[4,128]{1,0:T(4,128)S(1)} %get-tuple-element.245), channel_id=1, source_target_pairs={{0,3},{1,0},{2,1},{3,2},{4,7},{5,4},{6,5},{7,6},{8,11},{9,8},{10,9... | collective-permute-start | bytes 6152 | tf_op jit(solution)/shard_map/ppermute | solution.py:359
  231.7 2.8 %copy.16 = bf16[1,4,4,60,1024]{4,2,3,1,0:T(4,128)(2,1)} copy(bf16[1,4,4,60,1024]{4,3,1,2,0:T(8,128)(2,1)S(1)} %slice_bitcast_fusion) | data formatting | bytes 3932160
  235.4 14.6 %shard_map.83 = f32[128,4,3584]{2,1,0:T(4,128)} custom-call(s32[1]{0:T(128)} %bitcast.28.idx_ref, bf16[2,512,512]{2,1,0:T(8,128)(2,1)S(1)} %copy-done.20, bf16[2,512,768]{2,1,0:T(8,128)(2,1)} %copy-done.16, bf16[2,512,512]{2,1,0:T(8,128)(2,1)S(1)} %get-tuple-element.196.refs_0_.refs_2_, bf16[2,512,256]{2,1,0:T(8,128)(2,1)S(1)} %get-tuple-element.216.refs_1_.refs_3_, ...), custom_call_target="tpu_custom_call" | custom-call | flops 7516192768 | bytes 24117248 | tf_op jit(solution)/shard_map/pallas_call | solution.py:270
  (199 shorter events, 41.9 us)
Async XLA Ops:
  7.2 100.1 %all-gather.2.cloned.1.call-start = ((), (), s32[]{:S(2)}) async-start(), calls=%async_computation | async-start | bytes 11010048 | tf_op jit(solution)/shard_map/all_gather | solution.py:384
  22.6 28.5 %collective-permute-start.5 = (bf16[128,3584]{1,0:T(8,128)(2,1)S(1)}, bf16[128,3584]{1,0:T(8,128)(2,1)S(1)}, u32[]{:S(2)}, u32[]{:S(2)}) collective-permute-start(bf16[128,3584]{1,0:T(8,128)(2,1)S(1)} %copy-done.21), channel_id=1, source_target_pairs={{0,1},{1,2},{2,3},{3,0},{4,5},{5,6},{6,7},{7,4},{8,9},{9,10},{10,1... | collective-permute-start | bytes 2752520 | tf_op jit(solution)/shard_map/ppermute | solution.py:359
  25.6 25.5 %collective-permute-start.4 = (bf16[128,3584]{1,0:T(8,128)(2,1)S(1)}, bf16[128,3584]{1,0:T(8,128)(2,1)S(1)}, u32[]{:S(2)}, u32[]{:S(2)}) collective-permute-start(bf16[128,3584]{1,0:T(8,128)(2,1)S(1)} %copy-done.21), channel_id=1, source_target_pairs={{0,16},{4,20},{8,24},{12,28},{16,0},{20,4},{24,8},{28,12},{1,17},{... | collective-permute-start | bytes 2752520 | tf_op jit(solution)/shard_map/ppermute | solution.py:356
  27.2 24.0 %collective-permute-start.3 = (bf16[128,3584]{1,0:T(8,128)(2,1)S(1)}, bf16[128,3584]{1,0:T(8,128)(2,1)}, u32[]{:S(2)}, u32[]{:S(2)}) collective-permute-start(bf16[128,3584]{1,0:T(8,128)(2,1)S(1)} %copy-done.21), channel_id=1, source_target_pairs={{0,8},{4,12},{8,0},{12,4},{16,24},{20,28},{24,16},{28,20},{1,9},{5... | collective-permute-start | bytes 2752520 | tf_op jit(solution)/shard_map/ppermute | solution.py:356
  28.6 16.7 %collective-permute-start.1 = (bf16[4,256]{1,0:T(4,128)(2,1)S(1)}, bf16[4,256]{1,0:T(4,128)(2,1)S(1)}, u32[]{:S(2)}, u32[]{:S(2)}) collective-permute-start(bf16[4,256]{1,0:T(4,128)(2,1)S(1)} %pad_maximum_fusion.5), channel_id=1, source_target_pairs={{0,2},{1,3},{2,0},{3,1},{4,6},{5,7},{6,4},{7,5},{8,10},{9,11},{10,... | collective-permute-start | bytes 6152 | tf_op jit(solution)/shard_map/ppermute | solution.py:359
  31.2 18.6 %collective-permute-start = (bf16[4,256]{1,0:T(4,128)(2,1)S(1)}, bf16[4,256]{1,0:T(4,128)(2,1)S(1)}, u32[]{:S(2)}, u32[]{:S(2)}) collective-permute-start(bf16[4,256]{1,0:T(4,128)(2,1)S(1)} %pad_maximum_fusion.5), channel_id=1, source_target_pairs={{0,1},{1,2},{2,3},{3,0},{4,5},{5,6},{6,7},{7,4},{8,9},{9,10},{10,1... | collective-permute-start | bytes 6152 | tf_op jit(solution)/shard_map/ppermute | solution.py:359
  45.3 5.8 %collective-permute-start.2 = (bf16[4,256]{1,0:T(4,128)(2,1)S(1)}, bf16[4,256]{1,0:T(4,128)(2,1)S(1)}, u32[]{:S(2)}, u32[]{:S(2)}) collective-permute-start(bf16[4,256]{1,0:T(4,128)(2,1)S(1)} %pad_maximum_fusion.5), channel_id=1, source_target_pairs={{0,3},{1,0},{2,1},{3,2},{4,7},{5,4},{6,5},{7,6},{8,11},{9,8},{10,9... | collective-permute-start | bytes 6152 | tf_op jit(solution)/shard_map/ppermute | solution.py:359
  51.1 80.9 %copy-start.24 = (bf16[128,3584]{1,0:T(8,128)(2,1)}, bf16[128,3584]{1,0:T(8,128)(2,1)S(1)}, u32[]{:S(2)}) copy-start(bf16[128,3584]{1,0:T(8,128)(2,1)S(1)} %collective-permute-done.5.refs_0_.refs_6_.refs_10_) | copy-start | bytes 2752516
  51.2 75.6 %copy-start.27 = (bf16[128,3584]{1,0:T(8,128)(2,1)}, bf16[128,3584]{1,0:T(8,128)(2,1)S(1)}, u32[]{:S(2)}) copy-start(bf16[128,3584]{1,0:T(8,128)(2,1)S(1)} %collective-permute-done.4.refs_2_.refs_4_.refs_8_) | copy-start | bytes 2752516
  51.2 22.9 %collective-permute-start.11 = (bf16[128,3584]{1,0:T(8,128)(2,1)S(1)}, bf16[128,3584]{1,0:T(8,128)(2,1)}, u32[]{:S(2)}, u32[]{:S(2)}) collective-permute-start(bf16[128,3584]{1,0:T(8,128)(2,1)S(1)} %collective-permute-done.5.refs_0_.refs_6_.refs_10_), channel_id=1, source_target_pairs={{0,1},{1,2},{2,3},{3,0},{4,5},{5,6},{6,7},{7,4},{8,9},{9,10},{10,1... | collective-permute-start | bytes 2752520 | tf_op jit(solution)/shard_map/ppermute | solution.py:359
  55.5 21.1 %collective-permute-start.8 = (bf16[4,4,64,256]{3,2,1,0:T(8,128)(2,1)S(1)}, bf16[4,4,64,256]{3,2,1,0:T(8,128)(2,1)S(1)}, u32[]{:S(2)}, u32[]{:S(2)}) collective-permute-start(bf16[4,4,64,256]{3,2,1,0:T(8,128)(2,1)S(1)} %get-tuple-element.238), channel_id=1, source_target_pairs={{0,24},{4,28},{8,16},{12,20},{16,8},{20,12},{24,0},{28,4},{1,25},{... | collective-permute-start | bytes 1572872 | tf_op jit(solution)/shard_map/ppermute | solution.py:356
  57.9 42.2 %collective-permute-start.10 = (bf16[128,3584]{1,0:T(8,128)(2,1)S(1)}, bf16[128,3584]{1,0:T(8,128)(2,1)S(1)}, u32[]{:S(2)}, u32[]{:S(2)}) collective-permute-start(bf16[128,3584]{1,0:T(8,128)(2,1)S(1)} %collective-permute-done.5.refs_0_.refs_6_.refs_10_), channel_id=1, source_target_pairs={{0,8},{4,12},{8,0},{12,4},{16,24},{20,28},{24,16},{28,20},{1,9},{5... | collective-permute-start | bytes 2752520 | tf_op jit(solution)/shard_map/ppermute | solution.py:356
  58.5 41.7 %collective-permute-start.9 = (bf16[128,3584]{1,0:T(8,128)(2,1)}, bf16[128,3584]{1,0:T(8,128)(2,1)}, u32[]{:S(2)}, u32[]{:S(2)}) collective-permute-start(bf16[128,3584]{1,0:T(8,128)(2,1)} %collective-permute-done.3.refs_1_.refs_3_.refs_7_), channel_id=1, source_target_pairs={{0,16},{4,20},{8,24},{12,28},{16,0},{20,4},{24,8},{28,12},{1,17},{... | collective-permute-start | bytes 2752520 | tf_op jit(solution)/shard_map/ppermute | solution.py:356
  74.1 27.0 %collective-permute-start.12 = (bf16[128,3584]{1,0:T(8,128)(2,1)S(1)}, bf16[128,3584]{1,0:T(8,128)(2,1)S(1)}, u32[]{:S(2)}, u32[]{:S(2)}) collective-permute-start(bf16[128,3584]{1,0:T(8,128)(2,1)S(1)} %copy-done.21), channel_id=1, source_target_pairs={{0,3},{1,0},{2,1},{3,2},{4,7},{5,4},{6,5},{7,6},{8,11},{9,8},{10,9... | collective-permute-start | bytes 2752520 | tf_op jit(solution)/shard_map/ppermute | solution.py:359
  75.1 23.4 %collective-permute-start.6 = (bf16[4,4,64,256]{3,2,1,0:T(8,128)(2,1)S(1)}, bf16[4,4,64,256]{3,2,1,0:T(8,128)(2,1)S(1)}, u32[]{:S(2)}, u32[]{:S(2)}) collective-permute-start(bf16[4,4,64,256]{3,2,1,0:T(8,128)(2,1)S(1)} %get-tuple-element.239), channel_id=1, source_target_pairs={{0,8},{4,12},{8,0},{12,4},{16,24},{20,28},{24,16},{28,20},{1,9},{5... | collective-permute-start | bytes 1572872 | tf_op jit(solution)/shard_map/ppermute | solution.py:356
  76.6 22.7 %collective-permute-start.7 = (bf16[4,4,64,256]{3,2,1,0:T(8,128)(2,1)S(1)}, bf16[4,4,64,256]{3,2,1,0:T(8,128)(2,1)S(1)}, u32[]{:S(2)}, u32[]{:S(2)}) collective-permute-start(bf16[4,4,64,256]{3,2,1,0:T(8,128)(2,1)S(1)} %get-tuple-element.240), channel_id=1, source_target_pairs={{0,16},{4,20},{8,24},{12,28},{16,0},{20,4},{24,8},{28,12},{1,17},{... | collective-permute-start | bytes 1572872 | tf_op jit(solution)/shard_map/ppermute | solution.py:356
  102.0 22.3 %collective-permute-start.14 = (bf16[128,3584]{1,0:T(8,128)(2,1)}, bf16[128,3584]{1,0:T(8,128)(2,1)}, u32[]{:S(2)}, u32[]{:S(2)}) collective-permute-start(bf16[128,3584]{1,0:T(8,128)(2,1)} %collective-permute-done.11.refs_3_.refs_9_.refs_13_), channel_id=1, source_target_pairs={{0,8},{4,12},{8,0},{12,4},{16,24},{20,28},{24,16},{28,20},{1,9},{5... | collective-permute-start | bytes 2752520 | tf_op jit(solution)/shard_map/ppermute | solution.py:356
  103.5 21.6 %collective-permute-start.13 = (bf16[128,3584]{1,0:T(8,128)(2,1)S(1)}, bf16[128,3584]{1,0:T(8,128)(2,1)}, u32[]{:S(2)}, u32[]{:S(2)}) collective-permute-start(bf16[128,3584]{1,0:T(8,128)(2,1)S(1)} %collective-permute-done.5.refs_0_.refs_6_.refs_10_), channel_id=1, source_target_pairs={{0,16},{4,20},{8,24},{12,28},{16,0},{20,4},{24,8},{28,12},{1,17},{... | collective-permute-start | bytes 2752520 | tf_op jit(solution)/shard_map/ppermute | solution.py:356
  104.4 22.3 %collective-permute-start.15 = (bf16[128,3584]{1,0:T(8,128)(2,1)}, bf16[128,3584]{1,0:T(8,128)(2,1)}, u32[]{:S(2)}, u32[]{:S(2)}) collective-permute-start(bf16[128,3584]{1,0:T(8,128)(2,1)} %collective-permute-done.3.refs_1_.refs_3_.refs_7_), channel_id=1, source_target_pairs={{0,3},{1,0},{2,1},{3,2},{4,7},{5,4},{6,5},{7,6},{8,11},{9,8},{10,9... | collective-permute-start | bytes 2752520 | tf_op jit(solution)/shard_map/ppermute | solution.py:359
  113.5 18.6 %copy-start.1 = (bf16[2,512,3584]{2,1,0:T(8,128)(2,1)S(1)}, bf16[2,512,3584]{2,1,0:T(8,128)(2,1)}, u32[]{:S(2)}) copy-start(bf16[2,512,3584]{2,1,0:T(8,128)(2,1)} %all-gather.2.cloned.1.call-done.refs_4_.refs_5_.refs_6_.refs_7_.refs_2_.refs_3_) | copy-start | bytes 22020100
  126.8 30.5 %copy-start.3 = (bf16[128,3584]{1,0:T(8,128)(2,1)S(1)}, bf16[128,3584]{1,0:T(8,128)(2,1)}, u32[]{:S(2)}) copy-start(bf16[128,3584]{1,0:T(8,128)(2,1)} %copy-done.2) | copy-start | bytes 2752516
  126.8 22.6 %collective-permute-start.18 = (bf16[128,3584]{1,0:T(8,128)(2,1)S(1)}, bf16[128,3584]{1,0:T(8,128)(2,1)S(1)}, u32[]{:S(2)}, u32[]{:S(2)}) collective-permute-start(bf16[128,3584]{1,0:T(8,128)(2,1)S(1)} %collective-permute-done.4.refs_2_.refs_4_.refs_8_), channel_id=1, source_target_pairs={{0,3},{1,0},{2,1},{3,2},{4,7},{5,4},{6,5},{7,6},{8,11},{9,8},{10,9... | collective-permute-start | bytes 2752520 | tf_op jit(solution)/shard_map/ppermute | solution.py:359
  131.0 20.7 %collective-permute-start.16 = (bf16[128,3584]{1,0:T(8,128)(2,1)}, bf16[128,3584]{1,0:T(8,128)(2,1)S(1)}, u32[]{:S(2)}, u32[]{:S(2)}) collective-permute-start(bf16[128,3584]{1,0:T(8,128)(2,1)} %collective-permute-done.13.refs_2_.refs_8_.refs_12_), channel_id=1, source_target_pairs={{0,8},{4,12},{8,0},{12,4},{16,24},{20,28},{24,16},{28,20},{1,9},{5... | collective-permute-start | bytes 2752520 | tf_op jit(solution)/shard_map/ppermute | solution.py:356
  131.6 20.4 %collective-permute-start.17 = (bf16[128,3584]{1,0:T(8,128)(2,1)}, bf16[128,3584]{1,0:T(8,128)(2,1)S(1)}, u32[]{:S(2)}, u32[]{:S(2)}) collective-permute-start(bf16[128,3584]{1,0:T(8,128)(2,1)} %collective-permute-done.11.refs_3_.refs_9_.refs_13_), channel_id=1, source_target_pairs={{0,16},{4,20},{8,24},{12,28},{16,0},{20,4},{24,8},{28,12},{1,17},{... | collective-permute-start | bytes 2752520 | tf_op jit(solution)/shard_map/ppermute | solution.py:356
  136.4 20.9 %copy-start.36 = (bf16[4,4,64,256]{3,2,1,0:T(8,128)(2,1)S(1)}, bf16[4,4,64,256]{3,2,1,0:T(8,128)(2,1)}, u32[]{:S(2)}) copy-start(bf16[4,4,64,256]{3,2,1,0:T(8,128)(2,1)} %get-tuple-element.134.refs_6_.refs_8_.refs_11_) | copy-start | bytes 1572868
  148.5 16.8 %copy-start.16 = (bf16[2,512,768]{2,1,0:T(8,128)(2,1)}, bf16[2,512,768]{2,1,0:T(8,128)(2,1)S(1)}, u32[]{:S(2)}) copy-start(bf16[2,512,768]{2,1,0:T(8,128)(2,1)S(1)} %get-tuple-element.178.refs_1_) | copy-start | bytes 4718596
  148.5 16.8 %copy-start.37 = (bf16[4,64,256]{2,1,0:T(8,128)(2,1)}, bf16[4,64,256]{2,1,0:T(8,128)(2,1)S(1)}, u32[]{:S(2)}) copy-start(bf16[4,64,256]{2,1,0:T(8,128)(2,1)S(1)} %get-tuple-element.202.refs_4_) | copy-start | bytes 393220
  148.5 16.8 %copy-start.39 = (bf16[4,64,256]{2,1,0:T(8,128)(2,1)}, bf16[4,64,256]{2,1,0:T(8,128)(2,1)S(1)}, u32[]{:S(2)}) copy-start(bf16[4,64,256]{2,1,0:T(8,128)(2,1)S(1)} %get-tuple-element.206.refs_8_) | copy-start | bytes 393220
  152.0 16.1 %copy-start.32 = (bf16[128,3584]{1,0:T(8,128)(2,1)S(1)}, bf16[128,3584]{1,0:T(8,128)(2,1)}, u32[]{:S(2)}) copy-start(bf16[128,3584]{1,0:T(8,128)(2,1)} %copy-done.30) | copy-start | bytes 2752516
  152.0 28.1 %collective-permute-start.21 = (bf16[4,64,256]{2,1,0:T(8,128)(2,1)}, bf16[4,64,256]{2,1,0:T(8,128)(2,1)S(1)}, u32[]{:S(2)}, u32[]{:S(2)}) collective-permute-start(bf16[4,64,256]{2,1,0:T(8,128)(2,1)} %get-tuple-element.165), channel_id=1, source_target_pairs={{0,8},{4,12},{8,0},{12,4},{16,24},{20,28},{24,16},{28,20},{1,9},{5... | collective-permute-start | bytes 393224 | tf_op jit(solution)/shard_map/ppermute | solution.py:356
  153.6 26.6 %collective-permute-start.22 = (bf16[4,64,256]{2,1,0:T(8,128)(2,1)S(1)}, bf16[4,64,256]{2,1,0:T(8,128)(2,1)}, u32[]{:S(2)}, u32[]{:S(2)}) collective-permute-start(bf16[4,64,256]{2,1,0:T(8,128)(2,1)S(1)} %get-tuple-element.166), channel_id=1, source_target_pairs={{0,16},{4,20},{8,24},{12,28},{16,0},{20,4},{24,8},{28,12},{1,17},{... | collective-permute-start | bytes 393224 | tf_op jit(solution)/shard_map/ppermute | solution.py:356
  153.9 26.3 %collective-permute-start.23 = (bf16[4,64,256]{2,1,0:T(8,128)(2,1)S(1)}, bf16[4,64,256]{2,1,0:T(8,128)(2,1)}, u32[]{:S(2)}, u32[]{:S(2)}) collective-permute-start(bf16[4,64,256]{2,1,0:T(8,128)(2,1)S(1)} %get-tuple-element.167), channel_id=1, source_target_pairs={{0,24},{4,28},{8,16},{12,20},{16,8},{20,12},{24,0},{28,4},{1,25},{... | collective-permute-start | bytes 393224 | tf_op jit(solution)/shard_map/ppermute | solution.py:356
  155.6 24.6 %collective-permute-start.19 = (bf16[128,3584]{1,0:T(8,128)(2,1)}, bf16[128,3584]{1,0:T(8,128)(2,1)S(1)}, u32[]{:S(2)}, u32[]{:S(2)}) collective-permute-start(bf16[128,3584]{1,0:T(8,128)(2,1)} %collective-permute-done.14.refs_4_.refs_10_.refs_14_), channel_id=1, source_target_pairs={{0,16},{4,20},{8,24},{12,28},{16,0},{20,4},{24,8},{28,12},{1,17},{... | collective-permute-start | bytes 2752520 | tf_op jit(solution)/shard_map/ppermute | solution.py:356
  155.9 24.4 %collective-permute-start.20 = (bf16[128,3584]{1,0:T(8,128)(2,1)}, bf16[128,3584]{1,0:T(8,128)(2,1)S(1)}, u32[]{:S(2)}, u32[]{:S(2)}) collective-permute-start(bf16[128,3584]{1,0:T(8,128)(2,1)} %collective-permute-done.9.refs_3_.refs_5_.refs_9_), channel_id=1, source_target_pairs={{0,3},{1,0},{2,1},{3,2},{4,7},{5,4},{6,5},{7,6},{8,11},{9,8},{10,9... | collective-permute-start | bytes 2752520 | tf_op jit(solution)/shard_map/ppermute | solution.py:359
  180.3 17.6 %collective-permute-start.24 = (bf16[512,3584]{1,0:T(8,128)(2,1)S(1)}, bf16[512,3584]{1,0:T(8,128)(2,1)S(1)}, u32[]{:S(2)}, u32[]{:S(2)}) collective-permute-start(bf16[512,3584]{1,0:T(8,128)(2,1)S(1)} %shard_map.79), channel_id=1, source_target_pairs={{0,4},{4,0},{8,12},{12,8},{16,20},{20,16},{24,28},{28,24},{1,5},{5... | collective-permute-start | bytes 11010056 | tf_op jit(solution)/shard_map/ppermute | solution.py:356
  180.3 14.9 %collective-permute-start.25 = (bf16[4,64,256]{2,1,0:T(8,128)(2,1)S(1)}, bf16[4,64,256]{2,1,0:T(8,128)(2,1)S(1)}, u32[]{:S(2)}, u32[]{:S(2)}) collective-permute-start(bf16[4,64,256]{2,1,0:T(8,128)(2,1)S(1)} %get-tuple-element.191), channel_id=1, source_target_pairs={{0,8},{4,12},{8,0},{12,4},{16,24},{20,28},{24,16},{28,20},{1,9},{5... | collective-permute-start | bytes 393224 | tf_op jit(solution)/shard_map/ppermute | solution.py:356
  181.0 14.9 %collective-permute-start.26 = (bf16[4,64,256]{2,1,0:T(8,128)(2,1)S(1)}, bf16[4,64,256]{2,1,0:T(8,128)(2,1)S(1)}, u32[]{:S(2)}, u32[]{:S(2)}) collective-permute-start(bf16[4,64,256]{2,1,0:T(8,128)(2,1)S(1)} %get-tuple-element.192), channel_id=1, source_target_pairs={{0,16},{4,20},{8,24},{12,28},{16,0},{20,4},{24,8},{28,12},{1,17},{... | collective-permute-start | bytes 393224 | tf_op jit(solution)/shard_map/ppermute | solution.py:356
  183.0 13.6 %collective-permute-start.27 = (bf16[4,64,256]{2,1,0:T(8,128)(2,1)S(1)}, bf16[4,64,256]{2,1,0:T(8,128)(2,1)S(1)}, u32[]{:S(2)}, u32[]{:S(2)}) collective-permute-start(bf16[4,64,256]{2,1,0:T(8,128)(2,1)S(1)} %get-tuple-element.194), channel_id=1, source_target_pairs={{0,8},{4,12},{8,0},{12,4},{16,24},{20,28},{24,16},{28,20},{1,9},{5... | collective-permute-start | bytes 393224 | tf_op jit(solution)/shard_map/ppermute | solution.py:356
  184.5 12.8 %collective-permute-start.28 = (bf16[4,64,256]{2,1,0:T(8,128)(2,1)S(1)}, bf16[4,64,256]{2,1,0:T(8,128)(2,1)S(1)}, u32[]{:S(2)}, u32[]{:S(2)}) collective-permute-start(bf16[4,64,256]{2,1,0:T(8,128)(2,1)S(1)} %get-tuple-element.195), channel_id=1, source_target_pairs={{0,8},{4,12},{8,0},{12,4},{16,24},{20,28},{24,16},{28,20},{1,9},{5... | collective-permute-start | bytes 393224 | tf_op jit(solution)/shard_map/ppermute | solution.py:356
  199.7 35.6 %collective-permute-start.37 = (bf16[512,3584]{1,0:T(8,128)(2,1)}, bf16[512,3584]{1,0:T(8,128)(2,1)}, u32[]{:S(2)}, u32[]{:S(2)}) collective-permute-start(bf16[512,3584]{1,0:T(8,128)(2,1)} %shard_map.81), channel_id=1, source_target_pairs={{0,4},{4,0},{8,12},{12,8},{16,20},{20,16},{24,28},{28,24},{1,5},{5... | collective-permute-start | bytes 11010056 | tf_op jit(solution)/shard_map/ppermute | solution.py:356
  199.7 7.6 %collective-permute-start.29 = (bf16[4,64,256]{2,1,0:T(8,128)(2,1)}, bf16[4,64,256]{2,1,0:T(8,128)(2,1)}, u32[]{:S(2)}, u32[]{:S(2)}) collective-permute-start(bf16[4,64,256]{2,1,0:T(8,128)(2,1)} %get-tuple-element.205), channel_id=1, source_target_pairs={{0,24},{4,28},{8,16},{12,20},{16,8},{20,12},{24,0},{28,4},{1,25},{... | collective-permute-start | bytes 393224 | tf_op jit(solution)/shard_map/ppermute | solution.py:356
  200.6 14.7 %collective-permute-start.30 = (bf16[4,64,256]{2,1,0:T(8,128)(2,1)}, bf16[4,64,256]{2,1,0:T(8,128)(2,1)}, u32[]{:S(2)}, u32[]{:S(2)}) collective-permute-start(bf16[4,64,256]{2,1,0:T(8,128)(2,1)} %copy-done.60), channel_id=1, source_target_pairs={{0,16},{4,20},{8,24},{12,28},{16,0},{20,4},{24,8},{28,12},{1,17},{... | collective-permute-start | bytes 393224 | tf_op jit(solution)/shard_map/ppermute | solution.py:356
  202.7 15.4 %collective-permute-start.32 = (bf16[4,64,256]{2,1,0:T(8,128)(2,1)}, bf16[4,64,256]{2,1,0:T(8,128)(2,1)}, u32[]{:S(2)}, u32[]{:S(2)}) collective-permute-start(bf16[4,64,256]{2,1,0:T(8,128)(2,1)} %copy-done.59), channel_id=1, source_target_pairs={{0,16},{4,20},{8,24},{12,28},{16,0},{20,4},{24,8},{28,12},{1,17},{... | collective-permute-start | bytes 393224 | tf_op jit(solution)/shard_map/ppermute | solution.py:356
  202.7 15.4 %collective-permute-start.31 = (bf16[4,64,256]{2,1,0:T(8,128)(2,1)}, bf16[4,64,256]{2,1,0:T(8,128)(2,1)}, u32[]{:S(2)}, u32[]{:S(2)}) collective-permute-start(bf16[4,64,256]{2,1,0:T(8,128)(2,1)} %copy-done.62), channel_id=1, source_target_pairs={{0,24},{4,28},{8,16},{12,20},{16,8},{20,12},{24,0},{28,4},{1,25},{... | collective-permute-start | bytes 393224 | tf_op jit(solution)/shard_map/ppermute | solution.py:356
  207.3 10.8 %collective-permute-start.33 = (bf16[4,64,256]{2,1,0:T(8,128)(2,1)}, bf16[4,64,256]{2,1,0:T(8,128)(2,1)}, u32[]{:S(2)}, u32[]{:S(2)}) collective-permute-start(bf16[4,64,256]{2,1,0:T(8,128)(2,1)} %copy-done.61), channel_id=1, source_target_pairs={{0,24},{4,28},{8,16},{12,20},{16,8},{20,12},{24,0},{28,4},{1,25},{... | collective-permute-start | bytes 393224 | tf_op jit(solution)/shard_map/ppermute | solution.py:356
  227.6 6.9 %collective-permute-start.36 = (f32[4,128]{1,0:T(4,128)S(1)}, f32[4,128]{1,0:T(4,128)S(1)}, u32[]{:S(2)}, u32[]{:S(2)}) collective-permute-start(f32[4,128]{1,0:T(4,128)S(1)} %get-tuple-element.243), channel_id=1, source_target_pairs={{0,1},{1,2},{2,3},{3,0},{4,5},{5,6},{6,7},{7,4},{8,9},{9,10},{10,1... | collective-permute-start | bytes 6152 | tf_op jit(solution)/shard_map/ppermute | solution.py:359
  228.1 6.5 %collective-permute-start.35 = (f32[4,128]{1,0:T(4,128)S(1)}, f32[4,128]{1,0:T(4,128)S(1)}, u32[]{:S(2)}, u32[]{:S(2)}) collective-permute-start(f32[4,128]{1,0:T(4,128)S(1)} %get-tuple-element.244), channel_id=1, source_target_pairs={{0,2},{1,3},{2,0},{3,1},{4,6},{5,7},{6,4},{7,5},{8,10},{9,11},{10,... | collective-permute-start | bytes 6152 | tf_op jit(solution)/shard_map/ppermute | solution.py:359
  228.2 6.3 %collective-permute-start.34 = (f32[4,128]{1,0:T(4,128)S(1)}, f32[4,128]{1,0:T(4,128)S(1)}, u32[]{:S(2)}, u32[]{:S(2)}) collective-permute-start(f32[4,128]{1,0:T(4,128)S(1)} %get-tuple-element.245), channel_id=1, source_target_pairs={{0,3},{1,0},{2,1},{3,2},{4,7},{5,4},{6,5},{7,6},{8,11},{9,8},{10,9... | collective-permute-start | bytes 6152 | tf_op jit(solution)/shard_map/ppermute | solution.py:359
  (58 other events, 219.7 us)
Sparse Core Ops, SparseCore 0:
  21.6 20.9 all-gather.1

commit v9 on v8

--- a/solution.py
+++ b/solution.py
@@ -134,7 +134,7 @@
     for q in range(group):
         for c in range(2):
             at = q * pair + c * block
-            weight[at : at + block, :] = weight_refs[c][0, q * block : (q + 1) * block]
+            weight[at : at + block, :] = weight_refs[c][q * block : (q + 1) * block]
     projected = nt_dot(weight[...], rows[...])
     slot_ids = lax.broadcasted_iota(jnp.int32, (slots, tokens), 0).astype(F32)
     slot_rows = lax.broadcasted_iota(jnp.int32, (slots, pair), 0)
@@ -168,9 +168,9 @@
             scatter_ref[half] = jnp.dot(order, terms[half], preferred_element_type=F32).astype(BF16)
 
 
-def project(index, items, weights, hidden, top_k, group=2):
+def project(index, items, own_weight, partner_weight, hidden, top_k, group=2):
     experts, sources, slots, pair = hidden[0].shape
-    width = weights.shape[2]
+    width = own_weight.shape[1]
     pieces = [piece for rows, _, _ in items for piece in rows]
     sizes = [p.shape[0] for p in pieces]
     count = sum(sizes)
@@ -180,8 +180,8 @@
         grid_spec=pltpu.PrefetchScalarGridSpec(
             num_scalar_prefetch=1,
             grid=(experts // group,),
-            in_specs=[pl.BlockSpec(memory_space=pl.ANY)] * len(sizes)
-            + [pl.BlockSpec((1, group * block, width), lambda e, idx, c=c: (c, e, 0)) for c in range(2)]
+            in_specs=[pl.BlockSpec(memory_space=pltpu.HBM)] * len(sizes)
+            + [pl.BlockSpec((group * block, width), lambda e, idx: (e, 0))] * 2
             + [
                 pl.BlockSpec((group, 1, slots, pair), lambda e, idx, k=k: (e, idx[k], 0, 0))
                 for _, _, k in items
@@ -202,10 +202,10 @@
         compiler_params=pltpu.CompilerParams(vmem_limit_bytes=VMEM_BYTES),
         cost_estimate=pl.CostEstimate(
             flops=4 * count * width * experts * pair,
-            bytes_accessed=2 * (count * width + weights.size),
+            bytes_accessed=2 * (count * width + 2 * own_weight.size),
             transcendentals=0,
         ),
-    )(index, *pieces, weights, weights, *[hidden[m] for _, m, _ in items])
+    )(index, *pieces, own_weight, partner_weight, *[hidden[m] for _, m, _ in items])
 
 
 def fill_rows(pieces, rows):
@@ -226,7 +226,7 @@
     return total
 
 
-def half_grad_kernel(terms, arrivals, last, idx_ref, *refs):
+def half_grad_kernel(terms, arrivals, last, *refs):
     scatters, arrived = refs[:terms], refs[terms : terms + arrivals]
     if last:
         pieces, (out_ref, rows, held) = refs[terms + arrivals : -3], refs[-3:]
@@ -252,51 +252,51 @@
     lax.fori_loop(0, block // group, move, 0, unroll=4)
 
 
-def half_grad(index, scatters, pieces, arrived, experts, tile, last):
+def half_grad(half, scatters, pieces, arrived, experts, tile, last):
     height = scatters[0].shape[1]
     width = pieces[0].shape[1]
     count = sum(p.shape[0] for p in pieces)
-    in_specs = [pl.BlockSpec((1,) + a.shape[1:], lambda i, idx: (idx[0], 0, 0)) for a in scatters]
-    in_specs += [pl.BlockSpec((height, tile), lambda i, idx: (0, i)) for _ in arrived]
-    in_specs += [pl.BlockSpec((p.shape[0], tile), lambda i, idx: (0, i)) for p in pieces]
+    in_specs = [pl.BlockSpec((1,) + a.shape[1:], lambda i: (half, 0, 0)) for a in scatters]
+    in_specs += [pl.BlockSpec((height, tile), lambda i: (0, i)) for _ in arrived]
+    in_specs += [pl.BlockSpec((p.shape[0], tile), lambda i: (0, i)) for p in pieces]
     scratch = [pltpu.VMEM((count, tile), BF16)]
     if last:
         scratch.append(pltpu.VMEM((height, tile), F32))
-        out_spec = pl.BlockSpec((height // experts, experts, tile), lambda i, idx: (0, 0, i))
+        out_spec = pl.BlockSpec((height // experts, experts, tile), lambda i: (0, 0, i))
         out_shape = jax.ShapeDtypeStruct((height // experts, experts, width), F32)
     else:
-        out_spec = pl.BlockSpec((height, tile), lambda i, idx: (0, i))
+        out_spec = pl.BlockSpec((height, tile), lambda i: (0, i))
         out_shape = jax.ShapeDtypeStruct((height, width), BF16)
     return pl.pallas_call(
         functools.partial(half_grad_kernel, len(scatters), len(arrived), last),
-        grid_spec=pltpu.PrefetchScalarGridSpec(
-            num_scalar_prefetch=1,
-            grid=(width // tile,),
-            in_specs=in_specs,
-            out_specs=out_spec,
-            scratch_shapes=scratch,
-        ),
+        grid=(width // tile,),
+        in_specs=in_specs,
+        out_specs=out_spec,
         out_shape=out_shape,
+        scratch_shapes=scratch,
         compiler_params=pltpu.CompilerParams(vmem_limit_bytes=VMEM_BYTES),
         cost_estimate=pl.CostEstimate(
             flops=2 * height * count * width,
             bytes_accessed=2 * count * (width + height) + 4 * height * width,
             transcendentals=0,
         ),
-    )(index, *scatters, *arrived, *pieces)
+    )(*scatters, *arrived, *pieces)
 
 
 def place_kernel(top_k, idx_ref, *refs):
     count = len(refs) - 5
+    block = refs[0].shape[2] // 2
     pieces, (out_ref, sum_ref, tails, out_sems, tail_sems) = refs[:count], refs[count:]
     experts, slots, pair = pieces[0].shape
     rows = tails.shape[2]
     slabs = count // 4
     stores, loads = [], []
     for i in range(count):
-        column = pl.multiple_of(idx_ref[slabs + i % 4] * pair, pair)
-        to = out_ref.at[idx_ref[i // 4], :, :, pl.ds(column, pair)]
-        stores.append(pltpu.make_async_copy(pieces[i], to, out_sems.at[i]))
+        for half in range(2):
+            column = pl.multiple_of(idx_ref[slabs + 2 * (i % 4) + half] * block, block)
+            to = out_ref.at[idx_ref[i // 4], :, :, pl.ds(column, block)]
+            part = pieces[i].at[:, :, half * block : (half + 1) * block]
+            stores.append(pltpu.make_async_copy(part, to, out_sems.at[2 * i + half]))
         loads.append(pltpu.make_async_copy(pieces[i].at[:, slots - rows :, :], tails.at[i], tail_sems.at[i]))
     for copy in loads + stores:
         copy.start()
@@ -319,14 +319,14 @@
         grid_spec=pltpu.PrefetchScalarGridSpec(
             num_scalar_prefetch=1,
             grid=(1,),
-            in_specs=[pl.BlockSpec(memory_space=pl.ANY)] * len(pieces),
+            in_specs=[pl.BlockSpec(memory_space=pltpu.HBM)] * len(pieces),
             out_specs=[
                 pl.BlockSpec(memory_space=pl.ANY),
                 pl.BlockSpec((slabs * experts, pair // 2), lambda i, idx: (0, 0)),
             ],
             scratch_shapes=[
                 pltpu.VMEM((len(pieces), experts, 16, pair), BF16),
-                pltpu.SemaphoreType.DMA((len(pieces),)),
+                pltpu.SemaphoreType.DMA((2 * len(pieces),)),
                 pltpu.SemaphoreType.DMA((len(pieces),)),
             ],
         ),
@@ -350,7 +350,7 @@
     me = lax.axis_index("exp")
     rep = lax.axis_index("rep")
     chip, core = lax.div(rep, 2), lax.rem(rep, 2)
-    chips = [jnp.bitwise_xor(chip, m) for m in range(4)]
+    blocks = [2 * jnp.bitwise_xor(chip, m) + jnp.bitwise_xor(core, c) for m in range(4) for c in range(2)]
 
     def across(array, bits):
         return lax.ppermute(array, "rep", [(i, i ^ bits) for i in range(reps)])
@@ -368,33 +368,40 @@
     index = jnp.stack(slabs + [me * experts]).astype(jnp.int32)
 
     def kernel(items):
-        *grads, scatter = project(index, items, weights, hidden, top_k)
+        *grads, scatter = project(index, items, own_weight, partner_weight, hidden, top_k)
         return grads, scatter
 
     def send_back(grads, chip_of):
         return [across(g, 2 * m) if m else g for g, m in zip(grads, chip_of)]
 
     x0, y0, next1 = across(grad_out, 2), across(grad_out, 4), around(grad_out, 1)
-    held = jnp.transpose(saved_hidden.reshape(experts, sources, most, 4, pair), (3, 0, 1, 2, 4))
+    held = jnp.transpose(saved_hidden.reshape(experts, sources, most, 8, block), (3, 0, 1, 2, 4))
     held = fence(held)
-    held = [lax.dynamic_index_in_dim(held, chips[m], axis=0, keepdims=False) for m in range(4)]
-    last_meta, down_proj, held = fence((meta, down_proj, held))
+    held = [lax.dynamic_index_in_dim(held, b, axis=0, keepdims=False) for b in blocks]
     own_weight = jnp.transpose(down_proj, (1, 0, 2)).reshape(experts * block, width)
-    cores = [[i, i + 1] for i in range(0, reps, 2)]
-    weights = lax.all_gather(own_weight, "rep", axis=0, axis_index_groups=cores)
+    last_meta, held, own_weight = fence((meta, held, own_weight))
     metas = [meta, around(meta, 1), around(meta, 2), around(last_meta, 3)]
-    metas, x0, y0, next1, held = fence((metas, x0, y0, next1, held))
+    metas, x0, y0, next1, held, own_weight = fence((metas, x0, y0, next1, held, own_weight))
 
     xy0, x1, next2 = across(x0, 4), across(next1, 2), around(next1, 1)
     own3 = around(fence((grad_out, next2))[0], -1)
+    partner_weight = across(own_weight, 1)
     metas = jnp.take(jnp.stack(metas), lax.rem(me - jnp.arange(sources) + sources, sources), axis=0)
     blank = jnp.zeros((experts, sources, SLOT_PAD - most - top_k, pair), BF16)
     metas = jnp.broadcast_to(metas[None], (experts, sources, top_k, pair))
     hidden = []
     for m in range(4):
-        piece = jnp.concatenate([held[m], blank, metas], axis=2)
-        hidden.append(across(piece, 2 * m) if m else piece)
-    hidden, xy0, x1, next2, own3, x0, y0, next1 = fence((hidden, xy0, x1, next2, own3, x0, y0, next1))
+        piece = jnp.concatenate([held[2 * m], held[2 * m + 1]], axis=3)
+        hidden.append(jnp.concatenate([piece, blank, metas], axis=2))
+    hidden = [
+        hidden[0],
+        across(fence((hidden[1], x1))[0], 2),
+        across(fence((hidden[2], xy0))[0], 4),
+        across(hidden[3], 6),
+    ]
+    hidden, xy0, x1, next2, own3, partner_weight, x0, y0, next1 = fence(
+        (hidden, xy0, x1, next2, own3, partner_weight, x0, y0, next1)
+    )
 
     y1, x2, x3 = across(next1, 4), across(next2, 2), around(x0, -1)
     grads0, scatter0 = kernel([([grad_out], 0, 0), ([x0], 1, 0), ([y0], 2, 0), ([xy0], 3, 0)])
@@ -412,7 +419,7 @@
     returned0 = send_back(grads0, (0, 1, 2, 3))
     grads2, scatter2 = kernel([([xy1], 3, 1), ([y2], 2, 2), ([own3], 0, 3), ([y3], 2, 3)])
     first = [grad_out, x0, y0, xy0, next1, x1, y1, next2, x2, x3]
-    other, mine = (1 - core).reshape(1), core.reshape(1)
+    mine, other = 0, 1
     partner = half_grad(other, [scatter0, scatter1], first, [], experts, 896, False)
     xy2, xy3, returned0, grads2, scatter2, partner, grads1 = fence(
         (xy2, xy3, returned0, grads2, scatter2, partner, grads1)
@@ -440,7 +447,7 @@
         returned2[3],
         returned3[1],
     ]
-    placed, combine = place(jnp.stack(slabs + chips).astype(jnp.int32), returned, top_k)
+    placed, combine = place(jnp.stack(slabs + blocks).astype(jnp.int32), returned, top_k)
     combine = combine.reshape(sources, experts, tokens)
     combines = [combine[0], around(combine[1], -1), around(combine[2], -2), around(combine[3], 1)]
     route_grad = 0.0

time: 258 us -> 234 us (0.907)
  between operations: 14.6 us -> 1.13 us
  local copies, waits for them, and re-layouts: 50.3 us -> 39.2 us
  Pallas kernels: 64.3 us -> 72.1 us
  starting transfers between devices: 51.9 us -> 48.8 us
  waiting for transfers between devices: 70.4 us -> 67.5 us
    unnamed x135 -> x109, local copies, waits for them, and re-layouts: 38.7 us -> 25.1 us
    ppermute x12, waiting for transfers between devices: 32.8 us -> 24.5 us  [around(): lax.ppermute(array, 'exp', [(i, (i + shift) % sources) for i in range(sou...]
    pallas_call x4, Pallas kernels: 33.7 us -> 41.2 us  [project(): pl.pallas_call(functools.partial(project_kernel, top_k, sizes, len(items)...]
    ppermute x26 -> x27, waiting for transfers between devices: 37.6 us -> 43 us  [across(): return lax.ppermute(array, 'rep', [(i, i ^ bits) for i in range(reps)])]
    ppermute x12, starting transfers between devices: 24.8 us -> 19.8 us  [around(): lax.ppermute(array, 'exp', [(i, (i + shift) % sources) for i in range(sou...]
    ppermute x26 -> x27, starting transfers between devices: 27 us -> 29 us  [across(): return lax.ppermute(array, 'rep', [(i, i ^ bits) for i in range(reps)])]
  transfers between devices with their start and end apart: 39 -> 39, of which waited for: 13 -> 13; matrix products, arithmetic and copies ran while one was open for 3% -> 9% of each run, Pallas kernels for 19% -> 25%
where the time goes in v9:
time: 234 us
  Pallas kernels  72.1 us (31%)
  waiting for transfers between devices  67.5 us (29%)
  starting transfers between devices  48.8 us (21%)
  local copies, waits for them, and re-layouts  39.2 us (17%)
  other arithmetic  4.79 us (2%)
    ppermute x27, waiting for transfers between devices, across(): return lax.ppermute(array, 'rep', [(i, i ^ bits) for i in range(reps)])  43 us
    pallas_call x4, Pallas kernels, project(): pl.pallas_call(functools.partial(project_kernel, top_k, sizes, len(items)...  41.2 us
    ppermute x27, starting transfers between devices, across(): return lax.ppermute(array, 'rep', [(i, i ^ bits) for i in range(reps)])  29 us
    pallas_call x3, Pallas kernels, half_grad(): pl.pallas_call(functools.partial(half_grad_kernel, len(scatters), len(arr...  28.4 us
    unnamed x109, local copies, waits for them, and re-layouts  25.1 us
    ppermute x12, waiting for transfers between devices, around(): lax.ppermute(array, 'exp', [(i, (i + shift) % sources) for i in range(sou...  24.5 us
    ppermute x12, starting transfers between devices, around(): lax.ppermute(array, 'exp', [(i, (i + shift) % sources) for i in range(sou...  19.8 us
    reshape x2, local copies, waits for them, and re-layouts, on_device_tokens(): saved_hidden.reshape(experts, sources, most, 8, block)  7.92 us
  transfers between devices with their start and end apart: 39, of which 13 were waited for; matrix products, arithmetic and copies ran while one was open for 9% of the time, Pallas kernels for 25%

profile of v9, /device:TPU:0, one launch (start us, length us, event | category | flops | bytes accessed | tf_op | source)
XLA Modules:
  0.0 233.7 jit_solution(16714429700389651866)
XLA Ops:
  0.6 3.1 %collective-permute-start.5 = (bf16[128,3584]{1,0:T(8,128)(2,1)}, bf16[128,3584]{1,0:T(8,128)(2,1)S(1)}, u32[]{:S(2)}, u32[]{:S(2)}) collective-permute-start(bf16[128,3584]{1,0:T(8,128)(2,1)} %refs_6_.1), channel_id=1, source_target_pairs={{0,1},{1,2},{2,3},{3,0},{4,5},{5,6},{6,7},{7,4},{8,9},{9,10},{10,1... | collective-permute-start | bytes 2752520 | tf_op jit(solution)/shard_map/ppermute | solution.py:359
  3.7 1.5 collective-permute-start.4
  5.2 1.5 collective-permute-start.3
  8.8 2.7 %collective-permute-start.1 = (bf16[4,256]{1,0:T(4,128)(2,1)S(1)}, bf16[4,256]{1,0:T(4,128)(2,1)S(1)}, u32[]{:S(2)}, u32[]{:S(2)}) collective-permute-start(bf16[4,256]{1,0:T(4,128)(2,1)S(1)} %pad_maximum_fusion.5), channel_id=1, source_target_pairs={{0,2},{1,3},{2,0},{3,1},{4,6},{5,7},{6,4},{7,5},{8,10},{9,11},{10,... | collective-permute-start | bytes 6152 | tf_op jit(solution)/shard_map/ppermute | solution.py:359
  11.7 4.3 %reshape.91 = bf16[4,4,60,8,128]{4,3,1,2,0:T(8,128)(2,1)} reshape(bf16[1,4,4,60,1024]{4,2,3,1,0:T(4,128)(2,1)} %param.8) | data formatting | bytes 3932160 | tf_op jit(solution)/shard_map/reshape | solution.py:378
  16.0 3.6 %copy.15 = bf16[4,4,60,8,128]{4,2,1,0,3:T(8,128)(2,1)} copy(bf16[4,4,60,8,128]{4,3,1,2,0:T(8,128)(2,1)} %reshape.91) | data formatting | bytes 3932160 | tf_op jit(solution)/shard_map/reshape | solution.py:378
  19.6 2.9 %dynamic-slice_bitcast_fusion = (bf16[4,4,60,128]{3,2,1,0:T(8,128)(2,1)S(1)}, bf16[4,4,60,128]{3,2,1,0:T(8,128)(2,1)}, bf16[4,4,60,128]{3,2,1,0:T(8,128)(2,1)}, ...) fusion(bf16[8,4,4,60,128]{4,3,2,1,0:T(8,128)(2,1)} %bitcast.58,, ...), kind=kLoop, calls=%fused_computation.7 | loop fusion | bytes 3932192 | tf_op jit(solution)/shard_map/jit(dynamic_index_in_dim)/squeeze | solution.py:380
  22.5 2.4 %copy.12 = bf16[4,128,3584]{2,1,0:T(8,128)(2,1)} copy(bf16[4,128,3584]{2,0,1:T(4,128)(2,1)S(1)} %bitcast.59) | data formatting | bytes 7340032 | tf_op jit(solution)/shard_map/transpose | solution.py:381
  24.9 3.6 %collective-permute-start.2 = (bf16[4,256]{1,0:T(4,128)(2,1)S(1)}, bf16[4,256]{1,0:T(4,128)(2,1)S(1)}, u32[]{:S(2)}, u32[]{:S(2)}) collective-permute-start(bf16[4,256]{1,0:T(4,128)(2,1)S(1)} %pad_maximum_fusion.5), channel_id=1, source_target_pairs={{0,3},{1,0},{2,1},{3,2},{4,7},{5,4},{6,5},{7,6},{8,11},{9,8},{10,9... | collective-permute-start | bytes 6152 | tf_op jit(solution)/shard_map/ppermute | solution.py:359
  28.5 1.3 collective-permute-done.2
  30.7 1.5 collective-permute-start.8
  32.2 1.5 collective-permute-start.6
  33.8 21.4 %collective-permute-done.11.refs_3_.refs_9_.refs_13_ = bf16[128,3584]{1,0:T(8,128)(2,1)} collective-permute-done((bf16[128,3584]{1,0:T(8,128)(2,1)S(1)}, bf16[128,3584]{1,0:T(8,128)(2,1)}, u32[]{:S(2)}, u32[]{:S(2)}) %collective-permute-start.11) | collective-permute-done | bytes 917536 | tf_op jit(solution)/shard_map/ppermute | solution.py:359
  55.1 1.7 collective-permute-start.12
  57.6 1.9 pad_maximum_fusion
  59.4 2.1 collective-permute-start.10
  63.0 12.3 %collective-permute-done.10.refs_9_.refs_6_.refs_4_.refs_5_ = bf16[4,4,64,256]{3,2,1,0:T(8,128)(2,1)S(1)} collective-permute-done((bf16[4,4,64,256]{3,2,1,0:T(8,128)(2,1)S(1)}, bf16[4,4,64,256]{3,2,1,0:T(8,128)(2,1)S(1)}, u32[]{:S(2)}, u32[]{:S(2)}) %collective-permute-start.10) | collective-permute-done | bytes 524320 | tf_op jit(solution)/shard_map/ppermute | solution.py:356
  76.1 8.7 %collective-permute-done.9.refs_8_.refs_10_.refs_7_.refs_9_ = bf16[4,4,64,256]{3,2,1,0:T(8,128)(2,1)S(1)} collective-permute-done((bf16[4,4,64,256]{3,2,1,0:T(8,128)(2,1)S(1)}, bf16[4,4,64,256]{3,2,1,0:T(8,128)(2,1)S(1)}, u32[]{:S(2)}, u32[]{:S(2)}) %collective-permute-start.9) | collective-permute-done | bytes 524320 | tf_op jit(solution)/shard_map/ppermute | solution.py:356
  87.5 1.2 collective-permute-start.14
  92.3 10.4 %shard_map.76 = (bf16[4,64,256]{2,1,0:T(8,128)(2,1)S(1)}, bf16[4,64,256]{2,1,0:T(8,128)(2,1)S(1)}, bf16[4,64,256]{2,1,0:T(8,128)(2,1)S(1)}, bf16[4,64,256]{2,1,0:T(8,128)(2,1)S(1)}, bf16[2,512,512]{2,1,0:T(8,128)(2,1)S(1)}) custom-call(s32[5]{0:T(128)S(1)} %stack.83.idx_ref, bf16[128,3584]{1,0:T(8,128)(2,1)S(1)} %copy-done.11, ...), custom_call_target="tpu_custom_call" | custom-call | flops 7516192768 | bytes 11010048 | tf_op jit(solution)/shard_map/pallas_call | solution.py:178
  102.7 6.3 %collective-permute-done.15.refs_4_.refs_10_.refs_14_ = bf16[128,3584]{1,0:T(8,128)(2,1)} collective-permute-done((bf16[128,3584]{1,0:T(8,128)(2,1)}, bf16[128,3584]{1,0:T(8,128)(2,1)}, u32[]{:S(2)}, u32[]{:S(2)}) %collective-permute-start.15) | collective-permute-done | bytes 917536 | tf_op jit(solution)/shard_map/ppermute | solution.py:356
  110.4 2.1 collective-permute-start.19
  112.5 1.2 collective-permute-start.17
  114.6 14.1 %shard_map.77 = (bf16[4,64,256]{2,1,0:T(8,128)(2,1)S(1)}, bf16[4,64,256]{2,1,0:T(8,128)(2,1)S(1)}, bf16[4,64,256]{2,1,0:T(8,128)(2,1)S(1)}, bf16[4,64,256]{2,1,0...) custom-call(s32[5]{0:T(128)S(1)} %stack.83.idx_ref, ...), custom_call_target="tpu_custom_call" | custom-call | flops 11274289152 | bytes 12845056 | tf_op jit(solution)/shard_map/pallas_call | solution.py:178
  131.1 1.8 collective-permute-done.17.refs_0_.refs_2_.refs_16_
  132.9 1.3 collective-permute-done.18.refs_1_.refs_3_.refs_17_
  134.6 1.5 collective-permute-start.23
  136.1 1.5 collective-permute-start.24
  138.5 1.5 collective-permute-start.21
  140.0 10.0 %shard_map.78 = (bf16[4,64,256]{2,1,0:T(8,128)(2,1)}, bf16[4,64,256]{2,1,0:T(8,128)(2,1)S(1)}, bf16[4,64,256]{2,1,0:T(8,128)(2,1)S(1)}, bf16[4,64,256]{2,1,0:T(8,128)(2,1)S(1)}, bf16[2,512,512]{2,1,0:T(8,128)(2,1)S(1)}) custom-call(s32[5]{0:T(128)S(1)} %stack.83.idx_ref, bf16[128,3584]{1,0:T(8,128)(2,1)S(1)} %collective-permute-done.17.refs_0_.refs_2_.refs_16_, ...), custom_call_target="tpu_custom_call" | custom-call | flops 7516192768 | bytes 11010048 | tf_op jit(solution)/shard_map/pallas_call | solution.py:178
  152.0 8.3 %shard_map.79 = bf16[512,3584]{1,0:T(8,128)(2,1)S(1)} custom-call(bf16[2,512,512]{2,1,0:T(8,128)(2,1)S(1)} %get-tuple-element.201.refs_0_, bf16[2,512,768]{2,1,0:T(8,128)(2,1)S(1)} %get-tuple-element.202.refs_1_, bf16[128,3584]{1,0:T(8,128)(2,1)S(1)} %copy-done.12, bf16[128,3584]{1,0:T(8,128)(2,1)} %collective-permute-done.3.refs_1_.refs_3_.refs_7_, ...), custom_call_target="tpu_custom_call" | custom-call | flops 4697620480 | bytes 17825792 | tf_op jit(solution)/shard_map/pallas_call | solution.py:270
  161.5 1.1 collective-permute-start.27
  163.1 1.5 collective-permute-start.29
  164.6 6.7 %shard_map.80 = (bf16[4,64,256]{2,1,0:T(8,128)(2,1)S(1)}, bf16[4,64,256]{2,1,0:T(8,128)(2,1)S(1)}, bf16[2,512,256]{2,1,0:T(8,128)(2,1)S(1)}) custom-call(s32[5]{0:T(128)S(1)} %stack.83.idx_ref, bf16[128,3584]{1,0:T(8,128)(2,1)S(1)} %collective-permute-done.20.refs_0_.refs_6_.refs_20_, bf16[128,3584]{1,0:T(8,128)(2,1)S(1)} %collective-permute-done.21.refs_1_.refs_7_.refs_21_, ...), custom_call_target="tpu_custom_call" | custom-call | flops 3758096384 | bytes 9175040 | tf_op jit(solution)/shard_map/pallas_call | solution.py:178
  171.4 5.5 %shard_map.81 = bf16[512,3584]{1,0:T(8,128)(2,1)} custom-call(bf16[2,512,512]{2,1,0:T(8,128)(2,1)S(1)} %get-tuple-element.220.refs_0_.refs_2_, bf16[2,512,256]{2,1,0:T(8,128)(2,1)S(1)} %get-tuple-element.240.refs_1_.refs_3_, bf16[128,3584]{1,0:T(8,128)(2,1)S(1)} %collective-permute-done.17.refs_0_.refs_2_.refs_16_, ...), custom_call_target="tpu_custom_call" | custom-call | flops 2818572288 | bytes 13631488 | tf_op jit(solution)/shard_map/pallas_call | solution.py:270
  179.5 1.8 copy-done.51
  181.3 1.4 collective-permute-start.30
  183.3 1.5 collective-permute-start.33
  184.8 1.5 collective-permute-start.32
  186.3 2.4 %collective-permute-done.30.refs_7_ = bf16[4,64,256]{2,1,0:T(8,128)(2,1)} collective-permute-done((bf16[4,64,256]{2,1,0:T(8,128)(2,1)}, bf16[4,64,256]{2,1,0:T(8,128)(2,1)}, u32[]{:S(2)}, u32[]{:S(2)}) %collective-permute-start.30) | collective-permute-done | bytes 131104 | tf_op jit(solution)/shard_map/ppermute | solution.py:356
  188.7 1.4 collective-permute-start.34
  190.2 6.7 %collective-permute-done.31.refs_10_ = bf16[4,64,256]{2,1,0:T(8,128)(2,1)} collective-permute-done((bf16[4,64,256]{2,1,0:T(8,128)(2,1)}, bf16[4,64,256]{2,1,0:T(8,128)(2,1)}, u32[]{:S(2)}, u32[]{:S(2)}) %collective-permute-start.31) | collective-permute-done | bytes 131104 | tf_op jit(solution)/shard_map/ppermute | solution.py:356
  196.9 2.7 %collective-permute-done.33.refs_14_ = bf16[4,64,256]{2,1,0:T(8,128)(2,1)} collective-permute-done((bf16[4,64,256]{2,1,0:T(8,128)(2,1)}, bf16[4,64,256]{2,1,0:T(8,128)(2,1)}, u32[]{:S(2)}, u32[]{:S(2)}) %collective-permute-start.33) | collective-permute-done | bytes 131104 | tf_op jit(solution)/shard_map/ppermute | solution.py:356
  208.7 2.5 %shard_map.82 = (bf16[4,4,64,1024]{3,2,1,0:T(8,128)(2,1)S(1)}, f32[16,128]{1,0:T(8,128)S(1)}) custom-call(s32[12]{0:T(128)S(1)} %stack.76.idx_ref, bf16[4,64,256]{2,1,0:T(8,128)(2,1)S(1)} %get-tuple-element.209.refs_0_, bf16[4,64,256]{2,1,0:T(8,128)(2,1)S(1)} %copy-done.22, bf16[4,64,256]{2,1,0:T(8,128)(2,1)S(1)} %copy-done.24, ...), custom_call_target="tpu_custom_call" | custom-call | bytes 4194304 | tf_op jit(solution)/shard_map/pallas_call | solution.py:317
  211.4 1.8 collective-permute-start.36
  213.3 1.9 collective-permute-start.35
  215.4 2.8 %copy.13 = bf16[1,4,4,60,1024]{4,2,3,1,0:T(4,128)(2,1)} copy(bf16[1,4,4,60,1024]{4,3,1,2,0:T(8,128)(2,1)S(1)} %slice_bitcast_fusion) | data formatting | bytes 3932160
  219.0 14.6 %shard_map.83 = f32[128,4,3584]{2,1,0:T(4,128)} custom-call(bf16[2,512,512]{2,1,0:T(8,128)(2,1)S(1)} %copy-done.10, bf16[2,512,768]{2,1,0:T(8,128)(2,1)} %copy-done.8, bf16[2,512,512]{2,1,0:T(8,128)(2,1)S(1)} %get-tuple-element.220.refs_0_.refs_2_, bf16[2,512,256]{2,1,0:T(8,128)(2,1)S(1)} %get-tuple-element.240.refs_1_.refs_3_, ...), custom_call_target="tpu_custom_call" | custom-call | flops 7516192768 | bytes 24117248 | tf_op jit(solution)/shard_map/pallas_call | solution.py:270
  (172 shorter events, 35.2 us)
Async XLA Ops:
  0.6 29.2 %collective-permute-start.5 = (bf16[128,3584]{1,0:T(8,128)(2,1)}, bf16[128,3584]{1,0:T(8,128)(2,1)S(1)}, u32[]{:S(2)}, u32[]{:S(2)}) collective-permute-start(bf16[128,3584]{1,0:T(8,128)(2,1)} %refs_6_.1), channel_id=1, source_target_pairs={{0,1},{1,2},{2,3},{3,0},{4,5},{5,6},{6,7},{7,4},{8,9},{9,10},{10,1... | collective-permute-start | bytes 2752520 | tf_op jit(solution)/shard_map/ppermute | solution.py:359
  3.7 26.1 %collective-permute-start.4 = (bf16[128,3584]{1,0:T(8,128)(2,1)}, bf16[128,3584]{1,0:T(8,128)(2,1)}, u32[]{:S(2)}, u32[]{:S(2)}) collective-permute-start(bf16[128,3584]{1,0:T(8,128)(2,1)} %refs_6_.1), channel_id=1, source_target_pairs={{0,16},{4,20},{8,24},{12,28},{16,0},{20,4},{24,8},{28,12},{1,17},{... | collective-permute-start | bytes 2752520 | tf_op jit(solution)/shard_map/ppermute | solution.py:356
  5.2 24.6 %collective-permute-start.3 = (bf16[128,3584]{1,0:T(8,128)(2,1)}, bf16[128,3584]{1,0:T(8,128)(2,1)}, u32[]{:S(2)}, u32[]{:S(2)}) collective-permute-start(bf16[128,3584]{1,0:T(8,128)(2,1)} %refs_6_.1), channel_id=1, source_target_pairs={{0,8},{4,12},{8,0},{12,4},{16,24},{20,28},{24,16},{28,20},{1,9},{5... | collective-permute-start | bytes 2752520 | tf_op jit(solution)/shard_map/ppermute | solution.py:356
  8.8 16.1 %collective-permute-start.1 = (bf16[4,256]{1,0:T(4,128)(2,1)S(1)}, bf16[4,256]{1,0:T(4,128)(2,1)S(1)}, u32[]{:S(2)}, u32[]{:S(2)}) collective-permute-start(bf16[4,256]{1,0:T(4,128)(2,1)S(1)} %pad_maximum_fusion.5), channel_id=1, source_target_pairs={{0,2},{1,3},{2,0},{3,1},{4,6},{5,7},{6,4},{7,5},{8,10},{9,11},{10,... | collective-permute-start | bytes 6152 | tf_op jit(solution)/shard_map/ppermute | solution.py:359
  11.4 17.1 %collective-permute-start = (bf16[4,256]{1,0:T(4,128)(2,1)S(1)}, bf16[4,256]{1,0:T(4,128)(2,1)S(1)}, u32[]{:S(2)}, u32[]{:S(2)}) collective-permute-start(bf16[4,256]{1,0:T(4,128)(2,1)S(1)} %pad_maximum_fusion.5), channel_id=1, source_target_pairs={{0,1},{1,2},{2,3},{3,0},{4,5},{5,6},{6,7},{7,4},{8,9},{9,10},{10,1... | collective-permute-start | bytes 6152 | tf_op jit(solution)/shard_map/ppermute | solution.py:359
  22.5 32.7 %copy-start.11 = (bf16[128,3584]{1,0:T(8,128)(2,1)S(1)}, bf16[128,3584]{1,0:T(8,128)(2,1)}, u32[]{:S(2)}) copy-start(bf16[128,3584]{1,0:T(8,128)(2,1)} %refs_6_.1) | copy-start | bytes 2752516
  24.9 4.9 %collective-permute-start.2 = (bf16[4,256]{1,0:T(4,128)(2,1)S(1)}, bf16[4,256]{1,0:T(4,128)(2,1)S(1)}, u32[]{:S(2)}, u32[]{:S(2)}) collective-permute-start(bf16[4,256]{1,0:T(4,128)(2,1)S(1)} %pad_maximum_fusion.5), channel_id=1, source_target_pairs={{0,3},{1,0},{2,1},{3,2},{4,7},{5,4},{6,5},{7,6},{8,11},{9,8},{10,9... | collective-permute-start | bytes 6152 | tf_op jit(solution)/shard_map/ppermute | solution.py:359
  29.8 57.7 %copy-start.14 = (bf16[128,3584]{1,0:T(8,128)(2,1)}, bf16[128,3584]{1,0:T(8,128)(2,1)S(1)}, u32[]{:S(2)}) copy-start(bf16[128,3584]{1,0:T(8,128)(2,1)S(1)} %collective-permute-done.5.refs_0_.refs_6_.refs_10_) | copy-start | bytes 2752516
  29.9 56.6 %collective-permute-start.13 = (bf16[512,3584]{1,0:T(8,128)(2,1)}, bf16[512,3584]{1,0:T(8,128)(2,1)}, u32[]{:S(2)}, u32[]{:S(2)}) collective-permute-start(bf16[512,3584]{1,0:T(8,128)(2,1)} %bitcast.25.refs_4_.refs_6_.refs_2_), channel_id=1, source_target_pairs={{0,4},{4,0},{8,12},{12,8},{16,20},{20,16},{24,28},{28,24},{1,5},{5... | collective-permute-start | bytes 11010056 | tf_op jit(solution)/shard_map/ppermute | solution.py:356
  29.9 25.2 %collective-permute-start.11 = (bf16[128,3584]{1,0:T(8,128)(2,1)S(1)}, bf16[128,3584]{1,0:T(8,128)(2,1)}, u32[]{:S(2)}, u32[]{:S(2)}) collective-permute-start(bf16[128,3584]{1,0:T(8,128)(2,1)S(1)} %collective-permute-done.5.refs_0_.refs_6_.refs_10_), channel_id=1, source_target_pairs={{0,1},{1,2},{2,3},{3,0},{4,5},{5,6},{6,7},{7,4},{8,9},{9,10},{10,1... | collective-permute-start | bytes 2752520 | tf_op jit(solution)/shard_map/ppermute | solution.py:359
  30.7 30.8 %collective-permute-start.8 = (bf16[128,3584]{1,0:T(8,128)(2,1)}, bf16[128,3584]{1,0:T(8,128)(2,1)}, u32[]{:S(2)}, u32[]{:S(2)}) collective-permute-start(bf16[128,3584]{1,0:T(8,128)(2,1)} %collective-permute-done.3.refs_1_.refs_3_.refs_7_), channel_id=1, source_target_pairs={{0,16},{4,20},{8,24},{12,28},{16,0},{20,4},{24,8},{28,12},{1,17},{... | collective-permute-start | bytes 2752520 | tf_op jit(solution)/shard_map/ppermute | solution.py:356
  32.2 29.8 %collective-permute-start.6 = (bf16[128,3584]{1,0:T(8,128)(2,1)S(1)}, bf16[128,3584]{1,0:T(8,128)(2,1)}, u32[]{:S(2)}, u32[]{:S(2)}) collective-permute-start(bf16[128,3584]{1,0:T(8,128)(2,1)S(1)} %collective-permute-done.5.refs_0_.refs_6_.refs_10_), channel_id=1, source_target_pairs={{0,8},{4,12},{8,0},{12,4},{16,24},{20,28},{24,16},{28,20},{1,9},{5... | collective-permute-start | bytes 2752520 | tf_op jit(solution)/shard_map/ppermute | solution.py:356
  55.1 31.3 %collective-permute-start.12 = (bf16[128,3584]{1,0:T(8,128)(2,1)S(1)}, bf16[128,3584]{1,0:T(8,128)(2,1)S(1)}, u32[]{:S(2)}, u32[]{:S(2)}) collective-permute-start(bf16[128,3584]{1,0:T(8,128)(2,1)S(1)} %copy-done.11), channel_id=1, source_target_pairs={{0,3},{1,0},{2,1},{3,2},{4,7},{5,4},{6,5},{7,6},{8,11},{9,8},{10,9... | collective-permute-start | bytes 2752520 | tf_op jit(solution)/shard_map/ppermute | solution.py:359
  59.4 15.9 %collective-permute-start.10 = (bf16[4,4,64,256]{3,2,1,0:T(8,128)(2,1)S(1)}, bf16[4,4,64,256]{3,2,1,0:T(8,128)(2,1)S(1)}, u32[]{:S(2)}, u32[]{:S(2)}) collective-permute-start(bf16[4,4,64,256]{3,2,1,0:T(8,128)(2,1)S(1)} %get-tuple-element.263), channel_id=1, source_target_pairs={{0,24},{4,28},{8,16},{12,20},{16,8},{20,12},{24,0},{28,4},{1,25},{... | collective-permute-start | bytes 1572872 | tf_op jit(solution)/shard_map/ppermute | solution.py:356
  61.5 23.3 %collective-permute-start.9 = (bf16[4,4,64,256]{3,2,1,0:T(8,128)(2,1)S(1)}, bf16[4,4,64,256]{3,2,1,0:T(8,128)(2,1)S(1)}, u32[]{:S(2)}, u32[]{:S(2)}) collective-permute-start(bf16[4,4,64,256]{3,2,1,0:T(8,128)(2,1)S(1)} %get-tuple-element.146), channel_id=1, source_target_pairs={{0,16},{4,20},{8,24},{12,28},{16,0},{20,4},{24,8},{28,12},{1,17},{... | collective-permute-start | bytes 1572872 | tf_op jit(solution)/shard_map/ppermute | solution.py:356
  62.0 23.6 %collective-permute-start.7 = (bf16[4,4,64,256]{3,2,1,0:T(8,128)(2,1)S(1)}, bf16[4,4,64,256]{3,2,1,0:T(8,128)(2,1)S(1)}, u32[]{:S(2)}, u32[]{:S(2)}) collective-permute-start(bf16[4,4,64,256]{3,2,1,0:T(8,128)(2,1)S(1)} %get-tuple-element.142), channel_id=1, source_target_pairs={{0,8},{4,12},{8,0},{12,4},{16,24},{20,28},{24,16},{28,20},{1,9},{5... | collective-permute-start | bytes 1572872 | tf_op jit(solution)/shard_map/ppermute | solution.py:356
  86.4 22.6 %collective-permute-start.15 = (bf16[128,3584]{1,0:T(8,128)(2,1)}, bf16[128,3584]{1,0:T(8,128)(2,1)}, u32[]{:S(2)}, u32[]{:S(2)}) collective-permute-start(bf16[128,3584]{1,0:T(8,128)(2,1)} %collective-permute-done.11.refs_3_.refs_9_.refs_13_), channel_id=1, source_target_pairs={{0,8},{4,12},{8,0},{12,4},{16,24},{20,28},{24,16},{28,20},{1,9},{5... | collective-permute-start | bytes 2752520 | tf_op jit(solution)/shard_map/ppermute | solution.py:356
  87.5 22.1 %collective-permute-start.14 = (bf16[128,3584]{1,0:T(8,128)(2,1)S(1)}, bf16[128,3584]{1,0:T(8,128)(2,1)}, u32[]{:S(2)}, u32[]{:S(2)}) collective-permute-start(bf16[128,3584]{1,0:T(8,128)(2,1)S(1)} %collective-permute-done.5.refs_0_.refs_6_.refs_10_), channel_id=1, source_target_pairs={{0,16},{4,20},{8,24},{12,28},{16,0},{20,4},{24,8},{28,12},{1,17},{... | collective-permute-start | bytes 2752520 | tf_op jit(solution)/shard_map/ppermute | solution.py:356
  88.8 21.7 %collective-permute-start.16 = (bf16[128,3584]{1,0:T(8,128)(2,1)}, bf16[128,3584]{1,0:T(8,128)(2,1)}, u32[]{:S(2)}, u32[]{:S(2)}) collective-permute-start(bf16[128,3584]{1,0:T(8,128)(2,1)} %collective-permute-done.3.refs_1_.refs_3_.refs_7_), channel_id=1, source_target_pairs={{0,3},{1,0},{2,1},{3,2},{4,7},{5,4},{6,5},{7,6},{8,11},{9,8},{10,9... | collective-permute-start | bytes 2752520 | tf_op jit(solution)/shard_map/ppermute | solution.py:359
  92.2 22.4 %copy-start.15 = (bf16[128,3584]{1,0:T(8,128)(2,1)S(1)}, bf16[128,3584]{1,0:T(8,128)(2,1)}, u32[]{:S(2)}) copy-start(bf16[128,3584]{1,0:T(8,128)(2,1)} %copy-done.14) | copy-start | bytes 2752516
  92.2 22.4 %copy-start.42 = (bf16[4,4,64,256]{3,2,1,0:T(8,128)(2,1)S(1)}, bf16[4,4,64,256]{3,2,1,0:T(8,128)(2,1)}, u32[]{:S(2)}) copy-start(bf16[4,4,64,256]{3,2,1,0:T(8,128)(2,1)} %copy-done.40) | copy-start | bytes 1572868
  92.2 22.4 %copy-start.45 = (bf16[4,4,64,256]{3,2,1,0:T(8,128)(2,1)S(1)}, bf16[4,4,64,256]{3,2,1,0:T(8,128)(2,1)}, u32[]{:S(2)}) copy-start(bf16[4,4,64,256]{3,2,1,0:T(8,128)(2,1)} %copy-done.43) | copy-start | bytes 1572868
  102.7 47.4 %copy-start.9 = (bf16[2,512,512]{2,1,0:T(8,128)(2,1)}, bf16[2,512,512]{2,1,0:T(8,128)(2,1)S(1)}, u32[]{:S(2)}) copy-start(bf16[2,512,512]{2,1,0:T(8,128)(2,1)S(1)} %get-tuple-element.201.refs_0_) | copy-start | bytes 3145732
  110.4 29.6 %copy-start.39 = (bf16[4,4,64,256]{3,2,1,0:T(8,128)(2,1)S(1)}, bf16[4,4,64,256]{3,2,1,0:T(8,128)(2,1)}, u32[]{:S(2)}) copy-start(bf16[4,4,64,256]{3,2,1,0:T(8,128)(2,1)} %copy-done.37) | copy-start | bytes 1572868
  110.4 20.6 %collective-permute-start.19 = (bf16[128,3584]{1,0:T(8,128)(2,1)}, bf16[128,3584]{1,0:T(8,128)(2,1)S(1)}, u32[]{:S(2)}, u32[]{:S(2)}) collective-permute-start(bf16[128,3584]{1,0:T(8,128)(2,1)} %collective-permute-done.4.refs_2_.refs_4_.refs_8_), channel_id=1, source_target_pairs={{0,3},{1,0},{2,1},{3,2},{4,7},{5,4},{6,5},{7,6},{8,11},{9,8},{10,9... | collective-permute-start | bytes 2752520 | tf_op jit(solution)/shard_map/ppermute | solution.py:359
  112.5 20.4 %collective-permute-start.17 = (bf16[128,3584]{1,0:T(8,128)(2,1)}, bf16[128,3584]{1,0:T(8,128)(2,1)S(1)}, u32[]{:S(2)}, u32[]{:S(2)}) collective-permute-start(bf16[128,3584]{1,0:T(8,128)(2,1)} %collective-permute-done.14.refs_2_.refs_8_.refs_12_), channel_id=1, source_target_pairs={{0,8},{4,12},{8,0},{12,4},{16,24},{20,28},{24,16},{28,20},{1,9},{5... | collective-permute-start | bytes 2752520 | tf_op jit(solution)/shard_map/ppermute | solution.py:356
  113.7 20.4 %collective-permute-start.18 = (bf16[128,3584]{1,0:T(8,128)(2,1)}, bf16[128,3584]{1,0:T(8,128)(2,1)S(1)}, u32[]{:S(2)}, u32[]{:S(2)}) collective-permute-start(bf16[128,3584]{1,0:T(8,128)(2,1)} %collective-permute-done.11.refs_3_.refs_9_.refs_13_), channel_id=1, source_target_pairs={{0,16},{4,20},{8,24},{12,28},{16,0},{20,4},{24,8},{28,12},{1,17},{... | collective-permute-start | bytes 2752520 | tf_op jit(solution)/shard_map/ppermute | solution.py:356
  132.9 38.5 %copy-start = (bf16[128,3584]{1,0:T(8,128)(2,1)}, bf16[128,3584]{1,0:T(8,128)(2,1)S(1)}, u32[]{:S(2)}) copy-start(bf16[128,3584]{1,0:T(8,128)(2,1)S(1)} %collective-permute-done.17.refs_0_.refs_2_.refs_16_) | copy-start | bytes 2752516
  134.1 37.3 %copy-start.2 = (bf16[128,3584]{1,0:T(8,128)(2,1)}, bf16[128,3584]{1,0:T(8,128)(2,1)S(1)}, u32[]{:S(2)}) copy-start(bf16[128,3584]{1,0:T(8,128)(2,1)S(1)} %collective-permute-done.18.refs_1_.refs_3_.refs_17_) | copy-start | bytes 2752516
  134.1 26.2 %collective-permute-start.22 = (bf16[4,64,256]{2,1,0:T(8,128)(2,1)S(1)}, bf16[4,64,256]{2,1,0:T(8,128)(2,1)S(1)}, u32[]{:S(2)}, u32[]{:S(2)}) collective-permute-start(bf16[4,64,256]{2,1,0:T(8,128)(2,1)S(1)} %get-tuple-element.189), channel_id=1, source_target_pairs={{0,8},{4,12},{8,0},{12,4},{16,24},{20,28},{24,16},{28,20},{1,9},{5... | collective-permute-start | bytes 393224 | tf_op jit(solution)/shard_map/ppermute | solution.py:356
  134.6 25.7 %collective-permute-start.23 = (bf16[4,64,256]{2,1,0:T(8,128)(2,1)S(1)}, bf16[4,64,256]{2,1,0:T(8,128)(2,1)S(1)}, u32[]{:S(2)}, u32[]{:S(2)}) collective-permute-start(bf16[4,64,256]{2,1,0:T(8,128)(2,1)S(1)} %get-tuple-element.190), channel_id=1, source_target_pairs={{0,16},{4,20},{8,24},{12,28},{16,0},{20,4},{24,8},{28,12},{1,17},{... | collective-permute-start | bytes 393224 | tf_op jit(solution)/shard_map/ppermute | solution.py:356
  136.1 24.2 %collective-permute-start.24 = (bf16[4,64,256]{2,1,0:T(8,128)(2,1)S(1)}, bf16[4,64,256]{2,1,0:T(8,128)(2,1)S(1)}, u32[]{:S(2)}, u32[]{:S(2)}) collective-permute-start(bf16[4,64,256]{2,1,0:T(8,128)(2,1)S(1)} %get-tuple-element.191), channel_id=1, source_target_pairs={{0,24},{4,28},{8,16},{12,20},{16,8},{20,12},{24,0},{28,4},{1,25},{... | collective-permute-start | bytes 393224 | tf_op jit(solution)/shard_map/ppermute | solution.py:356
  137.6 22.7 %collective-permute-start.20 = (bf16[128,3584]{1,0:T(8,128)(2,1)}, bf16[128,3584]{1,0:T(8,128)(2,1)S(1)}, u32[]{:S(2)}, u32[]{:S(2)}) collective-permute-start(bf16[128,3584]{1,0:T(8,128)(2,1)} %collective-permute-done.15.refs_4_.refs_10_.refs_14_), channel_id=1, source_target_pairs={{0,16},{4,20},{8,24},{12,28},{16,0},{20,4},{24,8},{28,12},{1,17},{... | collective-permute-start | bytes 2752520 | tf_op jit(solution)/shard_map/ppermute | solution.py:356
  138.5 21.8 %collective-permute-start.21 = (bf16[128,3584]{1,0:T(8,128)(2,1)}, bf16[128,3584]{1,0:T(8,128)(2,1)S(1)}, u32[]{:S(2)}, u32[]{:S(2)}) collective-permute-start(bf16[128,3584]{1,0:T(8,128)(2,1)} %collective-permute-done.8.refs_3_.refs_5_.refs_9_), channel_id=1, source_target_pairs={{0,3},{1,0},{2,1},{3,2},{4,7},{5,4},{6,5},{7,6},{8,11},{9,8},{10,9... | collective-permute-start | bytes 2752520 | tf_op jit(solution)/shard_map/ppermute | solution.py:359
  160.4 19.1 %collective-permute-start.25 = (bf16[512,3584]{1,0:T(8,128)(2,1)S(1)}, bf16[512,3584]{1,0:T(8,128)(2,1)S(1)}, u32[]{:S(2)}, u32[]{:S(2)}) collective-permute-start(bf16[512,3584]{1,0:T(8,128)(2,1)S(1)} %shard_map.79), channel_id=1, source_target_pairs={{0,4},{4,0},{8,12},{12,8},{16,20},{20,16},{24,28},{28,24},{1,5},{5... | collective-permute-start | bytes 11010056 | tf_op jit(solution)/shard_map/ppermute | solution.py:356
  160.5 16.4 %collective-permute-start.26 = (bf16[4,64,256]{2,1,0:T(8,128)(2,1)S(1)}, bf16[4,64,256]{2,1,0:T(8,128)(2,1)S(1)}, u32[]{:S(2)}, u32[]{:S(2)}) collective-permute-start(bf16[4,64,256]{2,1,0:T(8,128)(2,1)S(1)} %get-tuple-element.215), channel_id=1, source_target_pairs={{0,8},{4,12},{8,0},{12,4},{16,24},{20,28},{24,16},{28,20},{1,9},{5... | collective-permute-start | bytes 393224 | tf_op jit(solution)/shard_map/ppermute | solution.py:356
  161.5 16.1 %collective-permute-start.27 = (bf16[4,64,256]{2,1,0:T(8,128)(2,1)S(1)}, bf16[4,64,256]{2,1,0:T(8,128)(2,1)S(1)}, u32[]{:S(2)}, u32[]{:S(2)}) collective-permute-start(bf16[4,64,256]{2,1,0:T(8,128)(2,1)S(1)} %get-tuple-element.216), channel_id=1, source_target_pairs={{0,16},{4,20},{8,24},{12,28},{16,0},{20,4},{24,8},{28,12},{1,17},{... | collective-permute-start | bytes 393224 | tf_op jit(solution)/shard_map/ppermute | solution.py:356
  162.6 15.6 %collective-permute-start.28 = (bf16[4,64,256]{2,1,0:T(8,128)(2,1)S(1)}, bf16[4,64,256]{2,1,0:T(8,128)(2,1)S(1)}, u32[]{:S(2)}, u32[]{:S(2)}) collective-permute-start(bf16[4,64,256]{2,1,0:T(8,128)(2,1)S(1)} %get-tuple-element.218), channel_id=1, source_target_pairs={{0,8},{4,12},{8,0},{12,4},{16,24},{20,28},{24,16},{28,20},{1,9},{5... | collective-permute-start | bytes 393224 | tf_op jit(solution)/shard_map/ppermute | solution.py:356
  163.1 15.8 %collective-permute-start.29 = (bf16[4,64,256]{2,1,0:T(8,128)(2,1)S(1)}, bf16[4,64,256]{2,1,0:T(8,128)(2,1)S(1)}, u32[]{:S(2)}, u32[]{:S(2)}) collective-permute-start(bf16[4,64,256]{2,1,0:T(8,128)(2,1)S(1)} %get-tuple-element.219), channel_id=1, source_target_pairs={{0,8},{4,12},{8,0},{12,4},{16,24},{20,28},{24,16},{28,20},{1,9},{5... | collective-permute-start | bytes 393224 | tf_op jit(solution)/shard_map/ppermute | solution.py:356
  181.3 37.7 %collective-permute-start.38 = (bf16[512,3584]{1,0:T(8,128)(2,1)}, bf16[512,3584]{1,0:T(8,128)(2,1)}, u32[]{:S(2)}, u32[]{:S(2)}) collective-permute-start(bf16[512,3584]{1,0:T(8,128)(2,1)} %shard_map.81), channel_id=1, source_target_pairs={{0,4},{4,0},{8,12},{12,8},{16,20},{20,16},{24,28},{28,24},{1,5},{5... | collective-permute-start | bytes 11010056 | tf_op jit(solution)/shard_map/ppermute | solution.py:356
  181.3 7.4 %collective-permute-start.30 = (bf16[4,64,256]{2,1,0:T(8,128)(2,1)}, bf16[4,64,256]{2,1,0:T(8,128)(2,1)}, u32[]{:S(2)}, u32[]{:S(2)}) collective-permute-start(bf16[4,64,256]{2,1,0:T(8,128)(2,1)} %get-tuple-element.229), channel_id=1, source_target_pairs={{0,24},{4,28},{8,16},{12,20},{16,8},{20,12},{24,0},{28,4},{1,25},{... | collective-permute-start | bytes 393224 | tf_op jit(solution)/shard_map/ppermute | solution.py:356
  182.8 14.2 %collective-permute-start.31 = (bf16[4,64,256]{2,1,0:T(8,128)(2,1)}, bf16[4,64,256]{2,1,0:T(8,128)(2,1)}, u32[]{:S(2)}, u32[]{:S(2)}) collective-permute-start(bf16[4,64,256]{2,1,0:T(8,128)(2,1)} %copy-done.47), channel_id=1, source_target_pairs={{0,16},{4,20},{8,24},{12,28},{16,0},{20,4},{24,8},{28,12},{1,17},{... | collective-permute-start | bytes 393224 | tf_op jit(solution)/shard_map/ppermute | solution.py:356
  183.3 16.4 %collective-permute-start.33 = (bf16[4,64,256]{2,1,0:T(8,128)(2,1)}, bf16[4,64,256]{2,1,0:T(8,128)(2,1)}, u32[]{:S(2)}, u32[]{:S(2)}) collective-permute-start(bf16[4,64,256]{2,1,0:T(8,128)(2,1)} %copy-done.46), channel_id=1, source_target_pairs={{0,16},{4,20},{8,24},{12,28},{16,0},{20,4},{24,8},{28,12},{1,17},{... | collective-permute-start | bytes 393224 | tf_op jit(solution)/shard_map/ppermute | solution.py:356
  184.8 14.9 %collective-permute-start.32 = (bf16[4,64,256]{2,1,0:T(8,128)(2,1)}, bf16[4,64,256]{2,1,0:T(8,128)(2,1)}, u32[]{:S(2)}, u32[]{:S(2)}) collective-permute-start(bf16[4,64,256]{2,1,0:T(8,128)(2,1)} %copy-done.49), channel_id=1, source_target_pairs={{0,24},{4,28},{8,16},{12,20},{16,8},{20,12},{24,0},{28,4},{1,25},{... | collective-permute-start | bytes 393224 | tf_op jit(solution)/shard_map/ppermute | solution.py:356
  188.7 11.0 %collective-permute-start.34 = (bf16[4,64,256]{2,1,0:T(8,128)(2,1)}, bf16[4,64,256]{2,1,0:T(8,128)(2,1)}, u32[]{:S(2)}, u32[]{:S(2)}) collective-permute-start(bf16[4,64,256]{2,1,0:T(8,128)(2,1)} %copy-done.48), channel_id=1, source_target_pairs={{0,24},{4,28},{8,16},{12,20},{16,8},{20,12},{24,0},{28,4},{1,25},{... | collective-permute-start | bytes 393224 | tf_op jit(solution)/shard_map/ppermute | solution.py:356
  211.3 6.9 %collective-permute-start.37 = (f32[4,128]{1,0:T(4,128)S(1)}, f32[4,128]{1,0:T(4,128)S(1)}, u32[]{:S(2)}, u32[]{:S(2)}) collective-permute-start(f32[4,128]{1,0:T(4,128)S(1)} %get-tuple-element.268), channel_id=1, source_target_pairs={{0,1},{1,2},{2,3},{3,0},{4,5},{5,6},{6,7},{7,4},{8,9},{9,10},{10,1... | collective-permute-start | bytes 6152 | tf_op jit(solution)/shard_map/ppermute | solution.py:359
  211.4 6.8 %collective-permute-start.36 = (f32[4,128]{1,0:T(4,128)S(1)}, f32[4,128]{1,0:T(4,128)S(1)}, u32[]{:S(2)}, u32[]{:S(2)}) collective-permute-start(f32[4,128]{1,0:T(4,128)S(1)} %get-tuple-element.269), channel_id=1, source_target_pairs={{0,2},{1,3},{2,0},{3,1},{4,6},{5,7},{6,4},{7,5},{8,10},{9,11},{10,... | collective-permute-start | bytes 6152 | tf_op jit(solution)/shard_map/ppermute | solution.py:359
  213.3 5.0 %collective-permute-start.35 = (f32[4,128]{1,0:T(4,128)S(1)}, f32[4,128]{1,0:T(4,128)S(1)}, u32[]{:S(2)}, u32[]{:S(2)}) collective-permute-start(f32[4,128]{1,0:T(4,128)S(1)} %get-tuple-element.270), channel_id=1, source_target_pairs={{0,3},{1,0},{2,1},{3,2},{4,7},{5,4},{6,5},{7,6},{8,11},{9,8},{10,9... | collective-permute-start | bytes 6152 | tf_op jit(solution)/shard_map/ppermute | solution.py:359
  (45 other events, 160.7 us)

commit v10 on v9

--- a/solution.py
+++ b/solution.py
@@ -134,7 +134,7 @@
     for q in range(group):
         for c in range(2):
             at = q * pair + c * block
-            weight[at : at + block, :] = weight_refs[c][q * block : (q + 1) * block]
+            weight[at : at + block, :] = weight_refs[c][0, q * block : (q + 1) * block]
     projected = nt_dot(weight[...], rows[...])
     slot_ids = lax.broadcasted_iota(jnp.int32, (slots, tokens), 0).astype(F32)
     slot_rows = lax.broadcasted_iota(jnp.int32, (slots, pair), 0)
@@ -168,9 +168,9 @@
             scatter_ref[half] = jnp.dot(order, terms[half], preferred_element_type=F32).astype(BF16)
 
 
-def project(index, items, own_weight, partner_weight, hidden, top_k, group=2):
+def project(index, items, weights, hidden, top_k, group=2):
     experts, sources, slots, pair = hidden[0].shape
-    width = own_weight.shape[1]
+    width = weights.shape[2]
     pieces = [piece for rows, _, _ in items for piece in rows]
     sizes = [p.shape[0] for p in pieces]
     count = sum(sizes)
@@ -180,8 +180,8 @@
         grid_spec=pltpu.PrefetchScalarGridSpec(
             num_scalar_prefetch=1,
             grid=(experts // group,),
-            in_specs=[pl.BlockSpec(memory_space=pltpu.HBM)] * len(sizes)
-            + [pl.BlockSpec((group * block, width), lambda e, idx: (e, 0))] * 2
+            in_specs=[pl.BlockSpec(memory_space=pl.ANY)] * len(sizes)
+            + [pl.BlockSpec((1, group * block, width), lambda e, idx, c=c: (c, e, 0)) for c in range(2)]
             + [
                 pl.BlockSpec((group, 1, slots, pair), lambda e, idx, k=k: (e, idx[k], 0, 0))
                 for _, _, k in items
@@ -202,10 +202,10 @@
         compiler_params=pltpu.CompilerParams(vmem_limit_bytes=VMEM_BYTES),
         cost_estimate=pl.CostEstimate(
             flops=4 * count * width * experts * pair,
-            bytes_accessed=2 * (count * width + 2 * own_weight.size),
+            bytes_accessed=2 * (count * width + weights.size),
             transcendentals=0,
         ),
-    )(index, *pieces, own_weight, partner_weight, *[hidden[m] for _, m, _ in items])
+    )(index, *pieces, weights, weights, *[hidden[m] for _, m, _ in items])
 
 
 def fill_rows(pieces, rows):
@@ -228,10 +228,7 @@
 
 def half_grad_kernel(terms, arrivals, last, *refs):
     scatters, arrived = refs[:terms], refs[terms : terms + arrivals]
-    if last:
-        pieces, (out_ref, rows, held) = refs[terms + arrivals : -3], refs[-3:]
-    else:
-        pieces, (out_ref, rows) = refs[terms + arrivals : -2], refs[-2:]
+    pieces, (out_ref, rows) = refs[terms + arrivals : -2], refs[-2:]
     fill_rows(pieces, rows)
     total = sum_terms(scatters, rows, 0)
     for array in arrived:
@@ -239,17 +236,7 @@
     if not last:
         out_ref[...] = total.astype(BF16)
         return
-    held[...] = total
-    block, experts, _ = out_ref.shape
-    group = 8 // experts
-
-    def move(i, carry):
-        both = held[pl.ds(pl.multiple_of(i * 8, 8), 8), :]
-        for j in range(group):
-            out_ref[i * group + j] = both[j * experts : (j + 1) * experts]
-        return carry
-
-    lax.fori_loop(0, block // group, move, 0, unroll=4)
+    out_ref[...] = total.reshape(out_ref.shape)
 
 
 def half_grad(half, scatters, pieces, arrived, experts, tile, last):
@@ -261,7 +248,6 @@
     in_specs += [pl.BlockSpec((p.shape[0], tile), lambda i: (0, i)) for p in pieces]
     scratch = [pltpu.VMEM((count, tile), BF16)]
     if last:
-        scratch.append(pltpu.VMEM((height, tile), F32))
         out_spec = pl.BlockSpec((height // experts, experts, tile), lambda i: (0, 0, i))
         out_shape = jax.ShapeDtypeStruct((height // experts, experts, width), F32)
     else:
@@ -319,7 +305,7 @@
         grid_spec=pltpu.PrefetchScalarGridSpec(
             num_scalar_prefetch=1,
             grid=(1,),
-            in_specs=[pl.BlockSpec(memory_space=pltpu.HBM)] * len(pieces),
+            in_specs=[pl.BlockSpec(memory_space=pl.ANY)] * len(pieces),
             out_specs=[
                 pl.BlockSpec(memory_space=pl.ANY),
                 pl.BlockSpec((slabs * experts, pair // 2), lambda i, idx: (0, 0)),
@@ -334,7 +320,7 @@
             jax.ShapeDtypeStruct((slabs, experts, slots, 4 * pair), BF16),
             jax.ShapeDtypeStruct((slabs * experts, pair // 2), F32),
         ],
-        compiler_params=pltpu.CompilerParams(vmem_limit_bytes=8 * 2**20),
+        compiler_params=pltpu.CompilerParams(vmem_limit_bytes=60 * 2**20),
         cost_estimate=pl.CostEstimate(
             flops=0, bytes_accessed=4 * len(pieces) * experts * slots * pair, transcendentals=0
         ),
@@ -368,7 +354,7 @@
     index = jnp.stack(slabs + [me * experts]).astype(jnp.int32)
 
     def kernel(items):
-        *grads, scatter = project(index, items, own_weight, partner_weight, hidden, top_k)
+        *grads, scatter = project(index, items, weights, hidden, top_k)
         return grads, scatter
 
     def send_back(grads, chip_of):
@@ -393,14 +379,16 @@
     for m in range(4):
         piece = jnp.concatenate([held[2 * m], held[2 * m + 1]], axis=3)
         hidden.append(jnp.concatenate([piece, blank, metas], axis=2))
+    diagonal = across(hidden[3], 6)
     hidden = [
         hidden[0],
-        across(fence((hidden[1], x1))[0], 2),
-        across(fence((hidden[2], xy0))[0], 4),
-        across(hidden[3], 6),
+        across(fence((hidden[1], x1, diagonal))[0], 2),
+        across(fence((hidden[2], xy0, diagonal))[0], 4),
+        diagonal,
     ]
-    hidden, xy0, x1, next2, own3, partner_weight, x0, y0, next1 = fence(
-        (hidden, xy0, x1, next2, own3, partner_weight, x0, y0, next1)
+    weights = jnp.stack([own_weight, partner_weight])
+    hidden, xy0, x1, next2, own3, weights, x0, y0, next1 = fence(
+        (hidden, xy0, x1, next2, own3, weights, x0, y0, next1)
     )
 
     y1, x2, x3 = across(next1, 4), across(next2, 2), around(x0, -1)
@@ -430,7 +418,8 @@
     grads3, scatter3 = kernel([([xy2], 3, 2), ([xy3], 3, 3)])
     late = [xy1, y2, own3, y3, xy2, xy3]
     later = half_grad(other, [scatter2, scatter3], late, [], experts, 896, False)
-    partner, returned1, later, grads3, scatter3 = fence((partner, returned1, later, grads3, scatter3))
+    partner, later = fence((partner, later))
+    returned1, grads3 = fence((returned1, grads3))
     later = across(later, 1)
     returned2 = send_back(grads2, (3, 2, 0, 2))
     returned3 = send_back(grads3, (3, 3))

time: 234 us -> 286 us (1.22)
  Pallas kernels: 72.1 us -> 128 us
  waiting for transfers between devices: 67.5 us -> 44.6 us
  other arithmetic: 4.79 us -> 14.7 us
  starting transfers between devices: 48.8 us -> 55.9 us
    pallas_call x1, Pallas kernels: 2.55 us -> 66.3 us  [place(): pl.pallas_call(functools.partial(place_kernel, top_k), grid_spec=pltpu.Pr...]
    ppermute x27, waiting for transfers between devices: 43 us -> 26.5 us  [across(): return lax.ppermute(array, 'rep', [(i, i ^ bits) for i in range(reps)])]
    pallas_call x4, Pallas kernels: 41.2 us -> 33.9 us  [project(): pl.pallas_call(functools.partial(project_kernel, top_k, sizes, len(items)...]
    another operation x0 -> x1, other arithmetic: none -> 6.88 us  [on_device_tokens(): weights = jnp.stack([own_weight, partner_weight])]
    ppermute x12, waiting for transfers between devices: 24.5 us -> 18.1 us  [around(): lax.ppermute(array, 'exp', [(i, (i + shift) % sources) for i in range(sou...]
    ppermute x12, starting transfers between devices: 19.8 us -> 24.3 us  [around(): lax.ppermute(array, 'exp', [(i, (i + shift) % sources) for i in range(sou...]
    unnamed x109 -> x117, local copies, waits for them, and re-layouts: 25.1 us -> 23.2 us
  transfers between devices with their start and end apart: 39 -> 39, of which waited for: 13 -> 15; matrix products, arithmetic and copies ran while one was open for 9% -> 12% of each run, Pallas kernels for 25% -> 40%
where the time goes in v10:
time: 286 us; the launch traced here: 285 us
  Pallas kernels  128 us (45%)
  starting transfers between devices  55.9 us (20%)
  waiting for transfers between devices  44.6 us (16%)
  local copies, waits for them, and re-layouts  40.5 us (14%)
  other arithmetic  14.7 us (5%)
    pallas_call x1, Pallas kernels, place(): pl.pallas_call(functools.partial(place_kernel, top_k), grid_spec=pltpu.Pr...  66.3 us
    pallas_call x4, Pallas kernels, project(): pl.pallas_call(functools.partial(project_kernel, top_k, sizes, len(items)...  33.9 us
    ppermute x27, starting transfers between devices, across(): return lax.ppermute(array, 'rep', [(i, i ^ bits) for i in range(reps)])  31.6 us
    pallas_call x3, Pallas kernels, half_grad(): pl.pallas_call(functools.partial(half_grad_kernel, len(scatters), len(arr...  27.6 us
    ppermute x27, waiting for transfers between devices, across(): return lax.ppermute(array, 'rep', [(i, i ^ bits) for i in range(reps)])  26.5 us
    ppermute x12, starting transfers between devices, around(): lax.ppermute(array, 'exp', [(i, (i + shift) % sources) for i in range(sou...  24.3 us
    unnamed x117, local copies, waits for them, and re-layouts  23.2 us
    ppermute x12, waiting for transfers between devices, around(): lax.ppermute(array, 'exp', [(i, (i + shift) % sources) for i in range(sou...  18.1 us
  transfers between devices with their start and end apart: 39, of which 15 were waited for; matrix products, arithmetic and copies ran while one was open for 12% of the time, Pallas kernels for 40%

profile of v10, /device:TPU:0, one launch (start us, length us, event | category | flops | bytes accessed | tf_op | source)
XLA Modules:
  0.0 284.7 jit_solution(7604274787399413721)
XLA Ops:
  0.6 3.1 %collective-permute-start.5 = (bf16[128,3584]{1,0:T(8,128)(2,1)}, bf16[128,3584]{1,0:T(8,128)(2,1)S(1)}, u32[]{:S(2)}, u32[]{:S(2)}) collective-permute-start(bf16[128,3584]{1,0:T(8,128)(2,1)} %refs_6_.1), channel_id=1, source_target_pairs={{0,1},{1,2},{2,3},{3,0},{4,5},{5,6},{6,7},{7,4},{8,9},{9,10},{10,1... | collective-permute-start | bytes 2752520 | tf_op jit(solution)/shard_map/ppermute | solution.py:345
  3.7 1.5 collective-permute-start.4
  5.2 1.5 collective-permute-start.3
  8.8 2.7 collective-permute-start.1
  11.7 4.3 %reshape.91 = bf16[4,4,60,8,128]{4,3,1,2,0:T(8,128)(2,1)} reshape(bf16[1,4,4,60,1024]{4,2,3,1,0:T(4,128)(2,1)} %param.8) | data formatting | bytes 3932160 | tf_op jit(solution)/shard_map/reshape | solution.py:364
  16.0 3.6 %copy.15 = bf16[4,4,60,8,128]{4,2,1,0,3:T(8,128)(2,1)} copy(bf16[4,4,60,8,128]{4,3,1,2,0:T(8,128)(2,1)} %reshape.91) | data formatting | bytes 3932160 | tf_op jit(solution)/shard_map/reshape | solution.py:364
  19.6 2.8 dynamic-slice_bitcast_fusion
  22.4 2.4 copy.12
  24.8 3.6 %collective-permute-start.2 = (bf16[4,256]{1,0:T(4,128)(2,1)S(1)}, bf16[4,256]{1,0:T(4,128)(2,1)S(1)}, u32[]{:S(2)}, u32[]{:S(2)}) collective-permute-start(bf16[4,256]{1,0:T(4,128)(2,1)S(1)} %pad_maximum_fusion.6), channel_id=1, source_target_pairs={{0,3},{1,0},{2,1},{3,2},{4,7},{5,4},{6,5},{7,6},{8,11},{9,8},{10,9... | collective-permute-start | bytes 6152 | tf_op jit(solution)/shard_map/ppermute | solution.py:345
  31.9 1.5 collective-permute-start.6
  33.4 1.5 collective-permute-start.9
  37.1 2.5 pad_maximum_fusion.1
  40.0 15.1 %collective-permute-done.11.refs_3_.refs_9_.refs_13_ = bf16[128,3584]{1,0:T(8,128)(2,1)} collective-permute-done((bf16[128,3584]{1,0:T(8,128)(2,1)S(1)}, bf16[128,3584]{1,0:T(8,128)(2,1)}, u32[]{:S(2)}, u32[]{:S(2)}) %collective-permute-start.11) | collective-permute-done | bytes 917536 | tf_op jit(solution)/shard_map/ppermute | solution.py:345
  55.1 1.7 collective-permute-start.12
  56.8 9.8 %collective-permute-done.7.refs_9_.refs_6_.refs_4_.refs_5_ = bf16[4,4,64,256]{3,2,1,0:T(8,128)(2,1)S(1)} collective-permute-done((bf16[4,4,64,256]{3,2,1,0:T(8,128)(2,1)S(1)}, bf16[4,4,64,256]{3,2,1,0:T(8,128)(2,1)S(1)}, u32[]{:S(2)}, u32[]{:S(2)}) %collective-permute-start.7) | collective-permute-done | bytes 524320 | tf_op jit(solution)/shard_map/ppermute | solution.py:342
  67.1 1.5 collective-permute-start.10
  69.2 6.9 %pad_maximum_fusion.refs_4_.refs_5_.refs_6_.refs_7_.refs_2_.refs_3_ = bf16[2,512,3584]{2,1,0:T(8,128)(2,1)} fusion(bf16[1,512,3584]{2,1,0:T(8,128)(2,1)} %bitcast.32, bf16[1,512,3584]{2,1,0:T(8,128)(2,1)} %bitcast.31), kind=kLoop, calls=%fused_computation.1 | loop fusion | flops 3670016 | bytes 14680064 | tf_op jit(solution)/shard_map/stack | solution.py:389
  76.0 3.7 %collective-permute-done.10.refs_8_.refs_10_.refs_7_.refs_9_ = bf16[4,4,64,256]{3,2,1,0:T(8,128)(2,1)S(1)} collective-permute-done((bf16[4,4,64,256]{3,2,1,0:T(8,128)(2,1)S(1)}, bf16[4,4,64,256]{3,2,1,0:T(8,128)(2,1)S(1)}, u32[]{:S(2)}, u32[]{:S(2)}) %collective-permute-start.10) | collective-permute-done | bytes 524320 | tf_op jit(solution)/shard_map/ppermute | solution.py:342
  84.7 3.4 %collective-permute-start.16 = (bf16[128,3584]{1,0:T(8,128)(2,1)}, bf16[128,3584]{1,0:T(8,128)(2,1)}, u32[]{:S(2)}, u32[]{:S(2)}) collective-permute-start(bf16[128,3584]{1,0:T(8,128)(2,1)} %collective-permute-done.3.refs_1_.refs_3_.refs_7_), channel_id=1, source_target_pairs={{0,3},{1,0},{2,1},{3,2},{4,7},{5,4},{6,5},{7,6},{8,11},{9,8},{10,9... | collective-permute-start | bytes 2752520 | tf_op jit(solution)/shard_map/ppermute | solution.py:345
  88.2 3.1 %copy-done = bf16[2,512,3584]{2,1,0:T(8,128)(2,1)S(1)} copy-done((bf16[2,512,3584]{2,1,0:T(8,128)(2,1)S(1)}, bf16[2,512,3584]{2,1,0:T(8,128)(2,1)}, u32[]{:S(2)}) %copy-start) | copy-done | bytes 7340056
  94.5 8.4 %shard_map.76 = (bf16[4,64,256]{2,1,0:T(8,128)(2,1)S(1)}, bf16[4,64,256]{2,1,0:T(8,128)(2,1)S(1)}, bf16[4,64,256]{2,1,0:T(8,128)(2,1)S(1)}, bf16[4,64,256]{2,1,0:T(8,128)(2,1)S(1)}, bf16[2,512,512]{2,1,0:T(8,128)(2,1)S(1)}) custom-call(s32[5]{0:T(128)S(1)} %stack.95.idx_ref, bf16[128,3584]{1,0:T(8,128)(2,1)S(1)} %copy-done.21, ...), custom_call_target="tpu_custom_call" | custom-call | flops 7516192768 | bytes 11010048 | tf_op jit(solution)/shard_map/pallas_call | solution.py:178
  104.3 1.7 collective-permute-done.16.refs_5_.refs_11_.refs_15_
  106.0 4.3 %collective-permute-start.19 = (bf16[128,3584]{1,0:T(8,128)(2,1)S(1)}, bf16[128,3584]{1,0:T(8,128)(2,1)S(1)}, u32[]{:S(2)}, u32[]{:S(2)}) collective-permute-start(bf16[128,3584]{1,0:T(8,128)(2,1)S(1)} %collective-permute-done.4.refs_2_.refs_4_.refs_8_), channel_id=1, source_target_pairs={{0,3},{1,0},{2,1},{3,2},{4,7},{5,4},{6,5},{7,6},{8,11},{9,8},{10,9... | collective-permute-start | bytes 2752520 | tf_op jit(solution)/shard_map/ppermute | solution.py:345
  110.3 1.3 collective-permute-start.17
  114.4 12.8 %shard_map.77 = (bf16[4,64,256]{2,1,0:T(8,128)(2,1)S(1)}, bf16[4,64,256]{2,1,0:T(8,128)(2,1)S(1)}, bf16[4,64,256]{2,1,0:T(8,128)(2,1)}, bf16[4,64,256]{2,1,0:T(8...) custom-call(s32[5]{0:T(128)S(1)} %stack.95.idx_ref, ...), custom_call_target="tpu_custom_call" | custom-call | flops 11274289152 | bytes 12845056 | tf_op jit(solution)/shard_map/pallas_call | solution.py:178
  130.9 2.1 collective-permute-start.22
  133.0 2.5 collective-permute-start.23
  135.5 1.5 collective-permute-start.20
  137.1 8.0 %shard_map.78 = (bf16[4,64,256]{2,1,0:T(8,128)(2,1)}, bf16[4,64,256]{2,1,0:T(8,128)(2,1)S(1)}, bf16[4,64,256]{2,1,0:T(8,128)(2,1)S(1)}, bf16[4,64,256]{2,1,0:T(8,128)(2,1)S(1)}, bf16[2,512,512]{2,1,0:T(8,128)(2,1)S(1)}) custom-call(s32[5]{0:T(128)S(1)} %stack.95.idx_ref, bf16[128,3584]{1,0:T(8,128)(2,1)S(1)} %collective-permute-done.17.refs_0_.refs_2_.refs_16_, ...), custom_call_target="tpu_custom_call" | custom-call | flops 7516192768 | bytes 11010048 | tf_op jit(solution)/shard_map/pallas_call | solution.py:178
  150.5 8.3 %shard_map.79 = bf16[512,3584]{1,0:T(8,128)(2,1)S(1)} custom-call(bf16[2,512,512]{2,1,0:T(8,128)(2,1)S(1)} %copy-done.19, bf16[2,512,768]{2,1,0:T(8,128)(2,1)S(1)} %copy-done.17, bf16[128,3584]{1,0:T(8,128)(2,1)S(1)} %copy-done.22, bf16[128,3584]{1,0:T(8,128)(2,1)} %collective-permute-done.3.refs_1_.refs_3_.refs_7_, bf16[128,3584]{1,0:T(8,128)(2,1)S(1)} %copy-done.28, ...), custom_call_target="tpu_custom_call" | custom-call | flops 4697620480 | bytes 17825792 | tf_op jit(solution)/shard_map/pallas_call | solution.py:256
  159.0 4.7 %shard_map.80 = (bf16[4,64,256]{2,1,0:T(8,128)(2,1)S(1)}, bf16[4,64,256]{2,1,0:T(8,128)(2,1)S(1)}, bf16[2,512,256]{2,1,0:T(8,128)(2,1)S(1)}) custom-call(s32[5]{0:T(128)S(1)} %stack.95.idx_ref, bf16[128,3584]{1,0:T(8,128)(2,1)S(1)} %collective-permute-done.20.refs_0_.refs_6_.refs_20_, bf16[128,3584]{1,0:T(8,128)(2,1)S(1)} %collective-permute-done.21.refs_1_.refs_7_.refs_21_, ...), custom_call_target="tpu_custom_call" | custom-call | flops 3758096384 | bytes 9175040 | tf_op jit(solution)/shard_map/pallas_call | solution.py:178
  163.8 5.5 %shard_map.82 = bf16[512,3584]{1,0:T(8,128)(2,1)} custom-call(bf16[2,512,512]{2,1,0:T(8,128)(2,1)S(1)} %get-tuple-element.236.refs_0_.refs_2_, bf16[2,512,256]{2,1,0:T(8,128)(2,1)S(1)} %get-tuple-element.237.refs_1_.refs_3_, bf16[128,3584]{1,0:T(8,128)(2,1)S(1)} %copy-done.9, bf16[128,3584]{1,0:T(8,128)(2,1)S(1)} %copy-done.12, ...), custom_call_target="tpu_custom_call" | custom-call | flops 2818572288 | bytes 13631488 | tf_op jit(solution)/shard_map/pallas_call | solution.py:256
  169.8 1.9 collective-permute-start.25
  172.3 1.5 collective-permute-start.28
  173.8 2.3 collective-permute-done.25.refs_5_
  176.8 1.3 collective-permute-start.29
  178.1 2.1 collective-permute-start.30
  180.5 1.3 collective-permute-done.28.refs_13_
  181.8 1.3 collective-permute-start.31
  184.2 3.4 %collective-permute-start.33 = (bf16[4,64,256]{2,1,0:T(8,128)(2,1)}, bf16[4,64,256]{2,1,0:T(8,128)(2,1)}, u32[]{:S(2)}, u32[]{:S(2)}) collective-permute-start(bf16[4,64,256]{2,1,0:T(8,128)(2,1)} %copy-done.44), channel_id=1, source_target_pairs={{0,24},{4,28},{8,16},{12,20},{16,8},{20,12},{24,0},{28,4},{1,25},{... | collective-permute-start | bytes 393224 | tf_op jit(solution)/shard_map/ppermute | solution.py:342
  188.2 4.0 %collective-permute-done.30.refs_10_ = bf16[4,64,256]{2,1,0:T(8,128)(2,1)} collective-permute-done((bf16[4,64,256]{2,1,0:T(8,128)(2,1)}, bf16[4,64,256]{2,1,0:T(8,128)(2,1)}, u32[]{:S(2)}, u32[]{:S(2)}) %collective-permute-start.30) | collective-permute-done | bytes 131104 | tf_op jit(solution)/shard_map/ppermute | solution.py:342
  192.2 1.4 collective-permute-done.32.refs_14_
  193.6 66.3 %shard_map.81 = (bf16[4,4,64,1024]{3,2,1,0:T(8,128)(2,1)}, f32[16,128]{1,0:T(8,128)}) custom-call(s32[12]{0:T(128)} %stack.85.idx_ref, bf16[4,64,256]{2,1,0:T(8,128)(2,1)} %copy-done.32, bf16[4,64,256]{2,1,0:T(8,128)(2,1)} %copy-done.48, bf16[4,64,256]{2,1,0:T(8,128)(2,1)} %copy-done.49, bf16[4,64,256]{2,1,0:T(8,128)(2,1)} %copy-done.50, ...), custom_call_target="tpu_custom_call" | custom-call | bytes 4194304 | tf_op jit(solution)/shard_map/pallas_call | solution.py:303
  260.7 2.0 collective-permute-start.36
  262.7 2.4 collective-permute-start.34
  265.3 2.0 slice_bitcast_fusion
  267.3 2.8 copy.13
  270.9 13.8 %shard_map.83 = f32[128,4,3584]{2,1,0:T(4,128)} custom-call(bf16[2,512,512]{2,1,0:T(8,128)(2,1)S(1)} %copy-done.20, bf16[2,512,768]{2,1,0:T(8,128)(2,1)} %copy-done.16, bf16[2,512,512]{2,1,0:T(8,128)(2,1)S(1)} %get-tuple-element.236.refs_0_.refs_2_, bf16[2,512,256]{2,1,0:T(8,128)(2,1)S(1)} %get-tuple-element.237.refs_1_.refs_3_, ...), custom_call_target="tpu_custom_call" | custom-call | flops 7516192768 | bytes 24117248 | tf_op jit(solution)/shard_map/pallas_call | solution.py:256
  (181 shorter events, 36.2 us)
Async XLA Ops:
  0.6 29.1 %collective-permute-start.5 = (bf16[128,3584]{1,0:T(8,128)(2,1)}, bf16[128,3584]{1,0:T(8,128)(2,1)S(1)}, u32[]{:S(2)}, u32[]{:S(2)}) collective-permute-start(bf16[128,3584]{1,0:T(8,128)(2,1)} %refs_6_.1), channel_id=1, source_target_pairs={{0,1},{1,2},{2,3},{3,0},{4,5},{5,6},{6,7},{7,4},{8,9},{9,10},{10,1... | collective-permute-start | bytes 2752520 | tf_op jit(solution)/shard_map/ppermute | solution.py:345
  3.7 26.0 %collective-permute-start.4 = (bf16[128,3584]{1,0:T(8,128)(2,1)}, bf16[128,3584]{1,0:T(8,128)(2,1)S(1)}, u32[]{:S(2)}, u32[]{:S(2)}) collective-permute-start(bf16[128,3584]{1,0:T(8,128)(2,1)} %refs_6_.1), channel_id=1, source_target_pairs={{0,16},{4,20},{8,24},{12,28},{16,0},{20,4},{24,8},{28,12},{1,17},{... | collective-permute-start | bytes 2752520 | tf_op jit(solution)/shard_map/ppermute | solution.py:342
  5.2 24.5 %collective-permute-start.3 = (bf16[128,3584]{1,0:T(8,128)(2,1)}, bf16[128,3584]{1,0:T(8,128)(2,1)}, u32[]{:S(2)}, u32[]{:S(2)}) collective-permute-start(bf16[128,3584]{1,0:T(8,128)(2,1)} %refs_6_.1), channel_id=1, source_target_pairs={{0,8},{4,12},{8,0},{12,4},{16,24},{20,28},{24,16},{28,20},{1,9},{5... | collective-permute-start | bytes 2752520 | tf_op jit(solution)/shard_map/ppermute | solution.py:342
  8.8 16.0 %collective-permute-start.1 = (bf16[4,256]{1,0:T(4,128)(2,1)S(1)}, bf16[4,256]{1,0:T(4,128)(2,1)S(1)}, u32[]{:S(2)}, u32[]{:S(2)}) collective-permute-start(bf16[4,256]{1,0:T(4,128)(2,1)S(1)} %pad_maximum_fusion.6), channel_id=1, source_target_pairs={{0,2},{1,3},{2,0},{3,1},{4,6},{5,7},{6,4},{7,5},{8,10},{9,11},{10,... | collective-permute-start | bytes 6152 | tf_op jit(solution)/shard_map/ppermute | solution.py:345
  11.5 17.0 %collective-permute-start = (bf16[4,256]{1,0:T(4,128)(2,1)S(1)}, bf16[4,256]{1,0:T(4,128)(2,1)S(1)}, u32[]{:S(2)}, u32[]{:S(2)}) collective-permute-start(bf16[4,256]{1,0:T(4,128)(2,1)S(1)} %pad_maximum_fusion.6), channel_id=1, source_target_pairs={{0,1},{1,2},{2,3},{3,0},{4,5},{5,6},{6,7},{7,4},{8,9},{9,10},{10,1... | collective-permute-start | bytes 6152 | tf_op jit(solution)/shard_map/ppermute | solution.py:345
  24.8 30.3 %copy-start.21 = (bf16[128,3584]{1,0:T(8,128)(2,1)S(1)}, bf16[128,3584]{1,0:T(8,128)(2,1)}, u32[]{:S(2)}) copy-start(bf16[128,3584]{1,0:T(8,128)(2,1)} %refs_6_.1) | copy-start | bytes 2752516
  24.8 4.9 %collective-permute-start.2 = (bf16[4,256]{1,0:T(4,128)(2,1)S(1)}, bf16[4,256]{1,0:T(4,128)(2,1)S(1)}, u32[]{:S(2)}, u32[]{:S(2)}) collective-permute-start(bf16[4,256]{1,0:T(4,128)(2,1)S(1)} %pad_maximum_fusion.6), channel_id=1, source_target_pairs={{0,3},{1,0},{2,1},{3,2},{4,7},{5,4},{6,5},{7,6},{8,11},{9,8},{10,9... | collective-permute-start | bytes 6152 | tf_op jit(solution)/shard_map/ppermute | solution.py:345
  29.7 82.6 %copy-start.24 = (bf16[128,3584]{1,0:T(8,128)(2,1)}, bf16[128,3584]{1,0:T(8,128)(2,1)S(1)}, u32[]{:S(2)}) copy-start(bf16[128,3584]{1,0:T(8,128)(2,1)S(1)} %collective-permute-done.5.refs_0_.refs_6_.refs_10_) | copy-start | bytes 2752516
  29.7 76.3 %copy-start.27 = (bf16[128,3584]{1,0:T(8,128)(2,1)}, bf16[128,3584]{1,0:T(8,128)(2,1)S(1)}, u32[]{:S(2)}) copy-start(bf16[128,3584]{1,0:T(8,128)(2,1)S(1)} %collective-permute-done.4.refs_2_.refs_4_.refs_8_) | copy-start | bytes 2752516
  29.8 39.4 %collective-permute-start.13 = (bf16[512,3584]{1,0:T(8,128)(2,1)}, bf16[512,3584]{1,0:T(8,128)(2,1)}, u32[]{:S(2)}, u32[]{:S(2)}) collective-permute-start(bf16[512,3584]{1,0:T(8,128)(2,1)} %bitcast.25), channel_id=1, source_target_pairs={{0,4},{4,0},{8,12},{12,8},{16,20},{20,16},{24,28},{28,24},{1,5},{5... | collective-permute-start | bytes 11010056 | tf_op jit(solution)/shard_map/ppermute | solution.py:342
  29.9 25.2 %collective-permute-start.11 = (bf16[128,3584]{1,0:T(8,128)(2,1)S(1)}, bf16[128,3584]{1,0:T(8,128)(2,1)}, u32[]{:S(2)}, u32[]{:S(2)}) collective-permute-start(bf16[128,3584]{1,0:T(8,128)(2,1)S(1)} %collective-permute-done.5.refs_0_.refs_6_.refs_10_), channel_id=1, source_target_pairs={{0,1},{1,2},{2,3},{3,0},{4,5},{5,6},{6,7},{7,4},{8,9},{9,10},{10,1... | collective-permute-start | bytes 2752520 | tf_op jit(solution)/shard_map/ppermute | solution.py:345
  31.9 36.7 %collective-permute-start.6 = (bf16[128,3584]{1,0:T(8,128)(2,1)S(1)}, bf16[128,3584]{1,0:T(8,128)(2,1)}, u32[]{:S(2)}, u32[]{:S(2)}) collective-permute-start(bf16[128,3584]{1,0:T(8,128)(2,1)S(1)} %collective-permute-done.5.refs_0_.refs_6_.refs_10_), channel_id=1, source_target_pairs={{0,8},{4,12},{8,0},{12,4},{16,24},{20,28},{24,16},{28,20},{1,9},{5... | collective-permute-start | bytes 2752520 | tf_op jit(solution)/shard_map/ppermute | solution.py:342
  33.4 33.7 %collective-permute-start.9 = (bf16[128,3584]{1,0:T(8,128)(2,1)}, bf16[128,3584]{1,0:T(8,128)(2,1)}, u32[]{:S(2)}, u32[]{:S(2)}) collective-permute-start(bf16[128,3584]{1,0:T(8,128)(2,1)} %collective-permute-done.3.refs_1_.refs_3_.refs_7_), channel_id=1, source_target_pairs={{0,16},{4,20},{8,24},{12,28},{16,0},{20,4},{24,8},{28,12},{1,17},{... | collective-permute-start | bytes 2752520 | tf_op jit(solution)/shard_map/ppermute | solution.py:342
  39.5 27.1 %collective-permute-start.7 = (bf16[4,4,64,256]{3,2,1,0:T(8,128)(2,1)S(1)}, bf16[4,4,64,256]{3,2,1,0:T(8,128)(2,1)S(1)}, u32[]{:S(2)}, u32[]{:S(2)}) collective-permute-start(bf16[4,4,64,256]{3,2,1,0:T(8,128)(2,1)S(1)} %get-tuple-element.263), channel_id=1, source_target_pairs={{0,24},{4,28},{8,16},{12,20},{16,8},{20,12},{24,0},{28,4},{1,25},{... | collective-permute-start | bytes 1572872 | tf_op jit(solution)/shard_map/ppermute | solution.py:342
  55.1 26.9 %collective-permute-start.12 = (bf16[128,3584]{1,0:T(8,128)(2,1)S(1)}, bf16[128,3584]{1,0:T(8,128)(2,1)S(1)}, u32[]{:S(2)}, u32[]{:S(2)}) collective-permute-start(bf16[128,3584]{1,0:T(8,128)(2,1)S(1)} %copy-done.21), channel_id=1, source_target_pairs={{0,3},{1,0},{2,1},{3,2},{4,7},{5,4},{6,5},{7,6},{8,11},{9,8},{10,9... | collective-permute-start | bytes 2752520 | tf_op jit(solution)/shard_map/ppermute | solution.py:345
  66.6 70.4 %copy-start.14 = (bf16[4,4,64,256]{3,2,1,0:T(8,128)(2,1)}, bf16[4,4,64,256]{3,2,1,0:T(8,128)(2,1)S(1)}, u32[]{:S(2)}) copy-start(bf16[4,4,64,256]{3,2,1,0:T(8,128)(2,1)S(1)} %collective-permute-done.7.refs_9_.refs_6_.refs_4_.refs_5_) | copy-start | bytes 1572868
  67.1 12.7 %collective-permute-start.10 = (bf16[4,4,64,256]{3,2,1,0:T(8,128)(2,1)S(1)}, bf16[4,4,64,256]{3,2,1,0:T(8,128)(2,1)S(1)}, u32[]{:S(2)}, u32[]{:S(2)}) collective-permute-start(bf16[4,4,64,256]{3,2,1,0:T(8,128)(2,1)S(1)} %get-tuple-element.147), channel_id=1, source_target_pairs={{0,16},{4,20},{8,24},{12,28},{16,0},{20,4},{24,8},{28,12},{1,17},{... | collective-permute-start | bytes 1572872 | tf_op jit(solution)/shard_map/ppermute | solution.py:342
  68.6 12.6 %collective-permute-start.8 = (bf16[4,4,64,256]{3,2,1,0:T(8,128)(2,1)S(1)}, bf16[4,4,64,256]{3,2,1,0:T(8,128)(2,1)S(1)}, u32[]{:S(2)}, u32[]{:S(2)}) collective-permute-start(bf16[4,4,64,256]{3,2,1,0:T(8,128)(2,1)S(1)} %get-tuple-element.143), channel_id=1, source_target_pairs={{0,8},{4,12},{8,0},{12,4},{16,24},{20,28},{24,16},{28,20},{1,9},{5... | collective-permute-start | bytes 1572872 | tf_op jit(solution)/shard_map/ppermute | solution.py:342
  83.0 20.9 %collective-permute-start.15 = (bf16[128,3584]{1,0:T(8,128)(2,1)}, bf16[128,3584]{1,0:T(8,128)(2,1)}, u32[]{:S(2)}, u32[]{:S(2)}) collective-permute-start(bf16[128,3584]{1,0:T(8,128)(2,1)} %collective-permute-done.11.refs_3_.refs_9_.refs_13_), channel_id=1, source_target_pairs={{0,8},{4,12},{8,0},{12,4},{16,24},{20,28},{24,16},{28,20},{1,9},{5... | collective-permute-start | bytes 2752520 | tf_op jit(solution)/shard_map/ppermute | solution.py:342
  83.8 20.5 %collective-permute-start.14 = (bf16[128,3584]{1,0:T(8,128)(2,1)S(1)}, bf16[128,3584]{1,0:T(8,128)(2,1)}, u32[]{:S(2)}, u32[]{:S(2)}) collective-permute-start(bf16[128,3584]{1,0:T(8,128)(2,1)S(1)} %collective-permute-done.5.refs_0_.refs_6_.refs_10_), channel_id=1, source_target_pairs={{0,16},{4,20},{8,24},{12,28},{16,0},{20,4},{24,8},{28,12},{1,17},{... | collective-permute-start | bytes 2752520 | tf_op jit(solution)/shard_map/ppermute | solution.py:342
  84.7 21.3 %collective-permute-start.16 = (bf16[128,3584]{1,0:T(8,128)(2,1)}, bf16[128,3584]{1,0:T(8,128)(2,1)}, u32[]{:S(2)}, u32[]{:S(2)}) collective-permute-start(bf16[128,3584]{1,0:T(8,128)(2,1)} %collective-permute-done.3.refs_1_.refs_3_.refs_7_), channel_id=1, source_target_pairs={{0,3},{1,0},{2,1},{3,2},{4,7},{5,4},{6,5},{7,6},{8,11},{9,8},{10,9... | collective-permute-start | bytes 2752520 | tf_op jit(solution)/shard_map/ppermute | solution.py:345
  103.9 23.2 %copy-start.32 = (bf16[4,64,256]{2,1,0:T(8,128)(2,1)}, bf16[4,64,256]{2,1,0:T(8,128)(2,1)S(1)}, u32[]{:S(2)}) copy-start(bf16[4,64,256]{2,1,0:T(8,128)(2,1)S(1)} %get-tuple-element.208.refs_0_) | copy-start | bytes 393220
  106.0 31.1 %copy-start.3 = (bf16[128,3584]{1,0:T(8,128)(2,1)S(1)}, bf16[128,3584]{1,0:T(8,128)(2,1)}, u32[]{:S(2)}) copy-start(bf16[128,3584]{1,0:T(8,128)(2,1)} %copy-done.2) | copy-start | bytes 2752516
  106.0 23.6 %collective-permute-start.19 = (bf16[128,3584]{1,0:T(8,128)(2,1)S(1)}, bf16[128,3584]{1,0:T(8,128)(2,1)S(1)}, u32[]{:S(2)}, u32[]{:S(2)}) collective-permute-start(bf16[128,3584]{1,0:T(8,128)(2,1)S(1)} %collective-permute-done.4.refs_2_.refs_4_.refs_8_), channel_id=1, source_target_pairs={{0,3},{1,0},{2,1},{3,2},{4,7},{5,4},{6,5},{7,6},{8,11},{9,8},{10,9... | collective-permute-start | bytes 2752520 | tf_op jit(solution)/shard_map/ppermute | solution.py:345
  110.3 20.0 %collective-permute-start.17 = (bf16[128,3584]{1,0:T(8,128)(2,1)}, bf16[128,3584]{1,0:T(8,128)(2,1)S(1)}, u32[]{:S(2)}, u32[]{:S(2)}) collective-permute-start(bf16[128,3584]{1,0:T(8,128)(2,1)} %collective-permute-done.14.refs_2_.refs_8_.refs_12_), channel_id=1, source_target_pairs={{0,8},{4,12},{8,0},{12,4},{16,24},{20,28},{24,16},{28,20},{1,9},{5... | collective-permute-start | bytes 2752520 | tf_op jit(solution)/shard_map/ppermute | solution.py:342
  111.6 19.3 %collective-permute-start.18 = (bf16[128,3584]{1,0:T(8,128)(2,1)}, bf16[128,3584]{1,0:T(8,128)(2,1)S(1)}, u32[]{:S(2)}, u32[]{:S(2)}) collective-permute-start(bf16[128,3584]{1,0:T(8,128)(2,1)} %collective-permute-done.11.refs_3_.refs_9_.refs_13_), channel_id=1, source_target_pairs={{0,16},{4,20},{8,24},{12,28},{16,0},{20,4},{24,8},{28,12},{1,17},{... | collective-permute-start | bytes 2752520 | tf_op jit(solution)/shard_map/ppermute | solution.py:342
  114.4 22.7 %copy-start.39 = (bf16[4,4,64,256]{3,2,1,0:T(8,128)(2,1)S(1)}, bf16[4,4,64,256]{3,2,1,0:T(8,128)(2,1)}, u32[]{:S(2)}) copy-start(bf16[4,4,64,256]{3,2,1,0:T(8,128)(2,1)} %copy-done.36) | copy-start | bytes 1572868
  130.9 18.4 %copy-start.22 = (bf16[128,3584]{1,0:T(8,128)(2,1)S(1)}, bf16[128,3584]{1,0:T(8,128)(2,1)}, u32[]{:S(2)}) copy-start(bf16[128,3584]{1,0:T(8,128)(2,1)} %refs_6_.1) | copy-start | bytes 2752516
  130.9 18.4 %copy-start.25 = (bf16[128,3584]{1,0:T(8,128)(2,1)S(1)}, bf16[128,3584]{1,0:T(8,128)(2,1)}, u32[]{:S(2)}) copy-start(bf16[128,3584]{1,0:T(8,128)(2,1)} %copy-done.24) | copy-start | bytes 2752516
  130.9 27.9 %collective-permute-start.22 = (bf16[4,64,256]{2,1,0:T(8,128)(2,1)S(1)}, bf16[4,64,256]{2,1,0:T(8,128)(2,1)S(1)}, u32[]{:S(2)}, u32[]{:S(2)}) collective-permute-start(bf16[4,64,256]{2,1,0:T(8,128)(2,1)S(1)} %get-tuple-element.188), channel_id=1, source_target_pairs={{0,8},{4,12},{8,0},{12,4},{16,24},{20,28},{24,16},{28,20},{1,9},{5... | collective-permute-start | bytes 393224 | tf_op jit(solution)/shard_map/ppermute | solution.py:342
  133.0 25.8 %collective-permute-start.23 = (bf16[4,64,256]{2,1,0:T(8,128)(2,1)S(1)}, bf16[4,64,256]{2,1,0:T(8,128)(2,1)S(1)}, u32[]{:S(2)}, u32[]{:S(2)}) collective-permute-start(bf16[4,64,256]{2,1,0:T(8,128)(2,1)S(1)} %get-tuple-element.189), channel_id=1, source_target_pairs={{0,16},{4,20},{8,24},{12,28},{16,0},{20,4},{24,8},{28,12},{1,17},{... | collective-permute-start | bytes 393224 | tf_op jit(solution)/shard_map/ppermute | solution.py:342
  135.5 23.3 %collective-permute-start.24 = (bf16[4,64,256]{2,1,0:T(8,128)(2,1)S(1)}, bf16[4,64,256]{2,1,0:T(8,128)(2,1)S(1)}, u32[]{:S(2)}, u32[]{:S(2)}) collective-permute-start(bf16[4,64,256]{2,1,0:T(8,128)(2,1)S(1)} %get-tuple-element.190), channel_id=1, source_target_pairs={{0,24},{4,28},{8,16},{12,20},{16,8},{20,12},{24,0},{28,4},{1,25},{... | collective-permute-start | bytes 393224 | tf_op jit(solution)/shard_map/ppermute | solution.py:342
  135.5 23.3 %collective-permute-start.20 = (bf16[128,3584]{1,0:T(8,128)(2,1)}, bf16[128,3584]{1,0:T(8,128)(2,1)S(1)}, u32[]{:S(2)}, u32[]{:S(2)}) collective-permute-start(bf16[128,3584]{1,0:T(8,128)(2,1)} %collective-permute-done.15.refs_4_.refs_10_.refs_14_), channel_id=1, source_target_pairs={{0,16},{4,20},{8,24},{12,28},{16,0},{20,4},{24,8},{28,12},{1,17},{... | collective-permute-start | bytes 2752520 | tf_op jit(solution)/shard_map/ppermute | solution.py:342
  137.1 21.8 %collective-permute-start.21 = (bf16[128,3584]{1,0:T(8,128)(2,1)}, bf16[128,3584]{1,0:T(8,128)(2,1)S(1)}, u32[]{:S(2)}, u32[]{:S(2)}) collective-permute-start(bf16[128,3584]{1,0:T(8,128)(2,1)} %collective-permute-done.9.refs_3_.refs_5_.refs_9_), channel_id=1, source_target_pairs={{0,3},{1,0},{2,1},{3,2},{4,7},{5,4},{6,5},{7,6},{8,11},{9,8},{10,9... | collective-permute-start | bytes 2752520 | tf_op jit(solution)/shard_map/ppermute | solution.py:345
  158.9 10.3 %collective-permute-start.37 = (bf16[512,3584]{1,0:T(8,128)(2,1)S(1)}, bf16[512,3584]{1,0:T(8,128)(2,1)S(1)}, u32[]{:S(2)}, u32[]{:S(2)}) collective-permute-start(bf16[512,3584]{1,0:T(8,128)(2,1)S(1)} %shard_map.79), channel_id=1, source_target_pairs={{0,4},{4,0},{8,12},{12,8},{16,20},{20,16},{24,28},{28,24},{1,5},{5... | collective-permute-start | bytes 11010056 | tf_op jit(solution)/shard_map/ppermute | solution.py:342
  169.2 101.6 %collective-permute-start.38 = (bf16[512,3584]{1,0:T(8,128)(2,1)}, bf16[512,3584]{1,0:T(8,128)(2,1)}, u32[]{:S(2)}, u32[]{:S(2)}) collective-permute-start(bf16[512,3584]{1,0:T(8,128)(2,1)} %shard_map.82), channel_id=1, source_target_pairs={{0,4},{4,0},{8,12},{12,8},{16,20},{20,16},{24,28},{28,24},{1,5},{5... | collective-permute-start | bytes 11010056 | tf_op jit(solution)/shard_map/ppermute | solution.py:342
  169.8 6.3 %collective-permute-start.25 = (bf16[4,64,256]{2,1,0:T(8,128)(2,1)S(1)}, bf16[4,64,256]{2,1,0:T(8,128)(2,1)S(1)}, u32[]{:S(2)}, u32[]{:S(2)}) collective-permute-start(bf16[4,64,256]{2,1,0:T(8,128)(2,1)S(1)} %get-tuple-element.213), channel_id=1, source_target_pairs={{0,8},{4,12},{8,0},{12,4},{16,24},{20,28},{24,16},{28,20},{1,9},{5... | collective-permute-start | bytes 393224 | tf_op jit(solution)/shard_map/ppermute | solution.py:342
  171.7 6.4 %collective-permute-start.26 = (bf16[4,64,256]{2,1,0:T(8,128)(2,1)}, bf16[4,64,256]{2,1,0:T(8,128)(2,1)}, u32[]{:S(2)}, u32[]{:S(2)}) collective-permute-start(bf16[4,64,256]{2,1,0:T(8,128)(2,1)} %get-tuple-element.214), channel_id=1, source_target_pairs={{0,16},{4,20},{8,24},{12,28},{16,0},{20,4},{24,8},{28,12},{1,17},{... | collective-permute-start | bytes 393224 | tf_op jit(solution)/shard_map/ppermute | solution.py:342
  171.8 8.5 %collective-permute-start.27 = (bf16[4,64,256]{2,1,0:T(8,128)(2,1)}, bf16[4,64,256]{2,1,0:T(8,128)(2,1)}, u32[]{:S(2)}, u32[]{:S(2)}) collective-permute-start(bf16[4,64,256]{2,1,0:T(8,128)(2,1)} %get-tuple-element.216), channel_id=1, source_target_pairs={{0,8},{4,12},{8,0},{12,4},{16,24},{20,28},{24,16},{28,20},{1,9},{5... | collective-permute-start | bytes 393224 | tf_op jit(solution)/shard_map/ppermute | solution.py:342
  172.3 9.5 %collective-permute-start.28 = (bf16[4,64,256]{2,1,0:T(8,128)(2,1)}, bf16[4,64,256]{2,1,0:T(8,128)(2,1)}, u32[]{:S(2)}, u32[]{:S(2)}) collective-permute-start(bf16[4,64,256]{2,1,0:T(8,128)(2,1)} %get-tuple-element.217), channel_id=1, source_target_pairs={{0,8},{4,12},{8,0},{12,4},{16,24},{20,28},{24,16},{28,20},{1,9},{5... | collective-permute-start | bytes 393224 | tf_op jit(solution)/shard_map/ppermute | solution.py:342
  176.8 7.4 %collective-permute-start.29 = (bf16[4,64,256]{2,1,0:T(8,128)(2,1)}, bf16[4,64,256]{2,1,0:T(8,128)(2,1)}, u32[]{:S(2)}, u32[]{:S(2)}) collective-permute-start(bf16[4,64,256]{2,1,0:T(8,128)(2,1)} %get-tuple-element.225), channel_id=1, source_target_pairs={{0,24},{4,28},{8,16},{12,20},{16,8},{20,12},{24,0},{28,4},{1,25},{... | collective-permute-start | bytes 393224 | tf_op jit(solution)/shard_map/ppermute | solution.py:342
  178.1 14.1 %collective-permute-start.30 = (bf16[4,64,256]{2,1,0:T(8,128)(2,1)}, bf16[4,64,256]{2,1,0:T(8,128)(2,1)}, u32[]{:S(2)}, u32[]{:S(2)}) collective-permute-start(bf16[4,64,256]{2,1,0:T(8,128)(2,1)} %copy-done.43), channel_id=1, source_target_pairs={{0,16},{4,20},{8,24},{12,28},{16,0},{20,4},{24,8},{28,12},{1,17},{... | collective-permute-start | bytes 393224 | tf_op jit(solution)/shard_map/ppermute | solution.py:342
  180.2 13.4 %collective-permute-start.32 = (bf16[4,64,256]{2,1,0:T(8,128)(2,1)S(1)}, bf16[4,64,256]{2,1,0:T(8,128)(2,1)}, u32[]{:S(2)}, u32[]{:S(2)}) collective-permute-start(bf16[4,64,256]{2,1,0:T(8,128)(2,1)S(1)} %get-tuple-element.232), channel_id=1, source_target_pairs={{0,16},{4,20},{8,24},{12,28},{16,0},{20,4},{24,8},{28,12},{1,17},{... | collective-permute-start | bytes 393224 | tf_op jit(solution)/shard_map/ppermute | solution.py:342
  181.8 11.8 %collective-permute-start.31 = (bf16[4,64,256]{2,1,0:T(8,128)(2,1)}, bf16[4,64,256]{2,1,0:T(8,128)(2,1)}, u32[]{:S(2)}, u32[]{:S(2)}) collective-permute-start(bf16[4,64,256]{2,1,0:T(8,128)(2,1)} %copy-done.45), channel_id=1, source_target_pairs={{0,24},{4,28},{8,16},{12,20},{16,8},{20,12},{24,0},{28,4},{1,25},{... | collective-permute-start | bytes 393224 | tf_op jit(solution)/shard_map/ppermute | solution.py:342
  184.2 9.4 %collective-permute-start.33 = (bf16[4,64,256]{2,1,0:T(8,128)(2,1)}, bf16[4,64,256]{2,1,0:T(8,128)(2,1)}, u32[]{:S(2)}, u32[]{:S(2)}) collective-permute-start(bf16[4,64,256]{2,1,0:T(8,128)(2,1)} %copy-done.44), channel_id=1, source_target_pairs={{0,24},{4,28},{8,16},{12,20},{16,8},{20,12},{24,0},{28,4},{1,25},{... | collective-permute-start | bytes 393224 | tf_op jit(solution)/shard_map/ppermute | solution.py:342
  260.7 9.3 %collective-permute-start.36 = (f32[4,128]{1,0:T(4,128)S(1)}, f32[4,128]{1,0:T(4,128)S(1)}, u32[]{:S(2)}, u32[]{:S(2)}) collective-permute-start(f32[4,128]{1,0:T(4,128)S(1)} %get-tuple-element.266), channel_id=1, source_target_pairs={{0,1},{1,2},{2,3},{3,0},{4,5},{5,6},{6,7},{7,4},{8,9},{9,10},{10,1... | collective-permute-start | bytes 6152 | tf_op jit(solution)/shard_map/ppermute | solution.py:345
  262.7 7.3 %collective-permute-start.35 = (f32[4,128]{1,0:T(4,128)S(1)}, f32[4,128]{1,0:T(4,128)S(1)}, u32[]{:S(2)}, u32[]{:S(2)}) collective-permute-start(f32[4,128]{1,0:T(4,128)S(1)} %get-tuple-element.267), channel_id=1, source_target_pairs={{0,2},{1,3},{2,0},{3,1},{4,6},{5,7},{6,4},{7,5},{8,10},{9,11},{10,... | collective-permute-start | bytes 6152 | tf_op jit(solution)/shard_map/ppermute | solution.py:345
  262.7 7.3 %collective-permute-start.34 = (f32[4,128]{1,0:T(4,128)S(1)}, f32[4,128]{1,0:T(4,128)S(1)}, u32[]{:S(2)}, u32[]{:S(2)}) collective-permute-start(f32[4,128]{1,0:T(4,128)S(1)} %get-tuple-element.268), channel_id=1, source_target_pairs={{0,3},{1,0},{2,1},{3,2},{4,7},{5,4},{6,5},{7,6},{8,11},{9,8},{10,9... | collective-permute-start | bytes 6152 | tf_op jit(solution)/shard_map/ppermute | solution.py:345
  (49 other events, 235.0 us)

commit v11 on v10

--- a/solution.py
+++ b/solution.py
@@ -73,7 +73,7 @@
 SLOT_PAD = 64
 F32 = jnp.float32
 BF16 = jnp.bfloat16
-VMEM_BYTES = 36 * 2**20
+VMEM_BYTES = 30 * 2**20
 
 
 def nt_dot(a, b):
@@ -270,27 +270,24 @@
 
 
 def place_kernel(top_k, idx_ref, *refs):
-    count = len(refs) - 5
+    count = len(refs) - 3
     block = refs[0].shape[2] // 2
-    pieces, (out_ref, sum_ref, tails, out_sems, tail_sems) = refs[:count], refs[count:]
+    pieces, (out_ref, sum_ref, out_sems) = refs[:count], refs[count:]
     experts, slots, pair = pieces[0].shape
-    rows = tails.shape[2]
+    rows = 16
     slabs = count // 4
-    stores, loads = [], []
+    stores = []
     for i in range(count):
         for half in range(2):
             column = pl.multiple_of(idx_ref[slabs + 2 * (i % 4) + half] * block, block)
             to = out_ref.at[idx_ref[i // 4], :, :, pl.ds(column, block)]
             part = pieces[i].at[:, :, half * block : (half + 1) * block]
             stores.append(pltpu.make_async_copy(part, to, out_sems.at[2 * i + half]))
-        loads.append(pltpu.make_async_copy(pieces[i].at[:, slots - rows :, :], tails.at[i], tail_sems.at[i]))
-    for copy in loads + stores:
+    for copy in stores:
         copy.start()
-    for copy in loads:
-        copy.wait()
     for k in range(slabs):
         for e in range(experts):
-            total = sum(tails[4 * k + m, e].astype(F32) for m in range(4))
+            total = sum(pieces[4 * k + m][e, slots - rows :].astype(F32) for m in range(4))
             row = total[rows - top_k : rows - top_k + 1]
             sum_ref[k * experts + e : k * experts + e + 1] = row[:, : pair // 2] + row[:, pair // 2 :]
     for copy in stores:
@@ -305,22 +302,20 @@
         grid_spec=pltpu.PrefetchScalarGridSpec(
             num_scalar_prefetch=1,
             grid=(1,),
-            in_specs=[pl.BlockSpec(memory_space=pl.ANY)] * len(pieces),
+            in_specs=[pl.BlockSpec((experts, slots, pair), lambda i, idx: (0, 0, 0))] * len(pieces),
             out_specs=[
                 pl.BlockSpec(memory_space=pl.ANY),
                 pl.BlockSpec((slabs * experts, pair // 2), lambda i, idx: (0, 0)),
             ],
             scratch_shapes=[
-                pltpu.VMEM((len(pieces), experts, 16, pair), BF16),
                 pltpu.SemaphoreType.DMA((2 * len(pieces),)),
-                pltpu.SemaphoreType.DMA((len(pieces),)),
             ],
         ),
         out_shape=[
             jax.ShapeDtypeStruct((slabs, experts, slots, 4 * pair), BF16),
             jax.ShapeDtypeStruct((slabs * experts, pair // 2), F32),
         ],
-        compiler_params=pltpu.CompilerParams(vmem_limit_bytes=60 * 2**20),
+        compiler_params=pltpu.CompilerParams(vmem_limit_bytes=48 * 2**20),
         cost_estimate=pl.CostEstimate(
             flops=0, bytes_accessed=4 * len(pieces) * experts * slots * pair, transcendentals=0
         ),
@@ -372,7 +367,8 @@
     xy0, x1, next2 = across(x0, 4), across(next1, 2), around(next1, 1)
     own3 = around(fence((grad_out, next2))[0], -1)
     partner_weight = across(own_weight, 1)
-    metas = jnp.take(jnp.stack(metas), lax.rem(me - jnp.arange(sources) + sources, sources), axis=0)
+    metas = jnp.stack([metas[(sources - 1 - i) % sources] for i in range(2 * sources - 1)])
+    metas = lax.dynamic_slice_in_dim(metas, sources - 1 - me, sources, axis=0)
     blank = jnp.zeros((experts, sources, SLOT_PAD - most - top_k, pair), BF16)
     metas = jnp.broadcast_to(metas[None], (experts, sources, top_k, pair))
     hidden = []
@@ -405,23 +401,22 @@
 
     xy2, xy3 = across(x2, 4), around(xy0, -1)
     returned0 = send_back(grads0, (0, 1, 2, 3))
+    returned1 = send_back(grads1, (0, 1, 2, 0, 1, 1))
     grads2, scatter2 = kernel([([xy1], 3, 1), ([y2], 2, 2), ([own3], 0, 3), ([y3], 2, 3)])
     first = [grad_out, x0, y0, xy0, next1, x1, y1, next2, x2, x3]
     mine, other = 0, 1
     partner = half_grad(other, [scatter0, scatter1], first, [], experts, 896, False)
-    xy2, xy3, returned0, grads2, scatter2, partner, grads1 = fence(
-        (xy2, xy3, returned0, grads2, scatter2, partner, grads1)
+    xy2, xy3, returned0, returned1, grads2, scatter2, partner = fence(
+        (xy2, xy3, returned0, returned1, grads2, scatter2, partner)
     )
 
     partner = across(partner, 1)
-    returned1 = send_back(grads1, (0, 1, 2, 0, 1, 1))
+    returned2 = send_back(grads2, (3, 2, 0, 2))
     grads3, scatter3 = kernel([([xy2], 3, 2), ([xy3], 3, 3)])
     late = [xy1, y2, own3, y3, xy2, xy3]
     later = half_grad(other, [scatter2, scatter3], late, [], experts, 896, False)
-    partner, later = fence((partner, later))
-    returned1, grads3 = fence((returned1, grads3))
+    partner, returned2, later, grads3, scatter3 = fence((partner, returned2, later, grads3, scatter3))
     later = across(later, 1)
-    returned2 = send_back(grads2, (3, 2, 0, 2))
     returned3 = send_back(grads3, (3, 3))
     returned = [
         *returned0,

time: 286 us -> 232 us (0.81)
  Pallas kernels: 128 us -> 62.6 us
  local copies, waits for them, and re-layouts: 40.5 us -> 51.9 us
  waiting for transfers between devices: 44.6 us -> 50.2 us
  starting transfers between devices: 55.9 us -> 52.8 us
    pallas_call x1, Pallas kernels: 66.3 us -> 2.77 us  [place(): pl.pallas_call(functools.partial(place_kernel, top_k), grid_spec=pltpu.Pr...]
    unnamed x117 -> x151, local copies, waits for them, and re-layouts: 23.2 us -> 38.3 us
    ppermute x12, waiting for transfers between devices: 18.1 us -> 23.9 us  [around(): lax.ppermute(array, 'exp', [(i, (i + shift) % sources) for i in range(sou...]
    ppermute x27, starting transfers between devices: 31.6 us -> 28.4 us  [across(): return lax.ppermute(array, 'rep', [(i, i ^ bits) for i in range(reps)])]
  transfers between devices with their start and end apart: 39 -> 39, of which waited for: 15 -> 14; matrix products, arithmetic and copies ran while one was open for 12% -> 12% of each run, Pallas kernels for 40% -> 21%
where the time goes in v11:
time: 232 us; the launch traced here: 231 us
  Pallas kernels  62.6 us (27%)
  starting transfers between devices  52.8 us (23%)
  local copies, waits for them, and re-layouts  51.9 us (22%)
  waiting for transfers between devices  50.2 us (22%)
  other arithmetic  12.2 us (5%)
    unnamed x151, local copies, waits for them, and re-layouts  38.3 us
    pallas_call x4, Pallas kernels, project(): pl.pallas_call(functools.partial(project_kernel, top_k, sizes, len(items)...  32.5 us
    ppermute x27, starting transfers between devices, across(): return lax.ppermute(array, 'rep', [(i, i ^ bits) for i in range(reps)])  28.4 us
    pallas_call x3, Pallas kernels, half_grad(): pl.pallas_call(functools.partial(half_grad_kernel, len(scatters), len(arr...  27.2 us
    ppermute x27, waiting for transfers between devices, across(): return lax.ppermute(array, 'rep', [(i, i ^ bits) for i in range(reps)])  26.4 us
    ppermute x12, starting transfers between devices, around(): lax.ppermute(array, 'exp', [(i, (i + shift) % sources) for i in range(sou...  24.4 us
    ppermute x12, waiting for transfers between devices, around(): lax.ppermute(array, 'exp', [(i, (i + shift) % sources) for i in range(sou...  23.9 us
    reshape x2, local copies, waits for them, and re-layouts, on_device_tokens(): saved_hidden.reshape(experts, sources, most, 8, block)  7.92 us
  transfers between devices with their start and end apart: 39, of which 14 were waited for; matrix products, arithmetic and copies ran while one was open for 12% of the time, Pallas kernels for 21%

profile of v11, /device:TPU:0, one launch (start us, length us, event | category | flops | bytes accessed | tf_op | source)
XLA Modules:
  0.0 230.8 jit_solution(7222485213365027231)
XLA Ops:
  0.6 3.1 %collective-permute-start.5 = (bf16[128,3584]{1,0:T(8,128)(2,1)}, bf16[128,3584]{1,0:T(8,128)(2,1)S(1)}, u32[]{:S(2)}, u32[]{:S(2)}) collective-permute-start(bf16[128,3584]{1,0:T(8,128)(2,1)} %refs_6_.1), channel_id=1, source_target_pairs={{0,1},{1,2},{2,3},{3,0},{4,5},{5,6},{6,7},{7,4},{8,9},{9,10},{10,1... | collective-permute-start | bytes 2752520 | tf_op jit(solution)/shard_map/ppermute | solution.py:340
  3.7 1.5 collective-permute-start.4
  5.2 1.5 collective-permute-start.3
  8.8 2.7 %collective-permute-start.1 = (bf16[4,256]{1,0:T(4,128)(2,1)S(1)}, bf16[4,256]{1,0:T(4,128)(2,1)S(1)}, u32[]{:S(2)}, u32[]{:S(2)}) collective-permute-start(bf16[4,256]{1,0:T(4,128)(2,1)S(1)} %pad_maximum_fusion.5), channel_id=1, source_target_pairs={{0,2},{1,3},{2,0},{3,1},{4,6},{5,7},{6,4},{7,5},{8,10},{9,11},{10,... | collective-permute-start | bytes 6152 | tf_op jit(solution)/shard_map/ppermute | solution.py:340
  11.7 4.3 %reshape.47 = bf16[4,4,60,8,128]{4,3,1,2,0:T(8,128)(2,1)} reshape(bf16[1,4,4,60,1024]{4,2,3,1,0:T(4,128)(2,1)} %param.8) | data formatting | bytes 3932160 | tf_op jit(solution)/shard_map/reshape | solution.py:359
  16.0 3.6 %copy.15 = bf16[4,4,60,8,128]{4,2,1,0,3:T(8,128)(2,1)} copy(bf16[4,4,60,8,128]{4,3,1,2,0:T(8,128)(2,1)} %reshape.47) | data formatting | bytes 3932160 | tf_op jit(solution)/shard_map/reshape | solution.py:359
  19.6 2.8 %dynamic-slice_bitcast_fusion = (bf16[4,4,60,128]{3,2,1,0:T(8,128)(2,1)S(1)}, bf16[4,4,60,128]{3,2,1,0:T(8,128)(2,1)S(1)}, bf16[4,4,60,128]{3,2,1,0:T(8,128)(2,1...) fusion(bf16[8,4,4,60,128]{4,3,2,1,0:T(8,128)(2,1)} %bitcast.65,, ...), kind=kLoop, calls=%fused_computation.7 | loop fusion | bytes 3932192 | tf_op jit(solution)/shard_map/jit(dynamic_index_in_dim)/squeeze | solution.py:361
  22.4 2.4 %copy.12 = bf16[4,128,3584]{2,1,0:T(8,128)(2,1)} copy(bf16[4,128,3584]{2,0,1:T(4,128)(2,1)S(1)} %bitcast.66) | data formatting | bytes 7340032 | tf_op jit(solution)/shard_map/transpose | solution.py:362
  24.8 3.6 %collective-permute-start.2 = (bf16[4,256]{1,0:T(4,128)(2,1)S(1)}, bf16[4,256]{1,0:T(4,128)(2,1)S(1)}, u32[]{:S(2)}, u32[]{:S(2)}) collective-permute-start(bf16[4,256]{1,0:T(4,128)(2,1)S(1)} %pad_maximum_fusion.5), channel_id=1, source_target_pairs={{0,3},{1,0},{2,1},{3,2},{4,7},{5,4},{6,5},{7,6},{8,11},{9,8},{10,9... | collective-permute-start | bytes 6152 | tf_op jit(solution)/shard_map/ppermute | solution.py:340
  30.7 1.5 collective-permute-start.6
  32.2 1.5 collective-permute-start.9
  33.9 2.5 %pad_maximum_fusion.1 = (bf16[4,4,64,256]{3,2,1,0:T(8,128)(2,1)S(1)}, bf16[4,4,64,256]{3,2,1,0:T(8,128)(2,1)S(1)}, bf16[4,4,64,256]{3,2,1,0:T(8,128)(2,1)S(1)}, bf16[4,4,64,256]{3,2,1,0:T(8,128)(2,1)}) fusion(bf16[4,4,4,256]{3,2,1,0:T(4,128)(2,1)S(1)} %broadcast_in_dim.49, bf16[4,4,60,128]{3,2,1,0:T(8,128)(2,1)S(1)} %get-tuple-element.144, ...), kind=kLoop, calls=%fused_computation.3 | loop fusion | flops 5505024 | bytes 4096000 | tf_op jit(solution)/shard_map/concatenate | solution.py:377
  36.8 18.2 %collective-permute-done.11.refs_3_.refs_9_.refs_13_ = bf16[128,3584]{1,0:T(8,128)(2,1)} collective-permute-done((bf16[128,3584]{1,0:T(8,128)(2,1)S(1)}, bf16[128,3584]{1,0:T(8,128)(2,1)}, u32[]{:S(2)}, u32[]{:S(2)}) %collective-permute-start.11) | collective-permute-done | bytes 917536 | tf_op jit(solution)/shard_map/ppermute | solution.py:340
  55.0 1.7 collective-permute-start.12
  56.8 8.7 %collective-permute-done.7.refs_9_.refs_6_.refs_4_.refs_5_ = bf16[4,4,64,256]{3,2,1,0:T(8,128)(2,1)S(1)} collective-permute-done((bf16[4,4,64,256]{3,2,1,0:T(8,128)(2,1)S(1)}, bf16[4,4,64,256]{3,2,1,0:T(8,128)(2,1)S(1)}, u32[]{:S(2)}, u32[]{:S(2)}) %collective-permute-start.7) | collective-permute-done | bytes 524320 | tf_op jit(solution)/shard_map/ppermute | solution.py:337
  65.9 1.5 collective-permute-start.10
  68.0 6.9 %pad_maximum_fusion.refs_4_.refs_5_.refs_6_.refs_7_.refs_2_.refs_3_ = bf16[2,512,3584]{2,1,0:T(8,128)(2,1)} fusion(bf16[1,512,3584]{2,1,0:T(8,128)(2,1)} %bitcast.31, bf16[1,512,3584]{2,1,0:T(8,128)(2,1)} %bitcast.30), kind=kLoop, calls=%fused_computation | loop fusion | flops 3670016 | bytes 14680064 | tf_op jit(solution)/shard_map/stack | solution.py:385
  74.8 3.7 %collective-permute-done.10.refs_8_.refs_10_.refs_7_.refs_9_ = bf16[4,4,64,256]{3,2,1,0:T(8,128)(2,1)S(1)} collective-permute-done((bf16[4,4,64,256]{3,2,1,0:T(8,128)(2,1)S(1)}, bf16[4,4,64,256]{3,2,1,0:T(8,128)(2,1)S(1)}, u32[]{:S(2)}, u32[]{:S(2)}) %collective-permute-start.10) | collective-permute-done | bytes 524320 | tf_op jit(solution)/shard_map/ppermute | solution.py:337
  83.5 3.4 %collective-permute-start.16 = (bf16[128,3584]{1,0:T(8,128)(2,1)}, bf16[128,3584]{1,0:T(8,128)(2,1)}, u32[]{:S(2)}, u32[]{:S(2)}) collective-permute-start(bf16[128,3584]{1,0:T(8,128)(2,1)} %collective-permute-done.3.refs_1_.refs_3_.refs_7_), channel_id=1, source_target_pairs={{0,3},{1,0},{2,1},{3,2},{4,7},{5,4},{6,5},{7,6},{8,11},{9,8},{10,9... | collective-permute-start | bytes 2752520 | tf_op jit(solution)/shard_map/ppermute | solution.py:340
  87.0 3.1 %copy-done = bf16[2,512,3584]{2,1,0:T(8,128)(2,1)S(1)} copy-done((bf16[2,512,3584]{2,1,0:T(8,128)(2,1)S(1)}, bf16[2,512,3584]{2,1,0:T(8,128)(2,1)}, u32[]{:S(2)}) %copy-start) | copy-done | bytes 7340056
  93.2 8.4 %shard_map.76 = (bf16[4,64,256]{2,1,0:T(8,128)(2,1)S(1)}, bf16[4,64,256]{2,1,0:T(8,128)(2,1)S(1)}, bf16[4,64,256]{2,1,0:T(8,128)(2,1)S(1)}, bf16[4,64,256]{2,1,0:T(8,128)(2,1)S(1)}, bf16[2,512,512]{2,1,0:T(8,128)(2,1)S(1)}) custom-call(s32[5]{0:T(128)S(1)} %stack.98.idx_ref, bf16[128,3584]{1,0:T(8,128)(2,1)S(1)} %copy-done.19, ...), custom_call_target="tpu_custom_call" | custom-call | flops 7516192768 | bytes 11010048 | tf_op jit(solution)/shard_map/pallas_call | solution.py:178
  103.0 1.8 collective-permute-done.16.refs_5_.refs_11_.refs_15_
  104.8 4.3 %collective-permute-start.19 = (bf16[128,3584]{1,0:T(8,128)(2,1)S(1)}, bf16[128,3584]{1,0:T(8,128)(2,1)S(1)}, u32[]{:S(2)}, u32[]{:S(2)}) collective-permute-start(bf16[128,3584]{1,0:T(8,128)(2,1)S(1)} %collective-permute-done.4.refs_2_.refs_4_.refs_8_), channel_id=1, source_target_pairs={{0,3},{1,0},{2,1},{3,2},{4,7},{5,4},{6,5},{7,6},{8,11},{9,8},{10,9... | collective-permute-start | bytes 2752520 | tf_op jit(solution)/shard_map/ppermute | solution.py:340
  111.1 12.1 %shard_map.77 = (bf16[4,64,256]{2,1,0:T(8,128)(2,1)S(1)}, bf16[4,64,256]{2,1,0:T(8,128)(2,1)S(1)}, bf16[4,64,256]{2,1,0:T(8,128)(2,1)S(1)}, bf16[4,64,256]{2,1,0...) custom-call(s32[5]{0:T(128)S(1)} %stack.98.idx_ref, ...), custom_call_target="tpu_custom_call" | custom-call | flops 11274289152 | bytes 12845056 | tf_op jit(solution)/shard_map/pallas_call | solution.py:178
  123.2 2.5 %collective-permute-done.19.refs_3_.refs_5_.refs_19_ = bf16[128,3584]{1,0:T(8,128)(2,1)S(1)} collective-permute-done((bf16[128,3584]{1,0:T(8,128)(2,1)S(1)}, bf16[128,3584]{1,0:T(8,128)(2,1)S(1)}, u32[]{:S(2)}, u32[]{:S(2)}) %collective-permute-start.19) | collective-permute-done | bytes 917536 | tf_op jit(solution)/shard_map/ppermute | solution.py:340
  125.7 3.3 %collective-permute-done.17.refs_0_.refs_2_.refs_16_ = bf16[128,3584]{1,0:T(8,128)(2,1)S(1)} collective-permute-done((bf16[128,3584]{1,0:T(8,128)(2,1)}, bf16[128,3584]{1,0:T(8,128)(2,1)S(1)}, u32[]{:S(2)}, u32[]{:S(2)}) %collective-permute-start.17) | collective-permute-done | bytes 917536 | tf_op jit(solution)/shard_map/ppermute | solution.py:337
  130.3 1.4 collective-permute-start.22
  131.7 2.5 %collective-permute-start.23 = (bf16[4,64,256]{2,1,0:T(8,128)(2,1)S(1)}, bf16[4,64,256]{2,1,0:T(8,128)(2,1)S(1)}, u32[]{:S(2)}, u32[]{:S(2)}) collective-permute-start(bf16[4,64,256]{2,1,0:T(8,128)(2,1)S(1)} %get-tuple-element.188), channel_id=1, source_target_pairs={{0,16},{4,20},{8,24},{12,28},{16,0},{20,4},{24,8},{28,12},{1,17},{... | collective-permute-start | bytes 393224 | tf_op jit(solution)/shard_map/ppermute | solution.py:337
  134.3 1.5 collective-permute-start.25
  135.7 2.0 collective-permute-start.20
  137.8 7.4 %shard_map.78 = (bf16[4,64,256]{2,1,0:T(8,128)(2,1)S(1)}, bf16[4,64,256]{2,1,0:T(8,128)(2,1)S(1)}, bf16[4,64,256]{2,1,0:T(8,128)(2,1)S(1)}, bf16[4,64,256]{2,1,0:T(8,128)(2,1)S(1)}, bf16[2,512,512]{2,1,0:T(8,128)(2,1)S(1)}) custom-call(s32[5]{0:T(128)S(1)} %stack.98.idx_ref, bf16[128,3584]{1,0:T(8,128)(2,1)S(1)} %collective-permute-done.17.refs_0_.refs_2_.refs_16_, ...), custom_call_target="tpu_custom_call" | custom-call | flops 7516192768 | bytes 11010048 | tf_op jit(solution)/shard_map/pallas_call | solution.py:178
  147.3 1.4 collective-permute-start.27
  150.0 8.3 %shard_map.79 = bf16[512,3584]{1,0:T(8,128)(2,1)S(1)} custom-call(bf16[2,512,512]{2,1,0:T(8,128)(2,1)S(1)} %get-tuple-element.205.refs_0_, bf16[2,512,768]{2,1,0:T(8,128)(2,1)S(1)} %get-tuple-element.206.refs_1_, bf16[128,3584]{1,0:T(8,128)(2,1)S(1)} %copy-done.20, bf16[128,3584]{1,0:T(8,128)(2,1)} %collective-permute-done.3.refs_1_.refs_3_.refs_7_, ...), custom_call_target="tpu_custom_call" | custom-call | flops 4697620480 | bytes 17825792 | tf_op jit(solution)/shard_map/pallas_call | solution.py:256
  158.3 1.8 copy-done.59
  162.1 1.5 collective-permute-start.30
  163.6 1.4 collective-permute-start.31
  165.6 4.7 %shard_map.80 = (bf16[4,64,256]{2,1,0:T(8,128)(2,1)S(1)}, bf16[4,64,256]{2,1,0:T(8,128)(2,1)S(1)}, bf16[2,512,256]{2,1,0:T(8,128)(2,1)S(1)}) custom-call(s32[5]{0:T(128)S(1)} %stack.98.idx_ref, bf16[128,3584]{1,0:T(8,128)(2,1)S(1)} %collective-permute-done.20.refs_0_.refs_6_.refs_20_, bf16[128,3584]{1,0:T(8,128)(2,1)S(1)} %collective-permute-done.21.refs_1_.refs_7_.refs_21_, ...), custom_call_target="tpu_custom_call" | custom-call | flops 3758096384 | bytes 9175040 | tf_op jit(solution)/shard_map/pallas_call | solution.py:178
  170.3 5.6 %shard_map.81 = bf16[512,3584]{1,0:T(8,128)(2,1)} custom-call(bf16[2,512,512]{2,1,0:T(8,128)(2,1)S(1)} %get-tuple-element.219.refs_0_.refs_2_, bf16[2,512,256]{2,1,0:T(8,128)(2,1)S(1)} %get-tuple-element.236.refs_1_.refs_3_, bf16[128,3584]{1,0:T(8,128)(2,1)S(1)} %collective-permute-done.17.refs_0_.refs_2_.refs_16_, ...), custom_call_target="tpu_custom_call" | custom-call | flops 2818572288 | bytes 13631488 | tf_op jit(solution)/shard_map/pallas_call | solution.py:256
  177.9 1.8 copy-done.2
  179.8 1.5 collective-permute-start.33
  181.2 1.5 collective-permute-start.34
  182.8 4.5 %collective-permute-done.33.refs_11_ = bf16[4,64,256]{2,1,0:T(8,128)(2,1)} collective-permute-done((bf16[4,64,256]{2,1,0:T(8,128)(2,1)}, bf16[4,64,256]{2,1,0:T(8,128)(2,1)}, u32[]{:S(2)}, u32[]{:S(2)}) %collective-permute-start.33) | collective-permute-done | bytes 131104 | tf_op jit(solution)/shard_map/ppermute | solution.py:337
  187.3 2.4 %collective-permute-done.34.refs_15_ = bf16[4,64,256]{2,1,0:T(8,128)(2,1)} collective-permute-done((bf16[4,64,256]{2,1,0:T(8,128)(2,1)}, bf16[4,64,256]{2,1,0:T(8,128)(2,1)}, u32[]{:S(2)}, u32[]{:S(2)}) %collective-permute-start.34) | collective-permute-done | bytes 131104 | tf_op jit(solution)/shard_map/ppermute | solution.py:337
  201.5 2.8 %shard_map.82 = (bf16[4,4,64,1024]{3,2,1,0:T(8,128)(2,1)S(1)}, f32[16,128]{1,0:T(8,128)S(1)}) custom-call(s32[12]{0:T(128)S(1)} %stack.88.idx_ref, bf16[4,64,256]{2,1,0:T(8,128)(2,1)S(1)} %get-tuple-element.207.refs_0_, bf16[4,64,256]{2,1,0:T(8,128)(2,1)S(1)} %copy-done.38, bf16[4,64,256]{2,1,0:T(8,128)(2,1)S(1)} %copy-done.40, ...), custom_call_target="tpu_custom_call" | custom-call | bytes 4194304 | tf_op jit(solution)/shard_map/pallas_call | solution.py:300
  204.3 2.1 collective-permute-start.37
  206.3 2.4 %collective-permute-start.35 = (f32[4,128]{1,0:T(4,128)S(1)}, f32[4,128]{1,0:T(4,128)S(1)}, u32[]{:S(2)}, u32[]{:S(2)}) collective-permute-start(f32[4,128]{1,0:T(4,128)S(1)} %get-tuple-element.266), channel_id=1, source_target_pairs={{0,3},{1,0},{2,1},{3,2},{4,7},{5,4},{6,5},{7,6},{8,11},{9,8},{10,9... | collective-permute-start | bytes 6152 | tf_op jit(solution)/shard_map/ppermute | solution.py:340
  209.1 2.8 %copy.13 = bf16[1,4,4,60,1024]{4,2,3,1,0:T(4,128)(2,1)} copy(bf16[1,4,4,60,1024]{4,3,1,2,0:T(8,128)(2,1)S(1)} %slice_bitcast_fusion) | data formatting | bytes 3932160
  217.4 13.4 %shard_map.83 = f32[128,4,3584]{2,1,0:T(4,128)} custom-call(bf16[2,512,512]{2,1,0:T(8,128)(2,1)S(1)} %copy-done.18, bf16[2,512,768]{2,1,0:T(8,128)(2,1)S(1)} %copy-done.16, bf16[2,512,512]{2,1,0:T(8,128)(2,1)S(1)} %get-tuple-element.219.refs_0_.refs_2_, bf16[2,512,256]{2,1,0:T(8,128)(2,1)S(1)} %get-tuple-element.236.refs_1_.refs_3_, ...), custom_call_target="tpu_custom_call" | custom-call | flops 7516192768 | bytes 24117248 | tf_op jit(solution)/shard_map/pallas_call | solution.py:256
  (211 shorter events, 44.4 us)
Async XLA Ops:
  0.6 29.1 %collective-permute-start.5 = (bf16[128,3584]{1,0:T(8,128)(2,1)}, bf16[128,3584]{1,0:T(8,128)(2,1)S(1)}, u32[]{:S(2)}, u32[]{:S(2)}) collective-permute-start(bf16[128,3584]{1,0:T(8,128)(2,1)} %refs_6_.1), channel_id=1, source_target_pairs={{0,1},{1,2},{2,3},{3,0},{4,5},{5,6},{6,7},{7,4},{8,9},{9,10},{10,1... | collective-permute-start | bytes 2752520 | tf_op jit(solution)/shard_map/ppermute | solution.py:340
  3.7 26.0 %collective-permute-start.4 = (bf16[128,3584]{1,0:T(8,128)(2,1)}, bf16[128,3584]{1,0:T(8,128)(2,1)S(1)}, u32[]{:S(2)}, u32[]{:S(2)}) collective-permute-start(bf16[128,3584]{1,0:T(8,128)(2,1)} %refs_6_.1), channel_id=1, source_target_pairs={{0,16},{4,20},{8,24},{12,28},{16,0},{20,4},{24,8},{28,12},{1,17},{... | collective-permute-start | bytes 2752520 | tf_op jit(solution)/shard_map/ppermute | solution.py:337
  5.2 24.5 %collective-permute-start.3 = (bf16[128,3584]{1,0:T(8,128)(2,1)}, bf16[128,3584]{1,0:T(8,128)(2,1)}, u32[]{:S(2)}, u32[]{:S(2)}) collective-permute-start(bf16[128,3584]{1,0:T(8,128)(2,1)} %refs_6_.1), channel_id=1, source_target_pairs={{0,8},{4,12},{8,0},{12,4},{16,24},{20,28},{24,16},{28,20},{1,9},{5... | collective-permute-start | bytes 2752520 | tf_op jit(solution)/shard_map/ppermute | solution.py:337
  8.8 16.0 %collective-permute-start.1 = (bf16[4,256]{1,0:T(4,128)(2,1)S(1)}, bf16[4,256]{1,0:T(4,128)(2,1)S(1)}, u32[]{:S(2)}, u32[]{:S(2)}) collective-permute-start(bf16[4,256]{1,0:T(4,128)(2,1)S(1)} %pad_maximum_fusion.5), channel_id=1, source_target_pairs={{0,2},{1,3},{2,0},{3,1},{4,6},{5,7},{6,4},{7,5},{8,10},{9,11},{10,... | collective-permute-start | bytes 6152 | tf_op jit(solution)/shard_map/ppermute | solution.py:340
  11.5 17.0 %collective-permute-start = (bf16[4,256]{1,0:T(4,128)(2,1)S(1)}, bf16[4,256]{1,0:T(4,128)(2,1)S(1)}, u32[]{:S(2)}, u32[]{:S(2)}) collective-permute-start(bf16[4,256]{1,0:T(4,128)(2,1)S(1)} %pad_maximum_fusion.5), channel_id=1, source_target_pairs={{0,1},{1,2},{2,3},{3,0},{4,5},{5,6},{6,7},{7,4},{8,9},{9,10},{10,1... | collective-permute-start | bytes 6152 | tf_op jit(solution)/shard_map/ppermute | solution.py:340
  24.8 4.9 %collective-permute-start.2 = (bf16[4,256]{1,0:T(4,128)(2,1)S(1)}, bf16[4,256]{1,0:T(4,128)(2,1)S(1)}, u32[]{:S(2)}, u32[]{:S(2)}) collective-permute-start(bf16[4,256]{1,0:T(4,128)(2,1)S(1)} %pad_maximum_fusion.5), channel_id=1, source_target_pairs={{0,3},{1,0},{2,1},{3,2},{4,7},{5,4},{6,5},{7,6},{8,11},{9,8},{10,9... | collective-permute-start | bytes 6152 | tf_op jit(solution)/shard_map/ppermute | solution.py:340
  29.7 81.3 %copy-start.22 = (bf16[128,3584]{1,0:T(8,128)(2,1)}, bf16[128,3584]{1,0:T(8,128)(2,1)S(1)}, u32[]{:S(2)}) copy-start(bf16[128,3584]{1,0:T(8,128)(2,1)S(1)} %collective-permute-done.5.refs_0_.refs_6_.refs_10_) | copy-start | bytes 2752516
  29.7 75.0 %copy-start.25 = (bf16[128,3584]{1,0:T(8,128)(2,1)}, bf16[128,3584]{1,0:T(8,128)(2,1)S(1)}, u32[]{:S(2)}) copy-start(bf16[128,3584]{1,0:T(8,128)(2,1)S(1)} %collective-permute-done.4.refs_2_.refs_4_.refs_8_) | copy-start | bytes 2752516
  29.7 38.2 %collective-permute-start.13 = (bf16[512,3584]{1,0:T(8,128)(2,1)}, bf16[512,3584]{1,0:T(8,128)(2,1)}, u32[]{:S(2)}, u32[]{:S(2)}) collective-permute-start(bf16[512,3584]{1,0:T(8,128)(2,1)} %bitcast.25), channel_id=1, source_target_pairs={{0,4},{4,0},{8,12},{12,8},{16,20},{20,16},{24,28},{28,24},{1,5},{5... | collective-permute-start | bytes 11010056 | tf_op jit(solution)/shard_map/ppermute | solution.py:337
  29.8 25.2 %collective-permute-start.11 = (bf16[128,3584]{1,0:T(8,128)(2,1)S(1)}, bf16[128,3584]{1,0:T(8,128)(2,1)}, u32[]{:S(2)}, u32[]{:S(2)}) collective-permute-start(bf16[128,3584]{1,0:T(8,128)(2,1)S(1)} %collective-permute-done.5.refs_0_.refs_6_.refs_10_), channel_id=1, source_target_pairs={{0,1},{1,2},{2,3},{3,0},{4,5},{5,6},{6,7},{7,4},{8,9},{9,10},{10,1... | collective-permute-start | bytes 2752520 | tf_op jit(solution)/shard_map/ppermute | solution.py:340
  30.7 36.7 %collective-permute-start.6 = (bf16[128,3584]{1,0:T(8,128)(2,1)S(1)}, bf16[128,3584]{1,0:T(8,128)(2,1)S(1)}, u32[]{:S(2)}, u32[]{:S(2)}) collective-permute-start(bf16[128,3584]{1,0:T(8,128)(2,1)S(1)} %collective-permute-done.5.refs_0_.refs_6_.refs_10_), channel_id=1, source_target_pairs={{0,8},{4,12},{8,0},{12,4},{16,24},{20,28},{24,16},{28,20},{1,9},{5... | collective-permute-start | bytes 2752520 | tf_op jit(solution)/shard_map/ppermute | solution.py:337
  32.2 33.7 %collective-permute-start.9 = (bf16[128,3584]{1,0:T(8,128)(2,1)}, bf16[128,3584]{1,0:T(8,128)(2,1)}, u32[]{:S(2)}, u32[]{:S(2)}) collective-permute-start(bf16[128,3584]{1,0:T(8,128)(2,1)} %collective-permute-done.3.refs_1_.refs_3_.refs_7_), channel_id=1, source_target_pairs={{0,16},{4,20},{8,24},{12,28},{16,0},{20,4},{24,8},{28,12},{1,17},{... | collective-permute-start | bytes 2752520 | tf_op jit(solution)/shard_map/ppermute | solution.py:337
  36.3 29.1 %collective-permute-start.7 = (bf16[4,4,64,256]{3,2,1,0:T(8,128)(2,1)S(1)}, bf16[4,4,64,256]{3,2,1,0:T(8,128)(2,1)S(1)}, u32[]{:S(2)}, u32[]{:S(2)}) collective-permute-start(bf16[4,4,64,256]{3,2,1,0:T(8,128)(2,1)S(1)} %get-tuple-element.261), channel_id=1, source_target_pairs={{0,24},{4,28},{8,16},{12,20},{16,8},{20,12},{24,0},{28,4},{1,25},{... | collective-permute-start | bytes 1572872 | tf_op jit(solution)/shard_map/ppermute | solution.py:337
  55.0 25.8 %collective-permute-start.12 = (bf16[128,3584]{1,0:T(8,128)(2,1)S(1)}, bf16[128,3584]{1,0:T(8,128)(2,1)S(1)}, u32[]{:S(2)}, u32[]{:S(2)}) collective-permute-start(bf16[128,3584]{1,0:T(8,128)(2,1)S(1)} %copy-done.19), channel_id=1, source_target_pairs={{0,3},{1,0},{2,1},{3,2},{4,7},{5,4},{6,5},{7,6},{8,11},{9,8},{10,9... | collective-permute-start | bytes 2752520 | tf_op jit(solution)/shard_map/ppermute | solution.py:340
  65.4 72.3 %copy-start.13 = (bf16[4,4,64,256]{3,2,1,0:T(8,128)(2,1)}, bf16[4,4,64,256]{3,2,1,0:T(8,128)(2,1)S(1)}, u32[]{:S(2)}) copy-start(bf16[4,4,64,256]{3,2,1,0:T(8,128)(2,1)S(1)} %collective-permute-done.7.refs_9_.refs_6_.refs_4_.refs_5_) | copy-start | bytes 1572868
  65.9 12.6 %collective-permute-start.10 = (bf16[4,4,64,256]{3,2,1,0:T(8,128)(2,1)S(1)}, bf16[4,4,64,256]{3,2,1,0:T(8,128)(2,1)S(1)}, u32[]{:S(2)}, u32[]{:S(2)}) collective-permute-start(bf16[4,4,64,256]{3,2,1,0:T(8,128)(2,1)S(1)} %get-tuple-element.146), channel_id=1, source_target_pairs={{0,16},{4,20},{8,24},{12,28},{16,0},{20,4},{24,8},{28,12},{1,17},{... | collective-permute-start | bytes 1572872 | tf_op jit(solution)/shard_map/ppermute | solution.py:337
  67.4 12.6 %collective-permute-start.8 = (bf16[4,4,64,256]{3,2,1,0:T(8,128)(2,1)S(1)}, bf16[4,4,64,256]{3,2,1,0:T(8,128)(2,1)S(1)}, u32[]{:S(2)}, u32[]{:S(2)}) collective-permute-start(bf16[4,4,64,256]{3,2,1,0:T(8,128)(2,1)S(1)} %get-tuple-element.142), channel_id=1, source_target_pairs={{0,8},{4,12},{8,0},{12,4},{16,24},{20,28},{24,16},{28,20},{1,9},{5... | collective-permute-start | bytes 1572872 | tf_op jit(solution)/shard_map/ppermute | solution.py:337
  81.7 20.4 %collective-permute-start.15 = (bf16[128,3584]{1,0:T(8,128)(2,1)}, bf16[128,3584]{1,0:T(8,128)(2,1)}, u32[]{:S(2)}, u32[]{:S(2)}) collective-permute-start(bf16[128,3584]{1,0:T(8,128)(2,1)} %collective-permute-done.11.refs_3_.refs_9_.refs_13_), channel_id=1, source_target_pairs={{0,8},{4,12},{8,0},{12,4},{16,24},{20,28},{24,16},{28,20},{1,9},{5... | collective-permute-start | bytes 2752520 | tf_op jit(solution)/shard_map/ppermute | solution.py:337
  82.5 20.5 %collective-permute-start.14 = (bf16[128,3584]{1,0:T(8,128)(2,1)S(1)}, bf16[128,3584]{1,0:T(8,128)(2,1)}, u32[]{:S(2)}, u32[]{:S(2)}) collective-permute-start(bf16[128,3584]{1,0:T(8,128)(2,1)S(1)} %collective-permute-done.5.refs_0_.refs_6_.refs_10_), channel_id=1, source_target_pairs={{0,16},{4,20},{8,24},{12,28},{16,0},{20,4},{24,8},{28,12},{1,17},{... | collective-permute-start | bytes 2752520 | tf_op jit(solution)/shard_map/ppermute | solution.py:337
  83.5 21.3 %collective-permute-start.16 = (bf16[128,3584]{1,0:T(8,128)(2,1)}, bf16[128,3584]{1,0:T(8,128)(2,1)}, u32[]{:S(2)}, u32[]{:S(2)}) collective-permute-start(bf16[128,3584]{1,0:T(8,128)(2,1)} %collective-permute-done.3.refs_1_.refs_3_.refs_7_), channel_id=1, source_target_pairs={{0,3},{1,0},{2,1},{3,2},{4,7},{5,4},{6,5},{7,6},{8,11},{9,8},{10,9... | collective-permute-start | bytes 2752520 | tf_op jit(solution)/shard_map/ppermute | solution.py:340
  101.6 48.3 %copy-start.17 = (bf16[2,512,512]{2,1,0:T(8,128)(2,1)}, bf16[2,512,512]{2,1,0:T(8,128)(2,1)S(1)}, u32[]{:S(2)}) copy-start(bf16[2,512,512]{2,1,0:T(8,128)(2,1)S(1)} %get-tuple-element.205.refs_0_) | copy-start | bytes 3145732
  104.8 33.0 %copy-start.5 = (bf16[128,3584]{1,0:T(8,128)(2,1)S(1)}, bf16[128,3584]{1,0:T(8,128)(2,1)}, u32[]{:S(2)}) copy-start(bf16[128,3584]{1,0:T(8,128)(2,1)} %copy-done.4) | copy-start | bytes 2752516
  104.8 33.0 %copy-start.62 = (bf16[4,4,64,256]{3,2,1,0:T(8,128)(2,1)S(1)}, bf16[4,4,64,256]{3,2,1,0:T(8,128)(2,1)}, u32[]{:S(2)}) copy-start(bf16[4,4,64,256]{3,2,1,0:T(8,128)(2,1)} %copy-done.60) | copy-start | bytes 1572868
  104.8 20.9 %collective-permute-start.19 = (bf16[128,3584]{1,0:T(8,128)(2,1)S(1)}, bf16[128,3584]{1,0:T(8,128)(2,1)S(1)}, u32[]{:S(2)}, u32[]{:S(2)}) collective-permute-start(bf16[128,3584]{1,0:T(8,128)(2,1)S(1)} %collective-permute-done.4.refs_2_.refs_4_.refs_8_), channel_id=1, source_target_pairs={{0,3},{1,0},{2,1},{3,2},{4,7},{5,4},{6,5},{7,6},{8,11},{9,8},{10,9... | collective-permute-start | bytes 2752520 | tf_op jit(solution)/shard_map/ppermute | solution.py:340
  109.1 20.0 %collective-permute-start.17 = (bf16[128,3584]{1,0:T(8,128)(2,1)}, bf16[128,3584]{1,0:T(8,128)(2,1)S(1)}, u32[]{:S(2)}, u32[]{:S(2)}) collective-permute-start(bf16[128,3584]{1,0:T(8,128)(2,1)} %collective-permute-done.14.refs_2_.refs_8_.refs_12_), channel_id=1, source_target_pairs={{0,8},{4,12},{8,0},{12,4},{16,24},{20,28},{24,16},{28,20},{1,9},{5... | collective-permute-start | bytes 2752520 | tf_op jit(solution)/shard_map/ppermute | solution.py:337
  110.4 19.9 %collective-permute-start.18 = (bf16[128,3584]{1,0:T(8,128)(2,1)}, bf16[128,3584]{1,0:T(8,128)(2,1)S(1)}, u32[]{:S(2)}, u32[]{:S(2)}) collective-permute-start(bf16[128,3584]{1,0:T(8,128)(2,1)} %collective-permute-done.11.refs_3_.refs_9_.refs_13_), channel_id=1, source_target_pairs={{0,16},{4,20},{8,24},{12,28},{16,0},{20,4},{24,8},{28,12},{1,17},{... | collective-permute-start | bytes 2752520 | tf_op jit(solution)/shard_map/ppermute | solution.py:337
  125.7 44.6 %copy-start.7 = (bf16[128,3584]{1,0:T(8,128)(2,1)}, bf16[128,3584]{1,0:T(8,128)(2,1)S(1)}, u32[]{:S(2)}) copy-start(bf16[128,3584]{1,0:T(8,128)(2,1)S(1)} %collective-permute-done.19.refs_3_.refs_5_.refs_19_) | copy-start | bytes 2752516
  129.0 41.3 %copy-start.9 = (bf16[128,3584]{1,0:T(8,128)(2,1)}, bf16[128,3584]{1,0:T(8,128)(2,1)S(1)}, u32[]{:S(2)}) copy-start(bf16[128,3584]{1,0:T(8,128)(2,1)S(1)} %collective-permute-done.17.refs_0_.refs_2_.refs_16_) | copy-start | bytes 2752516
  130.3 40.0 %copy-start.11 = (bf16[128,3584]{1,0:T(8,128)(2,1)}, bf16[128,3584]{1,0:T(8,128)(2,1)S(1)}, u32[]{:S(2)}) copy-start(bf16[128,3584]{1,0:T(8,128)(2,1)S(1)} %collective-permute-done.18.refs_1_.refs_3_.refs_17_) | copy-start | bytes 2752516
  130.3 7.5 %collective-permute-start.22 = (bf16[4,64,256]{2,1,0:T(8,128)(2,1)S(1)}, bf16[4,64,256]{2,1,0:T(8,128)(2,1)S(1)}, u32[]{:S(2)}, u32[]{:S(2)}) collective-permute-start(bf16[4,64,256]{2,1,0:T(8,128)(2,1)S(1)} %get-tuple-element.187), channel_id=1, source_target_pairs={{0,8},{4,12},{8,0},{12,4},{16,24},{20,28},{24,16},{28,20},{1,9},{5... | collective-permute-start | bytes 393224 | tf_op jit(solution)/shard_map/ppermute | solution.py:337
  131.7 14.2 %collective-permute-start.23 = (bf16[4,64,256]{2,1,0:T(8,128)(2,1)S(1)}, bf16[4,64,256]{2,1,0:T(8,128)(2,1)S(1)}, u32[]{:S(2)}, u32[]{:S(2)}) collective-permute-start(bf16[4,64,256]{2,1,0:T(8,128)(2,1)S(1)} %get-tuple-element.188), channel_id=1, source_target_pairs={{0,16},{4,20},{8,24},{12,28},{16,0},{20,4},{24,8},{28,12},{1,17},{... | collective-permute-start | bytes 393224 | tf_op jit(solution)/shard_map/ppermute | solution.py:337
  134.3 12.3 %collective-permute-start.24 = (bf16[4,64,256]{2,1,0:T(8,128)(2,1)S(1)}, bf16[4,64,256]{2,1,0:T(8,128)(2,1)S(1)}, u32[]{:S(2)}, u32[]{:S(2)}) collective-permute-start(bf16[4,64,256]{2,1,0:T(8,128)(2,1)S(1)} %get-tuple-element.189), channel_id=1, source_target_pairs={{0,24},{4,28},{8,16},{12,20},{16,8},{20,12},{24,0},{28,4},{1,25},{... | collective-permute-start | bytes 393224 | tf_op jit(solution)/shard_map/ppermute | solution.py:337
  134.3 14.4 %collective-permute-start.25 = (bf16[4,64,256]{2,1,0:T(8,128)(2,1)S(1)}, bf16[4,64,256]{2,1,0:T(8,128)(2,1)S(1)}, u32[]{:S(2)}, u32[]{:S(2)}) collective-permute-start(bf16[4,64,256]{2,1,0:T(8,128)(2,1)S(1)} %get-tuple-element.191), channel_id=1, source_target_pairs={{0,8},{4,12},{8,0},{12,4},{16,24},{20,28},{24,16},{28,20},{1,9},{5... | collective-permute-start | bytes 393224 | tf_op jit(solution)/shard_map/ppermute | solution.py:337
  135.7 26.3 %collective-permute-start.20 = (bf16[128,3584]{1,0:T(8,128)(2,1)}, bf16[128,3584]{1,0:T(8,128)(2,1)S(1)}, u32[]{:S(2)}, u32[]{:S(2)}) collective-permute-start(bf16[128,3584]{1,0:T(8,128)(2,1)} %collective-permute-done.15.refs_4_.refs_10_.refs_14_), channel_id=1, source_target_pairs={{0,16},{4,20},{8,24},{12,28},{16,0},{20,4},{24,8},{28,12},{1,17},{... | collective-permute-start | bytes 2752520 | tf_op jit(solution)/shard_map/ppermute | solution.py:337
  137.8 24.3 %collective-permute-start.21 = (bf16[128,3584]{1,0:T(8,128)(2,1)}, bf16[128,3584]{1,0:T(8,128)(2,1)S(1)}, u32[]{:S(2)}, u32[]{:S(2)}) collective-permute-start(bf16[128,3584]{1,0:T(8,128)(2,1)} %collective-permute-done.9.refs_3_.refs_5_.refs_9_), channel_id=1, source_target_pairs={{0,3},{1,0},{2,1},{3,2},{4,7},{5,4},{6,5},{7,6},{8,11},{9,8},{10,9... | collective-permute-start | bytes 2752520 | tf_op jit(solution)/shard_map/ppermute | solution.py:340
  146.5 13.6 %collective-permute-start.26 = (bf16[4,64,256]{2,1,0:T(8,128)(2,1)S(1)}, bf16[4,64,256]{2,1,0:T(8,128)(2,1)S(1)}, u32[]{:S(2)}, u32[]{:S(2)}) collective-permute-start(bf16[4,64,256]{2,1,0:T(8,128)(2,1)S(1)} %get-tuple-element.192), channel_id=1, source_target_pairs={{0,16},{4,20},{8,24},{12,28},{16,0},{20,4},{24,8},{28,12},{1,17},{... | collective-permute-start | bytes 393224 | tf_op jit(solution)/shard_map/ppermute | solution.py:337
  147.3 13.5 %collective-permute-start.27 = (bf16[4,64,256]{2,1,0:T(8,128)(2,1)S(1)}, bf16[4,64,256]{2,1,0:T(8,128)(2,1)S(1)}, u32[]{:S(2)}, u32[]{:S(2)}) collective-permute-start(bf16[4,64,256]{2,1,0:T(8,128)(2,1)S(1)} %get-tuple-element.194), channel_id=1, source_target_pairs={{0,8},{4,12},{8,0},{12,4},{16,24},{20,28},{24,16},{28,20},{1,9},{5... | collective-permute-start | bytes 393224 | tf_op jit(solution)/shard_map/ppermute | solution.py:337
  149.3 12.1 %collective-permute-start.28 = (bf16[4,64,256]{2,1,0:T(8,128)(2,1)S(1)}, bf16[4,64,256]{2,1,0:T(8,128)(2,1)S(1)}, u32[]{:S(2)}, u32[]{:S(2)}) collective-permute-start(bf16[4,64,256]{2,1,0:T(8,128)(2,1)S(1)} %get-tuple-element.195), channel_id=1, source_target_pairs={{0,8},{4,12},{8,0},{12,4},{16,24},{20,28},{24,16},{28,20},{1,9},{5... | collective-permute-start | bytes 393224 | tf_op jit(solution)/shard_map/ppermute | solution.py:337
  162.1 15.9 %collective-permute-start.29 = (bf16[512,3584]{1,0:T(8,128)(2,1)}, bf16[512,3584]{1,0:T(8,128)(2,1)S(1)}, u32[]{:S(2)}, u32[]{:S(2)}) collective-permute-start(bf16[512,3584]{1,0:T(8,128)(2,1)} %copy-done.59), channel_id=1, source_target_pairs={{0,4},{4,0},{8,12},{12,8},{16,20},{20,16},{24,28},{28,24},{1,5},{5... | collective-permute-start | bytes 11010056 | tf_op jit(solution)/shard_map/ppermute | solution.py:337
  162.1 13.9 %collective-permute-start.30 = (bf16[4,64,256]{2,1,0:T(8,128)(2,1)S(1)}, bf16[4,64,256]{2,1,0:T(8,128)(2,1)S(1)}, u32[]{:S(2)}, u32[]{:S(2)}) collective-permute-start(bf16[4,64,256]{2,1,0:T(8,128)(2,1)S(1)} %get-tuple-element.215), channel_id=1, source_target_pairs={{0,24},{4,28},{8,16},{12,20},{16,8},{20,12},{24,0},{28,4},{1,25},{... | collective-permute-start | bytes 393224 | tf_op jit(solution)/shard_map/ppermute | solution.py:337
  163.6 13.0 %collective-permute-start.31 = (bf16[4,64,256]{2,1,0:T(8,128)(2,1)S(1)}, bf16[4,64,256]{2,1,0:T(8,128)(2,1)S(1)}, u32[]{:S(2)}, u32[]{:S(2)}) collective-permute-start(bf16[4,64,256]{2,1,0:T(8,128)(2,1)S(1)} %get-tuple-element.216), channel_id=1, source_target_pairs={{0,16},{4,20},{8,24},{12,28},{16,0},{20,4},{24,8},{28,12},{1,17},{... | collective-permute-start | bytes 393224 | tf_op jit(solution)/shard_map/ppermute | solution.py:337
  165.0 12.3 %collective-permute-start.32 = (bf16[4,64,256]{2,1,0:T(8,128)(2,1)S(1)}, bf16[4,64,256]{2,1,0:T(8,128)(2,1)S(1)}, u32[]{:S(2)}, u32[]{:S(2)}) collective-permute-start(bf16[4,64,256]{2,1,0:T(8,128)(2,1)S(1)} %get-tuple-element.218), channel_id=1, source_target_pairs={{0,16},{4,20},{8,24},{12,28},{16,0},{20,4},{24,8},{28,12},{1,17},{... | collective-permute-start | bytes 393224 | tf_op jit(solution)/shard_map/ppermute | solution.py:337
  179.8 32.9 %collective-permute-start.38 = (bf16[512,3584]{1,0:T(8,128)(2,1)}, bf16[512,3584]{1,0:T(8,128)(2,1)}, u32[]{:S(2)}, u32[]{:S(2)}) collective-permute-start(bf16[512,3584]{1,0:T(8,128)(2,1)} %shard_map.81), channel_id=1, source_target_pairs={{0,4},{4,0},{8,12},{12,8},{16,20},{20,16},{24,28},{28,24},{1,5},{5... | collective-permute-start | bytes 11010056 | tf_op jit(solution)/shard_map/ppermute | solution.py:337
  179.8 7.5 %collective-permute-start.33 = (bf16[4,64,256]{2,1,0:T(8,128)(2,1)}, bf16[4,64,256]{2,1,0:T(8,128)(2,1)}, u32[]{:S(2)}, u32[]{:S(2)}) collective-permute-start(bf16[4,64,256]{2,1,0:T(8,128)(2,1)} %copy-done.66), channel_id=1, source_target_pairs={{0,24},{4,28},{8,16},{12,20},{16,8},{20,12},{24,0},{28,4},{1,25},{... | collective-permute-start | bytes 393224 | tf_op jit(solution)/shard_map/ppermute | solution.py:337
  181.2 8.5 %collective-permute-start.34 = (bf16[4,64,256]{2,1,0:T(8,128)(2,1)}, bf16[4,64,256]{2,1,0:T(8,128)(2,1)}, u32[]{:S(2)}, u32[]{:S(2)}) collective-permute-start(bf16[4,64,256]{2,1,0:T(8,128)(2,1)} %copy-done.65), channel_id=1, source_target_pairs={{0,24},{4,28},{8,16},{12,20},{16,8},{20,12},{24,0},{28,4},{1,25},{... | collective-permute-start | bytes 393224 | tf_op jit(solution)/shard_map/ppermute | solution.py:337
  204.3 7.6 %collective-permute-start.37 = (f32[4,128]{1,0:T(4,128)S(1)}, f32[4,128]{1,0:T(4,128)S(1)}, u32[]{:S(2)}, u32[]{:S(2)}) collective-permute-start(f32[4,128]{1,0:T(4,128)S(1)} %get-tuple-element.264), channel_id=1, source_target_pairs={{0,1},{1,2},{2,3},{3,0},{4,5},{5,6},{6,7},{7,4},{8,9},{9,10},{10,1... | collective-permute-start | bytes 6152 | tf_op jit(solution)/shard_map/ppermute | solution.py:340
  206.3 5.6 %collective-permute-start.36 = (f32[4,128]{1,0:T(4,128)S(1)}, f32[4,128]{1,0:T(4,128)S(1)}, u32[]{:S(2)}, u32[]{:S(2)}) collective-permute-start(f32[4,128]{1,0:T(4,128)S(1)} %get-tuple-element.265), channel_id=1, source_target_pairs={{0,2},{1,3},{2,0},{3,1},{4,6},{5,7},{6,4},{7,5},{8,10},{9,11},{10,... | collective-permute-start | bytes 6152 | tf_op jit(solution)/shard_map/ppermute | solution.py:340
  206.3 5.6 %collective-permute-start.35 = (f32[4,128]{1,0:T(4,128)S(1)}, f32[4,128]{1,0:T(4,128)S(1)}, u32[]{:S(2)}, u32[]{:S(2)}) collective-permute-start(f32[4,128]{1,0:T(4,128)S(1)} %get-tuple-element.266), channel_id=1, source_target_pairs={{0,3},{1,0},{2,1},{3,2},{4,7},{5,4},{6,5},{7,6},{8,11},{9,8},{10,9... | collective-permute-start | bytes 6152 | tf_op jit(solution)/shard_map/ppermute | solution.py:340
  (63 other events, 361.5 us)

commit v12 on v11

--- a/solution.py
+++ b/solution.py
@@ -260,7 +260,7 @@
         out_specs=out_spec,
         out_shape=out_shape,
         scratch_shapes=scratch,
-        compiler_params=pltpu.CompilerParams(vmem_limit_bytes=VMEM_BYTES),
+        compiler_params=pltpu.CompilerParams(vmem_limit_bytes=2 * VMEM_BYTES if last else VMEM_BYTES),
         cost_estimate=pl.CostEstimate(
             flops=2 * height * count * width,
             bytes_accessed=2 * count * (width + height) + 4 * height * width,
@@ -315,7 +315,7 @@
             jax.ShapeDtypeStruct((slabs, experts, slots, 4 * pair), BF16),
             jax.ShapeDtypeStruct((slabs * experts, pair // 2), F32),
         ],
-        compiler_params=pltpu.CompilerParams(vmem_limit_bytes=48 * 2**20),
+        compiler_params=pltpu.CompilerParams(vmem_limit_bytes=61 * 2**20),
         cost_estimate=pl.CostEstimate(
             flops=0, bytes_accessed=4 * len(pieces) * experts * slots * pair, transcendentals=0
         ),

time: 232 us -> 215 us (0.927)
  local copies, waits for them, and re-layouts: 51.9 us -> 31.6 us
  Pallas kernels: 62.6 us -> 66.1 us
    unnamed x151 -> x109, local copies, waits for them, and re-layouts: 38.3 us -> 15 us
  transfers between devices with their start and end apart: 39 -> 39, of which waited for: 14 -> 15; matrix products, arithmetic and copies ran while one was open for 12% -> 15% of each run, Pallas kernels for 21% -> 24%
where the time goes in v12:
time: 215 us; the launch traced here: 214 us
  Pallas kernels  66.1 us (31%)
  starting transfers between devices  52.5 us (24%)
  waiting for transfers between devices  50.2 us (23%)
  local copies, waits for them, and re-layouts  31.6 us (15%)
  other arithmetic  12.2 us (6%)
    pallas_call x4, Pallas kernels, project(): pl.pallas_call(functools.partial(project_kernel, top_k, sizes, len(items)...  32.5 us
    pallas_call x3, Pallas kernels, half_grad(): pl.pallas_call(functools.partial(half_grad_kernel, len(scatters), len(arr...  29 us
    ppermute x27, starting transfers between devices, across(): return lax.ppermute(array, 'rep', [(i, i ^ bits) for i in range(reps)])  28.8 us
    ppermute x27, waiting for transfers between devices, across(): return lax.ppermute(array, 'rep', [(i, i ^ bits) for i in range(reps)])  26.4 us
    ppermute x12, waiting for transfers between devices, around(): lax.ppermute(array, 'exp', [(i, (i + shift) % sources) for i in range(sou...  23.8 us
    ppermute x12, starting transfers between devices, around(): lax.ppermute(array, 'exp', [(i, (i + shift) % sources) for i in range(sou...  23.7 us
    unnamed x109, local copies, waits for them, and re-layouts  15 us
    reshape x2, local copies, waits for them, and re-layouts, on_device_tokens(): saved_hidden.reshape(experts, sources, most, 8, block)  7.92 us
  transfers between devices with their start and end apart: 39, of which 15 were waited for; matrix products, arithmetic and copies ran while one was open for 15% of the time, Pallas kernels for 24%

profile of v12, /device:TPU:0, one launch (start us, length us, event | category | flops | bytes accessed | tf_op | source)
XLA Modules:
  0.0 213.9 jit_solution(14157156435368045541)
XLA Ops:
  0.6 3.1 %collective-permute-start.5 = (bf16[128,3584]{1,0:T(8,128)(2,1)}, bf16[128,3584]{1,0:T(8,128)(2,1)S(1)}, u32[]{:S(2)}, u32[]{:S(2)}) collective-permute-start(bf16[128,3584]{1,0:T(8,128)(2,1)} %refs_6_.1), channel_id=1, source_target_pairs={{0,1},{1,2},{2,3},{3,0},{4,5},{5,6},{6,7},{7,4},{8,9},{9,10},{10,1... | collective-permute-start | bytes 2752520 | tf_op jit(solution)/shard_map/ppermute | solution.py:340
  3.7 1.5 collective-permute-start.4
  5.2 1.5 collective-permute-start.3
  8.8 2.7 %collective-permute-start.1 = (bf16[4,256]{1,0:T(4,128)(2,1)S(1)}, bf16[4,256]{1,0:T(4,128)(2,1)S(1)}, u32[]{:S(2)}, u32[]{:S(2)}) collective-permute-start(bf16[4,256]{1,0:T(4,128)(2,1)S(1)} %pad_maximum_fusion.5), channel_id=1, source_target_pairs={{0,2},{1,3},{2,0},{3,1},{4,6},{5,7},{6,4},{7,5},{8,10},{9,11},{10,... | collective-permute-start | bytes 6152 | tf_op jit(solution)/shard_map/ppermute | solution.py:340
  11.7 4.3 %reshape.47 = bf16[4,4,60,8,128]{4,3,1,2,0:T(8,128)(2,1)} reshape(bf16[1,4,4,60,1024]{4,2,3,1,0:T(4,128)(2,1)} %param.8) | data formatting | bytes 3932160 | tf_op jit(solution)/shard_map/reshape | solution.py:359
  16.0 3.6 %copy.15 = bf16[4,4,60,8,128]{4,2,1,0,3:T(8,128)(2,1)} copy(bf16[4,4,60,8,128]{4,3,1,2,0:T(8,128)(2,1)} %reshape.47) | data formatting | bytes 3932160 | tf_op jit(solution)/shard_map/reshape | solution.py:359
  19.6 2.8 %dynamic-slice_bitcast_fusion = (bf16[4,4,60,128]{3,2,1,0:T(8,128)(2,1)S(1)}, bf16[4,4,60,128]{3,2,1,0:T(8,128)(2,1)S(1)}, bf16[4,4,60,128]{3,2,1,0:T(8,128)(2,1...) fusion(bf16[8,4,4,60,128]{4,3,2,1,0:T(8,128)(2,1)} %bitcast.65,, ...), kind=kLoop, calls=%fused_computation.7 | loop fusion | bytes 3932192 | tf_op jit(solution)/shard_map/jit(dynamic_index_in_dim)/squeeze | solution.py:361
  22.4 2.4 %copy.12 = bf16[4,128,3584]{2,1,0:T(8,128)(2,1)} copy(bf16[4,128,3584]{2,0,1:T(4,128)(2,1)S(1)} %bitcast.66) | data formatting | bytes 7340032 | tf_op jit(solution)/shard_map/transpose | solution.py:362
  24.8 3.6 %collective-permute-start.2 = (bf16[4,256]{1,0:T(4,128)(2,1)S(1)}, bf16[4,256]{1,0:T(4,128)(2,1)S(1)}, u32[]{:S(2)}, u32[]{:S(2)}) collective-permute-start(bf16[4,256]{1,0:T(4,128)(2,1)S(1)} %pad_maximum_fusion.5), channel_id=1, source_target_pairs={{0,3},{1,0},{2,1},{3,2},{4,7},{5,4},{6,5},{7,6},{8,11},{9,8},{10,9... | collective-permute-start | bytes 6152 | tf_op jit(solution)/shard_map/ppermute | solution.py:340
  28.4 1.3 collective-permute-done.2
  30.7 1.5 collective-permute-start.6
  32.2 1.5 collective-permute-start.9
  33.9 2.5 %pad_maximum_fusion.1 = (bf16[4,4,64,256]{3,2,1,0:T(8,128)(2,1)S(1)}, bf16[4,4,64,256]{3,2,1,0:T(8,128)(2,1)S(1)}, bf16[4,4,64,256]{3,2,1,0:T(8,128)(2,1)S(1)}, bf16[4,4,64,256]{3,2,1,0:T(8,128)(2,1)}) fusion(bf16[4,4,4,256]{3,2,1,0:T(4,128)(2,1)S(1)} %broadcast_in_dim.49, bf16[4,4,60,128]{3,2,1,0:T(8,128)(2,1)S(1)} %get-tuple-element.144, ...), kind=kLoop, calls=%fused_computation.3 | loop fusion | flops 5505024 | bytes 4096000 | tf_op jit(solution)/shard_map/concatenate | solution.py:377
  36.8 18.2 %collective-permute-done.11.refs_3_.refs_9_.refs_13_ = bf16[128,3584]{1,0:T(8,128)(2,1)} collective-permute-done((bf16[128,3584]{1,0:T(8,128)(2,1)S(1)}, bf16[128,3584]{1,0:T(8,128)(2,1)}, u32[]{:S(2)}, u32[]{:S(2)}) %collective-permute-start.11) | collective-permute-done | bytes 917536 | tf_op jit(solution)/shard_map/ppermute | solution.py:340
  55.1 1.7 collective-permute-start.12
  56.8 8.6 %collective-permute-done.7.refs_9_.refs_6_.refs_4_.refs_5_ = bf16[4,4,64,256]{3,2,1,0:T(8,128)(2,1)S(1)} collective-permute-done((bf16[4,4,64,256]{3,2,1,0:T(8,128)(2,1)S(1)}, bf16[4,4,64,256]{3,2,1,0:T(8,128)(2,1)S(1)}, u32[]{:S(2)}, u32[]{:S(2)}) %collective-permute-start.7) | collective-permute-done | bytes 524320 | tf_op jit(solution)/shard_map/ppermute | solution.py:337
  65.9 1.5 collective-permute-start.10
  68.0 6.9 %pad_maximum_fusion.refs_4_.refs_5_.refs_6_.refs_7_.refs_2_.refs_3_ = bf16[2,512,3584]{2,1,0:T(8,128)(2,1)} fusion(bf16[1,512,3584]{2,1,0:T(8,128)(2,1)} %bitcast.31, bf16[1,512,3584]{2,1,0:T(8,128)(2,1)} %bitcast.30), kind=kLoop, calls=%fused_computation | loop fusion | flops 3670016 | bytes 14680064 | tf_op jit(solution)/shard_map/stack | solution.py:385
  74.8 3.7 %collective-permute-done.10.refs_8_.refs_10_.refs_7_.refs_9_ = bf16[4,4,64,256]{3,2,1,0:T(8,128)(2,1)S(1)} collective-permute-done((bf16[4,4,64,256]{3,2,1,0:T(8,128)(2,1)S(1)}, bf16[4,4,64,256]{3,2,1,0:T(8,128)(2,1)S(1)}, u32[]{:S(2)}, u32[]{:S(2)}) %collective-permute-start.10) | collective-permute-done | bytes 524320 | tf_op jit(solution)/shard_map/ppermute | solution.py:337
  83.5 3.4 %collective-permute-start.16 = (bf16[128,3584]{1,0:T(8,128)(2,1)}, bf16[128,3584]{1,0:T(8,128)(2,1)}, u32[]{:S(2)}, u32[]{:S(2)}) collective-permute-start(bf16[128,3584]{1,0:T(8,128)(2,1)} %collective-permute-done.3.refs_1_.refs_3_.refs_7_), channel_id=1, source_target_pairs={{0,3},{1,0},{2,1},{3,2},{4,7},{5,4},{6,5},{7,6},{8,11},{9,8},{10,9... | collective-permute-start | bytes 2752520 | tf_op jit(solution)/shard_map/ppermute | solution.py:340
  87.0 3.1 %copy-done = bf16[2,512,3584]{2,1,0:T(8,128)(2,1)S(1)} copy-done((bf16[2,512,3584]{2,1,0:T(8,128)(2,1)S(1)}, bf16[2,512,3584]{2,1,0:T(8,128)(2,1)}, u32[]{:S(2)}) %copy-start) | copy-done | bytes 7340056
  93.3 8.4 %shard_map.76 = (bf16[4,64,256]{2,1,0:T(8,128)(2,1)S(1)}, bf16[4,64,256]{2,1,0:T(8,128)(2,1)S(1)}, bf16[4,64,256]{2,1,0:T(8,128)(2,1)S(1)}, bf16[4,64,256]{2,1,0:T(8,128)(2,1)S(1)}, bf16[2,512,512]{2,1,0:T(8,128)(2,1)S(1)}) custom-call(s32[5]{0:T(128)S(1)} %stack.98.idx_ref, bf16[128,3584]{1,0:T(8,128)(2,1)S(1)} %copy-done.15, ...), custom_call_target="tpu_custom_call" | custom-call | flops 7516192768 | bytes 11010048 | tf_op jit(solution)/shard_map/pallas_call | solution.py:178
  103.1 1.8 collective-permute-done.16.refs_5_.refs_11_.refs_15_
  104.8 4.3 %collective-permute-start.19 = (bf16[128,3584]{1,0:T(8,128)(2,1)S(1)}, bf16[128,3584]{1,0:T(8,128)(2,1)S(1)}, u32[]{:S(2)}, u32[]{:S(2)}) collective-permute-start(bf16[128,3584]{1,0:T(8,128)(2,1)S(1)} %collective-permute-done.4.refs_2_.refs_4_.refs_8_), channel_id=1, source_target_pairs={{0,3},{1,0},{2,1},{3,2},{4,7},{5,4},{6,5},{7,6},{8,11},{9,8},{10,9... | collective-permute-start | bytes 2752520 | tf_op jit(solution)/shard_map/ppermute | solution.py:340
  109.1 1.3 collective-permute-start.17
  111.1 12.1 %shard_map.77 = (bf16[4,64,256]{2,1,0:T(8,128)(2,1)S(1)}, bf16[4,64,256]{2,1,0:T(8,128)(2,1)S(1)}, bf16[4,64,256]{2,1,0:T(8,128)(2,1)S(1)}, bf16[4,64,256]{2,1,0...) custom-call(s32[5]{0:T(128)S(1)} %stack.98.idx_ref, ...), custom_call_target="tpu_custom_call" | custom-call | flops 11274289152 | bytes 12845056 | tf_op jit(solution)/shard_map/pallas_call | solution.py:178
  123.2 2.5 %collective-permute-done.19.refs_3_.refs_5_.refs_19_ = bf16[128,3584]{1,0:T(8,128)(2,1)S(1)} collective-permute-done((bf16[128,3584]{1,0:T(8,128)(2,1)S(1)}, bf16[128,3584]{1,0:T(8,128)(2,1)S(1)}, u32[]{:S(2)}, u32[]{:S(2)}) %collective-permute-start.19) | collective-permute-done | bytes 917536 | tf_op jit(solution)/shard_map/ppermute | solution.py:340
  125.8 3.3 %collective-permute-done.17.refs_0_.refs_2_.refs_16_ = bf16[128,3584]{1,0:T(8,128)(2,1)S(1)} collective-permute-done((bf16[128,3584]{1,0:T(8,128)(2,1)}, bf16[128,3584]{1,0:T(8,128)(2,1)S(1)}, u32[]{:S(2)}, u32[]{:S(2)}) %collective-permute-start.17) | collective-permute-done | bytes 917536 | tf_op jit(solution)/shard_map/ppermute | solution.py:337
  130.4 1.4 collective-permute-start.22
  131.8 2.5 %collective-permute-start.23 = (bf16[4,64,256]{2,1,0:T(8,128)(2,1)S(1)}, bf16[4,64,256]{2,1,0:T(8,128)(2,1)S(1)}, u32[]{:S(2)}, u32[]{:S(2)}) collective-permute-start(bf16[4,64,256]{2,1,0:T(8,128)(2,1)S(1)} %get-tuple-element.188), channel_id=1, source_target_pairs={{0,16},{4,20},{8,24},{12,28},{16,0},{20,4},{24,8},{28,12},{1,17},{... | collective-permute-start | bytes 393224 | tf_op jit(solution)/shard_map/ppermute | solution.py:337
  134.4 1.5 collective-permute-start.25
  135.8 2.0 collective-permute-start.20
  137.9 7.4 %shard_map.78 = (bf16[4,64,256]{2,1,0:T(8,128)(2,1)S(1)}, bf16[4,64,256]{2,1,0:T(8,128)(2,1)S(1)}, bf16[4,64,256]{2,1,0:T(8,128)(2,1)S(1)}, bf16[4,64,256]{2,1,0:T(8,128)(2,1)S(1)}, bf16[2,512,512]{2,1,0:T(8,128)(2,1)S(1)}) custom-call(s32[5]{0:T(128)S(1)} %stack.98.idx_ref, bf16[128,3584]{1,0:T(8,128)(2,1)S(1)} %collective-permute-done.17.refs_0_.refs_2_.refs_16_, ...), custom_call_target="tpu_custom_call" | custom-call | flops 7516192768 | bytes 11010048 | tf_op jit(solution)/shard_map/pallas_call | solution.py:178
  146.1 1.4 collective-permute-start.27
  148.1 8.3 %shard_map.79 = bf16[512,3584]{1,0:T(8,128)(2,1)S(1)} custom-call(bf16[2,512,512]{2,1,0:T(8,128)(2,1)S(1)} %get-tuple-element.205.refs_0_, bf16[2,512,768]{2,1,0:T(8,128)(2,1)S(1)} %get-tuple-element.206.refs_1_, bf16[128,3584]{1,0:T(8,128)(2,1)S(1)} %copy-done.16, bf16[128,3584]{1,0:T(8,128)(2,1)} %collective-permute-done.3.refs_1_.refs_3_.refs_7_, ...), custom_call_target="tpu_custom_call" | custom-call | flops 4697620480 | bytes 17825792 | tf_op jit(solution)/shard_map/pallas_call | solution.py:256
  157.5 1.8 collective-permute-start.30
  159.7 1.7 collective-permute-start.32
  161.3 4.7 %shard_map.80 = (bf16[4,64,256]{2,1,0:T(8,128)(2,1)S(1)}, bf16[4,64,256]{2,1,0:T(8,128)(2,1)S(1)}, bf16[2,512,256]{2,1,0:T(8,128)(2,1)S(1)}) custom-call(s32[5]{0:T(128)S(1)} %stack.98.idx_ref, bf16[128,3584]{1,0:T(8,128)(2,1)S(1)} %collective-permute-done.20.refs_0_.refs_6_.refs_20_, bf16[128,3584]{1,0:T(8,128)(2,1)S(1)} %collective-permute-done.21.refs_1_.refs_7_.refs_21_, ...), custom_call_target="tpu_custom_call" | custom-call | flops 3758096384 | bytes 9175040 | tf_op jit(solution)/shard_map/pallas_call | solution.py:178
  166.1 5.5 %shard_map.81 = bf16[512,3584]{1,0:T(8,128)(2,1)} custom-call(bf16[2,512,512]{2,1,0:T(8,128)(2,1)S(1)} %get-tuple-element.219.refs_0_.refs_2_, bf16[2,512,256]{2,1,0:T(8,128)(2,1)S(1)} %get-tuple-element.236.refs_1_.refs_3_, bf16[128,3584]{1,0:T(8,128)(2,1)S(1)} %collective-permute-done.17.refs_0_.refs_2_.refs_16_, ...), custom_call_target="tpu_custom_call" | custom-call | flops 2818572288 | bytes 13631488 | tf_op jit(solution)/shard_map/pallas_call | solution.py:256
  171.7 1.9 copy-done.34
  174.7 1.7 collective-permute-start.34
  177.1 3.6 %collective-permute-done.33.refs_11_ = bf16[4,64,256]{2,1,0:T(8,128)(2,1)S(1)} collective-permute-done((bf16[4,64,256]{2,1,0:T(8,128)(2,1)S(1)}, bf16[4,64,256]{2,1,0:T(8,128)(2,1)S(1)}, u32[]{:S(2)}, u32[]{:S(2)}) %collective-permute-start.33) | collective-permute-done | bytes 131104 | tf_op jit(solution)/shard_map/ppermute | solution.py:337
  180.7 2.4 %collective-permute-done.34.refs_15_ = bf16[4,64,256]{2,1,0:T(8,128)(2,1)S(1)} collective-permute-done((bf16[4,64,256]{2,1,0:T(8,128)(2,1)S(1)}, bf16[4,64,256]{2,1,0:T(8,128)(2,1)S(1)}, u32[]{:S(2)}, u32[]{:S(2)}) %collective-permute-start.34) | collective-permute-done | bytes 131104 | tf_op jit(solution)/shard_map/ppermute | solution.py:337
  183.8 4.5 %shard_map.82 = (bf16[4,4,64,1024]{3,2,1,0:T(8,128)(2,1)}, f32[16,128]{1,0:T(8,128)}) custom-call(s32[12]{0:T(128)} %stack.88.idx_ref, bf16[4,64,256]{2,1,0:T(8,128)(2,1)} %copy-done.25, bf16[4,64,256]{2,1,0:T(8,128)(2,1)} %copy-done.35, bf16[4,64,256]{2,1,0:T(8,128)(2,1)} %copy-done.36, bf16[4,64,256]{2,1,0:T(8,128)(2,1)} %copy-done.37, ...), custom_call_target="tpu_custom_call" | custom-call | bytes 4194304 | tf_op jit(solution)/shard_map/pallas_call | solution.py:300
  190.6 2.4 %collective-permute-start.35 = (f32[4,128]{1,0:T(4,128)S(1)}, f32[4,128]{1,0:T(4,128)S(1)}, u32[]{:S(2)}, u32[]{:S(2)}) collective-permute-start(f32[4,128]{1,0:T(4,128)S(1)} %get-tuple-element.266), channel_id=1, source_target_pairs={{0,3},{1,0},{2,1},{3,2},{4,7},{5,4},{6,5},{7,6},{8,11},{9,8},{10,9... | collective-permute-start | bytes 6152 | tf_op jit(solution)/shard_map/ppermute | solution.py:340
  193.0 1.9 slice_bitcast_fusion
  194.9 2.8 %copy.13 = bf16[1,4,4,60,1024]{4,2,3,1,0:T(4,128)(2,1)} copy(bf16[1,4,4,60,1024]{4,3,1,2,0:T(8,128)(2,1)S(1)} %slice_bitcast_fusion) | data formatting | bytes 3932160
  198.4 15.3 %shard_map.83 = f32[128,4,3584]{2,1,0:T(4,128)} custom-call(bf16[2,512,512]{2,1,0:T(8,128)(2,1)} %copy-done.14, bf16[2,512,768]{2,1,0:T(8,128)(2,1)} %copy-done.13, bf16[2,512,512]{2,1,0:T(8,128)(2,1)} %copy-done.4, bf16[2,512,256]{2,1,0:T(8,128)(2,1)} %copy-done.10, bf16[512,3584]{1,0:T(8,128)(2,1)} %copy-done.34, ...), custom_call_target="tpu_custom_call" | custom-call | flops 7516192768 | bytes 24117248 | tf_op jit(solution)/shard_map/pallas_call | solution.py:256
  (169 shorter events, 24.7 us)
Async XLA Ops:
  0.6 29.1 %collective-permute-start.5 = (bf16[128,3584]{1,0:T(8,128)(2,1)}, bf16[128,3584]{1,0:T(8,128)(2,1)S(1)}, u32[]{:S(2)}, u32[]{:S(2)}) collective-permute-start(bf16[128,3584]{1,0:T(8,128)(2,1)} %refs_6_.1), channel_id=1, source_target_pairs={{0,1},{1,2},{2,3},{3,0},{4,5},{5,6},{6,7},{7,4},{8,9},{9,10},{10,1... | collective-permute-start | bytes 2752520 | tf_op jit(solution)/shard_map/ppermute | solution.py:340
  3.7 26.1 %collective-permute-start.4 = (bf16[128,3584]{1,0:T(8,128)(2,1)}, bf16[128,3584]{1,0:T(8,128)(2,1)S(1)}, u32[]{:S(2)}, u32[]{:S(2)}) collective-permute-start(bf16[128,3584]{1,0:T(8,128)(2,1)} %refs_6_.1), channel_id=1, source_target_pairs={{0,16},{4,20},{8,24},{12,28},{16,0},{20,4},{24,8},{28,12},{1,17},{... | collective-permute-start | bytes 2752520 | tf_op jit(solution)/shard_map/ppermute | solution.py:337
  5.2 24.5 %collective-permute-start.3 = (bf16[128,3584]{1,0:T(8,128)(2,1)}, bf16[128,3584]{1,0:T(8,128)(2,1)}, u32[]{:S(2)}, u32[]{:S(2)}) collective-permute-start(bf16[128,3584]{1,0:T(8,128)(2,1)} %refs_6_.1), channel_id=1, source_target_pairs={{0,8},{4,12},{8,0},{12,4},{16,24},{20,28},{24,16},{28,20},{1,9},{5... | collective-permute-start | bytes 2752520 | tf_op jit(solution)/shard_map/ppermute | solution.py:337
  8.8 16.0 %collective-permute-start.1 = (bf16[4,256]{1,0:T(4,128)(2,1)S(1)}, bf16[4,256]{1,0:T(4,128)(2,1)S(1)}, u32[]{:S(2)}, u32[]{:S(2)}) collective-permute-start(bf16[4,256]{1,0:T(4,128)(2,1)S(1)} %pad_maximum_fusion.5), channel_id=1, source_target_pairs={{0,2},{1,3},{2,0},{3,1},{4,6},{5,7},{6,4},{7,5},{8,10},{9,11},{10,... | collective-permute-start | bytes 6152 | tf_op jit(solution)/shard_map/ppermute | solution.py:340
  11.5 17.0 %collective-permute-start = (bf16[4,256]{1,0:T(4,128)(2,1)S(1)}, bf16[4,256]{1,0:T(4,128)(2,1)S(1)}, u32[]{:S(2)}, u32[]{:S(2)}) collective-permute-start(bf16[4,256]{1,0:T(4,128)(2,1)S(1)} %pad_maximum_fusion.5), channel_id=1, source_target_pairs={{0,1},{1,2},{2,3},{3,0},{4,5},{5,6},{6,7},{7,4},{8,9},{9,10},{10,1... | collective-permute-start | bytes 6152 | tf_op jit(solution)/shard_map/ppermute | solution.py:340
  24.8 30.2 %copy-start.15 = (bf16[128,3584]{1,0:T(8,128)(2,1)S(1)}, bf16[128,3584]{1,0:T(8,128)(2,1)}, u32[]{:S(2)}) copy-start(bf16[128,3584]{1,0:T(8,128)(2,1)} %refs_6_.1) | copy-start | bytes 2752516
  24.8 4.9 %collective-permute-start.2 = (bf16[4,256]{1,0:T(4,128)(2,1)S(1)}, bf16[4,256]{1,0:T(4,128)(2,1)S(1)}, u32[]{:S(2)}, u32[]{:S(2)}) collective-permute-start(bf16[4,256]{1,0:T(4,128)(2,1)S(1)} %pad_maximum_fusion.5), channel_id=1, source_target_pairs={{0,3},{1,0},{2,1},{3,2},{4,7},{5,4},{6,5},{7,6},{8,11},{9,8},{10,9... | collective-permute-start | bytes 6152 | tf_op jit(solution)/shard_map/ppermute | solution.py:340
  29.8 81.3 %copy-start.17 = (bf16[128,3584]{1,0:T(8,128)(2,1)}, bf16[128,3584]{1,0:T(8,128)(2,1)S(1)}, u32[]{:S(2)}) copy-start(bf16[128,3584]{1,0:T(8,128)(2,1)S(1)} %collective-permute-done.5.refs_0_.refs_6_.refs_10_) | copy-start | bytes 2752516
  29.8 75.1 %copy-start.19 = (bf16[128,3584]{1,0:T(8,128)(2,1)}, bf16[128,3584]{1,0:T(8,128)(2,1)S(1)}, u32[]{:S(2)}) copy-start(bf16[128,3584]{1,0:T(8,128)(2,1)S(1)} %collective-permute-done.4.refs_2_.refs_4_.refs_8_) | copy-start | bytes 2752516
  29.8 38.2 %collective-permute-start.13 = (bf16[512,3584]{1,0:T(8,128)(2,1)}, bf16[512,3584]{1,0:T(8,128)(2,1)}, u32[]{:S(2)}, u32[]{:S(2)}) collective-permute-start(bf16[512,3584]{1,0:T(8,128)(2,1)} %bitcast.25), channel_id=1, source_target_pairs={{0,4},{4,0},{8,12},{12,8},{16,20},{20,16},{24,28},{28,24},{1,5},{5... | collective-permute-start | bytes 11010056 | tf_op jit(solution)/shard_map/ppermute | solution.py:337
  29.9 25.2 %collective-permute-start.11 = (bf16[128,3584]{1,0:T(8,128)(2,1)S(1)}, bf16[128,3584]{1,0:T(8,128)(2,1)}, u32[]{:S(2)}, u32[]{:S(2)}) collective-permute-start(bf16[128,3584]{1,0:T(8,128)(2,1)S(1)} %collective-permute-done.5.refs_0_.refs_6_.refs_10_), channel_id=1, source_target_pairs={{0,1},{1,2},{2,3},{3,0},{4,5},{5,6},{6,7},{7,4},{8,9},{9,10},{10,1... | collective-permute-start | bytes 2752520 | tf_op jit(solution)/shard_map/ppermute | solution.py:340
  30.7 36.7 %collective-permute-start.6 = (bf16[128,3584]{1,0:T(8,128)(2,1)S(1)}, bf16[128,3584]{1,0:T(8,128)(2,1)S(1)}, u32[]{:S(2)}, u32[]{:S(2)}) collective-permute-start(bf16[128,3584]{1,0:T(8,128)(2,1)S(1)} %collective-permute-done.5.refs_0_.refs_6_.refs_10_), channel_id=1, source_target_pairs={{0,8},{4,12},{8,0},{12,4},{16,24},{20,28},{24,16},{28,20},{1,9},{5... | collective-permute-start | bytes 2752520 | tf_op jit(solution)/shard_map/ppermute | solution.py:337
  32.2 33.7 %collective-permute-start.9 = (bf16[128,3584]{1,0:T(8,128)(2,1)}, bf16[128,3584]{1,0:T(8,128)(2,1)}, u32[]{:S(2)}, u32[]{:S(2)}) collective-permute-start(bf16[128,3584]{1,0:T(8,128)(2,1)} %collective-permute-done.3.refs_1_.refs_3_.refs_7_), channel_id=1, source_target_pairs={{0,16},{4,20},{8,24},{12,28},{16,0},{20,4},{24,8},{28,12},{1,17},{... | collective-permute-start | bytes 2752520 | tf_op jit(solution)/shard_map/ppermute | solution.py:337
  36.3 29.1 %collective-permute-start.7 = (bf16[4,4,64,256]{3,2,1,0:T(8,128)(2,1)S(1)}, bf16[4,4,64,256]{3,2,1,0:T(8,128)(2,1)S(1)}, u32[]{:S(2)}, u32[]{:S(2)}) collective-permute-start(bf16[4,4,64,256]{3,2,1,0:T(8,128)(2,1)S(1)} %get-tuple-element.261), channel_id=1, source_target_pairs={{0,24},{4,28},{8,16},{12,20},{16,8},{20,12},{24,0},{28,4},{1,25},{... | collective-permute-start | bytes 1572872 | tf_op jit(solution)/shard_map/ppermute | solution.py:337
  55.1 25.7 %collective-permute-start.12 = (bf16[128,3584]{1,0:T(8,128)(2,1)S(1)}, bf16[128,3584]{1,0:T(8,128)(2,1)S(1)}, u32[]{:S(2)}, u32[]{:S(2)}) collective-permute-start(bf16[128,3584]{1,0:T(8,128)(2,1)S(1)} %copy-done.15), channel_id=1, source_target_pairs={{0,3},{1,0},{2,1},{3,2},{4,7},{5,4},{6,5},{7,6},{8,11},{9,8},{10,9... | collective-permute-start | bytes 2752520 | tf_op jit(solution)/shard_map/ppermute | solution.py:340
  65.9 12.6 %collective-permute-start.10 = (bf16[4,4,64,256]{3,2,1,0:T(8,128)(2,1)S(1)}, bf16[4,4,64,256]{3,2,1,0:T(8,128)(2,1)S(1)}, u32[]{:S(2)}, u32[]{:S(2)}) collective-permute-start(bf16[4,4,64,256]{3,2,1,0:T(8,128)(2,1)S(1)} %get-tuple-element.146), channel_id=1, source_target_pairs={{0,16},{4,20},{8,24},{12,28},{16,0},{20,4},{24,8},{28,12},{1,17},{... | collective-permute-start | bytes 1572872 | tf_op jit(solution)/shard_map/ppermute | solution.py:337
  67.4 12.6 %collective-permute-start.8 = (bf16[4,4,64,256]{3,2,1,0:T(8,128)(2,1)S(1)}, bf16[4,4,64,256]{3,2,1,0:T(8,128)(2,1)S(1)}, u32[]{:S(2)}, u32[]{:S(2)}) collective-permute-start(bf16[4,4,64,256]{3,2,1,0:T(8,128)(2,1)S(1)} %get-tuple-element.142), channel_id=1, source_target_pairs={{0,8},{4,12},{8,0},{12,4},{16,24},{20,28},{24,16},{28,20},{1,9},{5... | collective-permute-start | bytes 1572872 | tf_op jit(solution)/shard_map/ppermute | solution.py:337
  81.8 20.4 %collective-permute-start.15 = (bf16[128,3584]{1,0:T(8,128)(2,1)}, bf16[128,3584]{1,0:T(8,128)(2,1)}, u32[]{:S(2)}, u32[]{:S(2)}) collective-permute-start(bf16[128,3584]{1,0:T(8,128)(2,1)} %collective-permute-done.11.refs_3_.refs_9_.refs_13_), channel_id=1, source_target_pairs={{0,8},{4,12},{8,0},{12,4},{16,24},{20,28},{24,16},{28,20},{1,9},{5... | collective-permute-start | bytes 2752520 | tf_op jit(solution)/shard_map/ppermute | solution.py:337
  82.6 20.5 %collective-permute-start.14 = (bf16[128,3584]{1,0:T(8,128)(2,1)S(1)}, bf16[128,3584]{1,0:T(8,128)(2,1)}, u32[]{:S(2)}, u32[]{:S(2)}) collective-permute-start(bf16[128,3584]{1,0:T(8,128)(2,1)S(1)} %collective-permute-done.5.refs_0_.refs_6_.refs_10_), channel_id=1, source_target_pairs={{0,16},{4,20},{8,24},{12,28},{16,0},{20,4},{24,8},{28,12},{1,17},{... | collective-permute-start | bytes 2752520 | tf_op jit(solution)/shard_map/ppermute | solution.py:337
  83.5 21.3 %collective-permute-start.16 = (bf16[128,3584]{1,0:T(8,128)(2,1)}, bf16[128,3584]{1,0:T(8,128)(2,1)}, u32[]{:S(2)}, u32[]{:S(2)}) collective-permute-start(bf16[128,3584]{1,0:T(8,128)(2,1)} %collective-permute-done.3.refs_1_.refs_3_.refs_7_), channel_id=1, source_target_pairs={{0,3},{1,0},{2,1},{3,2},{4,7},{5,4},{6,5},{7,6},{8,11},{9,8},{10,9... | collective-permute-start | bytes 2752520 | tf_op jit(solution)/shard_map/ppermute | solution.py:340
  101.7 46.4 %copy-start.14 = (bf16[2,512,512]{2,1,0:T(8,128)(2,1)}, bf16[2,512,512]{2,1,0:T(8,128)(2,1)S(1)}, u32[]{:S(2)}) copy-start(bf16[2,512,512]{2,1,0:T(8,128)(2,1)S(1)} %get-tuple-element.205.refs_0_) | copy-start | bytes 3145732
  104.8 33.0 %copy-start.6 = (bf16[128,3584]{1,0:T(8,128)(2,1)S(1)}, bf16[128,3584]{1,0:T(8,128)(2,1)}, u32[]{:S(2)}) copy-start(bf16[128,3584]{1,0:T(8,128)(2,1)} %copy-done.5) | copy-start | bytes 2752516
  104.8 33.0 %copy-start.12 = (bf16[4,4,64,256]{3,2,1,0:T(8,128)(2,1)S(1)}, bf16[4,4,64,256]{3,2,1,0:T(8,128)(2,1)}, u32[]{:S(2)}) copy-start(bf16[4,4,64,256]{3,2,1,0:T(8,128)(2,1)} %copy-done.11) | copy-start | bytes 1572868
  104.8 20.9 %collective-permute-start.19 = (bf16[128,3584]{1,0:T(8,128)(2,1)S(1)}, bf16[128,3584]{1,0:T(8,128)(2,1)S(1)}, u32[]{:S(2)}, u32[]{:S(2)}) collective-permute-start(bf16[128,3584]{1,0:T(8,128)(2,1)S(1)} %collective-permute-done.4.refs_2_.refs_4_.refs_8_), channel_id=1, source_target_pairs={{0,3},{1,0},{2,1},{3,2},{4,7},{5,4},{6,5},{7,6},{8,11},{9,8},{10,9... | collective-permute-start | bytes 2752520 | tf_op jit(solution)/shard_map/ppermute | solution.py:340
  109.1 20.0 %collective-permute-start.17 = (bf16[128,3584]{1,0:T(8,128)(2,1)}, bf16[128,3584]{1,0:T(8,128)(2,1)S(1)}, u32[]{:S(2)}, u32[]{:S(2)}) collective-permute-start(bf16[128,3584]{1,0:T(8,128)(2,1)} %collective-permute-done.14.refs_2_.refs_8_.refs_12_), channel_id=1, source_target_pairs={{0,8},{4,12},{8,0},{12,4},{16,24},{20,28},{24,16},{28,20},{1,9},{5... | collective-permute-start | bytes 2752520 | tf_op jit(solution)/shard_map/ppermute | solution.py:337
  110.4 19.9 %collective-permute-start.18 = (bf16[128,3584]{1,0:T(8,128)(2,1)}, bf16[128,3584]{1,0:T(8,128)(2,1)S(1)}, u32[]{:S(2)}, u32[]{:S(2)}) collective-permute-start(bf16[128,3584]{1,0:T(8,128)(2,1)} %collective-permute-done.11.refs_3_.refs_9_.refs_13_), channel_id=1, source_target_pairs={{0,16},{4,20},{8,24},{12,28},{16,0},{20,4},{24,8},{28,12},{1,17},{... | collective-permute-start | bytes 2752520 | tf_op jit(solution)/shard_map/ppermute | solution.py:337
  125.8 40.3 %copy-start.7 = (bf16[128,3584]{1,0:T(8,128)(2,1)}, bf16[128,3584]{1,0:T(8,128)(2,1)S(1)}, u32[]{:S(2)}) copy-start(bf16[128,3584]{1,0:T(8,128)(2,1)S(1)} %collective-permute-done.19.refs_3_.refs_5_.refs_19_) | copy-start | bytes 2752516
  129.1 37.0 %copy-start.8 = (bf16[128,3584]{1,0:T(8,128)(2,1)}, bf16[128,3584]{1,0:T(8,128)(2,1)S(1)}, u32[]{:S(2)}) copy-start(bf16[128,3584]{1,0:T(8,128)(2,1)S(1)} %collective-permute-done.17.refs_0_.refs_2_.refs_16_) | copy-start | bytes 2752516
  130.4 35.7 %copy-start.9 = (bf16[128,3584]{1,0:T(8,128)(2,1)}, bf16[128,3584]{1,0:T(8,128)(2,1)S(1)}, u32[]{:S(2)}) copy-start(bf16[128,3584]{1,0:T(8,128)(2,1)S(1)} %collective-permute-done.18.refs_1_.refs_3_.refs_17_) | copy-start | bytes 2752516
  130.4 7.5 %collective-permute-start.22 = (bf16[4,64,256]{2,1,0:T(8,128)(2,1)S(1)}, bf16[4,64,256]{2,1,0:T(8,128)(2,1)S(1)}, u32[]{:S(2)}, u32[]{:S(2)}) collective-permute-start(bf16[4,64,256]{2,1,0:T(8,128)(2,1)S(1)} %get-tuple-element.187), channel_id=1, source_target_pairs={{0,8},{4,12},{8,0},{12,4},{16,24},{20,28},{24,16},{28,20},{1,9},{5... | collective-permute-start | bytes 393224 | tf_op jit(solution)/shard_map/ppermute | solution.py:337
  131.8 14.2 %collective-permute-start.23 = (bf16[4,64,256]{2,1,0:T(8,128)(2,1)S(1)}, bf16[4,64,256]{2,1,0:T(8,128)(2,1)S(1)}, u32[]{:S(2)}, u32[]{:S(2)}) collective-permute-start(bf16[4,64,256]{2,1,0:T(8,128)(2,1)S(1)} %get-tuple-element.188), channel_id=1, source_target_pairs={{0,16},{4,20},{8,24},{12,28},{16,0},{20,4},{24,8},{28,12},{1,17},{... | collective-permute-start | bytes 393224 | tf_op jit(solution)/shard_map/ppermute | solution.py:337
  134.3 11.7 %collective-permute-start.24 = (bf16[4,64,256]{2,1,0:T(8,128)(2,1)S(1)}, bf16[4,64,256]{2,1,0:T(8,128)(2,1)S(1)}, u32[]{:S(2)}, u32[]{:S(2)}) collective-permute-start(bf16[4,64,256]{2,1,0:T(8,128)(2,1)S(1)} %get-tuple-element.189), channel_id=1, source_target_pairs={{0,24},{4,28},{8,16},{12,20},{16,8},{20,12},{24,0},{28,4},{1,25},{... | collective-permute-start | bytes 393224 | tf_op jit(solution)/shard_map/ppermute | solution.py:337
  134.4 13.1 %collective-permute-start.25 = (bf16[4,64,256]{2,1,0:T(8,128)(2,1)S(1)}, bf16[4,64,256]{2,1,0:T(8,128)(2,1)S(1)}, u32[]{:S(2)}, u32[]{:S(2)}) collective-permute-start(bf16[4,64,256]{2,1,0:T(8,128)(2,1)S(1)} %get-tuple-element.191), channel_id=1, source_target_pairs={{0,8},{4,12},{8,0},{12,4},{16,24},{20,28},{24,16},{28,20},{1,9},{5... | collective-permute-start | bytes 393224 | tf_op jit(solution)/shard_map/ppermute | solution.py:337
  135.8 21.6 %collective-permute-start.20 = (bf16[128,3584]{1,0:T(8,128)(2,1)}, bf16[128,3584]{1,0:T(8,128)(2,1)S(1)}, u32[]{:S(2)}, u32[]{:S(2)}) collective-permute-start(bf16[128,3584]{1,0:T(8,128)(2,1)} %collective-permute-done.15.refs_4_.refs_10_.refs_14_), channel_id=1, source_target_pairs={{0,16},{4,20},{8,24},{12,28},{16,0},{20,4},{24,8},{28,12},{1,17},{... | collective-permute-start | bytes 2752520 | tf_op jit(solution)/shard_map/ppermute | solution.py:337
  137.8 19.6 %collective-permute-start.21 = (bf16[128,3584]{1,0:T(8,128)(2,1)}, bf16[128,3584]{1,0:T(8,128)(2,1)S(1)}, u32[]{:S(2)}, u32[]{:S(2)}) collective-permute-start(bf16[128,3584]{1,0:T(8,128)(2,1)} %collective-permute-done.9.refs_3_.refs_5_.refs_9_), channel_id=1, source_target_pairs={{0,3},{1,0},{2,1},{3,2},{4,7},{5,4},{6,5},{7,6},{8,11},{9,8},{10,9... | collective-permute-start | bytes 2752520 | tf_op jit(solution)/shard_map/ppermute | solution.py:340
  146.0 11.4 %collective-permute-start.26 = (bf16[4,64,256]{2,1,0:T(8,128)(2,1)S(1)}, bf16[4,64,256]{2,1,0:T(8,128)(2,1)S(1)}, u32[]{:S(2)}, u32[]{:S(2)}) collective-permute-start(bf16[4,64,256]{2,1,0:T(8,128)(2,1)S(1)} %get-tuple-element.192), channel_id=1, source_target_pairs={{0,16},{4,20},{8,24},{12,28},{16,0},{20,4},{24,8},{28,12},{1,17},{... | collective-permute-start | bytes 393224 | tf_op jit(solution)/shard_map/ppermute | solution.py:337
  146.1 11.3 %collective-permute-start.27 = (bf16[4,64,256]{2,1,0:T(8,128)(2,1)S(1)}, bf16[4,64,256]{2,1,0:T(8,128)(2,1)S(1)}, u32[]{:S(2)}, u32[]{:S(2)}) collective-permute-start(bf16[4,64,256]{2,1,0:T(8,128)(2,1)S(1)} %get-tuple-element.194), channel_id=1, source_target_pairs={{0,8},{4,12},{8,0},{12,4},{16,24},{20,28},{24,16},{28,20},{1,9},{5... | collective-permute-start | bytes 393224 | tf_op jit(solution)/shard_map/ppermute | solution.py:337
  147.5 9.9 %collective-permute-start.28 = (bf16[4,64,256]{2,1,0:T(8,128)(2,1)S(1)}, bf16[4,64,256]{2,1,0:T(8,128)(2,1)S(1)}, u32[]{:S(2)}, u32[]{:S(2)}) collective-permute-start(bf16[4,64,256]{2,1,0:T(8,128)(2,1)S(1)} %get-tuple-element.195), channel_id=1, source_target_pairs={{0,8},{4,12},{8,0},{12,4},{16,24},{20,28},{24,16},{28,20},{1,9},{5... | collective-permute-start | bytes 393224 | tf_op jit(solution)/shard_map/ppermute | solution.py:337
  157.4 14.2 %collective-permute-start.29 = (bf16[512,3584]{1,0:T(8,128)(2,1)S(1)}, bf16[512,3584]{1,0:T(8,128)(2,1)S(1)}, u32[]{:S(2)}, u32[]{:S(2)}) collective-permute-start(bf16[512,3584]{1,0:T(8,128)(2,1)S(1)} %shard_map.79), channel_id=1, source_target_pairs={{0,4},{4,0},{8,12},{12,8},{16,20},{20,16},{24,28},{28,24},{1,5},{5... | collective-permute-start | bytes 11010056 | tf_op jit(solution)/shard_map/ppermute | solution.py:337
  157.5 14.1 %collective-permute-start.30 = (bf16[4,64,256]{2,1,0:T(8,128)(2,1)S(1)}, bf16[4,64,256]{2,1,0:T(8,128)(2,1)S(1)}, u32[]{:S(2)}, u32[]{:S(2)}) collective-permute-start(bf16[4,64,256]{2,1,0:T(8,128)(2,1)S(1)} %get-tuple-element.215), channel_id=1, source_target_pairs={{0,24},{4,28},{8,16},{12,20},{16,8},{20,12},{24,0},{28,4},{1,25},{... | collective-permute-start | bytes 393224 | tf_op jit(solution)/shard_map/ppermute | solution.py:337
  159.3 12.3 %collective-permute-start.31 = (bf16[4,64,256]{2,1,0:T(8,128)(2,1)S(1)}, bf16[4,64,256]{2,1,0:T(8,128)(2,1)S(1)}, u32[]{:S(2)}, u32[]{:S(2)}) collective-permute-start(bf16[4,64,256]{2,1,0:T(8,128)(2,1)S(1)} %get-tuple-element.216), channel_id=1, source_target_pairs={{0,16},{4,20},{8,24},{12,28},{16,0},{20,4},{24,8},{28,12},{1,17},{... | collective-permute-start | bytes 393224 | tf_op jit(solution)/shard_map/ppermute | solution.py:337
  159.7 11.9 %collective-permute-start.32 = (bf16[4,64,256]{2,1,0:T(8,128)(2,1)S(1)}, bf16[4,64,256]{2,1,0:T(8,128)(2,1)S(1)}, u32[]{:S(2)}, u32[]{:S(2)}) collective-permute-start(bf16[4,64,256]{2,1,0:T(8,128)(2,1)S(1)} %get-tuple-element.218), channel_id=1, source_target_pairs={{0,16},{4,20},{8,24},{12,28},{16,0},{20,4},{24,8},{28,12},{1,17},{... | collective-permute-start | bytes 393224 | tf_op jit(solution)/shard_map/ppermute | solution.py:337
  173.5 24.9 %collective-permute-start.38 = (bf16[512,3584]{1,0:T(8,128)(2,1)}, bf16[512,3584]{1,0:T(8,128)(2,1)}, u32[]{:S(2)}, u32[]{:S(2)}) collective-permute-start(bf16[512,3584]{1,0:T(8,128)(2,1)} %shard_map.81), channel_id=1, source_target_pairs={{0,4},{4,0},{8,12},{12,8},{16,20},{20,16},{24,28},{28,24},{1,5},{5... | collective-permute-start | bytes 11010056 | tf_op jit(solution)/shard_map/ppermute | solution.py:337
  173.5 7.2 %collective-permute-start.33 = (bf16[4,64,256]{2,1,0:T(8,128)(2,1)S(1)}, bf16[4,64,256]{2,1,0:T(8,128)(2,1)S(1)}, u32[]{:S(2)}, u32[]{:S(2)}) collective-permute-start(bf16[4,64,256]{2,1,0:T(8,128)(2,1)S(1)} %get-tuple-element.229), channel_id=1, source_target_pairs={{0,24},{4,28},{8,16},{12,20},{16,8},{20,12},{24,0},{28,4},{1,25},{... | collective-permute-start | bytes 393224 | tf_op jit(solution)/shard_map/ppermute | solution.py:337
  174.7 8.4 %collective-permute-start.34 = (bf16[4,64,256]{2,1,0:T(8,128)(2,1)S(1)}, bf16[4,64,256]{2,1,0:T(8,128)(2,1)S(1)}, u32[]{:S(2)}, u32[]{:S(2)}) collective-permute-start(bf16[4,64,256]{2,1,0:T(8,128)(2,1)S(1)} %get-tuple-element.233), channel_id=1, source_target_pairs={{0,24},{4,28},{8,16},{12,20},{16,8},{20,12},{24,0},{28,4},{1,25},{... | collective-permute-start | bytes 393224 | tf_op jit(solution)/shard_map/ppermute | solution.py:337
  189.1 8.5 %collective-permute-start.37 = (f32[4,128]{1,0:T(4,128)S(1)}, f32[4,128]{1,0:T(4,128)S(1)}, u32[]{:S(2)}, u32[]{:S(2)}) collective-permute-start(f32[4,128]{1,0:T(4,128)S(1)} %get-tuple-element.264), channel_id=1, source_target_pairs={{0,1},{1,2},{2,3},{3,0},{4,5},{5,6},{6,7},{7,4},{8,9},{9,10},{10,1... | collective-permute-start | bytes 6152 | tf_op jit(solution)/shard_map/ppermute | solution.py:340
  189.9 7.7 %collective-permute-start.36 = (f32[4,128]{1,0:T(4,128)S(1)}, f32[4,128]{1,0:T(4,128)S(1)}, u32[]{:S(2)}, u32[]{:S(2)}) collective-permute-start(f32[4,128]{1,0:T(4,128)S(1)} %get-tuple-element.265), channel_id=1, source_target_pairs={{0,2},{1,3},{2,0},{3,1},{4,6},{5,7},{6,4},{7,5},{8,10},{9,11},{10,... | collective-permute-start | bytes 6152 | tf_op jit(solution)/shard_map/ppermute | solution.py:340
  190.6 7.1 %collective-permute-start.35 = (f32[4,128]{1,0:T(4,128)S(1)}, f32[4,128]{1,0:T(4,128)S(1)}, u32[]{:S(2)}, u32[]{:S(2)}) collective-permute-start(f32[4,128]{1,0:T(4,128)S(1)} %get-tuple-element.266), channel_id=1, source_target_pairs={{0,3},{1,0},{2,1},{3,2},{4,7},{5,4},{6,5},{7,6},{8,11},{9,8},{10,9... | collective-permute-start | bytes 6152 | tf_op jit(solution)/shard_map/ppermute | solution.py:340
  (42 other events, 411.0 us)

commit v13 on v12

--- a/solution.py
+++ b/solution.py
@@ -234,12 +234,12 @@
     for array in arrived:
         total += array[...].astype(F32)
     if not last:
-        out_ref[...] = total.astype(BF16)
+        out_ref[...] = total.astype(out_ref.dtype)
         return
     out_ref[...] = total.reshape(out_ref.shape)
 
 
-def half_grad(half, scatters, pieces, arrived, experts, tile, last):
+def half_grad(half, scatters, pieces, arrived, experts, tile, last, dtype=BF16):
     height = scatters[0].shape[1]
     width = pieces[0].shape[1]
     count = sum(p.shape[0] for p in pieces)
@@ -252,7 +252,7 @@
         out_shape = jax.ShapeDtypeStruct((height // experts, experts, width), F32)
     else:
         out_spec = pl.BlockSpec((height, tile), lambda i: (0, i))
-        out_shape = jax.ShapeDtypeStruct((height, width), BF16)
+        out_shape = jax.ShapeDtypeStruct((height, width), dtype)
     return pl.pallas_call(
         functools.partial(half_grad_kernel, len(scatters), len(arrived), last),
         grid=(width // tile,),
@@ -405,19 +405,20 @@
     grads2, scatter2 = kernel([([xy1], 3, 1), ([y2], 2, 2), ([own3], 0, 3), ([y3], 2, 3)])
     first = [grad_out, x0, y0, xy0, next1, x1, y1, next2, x2, x3]
     mine, other = 0, 1
-    partner = half_grad(other, [scatter0, scatter1], first, [], experts, 896, False)
-    xy2, xy3, returned0, returned1, grads2, scatter2, partner = fence(
-        (xy2, xy3, returned0, returned1, grads2, scatter2, partner)
-    )
-
-    partner = across(partner, 1)
+    xy2, xy3, returned0, returned1, grads2, scatter2 = fence(
+        (xy2, xy3, returned0, returned1, grads2, scatter2)
+    )
+
     returned2 = send_back(grads2, (3, 2, 0, 2))
     grads3, scatter3 = kernel([([xy2], 3, 2), ([xy3], 3, 3)])
     late = [xy1, y2, own3, y3, xy2, xy3]
-    later = half_grad(other, [scatter2, scatter3], late, [], experts, 896, False)
-    partner, returned2, later, grads3, scatter3 = fence((partner, returned2, later, grads3, scatter3))
+    scatters = [scatter0, scatter1, scatter2, scatter3]
+    later = half_grad(other, scatters, first + late, [], experts, 896, False)
+    returned2, later, grads3, scatter0 = fence((returned2, later, grads3, scatter0))
+    early = half_grad(mine, [scatter0, scatter1], first, [], experts, 896, False, F32)
     later = across(later, 1)
     returned3 = send_back(grads3, (3, 3))
+    returned3, early = fence((returned3, early))
     returned = [
         *returned0,
         *returned1[:3],
@@ -443,8 +444,7 @@
     hidden_grad = jnp.transpose(placed[:, :, :most], (1, 0, 2, 3)).reshape(saved_hidden.shape)
     route_grad = ROUTE_SCALE * route_grad.T
     affinity_grad = (route_grad - jnp.sum(route_grad * shares, axis=-1, keepdims=True)) / totals
-    scatters = [scatter0, scatter1, scatter2, scatter3]
-    down_grad = half_grad(mine, scatters, first + late, [partner, later], experts, 896, True)
+    down_grad = half_grad(mine, [scatter2, scatter3], late, [later, early], experts, 896, True)
     return (affinity_grad, hidden_grad, down_grad)
 
 

time: 215 us -> 238 us (1.11)
  waiting for transfers between devices: 50.2 us -> 61.3 us
  local copies, waits for them, and re-layouts: 31.6 us -> 41.4 us
  Pallas kernels: 66.1 us -> 68.7 us
    ppermute x27 -> x26, waiting for transfers between devices: 26.4 us -> 36.7 us  [across(): return lax.ppermute(array, 'rep', [(i, i ^ bits) for i in range(reps)])]
    unnamed x109 -> x123, local copies, waits for them, and re-layouts: 15 us -> 24.7 us
    pallas_call x3, Pallas kernels: 29 us -> 32 us  [half_grad(): pl.pallas_call(functools.partial(half_grad_kernel, len(scatters), len(arr...]
    ppermute x27 -> x26, starting transfers between devices: 28.8 us -> 28.7 us  [across(): return lax.ppermute(array, 'rep', [(i, i ^ bits) for i in range(reps)])]
  transfers between devices with their start and end apart: 39 -> 38, of which waited for: 15 -> 13; matrix products, arithmetic and copies ran while one was open for 15% -> 13% of each run, Pallas kernels for 24% -> 24%
where the time goes in v13:
time: 238 us; the launch traced here: 237 us
  Pallas kernels  68.7 us (29%)
  waiting for transfers between devices  61.3 us (26%)
  starting transfers between devices  52.4 us (22%)
  local copies, waits for them, and re-layouts  41.4 us (17%)
  other arithmetic  11.5 us (5%)
    ppermute x26, waiting for transfers between devices, across(): return lax.ppermute(array, 'rep', [(i, i ^ bits) for i in range(reps)])  36.7 us
    pallas_call x4, Pallas kernels, project(): pl.pallas_call(functools.partial(project_kernel, top_k, sizes, len(items)...  32.2 us
    pallas_call x3, Pallas kernels, half_grad(): pl.pallas_call(functools.partial(half_grad_kernel, len(scatters), len(arr...  32 us
    ppermute x26, starting transfers between devices, across(): return lax.ppermute(array, 'rep', [(i, i ^ bits) for i in range(reps)])  28.7 us
    unnamed x123, local copies, waits for them, and re-layouts  24.7 us
    ppermute x12, waiting for transfers between devices, around(): lax.ppermute(array, 'exp', [(i, (i + shift) % sources) for i in range(sou...  24.6 us
    ppermute x12, starting transfers between devices, around(): lax.ppermute(array, 'exp', [(i, (i + shift) % sources) for i in range(sou...  23.6 us
    reshape x2, local copies, waits for them, and re-layouts, on_device_tokens(): saved_hidden.reshape(experts, sources, most, 8, block)  7.92 us
  transfers between devices with their start and end apart: 38, of which 13 were waited for; matrix products, arithmetic and copies ran while one was open for 13% of the time, Pallas kernels for 24%

profile of v13, /device:TPU:0, one launch (start us, length us, event | category | flops | bytes accessed | tf_op | source)
XLA Modules:
  0.0 236.6 jit_solution(14858989829561055893)
XLA Ops:
  0.6 3.1 %collective-permute-start.5 = (bf16[128,3584]{1,0:T(8,128)(2,1)}, bf16[128,3584]{1,0:T(8,128)(2,1)S(1)}, u32[]{:S(2)}, u32[]{:S(2)}) collective-permute-start(bf16[128,3584]{1,0:T(8,128)(2,1)} %refs_2_.1), channel_id=1, source_target_pairs={{0,1},{1,2},{2,3},{3,0},{4,5},{5,6},{6,7},{7,4},{8,9},{9,10},{10,1... | collective-permute-start | bytes 2752520 | tf_op jit(solution)/shard_map/ppermute | solution.py:340
  3.7 1.5 collective-permute-start.4
  5.2 1.5 collective-permute-start.3
  8.8 2.7 %collective-permute-start.1 = (bf16[4,256]{1,0:T(4,128)(2,1)S(1)}, bf16[4,256]{1,0:T(4,128)(2,1)S(1)}, u32[]{:S(2)}, u32[]{:S(2)}) collective-permute-start(bf16[4,256]{1,0:T(4,128)(2,1)S(1)} %pad_maximum_fusion.5), channel_id=1, source_target_pairs={{0,2},{1,3},{2,0},{3,1},{4,6},{5,7},{6,4},{7,5},{8,10},{9,11},{10,... | collective-permute-start | bytes 6152 | tf_op jit(solution)/shard_map/ppermute | solution.py:340
  11.7 4.3 %reshape.47 = bf16[4,4,60,8,128]{4,3,1,2,0:T(8,128)(2,1)} reshape(bf16[1,4,4,60,1024]{4,2,3,1,0:T(4,128)(2,1)} %param.8) | data formatting | bytes 3932160 | tf_op jit(solution)/shard_map/reshape | solution.py:359
  16.0 3.6 %copy.15 = bf16[4,4,60,8,128]{4,2,1,0,3:T(8,128)(2,1)} copy(bf16[4,4,60,8,128]{4,3,1,2,0:T(8,128)(2,1)} %reshape.47) | data formatting | bytes 3932160 | tf_op jit(solution)/shard_map/reshape | solution.py:359
  19.6 2.9 %dynamic-slice_bitcast_fusion = (bf16[4,4,60,128]{3,2,1,0:T(8,128)(2,1)S(1)}, bf16[4,4,60,128]{3,2,1,0:T(8,128)(2,1)}, bf16[4,4,60,128]{3,2,1,0:T(8,128)(2,1)}, ...) fusion(bf16[8,4,4,60,128]{4,3,2,1,0:T(8,128)(2,1)} %bitcast.65,, ...), kind=kLoop, calls=%fused_computation.7 | loop fusion | bytes 3932192 | tf_op jit(solution)/shard_map/jit(dynamic_index_in_dim)/squeeze | solution.py:361
  22.5 2.4 %copy.12 = bf16[4,128,3584]{2,1,0:T(8,128)(2,1)} copy(bf16[4,128,3584]{2,0,1:T(4,128)(2,1)S(1)} %bitcast.66) | data formatting | bytes 7340032 | tf_op jit(solution)/shard_map/transpose | solution.py:362
  24.9 3.6 %collective-permute-start.2 = (bf16[4,256]{1,0:T(4,128)(2,1)S(1)}, bf16[4,256]{1,0:T(4,128)(2,1)S(1)}, u32[]{:S(2)}, u32[]{:S(2)}) collective-permute-start(bf16[4,256]{1,0:T(4,128)(2,1)S(1)} %pad_maximum_fusion.5), channel_id=1, source_target_pairs={{0,3},{1,0},{2,1},{3,2},{4,7},{5,4},{6,5},{7,6},{8,11},{9,8},{10,9... | collective-permute-start | bytes 6152 | tf_op jit(solution)/shard_map/ppermute | solution.py:340
  28.5 1.3 collective-permute-done.2
  30.7 1.5 collective-permute-start.6
  32.2 1.5 collective-permute-start.9
  33.9 1.9 pad_maximum_fusion.1
  36.3 18.9 %collective-permute-done.11.refs_3_.refs_11_.refs_9_ = bf16[128,3584]{1,0:T(8,128)(2,1)} collective-permute-done((bf16[128,3584]{1,0:T(8,128)(2,1)S(1)}, bf16[128,3584]{1,0:T(8,128)(2,1)}, u32[]{:S(2)}, u32[]{:S(2)}) %collective-permute-start.11) | collective-permute-done | bytes 917536 | tf_op jit(solution)/shard_map/ppermute | solution.py:340
  55.1 1.7 collective-permute-start.12
  56.9 8.5 %collective-permute-done.7.refs_9_.refs_6_.refs_4_.refs_5_ = bf16[4,4,64,256]{3,2,1,0:T(8,128)(2,1)S(1)} collective-permute-done((bf16[4,4,64,256]{3,2,1,0:T(8,128)(2,1)S(1)}, bf16[4,4,64,256]{3,2,1,0:T(8,128)(2,1)S(1)}, u32[]{:S(2)}, u32[]{:S(2)}) %collective-permute-start.7) | collective-permute-done | bytes 524320 | tf_op jit(solution)/shard_map/ppermute | solution.py:337
  65.8 1.5 collective-permute-start.10
  67.9 6.9 %pad_maximum_fusion.refs_4_.refs_5_.refs_6_.refs_7_.refs_2_.refs_3_ = bf16[2,512,3584]{2,1,0:T(8,128)(2,1)} fusion(bf16[1,512,3584]{2,1,0:T(8,128)(2,1)} %bitcast.31, bf16[1,512,3584]{2,1,0:T(8,128)(2,1)} %bitcast.30), kind=kLoop, calls=%fused_computation | loop fusion | flops 3670016 | bytes 14680064 | tf_op jit(solution)/shard_map/stack | solution.py:385
  74.7 3.8 %collective-permute-done.10.refs_8_.refs_10_.refs_7_.refs_9_ = bf16[4,4,64,256]{3,2,1,0:T(8,128)(2,1)S(1)} collective-permute-done((bf16[4,4,64,256]{3,2,1,0:T(8,128)(2,1)S(1)}, bf16[4,4,64,256]{3,2,1,0:T(8,128)(2,1)S(1)}, u32[]{:S(2)}, u32[]{:S(2)}) %collective-permute-start.10) | collective-permute-done | bytes 524320 | tf_op jit(solution)/shard_map/ppermute | solution.py:337
  83.5 3.4 %collective-permute-start.16 = (bf16[128,3584]{1,0:T(8,128)(2,1)}, bf16[128,3584]{1,0:T(8,128)(2,1)}, u32[]{:S(2)}, u32[]{:S(2)}) collective-permute-start(bf16[128,3584]{1,0:T(8,128)(2,1)} %collective-permute-done.3.refs_1_.refs_5_.refs_3_), channel_id=1, source_target_pairs={{0,3},{1,0},{2,1},{3,2},{4,7},{5,4},{6,5},{7,6},{8,11},{9,8},{10,9... | collective-permute-start | bytes 2752520 | tf_op jit(solution)/shard_map/ppermute | solution.py:340
  87.0 3.1 %copy-done = bf16[2,512,3584]{2,1,0:T(8,128)(2,1)S(1)} copy-done((bf16[2,512,3584]{2,1,0:T(8,128)(2,1)S(1)}, bf16[2,512,3584]{2,1,0:T(8,128)(2,1)}, u32[]{:S(2)}) %copy-start) | copy-done | bytes 7340056
  94.6 8.1 %shard_map.76 = (bf16[4,64,256]{2,1,0:T(8,128)(2,1)S(1)}, bf16[4,64,256]{2,1,0:T(8,128)(2,1)S(1)}, bf16[4,64,256]{2,1,0:T(8,128)(2,1)S(1)}, bf16[4,64,256]{2,1,0:T(8,128)(2,1)S(1)}, bf16[2,512,512]{2,1,0:T(8,128)(2,1)S(1)}) custom-call(s32[5]{0:T(128)S(1)} %stack.98.idx_ref, bf16[128,3584]{1,0:T(8,128)(2,1)S(1)} %copy-done.10, ...), custom_call_target="tpu_custom_call" | custom-call | flops 7516192768 | bytes 11010048 | tf_op jit(solution)/shard_map/pallas_call | solution.py:178
  103.1 1.8 collective-permute-done.16.refs_5_.refs_13_.refs_11_
  104.8 4.3 %collective-permute-start.19 = (bf16[128,3584]{1,0:T(8,128)(2,1)S(1)}, bf16[128,3584]{1,0:T(8,128)(2,1)S(1)}, u32[]{:S(2)}, u32[]{:S(2)}) collective-permute-start(bf16[128,3584]{1,0:T(8,128)(2,1)S(1)} %copy-done.17), channel_id=1, source_target_pairs={{0,3},{1,0},{2,1},{3,2},{4,7},{5,4},{6,5},{7,6},{8,11},{9,8},{10,9... | collective-permute-start | bytes 2752520 | tf_op jit(solution)/shard_map/ppermute | solution.py:340
  111.0 12.1 %shard_map.77 = (bf16[4,64,256]{2,1,0:T(8,128)(2,1)S(1)}, bf16[4,64,256]{2,1,0:T(8,128)(2,1)S(1)}, bf16[4,64,256]{2,1,0:T(8,128)(2,1)S(1)}, bf16[4,64,256]{2,1,0...) custom-call(s32[5]{0:T(128)S(1)} %stack.98.idx_ref, ...), custom_call_target="tpu_custom_call" | custom-call | flops 11274289152 | bytes 12845056 | tf_op jit(solution)/shard_map/pallas_call | solution.py:178
  123.1 2.6 %collective-permute-done.19.refs_3_.refs_17_.refs_7_ = bf16[128,3584]{1,0:T(8,128)(2,1)S(1)} collective-permute-done((bf16[128,3584]{1,0:T(8,128)(2,1)S(1)}, bf16[128,3584]{1,0:T(8,128)(2,1)S(1)}, u32[]{:S(2)}, u32[]{:S(2)}) %collective-permute-start.19) | collective-permute-done | bytes 917536 | tf_op jit(solution)/shard_map/ppermute | solution.py:340
  125.7 3.5 %collective-permute-done.17.refs_0_.refs_14_.refs_4_ = bf16[128,3584]{1,0:T(8,128)(2,1)S(1)} collective-permute-done((bf16[128,3584]{1,0:T(8,128)(2,1)}, bf16[128,3584]{1,0:T(8,128)(2,1)S(1)}, u32[]{:S(2)}, u32[]{:S(2)}) %collective-permute-start.17) | collective-permute-done | bytes 917536 | tf_op jit(solution)/shard_map/ppermute | solution.py:337
  130.8 1.9 collective-permute-start.20
  133.3 1.9 collective-permute-start.24
  135.6 1.6 collective-permute-start.25
  137.2 18.5 %collective-permute-done.23.refs_2_ = bf16[4,64,256]{2,1,0:T(8,128)(2,1)S(1)} collective-permute-done((bf16[4,64,256]{2,1,0:T(8,128)(2,1)S(1)}, bf16[4,64,256]{2,1,0:T(8,128)(2,1)S(1)}, u32[]{:S(2)}, u32[]{:S(2)}) %collective-permute-start.23) | collective-permute-done | bytes 131104 | tf_op jit(solution)/shard_map/ppermute | solution.py:337
  156.5 1.7 collective-permute-start.27
  158.6 7.4 %shard_map.78 = (bf16[4,64,256]{2,1,0:T(8,128)(2,1)S(1)}, bf16[4,64,256]{2,1,0:T(8,128)(2,1)S(1)}, bf16[4,64,256]{2,1,0:T(8,128)(2,1)S(1)}, bf16[4,64,256]{2,1,0:T(8,128)(2,1)S(1)}, bf16[2,512,512]{2,1,0:T(8,128)(2,1)S(1)}) custom-call(s32[5]{0:T(128)S(1)} %stack.98.idx_ref, bf16[128,3584]{1,0:T(8,128)(2,1)S(1)} %collective-permute-done.17.refs_0_.refs_14_.refs_4_, ...), custom_call_target="tpu_custom_call" | custom-call | flops 7516192768 | bytes 11010048 | tf_op jit(solution)/shard_map/pallas_call | solution.py:178
  166.2 1.6 collective-permute-start.29
  167.8 1.6 collective-permute-start.30
  169.8 4.7 %shard_map.79 = (bf16[4,64,256]{2,1,0:T(8,128)(2,1)S(1)}, bf16[4,64,256]{2,1,0:T(8,128)(2,1)S(1)}, bf16[2,512,256]{2,1,0:T(8,128)(2,1)S(1)}) custom-call(s32[5]{0:T(128)S(1)} %stack.98.idx_ref, bf16[128,3584]{1,0:T(8,128)(2,1)S(1)} %collective-permute-done.20.refs_0_.refs_18_.refs_8_, bf16[128,3584]{1,0:T(8,128)(2,1)S(1)} %collective-permute-done.21.refs_1_.refs_19_.refs_9_, ...), custom_call_target="tpu_custom_call" | custom-call | flops 3758096384 | bytes 9175040 | tf_op jit(solution)/shard_map/pallas_call | solution.py:178
  174.6 12.6 %shard_map.80 = bf16[512,3584]{1,0:T(8,128)(2,1)} custom-call(bf16[2,512,512]{2,1,0:T(8,128)(2,1)S(1)} %get-tuple-element.231.refs_0_, bf16[2,512,768]{2,1,0:T(8,128)(2,1)S(1)} %get-tuple-element.218.refs_1_, bf16[2,512,512]{2,1,0:T(8,128)(2,1)S(1)} %get-tuple-element.219.refs_2_.refs_0_, bf16[2,512,256]{2,1,0:T(8,128)(2,1)S(1)} %get-tuple-element.222.refs_3_.refs_1_, ...), custom_call_target="tpu_custom_call" | custom-call | flops 7516192768 | bytes 24117248 | tf_op jit(solution)/shard_map/pallas_call | solution.py:256
  188.1 1.4 collective-permute-start.32
  189.5 1.5 collective-permute-start.33
  191.0 1.4 copy-done.6
  192.4 1.2 copy-done.9
  198.3 8.4 %shard_map.81.refs_3_ = f32[512,3584]{1,0:T(8,128)S(1)} custom-call(bf16[2,512,512]{2,1,0:T(8,128)(2,1)S(1)} %copy-done.9, bf16[2,512,768]{2,1,0:T(8,128)(2,1)S(1)} %copy-done.6, bf16[128,3584]{1,0:T(8,128)(2,1)S(1)} %copy-done.12, bf16[128,3584]{1,0:T(8,128)(2,1)} %collective-permute-done.3.refs_1_.refs_5_.refs_3_, bf16[128,3584]{1,0:T(8,128)(2,1)S(1)} %copy-done.19, ...), custom_call_target="tpu_custom_call" | custom-call | flops 4697620480 | bytes 17825792 | tf_op jit(solution)/shard_map/pallas_call | solution.py:256
  206.8 3.0 %copy-done.2 = f32[512,3584]{1,0:T(8,128)} copy-done((f32[512,3584]{1,0:T(8,128)}, f32[512,3584]{1,0:T(8,128)S(1)}, u32[]{:S(2)}) %copy-start.2) | copy-done | bytes 7340056
  211.0 4.5 %shard_map.82 = (bf16[4,4,64,1024]{3,2,1,0:T(8,128)(2,1)}, f32[16,128]{1,0:T(8,128)}) custom-call(s32[12]{0:T(128)} %stack.88.idx_ref, bf16[4,64,256]{2,1,0:T(8,128)(2,1)} %copy-done.33, bf16[4,64,256]{2,1,0:T(8,128)(2,1)} %copy-done.44, bf16[4,64,256]{2,1,0:T(8,128)(2,1)} %copy-done.45, bf16[4,64,256]{2,1,0:T(8,128)(2,1)} %copy-done.46, ...), custom_call_target="tpu_custom_call" | custom-call | bytes 4194304 | tf_op jit(solution)/shard_map/pallas_call | solution.py:300
  217.4 2.8 %collective-permute-start.34 = (f32[4,128]{1,0:T(4,128)S(1)}, f32[4,128]{1,0:T(4,128)S(1)}, u32[]{:S(2)}, u32[]{:S(2)}) collective-permute-start(f32[4,128]{1,0:T(4,128)S(1)} %get-tuple-element.268), channel_id=1, source_target_pairs={{0,3},{1,0},{2,1},{3,2},{4,7},{5,4},{6,5},{7,6},{8,11},{9,8},{10,9... | collective-permute-start | bytes 6152 | tf_op jit(solution)/shard_map/ppermute | solution.py:340
  220.2 1.9 slice_bitcast_fusion
  222.1 2.8 %copy.13 = bf16[1,4,4,60,1024]{4,2,3,1,0:T(4,128)(2,1)} copy(bf16[1,4,4,60,1024]{4,3,1,2,0:T(8,128)(2,1)S(1)} %slice_bitcast_fusion) | data formatting | bytes 3932160
  225.6 11.0 %shard_map.83 = f32[128,4,3584]{2,1,0:T(4,128)} custom-call(bf16[2,512,512]{2,1,0:T(8,128)(2,1)} %copy-done.7, bf16[2,512,256]{2,1,0:T(8,128)(2,1)} %copy-done.32, bf16[512,3584]{1,0:T(8,128)(2,1)} %collective-permute-done.37.refs_2_, f32[512,3584]{1,0:T(8,128)} %copy-done.2, bf16[128,3584]{1,0:T(8,128)(2,1)} %copy-done.30, bf16[128,3584]{1,0:T(8,128)(2,1)} %copy-done.31, ...), custom_call_target="tpu_custom_call" | custom-call | flops 2818572288 | bytes 13631488 | tf_op jit(solution)/shard_map/pallas_call | solution.py:256
  (181 shorter events, 30.0 us)
Async XLA Ops:
  0.6 29.2 %collective-permute-start.5 = (bf16[128,3584]{1,0:T(8,128)(2,1)}, bf16[128,3584]{1,0:T(8,128)(2,1)S(1)}, u32[]{:S(2)}, u32[]{:S(2)}) collective-permute-start(bf16[128,3584]{1,0:T(8,128)(2,1)} %refs_2_.1), channel_id=1, source_target_pairs={{0,1},{1,2},{2,3},{3,0},{4,5},{5,6},{6,7},{7,4},{8,9},{9,10},{10,1... | collective-permute-start | bytes 2752520 | tf_op jit(solution)/shard_map/ppermute | solution.py:340
  3.7 26.1 %collective-permute-start.4 = (bf16[128,3584]{1,0:T(8,128)(2,1)}, bf16[128,3584]{1,0:T(8,128)(2,1)S(1)}, u32[]{:S(2)}, u32[]{:S(2)}) collective-permute-start(bf16[128,3584]{1,0:T(8,128)(2,1)} %refs_2_.1), channel_id=1, source_target_pairs={{0,16},{4,20},{8,24},{12,28},{16,0},{20,4},{24,8},{28,12},{1,17},{... | collective-permute-start | bytes 2752520 | tf_op jit(solution)/shard_map/ppermute | solution.py:337
  5.2 24.6 %collective-permute-start.3 = (bf16[128,3584]{1,0:T(8,128)(2,1)}, bf16[128,3584]{1,0:T(8,128)(2,1)}, u32[]{:S(2)}, u32[]{:S(2)}) collective-permute-start(bf16[128,3584]{1,0:T(8,128)(2,1)} %refs_2_.1), channel_id=1, source_target_pairs={{0,8},{4,12},{8,0},{12,4},{16,24},{20,28},{24,16},{28,20},{1,9},{5... | collective-permute-start | bytes 2752520 | tf_op jit(solution)/shard_map/ppermute | solution.py:337
  8.8 16.1 %collective-permute-start.1 = (bf16[4,256]{1,0:T(4,128)(2,1)S(1)}, bf16[4,256]{1,0:T(4,128)(2,1)S(1)}, u32[]{:S(2)}, u32[]{:S(2)}) collective-permute-start(bf16[4,256]{1,0:T(4,128)(2,1)S(1)} %pad_maximum_fusion.5), channel_id=1, source_target_pairs={{0,2},{1,3},{2,0},{3,1},{4,6},{5,7},{6,4},{7,5},{8,10},{9,11},{10,... | collective-permute-start | bytes 6152 | tf_op jit(solution)/shard_map/ppermute | solution.py:340
  11.4 17.1 %collective-permute-start = (bf16[4,256]{1,0:T(4,128)(2,1)S(1)}, bf16[4,256]{1,0:T(4,128)(2,1)S(1)}, u32[]{:S(2)}, u32[]{:S(2)}) collective-permute-start(bf16[4,256]{1,0:T(4,128)(2,1)S(1)} %pad_maximum_fusion.5), channel_id=1, source_target_pairs={{0,1},{1,2},{2,3},{3,0},{4,5},{5,6},{6,7},{7,4},{8,9},{9,10},{10,1... | collective-permute-start | bytes 6152 | tf_op jit(solution)/shard_map/ppermute | solution.py:340
  24.9 4.9 %collective-permute-start.2 = (bf16[4,256]{1,0:T(4,128)(2,1)S(1)}, bf16[4,256]{1,0:T(4,128)(2,1)S(1)}, u32[]{:S(2)}, u32[]{:S(2)}) collective-permute-start(bf16[4,256]{1,0:T(4,128)(2,1)S(1)} %pad_maximum_fusion.5), channel_id=1, source_target_pairs={{0,3},{1,0},{2,1},{3,2},{4,7},{5,4},{6,5},{7,6},{8,11},{9,8},{10,9... | collective-permute-start | bytes 6152 | tf_op jit(solution)/shard_map/ppermute | solution.py:340
  29.8 81.1 %copy-start.13 = (bf16[128,3584]{1,0:T(8,128)(2,1)}, bf16[128,3584]{1,0:T(8,128)(2,1)S(1)}, u32[]{:S(2)}) copy-start(bf16[128,3584]{1,0:T(8,128)(2,1)S(1)} %collective-permute-done.5.refs_0_.refs_8_.refs_6_) | copy-start | bytes 2752516
  29.9 38.0 %collective-permute-start.13 = (bf16[512,3584]{1,0:T(8,128)(2,1)}, bf16[512,3584]{1,0:T(8,128)(2,1)}, u32[]{:S(2)}, u32[]{:S(2)}) collective-permute-start(bf16[512,3584]{1,0:T(8,128)(2,1)} %bitcast.25), channel_id=1, source_target_pairs={{0,4},{4,0},{8,12},{12,8},{16,20},{20,16},{24,28},{28,24},{1,5},{5... | collective-permute-start | bytes 11010056 | tf_op jit(solution)/shard_map/ppermute | solution.py:337
  30.0 25.2 %collective-permute-start.11 = (bf16[128,3584]{1,0:T(8,128)(2,1)S(1)}, bf16[128,3584]{1,0:T(8,128)(2,1)}, u32[]{:S(2)}, u32[]{:S(2)}) collective-permute-start(bf16[128,3584]{1,0:T(8,128)(2,1)S(1)} %collective-permute-done.5.refs_0_.refs_8_.refs_6_), channel_id=1, source_target_pairs={{0,1},{1,2},{2,3},{3,0},{4,5},{5,6},{6,7},{7,4},{8,9},{9,10},{10,1... | collective-permute-start | bytes 2752520 | tf_op jit(solution)/shard_map/ppermute | solution.py:340
  30.7 36.6 %collective-permute-start.6 = (bf16[128,3584]{1,0:T(8,128)(2,1)S(1)}, bf16[128,3584]{1,0:T(8,128)(2,1)S(1)}, u32[]{:S(2)}, u32[]{:S(2)}) collective-permute-start(bf16[128,3584]{1,0:T(8,128)(2,1)S(1)} %collective-permute-done.5.refs_0_.refs_8_.refs_6_), channel_id=1, source_target_pairs={{0,8},{4,12},{8,0},{12,4},{16,24},{20,28},{24,16},{28,20},{1,9},{5... | collective-permute-start | bytes 2752520 | tf_op jit(solution)/shard_map/ppermute | solution.py:337
  32.2 33.6 %collective-permute-start.9 = (bf16[128,3584]{1,0:T(8,128)(2,1)}, bf16[128,3584]{1,0:T(8,128)(2,1)S(1)}, u32[]{:S(2)}, u32[]{:S(2)}) collective-permute-start(bf16[128,3584]{1,0:T(8,128)(2,1)} %collective-permute-done.3.refs_1_.refs_5_.refs_3_), channel_id=1, source_target_pairs={{0,16},{4,20},{8,24},{12,28},{16,0},{20,4},{24,8},{28,12},{1,17},{... | collective-permute-start | bytes 2752520 | tf_op jit(solution)/shard_map/ppermute | solution.py:337
  35.7 29.7 %collective-permute-start.7 = (bf16[4,4,64,256]{3,2,1,0:T(8,128)(2,1)S(1)}, bf16[4,4,64,256]{3,2,1,0:T(8,128)(2,1)S(1)}, u32[]{:S(2)}, u32[]{:S(2)}) collective-permute-start(bf16[4,4,64,256]{3,2,1,0:T(8,128)(2,1)S(1)} %get-tuple-element.263), channel_id=1, source_target_pairs={{0,24},{4,28},{8,16},{12,20},{16,8},{20,12},{24,0},{28,4},{1,25},{... | collective-permute-start | bytes 1572872 | tf_op jit(solution)/shard_map/ppermute | solution.py:337
  55.1 25.5 %collective-permute-start.12 = (bf16[128,3584]{1,0:T(8,128)(2,1)S(1)}, bf16[128,3584]{1,0:T(8,128)(2,1)S(1)}, u32[]{:S(2)}, u32[]{:S(2)}) collective-permute-start(bf16[128,3584]{1,0:T(8,128)(2,1)S(1)} %copy-done.10), channel_id=1, source_target_pairs={{0,3},{1,0},{2,1},{3,2},{4,7},{5,4},{6,5},{7,6},{8,11},{9,8},{10,9... | collective-permute-start | bytes 2752520 | tf_op jit(solution)/shard_map/ppermute | solution.py:340
  65.8 12.7 %collective-permute-start.10 = (bf16[4,4,64,256]{3,2,1,0:T(8,128)(2,1)S(1)}, bf16[4,4,64,256]{3,2,1,0:T(8,128)(2,1)S(1)}, u32[]{:S(2)}, u32[]{:S(2)}) collective-permute-start(bf16[4,4,64,256]{3,2,1,0:T(8,128)(2,1)S(1)} %get-tuple-element.147), channel_id=1, source_target_pairs={{0,16},{4,20},{8,24},{12,28},{16,0},{20,4},{24,8},{28,12},{1,17},{... | collective-permute-start | bytes 1572872 | tf_op jit(solution)/shard_map/ppermute | solution.py:337
  67.3 12.6 %collective-permute-start.8 = (bf16[4,4,64,256]{3,2,1,0:T(8,128)(2,1)S(1)}, bf16[4,4,64,256]{3,2,1,0:T(8,128)(2,1)S(1)}, u32[]{:S(2)}, u32[]{:S(2)}) collective-permute-start(bf16[4,4,64,256]{3,2,1,0:T(8,128)(2,1)S(1)} %get-tuple-element.143), channel_id=1, source_target_pairs={{0,8},{4,12},{8,0},{12,4},{16,24},{20,28},{24,16},{28,20},{1,9},{5... | collective-permute-start | bytes 1572872 | tf_op jit(solution)/shard_map/ppermute | solution.py:337
  81.6 21.0 %collective-permute-start.15 = (bf16[128,3584]{1,0:T(8,128)(2,1)}, bf16[128,3584]{1,0:T(8,128)(2,1)}, u32[]{:S(2)}, u32[]{:S(2)}) collective-permute-start(bf16[128,3584]{1,0:T(8,128)(2,1)} %collective-permute-done.11.refs_3_.refs_11_.refs_9_), channel_id=1, source_target_pairs={{0,8},{4,12},{8,0},{12,4},{16,24},{20,28},{24,16},{28,20},{1,9},{5... | collective-permute-start | bytes 2752520 | tf_op jit(solution)/shard_map/ppermute | solution.py:337
  82.6 20.5 %collective-permute-start.14 = (bf16[128,3584]{1,0:T(8,128)(2,1)S(1)}, bf16[128,3584]{1,0:T(8,128)(2,1)}, u32[]{:S(2)}, u32[]{:S(2)}) collective-permute-start(bf16[128,3584]{1,0:T(8,128)(2,1)S(1)} %collective-permute-done.5.refs_0_.refs_8_.refs_6_), channel_id=1, source_target_pairs={{0,16},{4,20},{8,24},{12,28},{16,0},{20,4},{24,8},{28,12},{1,17},{... | collective-permute-start | bytes 2752520 | tf_op jit(solution)/shard_map/ppermute | solution.py:337
  83.5 21.3 %collective-permute-start.16 = (bf16[128,3584]{1,0:T(8,128)(2,1)}, bf16[128,3584]{1,0:T(8,128)(2,1)}, u32[]{:S(2)}, u32[]{:S(2)}) collective-permute-start(bf16[128,3584]{1,0:T(8,128)(2,1)} %collective-permute-done.3.refs_1_.refs_5_.refs_3_), channel_id=1, source_target_pairs={{0,3},{1,0},{2,1},{3,2},{4,7},{5,4},{6,5},{7,6},{8,11},{9,8},{10,9... | collective-permute-start | bytes 2752520 | tf_op jit(solution)/shard_map/ppermute | solution.py:340
  102.7 71.9 %copy-start.8 = (bf16[2,512,512]{2,1,0:T(8,128)(2,1)}, bf16[2,512,512]{2,1,0:T(8,128)(2,1)S(1)}, u32[]{:S(2)}) copy-start(bf16[2,512,512]{2,1,0:T(8,128)(2,1)S(1)} %get-tuple-element.231.refs_0_) | copy-start | bytes 3145732
  104.8 53.7 %copy-start.21 = (bf16[128,3584]{1,0:T(8,128)(2,1)S(1)}, bf16[128,3584]{1,0:T(8,128)(2,1)}, u32[]{:S(2)}) copy-start(bf16[128,3584]{1,0:T(8,128)(2,1)} %copy-done.20) | copy-start | bytes 2752516
  104.8 20.9 %collective-permute-start.19 = (bf16[128,3584]{1,0:T(8,128)(2,1)S(1)}, bf16[128,3584]{1,0:T(8,128)(2,1)S(1)}, u32[]{:S(2)}, u32[]{:S(2)}) collective-permute-start(bf16[128,3584]{1,0:T(8,128)(2,1)S(1)} %copy-done.17), channel_id=1, source_target_pairs={{0,3},{1,0},{2,1},{3,2},{4,7},{5,4},{6,5},{7,6},{8,11},{9,8},{10,9... | collective-permute-start | bytes 2752520 | tf_op jit(solution)/shard_map/ppermute | solution.py:340
  109.1 20.1 %collective-permute-start.17 = (bf16[128,3584]{1,0:T(8,128)(2,1)}, bf16[128,3584]{1,0:T(8,128)(2,1)S(1)}, u32[]{:S(2)}, u32[]{:S(2)}) collective-permute-start(bf16[128,3584]{1,0:T(8,128)(2,1)} %collective-permute-done.14.refs_2_.refs_10_.refs_8_), channel_id=1, source_target_pairs={{0,8},{4,12},{8,0},{12,4},{16,24},{20,28},{24,16},{28,20},{1,9},{5... | collective-permute-start | bytes 2752520 | tf_op jit(solution)/shard_map/ppermute | solution.py:337
  110.3 19.7 %collective-permute-start.18 = (bf16[128,3584]{1,0:T(8,128)(2,1)}, bf16[128,3584]{1,0:T(8,128)(2,1)S(1)}, u32[]{:S(2)}, u32[]{:S(2)}) collective-permute-start(bf16[128,3584]{1,0:T(8,128)(2,1)} %collective-permute-done.11.refs_3_.refs_11_.refs_9_), channel_id=1, source_target_pairs={{0,16},{4,20},{8,24},{12,28},{16,0},{20,4},{24,8},{28,12},{1,17},{... | collective-permute-start | bytes 2752520 | tf_op jit(solution)/shard_map/ppermute | solution.py:337
  123.1 42.9 %copy-start.34 = (bf16[4,64,256]{2,1,0:T(8,128)(2,1)}, bf16[4,64,256]{2,1,0:T(8,128)(2,1)S(1)}, u32[]{:S(2)}) copy-start(bf16[4,64,256]{2,1,0:T(8,128)(2,1)S(1)} %get-tuple-element.210.refs_4_) | copy-start | bytes 393220
  123.1 42.9 %copy-start.35 = (bf16[4,64,256]{2,1,0:T(8,128)(2,1)}, bf16[4,64,256]{2,1,0:T(8,128)(2,1)S(1)}, u32[]{:S(2)}) copy-start(bf16[4,64,256]{2,1,0:T(8,128)(2,1)S(1)} %get-tuple-element.226.refs_8_) | copy-start | bytes 393220
  123.1 51.4 %copy-start.5 = (bf16[2,512,768]{2,1,0:T(8,128)(2,1)}, bf16[2,512,768]{2,1,0:T(8,128)(2,1)S(1)}, u32[]{:S(2)}) copy-start(bf16[2,512,768]{2,1,0:T(8,128)(2,1)S(1)} %get-tuple-element.218.refs_1_) | copy-start | bytes 4718596
  125.7 48.8 %copy-start.29 = (bf16[128,3584]{1,0:T(8,128)(2,1)}, bf16[128,3584]{1,0:T(8,128)(2,1)S(1)}, u32[]{:S(2)}) copy-start(bf16[128,3584]{1,0:T(8,128)(2,1)S(1)} %collective-permute-done.19.refs_3_.refs_17_.refs_7_) | copy-start | bytes 2752516
  129.2 45.3 %copy-start.30 = (bf16[128,3584]{1,0:T(8,128)(2,1)}, bf16[128,3584]{1,0:T(8,128)(2,1)S(1)}, u32[]{:S(2)}) copy-start(bf16[128,3584]{1,0:T(8,128)(2,1)S(1)} %collective-permute-done.17.refs_0_.refs_14_.refs_4_) | copy-start | bytes 2752516
  130.0 44.5 %copy-start.31 = (bf16[128,3584]{1,0:T(8,128)(2,1)}, bf16[128,3584]{1,0:T(8,128)(2,1)S(1)}, u32[]{:S(2)}) copy-start(bf16[128,3584]{1,0:T(8,128)(2,1)S(1)} %collective-permute-done.18.refs_1_.refs_15_.refs_5_) | copy-start | bytes 2752516
  130.0 5.5 %collective-permute-start.22 = (bf16[4,64,256]{2,1,0:T(8,128)(2,1)S(1)}, bf16[4,64,256]{2,1,0:T(8,128)(2,1)S(1)}, u32[]{:S(2)}, u32[]{:S(2)}) collective-permute-start(bf16[4,64,256]{2,1,0:T(8,128)(2,1)S(1)} %get-tuple-element.188), channel_id=1, source_target_pairs={{0,8},{4,12},{8,0},{12,4},{16,24},{20,28},{24,16},{28,20},{1,9},{5... | collective-permute-start | bytes 393224 | tf_op jit(solution)/shard_map/ppermute | solution.py:337
  130.8 35.3 %collective-permute-start.20 = (bf16[128,3584]{1,0:T(8,128)(2,1)}, bf16[128,3584]{1,0:T(8,128)(2,1)S(1)}, u32[]{:S(2)}, u32[]{:S(2)}) collective-permute-start(bf16[128,3584]{1,0:T(8,128)(2,1)} %collective-permute-done.15.refs_4_.refs_12_.refs_10_), channel_id=1, source_target_pairs={{0,16},{4,20},{8,24},{12,28},{16,0},{20,4},{24,8},{28,12},{1,17},{... | collective-permute-start | bytes 2752520 | tf_op jit(solution)/shard_map/ppermute | solution.py:337
  132.7 33.4 %collective-permute-start.21 = (bf16[128,3584]{1,0:T(8,128)(2,1)S(1)}, bf16[128,3584]{1,0:T(8,128)(2,1)S(1)}, u32[]{:S(2)}, u32[]{:S(2)}) collective-permute-start(bf16[128,3584]{1,0:T(8,128)(2,1)S(1)} %copy-done.27), channel_id=1, source_target_pairs={{0,3},{1,0},{2,1},{3,2},{4,7},{5,4},{6,5},{7,6},{8,11},{9,8},{10,9... | collective-permute-start | bytes 2752520 | tf_op jit(solution)/shard_map/ppermute | solution.py:340
  132.7 23.0 %collective-permute-start.23 = (bf16[4,64,256]{2,1,0:T(8,128)(2,1)S(1)}, bf16[4,64,256]{2,1,0:T(8,128)(2,1)S(1)}, u32[]{:S(2)}, u32[]{:S(2)}) collective-permute-start(bf16[4,64,256]{2,1,0:T(8,128)(2,1)S(1)} %get-tuple-element.189), channel_id=1, source_target_pairs={{0,16},{4,20},{8,24},{12,28},{16,0},{20,4},{24,8},{28,12},{1,17},{... | collective-permute-start | bytes 393224 | tf_op jit(solution)/shard_map/ppermute | solution.py:337
  133.3 23.2 %collective-permute-start.24 = (bf16[4,64,256]{2,1,0:T(8,128)(2,1)S(1)}, bf16[4,64,256]{2,1,0:T(8,128)(2,1)S(1)}, u32[]{:S(2)}, u32[]{:S(2)}) collective-permute-start(bf16[4,64,256]{2,1,0:T(8,128)(2,1)S(1)} %get-tuple-element.190), channel_id=1, source_target_pairs={{0,24},{4,28},{8,16},{12,20},{16,8},{20,12},{24,0},{28,4},{1,25},{... | collective-permute-start | bytes 393224 | tf_op jit(solution)/shard_map/ppermute | solution.py:337
  135.6 30.4 %copy-start.44 = (bf16[4,64,256]{2,1,0:T(8,128)(2,1)}, bf16[4,64,256]{2,1,0:T(8,128)(2,1)S(1)}, u32[]{:S(2)}) copy-start(bf16[4,64,256]{2,1,0:T(8,128)(2,1)S(1)} %collective-permute-done.22.refs_1_) | copy-start | bytes 393220
  135.6 22.6 %collective-permute-start.25 = (bf16[4,64,256]{2,1,0:T(8,128)(2,1)S(1)}, bf16[4,64,256]{2,1,0:T(8,128)(2,1)S(1)}, u32[]{:S(2)}, u32[]{:S(2)}) collective-permute-start(bf16[4,64,256]{2,1,0:T(8,128)(2,1)S(1)} %get-tuple-element.192), channel_id=1, source_target_pairs={{0,8},{4,12},{8,0},{12,4},{16,24},{20,28},{24,16},{28,20},{1,9},{5... | collective-permute-start | bytes 393224 | tf_op jit(solution)/shard_map/ppermute | solution.py:337
  155.7 10.3 %collective-permute-start.26 = (bf16[4,64,256]{2,1,0:T(8,128)(2,1)S(1)}, bf16[4,64,256]{2,1,0:T(8,128)(2,1)S(1)}, u32[]{:S(2)}, u32[]{:S(2)}) collective-permute-start(bf16[4,64,256]{2,1,0:T(8,128)(2,1)S(1)} %get-tuple-element.193), channel_id=1, source_target_pairs={{0,16},{4,20},{8,24},{12,28},{16,0},{20,4},{24,8},{28,12},{1,17},{... | collective-permute-start | bytes 393224 | tf_op jit(solution)/shard_map/ppermute | solution.py:337
  156.5 9.5 %collective-permute-start.27 = (bf16[4,64,256]{2,1,0:T(8,128)(2,1)S(1)}, bf16[4,64,256]{2,1,0:T(8,128)(2,1)S(1)}, u32[]{:S(2)}, u32[]{:S(2)}) collective-permute-start(bf16[4,64,256]{2,1,0:T(8,128)(2,1)S(1)} %get-tuple-element.195), channel_id=1, source_target_pairs={{0,8},{4,12},{8,0},{12,4},{16,24},{20,28},{24,16},{28,20},{1,9},{5... | collective-permute-start | bytes 393224 | tf_op jit(solution)/shard_map/ppermute | solution.py:337
  158.2 7.9 %collective-permute-start.28 = (bf16[4,64,256]{2,1,0:T(8,128)(2,1)S(1)}, bf16[4,64,256]{2,1,0:T(8,128)(2,1)S(1)}, u32[]{:S(2)}, u32[]{:S(2)}) collective-permute-start(bf16[4,64,256]{2,1,0:T(8,128)(2,1)S(1)} %get-tuple-element.196), channel_id=1, source_target_pairs={{0,8},{4,12},{8,0},{12,4},{16,24},{20,28},{24,16},{28,20},{1,9},{5... | collective-permute-start | bytes 393224 | tf_op jit(solution)/shard_map/ppermute | solution.py:337
  166.2 21.1 %collective-permute-start.29 = (bf16[4,64,256]{2,1,0:T(8,128)(2,1)S(1)}, bf16[4,64,256]{2,1,0:T(8,128)(2,1)S(1)}, u32[]{:S(2)}, u32[]{:S(2)}) collective-permute-start(bf16[4,64,256]{2,1,0:T(8,128)(2,1)S(1)} %get-tuple-element.213), channel_id=1, source_target_pairs={{0,24},{4,28},{8,16},{12,20},{16,8},{20,12},{24,0},{28,4},{1,25},{... | collective-permute-start | bytes 393224 | tf_op jit(solution)/shard_map/ppermute | solution.py:337
  167.8 19.5 %collective-permute-start.30 = (bf16[4,64,256]{2,1,0:T(8,128)(2,1)S(1)}, bf16[4,64,256]{2,1,0:T(8,128)(2,1)S(1)}, u32[]{:S(2)}, u32[]{:S(2)}) collective-permute-start(bf16[4,64,256]{2,1,0:T(8,128)(2,1)S(1)} %get-tuple-element.214), channel_id=1, source_target_pairs={{0,16},{4,20},{8,24},{12,28},{16,0},{20,4},{24,8},{28,12},{1,17},{... | collective-permute-start | bytes 393224 | tf_op jit(solution)/shard_map/ppermute | solution.py:337
  169.4 17.9 %collective-permute-start.31 = (bf16[4,64,256]{2,1,0:T(8,128)(2,1)S(1)}, bf16[4,64,256]{2,1,0:T(8,128)(2,1)S(1)}, u32[]{:S(2)}, u32[]{:S(2)}) collective-permute-start(bf16[4,64,256]{2,1,0:T(8,128)(2,1)S(1)} %get-tuple-element.216), channel_id=1, source_target_pairs={{0,16},{4,20},{8,24},{12,28},{16,0},{20,4},{24,8},{28,12},{1,17},{... | collective-permute-start | bytes 393224 | tf_op jit(solution)/shard_map/ppermute | solution.py:337
  187.3 38.3 %collective-permute-start.37 = (bf16[512,3584]{1,0:T(8,128)(2,1)}, bf16[512,3584]{1,0:T(8,128)(2,1)}, u32[]{:S(2)}, u32[]{:S(2)}) collective-permute-start(bf16[512,3584]{1,0:T(8,128)(2,1)} %shard_map.80), channel_id=1, source_target_pairs={{0,4},{4,0},{8,12},{12,8},{16,20},{20,16},{24,28},{28,24},{1,5},{5... | collective-permute-start | bytes 11010056 | tf_op jit(solution)/shard_map/ppermute | solution.py:337
  188.1 21.7 %collective-permute-start.32 = (bf16[4,64,256]{2,1,0:T(8,128)(2,1)S(1)}, bf16[4,64,256]{2,1,0:T(8,128)(2,1)S(1)}, u32[]{:S(2)}, u32[]{:S(2)}) collective-permute-start(bf16[4,64,256]{2,1,0:T(8,128)(2,1)S(1)} %get-tuple-element.229), channel_id=1, source_target_pairs={{0,24},{4,28},{8,16},{12,20},{16,8},{20,12},{24,0},{28,4},{1,25},{... | collective-permute-start | bytes 393224 | tf_op jit(solution)/shard_map/ppermute | solution.py:337
  189.5 20.3 %collective-permute-start.33 = (bf16[4,64,256]{2,1,0:T(8,128)(2,1)S(1)}, bf16[4,64,256]{2,1,0:T(8,128)(2,1)S(1)}, u32[]{:S(2)}, u32[]{:S(2)}) collective-permute-start(bf16[4,64,256]{2,1,0:T(8,128)(2,1)S(1)} %get-tuple-element.230), channel_id=1, source_target_pairs={{0,24},{4,28},{8,16},{12,20},{16,8},{20,12},{24,0},{28,4},{1,25},{... | collective-permute-start | bytes 393224 | tf_op jit(solution)/shard_map/ppermute | solution.py:337
  216.4 8.5 %collective-permute-start.36 = (f32[4,128]{1,0:T(4,128)S(1)}, f32[4,128]{1,0:T(4,128)S(1)}, u32[]{:S(2)}, u32[]{:S(2)}) collective-permute-start(f32[4,128]{1,0:T(4,128)S(1)} %get-tuple-element.266), channel_id=1, source_target_pairs={{0,1},{1,2},{2,3},{3,0},{4,5},{5,6},{6,7},{7,4},{8,9},{9,10},{10,1... | collective-permute-start | bytes 6152 | tf_op jit(solution)/shard_map/ppermute | solution.py:340
  216.4 8.5 %collective-permute-start.35 = (f32[4,128]{1,0:T(4,128)S(1)}, f32[4,128]{1,0:T(4,128)S(1)}, u32[]{:S(2)}, u32[]{:S(2)}) collective-permute-start(f32[4,128]{1,0:T(4,128)S(1)} %get-tuple-element.267), channel_id=1, source_target_pairs={{0,2},{1,3},{2,0},{3,1},{4,6},{5,7},{6,4},{7,5},{8,10},{9,11},{10,... | collective-permute-start | bytes 6152 | tf_op jit(solution)/shard_map/ppermute | solution.py:340
  217.4 7.5 %collective-permute-start.34 = (f32[4,128]{1,0:T(4,128)S(1)}, f32[4,128]{1,0:T(4,128)S(1)}, u32[]{:S(2)}, u32[]{:S(2)}) collective-permute-start(f32[4,128]{1,0:T(4,128)S(1)} %get-tuple-element.268), channel_id=1, source_target_pairs={{0,3},{1,0},{2,1},{3,2},{4,7},{5,4},{6,5},{7,6},{8,11},{9,8},{10,9... | collective-permute-start | bytes 6152 | tf_op jit(solution)/shard_map/ppermute | solution.py:340
  (48 other events, 400.2 us)

commit v14 on v12

--- a/solution.py
+++ b/solution.py
@@ -415,9 +415,9 @@
     grads3, scatter3 = kernel([([xy2], 3, 2), ([xy3], 3, 3)])
     late = [xy1, y2, own3, y3, xy2, xy3]
     later = half_grad(other, [scatter2, scatter3], late, [], experts, 896, False)
-    partner, returned2, later, grads3, scatter3 = fence((partner, returned2, later, grads3, scatter3))
+    returned3 = send_back(grads3, (3, 3))
+    partner, returned2, returned3, later = fence((partner, returned2, returned3, later))
     later = across(later, 1)
-    returned3 = send_back(grads3, (3, 3))
     returned = [
         *returned0,
         *returned1[:3],

time: 215 us -> 209 us (0.972)
  waiting for transfers between devices: 50.2 us -> 45.2 us
    ppermute x27, waiting for transfers between devices: 26.4 us -> 21.4 us  [across(): return lax.ppermute(array, 'rep', [(i, i ^ bits) for i in range(reps)])]
  transfers between devices with their start and end apart: 39 -> 39, of which waited for: 15 -> 14; matrix products, arithmetic and copies ran while one was open for 15% -> 15% of each run, Pallas kernels for 24% -> 24%
where the time goes in v14:
time: 209 us; the launch traced here: 208 us
  Pallas kernels  66.1 us (32%)
  starting transfers between devices  52.6 us (25%)
  waiting for transfers between devices  45.2 us (22%)
  local copies, waits for them, and re-layouts  30.9 us (15%)
  other arithmetic  12.2 us (6%)
    pallas_call x4, Pallas kernels, project(): pl.pallas_call(functools.partial(project_kernel, top_k, sizes, len(items)...  32.5 us
    pallas_call x3, Pallas kernels, half_grad(): pl.pallas_call(functools.partial(half_grad_kernel, len(scatters), len(arr...  29 us
    ppermute x27, starting transfers between devices, across(): return lax.ppermute(array, 'rep', [(i, i ^ bits) for i in range(reps)])  28.9 us
    ppermute x12, waiting for transfers between devices, around(): lax.ppermute(array, 'exp', [(i, (i + shift) % sources) for i in range(sou...  23.8 us
    ppermute x12, starting transfers between devices, around(): lax.ppermute(array, 'exp', [(i, (i + shift) % sources) for i in range(sou...  23.7 us
    ppermute x27, waiting for transfers between devices, across(): return lax.ppermute(array, 'rep', [(i, i ^ bits) for i in range(reps)])  21.4 us
    unnamed x109, local copies, waits for them, and re-layouts  14.3 us
    reshape x2, local copies, waits for them, and re-layouts, on_device_tokens(): saved_hidden.reshape(experts, sources, most, 8, block)  7.92 us
  transfers between devices with their start and end apart: 39, of which 14 were waited for; matrix products, arithmetic and copies ran while one was open for 15% of the time, Pallas kernels for 24%

profile of v14, /device:TPU:0, one launch (start us, length us, event | category | flops | bytes accessed | tf_op | source)
XLA Modules:
  0.0 208.3 jit_solution(2116686216151196719)
XLA Ops:
  0.6 3.1 %collective-permute-start.5 = (bf16[128,3584]{1,0:T(8,128)(2,1)}, bf16[128,3584]{1,0:T(8,128)(2,1)S(1)}, u32[]{:S(2)}, u32[]{:S(2)}) collective-permute-start(bf16[128,3584]{1,0:T(8,128)(2,1)} %refs_6_.1), channel_id=1, source_target_pairs={{0,1},{1,2},{2,3},{3,0},{4,5},{5,6},{6,7},{7,4},{8,9},{9,10},{10,1... | collective-permute-start | bytes 2752520 | tf_op jit(solution)/shard_map/ppermute | solution.py:340
  3.7 1.5 collective-permute-start.4
  5.2 1.5 collective-permute-start.3
  8.8 2.7 %collective-permute-start.1 = (bf16[4,256]{1,0:T(4,128)(2,1)S(1)}, bf16[4,256]{1,0:T(4,128)(2,1)S(1)}, u32[]{:S(2)}, u32[]{:S(2)}) collective-permute-start(bf16[4,256]{1,0:T(4,128)(2,1)S(1)} %pad_maximum_fusion.5), channel_id=1, source_target_pairs={{0,2},{1,3},{2,0},{3,1},{4,6},{5,7},{6,4},{7,5},{8,10},{9,11},{10,... | collective-permute-start | bytes 6152 | tf_op jit(solution)/shard_map/ppermute | solution.py:340
  11.7 4.3 %reshape.47 = bf16[4,4,60,8,128]{4,3,1,2,0:T(8,128)(2,1)} reshape(bf16[1,4,4,60,1024]{4,2,3,1,0:T(4,128)(2,1)} %param.8) | data formatting | bytes 3932160 | tf_op jit(solution)/shard_map/reshape | solution.py:359
  16.0 3.6 %copy.15 = bf16[4,4,60,8,128]{4,2,1,0,3:T(8,128)(2,1)} copy(bf16[4,4,60,8,128]{4,3,1,2,0:T(8,128)(2,1)} %reshape.47) | data formatting | bytes 3932160 | tf_op jit(solution)/shard_map/reshape | solution.py:359
  19.6 2.8 %dynamic-slice_bitcast_fusion = (bf16[4,4,60,128]{3,2,1,0:T(8,128)(2,1)S(1)}, bf16[4,4,60,128]{3,2,1,0:T(8,128)(2,1)S(1)}, bf16[4,4,60,128]{3,2,1,0:T(8,128)(2,1...) fusion(bf16[8,4,4,60,128]{4,3,2,1,0:T(8,128)(2,1)} %bitcast.65,, ...), kind=kLoop, calls=%fused_computation.7 | loop fusion | bytes 3932192 | tf_op jit(solution)/shard_map/jit(dynamic_index_in_dim)/squeeze | solution.py:361
  22.4 2.4 %copy.12 = bf16[4,128,3584]{2,1,0:T(8,128)(2,1)} copy(bf16[4,128,3584]{2,0,1:T(4,128)(2,1)S(1)} %bitcast.66) | data formatting | bytes 7340032 | tf_op jit(solution)/shard_map/transpose | solution.py:362
  24.8 3.6 %collective-permute-start.2 = (bf16[4,256]{1,0:T(4,128)(2,1)S(1)}, bf16[4,256]{1,0:T(4,128)(2,1)S(1)}, u32[]{:S(2)}, u32[]{:S(2)}) collective-permute-start(bf16[4,256]{1,0:T(4,128)(2,1)S(1)} %pad_maximum_fusion.5), channel_id=1, source_target_pairs={{0,3},{1,0},{2,1},{3,2},{4,7},{5,4},{6,5},{7,6},{8,11},{9,8},{10,9... | collective-permute-start | bytes 6152 | tf_op jit(solution)/shard_map/ppermute | solution.py:340
  28.4 1.3 collective-permute-done.2
  30.7 1.5 collective-permute-start.6
  32.2 1.5 collective-permute-start.9
  33.9 2.5 %pad_maximum_fusion.1 = (bf16[4,4,64,256]{3,2,1,0:T(8,128)(2,1)S(1)}, bf16[4,4,64,256]{3,2,1,0:T(8,128)(2,1)S(1)}, bf16[4,4,64,256]{3,2,1,0:T(8,128)(2,1)S(1)}, bf16[4,4,64,256]{3,2,1,0:T(8,128)(2,1)}) fusion(bf16[4,4,4,256]{3,2,1,0:T(4,128)(2,1)S(1)} %broadcast_in_dim.49, bf16[4,4,60,128]{3,2,1,0:T(8,128)(2,1)S(1)} %get-tuple-element.143, ...), kind=kLoop, calls=%fused_computation.3 | loop fusion | flops 5505024 | bytes 4096000 | tf_op jit(solution)/shard_map/concatenate | solution.py:377
  36.8 18.2 %collective-permute-done.11.refs_3_.refs_9_.refs_13_ = bf16[128,3584]{1,0:T(8,128)(2,1)} collective-permute-done((bf16[128,3584]{1,0:T(8,128)(2,1)S(1)}, bf16[128,3584]{1,0:T(8,128)(2,1)}, u32[]{:S(2)}, u32[]{:S(2)}) %collective-permute-start.11) | collective-permute-done | bytes 917536 | tf_op jit(solution)/shard_map/ppermute | solution.py:340
  55.1 1.7 collective-permute-start.12
  56.8 8.6 %collective-permute-done.7.refs_9_.refs_6_.refs_4_.refs_5_ = bf16[4,4,64,256]{3,2,1,0:T(8,128)(2,1)S(1)} collective-permute-done((bf16[4,4,64,256]{3,2,1,0:T(8,128)(2,1)S(1)}, bf16[4,4,64,256]{3,2,1,0:T(8,128)(2,1)S(1)}, u32[]{:S(2)}, u32[]{:S(2)}) %collective-permute-start.7) | collective-permute-done | bytes 524320 | tf_op jit(solution)/shard_map/ppermute | solution.py:337
  65.9 1.5 collective-permute-start.10
  68.0 6.9 %pad_maximum_fusion.refs_4_.refs_5_.refs_6_.refs_7_.refs_2_.refs_3_ = bf16[2,512,3584]{2,1,0:T(8,128)(2,1)} fusion(bf16[1,512,3584]{2,1,0:T(8,128)(2,1)} %bitcast.31, bf16[1,512,3584]{2,1,0:T(8,128)(2,1)} %bitcast.30), kind=kLoop, calls=%fused_computation | loop fusion | flops 3670016 | bytes 14680064 | tf_op jit(solution)/shard_map/stack | solution.py:385
  74.8 3.7 %collective-permute-done.10.refs_8_.refs_10_.refs_7_.refs_9_ = bf16[4,4,64,256]{3,2,1,0:T(8,128)(2,1)S(1)} collective-permute-done((bf16[4,4,64,256]{3,2,1,0:T(8,128)(2,1)S(1)}, bf16[4,4,64,256]{3,2,1,0:T(8,128)(2,1)S(1)}, u32[]{:S(2)}, u32[]{:S(2)}) %collective-permute-start.10) | collective-permute-done | bytes 524320 | tf_op jit(solution)/shard_map/ppermute | solution.py:337
  83.5 3.4 %collective-permute-start.16 = (bf16[128,3584]{1,0:T(8,128)(2,1)}, bf16[128,3584]{1,0:T(8,128)(2,1)}, u32[]{:S(2)}, u32[]{:S(2)}) collective-permute-start(bf16[128,3584]{1,0:T(8,128)(2,1)} %collective-permute-done.3.refs_1_.refs_3_.refs_7_), channel_id=1, source_target_pairs={{0,3},{1,0},{2,1},{3,2},{4,7},{5,4},{6,5},{7,6},{8,11},{9,8},{10,9... | collective-permute-start | bytes 2752520 | tf_op jit(solution)/shard_map/ppermute | solution.py:340
  87.0 3.1 %copy-done = bf16[2,512,3584]{2,1,0:T(8,128)(2,1)S(1)} copy-done((bf16[2,512,3584]{2,1,0:T(8,128)(2,1)S(1)}, bf16[2,512,3584]{2,1,0:T(8,128)(2,1)}, u32[]{:S(2)}) %copy-start) | copy-done | bytes 7340056
  93.3 8.4 %shard_map.76 = (bf16[4,64,256]{2,1,0:T(8,128)(2,1)S(1)}, bf16[4,64,256]{2,1,0:T(8,128)(2,1)S(1)}, bf16[4,64,256]{2,1,0:T(8,128)(2,1)S(1)}, bf16[4,64,256]{2,1,0:T(8,128)(2,1)S(1)}, bf16[2,512,512]{2,1,0:T(8,128)(2,1)S(1)}) custom-call(s32[5]{0:T(128)S(1)} %stack.98.idx_ref, bf16[128,3584]{1,0:T(8,128)(2,1)S(1)} %copy-done.15, ...), custom_call_target="tpu_custom_call" | custom-call | flops 7516192768 | bytes 11010048 | tf_op jit(solution)/shard_map/pallas_call | solution.py:178
  103.1 1.8 collective-permute-done.16.refs_5_.refs_11_.refs_15_
  104.8 4.3 %collective-permute-start.19 = (bf16[128,3584]{1,0:T(8,128)(2,1)S(1)}, bf16[128,3584]{1,0:T(8,128)(2,1)S(1)}, u32[]{:S(2)}, u32[]{:S(2)}) collective-permute-start(bf16[128,3584]{1,0:T(8,128)(2,1)S(1)} %collective-permute-done.4.refs_2_.refs_4_.refs_8_), channel_id=1, source_target_pairs={{0,3},{1,0},{2,1},{3,2},{4,7},{5,4},{6,5},{7,6},{8,11},{9,8},{10,9... | collective-permute-start | bytes 2752520 | tf_op jit(solution)/shard_map/ppermute | solution.py:340
  109.1 1.3 collective-permute-start.17
  111.1 12.1 %shard_map.77 = (bf16[4,64,256]{2,1,0:T(8,128)(2,1)S(1)}, bf16[4,64,256]{2,1,0:T(8,128)(2,1)S(1)}, bf16[4,64,256]{2,1,0:T(8,128)(2,1)S(1)}, bf16[4,64,256]{2,1,0...) custom-call(s32[5]{0:T(128)S(1)} %stack.98.idx_ref, ...), custom_call_target="tpu_custom_call" | custom-call | flops 11274289152 | bytes 12845056 | tf_op jit(solution)/shard_map/pallas_call | solution.py:178
  123.2 2.5 %collective-permute-done.19.refs_3_.refs_5_.refs_19_ = bf16[128,3584]{1,0:T(8,128)(2,1)S(1)} collective-permute-done((bf16[128,3584]{1,0:T(8,128)(2,1)S(1)}, bf16[128,3584]{1,0:T(8,128)(2,1)S(1)}, u32[]{:S(2)}, u32[]{:S(2)}) %collective-permute-start.19) | collective-permute-done | bytes 917536 | tf_op jit(solution)/shard_map/ppermute | solution.py:340
  125.8 3.3 %collective-permute-done.17.refs_0_.refs_2_.refs_16_ = bf16[128,3584]{1,0:T(8,128)(2,1)S(1)} collective-permute-done((bf16[128,3584]{1,0:T(8,128)(2,1)}, bf16[128,3584]{1,0:T(8,128)(2,1)S(1)}, u32[]{:S(2)}, u32[]{:S(2)}) %collective-permute-start.17) | collective-permute-done | bytes 917536 | tf_op jit(solution)/shard_map/ppermute | solution.py:337
  129.1 1.3 collective-permute-done.18.refs_1_.refs_3_.refs_17_
  130.4 1.4 collective-permute-start.22
  131.8 2.5 %collective-permute-start.23 = (bf16[4,64,256]{2,1,0:T(8,128)(2,1)S(1)}, bf16[4,64,256]{2,1,0:T(8,128)(2,1)S(1)}, u32[]{:S(2)}, u32[]{:S(2)}) collective-permute-start(bf16[4,64,256]{2,1,0:T(8,128)(2,1)S(1)} %get-tuple-element.187), channel_id=1, source_target_pairs={{0,16},{4,20},{8,24},{12,28},{16,0},{20,4},{24,8},{28,12},{1,17},{... | collective-permute-start | bytes 393224 | tf_op jit(solution)/shard_map/ppermute | solution.py:337
  134.4 1.5 collective-permute-start.25
  135.8 2.0 collective-permute-start.20
  137.9 7.4 %shard_map.78 = (bf16[4,64,256]{2,1,0:T(8,128)(2,1)S(1)}, bf16[4,64,256]{2,1,0:T(8,128)(2,1)S(1)}, bf16[4,64,256]{2,1,0:T(8,128)(2,1)S(1)}, bf16[4,64,256]{2,1,0:T(8,128)(2,1)S(1)}, bf16[2,512,512]{2,1,0:T(8,128)(2,1)S(1)}) custom-call(s32[5]{0:T(128)S(1)} %stack.98.idx_ref, bf16[128,3584]{1,0:T(8,128)(2,1)S(1)} %collective-permute-done.17.refs_0_.refs_2_.refs_16_, ...), custom_call_target="tpu_custom_call" | custom-call | flops 7516192768 | bytes 11010048 | tf_op jit(solution)/shard_map/pallas_call | solution.py:178
  146.1 1.4 collective-permute-start.27
  148.1 8.3 %shard_map.79 = bf16[512,3584]{1,0:T(8,128)(2,1)S(1)} custom-call(bf16[2,512,512]{2,1,0:T(8,128)(2,1)S(1)} %get-tuple-element.204.refs_0_, bf16[2,512,768]{2,1,0:T(8,128)(2,1)S(1)} %get-tuple-element.205.refs_1_, bf16[128,3584]{1,0:T(8,128)(2,1)S(1)} %copy-done.16, bf16[128,3584]{1,0:T(8,128)(2,1)} %collective-permute-done.3.refs_1_.refs_3_.refs_7_, ...), custom_call_target="tpu_custom_call" | custom-call | flops 4697620480 | bytes 17825792 | tf_op jit(solution)/shard_map/pallas_call | solution.py:256
  157.5 1.8 collective-permute-start.30
  159.7 1.7 collective-permute-start.32
  161.3 4.7 %shard_map.80 = (bf16[4,64,256]{2,1,0:T(8,128)(2,1)S(1)}, bf16[4,64,256]{2,1,0:T(8,128)(2,1)S(1)}, bf16[2,512,256]{2,1,0:T(8,128)(2,1)S(1)}) custom-call(s32[5]{0:T(128)S(1)} %stack.98.idx_ref, bf16[128,3584]{1,0:T(8,128)(2,1)S(1)} %collective-permute-done.20.refs_0_.refs_6_.refs_20_, bf16[128,3584]{1,0:T(8,128)(2,1)S(1)} %collective-permute-done.21.refs_1_.refs_7_.refs_21_, ...), custom_call_target="tpu_custom_call" | custom-call | flops 3758096384 | bytes 9175040 | tf_op jit(solution)/shard_map/pallas_call | solution.py:178
  166.0 1.2 collective-permute-start.33
  167.3 1.7 collective-permute-start.34
  169.1 5.5 %shard_map.81 = bf16[512,3584]{1,0:T(8,128)(2,1)} custom-call(bf16[2,512,512]{2,1,0:T(8,128)(2,1)S(1)} %get-tuple-element.222.refs_0_.refs_2_, bf16[2,512,256]{2,1,0:T(8,128)(2,1)S(1)} %get-tuple-element.223.refs_1_.refs_3_, bf16[128,3584]{1,0:T(8,128)(2,1)S(1)} %collective-permute-done.17.refs_0_.refs_2_.refs_16_, ...), custom_call_target="tpu_custom_call" | custom-call | flops 2818572288 | bytes 13631488 | tf_op jit(solution)/shard_map/pallas_call | solution.py:256
  175.6 1.8 copy-done.34
  178.2 4.6 %shard_map.82 = (bf16[4,4,64,1024]{3,2,1,0:T(8,128)(2,1)}, f32[16,128]{1,0:T(8,128)}) custom-call(s32[12]{0:T(128)} %stack.88.idx_ref, bf16[4,64,256]{2,1,0:T(8,128)(2,1)} %copy-done.25, bf16[4,64,256]{2,1,0:T(8,128)(2,1)} %copy-done.35, bf16[4,64,256]{2,1,0:T(8,128)(2,1)} %copy-done.36, bf16[4,64,256]{2,1,0:T(8,128)(2,1)} %copy-done.37, ...), custom_call_target="tpu_custom_call" | custom-call | bytes 4194304 | tf_op jit(solution)/shard_map/pallas_call | solution.py:300
  184.9 2.4 %collective-permute-start.35 = (f32[4,128]{1,0:T(4,128)S(1)}, f32[4,128]{1,0:T(4,128)S(1)}, u32[]{:S(2)}, u32[]{:S(2)}) collective-permute-start(f32[4,128]{1,0:T(4,128)S(1)} %get-tuple-element.264), channel_id=1, source_target_pairs={{0,3},{1,0},{2,1},{3,2},{4,7},{5,4},{6,5},{7,6},{8,11},{9,8},{10,9... | collective-permute-start | bytes 6152 | tf_op jit(solution)/shard_map/ppermute | solution.py:340
  187.4 1.9 slice_bitcast_fusion
  189.3 2.8 %copy.13 = bf16[1,4,4,60,1024]{4,2,3,1,0:T(4,128)(2,1)} copy(bf16[1,4,4,60,1024]{4,3,1,2,0:T(8,128)(2,1)S(1)} %slice_bitcast_fusion) | data formatting | bytes 3932160
  192.8 15.3 %shard_map.83 = f32[128,4,3584]{2,1,0:T(4,128)} custom-call(bf16[2,512,512]{2,1,0:T(8,128)(2,1)} %copy-done.14, bf16[2,512,768]{2,1,0:T(8,128)(2,1)} %copy-done.13, bf16[2,512,512]{2,1,0:T(8,128)(2,1)} %copy-done.4, bf16[2,512,256]{2,1,0:T(8,128)(2,1)} %copy-done.10, bf16[512,3584]{1,0:T(8,128)(2,1)} %copy-done.34, ...), custom_call_target="tpu_custom_call" | custom-call | flops 7516192768 | bytes 24117248 | tf_op jit(solution)/shard_map/pallas_call | solution.py:256
  (169 shorter events, 22.5 us)
Async XLA Ops:
  0.6 29.1 %collective-permute-start.5 = (bf16[128,3584]{1,0:T(8,128)(2,1)}, bf16[128,3584]{1,0:T(8,128)(2,1)S(1)}, u32[]{:S(2)}, u32[]{:S(2)}) collective-permute-start(bf16[128,3584]{1,0:T(8,128)(2,1)} %refs_6_.1), channel_id=1, source_target_pairs={{0,1},{1,2},{2,3},{3,0},{4,5},{5,6},{6,7},{7,4},{8,9},{9,10},{10,1... | collective-permute-start | bytes 2752520 | tf_op jit(solution)/shard_map/ppermute | solution.py:340
  3.7 26.1 %collective-permute-start.4 = (bf16[128,3584]{1,0:T(8,128)(2,1)}, bf16[128,3584]{1,0:T(8,128)(2,1)S(1)}, u32[]{:S(2)}, u32[]{:S(2)}) collective-permute-start(bf16[128,3584]{1,0:T(8,128)(2,1)} %refs_6_.1), channel_id=1, source_target_pairs={{0,16},{4,20},{8,24},{12,28},{16,0},{20,4},{24,8},{28,12},{1,17},{... | collective-permute-start | bytes 2752520 | tf_op jit(solution)/shard_map/ppermute | solution.py:337
  5.2 24.5 %collective-permute-start.3 = (bf16[128,3584]{1,0:T(8,128)(2,1)}, bf16[128,3584]{1,0:T(8,128)(2,1)}, u32[]{:S(2)}, u32[]{:S(2)}) collective-permute-start(bf16[128,3584]{1,0:T(8,128)(2,1)} %refs_6_.1), channel_id=1, source_target_pairs={{0,8},{4,12},{8,0},{12,4},{16,24},{20,28},{24,16},{28,20},{1,9},{5... | collective-permute-start | bytes 2752520 | tf_op jit(solution)/shard_map/ppermute | solution.py:337
  8.8 16.0 %collective-permute-start.1 = (bf16[4,256]{1,0:T(4,128)(2,1)S(1)}, bf16[4,256]{1,0:T(4,128)(2,1)S(1)}, u32[]{:S(2)}, u32[]{:S(2)}) collective-permute-start(bf16[4,256]{1,0:T(4,128)(2,1)S(1)} %pad_maximum_fusion.5), channel_id=1, source_target_pairs={{0,2},{1,3},{2,0},{3,1},{4,6},{5,7},{6,4},{7,5},{8,10},{9,11},{10,... | collective-permute-start | bytes 6152 | tf_op jit(solution)/shard_map/ppermute | solution.py:340
  11.5 17.0 %collective-permute-start = (bf16[4,256]{1,0:T(4,128)(2,1)S(1)}, bf16[4,256]{1,0:T(4,128)(2,1)S(1)}, u32[]{:S(2)}, u32[]{:S(2)}) collective-permute-start(bf16[4,256]{1,0:T(4,128)(2,1)S(1)} %pad_maximum_fusion.5), channel_id=1, source_target_pairs={{0,1},{1,2},{2,3},{3,0},{4,5},{5,6},{6,7},{7,4},{8,9},{9,10},{10,1... | collective-permute-start | bytes 6152 | tf_op jit(solution)/shard_map/ppermute | solution.py:340
  24.8 30.2 %copy-start.15 = (bf16[128,3584]{1,0:T(8,128)(2,1)S(1)}, bf16[128,3584]{1,0:T(8,128)(2,1)}, u32[]{:S(2)}) copy-start(bf16[128,3584]{1,0:T(8,128)(2,1)} %refs_6_.1) | copy-start | bytes 2752516
  24.8 4.9 %collective-permute-start.2 = (bf16[4,256]{1,0:T(4,128)(2,1)S(1)}, bf16[4,256]{1,0:T(4,128)(2,1)S(1)}, u32[]{:S(2)}, u32[]{:S(2)}) collective-permute-start(bf16[4,256]{1,0:T(4,128)(2,1)S(1)} %pad_maximum_fusion.5), channel_id=1, source_target_pairs={{0,3},{1,0},{2,1},{3,2},{4,7},{5,4},{6,5},{7,6},{8,11},{9,8},{10,9... | collective-permute-start | bytes 6152 | tf_op jit(solution)/shard_map/ppermute | solution.py:340
  29.8 81.3 %copy-start.17 = (bf16[128,3584]{1,0:T(8,128)(2,1)}, bf16[128,3584]{1,0:T(8,128)(2,1)S(1)}, u32[]{:S(2)}) copy-start(bf16[128,3584]{1,0:T(8,128)(2,1)S(1)} %collective-permute-done.5.refs_0_.refs_6_.refs_10_) | copy-start | bytes 2752516
  29.8 75.1 %copy-start.19 = (bf16[128,3584]{1,0:T(8,128)(2,1)}, bf16[128,3584]{1,0:T(8,128)(2,1)S(1)}, u32[]{:S(2)}) copy-start(bf16[128,3584]{1,0:T(8,128)(2,1)S(1)} %collective-permute-done.4.refs_2_.refs_4_.refs_8_) | copy-start | bytes 2752516
  29.8 38.2 %collective-permute-start.13 = (bf16[512,3584]{1,0:T(8,128)(2,1)}, bf16[512,3584]{1,0:T(8,128)(2,1)}, u32[]{:S(2)}, u32[]{:S(2)}) collective-permute-start(bf16[512,3584]{1,0:T(8,128)(2,1)} %bitcast.25), channel_id=1, source_target_pairs={{0,4},{4,0},{8,12},{12,8},{16,20},{20,16},{24,28},{28,24},{1,5},{5... | collective-permute-start | bytes 11010056 | tf_op jit(solution)/shard_map/ppermute | solution.py:337
  29.9 25.2 %collective-permute-start.11 = (bf16[128,3584]{1,0:T(8,128)(2,1)S(1)}, bf16[128,3584]{1,0:T(8,128)(2,1)}, u32[]{:S(2)}, u32[]{:S(2)}) collective-permute-start(bf16[128,3584]{1,0:T(8,128)(2,1)S(1)} %collective-permute-done.5.refs_0_.refs_6_.refs_10_), channel_id=1, source_target_pairs={{0,1},{1,2},{2,3},{3,0},{4,5},{5,6},{6,7},{7,4},{8,9},{9,10},{10,1... | collective-permute-start | bytes 2752520 | tf_op jit(solution)/shard_map/ppermute | solution.py:340
  30.7 36.7 %collective-permute-start.6 = (bf16[128,3584]{1,0:T(8,128)(2,1)S(1)}, bf16[128,3584]{1,0:T(8,128)(2,1)S(1)}, u32[]{:S(2)}, u32[]{:S(2)}) collective-permute-start(bf16[128,3584]{1,0:T(8,128)(2,1)S(1)} %collective-permute-done.5.refs_0_.refs_6_.refs_10_), channel_id=1, source_target_pairs={{0,8},{4,12},{8,0},{12,4},{16,24},{20,28},{24,16},{28,20},{1,9},{5... | collective-permute-start | bytes 2752520 | tf_op jit(solution)/shard_map/ppermute | solution.py:337
  32.2 33.7 %collective-permute-start.9 = (bf16[128,3584]{1,0:T(8,128)(2,1)}, bf16[128,3584]{1,0:T(8,128)(2,1)}, u32[]{:S(2)}, u32[]{:S(2)}) collective-permute-start(bf16[128,3584]{1,0:T(8,128)(2,1)} %collective-permute-done.3.refs_1_.refs_3_.refs_7_), channel_id=1, source_target_pairs={{0,16},{4,20},{8,24},{12,28},{16,0},{20,4},{24,8},{28,12},{1,17},{... | collective-permute-start | bytes 2752520 | tf_op jit(solution)/shard_map/ppermute | solution.py:337
  36.3 29.1 %collective-permute-start.7 = (bf16[4,4,64,256]{3,2,1,0:T(8,128)(2,1)S(1)}, bf16[4,4,64,256]{3,2,1,0:T(8,128)(2,1)S(1)}, u32[]{:S(2)}, u32[]{:S(2)}) collective-permute-start(bf16[4,4,64,256]{3,2,1,0:T(8,128)(2,1)S(1)} %get-tuple-element.259), channel_id=1, source_target_pairs={{0,24},{4,28},{8,16},{12,20},{16,8},{20,12},{24,0},{28,4},{1,25},{... | collective-permute-start | bytes 1572872 | tf_op jit(solution)/shard_map/ppermute | solution.py:337
  55.1 25.7 %collective-permute-start.12 = (bf16[128,3584]{1,0:T(8,128)(2,1)S(1)}, bf16[128,3584]{1,0:T(8,128)(2,1)S(1)}, u32[]{:S(2)}, u32[]{:S(2)}) collective-permute-start(bf16[128,3584]{1,0:T(8,128)(2,1)S(1)} %copy-done.15), channel_id=1, source_target_pairs={{0,3},{1,0},{2,1},{3,2},{4,7},{5,4},{6,5},{7,6},{8,11},{9,8},{10,9... | collective-permute-start | bytes 2752520 | tf_op jit(solution)/shard_map/ppermute | solution.py:340
  65.9 12.6 %collective-permute-start.10 = (bf16[4,4,64,256]{3,2,1,0:T(8,128)(2,1)S(1)}, bf16[4,4,64,256]{3,2,1,0:T(8,128)(2,1)S(1)}, u32[]{:S(2)}, u32[]{:S(2)}) collective-permute-start(bf16[4,4,64,256]{3,2,1,0:T(8,128)(2,1)S(1)} %get-tuple-element.145), channel_id=1, source_target_pairs={{0,16},{4,20},{8,24},{12,28},{16,0},{20,4},{24,8},{28,12},{1,17},{... | collective-permute-start | bytes 1572872 | tf_op jit(solution)/shard_map/ppermute | solution.py:337
  67.4 12.6 %collective-permute-start.8 = (bf16[4,4,64,256]{3,2,1,0:T(8,128)(2,1)S(1)}, bf16[4,4,64,256]{3,2,1,0:T(8,128)(2,1)S(1)}, u32[]{:S(2)}, u32[]{:S(2)}) collective-permute-start(bf16[4,4,64,256]{3,2,1,0:T(8,128)(2,1)S(1)} %get-tuple-element.141), channel_id=1, source_target_pairs={{0,8},{4,12},{8,0},{12,4},{16,24},{20,28},{24,16},{28,20},{1,9},{5... | collective-permute-start | bytes 1572872 | tf_op jit(solution)/shard_map/ppermute | solution.py:337
  81.8 20.4 %collective-permute-start.15 = (bf16[128,3584]{1,0:T(8,128)(2,1)}, bf16[128,3584]{1,0:T(8,128)(2,1)}, u32[]{:S(2)}, u32[]{:S(2)}) collective-permute-start(bf16[128,3584]{1,0:T(8,128)(2,1)} %collective-permute-done.11.refs_3_.refs_9_.refs_13_), channel_id=1, source_target_pairs={{0,8},{4,12},{8,0},{12,4},{16,24},{20,28},{24,16},{28,20},{1,9},{5... | collective-permute-start | bytes 2752520 | tf_op jit(solution)/shard_map/ppermute | solution.py:337
  82.6 20.5 %collective-permute-start.14 = (bf16[128,3584]{1,0:T(8,128)(2,1)S(1)}, bf16[128,3584]{1,0:T(8,128)(2,1)}, u32[]{:S(2)}, u32[]{:S(2)}) collective-permute-start(bf16[128,3584]{1,0:T(8,128)(2,1)S(1)} %collective-permute-done.5.refs_0_.refs_6_.refs_10_), channel_id=1, source_target_pairs={{0,16},{4,20},{8,24},{12,28},{16,0},{20,4},{24,8},{28,12},{1,17},{... | collective-permute-start | bytes 2752520 | tf_op jit(solution)/shard_map/ppermute | solution.py:337
  83.5 21.3 %collective-permute-start.16 = (bf16[128,3584]{1,0:T(8,128)(2,1)}, bf16[128,3584]{1,0:T(8,128)(2,1)}, u32[]{:S(2)}, u32[]{:S(2)}) collective-permute-start(bf16[128,3584]{1,0:T(8,128)(2,1)} %collective-permute-done.3.refs_1_.refs_3_.refs_7_), channel_id=1, source_target_pairs={{0,3},{1,0},{2,1},{3,2},{4,7},{5,4},{6,5},{7,6},{8,11},{9,8},{10,9... | collective-permute-start | bytes 2752520 | tf_op jit(solution)/shard_map/ppermute | solution.py:340
  101.7 46.4 %copy-start.14 = (bf16[2,512,512]{2,1,0:T(8,128)(2,1)}, bf16[2,512,512]{2,1,0:T(8,128)(2,1)S(1)}, u32[]{:S(2)}) copy-start(bf16[2,512,512]{2,1,0:T(8,128)(2,1)S(1)} %get-tuple-element.204.refs_0_) | copy-start | bytes 3145732
  104.8 33.0 %copy-start.6 = (bf16[128,3584]{1,0:T(8,128)(2,1)S(1)}, bf16[128,3584]{1,0:T(8,128)(2,1)}, u32[]{:S(2)}) copy-start(bf16[128,3584]{1,0:T(8,128)(2,1)} %copy-done.5) | copy-start | bytes 2752516
  104.8 33.0 %copy-start.12 = (bf16[4,4,64,256]{3,2,1,0:T(8,128)(2,1)S(1)}, bf16[4,4,64,256]{3,2,1,0:T(8,128)(2,1)}, u32[]{:S(2)}) copy-start(bf16[4,4,64,256]{3,2,1,0:T(8,128)(2,1)} %copy-done.11) | copy-start | bytes 1572868
  104.8 20.9 %collective-permute-start.19 = (bf16[128,3584]{1,0:T(8,128)(2,1)S(1)}, bf16[128,3584]{1,0:T(8,128)(2,1)S(1)}, u32[]{:S(2)}, u32[]{:S(2)}) collective-permute-start(bf16[128,3584]{1,0:T(8,128)(2,1)S(1)} %collective-permute-done.4.refs_2_.refs_4_.refs_8_), channel_id=1, source_target_pairs={{0,3},{1,0},{2,1},{3,2},{4,7},{5,4},{6,5},{7,6},{8,11},{9,8},{10,9... | collective-permute-start | bytes 2752520 | tf_op jit(solution)/shard_map/ppermute | solution.py:340
  109.1 20.0 %collective-permute-start.17 = (bf16[128,3584]{1,0:T(8,128)(2,1)}, bf16[128,3584]{1,0:T(8,128)(2,1)S(1)}, u32[]{:S(2)}, u32[]{:S(2)}) collective-permute-start(bf16[128,3584]{1,0:T(8,128)(2,1)} %collective-permute-done.14.refs_2_.refs_8_.refs_12_), channel_id=1, source_target_pairs={{0,8},{4,12},{8,0},{12,4},{16,24},{20,28},{24,16},{28,20},{1,9},{5... | collective-permute-start | bytes 2752520 | tf_op jit(solution)/shard_map/ppermute | solution.py:337
  110.4 19.9 %collective-permute-start.18 = (bf16[128,3584]{1,0:T(8,128)(2,1)}, bf16[128,3584]{1,0:T(8,128)(2,1)S(1)}, u32[]{:S(2)}, u32[]{:S(2)}) collective-permute-start(bf16[128,3584]{1,0:T(8,128)(2,1)} %collective-permute-done.11.refs_3_.refs_9_.refs_13_), channel_id=1, source_target_pairs={{0,16},{4,20},{8,24},{12,28},{16,0},{20,4},{24,8},{28,12},{1,17},{... | collective-permute-start | bytes 2752520 | tf_op jit(solution)/shard_map/ppermute | solution.py:337
  125.8 43.3 %copy-start.7 = (bf16[128,3584]{1,0:T(8,128)(2,1)}, bf16[128,3584]{1,0:T(8,128)(2,1)S(1)}, u32[]{:S(2)}) copy-start(bf16[128,3584]{1,0:T(8,128)(2,1)S(1)} %collective-permute-done.19.refs_3_.refs_5_.refs_19_) | copy-start | bytes 2752516
  129.1 40.0 %copy-start.8 = (bf16[128,3584]{1,0:T(8,128)(2,1)}, bf16[128,3584]{1,0:T(8,128)(2,1)S(1)}, u32[]{:S(2)}) copy-start(bf16[128,3584]{1,0:T(8,128)(2,1)S(1)} %collective-permute-done.17.refs_0_.refs_2_.refs_16_) | copy-start | bytes 2752516
  130.4 38.7 %copy-start.9 = (bf16[128,3584]{1,0:T(8,128)(2,1)}, bf16[128,3584]{1,0:T(8,128)(2,1)S(1)}, u32[]{:S(2)}) copy-start(bf16[128,3584]{1,0:T(8,128)(2,1)S(1)} %collective-permute-done.18.refs_1_.refs_3_.refs_17_) | copy-start | bytes 2752516
  130.4 7.5 %collective-permute-start.22 = (bf16[4,64,256]{2,1,0:T(8,128)(2,1)S(1)}, bf16[4,64,256]{2,1,0:T(8,128)(2,1)S(1)}, u32[]{:S(2)}, u32[]{:S(2)}) collective-permute-start(bf16[4,64,256]{2,1,0:T(8,128)(2,1)S(1)} %get-tuple-element.186), channel_id=1, source_target_pairs={{0,8},{4,12},{8,0},{12,4},{16,24},{20,28},{24,16},{28,20},{1,9},{5... | collective-permute-start | bytes 393224 | tf_op jit(solution)/shard_map/ppermute | solution.py:337
  131.8 14.2 %collective-permute-start.23 = (bf16[4,64,256]{2,1,0:T(8,128)(2,1)S(1)}, bf16[4,64,256]{2,1,0:T(8,128)(2,1)S(1)}, u32[]{:S(2)}, u32[]{:S(2)}) collective-permute-start(bf16[4,64,256]{2,1,0:T(8,128)(2,1)S(1)} %get-tuple-element.187), channel_id=1, source_target_pairs={{0,16},{4,20},{8,24},{12,28},{16,0},{20,4},{24,8},{28,12},{1,17},{... | collective-permute-start | bytes 393224 | tf_op jit(solution)/shard_map/ppermute | solution.py:337
  134.3 11.7 %collective-permute-start.24 = (bf16[4,64,256]{2,1,0:T(8,128)(2,1)S(1)}, bf16[4,64,256]{2,1,0:T(8,128)(2,1)S(1)}, u32[]{:S(2)}, u32[]{:S(2)}) collective-permute-start(bf16[4,64,256]{2,1,0:T(8,128)(2,1)S(1)} %get-tuple-element.188), channel_id=1, source_target_pairs={{0,24},{4,28},{8,16},{12,20},{16,8},{20,12},{24,0},{28,4},{1,25},{... | collective-permute-start | bytes 393224 | tf_op jit(solution)/shard_map/ppermute | solution.py:337
  134.4 13.1 %collective-permute-start.25 = (bf16[4,64,256]{2,1,0:T(8,128)(2,1)S(1)}, bf16[4,64,256]{2,1,0:T(8,128)(2,1)S(1)}, u32[]{:S(2)}, u32[]{:S(2)}) collective-permute-start(bf16[4,64,256]{2,1,0:T(8,128)(2,1)S(1)} %get-tuple-element.190), channel_id=1, source_target_pairs={{0,8},{4,12},{8,0},{12,4},{16,24},{20,28},{24,16},{28,20},{1,9},{5... | collective-permute-start | bytes 393224 | tf_op jit(solution)/shard_map/ppermute | solution.py:337
  135.8 21.6 %collective-permute-start.20 = (bf16[128,3584]{1,0:T(8,128)(2,1)}, bf16[128,3584]{1,0:T(8,128)(2,1)S(1)}, u32[]{:S(2)}, u32[]{:S(2)}) collective-permute-start(bf16[128,3584]{1,0:T(8,128)(2,1)} %collective-permute-done.15.refs_4_.refs_10_.refs_14_), channel_id=1, source_target_pairs={{0,16},{4,20},{8,24},{12,28},{16,0},{20,4},{24,8},{28,12},{1,17},{... | collective-permute-start | bytes 2752520 | tf_op jit(solution)/shard_map/ppermute | solution.py:337
  137.8 19.6 %collective-permute-start.21 = (bf16[128,3584]{1,0:T(8,128)(2,1)}, bf16[128,3584]{1,0:T(8,128)(2,1)S(1)}, u32[]{:S(2)}, u32[]{:S(2)}) collective-permute-start(bf16[128,3584]{1,0:T(8,128)(2,1)} %collective-permute-done.9.refs_3_.refs_5_.refs_9_), channel_id=1, source_target_pairs={{0,3},{1,0},{2,1},{3,2},{4,7},{5,4},{6,5},{7,6},{8,11},{9,8},{10,9... | collective-permute-start | bytes 2752520 | tf_op jit(solution)/shard_map/ppermute | solution.py:340
  146.0 11.4 %collective-permute-start.26 = (bf16[4,64,256]{2,1,0:T(8,128)(2,1)S(1)}, bf16[4,64,256]{2,1,0:T(8,128)(2,1)S(1)}, u32[]{:S(2)}, u32[]{:S(2)}) collective-permute-start(bf16[4,64,256]{2,1,0:T(8,128)(2,1)S(1)} %get-tuple-element.191), channel_id=1, source_target_pairs={{0,16},{4,20},{8,24},{12,28},{16,0},{20,4},{24,8},{28,12},{1,17},{... | collective-permute-start | bytes 393224 | tf_op jit(solution)/shard_map/ppermute | solution.py:337
  146.1 11.3 %collective-permute-start.27 = (bf16[4,64,256]{2,1,0:T(8,128)(2,1)S(1)}, bf16[4,64,256]{2,1,0:T(8,128)(2,1)S(1)}, u32[]{:S(2)}, u32[]{:S(2)}) collective-permute-start(bf16[4,64,256]{2,1,0:T(8,128)(2,1)S(1)} %get-tuple-element.193), channel_id=1, source_target_pairs={{0,8},{4,12},{8,0},{12,4},{16,24},{20,28},{24,16},{28,20},{1,9},{5... | collective-permute-start | bytes 393224 | tf_op jit(solution)/shard_map/ppermute | solution.py:337
  147.5 9.9 %collective-permute-start.28 = (bf16[4,64,256]{2,1,0:T(8,128)(2,1)S(1)}, bf16[4,64,256]{2,1,0:T(8,128)(2,1)S(1)}, u32[]{:S(2)}, u32[]{:S(2)}) collective-permute-start(bf16[4,64,256]{2,1,0:T(8,128)(2,1)S(1)} %get-tuple-element.194), channel_id=1, source_target_pairs={{0,8},{4,12},{8,0},{12,4},{16,24},{20,28},{24,16},{28,20},{1,9},{5... | collective-permute-start | bytes 393224 | tf_op jit(solution)/shard_map/ppermute | solution.py:337
  157.4 18.2 %collective-permute-start.29 = (bf16[512,3584]{1,0:T(8,128)(2,1)S(1)}, bf16[512,3584]{1,0:T(8,128)(2,1)S(1)}, u32[]{:S(2)}, u32[]{:S(2)}) collective-permute-start(bf16[512,3584]{1,0:T(8,128)(2,1)S(1)} %shard_map.79), channel_id=1, source_target_pairs={{0,4},{4,0},{8,12},{12,8},{16,20},{20,16},{24,28},{28,24},{1,5},{5... | collective-permute-start | bytes 11010056 | tf_op jit(solution)/shard_map/ppermute | solution.py:337
  157.5 9.8 %collective-permute-start.30 = (bf16[4,64,256]{2,1,0:T(8,128)(2,1)S(1)}, bf16[4,64,256]{2,1,0:T(8,128)(2,1)S(1)}, u32[]{:S(2)}, u32[]{:S(2)}) collective-permute-start(bf16[4,64,256]{2,1,0:T(8,128)(2,1)S(1)} %get-tuple-element.214), channel_id=1, source_target_pairs={{0,24},{4,28},{8,16},{12,20},{16,8},{20,12},{24,0},{28,4},{1,25},{... | collective-permute-start | bytes 393224 | tf_op jit(solution)/shard_map/ppermute | solution.py:337
  159.3 15.2 %collective-permute-start.31 = (bf16[4,64,256]{2,1,0:T(8,128)(2,1)S(1)}, bf16[4,64,256]{2,1,0:T(8,128)(2,1)S(1)}, u32[]{:S(2)}, u32[]{:S(2)}) collective-permute-start(bf16[4,64,256]{2,1,0:T(8,128)(2,1)S(1)} %get-tuple-element.215), channel_id=1, source_target_pairs={{0,16},{4,20},{8,24},{12,28},{16,0},{20,4},{24,8},{28,12},{1,17},{... | collective-permute-start | bytes 393224 | tf_op jit(solution)/shard_map/ppermute | solution.py:337
  159.7 15.9 %collective-permute-start.32 = (bf16[4,64,256]{2,1,0:T(8,128)(2,1)S(1)}, bf16[4,64,256]{2,1,0:T(8,128)(2,1)S(1)}, u32[]{:S(2)}, u32[]{:S(2)}) collective-permute-start(bf16[4,64,256]{2,1,0:T(8,128)(2,1)S(1)} %get-tuple-element.217), channel_id=1, source_target_pairs={{0,16},{4,20},{8,24},{12,28},{16,0},{20,4},{24,8},{28,12},{1,17},{... | collective-permute-start | bytes 393224 | tf_op jit(solution)/shard_map/ppermute | solution.py:337
  166.0 9.5 %collective-permute-start.33 = (bf16[4,64,256]{2,1,0:T(8,128)(2,1)S(1)}, bf16[4,64,256]{2,1,0:T(8,128)(2,1)S(1)}, u32[]{:S(2)}, u32[]{:S(2)}) collective-permute-start(bf16[4,64,256]{2,1,0:T(8,128)(2,1)S(1)} %get-tuple-element.220), channel_id=1, source_target_pairs={{0,24},{4,28},{8,16},{12,20},{16,8},{20,12},{24,0},{28,4},{1,25},{... | collective-permute-start | bytes 393224 | tf_op jit(solution)/shard_map/ppermute | solution.py:337
  167.3 8.3 %collective-permute-start.34 = (bf16[4,64,256]{2,1,0:T(8,128)(2,1)S(1)}, bf16[4,64,256]{2,1,0:T(8,128)(2,1)S(1)}, u32[]{:S(2)}, u32[]{:S(2)}) collective-permute-start(bf16[4,64,256]{2,1,0:T(8,128)(2,1)S(1)} %get-tuple-element.221), channel_id=1, source_target_pairs={{0,24},{4,28},{8,16},{12,20},{16,8},{20,12},{24,0},{28,4},{1,25},{... | collective-permute-start | bytes 393224 | tf_op jit(solution)/shard_map/ppermute | solution.py:337
  177.4 15.4 %collective-permute-start.38 = (bf16[512,3584]{1,0:T(8,128)(2,1)}, bf16[512,3584]{1,0:T(8,128)(2,1)}, u32[]{:S(2)}, u32[]{:S(2)}) collective-permute-start(bf16[512,3584]{1,0:T(8,128)(2,1)} %shard_map.81), channel_id=1, source_target_pairs={{0,4},{4,0},{8,12},{12,8},{16,20},{20,16},{24,28},{28,24},{1,5},{5... | collective-permute-start | bytes 11010056 | tf_op jit(solution)/shard_map/ppermute | solution.py:337
  183.5 8.5 %collective-permute-start.37 = (f32[4,128]{1,0:T(4,128)S(1)}, f32[4,128]{1,0:T(4,128)S(1)}, u32[]{:S(2)}, u32[]{:S(2)}) collective-permute-start(f32[4,128]{1,0:T(4,128)S(1)} %get-tuple-element.262), channel_id=1, source_target_pairs={{0,1},{1,2},{2,3},{3,0},{4,5},{5,6},{6,7},{7,4},{8,9},{9,10},{10,1... | collective-permute-start | bytes 6152 | tf_op jit(solution)/shard_map/ppermute | solution.py:340
  184.6 7.4 %collective-permute-start.36 = (f32[4,128]{1,0:T(4,128)S(1)}, f32[4,128]{1,0:T(4,128)S(1)}, u32[]{:S(2)}, u32[]{:S(2)}) collective-permute-start(f32[4,128]{1,0:T(4,128)S(1)} %get-tuple-element.263), channel_id=1, source_target_pairs={{0,2},{1,3},{2,0},{3,1},{4,6},{5,7},{6,4},{7,5},{8,10},{9,11},{10,... | collective-permute-start | bytes 6152 | tf_op jit(solution)/shard_map/ppermute | solution.py:340
  184.9 7.1 %collective-permute-start.35 = (f32[4,128]{1,0:T(4,128)S(1)}, f32[4,128]{1,0:T(4,128)S(1)}, u32[]{:S(2)}, u32[]{:S(2)}) collective-permute-start(f32[4,128]{1,0:T(4,128)S(1)} %get-tuple-element.264), channel_id=1, source_target_pairs={{0,3},{1,0},{2,1},{3,2},{4,7},{5,4},{6,5},{7,6},{8,11},{9,8},{10,9... | collective-permute-start | bytes 6152 | tf_op jit(solution)/shard_map/ppermute | solution.py:340
  (42 other events, 403.8 us)

commit v15 on v14

--- a/solution.py
+++ b/solution.py
@@ -444,7 +444,7 @@
     route_grad = ROUTE_SCALE * route_grad.T
     affinity_grad = (route_grad - jnp.sum(route_grad * shares, axis=-1, keepdims=True)) / totals
     scatters = [scatter0, scatter1, scatter2, scatter3]
-    down_grad = half_grad(mine, scatters, first + late, [partner, later], experts, 896, True)
+    down_grad = half_grad(mine, scatters, first + late, [partner, later], experts, 512, True)
     return (affinity_grad, hidden_grad, down_grad)
 
 

time: 209 us -> 209 us (level)
  no operation moved by 1% of the time
where the time goes in v15:
time: 209 us; the launch traced here: 208 us
  Pallas kernels  66.3 us (32%)
  starting transfers between devices  52.6 us (25%)
  waiting for transfers between devices  45.2 us (22%)
  local copies, waits for them, and re-layouts  30.9 us (15%)
  other arithmetic  12.2 us (6%)
    pallas_call x4, Pallas kernels, project(): pl.pallas_call(functools.partial(project_kernel, top_k, sizes, len(items)...  32.5 us
    pallas_call x3, Pallas kernels, half_grad(): pl.pallas_call(functools.partial(half_grad_kernel, len(scatters), len(arr...  29.2 us
    ppermute x27, starting transfers between devices, across(): return lax.ppermute(array, 'rep', [(i, i ^ bits) for i in range(reps)])  28.9 us
    ppermute x12, waiting for transfers between devices, around(): lax.ppermute(array, 'exp', [(i, (i + shift) % sources) for i in range(sou...  23.8 us
    ppermute x12, starting transfers between devices, around(): lax.ppermute(array, 'exp', [(i, (i + shift) % sources) for i in range(sou...  23.7 us
    ppermute x27, waiting for transfers between devices, across(): return lax.ppermute(array, 'rep', [(i, i ^ bits) for i in range(reps)])  21.4 us
    unnamed x109, local copies, waits for them, and re-layouts  14.3 us
    reshape x2, local copies, waits for them, and re-layouts, on_device_tokens(): saved_hidden.reshape(experts, sources, most, 8, block)  7.92 us
  transfers between devices with their start and end apart: 39, of which 14 were waited for; matrix products, arithmetic and copies ran while one was open for 15% of the time, Pallas kernels for 24%

profile of v15, /device:TPU:0, one launch (start us, length us, event | category | flops | bytes accessed | tf_op | source)
XLA Modules:
  0.0 208.5 jit_solution(2050194129606651237)
XLA Ops:
  0.6 3.1 %collective-permute-start.5 = (bf16[128,3584]{1,0:T(8,128)(2,1)}, bf16[128,3584]{1,0:T(8,128)(2,1)S(1)}, u32[]{:S(2)}, u32[]{:S(2)}) collective-permute-start(bf16[128,3584]{1,0:T(8,128)(2,1)} %refs_6_.1), channel_id=1, source_target_pairs={{0,1},{1,2},{2,3},{3,0},{4,5},{5,6},{6,7},{7,4},{8,9},{9,10},{10,1... | collective-permute-start | bytes 2752520 | tf_op jit(solution)/shard_map/ppermute | solution.py:340
  3.7 1.5 collective-permute-start.4
  5.2 1.5 collective-permute-start.3
  8.8 2.7 %collective-permute-start.1 = (bf16[4,256]{1,0:T(4,128)(2,1)S(1)}, bf16[4,256]{1,0:T(4,128)(2,1)S(1)}, u32[]{:S(2)}, u32[]{:S(2)}) collective-permute-start(bf16[4,256]{1,0:T(4,128)(2,1)S(1)} %pad_maximum_fusion.5), channel_id=1, source_target_pairs={{0,2},{1,3},{2,0},{3,1},{4,6},{5,7},{6,4},{7,5},{8,10},{9,11},{10,... | collective-permute-start | bytes 6152 | tf_op jit(solution)/shard_map/ppermute | solution.py:340
  11.7 4.3 %reshape.47 = bf16[4,4,60,8,128]{4,3,1,2,0:T(8,128)(2,1)} reshape(bf16[1,4,4,60,1024]{4,2,3,1,0:T(4,128)(2,1)} %param.8) | data formatting | bytes 3932160 | tf_op jit(solution)/shard_map/reshape | solution.py:359
  16.0 3.6 %copy.15 = bf16[4,4,60,8,128]{4,2,1,0,3:T(8,128)(2,1)} copy(bf16[4,4,60,8,128]{4,3,1,2,0:T(8,128)(2,1)} %reshape.47) | data formatting | bytes 3932160 | tf_op jit(solution)/shard_map/reshape | solution.py:359
  19.6 2.8 %dynamic-slice_bitcast_fusion = (bf16[4,4,60,128]{3,2,1,0:T(8,128)(2,1)S(1)}, bf16[4,4,60,128]{3,2,1,0:T(8,128)(2,1)S(1)}, bf16[4,4,60,128]{3,2,1,0:T(8,128)(2,1...) fusion(bf16[8,4,4,60,128]{4,3,2,1,0:T(8,128)(2,1)} %bitcast.65,, ...), kind=kLoop, calls=%fused_computation.7 | loop fusion | bytes 3932192 | tf_op jit(solution)/shard_map/jit(dynamic_index_in_dim)/squeeze | solution.py:361
  22.4 2.4 %copy.12 = bf16[4,128,3584]{2,1,0:T(8,128)(2,1)} copy(bf16[4,128,3584]{2,0,1:T(4,128)(2,1)S(1)} %bitcast.66) | data formatting | bytes 7340032 | tf_op jit(solution)/shard_map/transpose | solution.py:362
  24.8 3.6 %collective-permute-start.2 = (bf16[4,256]{1,0:T(4,128)(2,1)S(1)}, bf16[4,256]{1,0:T(4,128)(2,1)S(1)}, u32[]{:S(2)}, u32[]{:S(2)}) collective-permute-start(bf16[4,256]{1,0:T(4,128)(2,1)S(1)} %pad_maximum_fusion.5), channel_id=1, source_target_pairs={{0,3},{1,0},{2,1},{3,2},{4,7},{5,4},{6,5},{7,6},{8,11},{9,8},{10,9... | collective-permute-start | bytes 6152 | tf_op jit(solution)/shard_map/ppermute | solution.py:340
  28.4 1.3 collective-permute-done.2
  30.7 1.5 collective-permute-start.6
  32.2 1.5 collective-permute-start.9
  33.9 2.5 %pad_maximum_fusion.1 = (bf16[4,4,64,256]{3,2,1,0:T(8,128)(2,1)S(1)}, bf16[4,4,64,256]{3,2,1,0:T(8,128)(2,1)S(1)}, bf16[4,4,64,256]{3,2,1,0:T(8,128)(2,1)S(1)}, bf16[4,4,64,256]{3,2,1,0:T(8,128)(2,1)}) fusion(bf16[4,4,4,256]{3,2,1,0:T(4,128)(2,1)S(1)} %broadcast_in_dim.49, bf16[4,4,60,128]{3,2,1,0:T(8,128)(2,1)S(1)} %get-tuple-element.143, ...), kind=kLoop, calls=%fused_computation.3 | loop fusion | flops 5505024 | bytes 4096000 | tf_op jit(solution)/shard_map/concatenate | solution.py:377
  36.8 18.2 %collective-permute-done.11.refs_3_.refs_9_.refs_13_ = bf16[128,3584]{1,0:T(8,128)(2,1)} collective-permute-done((bf16[128,3584]{1,0:T(8,128)(2,1)S(1)}, bf16[128,3584]{1,0:T(8,128)(2,1)}, u32[]{:S(2)}, u32[]{:S(2)}) %collective-permute-start.11) | collective-permute-done | bytes 917536 | tf_op jit(solution)/shard_map/ppermute | solution.py:340
  55.1 1.7 collective-permute-start.12
  56.8 8.6 %collective-permute-done.7.refs_9_.refs_6_.refs_4_.refs_5_ = bf16[4,4,64,256]{3,2,1,0:T(8,128)(2,1)S(1)} collective-permute-done((bf16[4,4,64,256]{3,2,1,0:T(8,128)(2,1)S(1)}, bf16[4,4,64,256]{3,2,1,0:T(8,128)(2,1)S(1)}, u32[]{:S(2)}, u32[]{:S(2)}) %collective-permute-start.7) | collective-permute-done | bytes 524320 | tf_op jit(solution)/shard_map/ppermute | solution.py:337
  65.9 1.5 collective-permute-start.10
  68.0 6.9 %pad_maximum_fusion.refs_4_.refs_5_.refs_6_.refs_7_.refs_2_.refs_3_ = bf16[2,512,3584]{2,1,0:T(8,128)(2,1)} fusion(bf16[1,512,3584]{2,1,0:T(8,128)(2,1)} %bitcast.31, bf16[1,512,3584]{2,1,0:T(8,128)(2,1)} %bitcast.30), kind=kLoop, calls=%fused_computation | loop fusion | flops 3670016 | bytes 14680064 | tf_op jit(solution)/shard_map/stack | solution.py:385
  74.8 3.7 %collective-permute-done.10.refs_8_.refs_10_.refs_7_.refs_9_ = bf16[4,4,64,256]{3,2,1,0:T(8,128)(2,1)S(1)} collective-permute-done((bf16[4,4,64,256]{3,2,1,0:T(8,128)(2,1)S(1)}, bf16[4,4,64,256]{3,2,1,0:T(8,128)(2,1)S(1)}, u32[]{:S(2)}, u32[]{:S(2)}) %collective-permute-start.10) | collective-permute-done | bytes 524320 | tf_op jit(solution)/shard_map/ppermute | solution.py:337
  83.5 3.4 %collective-permute-start.16 = (bf16[128,3584]{1,0:T(8,128)(2,1)}, bf16[128,3584]{1,0:T(8,128)(2,1)}, u32[]{:S(2)}, u32[]{:S(2)}) collective-permute-start(bf16[128,3584]{1,0:T(8,128)(2,1)} %collective-permute-done.3.refs_1_.refs_3_.refs_7_), channel_id=1, source_target_pairs={{0,3},{1,0},{2,1},{3,2},{4,7},{5,4},{6,5},{7,6},{8,11},{9,8},{10,9... | collective-permute-start | bytes 2752520 | tf_op jit(solution)/shard_map/ppermute | solution.py:340
  87.0 3.1 %copy-done = bf16[2,512,3584]{2,1,0:T(8,128)(2,1)S(1)} copy-done((bf16[2,512,3584]{2,1,0:T(8,128)(2,1)S(1)}, bf16[2,512,3584]{2,1,0:T(8,128)(2,1)}, u32[]{:S(2)}) %copy-start) | copy-done | bytes 7340056
  93.3 8.4 %shard_map.76 = (bf16[4,64,256]{2,1,0:T(8,128)(2,1)S(1)}, bf16[4,64,256]{2,1,0:T(8,128)(2,1)S(1)}, bf16[4,64,256]{2,1,0:T(8,128)(2,1)S(1)}, bf16[4,64,256]{2,1,0:T(8,128)(2,1)S(1)}, bf16[2,512,512]{2,1,0:T(8,128)(2,1)S(1)}) custom-call(s32[5]{0:T(128)S(1)} %stack.98.idx_ref, bf16[128,3584]{1,0:T(8,128)(2,1)S(1)} %copy-done.15, ...), custom_call_target="tpu_custom_call" | custom-call | flops 7516192768 | bytes 11010048 | tf_op jit(solution)/shard_map/pallas_call | solution.py:178
  103.1 1.8 collective-permute-done.16.refs_5_.refs_11_.refs_15_
  104.8 4.3 %collective-permute-start.19 = (bf16[128,3584]{1,0:T(8,128)(2,1)S(1)}, bf16[128,3584]{1,0:T(8,128)(2,1)S(1)}, u32[]{:S(2)}, u32[]{:S(2)}) collective-permute-start(bf16[128,3584]{1,0:T(8,128)(2,1)S(1)} %collective-permute-done.4.refs_2_.refs_4_.refs_8_), channel_id=1, source_target_pairs={{0,3},{1,0},{2,1},{3,2},{4,7},{5,4},{6,5},{7,6},{8,11},{9,8},{10,9... | collective-permute-start | bytes 2752520 | tf_op jit(solution)/shard_map/ppermute | solution.py:340
  109.1 1.3 collective-permute-start.17
  111.1 12.1 %shard_map.77 = (bf16[4,64,256]{2,1,0:T(8,128)(2,1)S(1)}, bf16[4,64,256]{2,1,0:T(8,128)(2,1)S(1)}, bf16[4,64,256]{2,1,0:T(8,128)(2,1)S(1)}, bf16[4,64,256]{2,1,0...) custom-call(s32[5]{0:T(128)S(1)} %stack.98.idx_ref, ...), custom_call_target="tpu_custom_call" | custom-call | flops 11274289152 | bytes 12845056 | tf_op jit(solution)/shard_map/pallas_call | solution.py:178
  123.2 2.5 %collective-permute-done.19.refs_3_.refs_5_.refs_19_ = bf16[128,3584]{1,0:T(8,128)(2,1)S(1)} collective-permute-done((bf16[128,3584]{1,0:T(8,128)(2,1)S(1)}, bf16[128,3584]{1,0:T(8,128)(2,1)S(1)}, u32[]{:S(2)}, u32[]{:S(2)}) %collective-permute-start.19) | collective-permute-done | bytes 917536 | tf_op jit(solution)/shard_map/ppermute | solution.py:340
  125.8 3.3 %collective-permute-done.17.refs_0_.refs_2_.refs_16_ = bf16[128,3584]{1,0:T(8,128)(2,1)S(1)} collective-permute-done((bf16[128,3584]{1,0:T(8,128)(2,1)}, bf16[128,3584]{1,0:T(8,128)(2,1)S(1)}, u32[]{:S(2)}, u32[]{:S(2)}) %collective-permute-start.17) | collective-permute-done | bytes 917536 | tf_op jit(solution)/shard_map/ppermute | solution.py:337
  129.1 1.3 collective-permute-done.18.refs_1_.refs_3_.refs_17_
  130.4 1.4 collective-permute-start.22
  131.8 2.5 %collective-permute-start.23 = (bf16[4,64,256]{2,1,0:T(8,128)(2,1)S(1)}, bf16[4,64,256]{2,1,0:T(8,128)(2,1)S(1)}, u32[]{:S(2)}, u32[]{:S(2)}) collective-permute-start(bf16[4,64,256]{2,1,0:T(8,128)(2,1)S(1)} %get-tuple-element.187), channel_id=1, source_target_pairs={{0,16},{4,20},{8,24},{12,28},{16,0},{20,4},{24,8},{28,12},{1,17},{... | collective-permute-start | bytes 393224 | tf_op jit(solution)/shard_map/ppermute | solution.py:337
  134.4 1.5 collective-permute-start.25
  135.8 2.0 collective-permute-start.20
  137.9 7.4 %shard_map.78 = (bf16[4,64,256]{2,1,0:T(8,128)(2,1)S(1)}, bf16[4,64,256]{2,1,0:T(8,128)(2,1)S(1)}, bf16[4,64,256]{2,1,0:T(8,128)(2,1)S(1)}, bf16[4,64,256]{2,1,0:T(8,128)(2,1)S(1)}, bf16[2,512,512]{2,1,0:T(8,128)(2,1)S(1)}) custom-call(s32[5]{0:T(128)S(1)} %stack.98.idx_ref, bf16[128,3584]{1,0:T(8,128)(2,1)S(1)} %collective-permute-done.17.refs_0_.refs_2_.refs_16_, ...), custom_call_target="tpu_custom_call" | custom-call | flops 7516192768 | bytes 11010048 | tf_op jit(solution)/shard_map/pallas_call | solution.py:178
  146.1 1.4 collective-permute-start.27
  148.1 8.3 %shard_map.79 = bf16[512,3584]{1,0:T(8,128)(2,1)S(1)} custom-call(bf16[2,512,512]{2,1,0:T(8,128)(2,1)S(1)} %get-tuple-element.204.refs_0_, bf16[2,512,768]{2,1,0:T(8,128)(2,1)S(1)} %get-tuple-element.205.refs_1_, bf16[128,3584]{1,0:T(8,128)(2,1)S(1)} %copy-done.16, bf16[128,3584]{1,0:T(8,128)(2,1)} %collective-permute-done.3.refs_1_.refs_3_.refs_7_, ...), custom_call_target="tpu_custom_call" | custom-call | flops 4697620480 | bytes 17825792 | tf_op jit(solution)/shard_map/pallas_call | solution.py:256
  157.5 1.8 collective-permute-start.30
  159.7 1.7 collective-permute-start.32
  161.3 4.7 %shard_map.80 = (bf16[4,64,256]{2,1,0:T(8,128)(2,1)S(1)}, bf16[4,64,256]{2,1,0:T(8,128)(2,1)S(1)}, bf16[2,512,256]{2,1,0:T(8,128)(2,1)S(1)}) custom-call(s32[5]{0:T(128)S(1)} %stack.98.idx_ref, bf16[128,3584]{1,0:T(8,128)(2,1)S(1)} %collective-permute-done.20.refs_0_.refs_6_.refs_20_, bf16[128,3584]{1,0:T(8,128)(2,1)S(1)} %collective-permute-done.21.refs_1_.refs_7_.refs_21_, ...), custom_call_target="tpu_custom_call" | custom-call | flops 3758096384 | bytes 9175040 | tf_op jit(solution)/shard_map/pallas_call | solution.py:178
  166.0 1.2 collective-permute-start.33
  167.3 1.7 collective-permute-start.34
  169.1 5.5 %shard_map.81 = bf16[512,3584]{1,0:T(8,128)(2,1)} custom-call(bf16[2,512,512]{2,1,0:T(8,128)(2,1)S(1)} %get-tuple-element.222.refs_0_.refs_2_, bf16[2,512,256]{2,1,0:T(8,128)(2,1)S(1)} %get-tuple-element.223.refs_1_.refs_3_, bf16[128,3584]{1,0:T(8,128)(2,1)S(1)} %collective-permute-done.17.refs_0_.refs_2_.refs_16_, ...), custom_call_target="tpu_custom_call" | custom-call | flops 2818572288 | bytes 13631488 | tf_op jit(solution)/shard_map/pallas_call | solution.py:256
  175.6 1.8 copy-done.34
  178.2 4.6 %shard_map.82 = (bf16[4,4,64,1024]{3,2,1,0:T(8,128)(2,1)}, f32[16,128]{1,0:T(8,128)}) custom-call(s32[12]{0:T(128)} %stack.88.idx_ref, bf16[4,64,256]{2,1,0:T(8,128)(2,1)} %copy-done.25, bf16[4,64,256]{2,1,0:T(8,128)(2,1)} %copy-done.35, bf16[4,64,256]{2,1,0:T(8,128)(2,1)} %copy-done.36, bf16[4,64,256]{2,1,0:T(8,128)(2,1)} %copy-done.37, ...), custom_call_target="tpu_custom_call" | custom-call | bytes 4194304 | tf_op jit(solution)/shard_map/pallas_call | solution.py:300
  184.9 2.4 %collective-permute-start.35 = (f32[4,128]{1,0:T(4,128)S(1)}, f32[4,128]{1,0:T(4,128)S(1)}, u32[]{:S(2)}, u32[]{:S(2)}) collective-permute-start(f32[4,128]{1,0:T(4,128)S(1)} %get-tuple-element.264), channel_id=1, source_target_pairs={{0,3},{1,0},{2,1},{3,2},{4,7},{5,4},{6,5},{7,6},{8,11},{9,8},{10,9... | collective-permute-start | bytes 6152 | tf_op jit(solution)/shard_map/ppermute | solution.py:340
  187.4 1.9 slice_bitcast_fusion
  189.3 2.8 %copy.13 = bf16[1,4,4,60,1024]{4,2,3,1,0:T(4,128)(2,1)} copy(bf16[1,4,4,60,1024]{4,3,1,2,0:T(8,128)(2,1)S(1)} %slice_bitcast_fusion) | data formatting | bytes 3932160
  192.8 15.5 %shard_map.83 = f32[128,4,3584]{2,1,0:T(4,128)} custom-call(bf16[2,512,512]{2,1,0:T(8,128)(2,1)} %copy-done.14, bf16[2,512,768]{2,1,0:T(8,128)(2,1)} %copy-done.13, bf16[2,512,512]{2,1,0:T(8,128)(2,1)} %copy-done.4, bf16[2,512,256]{2,1,0:T(8,128)(2,1)} %copy-done.10, bf16[512,3584]{1,0:T(8,128)(2,1)} %copy-done.34, ...), custom_call_target="tpu_custom_call" | custom-call | flops 7516192768 | bytes 24117248 | tf_op jit(solution)/shard_map/pallas_call | solution.py:256
  (169 shorter events, 22.5 us)
Async XLA Ops:
  0.6 29.1 %collective-permute-start.5 = (bf16[128,3584]{1,0:T(8,128)(2,1)}, bf16[128,3584]{1,0:T(8,128)(2,1)S(1)}, u32[]{:S(2)}, u32[]{:S(2)}) collective-permute-start(bf16[128,3584]{1,0:T(8,128)(2,1)} %refs_6_.1), channel_id=1, source_target_pairs={{0,1},{1,2},{2,3},{3,0},{4,5},{5,6},{6,7},{7,4},{8,9},{9,10},{10,1... | collective-permute-start | bytes 2752520 | tf_op jit(solution)/shard_map/ppermute | solution.py:340
  3.7 26.1 %collective-permute-start.4 = (bf16[128,3584]{1,0:T(8,128)(2,1)}, bf16[128,3584]{1,0:T(8,128)(2,1)S(1)}, u32[]{:S(2)}, u32[]{:S(2)}) collective-permute-start(bf16[128,3584]{1,0:T(8,128)(2,1)} %refs_6_.1), channel_id=1, source_target_pairs={{0,16},{4,20},{8,24},{12,28},{16,0},{20,4},{24,8},{28,12},{1,17},{... | collective-permute-start | bytes 2752520 | tf_op jit(solution)/shard_map/ppermute | solution.py:337
  5.2 24.5 %collective-permute-start.3 = (bf16[128,3584]{1,0:T(8,128)(2,1)}, bf16[128,3584]{1,0:T(8,128)(2,1)}, u32[]{:S(2)}, u32[]{:S(2)}) collective-permute-start(bf16[128,3584]{1,0:T(8,128)(2,1)} %refs_6_.1), channel_id=1, source_target_pairs={{0,8},{4,12},{8,0},{12,4},{16,24},{20,28},{24,16},{28,20},{1,9},{5... | collective-permute-start | bytes 2752520 | tf_op jit(solution)/shard_map/ppermute | solution.py:337
  8.8 16.0 %collective-permute-start.1 = (bf16[4,256]{1,0:T(4,128)(2,1)S(1)}, bf16[4,256]{1,0:T(4,128)(2,1)S(1)}, u32[]{:S(2)}, u32[]{:S(2)}) collective-permute-start(bf16[4,256]{1,0:T(4,128)(2,1)S(1)} %pad_maximum_fusion.5), channel_id=1, source_target_pairs={{0,2},{1,3},{2,0},{3,1},{4,6},{5,7},{6,4},{7,5},{8,10},{9,11},{10,... | collective-permute-start | bytes 6152 | tf_op jit(solution)/shard_map/ppermute | solution.py:340
  11.5 17.0 %collective-permute-start = (bf16[4,256]{1,0:T(4,128)(2,1)S(1)}, bf16[4,256]{1,0:T(4,128)(2,1)S(1)}, u32[]{:S(2)}, u32[]{:S(2)}) collective-permute-start(bf16[4,256]{1,0:T(4,128)(2,1)S(1)} %pad_maximum_fusion.5), channel_id=1, source_target_pairs={{0,1},{1,2},{2,3},{3,0},{4,5},{5,6},{6,7},{7,4},{8,9},{9,10},{10,1... | collective-permute-start | bytes 6152 | tf_op jit(solution)/shard_map/ppermute | solution.py:340
  24.8 30.2 %copy-start.15 = (bf16[128,3584]{1,0:T(8,128)(2,1)S(1)}, bf16[128,3584]{1,0:T(8,128)(2,1)}, u32[]{:S(2)}) copy-start(bf16[128,3584]{1,0:T(8,128)(2,1)} %refs_6_.1) | copy-start | bytes 2752516
  24.8 4.9 %collective-permute-start.2 = (bf16[4,256]{1,0:T(4,128)(2,1)S(1)}, bf16[4,256]{1,0:T(4,128)(2,1)S(1)}, u32[]{:S(2)}, u32[]{:S(2)}) collective-permute-start(bf16[4,256]{1,0:T(4,128)(2,1)S(1)} %pad_maximum_fusion.5), channel_id=1, source_target_pairs={{0,3},{1,0},{2,1},{3,2},{4,7},{5,4},{6,5},{7,6},{8,11},{9,8},{10,9... | collective-permute-start | bytes 6152 | tf_op jit(solution)/shard_map/ppermute | solution.py:340
  29.8 81.3 %copy-start.17 = (bf16[128,3584]{1,0:T(8,128)(2,1)}, bf16[128,3584]{1,0:T(8,128)(2,1)S(1)}, u32[]{:S(2)}) copy-start(bf16[128,3584]{1,0:T(8,128)(2,1)S(1)} %collective-permute-done.5.refs_0_.refs_6_.refs_10_) | copy-start | bytes 2752516
  29.8 75.1 %copy-start.19 = (bf16[128,3584]{1,0:T(8,128)(2,1)}, bf16[128,3584]{1,0:T(8,128)(2,1)S(1)}, u32[]{:S(2)}) copy-start(bf16[128,3584]{1,0:T(8,128)(2,1)S(1)} %collective-permute-done.4.refs_2_.refs_4_.refs_8_) | copy-start | bytes 2752516
  29.8 38.2 %collective-permute-start.13 = (bf16[512,3584]{1,0:T(8,128)(2,1)}, bf16[512,3584]{1,0:T(8,128)(2,1)}, u32[]{:S(2)}, u32[]{:S(2)}) collective-permute-start(bf16[512,3584]{1,0:T(8,128)(2,1)} %bitcast.25), channel_id=1, source_target_pairs={{0,4},{4,0},{8,12},{12,8},{16,20},{20,16},{24,28},{28,24},{1,5},{5... | collective-permute-start | bytes 11010056 | tf_op jit(solution)/shard_map/ppermute | solution.py:337
  29.9 25.2 %collective-permute-start.11 = (bf16[128,3584]{1,0:T(8,128)(2,1)S(1)}, bf16[128,3584]{1,0:T(8,128)(2,1)}, u32[]{:S(2)}, u32[]{:S(2)}) collective-permute-start(bf16[128,3584]{1,0:T(8,128)(2,1)S(1)} %collective-permute-done.5.refs_0_.refs_6_.refs_10_), channel_id=1, source_target_pairs={{0,1},{1,2},{2,3},{3,0},{4,5},{5,6},{6,7},{7,4},{8,9},{9,10},{10,1... | collective-permute-start | bytes 2752520 | tf_op jit(solution)/shard_map/ppermute | solution.py:340
  30.7 36.7 %collective-permute-start.6 = (bf16[128,3584]{1,0:T(8,128)(2,1)S(1)}, bf16[128,3584]{1,0:T(8,128)(2,1)S(1)}, u32[]{:S(2)}, u32[]{:S(2)}) collective-permute-start(bf16[128,3584]{1,0:T(8,128)(2,1)S(1)} %collective-permute-done.5.refs_0_.refs_6_.refs_10_), channel_id=1, source_target_pairs={{0,8},{4,12},{8,0},{12,4},{16,24},{20,28},{24,16},{28,20},{1,9},{5... | collective-permute-start | bytes 2752520 | tf_op jit(solution)/shard_map/ppermute | solution.py:337
  32.2 33.7 %collective-permute-start.9 = (bf16[128,3584]{1,0:T(8,128)(2,1)}, bf16[128,3584]{1,0:T(8,128)(2,1)}, u32[]{:S(2)}, u32[]{:S(2)}) collective-permute-start(bf16[128,3584]{1,0:T(8,128)(2,1)} %collective-permute-done.3.refs_1_.refs_3_.refs_7_), channel_id=1, source_target_pairs={{0,16},{4,20},{8,24},{12,28},{16,0},{20,4},{24,8},{28,12},{1,17},{... | collective-permute-start | bytes 2752520 | tf_op jit(solution)/shard_map/ppermute | solution.py:337
  36.3 29.1 %collective-permute-start.7 = (bf16[4,4,64,256]{3,2,1,0:T(8,128)(2,1)S(1)}, bf16[4,4,64,256]{3,2,1,0:T(8,128)(2,1)S(1)}, u32[]{:S(2)}, u32[]{:S(2)}) collective-permute-start(bf16[4,4,64,256]{3,2,1,0:T(8,128)(2,1)S(1)} %get-tuple-element.259), channel_id=1, source_target_pairs={{0,24},{4,28},{8,16},{12,20},{16,8},{20,12},{24,0},{28,4},{1,25},{... | collective-permute-start | bytes 1572872 | tf_op jit(solution)/shard_map/ppermute | solution.py:337
  55.1 25.7 %collective-permute-start.12 = (bf16[128,3584]{1,0:T(8,128)(2,1)S(1)}, bf16[128,3584]{1,0:T(8,128)(2,1)S(1)}, u32[]{:S(2)}, u32[]{:S(2)}) collective-permute-start(bf16[128,3584]{1,0:T(8,128)(2,1)S(1)} %copy-done.15), channel_id=1, source_target_pairs={{0,3},{1,0},{2,1},{3,2},{4,7},{5,4},{6,5},{7,6},{8,11},{9,8},{10,9... | collective-permute-start | bytes 2752520 | tf_op jit(solution)/shard_map/ppermute | solution.py:340
  65.9 12.6 %collective-permute-start.10 = (bf16[4,4,64,256]{3,2,1,0:T(8,128)(2,1)S(1)}, bf16[4,4,64,256]{3,2,1,0:T(8,128)(2,1)S(1)}, u32[]{:S(2)}, u32[]{:S(2)}) collective-permute-start(bf16[4,4,64,256]{3,2,1,0:T(8,128)(2,1)S(1)} %get-tuple-element.145), channel_id=1, source_target_pairs={{0,16},{4,20},{8,24},{12,28},{16,0},{20,4},{24,8},{28,12},{1,17},{... | collective-permute-start | bytes 1572872 | tf_op jit(solution)/shard_map/ppermute | solution.py:337
  67.4 12.6 %collective-permute-start.8 = (bf16[4,4,64,256]{3,2,1,0:T(8,128)(2,1)S(1)}, bf16[4,4,64,256]{3,2,1,0:T(8,128)(2,1)S(1)}, u32[]{:S(2)}, u32[]{:S(2)}) collective-permute-start(bf16[4,4,64,256]{3,2,1,0:T(8,128)(2,1)S(1)} %get-tuple-element.141), channel_id=1, source_target_pairs={{0,8},{4,12},{8,0},{12,4},{16,24},{20,28},{24,16},{28,20},{1,9},{5... | collective-permute-start | bytes 1572872 | tf_op jit(solution)/shard_map/ppermute | solution.py:337
  81.8 20.4 %collective-permute-start.15 = (bf16[128,3584]{1,0:T(8,128)(2,1)}, bf16[128,3584]{1,0:T(8,128)(2,1)}, u32[]{:S(2)}, u32[]{:S(2)}) collective-permute-start(bf16[128,3584]{1,0:T(8,128)(2,1)} %collective-permute-done.11.refs_3_.refs_9_.refs_13_), channel_id=1, source_target_pairs={{0,8},{4,12},{8,0},{12,4},{16,24},{20,28},{24,16},{28,20},{1,9},{5... | collective-permute-start | bytes 2752520 | tf_op jit(solution)/shard_map/ppermute | solution.py:337
  82.6 20.5 %collective-permute-start.14 = (bf16[128,3584]{1,0:T(8,128)(2,1)S(1)}, bf16[128,3584]{1,0:T(8,128)(2,1)}, u32[]{:S(2)}, u32[]{:S(2)}) collective-permute-start(bf16[128,3584]{1,0:T(8,128)(2,1)S(1)} %collective-permute-done.5.refs_0_.refs_6_.refs_10_), channel_id=1, source_target_pairs={{0,16},{4,20},{8,24},{12,28},{16,0},{20,4},{24,8},{28,12},{1,17},{... | collective-permute-start | bytes 2752520 | tf_op jit(solution)/shard_map/ppermute | solution.py:337
  83.5 21.3 %collective-permute-start.16 = (bf16[128,3584]{1,0:T(8,128)(2,1)}, bf16[128,3584]{1,0:T(8,128)(2,1)}, u32[]{:S(2)}, u32[]{:S(2)}) collective-permute-start(bf16[128,3584]{1,0:T(8,128)(2,1)} %collective-permute-done.3.refs_1_.refs_3_.refs_7_), channel_id=1, source_target_pairs={{0,3},{1,0},{2,1},{3,2},{4,7},{5,4},{6,5},{7,6},{8,11},{9,8},{10,9... | collective-permute-start | bytes 2752520 | tf_op jit(solution)/shard_map/ppermute | solution.py:340
  101.7 46.4 %copy-start.14 = (bf16[2,512,512]{2,1,0:T(8,128)(2,1)}, bf16[2,512,512]{2,1,0:T(8,128)(2,1)S(1)}, u32[]{:S(2)}) copy-start(bf16[2,512,512]{2,1,0:T(8,128)(2,1)S(1)} %get-tuple-element.204.refs_0_) | copy-start | bytes 3145732
  104.8 33.0 %copy-start.6 = (bf16[128,3584]{1,0:T(8,128)(2,1)S(1)}, bf16[128,3584]{1,0:T(8,128)(2,1)}, u32[]{:S(2)}) copy-start(bf16[128,3584]{1,0:T(8,128)(2,1)} %copy-done.5) | copy-start | bytes 2752516
  104.8 33.0 %copy-start.12 = (bf16[4,4,64,256]{3,2,1,0:T(8,128)(2,1)S(1)}, bf16[4,4,64,256]{3,2,1,0:T(8,128)(2,1)}, u32[]{:S(2)}) copy-start(bf16[4,4,64,256]{3,2,1,0:T(8,128)(2,1)} %copy-done.11) | copy-start | bytes 1572868
  104.8 20.9 %collective-permute-start.19 = (bf16[128,3584]{1,0:T(8,128)(2,1)S(1)}, bf16[128,3584]{1,0:T(8,128)(2,1)S(1)}, u32[]{:S(2)}, u32[]{:S(2)}) collective-permute-start(bf16[128,3584]{1,0:T(8,128)(2,1)S(1)} %collective-permute-done.4.refs_2_.refs_4_.refs_8_), channel_id=1, source_target_pairs={{0,3},{1,0},{2,1},{3,2},{4,7},{5,4},{6,5},{7,6},{8,11},{9,8},{10,9... | collective-permute-start | bytes 2752520 | tf_op jit(solution)/shard_map/ppermute | solution.py:340
  109.1 20.0 %collective-permute-start.17 = (bf16[128,3584]{1,0:T(8,128)(2,1)}, bf16[128,3584]{1,0:T(8,128)(2,1)S(1)}, u32[]{:S(2)}, u32[]{:S(2)}) collective-permute-start(bf16[128,3584]{1,0:T(8,128)(2,1)} %collective-permute-done.14.refs_2_.refs_8_.refs_12_), channel_id=1, source_target_pairs={{0,8},{4,12},{8,0},{12,4},{16,24},{20,28},{24,16},{28,20},{1,9},{5... | collective-permute-start | bytes 2752520 | tf_op jit(solution)/shard_map/ppermute | solution.py:337
  110.4 19.9 %collective-permute-start.18 = (bf16[128,3584]{1,0:T(8,128)(2,1)}, bf16[128,3584]{1,0:T(8,128)(2,1)S(1)}, u32[]{:S(2)}, u32[]{:S(2)}) collective-permute-start(bf16[128,3584]{1,0:T(8,128)(2,1)} %collective-permute-done.11.refs_3_.refs_9_.refs_13_), channel_id=1, source_target_pairs={{0,16},{4,20},{8,24},{12,28},{16,0},{20,4},{24,8},{28,12},{1,17},{... | collective-permute-start | bytes 2752520 | tf_op jit(solution)/shard_map/ppermute | solution.py:337
  125.8 43.3 %copy-start.7 = (bf16[128,3584]{1,0:T(8,128)(2,1)}, bf16[128,3584]{1,0:T(8,128)(2,1)S(1)}, u32[]{:S(2)}) copy-start(bf16[128,3584]{1,0:T(8,128)(2,1)S(1)} %collective-permute-done.19.refs_3_.refs_5_.refs_19_) | copy-start | bytes 2752516
  129.1 40.0 %copy-start.8 = (bf16[128,3584]{1,0:T(8,128)(2,1)}, bf16[128,3584]{1,0:T(8,128)(2,1)S(1)}, u32[]{:S(2)}) copy-start(bf16[128,3584]{1,0:T(8,128)(2,1)S(1)} %collective-permute-done.17.refs_0_.refs_2_.refs_16_) | copy-start | bytes 2752516
  130.4 38.7 %copy-start.9 = (bf16[128,3584]{1,0:T(8,128)(2,1)}, bf16[128,3584]{1,0:T(8,128)(2,1)S(1)}, u32[]{:S(2)}) copy-start(bf16[128,3584]{1,0:T(8,128)(2,1)S(1)} %collective-permute-done.18.refs_1_.refs_3_.refs_17_) | copy-start | bytes 2752516
  130.4 7.5 %collective-permute-start.22 = (bf16[4,64,256]{2,1,0:T(8,128)(2,1)S(1)}, bf16[4,64,256]{2,1,0:T(8,128)(2,1)S(1)}, u32[]{:S(2)}, u32[]{:S(2)}) collective-permute-start(bf16[4,64,256]{2,1,0:T(8,128)(2,1)S(1)} %get-tuple-element.186), channel_id=1, source_target_pairs={{0,8},{4,12},{8,0},{12,4},{16,24},{20,28},{24,16},{28,20},{1,9},{5... | collective-permute-start | bytes 393224 | tf_op jit(solution)/shard_map/ppermute | solution.py:337
  131.8 14.2 %collective-permute-start.23 = (bf16[4,64,256]{2,1,0:T(8,128)(2,1)S(1)}, bf16[4,64,256]{2,1,0:T(8,128)(2,1)S(1)}, u32[]{:S(2)}, u32[]{:S(2)}) collective-permute-start(bf16[4,64,256]{2,1,0:T(8,128)(2,1)S(1)} %get-tuple-element.187), channel_id=1, source_target_pairs={{0,16},{4,20},{8,24},{12,28},{16,0},{20,4},{24,8},{28,12},{1,17},{... | collective-permute-start | bytes 393224 | tf_op jit(solution)/shard_map/ppermute | solution.py:337
  134.3 11.7 %collective-permute-start.24 = (bf16[4,64,256]{2,1,0:T(8,128)(2,1)S(1)}, bf16[4,64,256]{2,1,0:T(8,128)(2,1)S(1)}, u32[]{:S(2)}, u32[]{:S(2)}) collective-permute-start(bf16[4,64,256]{2,1,0:T(8,128)(2,1)S(1)} %get-tuple-element.188), channel_id=1, source_target_pairs={{0,24},{4,28},{8,16},{12,20},{16,8},{20,12},{24,0},{28,4},{1,25},{... | collective-permute-start | bytes 393224 | tf_op jit(solution)/shard_map/ppermute | solution.py:337
  134.4 13.1 %collective-permute-start.25 = (bf16[4,64,256]{2,1,0:T(8,128)(2,1)S(1)}, bf16[4,64,256]{2,1,0:T(8,128)(2,1)S(1)}, u32[]{:S(2)}, u32[]{:S(2)}) collective-permute-start(bf16[4,64,256]{2,1,0:T(8,128)(2,1)S(1)} %get-tuple-element.190), channel_id=1, source_target_pairs={{0,8},{4,12},{8,0},{12,4},{16,24},{20,28},{24,16},{28,20},{1,9},{5... | collective-permute-start | bytes 393224 | tf_op jit(solution)/shard_map/ppermute | solution.py:337
  135.8 21.6 %collective-permute-start.20 = (bf16[128,3584]{1,0:T(8,128)(2,1)}, bf16[128,3584]{1,0:T(8,128)(2,1)S(1)}, u32[]{:S(2)}, u32[]{:S(2)}) collective-permute-start(bf16[128,3584]{1,0:T(8,128)(2,1)} %collective-permute-done.15.refs_4_.refs_10_.refs_14_), channel_id=1, source_target_pairs={{0,16},{4,20},{8,24},{12,28},{16,0},{20,4},{24,8},{28,12},{1,17},{... | collective-permute-start | bytes 2752520 | tf_op jit(solution)/shard_map/ppermute | solution.py:337
  137.8 19.6 %collective-permute-start.21 = (bf16[128,3584]{1,0:T(8,128)(2,1)}, bf16[128,3584]{1,0:T(8,128)(2,1)S(1)}, u32[]{:S(2)}, u32[]{:S(2)}) collective-permute-start(bf16[128,3584]{1,0:T(8,128)(2,1)} %collective-permute-done.9.refs_3_.refs_5_.refs_9_), channel_id=1, source_target_pairs={{0,3},{1,0},{2,1},{3,2},{4,7},{5,4},{6,5},{7,6},{8,11},{9,8},{10,9... | collective-permute-start | bytes 2752520 | tf_op jit(solution)/shard_map/ppermute | solution.py:340
  146.0 11.4 %collective-permute-start.26 = (bf16[4,64,256]{2,1,0:T(8,128)(2,1)S(1)}, bf16[4,64,256]{2,1,0:T(8,128)(2,1)S(1)}, u32[]{:S(2)}, u32[]{:S(2)}) collective-permute-start(bf16[4,64,256]{2,1,0:T(8,128)(2,1)S(1)} %get-tuple-element.191), channel_id=1, source_target_pairs={{0,16},{4,20},{8,24},{12,28},{16,0},{20,4},{24,8},{28,12},{1,17},{... | collective-permute-start | bytes 393224 | tf_op jit(solution)/shard_map/ppermute | solution.py:337
  146.1 11.3 %collective-permute-start.27 = (bf16[4,64,256]{2,1,0:T(8,128)(2,1)S(1)}, bf16[4,64,256]{2,1,0:T(8,128)(2,1)S(1)}, u32[]{:S(2)}, u32[]{:S(2)}) collective-permute-start(bf16[4,64,256]{2,1,0:T(8,128)(2,1)S(1)} %get-tuple-element.193), channel_id=1, source_target_pairs={{0,8},{4,12},{8,0},{12,4},{16,24},{20,28},{24,16},{28,20},{1,9},{5... | collective-permute-start | bytes 393224 | tf_op jit(solution)/shard_map/ppermute | solution.py:337
  147.5 9.9 %collective-permute-start.28 = (bf16[4,64,256]{2,1,0:T(8,128)(2,1)S(1)}, bf16[4,64,256]{2,1,0:T(8,128)(2,1)S(1)}, u32[]{:S(2)}, u32[]{:S(2)}) collective-permute-start(bf16[4,64,256]{2,1,0:T(8,128)(2,1)S(1)} %get-tuple-element.194), channel_id=1, source_target_pairs={{0,8},{4,12},{8,0},{12,4},{16,24},{20,28},{24,16},{28,20},{1,9},{5... | collective-permute-start | bytes 393224 | tf_op jit(solution)/shard_map/ppermute | solution.py:337
  157.4 18.2 %collective-permute-start.29 = (bf16[512,3584]{1,0:T(8,128)(2,1)S(1)}, bf16[512,3584]{1,0:T(8,128)(2,1)S(1)}, u32[]{:S(2)}, u32[]{:S(2)}) collective-permute-start(bf16[512,3584]{1,0:T(8,128)(2,1)S(1)} %shard_map.79), channel_id=1, source_target_pairs={{0,4},{4,0},{8,12},{12,8},{16,20},{20,16},{24,28},{28,24},{1,5},{5... | collective-permute-start | bytes 11010056 | tf_op jit(solution)/shard_map/ppermute | solution.py:337
  157.5 9.8 %collective-permute-start.30 = (bf16[4,64,256]{2,1,0:T(8,128)(2,1)S(1)}, bf16[4,64,256]{2,1,0:T(8,128)(2,1)S(1)}, u32[]{:S(2)}, u32[]{:S(2)}) collective-permute-start(bf16[4,64,256]{2,1,0:T(8,128)(2,1)S(1)} %get-tuple-element.214), channel_id=1, source_target_pairs={{0,24},{4,28},{8,16},{12,20},{16,8},{20,12},{24,0},{28,4},{1,25},{... | collective-permute-start | bytes 393224 | tf_op jit(solution)/shard_map/ppermute | solution.py:337
  159.3 15.2 %collective-permute-start.31 = (bf16[4,64,256]{2,1,0:T(8,128)(2,1)S(1)}, bf16[4,64,256]{2,1,0:T(8,128)(2,1)S(1)}, u32[]{:S(2)}, u32[]{:S(2)}) collective-permute-start(bf16[4,64,256]{2,1,0:T(8,128)(2,1)S(1)} %get-tuple-element.215), channel_id=1, source_target_pairs={{0,16},{4,20},{8,24},{12,28},{16,0},{20,4},{24,8},{28,12},{1,17},{... | collective-permute-start | bytes 393224 | tf_op jit(solution)/shard_map/ppermute | solution.py:337
  159.7 15.9 %collective-permute-start.32 = (bf16[4,64,256]{2,1,0:T(8,128)(2,1)S(1)}, bf16[4,64,256]{2,1,0:T(8,128)(2,1)S(1)}, u32[]{:S(2)}, u32[]{:S(2)}) collective-permute-start(bf16[4,64,256]{2,1,0:T(8,128)(2,1)S(1)} %get-tuple-element.217), channel_id=1, source_target_pairs={{0,16},{4,20},{8,24},{12,28},{16,0},{20,4},{24,8},{28,12},{1,17},{... | collective-permute-start | bytes 393224 | tf_op jit(solution)/shard_map/ppermute | solution.py:337
  166.0 9.5 %collective-permute-start.33 = (bf16[4,64,256]{2,1,0:T(8,128)(2,1)S(1)}, bf16[4,64,256]{2,1,0:T(8,128)(2,1)S(1)}, u32[]{:S(2)}, u32[]{:S(2)}) collective-permute-start(bf16[4,64,256]{2,1,0:T(8,128)(2,1)S(1)} %get-tuple-element.220), channel_id=1, source_target_pairs={{0,24},{4,28},{8,16},{12,20},{16,8},{20,12},{24,0},{28,4},{1,25},{... | collective-permute-start | bytes 393224 | tf_op jit(solution)/shard_map/ppermute | solution.py:337
  167.3 8.3 %collective-permute-start.34 = (bf16[4,64,256]{2,1,0:T(8,128)(2,1)S(1)}, bf16[4,64,256]{2,1,0:T(8,128)(2,1)S(1)}, u32[]{:S(2)}, u32[]{:S(2)}) collective-permute-start(bf16[4,64,256]{2,1,0:T(8,128)(2,1)S(1)} %get-tuple-element.221), channel_id=1, source_target_pairs={{0,24},{4,28},{8,16},{12,20},{16,8},{20,12},{24,0},{28,4},{1,25},{... | collective-permute-start | bytes 393224 | tf_op jit(solution)/shard_map/ppermute | solution.py:337
  177.4 15.4 %collective-permute-start.38 = (bf16[512,3584]{1,0:T(8,128)(2,1)}, bf16[512,3584]{1,0:T(8,128)(2,1)}, u32[]{:S(2)}, u32[]{:S(2)}) collective-permute-start(bf16[512,3584]{1,0:T(8,128)(2,1)} %shard_map.81), channel_id=1, source_target_pairs={{0,4},{4,0},{8,12},{12,8},{16,20},{20,16},{24,28},{28,24},{1,5},{5... | collective-permute-start | bytes 11010056 | tf_op jit(solution)/shard_map/ppermute | solution.py:337
  183.5 8.5 %collective-permute-start.37 = (f32[4,128]{1,0:T(4,128)S(1)}, f32[4,128]{1,0:T(4,128)S(1)}, u32[]{:S(2)}, u32[]{:S(2)}) collective-permute-start(f32[4,128]{1,0:T(4,128)S(1)} %get-tuple-element.262), channel_id=1, source_target_pairs={{0,1},{1,2},{2,3},{3,0},{4,5},{5,6},{6,7},{7,4},{8,9},{9,10},{10,1... | collective-permute-start | bytes 6152 | tf_op jit(solution)/shard_map/ppermute | solution.py:340
  184.6 7.4 %collective-permute-start.36 = (f32[4,128]{1,0:T(4,128)S(1)}, f32[4,128]{1,0:T(4,128)S(1)}, u32[]{:S(2)}, u32[]{:S(2)}) collective-permute-start(f32[4,128]{1,0:T(4,128)S(1)} %get-tuple-element.263), channel_id=1, source_target_pairs={{0,2},{1,3},{2,0},{3,1},{4,6},{5,7},{6,4},{7,5},{8,10},{9,11},{10,... | collective-permute-start | bytes 6152 | tf_op jit(solution)/shard_map/ppermute | solution.py:340
  184.9 7.1 %collective-permute-start.35 = (f32[4,128]{1,0:T(4,128)S(1)}, f32[4,128]{1,0:T(4,128)S(1)}, u32[]{:S(2)}, u32[]{:S(2)}) collective-permute-start(f32[4,128]{1,0:T(4,128)S(1)} %get-tuple-element.264), channel_id=1, source_target_pairs={{0,3},{1,0},{2,1},{3,2},{4,7},{5,4},{6,5},{7,6},{8,11},{9,8},{10,9... | collective-permute-start | bytes 6152 | tf_op jit(solution)/shard_map/ppermute | solution.py:340
  (42 other events, 403.8 us)
